TPU v7x, 32 devices: a whole 2x2x4 slice. The times are simulated.
32 devices in a mesh: row: 4 (over z), col: 2 (over y), depth: 4 (over x, core).
Axes of the slice: x: 2, y: 2, z: 4, core: 2. Of those that a mesh axis runs over, the one named last changes fastest.
Arguments:
- tokens: bfloat16 [768, 8192], P('col', 'depth'), may hold values from -6 to 6
- weight: bfloat16 [4096, 3, 8192], P(('row', 'col'), None, 'depth'), may hold values from -0.0625 to 0.0625
- taps: float32 [7, 256], P(None, 'row'), may hold values from -3 to 3
- upstream: bfloat16 [768, 4096], P(('col', 'depth'), 'row'), may hold values from -6 to 6
Outputs:
- output: bfloat16 [768, 4096], P(('col', 'depth'), 'row')
- grad_tokens: bfloat16 [768, 8192], P('col', 'depth')
- grad_weight: float32 [4096, 3, 8192], P(('row', 'col'), None, 'depth')
- grad_taps: float32 [7, 256], P(None, 'row')
All inputs are finite; a program needn't handle non-finite values.
Results may differ from a plain program's by a relative error of at most 0.034.
Values may be sent and summed in bfloat16 or wider, within the bound.
No kernel may reach another device: no remote copies, remote signals or barrier semaphores. Data moves between devices by JAX's collectives and lax.ppermute only.
A program may use at most 128 MiB of HBM per device.

v0:
```python
import jax
import jax.numpy as jnp
from jax import lax
from jax.sharding import PartitionSpec as P

GROUP = 16
KT = 7


def passed_along(value, axis, steps):
    count = lax.axis_size(axis)
    leading, last = (max(0, -steps), min(count, count - steps))
    return lax.ppermute(value, axis, [(source, source + steps) for source in range(leading, last)])


def on_device(tokens, weight, taps, upstream):
    local_tok = upstream.shape[0]
    channels = upstream.shape[1]
    margin = KT - 1
    panel_full = lax.all_gather(weight, "col", axis=0, tiled=True)
    summed_proj = lax.psum_scatter(
        jnp.einsum("td,csd->tsc", tokens, panel_full, preferred_element_type=jnp.float32).astype(
            jnp.bfloat16
        ),
        "depth",
        scatter_dimension=0,
        tiled=True,
    )
    rounded = lax.optimization_barrier(summed_proj).astype(jnp.float32)
    query_part = rounded[:, 0, :]
    key_part = rounded[:, 1, :]
    value_part = rounded[:, 2, :]
    mixed = key_part * value_part
    spread = jnp.repeat(taps, GROUP, axis=1)
    earlier = passed_along(mixed[local_tok - margin :], ("col", "depth"), 1)
    padded = jnp.concatenate([earlier, mixed], 0)
    filtered = jnp.zeros((local_tok, channels), jnp.float32)
    for offset in range(KT):
        first_row = margin - offset
        filtered = filtered + spread[offset] * padded[first_row : first_row + local_tok]
    output = (query_part * filtered).astype(jnp.bfloat16)
    upstream_f = upstream.astype(jnp.float32)
    grad_query = upstream_f * filtered
    grad_filtered = upstream_f * query_part
    later = passed_along(grad_filtered[:margin], ("col", "depth"), -1)
    padded_grad = jnp.concatenate([grad_filtered, later], 0)
    grad_mixed = jnp.zeros((local_tok, channels), jnp.float32)
    for offset in range(KT):
        grad_mixed = grad_mixed + spread[offset] * padded_grad[offset : offset + local_tok]
    grad_key = grad_mixed * value_part
    grad_value = grad_mixed * key_part
    grad_proj = jnp.stack([grad_query, grad_key, grad_value], axis=1).astype(jnp.bfloat16)
    tap_rows = []
    for offset in range(KT):
        first_row = margin - offset
        summed = jnp.sum(grad_filtered * padded[first_row : first_row + local_tok], axis=0)
        tap_rows.append(summed.reshape(-1, GROUP).sum(axis=1))
    grad_taps = lax.psum(jnp.stack(tap_rows, 0), ("col", "depth"))
    grad_group = lax.all_gather(grad_proj, "depth", axis=0, tiled=True)
    grad_weight = lax.psum_scatter(
        jnp.einsum("tsc,td->csd", grad_group, tokens, preferred_element_type=jnp.float32).astype(
            jnp.bfloat16
        ),
        "col",
        scatter_dimension=0,
        tiled=True,
    ).astype(jnp.float32)
    partial_in = jnp.einsum(
        "tsc,csd->td", grad_group, panel_full, preferred_element_type=jnp.float32
    )
    grad_tokens = lax.psum(partial_in.astype(jnp.bfloat16), "row")
    return (output, grad_tokens, grad_weight, grad_taps)


def solution(mesh):
    in_specs = (
        P("col", "depth"),
        P(("row", "col"), None, "depth"),
        P(None, "row"),
        P(("col", "depth"), "row"),
    )
    out_specs = (
        P(("col", "depth"), "row"),
        P("col", "depth"),
        P(("row", "col"), None, "depth"),
        P(None, "row"),
    )
    return jax.shard_map(
        on_device, mesh=mesh, in_specs=in_specs, out_specs=out_specs, check_vma=False
    )
```

profile of v0, /device:TPU:0, one launch (start us, length us, event | category | flops | bytes accessed | tf_op | source)
XLA Modules:
  0.0 520.4 jit_solution(14107191586877993569)
XLA Ops:
  7.2 0.0 all-gather.3.cloned.1.call-start
  7.2 0.7 all-gather.3.cloned.1.call-update
  7.9 0.0 reduce-scatter.7.cloned.1.call-start
  8.0 156.9 %all-gather.3.cloned.1.call-done = bf16[1024,3,2048]{2,0,1:T(8,128)(2,1)} async-done(((bf16[512,3,2048]{2,0,1:T(8,128)(2,1)}), bf16[1024,3,2048]{2,0,1:T(8,128)(2,1)}) %all-gather.3.cloned.1.call-update) | async-done | bytes 12582928 | tf_op jit(solution)/shard_map/all_gather | solution.py:20
  164.8 10.7 %convolution_convert_fusion = bf16[1024,3,384]{2,0,1:T(8,128)(2,1)} fusion(bf16[1024,3,2048]{2,0,1:T(8,128)(2,1)} %all-gather.3.cloned.1.call-done, bf16[384,2048]{1,0:T(8,128)(2,1)S(1)} %copy-done), kind=kOutput, calls=%fused_computation.2 | convolution fusion | flops 4833017856 | bytes 16515072 | tf_op jit(solution)/shard_map/td,csd->tsc/dot_general | solution.py:22
  175.6 4.3 copy.21
  179.8 0.0 reduce-scatter.7.cloned.1.call-update
  179.9 0.0 all-gather.5.cloned.1.call-start
  179.9 33.2 %reduce-scatter.7.cloned.1.call-done = bf16[96,3072]{1,0:T(8,128)(2,1)} async-done(((bf16[384,3072]{1,0:T(8,128)(2,1)}), bf16[96,3072]{1,0:T(8,128)(2,1)}) %reduce-scatter.7.cloned.1.call-update) | async-done | bytes 589840
  213.1 2.2 copy.22
  215.3 1.2 convert_element_type.30
  216.5 0.1 fusion.16
  216.6 0.8 copy-done.2
  217.4 1.0 slice.147
  218.4 2.6 collective-permute-start
  221.0 1.1 copy.16
  222.1 6.7 %multiply_reduce_fusion = (f32[1024]{0:T(1024)S(1)}, f32[1024]{0:T(1024)S(1)}, f32[1024]{0:T(1024)S(1)}, f32[1024]{0:T(1024)S(1)}, f32[1024]{0:T(1024)S(1)}, /*i...) fusion(f32[96,1024]{0,1:T(8,128)} %copy-done.2, f32[6,1024]{0,1:T(8,128)} %collective-permute-done, ...), kind=kLoop, calls=%fused_computation.40 | loop fusion | flops 2155520 | bytes 1429504 | tf_op jit(solution)/shard_map/reduce_sum | solution.py:56
  228.7 1.3 collective-permute-start.1
  230.1 0.1 broadcast_in_dim.29
  230.1 0.1 broadcast_in_dim.30
  230.2 0.1 broadcast_in_dim.37
  230.3 0.1 broadcast_in_dim.38
  230.4 0.1 broadcast_in_dim.35
  230.4 0.1 broadcast_in_dim.36
  230.5 0.1 broadcast_in_dim.33
  230.6 0.1 broadcast_in_dim.34
  230.7 0.1 broadcast_in_dim.31
  230.7 0.1 broadcast_in_dim.32
  230.8 0.1 broadcast_in_dim.41
  230.9 0.1 broadcast_in_dim.42
  231.0 0.1 broadcast_in_dim.39
  231.0 0.1 broadcast_in_dim.40
  231.1 6.3 %collective-permute-done.1 = f32[6,1024]{0,1:T(8,128)} collective-permute-done((f32[6,1024]{0,1:T(8,128)}, f32[6,1024]{0,1:T(8,128)}, u32[]{:S(2)}, u32[]{:S(2)}) %collective-permute-start.1) | collective-permute-done | bytes 24608 | tf_op jit(solution)/shard_map/ppermute | solution.py:13
  237.5 10.2 %fusion.17 = (bf16[96,1,1024]{0,2,1:T(8,128)(2,1)S(1)}, f32[96,1024]{0,1:T(8,128)S(1)}, bf16[96,1,1024]{0,2,1:T(8,128)(2,1)S(1)}, f32[96,1024]{0,1:T(8,128)S(1)}) fusion(f32[96,3,1024]{0,2,1:T(8,128)S(1)} %convert_element_type.30, f32[6,1024]{0,1:T(8,128)} %collective-permute-done.1, f32[96,1024]{0,1:T(8,128)} %get-tuple-element.23, ...), kind=kLoop, calls=%fused_computation.52 | loop fusion | flops 4227072 | bytes 2633728 | tf_op jit(solution)/shard_map/stack | solution.py:52
  247.7 0.1 fusion.18
  247.8 0.2 pad_maximum_fusion
  248.0 1.1 copy.17
  249.1 0.0 all-gather.5.cloned.1.call-update
  249.1 0.2 reduce-scatter.5.cloned.1.call-start
  249.3 33.6 %all-gather.5.cloned.1.call-done = bf16[384,3,1024]{2,0,1:T(8,128)(2,1)} async-done(((bf16[96,3,1024]{2,0,1:T(8,128)(2,1)}), bf16[384,3,1024]{2,0,1:T(8,128)(2,1)}) %all-gather.5.cloned.1.call-update) | async-done | bytes 2359312 | tf_op jit(solution)/shard_map/all_gather | solution.py:59
  282.9 11.3 %convert_bitcast_fusion = bf16[1024,3,2048]{2,0,1:T(8,128)(2,1)} fusion(bf16[384,3,1024]{2,0,1:T(8,128)(2,1)} %all-gather.5.cloned.1.call-done, bf16[384,2048]{1,0:T(8,128)(2,1)S(1)} %copy-done), kind=kOutput, calls=%fused_computation | convolution fusion | flops 4838129664 | bytes 16515072 | tf_op jit(solution)/shard_map/tsc,td->csd/dot_general | solution.py:61
  294.3 0.0 reduce-scatter.5.cloned.1.call-update
  294.3 0.0 all-reduce.2.cloned.1.call-start
  294.3 9.6 %bitcast_convert_fusion = bf16[384,2048]{1,0:T(8,128)(2,1)} fusion(bf16[384,3,1024]{2,0,1:T(8,128)(2,1)} %all-gather.5.cloned.1.call-done, bf16[1024,3,2048]{2,0,1:T(8,128)(2,1)} %all-gather.3.cloned.1.call-done), kind=kOutput, calls=%fused_computation.1 | convolution fusion | flops 4832624640 | bytes 16515072 | tf_op jit(solution)/shard_map/tsc,csd->td/dot_general | solution.py:68
  304.0 0.1 reshape.64
  304.0 0.1 reshape.63
  304.1 0.1 reduce_sum.139
  304.2 0.1 reduce_sum.137
  304.3 0.1 reshape.62
  304.4 0.1 reduce_sum.135
  304.5 0.1 reshape.61
  304.6 0.1 reduce_sum.133
  304.7 0.1 reshape.60
  304.8 0.1 reduce_sum.131
  304.9 0.1 reshape.59
  305.0 0.1 reduce_sum.129
  305.1 0.1 reshape.58
  305.2 0.1 reduce_sum.127
  305.4 14.1 %psum.15 = f32[7,64]{1,0:T(8,128)} all-reduce(f32[7,64]{1,0:T(8,128)S(1)} %stack.51), channel_id=1, replica_groups=mesh['row'=4,'col'=2,'depth'=4] {'col','depth'}, use_global_device_ids=true, to_apply=%region_17.0 | all-reduce | flops 448 | bytes 3584 | tf_op jit(solution)/shard_map/psum | solution.py:58
  319.5 0.8 copy.18
  320.3 118.8 %reduce-scatter.5.cloned.1.call-done = bf16[512,3,2048]{2,0,1:T(8,128)(2,1)} async-done(((bf16[1024,3,2048]{2,0,1:T(8,128)(2,1)}), bf16[512,3,2048]{2,0,1:T(8,128)(2,1)}) %reduce-scatter.5.cloned.1.call-update) | async-done | bytes 6291472 | tf_op jit(solution)/shard_map/reduce_scatter | solution.py:60
  439.1 9.2 %convert_element_type.36 = f32[512,3,2048]{2,0,1:T(8,128)} convert(bf16[512,3,2048]{2,0,1:T(8,128)(2,1)} %reduce-scatter.5.cloned.1.call-done) | non-fusion elementwise | flops 3145728 | bytes 18874368 | tf_op jit(solution)/shard_map/convert_element_type | solution.py:67
  448.3 62.8 %all-reduce.2.cloned.1.call-done = bf16[384,2048]{1,0:T(8,128)(2,1)} async-done(((bf16[384,2048]{1,0:T(8,128)(2,1)}), bf16[384,2048]{1,0:T(8,128)(2,1)}) %all-reduce.2.cloned.1.call-update) | async-done | bytes 1572880 | tf_op jit(solution)/shard_map/psum | solution.py:71
  511.1 2.7 copy.24
  (11 shorter events, 0.1 us)
Async XLA Ops:
  7.2 157.7 %copy-start = (bf16[384,2048]{1,0:T(8,128)(2,1)S(1)}, bf16[384,2048]{1,0:T(8,128)(2,1)}, u32[]{:S(2)}) copy-start(bf16[384,2048]{1,0:T(8,128)(2,1)} %param.4) | copy-start | bytes 4718596
  7.2 157.7 %all-gather.3.cloned.1.call-start = ((), (), s32[]{:S(2)}) async-start(), calls=%async_computation.2 | async-start | bytes 18874368 | tf_op jit(solution)/shard_map/all_gather | solution.py:20
  7.9 205.1 %reduce-scatter.7.cloned.1.call-start = ((), (), s32[]{:S(2)}) async-start(), calls=%async_computation.6 | async-start | bytes 2949120
  179.9 103.1 %all-gather.5.cloned.1.call-start = ((), (), s32[]{:S(2)}) async-start(), calls=%async_computation.3 | async-start | bytes 2949120 | tf_op jit(solution)/shard_map/all_gather | solution.py:59
  216.5 13.5 %copy-start.3 = (f32[7,64]{1,0:T(8,128)S(1)}, f32[7,64]{1,0:T(8,128)}, u32[]{:S(2)}) copy-start(f32[7,64]{1,0:T(8,128)} %param.6) | copy-start | bytes 5380
  216.6 0.8 copy-start.2
  218.4 3.7 collective-permute-start
  228.7 8.7 %collective-permute-start.1 = (f32[6,1024]{0,1:T(8,128)}, f32[6,1024]{0,1:T(8,128)}, u32[]{:S(2)}, u32[]{:S(2)}) collective-permute-start(f32[6,1024]{0,1:T(8,128)} %bitcast.68), channel_id=1, source_target_pairs={{1,0},{2,1},{3,2},{4,3},{5,4},{6,5},{7,6},{9,8},{10,9},{11,10},{12... | collective-permute-start | bytes 73736 | tf_op jit(solution)/shard_map/ppermute | solution.py:13
  249.1 190.0 %reduce-scatter.5.cloned.1.call-start = ((), (), s32[]{:S(2)}) async-start(), calls=%async_computation.5 | async-start | bytes 18874368 | tf_op jit(solution)/shard_map/reduce_scatter | solution.py:60
  294.3 216.8 %all-reduce.2.cloned.1.call-start = ((), (), s32[]{:S(2)}) async-start(), calls=%async_computation.4 | async-start | bytes 3145728 | tf_op jit(solution)/shard_map/psum | solution.py:71
  439.1 74.8 %copy-start.1 = (bf16[384,2048]{1,0:T(8,128)(2,1)S(1)}, bf16[384,2048]{1,0:T(8,128)(2,1)}, u32[]{:S(2)}) copy-start(bf16[384,2048]{1,0:T(8,128)(2,1)} %param.4) | copy-start | bytes 4718596
Sparse Core Ops, SparseCore 0:
  9.6 155.2 all-gather.2
  180.0 33.0 reduce-scatter.6
  249.2 33.6 all-gather.4
  294.4 144.6 reduce-scatter.4
  442.0 69.0 all-reduce.1
where the time goes:
time: 521 us; the launch traced here: 520 us
  waiting for transfers between devices  412 us (79%)
  matrix products  31.7 us (6%)
  other arithmetic  28.5 us (5%)
  local copies, waits for them, and re-layouts  15.6 us (3%)
  blocking collectives  14.1 us (3%)
  between operations  13.9 us (3%)
    all_gather x1, waiting for transfers between devices, on_device(): panel_full = lax.all_gather(weight, 'col', axis=0, tiled=True)  157 us
    reduce_scatter x1, waiting for transfers between devices, on_device(): lax.psum_scatter(jnp.einsum('tsc,td->csd', grad_group, tokens, preferred_...  119 us
    psum x1, waiting for transfers between devices, on_device(): grad_tokens = lax.psum(partial_in.astype(jnp.bfloat16), 'row')  62.8 us
    unnamed x6, waiting for transfers between devices  33.9 us
    all_gather x1, waiting for transfers between devices, on_device(): grad_group = lax.all_gather(grad_proj, 'depth', axis=0, tiled=True)  33.6 us
    psum x1, blocking collectives, on_device(): grad_taps = lax.psum(jnp.stack(tap_rows, 0), ('col', 'depth'))  14.1 us
    unnamed x13, local copies, waits for them, and re-layouts  11.9 us
    dot_general x1, matrix products, on_device(): jnp.einsum('tsc,td->csd', grad_group, tokens, preferred_element_type=jnp....  11.3 us
  transfers between devices with their start and end apart: 7, of which 6 were waited for; matrix products, arithmetic and copies ran while one was open for 4% of the time, Pallas kernels for 0%

commit v1 on v0

v1 whole, which is shorter than its diff:
```python
import functools

import jax
import jax.numpy as jnp
from jax import lax
from jax.experimental import pallas as pl
from jax.experimental.pallas import tpu as pltpu
from jax.sharding import PartitionSpec as P

GROUP = 16
KT = 7
PAD = 8
LANES = 128
VMEM_LIMIT = 48 * 1024 * 1024


def swap(value, axis, flip):
    count = lax.axis_size(axis)
    return lax.ppermute(value, axis, [(i, i ^ flip) for i in range(count)])


def params():
    return pltpu.CompilerParams(vmem_limit_bytes=VMEM_LIMIT)


def project_kernel(place, x_ref, w_ref, keep_ref, send_ref, *, count, width):
    stream = pl.program_id(0)
    core = place[0] % 2
    x = x_ref[...]
    nt = (((1,), (1,)), ((), ()))
    if width % LANES == 0:
        whole = lax.dot_general(x, w_ref[0], nt, preferred_element_type=jnp.float32).astype(jnp.bfloat16)
        blocks = [whole[:, j * width : (j + 1) * width] for j in range(count)]
    else:
        blocks = [
            lax.dot_general(
                x, w_ref[0, j * width : (j + 1) * width, :], nt, preferred_element_type=jnp.float32
            ).astype(jnp.bfloat16)
            for j in range(count)
        ]
    for mine in range(2):

        @pl.when(core == mine)
        def _():
            for j in range(count):
                at = (j ^ place[0]) // 2
                if j % 2 == mine:
                    keep_ref[at, stream] = blocks[j]
                else:
                    send_ref[at, stream] = blocks[j]


def project(place, x, w, count):
    tok, feat = x.shape
    streams, channels, _ = w.shape
    width = channels // count
    part = jax.ShapeDtypeStruct((count // 2, streams, tok, width), jnp.bfloat16)
    spec = pl.BlockSpec((count // 2, streams, tok, width), lambda s, _: (0, 0, 0, 0))
    return pl.pallas_call(
        functools.partial(project_kernel, count=count, width=width),
        grid_spec=pltpu.PrefetchScalarGridSpec(
            num_scalar_prefetch=1,
            grid=(streams,),
            in_specs=[
                pl.BlockSpec((tok, feat), lambda s, _: (0, 0)),
                pl.BlockSpec((1, channels, feat), lambda s, _: (s, 0, 0)),
            ],
            out_specs=[spec, spec],
        ),
        out_shape=[part, part],
        compiler_params=params(),
        cost_estimate=pl.CostEstimate(
            flops=2 * tok * feat * channels * streams,
            bytes_accessed=2 * (tok * feat + channels * streams * feat + tok * channels * streams),
            transcendentals=0,
        ),
        name="project",
    )(place, x, w)


def middle_kernel(place, taps_ref, up_ref, *refs, groups, terms, tile):
    part_refs = refs[: groups * terms]
    grad_ref, out_ref, grad_taps_ref, q_s, k_s, v_s, mixed_s, gf_s = refs[groups * terms :]
    col = place[1]
    tok = part_refs[0].shape[2]
    width = part_refs[0].shape[3]
    total = groups * tok
    mixed_s[0:PAD, :] = jnp.zeros((PAD, width), jnp.float32)
    gf_s[total : total + PAD, :] = jnp.zeros((PAD, width), jnp.float32)
    for k in range(groups):
        start = (col ^ k) * tok
        for i in range(tok // tile):
            inside = slice(i * tile, (i + 1) * tile)
            rows = pl.ds(pl.multiple_of(start + i * tile, tile), tile)
            streams = []
            for s in range(3):
                acc = None
                for ref in part_refs[k * terms : (k + 1) * terms]:
                    term = ref[0, s, inside, :].astype(jnp.float32)
                    acc = term if acc is None else acc + term
                streams.append(acc.astype(jnp.bfloat16).astype(jnp.float32))
            query, key, value = streams
            q_s[rows, :] = query
            k_s[rows, :] = key
            v_s[rows, :] = value
            mixed_s[pl.ds(pl.multiple_of(start + i * tile + PAD, PAD), tile), :] = key * value
            gf_s[rows, :] = up_ref[rows, :].astype(jnp.float32) * query
    taps = taps_ref[...]
    sums = [jnp.zeros((8, width), jnp.float32) for _ in range(KT)]
    for a in range(groups):
        for i in range(tok // tile):
            first = a * tok + i * tile
            rows = slice(first, first + tile)
            inside = slice(i * tile, (i + 1) * tile)
            gf = gf_s[rows, :]
            filtered = jnp.zeros((tile, width), jnp.float32)
            grad_mixed = jnp.zeros((tile, width), jnp.float32)
            for j in range(KT):
                shifted = mixed_s[first + PAD - j : first + PAD - j + tile, :]
                filtered = filtered + taps[j : j + 1, :] * shifted
                sums[j] = sums[j] + (gf * shifted).reshape(tile // 8, 8, width).sum(axis=0)
                grad_mixed = grad_mixed + taps[j : j + 1, :] * gf_s[first + j : first + j + tile, :]
            out_ref[rows, :] = (q_s[rows, :] * filtered).astype(jnp.bfloat16)
            at = col ^ a
            grad_ref[at, 0, inside, :] = (up_ref[rows, :].astype(jnp.float32) * filtered).astype(jnp.bfloat16)
            grad_ref[at, 1, inside, :] = (grad_mixed * v_s[rows, :]).astype(jnp.bfloat16)
            grad_ref[at, 2, inside, :] = (grad_mixed * k_s[rows, :]).astype(jnp.bfloat16)
    for j in range(KT):
        grad_taps_ref[j : j + 1, :] = sums[j].sum(axis=0, keepdims=True)
    grad_taps_ref[KT : KT + 1, :] = jnp.zeros((1, width), jnp.float32)


def middle(place, taps, up, parts):
    groups, terms = len(parts), len(parts[0])
    _, _, tok, width = parts[0][0].shape
    total = groups * tok
    whole = lambda *shape: pl.BlockSpec(shape, lambda i, _: (0,) * len(shape))
    return pl.pallas_call(
        functools.partial(middle_kernel, groups=groups, terms=terms, tile=64),
        grid_spec=pltpu.PrefetchScalarGridSpec(
            num_scalar_prefetch=1,
            grid=(1,),
            in_specs=[whole(KT, width), whole(total, width)] + [whole(1, 3, tok, width)] * (groups * terms),
            out_specs=[whole(groups, 3, tok, width), whole(total, width), whole(8, width)],
            scratch_shapes=[pltpu.VMEM((total, width), jnp.float32)] * 3
            + [pltpu.VMEM((total + PAD, width), jnp.float32)] * 2,
        ),
        out_shape=[
            jax.ShapeDtypeStruct((groups, 3, tok, width), jnp.bfloat16),
            jax.ShapeDtypeStruct((total, width), jnp.bfloat16),
            jax.ShapeDtypeStruct((8, width), jnp.float32),
        ],
        compiler_params=params(),
        cost_estimate=pl.CostEstimate(
            flops=60 * total * width,
            bytes_accessed=2 * total * width * (3 * terms + 5),
            transcendentals=0,
        ),
        name="middle",
    )(place, taps, up, *[term for terms_of in parts for term in terms_of])


def assemble(place, grad_refs, whole_s, width):
    for r, ref in enumerate(grad_refs):
        at = pl.multiple_of((place[0] ^ r) * width, width)
        for k in range(ref.shape[0]):
            for s in range(3):
                tok = ref.shape[2]
                whole_s[s, k * tok : (k + 1) * tok, pl.ds(at, width)] = ref[k, s]


def input_grad_kernel(place, *refs, width, count):
    grad_refs = refs[:count]
    w_ref, out_ref = refs[count : count + 2]
    acc = jnp.zeros(out_ref.shape, jnp.float32)
    if width % LANES == 0:
        whole_s = refs[count + 2]

        @pl.when(pl.program_id(0) == 0)
        def _():
            assemble(place, grad_refs, whole_s, width)

        for s in range(3):
            acc = acc + jnp.dot(whole_s[s], w_ref[s], preferred_element_type=jnp.float32)
    else:
        for r, ref in enumerate(grad_refs):
            rows = pl.ds(pl.multiple_of((place[0] ^ r) * width, width), width)
            for s in range(3):
                acc = acc + jnp.dot(ref[0, s], w_ref[s, rows, :], preferred_element_type=jnp.float32)
    out_ref[...] = acc.astype(jnp.bfloat16)


def input_grad(place, grads, w, k):
    count = len(grads)
    _, _, tok, width = grads[0].shape
    streams, channels, feat = w.shape
    step = min(512, feat)
    wide = width % LANES == 0
    return pl.pallas_call(
        functools.partial(input_grad_kernel, width=width, count=count),
        grid_spec=pltpu.PrefetchScalarGridSpec(
            num_scalar_prefetch=1,
            grid=(feat // step,),
            in_specs=[pl.BlockSpec((1, streams, tok, width), lambda i, _: (k, 0, 0, 0))] * count
            + [pl.BlockSpec((streams, channels, step), lambda i, _: (0, 0, i))],
            out_specs=pl.BlockSpec((tok, step), lambda i, _: (0, i)),
            scratch_shapes=[pltpu.VMEM((streams, tok, channels), jnp.bfloat16)] if wide else [],
        ),
        out_shape=jax.ShapeDtypeStruct((tok, feat), jnp.bfloat16),
        compiler_params=params(),
        cost_estimate=pl.CostEstimate(
            flops=2 * tok * feat * channels * streams,
            bytes_accessed=2 * (tok * feat + channels * streams * feat + tok * channels * streams),
            transcendentals=0,
        ),
        name="input_grad",
    )(place, *grads, w)


def weight_grad_kernel(place, *refs, width, count, groups):
    grad_refs = refs[:count]
    x_refs = refs[count : count + groups]
    out_ref = refs[count + groups]
    tn = (((0,), (0,)), ((), ()))
    tok = x_refs[0].shape[0]
    s = pl.program_id(0)
    if width % LANES == 0:
        whole_s = refs[count + groups + 1]

        @pl.when((pl.program_id(0) == 0) & (pl.program_id(1) == 0))
        def _():
            assemble(place, grad_refs, whole_s, width)

        acc = None
        for k in range(groups):
            rows = slice(k * tok, (k + 1) * tok)
            term = lax.dot_general(whole_s[s, rows, :], x_refs[k][...], tn, preferred_element_type=jnp.float32)
            acc = term if acc is None else acc + term
        out_ref[0] = acc
    else:
        for r, ref in enumerate(grad_refs):
            acc = None
            for k in range(groups):
                term = lax.dot_general(ref[k, 0], x_refs[k][...], tn, preferred_element_type=jnp.float32)
                acc = term if acc is None else acc + term
            out_ref[0, pl.ds(pl.multiple_of((place[0] ^ r) * width, width), width), :] = acc


def weight_grad(place, grads, xs):
    count, groups = len(grads), len(xs)
    _, streams, tok, width = grads[0].shape
    feat = xs[0].shape[1]
    channels = width * count
    step = min(512, feat)
    wide = width % LANES == 0
    return pl.pallas_call(
        functools.partial(weight_grad_kernel, width=width, count=count, groups=groups),
        grid_spec=pltpu.PrefetchScalarGridSpec(
            num_scalar_prefetch=1,
            grid=(streams, feat // step),
            in_specs=[
                pl.BlockSpec((groups, streams, tok, width), lambda s, i, _: (0, 0, 0, 0))
                if wide
                else pl.BlockSpec((groups, 1, tok, width), lambda s, i, _: (0, s, 0, 0))
            ]
            * count
            + [pl.BlockSpec((tok, step), lambda s, i, _: (0, i))] * groups,
            out_specs=pl.BlockSpec((1, channels, step), lambda s, i, _: (s, 0, i)),
            scratch_shapes=[pltpu.VMEM((streams, groups * tok, channels), jnp.bfloat16)] if wide else [],
        ),
        out_shape=jax.ShapeDtypeStruct((streams, channels, feat), jnp.float32),
        compiler_params=params(),
        cost_estimate=pl.CostEstimate(
            flops=2 * groups * tok * feat * channels * streams,
            bytes_accessed=4 * channels * streams * feat + 2 * groups * tok * (feat + channels * streams),
            transcendentals=0,
        ),
        name="weight_grad",
    )(place, *grads, *xs)


def on_device(tokens, weight, taps, upstream):
    n_col = lax.axis_size("col")
    n_depth = lax.axis_size("depth")
    both = ("col", "depth")
    depth_at = lax.axis_index("depth")
    col_at = lax.axis_index("col")
    place = jnp.stack([depth_at, col_at]).astype(jnp.int32)
    w = jnp.transpose(weight, (1, 0, 2))
    own_groups = w.shape[1] // n_depth // GROUP
    xs = [tokens] + [swap(tokens, "col", k) for k in range(1, n_col)]
    up = lax.all_to_all(upstream, both, split_axis=1, concat_axis=0, tiled=True)
    first_group = (col_at * n_depth + depth_at) * own_groups
    own_taps = jnp.repeat(lax.dynamic_slice_in_dim(taps, first_group, own_groups, axis=1), GROUP, axis=1)
    parts = []
    for x in xs:
        keep, send = project(place, x, w, n_depth)
        near = swap(send, "depth", 1)
        terms = [keep, near]
        for r in range(2, n_depth, 2):
            pair = (keep[r // 2].astype(jnp.float32) + near[r // 2].astype(jnp.float32)).astype(jnp.bfloat16)
            terms.append(swap(pair[None], "depth", r))
        parts.append(terms)
    grad_own, output, tap_sums = middle(place, own_taps, up, parts)
    grads = [grad_own, swap(grad_own, "depth", 1)]
    for r in range(2, n_depth, 2):
        far = swap(grad_own, "depth", r)
        grads += [far, swap(far, "depth", 1)]
    total = None
    for k in range(1, n_col):
        term = swap(input_grad(place, grads, w, k), "col", k).astype(jnp.float32)
        total = term if total is None else total + term
    partial_in = input_grad(place, grads, w, 0).astype(jnp.float32) + total
    grad_tokens = lax.psum(partial_in.astype(jnp.bfloat16), "row")
    grad_weight = jnp.transpose(weight_grad(place, grads, xs), (1, 0, 2))
    output = lax.all_to_all(output, both, split_axis=0, concat_axis=1, tiled=True)
    own_grad_taps = tap_sums[:KT].reshape(KT, own_groups, GROUP).sum(axis=2)
    grad_taps = lax.all_gather(own_grad_taps, both, axis=1, tiled=True)
    return (output, grad_tokens, grad_weight, grad_taps)


def solution(mesh):
    in_specs = (
        P("col", "depth"),
        P(("row", "col"), None, "depth"),
        P(None, "row"),
        P(("col", "depth"), "row"),
    )
    out_specs = (
        P(("col", "depth"), "row"),
        P("col", "depth"),
        P(("row", "col"), None, "depth"),
        P(None, "row"),
    )
    return jax.shard_map(
        on_device, mesh=mesh, in_specs=in_specs, out_specs=out_specs, check_vma=False
    )
```

time: 521 us -> 217 us (0.42)
  waiting for transfers between devices: 412 us -> 124 us
  Pallas kernels: 0 us -> 38.4 us
  matrix products: 31.7 us -> 0 us
  other arithmetic: 28.5 us -> 3.5 us
  starting transfers between devices: 4.24 us -> 14.5 us
    all_gather x2 -> x0, waiting for transfers between devices: 190 us -> none  [the longest x1 157 us: on_device(): panel_full = lax.all_gather(weight, 'col', axis=0, tiled=True)]
    reduce_scatter x1 -> x0, waiting for transfers between devices: 119 us -> none  [on_device(): lax.psum_scatter(jnp.einsum('tsc,td->csd', grad_group, tokens, preferred_...]
    ppermute x2 -> x9, waiting for transfers between devices: 6.33 us -> 72.6 us  [swap(): return lax.ppermute(value, axis, [(i, i ^ flip) for i in range(count)])]
    pallas_call x0 -> x6, Pallas kernels: none -> 38.4 us  [the longest x1 12.4 us: weight_grad(): pl.pallas_call(functools.partial(weight_grad_kernel, width=width, count=c...]
    unnamed x6 -> x1, waiting for transfers between devices: 33.9 us -> 0.02 us
    dot_general x3 -> x0, matrix products: 31.7 us -> none  [the longest x1 11.3 us: on_device(): jnp.einsum('tsc,td->csd', grad_group, tokens, preferred_element_type=jnp....]
    psum x1, waiting for transfers between devices: 62.8 us -> 39.8 us  [on_device(): grad_tokens = lax.psum(partial_in.astype(jnp.bfloat16), 'row')]
    psum x1 -> x0, blocking collectives: 14.1 us -> none  [on_device(): grad_taps = lax.psum(jnp.stack(tap_rows, 0), ('col', 'depth'))]
  transfers between devices with their start and end apart: 7 -> 12, of which waited for: 6 -> 6; matrix products, arithmetic and copies ran while one was open for 4% -> 2% of each run, Pallas kernels for 0% -> 14%
where the time goes in v1:
time: 217 us
  waiting for transfers between devices  124 us (57%)
  Pallas kernels  38.4 us (18%)
  starting transfers between devices  14.5 us (7%)
  between operations  14.2 us (7%)
  local copies, waits for them, and re-layouts  12.8 us (6%)
  blocking collectives  9.49 us (4%)
  other arithmetic  3.5 us (2%)
    ppermute x9, waiting for transfers between devices, swap(): return lax.ppermute(value, axis, [(i, i ^ flip) for i in range(count)])  72.6 us
    psum x1, waiting for transfers between devices, on_device(): grad_tokens = lax.psum(partial_in.astype(jnp.bfloat16), 'row')  39.8 us
    pallas_call x1, Pallas kernels, weight_grad(): pl.pallas_call(functools.partial(weight_grad_kernel, width=width, count=c...  12.4 us
    pallas_call x2, Pallas kernels, input_grad(): pl.pallas_call(functools.partial(input_grad_kernel, width=width, count=co...  12.2 us
    pallas_call x2, Pallas kernels, project(): pl.pallas_call(functools.partial(project_kernel, count=count, width=width...  11.8 us
    all_to_all x1, waiting for transfers between devices, on_device(): up = lax.all_to_all(upstream, both, split_axis=1, concat_axis=0, tiled=True)  11.1 us
    unnamed x22, local copies, waits for them, and re-layouts  11 us
    all_gather x1, blocking collectives, on_device(): grad_taps = lax.all_gather(own_grad_taps, both, axis=1, tiled=True)  9.49 us
  transfers between devices with their start and end apart: 12, of which 6 were waited for; matrix products, arithmetic and copies ran while one was open for 2% of the time, Pallas kernels for 14%

profile of v1, /device:TPU:0, one launch (start us, length us, event | category | flops | bytes accessed | tf_op | source)
XLA Modules:
  0.0 216.5 jit_solution(15478626671513473553)
XLA Ops:
  7.2 0.0 copy-start
  7.2 3.0 %collective-permute-start.2 = (bf16[384,2048]{1,0:T(8,128)(2,1)}, bf16[384,2048]{1,0:T(8,128)(2,1)S(1)}, u32[]{:S(2)}, u32[]{:S(2)}) collective-permute-start(bf16[384,2048]{1,0:T(8,128)(2,1)} %refs_4_.1), channel_id=1, source_target_pairs={{0,4},{4,0},{1,5},{5,1},{2,6},{6,2},{3,7},{7,3},{8,12},{12,8},{9,1... | collective-permute-start | bytes 4718600 | tf_op jit(solution)/shard_map/ppermute | solution.py:19
  10.2 0.1 pad_add_fusion.place
  10.3 0.0 copy-start.1
  10.3 1.4 copy-done.1
  11.7 5.9 %project.2 = (bf16[2,3,384,128]{3,2,1,0:T(8,128)(2,1)S(1)}, bf16[2,3,384,128]{3,2,1,0:T(8,128)(2,1)S(1)}) custom-call(s32[2]{0:T(128)S(1)} %pad_add_fusion.place, bf16[384,2048]{1,0:T(8,128)(2,1)S(1)} %copy-done.1, bf16[3,512,2048]{2,1,0:T(8,128)(2,1)} %bitcast.22), custom_call_target="tpu_custom_call" | custom-call | flops 2415919104 | bytes 9043968 | tf_op jit(solution)/shard_map/project/pallas_call | solution.py:59
  17.6 0.1 collective-permute-start
  17.7 27.1 %collective-permute-done.2.x_ref.refs_5_ = bf16[384,2048]{1,0:T(8,128)(2,1)S(1)} collective-permute-done((bf16[384,2048]{1,0:T(8,128)(2,1)}, bf16[384,2048]{1,0:T(8,128)(2,1)S(1)}, u32[]{:S(2)}, u32[]{:S(2)}) %collective-permute-start.2) | collective-permute-done | bytes 1572896 | tf_op jit(solution)/shard_map/ppermute | solution.py:19
  44.8 5.9 %project.3 = (bf16[2,3,384,128]{3,2,1,0:T(8,128)(2,1)S(1)}, bf16[2,3,384,128]{3,2,1,0:T(8,128)(2,1)S(1)}) custom-call(s32[2]{0:T(128)S(1)} %pad_add_fusion.place, bf16[384,2048]{1,0:T(8,128)(2,1)S(1)} %collective-permute-done.2.x_ref.refs_5_, bf16[3,512,2048]{2,1,0:T(8,128)(2,1)} %bitcast.23), custom_call_target="tpu_custom_call" | custom-call | flops 2415919104 | bytes 9043968 | tf_op jit(solution)/shard_map/project/pallas_call | solution.py:59
  50.7 0.0 copy-done.3
  50.7 0.0 copy-start.9
  50.7 0.1 collective-permute-start.3
  50.8 0.0 collective-permute-done.refs_1_
  50.8 0.8 add_convert_fusion.2
  51.6 1.7 collective-permute-start.1
  53.3 0.0 collective-permute-done.3.refs_4_
  53.3 0.8 add_convert_fusion.1
  54.1 1.2 collective-permute-start.4
  55.3 0.0 copy-done
  55.3 0.7 copy_bitcast_fusion.1
  56.0 3.4 %all-to-all-start = ((bf16[96,8,128]{2,0,1:T(8,128)(2,1)}), bf16[96,8,128]{2,0,1:T(8,128)(2,1)S(1)}, u32[]{:S(2)}, u32[]{:S(2)}) async-start(bf16[96,8,128]{2,0,1:T(8,128)(2,1)} %copy_bitcast_fusion.1), calls=%async_computation | async-start | bytes 393216 | tf_op jit(solution)/shard_map/all_to_all | solution.py:292
  59.4 0.0 all-reduce.2.cloned.1.call-start
  59.5 0.0 copy-done.9
  59.5 0.1 constant_dynamic-slice_fusion
  59.6 0.1 broadcast_in_dim.2
  59.6 0.1 reshape.20.taps_ref
  59.7 11.1 %all-to-all-done = bf16[96,8,128]{2,0,1:T(8,128)(2,1)S(1)} async-done(((bf16[96,8,128]{2,0,1:T(8,128)(2,1)}), bf16[96,8,128]{2,0,1:T(8,128)(2,1)S(1)}, u32[]{:S(2)}, u32[]{:S(2)}) %all-to-all-start) | async-done | bytes 196640 | tf_op jit(solution)/shard_map/all_to_all | solution.py:292
  70.8 0.0 collective-permute-done.1.refs_2_
  70.8 0.0 copy-start.5
  70.8 0.7 copy-done.5
  71.5 0.0 collective-permute-done.4.refs_5_
  71.5 0.0 copy-start.7
  71.5 0.7 copy-done.7
  72.3 0.0 copy-start.6
  72.3 1.0 copy-done.6
  73.2 0.0 copy-start.8
  73.2 1.0 copy-done.8
  74.2 2.1 middle.1
  76.3 1.2 collective-permute-start.6
  77.5 0.0 collective-permute-start.5
  77.5 13.5 %collective-permute-done.6.refs_2_ = bf16[2,3,384,128]{3,2,1,0:T(8,128)(2,1)S(1)} collective-permute-done((bf16[2,3,384,128]{3,2,1,0:T(8,128)(2,1)S(1)}, bf16[2,3,384,128]{3,2,1,0:T(8,128)(2,1)S(1)}, u32[]{:S(2)}, u32[]{:S(2)}) %collective-permute-start.6) | collective-permute-done | bytes 589856 | tf_op jit(solution)/shard_map/ppermute | solution.py:19
  91.0 0.0 collective-permute-start.7
  91.0 0.0 collective-permute-done.5.refs_1_
  91.0 2.0 collective-permute-done.7.refs_3_
  93.0 6.1 %input_grad.3 = bf16[384,2048]{1,0:T(8,128)(2,1)S(1)} custom-call(s32[2]{0:T(128)S(1)} %pad_add_fusion.place, bf16[2,3,384,128]{3,2,1,0:T(8,128)(2,1)S(1)} %get-tuple-element.16.refs_0_, bf16[2,3,384,128]{3,2,1,0:T(8,128)(2,1)S(1)} %collective-permute-done.5.refs_1_, bf16[2,3,384,128]{3,2,1,0:T(8,128)(2,1)S(1)} %collective-permute-done.6.refs_2_, ...), custom_call_target="tpu_custom_call" | custom-call | flops 2415919104 | bytes 9043968 | tf_op jit(solution)/shard_map/input_grad/pallas_call | solution.py:199
  99.1 0.4 collective-permute-start.8
  99.5 6.1 %input_grad.2 = bf16[384,2048]{1,0:T(8,128)(2,1)S(1)} custom-call(s32[2]{0:T(128)S(1)} %pad_add_fusion.place, bf16[2,3,384,128]{3,2,1,0:T(8,128)(2,1)S(1)} %get-tuple-element.16.refs_0_, bf16[2,3,384,128]{3,2,1,0:T(8,128)(2,1)S(1)} %collective-permute-done.5.refs_1_, bf16[2,3,384,128]{3,2,1,0:T(8,128)(2,1)S(1)} %collective-permute-done.6.refs_2_, ...), custom_call_target="tpu_custom_call" | custom-call | flops 2415919104 | bytes 9043968 | tf_op jit(solution)/shard_map/input_grad/pallas_call | solution.py:199
  105.6 30.0 %collective-permute-done.8 = bf16[384,2048]{1,0:T(8,128)(2,1)S(1)} collective-permute-done((bf16[384,2048]{1,0:T(8,128)(2,1)S(1)}, bf16[384,2048]{1,0:T(8,128)(2,1)S(1)}, u32[]{:S(2)}, u32[]{:S(2)}) %collective-permute-start.8) | collective-permute-done | bytes 1572896 | tf_op jit(solution)/shard_map/ppermute | solution.py:19
  135.6 1.8 add_convert_fusion
  137.3 0.0 all-reduce.2.cloned.1.call-update
  137.4 3.4 %all-to-all-start.1 = ((bf16[8,96,128]{2,1,0:T(8,128)(2,1)}), bf16[8,96,128]{2,1,0:T(8,128)(2,1)S(1)}, u32[]{:S(2)}, u32[]{:S(2)}) async-start(bf16[8,96,128]{2,1,0:T(8,128)(2,1)} %bitcast.5), calls=%async_computation.1 | async-start | bytes 393216 | tf_op jit(solution)/shard_map/all_to_all | solution.py:316
  140.8 0.1 reshape.21
  140.8 0.1 reduce_sum.9
  140.9 0.1 copy.15
  141.0 9.5 %all_gather.3 = f32[7,64]{0,1:T(8,128)S(1)} all-gather(f32[7,8]{0,1:T(8,128)S(1)} %copy.15), channel_id=1, replica_groups=mesh['row'=4,'col'=2,'depth'=4] {'col','depth'}, dimensions={1}, use_global_device_ids=true | all-gather | bytes 2016 | tf_op jit(solution)/shard_map/all_gather | solution.py:318
  150.5 0.7 copy.16
  151.2 0.0 all-to-all-done.1
  151.2 0.7 copy_bitcast_fusion
  151.9 0.0 copy-start.2
  151.9 1.4 copy-done.2
  153.3 1.4 copy-done.4
  154.7 12.4 %weight_grad.1 = f32[3,512,2048]{2,1,0:T(8,128)} custom-call(s32[2]{0:T(128)S(1)} %pad_add_fusion.place, bf16[2,3,384,128]{3,2,1,0:T(8,128)(2,1)S(1)} %get-tuple-element.16.refs_0_, bf16[2,3,384,128]{3,2,1,0:T(8,128)(2,1)S(1)} %collective-permute-done.5.refs_1_, bf16[2,3,384,128]{3,2,1,0:T(8,128)(2,1)S(1)} %collective-permute-done.6.refs_2_, ...), custom_call_target="tpu_custom_call" | custom-call | flops 4831838208 | bytes 18087936 | tf_op jit(solution)/shard_map/weight_grad/pallas_call | solution.py:256
  167.1 39.8 %all-reduce.2.cloned.1.call-done = bf16[384,2048]{1,0:T(8,128)(2,1)} async-done(((bf16[384,2048]{1,0:T(8,128)(2,1)}), bf16[384,2048]{1,0:T(8,128)(2,1)}) %all-reduce.2.cloned.1.call-update) | async-done | bytes 1572880 | tf_op jit(solution)/shard_map/psum | solution.py:314
  206.9 2.7 %copy.22 = bf16[384,2048]{1,0:T(8,128)(2,1)} copy(bf16[384,2048]{1,0:T(8,128)(2,1)} %all-reduce.2.cloned.1.call-done) | data formatting | bytes 3145728
  (2 shorter events, 0.0 us)
Async XLA Ops:
  7.2 48.1 %copy-start = (bf16[96,1024]{1,0:T(8,128)(2,1)S(1)}, bf16[96,1024]{1,0:T(8,128)(2,1)}, u32[]{:S(2)}) copy-start(bf16[96,1024]{1,0:T(8,128)(2,1)} %param.7) | copy-start | bytes 589828
  7.2 37.6 %collective-permute-start.2 = (bf16[384,2048]{1,0:T(8,128)(2,1)}, bf16[384,2048]{1,0:T(8,128)(2,1)S(1)}, u32[]{:S(2)}, u32[]{:S(2)}) collective-permute-start(bf16[384,2048]{1,0:T(8,128)(2,1)} %refs_4_.1), channel_id=1, source_target_pairs={{0,4},{4,0},{1,5},{5,1},{2,6},{6,2},{3,7},{7,3},{8,12},{12,8},{9,1... | collective-permute-start | bytes 4718600 | tf_op jit(solution)/shard_map/ppermute | solution.py:19
  10.3 1.4 copy-start.1
  17.6 33.2 %collective-permute-start = (bf16[2,3,384,128]{3,2,1,0:T(8,128)(2,1)S(1)}, bf16[2,3,384,128]{3,2,1,0:T(8,128)(2,1)S(1)}, u32[]{:S(2)}, u32[]{:S(2)}) collective-permute-start(bf16[2,3,384,128]{3,2,1,0:T(8,128)(2,1)S(1)} %get-tuple-element.12), channel_id=1, source_target_pairs={{0,1},{1,0},{2,3},{3,2},{4,5},{5,4},{6,7},{7,6},{8,9},{9,8},{10,11... | collective-permute-start | bytes 1769480 | tf_op jit(solution)/shard_map/ppermute | solution.py:19
  44.8 5.9 %copy-start.3 = (bf16[384,2048]{1,0:T(8,128)(2,1)}, bf16[384,2048]{1,0:T(8,128)(2,1)S(1)}, u32[]{:S(2)}) copy-start(bf16[384,2048]{1,0:T(8,128)(2,1)S(1)} %collective-permute-done.2.x_ref.refs_5_) | copy-start | bytes 4718596
  50.7 8.8 %copy-start.9 = (f32[7,64]{1,0:T(8,128)S(1)}, f32[7,64]{1,0:T(8,128)}, u32[]{:S(2)}) copy-start(f32[7,64]{1,0:T(8,128)} %param.6) | copy-start | bytes 5380
  50.7 2.6 %collective-permute-start.3 = (bf16[2,3,384,128]{3,2,1,0:T(8,128)(2,1)S(1)}, bf16[2,3,384,128]{3,2,1,0:T(8,128)(2,1)S(1)}, u32[]{:S(2)}, u32[]{:S(2)}) collective-permute-start(bf16[2,3,384,128]{3,2,1,0:T(8,128)(2,1)S(1)} %get-tuple-element.14), channel_id=1, source_target_pairs={{0,1},{1,0},{2,3},{3,2},{4,5},{5,4},{6,7},{7,6},{8,9},{9,8},{10,11... | collective-permute-start | bytes 1769480 | tf_op jit(solution)/shard_map/ppermute | solution.py:19
  51.6 19.2 %collective-permute-start.1 = (bf16[1,3,384,128]{3,2,1,0:T(8,128)(2,1)}, bf16[1,3,384,128]{3,2,1,0:T(8,128)(2,1)S(1)}, u32[]{:S(2)}, u32[]{:S(2)}) collective-permute-start(bf16[1,3,384,128]{3,2,1,0:T(8,128)(2,1)} %add_convert_fusion.2), channel_id=1, source_target_pairs={{0,2},{1,3},{2,0},{3,1},{4,6},{5,7},{6,4},{7,5},{8,10},{9,11},{10,... | collective-permute-start | bytes 884744 | tf_op jit(solution)/shard_map/ppermute | solution.py:19
  54.1 17.4 %collective-permute-start.4 = (bf16[1,3,384,128]{3,2,1,0:T(8,128)(2,1)}, bf16[1,3,384,128]{3,2,1,0:T(8,128)(2,1)S(1)}, u32[]{:S(2)}, u32[]{:S(2)}) collective-permute-start(bf16[1,3,384,128]{3,2,1,0:T(8,128)(2,1)} %add_convert_fusion.1), channel_id=1, source_target_pairs={{0,2},{1,3},{2,0},{3,1},{4,6},{5,7},{6,4},{7,5},{8,10},{9,11},{10,... | collective-permute-start | bytes 884744 | tf_op jit(solution)/shard_map/ppermute | solution.py:19
  56.0 14.8 %all-to-all-start = ((bf16[96,8,128]{2,0,1:T(8,128)(2,1)}), bf16[96,8,128]{2,0,1:T(8,128)(2,1)S(1)}, u32[]{:S(2)}, u32[]{:S(2)}) async-start(bf16[96,8,128]{2,0,1:T(8,128)(2,1)} %copy_bitcast_fusion.1), calls=%async_computation | async-start | bytes 393216 | tf_op jit(solution)/shard_map/all_to_all | solution.py:292
  59.4 147.5 %all-reduce.2.cloned.1.call-start = ((), (), s32[]{:S(2)}) async-start(), calls=%async_computation.2 | async-start | bytes 3145728 | tf_op jit(solution)/shard_map/psum | solution.py:314
  70.8 0.7 copy-start.5
  71.5 0.7 copy-start.7
  72.3 1.0 copy-start.6
  73.2 1.0 copy-start.8
  76.3 14.7 %collective-permute-start.6 = (bf16[2,3,384,128]{3,2,1,0:T(8,128)(2,1)S(1)}, bf16[2,3,384,128]{3,2,1,0:T(8,128)(2,1)S(1)}, u32[]{:S(2)}, u32[]{:S(2)}) collective-permute-start(bf16[2,3,384,128]{3,2,1,0:T(8,128)(2,1)S(1)} %get-tuple-element.16.refs_0_), channel_id=1, source_target_pairs={{0,2},{1,3},{2,0},{3,1},{4,6},{5,7},{6,4},{7,5},{8,10},{9,11},{10,... | collective-permute-start | bytes 1769480 | tf_op jit(solution)/shard_map/ppermute | solution.py:19
  77.5 13.5 %collective-permute-start.5 = (bf16[2,3,384,128]{3,2,1,0:T(8,128)(2,1)S(1)}, bf16[2,3,384,128]{3,2,1,0:T(8,128)(2,1)S(1)}, u32[]{:S(2)}, u32[]{:S(2)}) collective-permute-start(bf16[2,3,384,128]{3,2,1,0:T(8,128)(2,1)S(1)} %get-tuple-element.16.refs_0_), channel_id=1, source_target_pairs={{0,1},{1,0},{2,3},{3,2},{4,5},{5,4},{6,7},{7,6},{8,9},{9,8},{10,11... | collective-permute-start | bytes 1769480 | tf_op jit(solution)/shard_map/ppermute | solution.py:19
  91.0 2.0 collective-permute-start.7
  99.1 36.5 %collective-permute-start.8 = (bf16[384,2048]{1,0:T(8,128)(2,1)S(1)}, bf16[384,2048]{1,0:T(8,128)(2,1)S(1)}, u32[]{:S(2)}, u32[]{:S(2)}) collective-permute-start(bf16[384,2048]{1,0:T(8,128)(2,1)S(1)} %input_grad.3), channel_id=1, source_target_pairs={{0,4},{4,0},{1,5},{5,1},{2,6},{6,2},{3,7},{7,3},{8,12},{12,8},{9,1... | collective-permute-start | bytes 4718600 | tf_op jit(solution)/shard_map/ppermute | solution.py:19
  137.4 13.8 %all-to-all-start.1 = ((bf16[8,96,128]{2,1,0:T(8,128)(2,1)}), bf16[8,96,128]{2,1,0:T(8,128)(2,1)S(1)}, u32[]{:S(2)}, u32[]{:S(2)}) async-start(bf16[8,96,128]{2,1,0:T(8,128)(2,1)} %bitcast.5), calls=%async_computation.1 | async-start | bytes 393216 | tf_op jit(solution)/shard_map/all_to_all | solution.py:316
  151.9 1.4 copy-start.2
  153.3 1.4 copy-start.4
Sparse Core Ops, SparseCore 0:
  137.5 69.4 all-reduce.1

commit v2 on v1

v2 whole, which is shorter than its diff:
```python
import functools

import jax
import jax.numpy as jnp
from jax import lax
from jax.experimental import pallas as pl
from jax.experimental.pallas import tpu as pltpu
from jax.sharding import PartitionSpec as P

GROUP = 16
KT = 7
PAD = 8
LANES = 128
VMEM_LIMIT = 48 * 1024 * 1024


def swap(value, axis, flip):
    count = lax.axis_size(axis)
    return lax.ppermute(value, axis, [(i, i ^ flip) for i in range(count)])


def params():
    return pltpu.CompilerParams(vmem_limit_bytes=VMEM_LIMIT)


def project_kernel(place, *refs, pieces, count, width):
    x_refs = refs[:pieces]
    w_ref, keep_ref, send_ref = refs[pieces : pieces + 3]
    stream = pl.program_id(0)
    core = place[0] % 2
    if pieces == 1:
        x = x_refs[0][...]
    else:
        x_out = refs[pieces + 3]
        third = x_refs[0].shape[0]
        parity = place[2] % 2

        @pl.when(stream == 0)
        def _():
            x_out[pl.ds(pl.multiple_of(parity * third, third), third), :] = x_refs[0][...]
            x_out[pl.ds(pl.multiple_of((1 - parity) * third, third), third), :] = x_refs[1][...]
            x_out[2 * third :, :] = x_refs[2][...]

        x = x_out[...]
    nt = (((1,), (1,)), ((), ()))
    if width % LANES == 0:
        whole = lax.dot_general(x, w_ref[0], nt, preferred_element_type=jnp.float32).astype(jnp.bfloat16)
        blocks = [whole[:, j * width : (j + 1) * width] for j in range(count)]
    else:
        blocks = [
            lax.dot_general(
                x, w_ref[0, j * width : (j + 1) * width, :], nt, preferred_element_type=jnp.float32
            ).astype(jnp.bfloat16)
            for j in range(count)
        ]
    for mine in range(2):

        @pl.when(core == mine)
        def _():
            for j in range(count):
                at = (j ^ place[0]) // 2
                if j % 2 == mine:
                    keep_ref[at, stream] = blocks[j]
                else:
                    send_ref[at, stream] = blocks[j]


def project(place, xs, w, count):
    tok, feat = sum(x.shape[0] for x in xs), xs[0].shape[1]
    streams, channels, _ = w.shape
    width = channels // count
    part = jax.ShapeDtypeStruct((count // 2, streams, tok, width), jnp.bfloat16)
    spec = pl.BlockSpec((count // 2, streams, tok, width), lambda s, _: (0, 0, 0, 0))
    joined = len(xs) > 1
    outs = pl.pallas_call(
        functools.partial(project_kernel, pieces=len(xs), count=count, width=width),
        grid_spec=pltpu.PrefetchScalarGridSpec(
            num_scalar_prefetch=1,
            grid=(streams,),
            in_specs=[pl.BlockSpec(x.shape, lambda s, _: (0, 0)) for x in xs]
            + [pl.BlockSpec((1, channels, feat), lambda s, _: (s, 0, 0))],
            out_specs=[spec, spec] + [pl.BlockSpec((tok, feat), lambda s, _: (0, 0))] * joined,
        ),
        out_shape=[part, part] + [jax.ShapeDtypeStruct((tok, feat), jnp.bfloat16)] * joined,
        compiler_params=params(),
        cost_estimate=pl.CostEstimate(
            flops=2 * tok * feat * channels * streams,
            bytes_accessed=2 * (tok * feat + channels * streams * feat + tok * channels * streams),
            transcendentals=0,
        ),
        name="project",
    )(place, *xs, w)
    return outs[0], outs[1], outs[2] if joined else xs[0]


def middle_kernel(place, taps_ref, up_ref, *refs, groups, terms, tile):
    part_refs = refs[: groups * terms]
    grad_refs = refs[groups * terms : groups * terms + groups]
    out_ref, q_s, k_s, v_s, mixed_s, gf_s, far_s = refs[groups * terms + groups :]
    col = place[1]
    tok = part_refs[0].shape[2]
    width = part_refs[0].shape[3]
    total = groups * tok
    mixed_s[0:PAD, :] = jnp.zeros((PAD, width), jnp.float32)
    gf_s[total : total + PAD, :] = jnp.zeros((PAD, width), jnp.float32)
    for k in range(groups):
        start = (col ^ k) * tok
        for i in range(tok // tile):
            inside = slice(i * tile, (i + 1) * tile)
            rows = pl.ds(pl.multiple_of(start + i * tile, tile), tile)
            streams = []
            for s in range(3):
                acc = None
                for ref in part_refs[k * terms : (k + 1) * terms]:
                    term = ref[0, s, inside, :].astype(jnp.float32)
                    acc = term if acc is None else acc + term
                streams.append(acc.astype(jnp.bfloat16).astype(jnp.float32))
            query, key, value = streams
            q_s[rows, :] = query
            k_s[rows, :] = key
            v_s[rows, :] = value
            mixed_s[pl.ds(pl.multiple_of(start + i * tile + PAD, PAD), tile), :] = key * value
            gf_s[rows, :] = up_ref[rows, :].astype(jnp.float32) * query
    taps = taps_ref[...]
    sums = [jnp.zeros((8, width), jnp.float32) for _ in range(KT)]
    for a in range(groups):
        for i in range(tok // tile):
            first = a * tok + i * tile
            rows = slice(first, first + tile)
            inside = slice(i * tile, (i + 1) * tile)
            gf = gf_s[rows, :]
            filtered = jnp.zeros((tile, width), jnp.float32)
            grad_mixed = jnp.zeros((tile, width), jnp.float32)
            for j in range(KT):
                shifted = mixed_s[first + PAD - j : first + PAD - j + tile, :]
                filtered = filtered + taps[j : j + 1, :] * shifted
                sums[j] = sums[j] + (gf * shifted).reshape(tile // 8, 8, width).sum(axis=0)
                grad_mixed = grad_mixed + taps[j : j + 1, :] * gf_s[first + j : first + j + tile, :]
            out_ref[first // tile, 0:tile, :] = (q_s[rows, :] * filtered).astype(jnp.bfloat16)
            at = col ^ a
            far_s[at, 0, inside, :] = (up_ref[rows, :].astype(jnp.float32) * filtered).astype(jnp.bfloat16)
            far_s[at, 1, inside, :] = (grad_mixed * v_s[rows, :]).astype(jnp.bfloat16)
            far_s[at, 2, inside, :] = (grad_mixed * k_s[rows, :]).astype(jnp.bfloat16)
    for k in range(groups):
        grad_refs[k][...] = far_s[k]
    rest = jnp.concatenate(
        [sums[j].sum(axis=0, keepdims=True) for j in range(KT)] + [jnp.zeros((1, width), jnp.float32)], axis=0
    )
    terms_of = []
    for _ in range(3):
        term = rest.astype(jnp.bfloat16).astype(jnp.float32)
        rest = rest - term
        terms_of.append(term)
    packed = jnp.concatenate(terms_of + [jnp.zeros((8, width), jnp.float32)], axis=0).astype(jnp.bfloat16)
    for i in range(out_ref.shape[0]):
        out_ref[i, tile : tile + 32, :] = packed


def middle(place, taps, up, parts, tile):
    groups, terms = len(parts), len(parts[0])
    _, _, tok, width = parts[0][0].shape
    total = groups * tok
    whole = lambda *shape: pl.BlockSpec(shape, lambda i, _: (0,) * len(shape))
    outs = pl.pallas_call(
        functools.partial(middle_kernel, groups=groups, terms=terms, tile=tile),
        grid_spec=pltpu.PrefetchScalarGridSpec(
            num_scalar_prefetch=1,
            grid=(1,),
            in_specs=[whole(KT, width), whole(total, width)] + [whole(1, 3, tok, width)] * (groups * terms),
            out_specs=[whole(3, tok, width)] * groups + [whole(total // tile, tile + 32, width)],
            scratch_shapes=[pltpu.VMEM((total, width), jnp.float32)] * 3
            + [pltpu.VMEM((total + PAD, width), jnp.float32)] * 2
            + [pltpu.VMEM((groups, 3, tok, width), jnp.bfloat16)],
        ),
        out_shape=[jax.ShapeDtypeStruct((3, tok, width), jnp.bfloat16)] * groups
        + [jax.ShapeDtypeStruct((total // tile, tile + 32, width), jnp.bfloat16)],
        compiler_params=params(),
        cost_estimate=pl.CostEstimate(
            flops=60 * total * width,
            bytes_accessed=2 * total * width * (3 * terms + 5),
            transcendentals=0,
        ),
        name="middle",
    )(place, taps, up, *[term for terms_of in parts for term in terms_of])
    return outs[:groups], outs[groups]


def assemble_kernel(place, *refs):
    grad_refs, out_ref = refs[:-1], refs[-1]
    width = grad_refs[0].shape[2]
    for r, ref in enumerate(grad_refs):
        at = pl.multiple_of((place[0] ^ r) * width, width)
        for s in range(3):
            out_ref[s, :, pl.ds(at, width)] = ref[s]


def assemble(place, grads):
    streams, tok, width = grads[0].shape
    out = jax.ShapeDtypeStruct((streams, tok, width * len(grads)), jnp.bfloat16)
    return pl.pallas_call(
        assemble_kernel,
        grid_spec=pltpu.PrefetchScalarGridSpec(
            num_scalar_prefetch=1,
            grid=(1,),
            in_specs=[pl.BlockSpec(grads[0].shape, lambda i, _: (0, 0, 0))] * len(grads),
            out_specs=pl.BlockSpec(out.shape, lambda i, _: (0, 0, 0)),
        ),
        out_shape=out,
        compiler_params=params(),
        cost_estimate=pl.CostEstimate(flops=0, bytes_accessed=4 * out.size, transcendentals=0),
        name="assemble",
    )(place, *grads)


def input_grad_kernel(place, *refs, width):
    grad_refs, w_ref, out_ref = refs[:-2], refs[-2], refs[-1]
    acc = jnp.zeros(out_ref.shape, jnp.float32)
    for r, ref in enumerate(grad_refs):
        for s in range(3):
            if len(grad_refs) == 1:
                rows = w_ref[s]
            else:
                rows = w_ref[s, pl.ds(pl.multiple_of((place[0] ^ r) * width, width), width), :]
            acc = acc + jnp.dot(ref[s], rows, preferred_element_type=jnp.float32)
    out_ref[...] = acc.astype(jnp.bfloat16)


def input_grad(place, grads, w, chunk, chunks):
    streams, tok, width = grads[0].shape
    _, channels, feat = w.shape
    step = feat // chunks
    return pl.pallas_call(
        functools.partial(input_grad_kernel, width=width),
        grid_spec=pltpu.PrefetchScalarGridSpec(
            num_scalar_prefetch=1,
            grid=(1,),
            in_specs=[pl.BlockSpec((streams, tok, width), lambda i, _: (0, 0, 0))] * len(grads)
            + [pl.BlockSpec((streams, channels, step), lambda i, _: (0, 0, chunk))],
            out_specs=pl.BlockSpec((tok, step), lambda i, _: (0, 0)),
        ),
        out_shape=jax.ShapeDtypeStruct((tok, step), jnp.bfloat16),
        compiler_params=params(),
        cost_estimate=pl.CostEstimate(
            flops=2 * tok * step * channels * streams,
            bytes_accessed=2 * (tok * step + channels * streams * step + tok * channels * streams),
            transcendentals=0,
        ),
        name="input_grad",
    )(place, *grads, w)


def weight_grad_kernel(place, *refs, groups, wide, chained):
    refs = refs[chained:]
    grad_refs = refs[:groups]
    x_refs = refs[groups : 2 * groups]
    out_ref = refs[2 * groups]
    tok, step = x_refs[0].shape
    width = grad_refs[0].shape[2]
    if wide:
        turned = refs[2 * groups + 1]

        @pl.when(pl.program_id(0) == 0)
        def _():
            for k in range(groups):
                for s in range(3):
                    turned[s * width : (s + 1) * width, k * tok : (k + 1) * tok] = grad_refs[k][s].T

        acc = None
        for k in range(groups):
            term = jnp.dot(
                turned[:, k * tok : (k + 1) * tok], x_refs[k][...], preferred_element_type=jnp.float32
            )
            acc = term if acc is None else acc + term
        for s in range(3):
            out_ref[s] = acc[s * width : (s + 1) * width, :]
    else:
        tn = (((0,), (0,)), ((), ()))
        for s in range(3):
            acc = None
            for k in range(groups):
                term = lax.dot_general(grad_refs[k][s], x_refs[k][...], tn, preferred_element_type=jnp.float32)
                acc = term if acc is None else acc + term
            out_ref[s] = acc


def weight_grad(place, earlier, grads, xs, r, count):
    groups = len(xs)
    streams, tok, width = grads[0].shape
    feat = xs[0].shape[1]
    channels = width * count
    step = min(512, feat)
    wide = width % LANES == 0
    chained = earlier is not None
    return pl.pallas_call(
        functools.partial(weight_grad_kernel, groups=groups, wide=wide, chained=chained),
        grid_spec=pltpu.PrefetchScalarGridSpec(
            num_scalar_prefetch=1,
            grid=(feat // step,),
            in_specs=[pl.BlockSpec(memory_space=pl.ANY)] * chained
            + [pl.BlockSpec((streams, tok, width), lambda i, _: (0, 0, 0))] * groups
            + [pl.BlockSpec((tok, step), lambda i, _: (0, i))] * groups,
            out_specs=pl.BlockSpec((streams, width, step), lambda i, at: (0, at[0] ^ r, i)),
            scratch_shapes=[pltpu.VMEM((streams * width, groups * tok), jnp.bfloat16)] if wide else [],
        ),
        out_shape=jax.ShapeDtypeStruct((streams, channels, feat), jnp.float32),
        input_output_aliases={1: 0} if chained else {},
        compiler_params=params(),
        cost_estimate=pl.CostEstimate(
            flops=2 * groups * tok * feat * width * streams,
            bytes_accessed=4 * width * streams * feat + 2 * groups * tok * (feat + width * streams),
            transcendentals=0,
        ),
        name="weight_grad",
    )(place, *([earlier] if chained else []), *grads, *xs)


def added(first, second):
    return (first.astype(jnp.float32) + second.astype(jnp.float32)).astype(jnp.bfloat16)


def sum_along_row(value):
    count = lax.axis_size("row")
    if count % 2:
        return lax.psum(value, "row")
    at = lax.axis_index("row")
    half = count // 2
    last = count - 1
    for i in range(half - 1):
        value = added(value, lax.ppermute(value, "row", [(i, i + 1), (last - i, last - i - 1)]))
    value = added(value, lax.ppermute(value, "row", [(half - 1, half), (half, half - 1)]))
    for i in reversed(range(half - 1)):
        outer = lax.ppermute(value, "row", [(i + 1, i), (last - i - 1, last - i)])
        value = jnp.where((at == i) | (at == last - i), outer, value)
    return value


def fetch_tokens(tokens, k):
    tok = tokens.shape[0]
    if tok % 48 or lax.axis_size("row") % 2:
        return [swap(tokens, "col", k)]
    third = tok // 3
    parity = lax.axis_index("row") % 2
    mine = swap(lax.dynamic_slice_in_dim(tokens, parity * third, third, axis=0), "col", k)
    return [mine, swap(mine, "row", 1), swap(tokens[2 * third :], "col", k)]


def on_device(tokens, weight, taps, upstream):
    n_col = lax.axis_size("col")
    n_depth = lax.axis_size("depth")
    both = ("col", "depth")
    local_tok = upstream.shape[0]
    depth_at = lax.axis_index("depth")
    col_at = lax.axis_index("col")
    place = jnp.stack([depth_at, col_at, lax.axis_index("row")]).astype(jnp.int32)
    w = jnp.transpose(weight, (1, 0, 2))
    width = w.shape[1] // n_depth
    own_groups = width // GROUP
    pieces = [fetch_tokens(tokens, k) for k in range(1, n_col)]
    up = lax.all_to_all(upstream, both, split_axis=1, concat_axis=0, tiled=True)
    own_tokens, up = lax.optimization_barrier((tokens, up))
    first_group = (col_at * n_depth + depth_at) * own_groups
    own_taps = jnp.repeat(lax.dynamic_slice_in_dim(taps, first_group, own_groups, axis=1), GROUP, axis=1)
    parts, xs = [], []
    for x_pieces in [[own_tokens]] + pieces:
        keep, send, x = project(place, x_pieces, w, n_depth)
        xs.append(x)
        near = swap(send, "depth", 1)
        terms = [keep, near]
        for r in range(2, n_depth, 2):
            terms.append(swap(added(keep[r // 2], near[r // 2])[None], "depth", r))
        parts.append(terms)
    own_grads, blocks = middle(place, own_taps, up, parts, local_tok)
    grads = [None] * n_col
    for k in reversed(range(n_col)):
        grads[k] = [own_grads[k], swap(own_grads[k], "depth", 1)]
        for r in range(2, n_depth, 2):
            far = swap(own_grads[k], "depth", r)
            grads[k] += [far, swap(far, "depth", 1)]
    chunks = 4
    lhs = [[assemble(place, of)] if width % LANES == 0 else of for of in grads]
    sent = [
        [swap(input_grad(place, lhs[k], w, c, chunks), "col", k) for c in range(chunks)] for k in range(1, n_col)
    ]
    done = []
    for c in range(chunks):
        total = input_grad(place, lhs[0], w, c, chunks).astype(jnp.float32)
        for of in sent:
            total = total + of[c].astype(jnp.float32)
        done.append(sum_along_row(total.astype(jnp.bfloat16)))
    grad_tokens = jnp.concatenate(done, axis=1)
    grad_weight = None
    for r in range(n_depth):
        grad_weight = weight_grad(place, grad_weight, [of[r] for of in grads], xs, r, n_depth)
    grad_weight = jnp.transpose(grad_weight, (1, 0, 2))
    blocks = lax.all_to_all(blocks, both, split_axis=0, concat_axis=0, tiled=True)
    output = jnp.transpose(blocks[:, :local_tok], (1, 0, 2)).reshape(local_tok, -1)
    sums = blocks[:, local_tok : local_tok + 24].astype(jnp.float32).reshape(-1, 3, 8, own_groups, GROUP)
    grad_taps = sums.sum(axis=(1, 4))[:, :KT].transpose(1, 0, 2).reshape(KT, -1)
    return (output, grad_tokens, grad_weight, grad_taps)


def solution(mesh):
    in_specs = (
        P("col", "depth"),
        P(("row", "col"), None, "depth"),
        P(None, "row"),
        P(("col", "depth"), "row"),
    )
    out_specs = (
        P(("col", "depth"), "row"),
        P("col", "depth"),
        P(("row", "col"), None, "depth"),
        P(None, "row"),
    )
    return jax.shard_map(
        on_device, mesh=mesh, in_specs=in_specs, out_specs=out_specs, check_vma=False
    )
```

time: 217 us -> 219 us (level)
  waiting for transfers between devices: 124 us -> 88.8 us
  starting transfers between devices: 14.5 us -> 42.1 us
  Pallas kernels: 38.4 us -> 60.5 us
  between operations: 14.2 us -> 1.12 us
  blocking collectives: 9.49 us -> 0 us
  local copies, waits for them, and re-layouts: 12.8 us -> 18.5 us
  other arithmetic: 3.5 us -> 6.64 us
    ppermute x0 -> x12, waiting for transfers between devices: none -> 50.7 us  [the longest x4 33.6 us: sum_along_row(): outer = lax.ppermute(value, 'row', [(i + 1, i), (last - i - 1, last - i)])]
    ppermute x9 -> x17, waiting for transfers between devices: 72.6 us -> 32 us  [swap(): return lax.ppermute(value, axis, [(i, i ^ flip) for i in range(count)])]
    psum x1 -> x0, waiting for transfers between devices: 39.8 us -> none  [on_device(): grad_tokens = lax.psum(partial_in.astype(jnp.bfloat16), 'row')]
    pallas_call x5 -> x16, Pallas kernels: 36.3 us -> 58 us  [the longest x8 21.7 us: input_grad(): pl.pallas_call(functools.partial(input_grad_kernel, width=width), grid_sp...]
    ppermute x0 -> x12, starting transfers between devices: none -> 19.6 us  [the longest x4 11.7 us: sum_along_row(): lax.ppermute(value, 'row', [(i, i + 1), (last - i, last - i - 1)])]
    all_gather x1 -> x0, blocking collectives: 9.49 us -> none  [on_device(): grad_taps = lax.all_gather(own_grad_taps, both, axis=1, tiled=True)]
    ppermute x9 -> x17, starting transfers between devices: 7.69 us -> 14.8 us  [swap(): return lax.ppermute(value, axis, [(i, i ^ flip) for i in range(count)])]
    all_to_all x1, waiting for transfers between devices: 11.1 us -> 6.16 us  [on_device(): up = lax.all_to_all(upstream, both, split_axis=1, concat_axis=0, tiled=True)]
  transfers between devices with their start and end apart: 12 -> 31, of which waited for: 6 -> 14; matrix products, arithmetic and copies ran while one was open for 2% -> 5% of each run, Pallas kernels for 14% -> 25%
where the time goes in v2:
time: 219 us; the launch traced here: 218 us
  waiting for transfers between devices  88.8 us (41%)
  Pallas kernels  60.5 us (28%)
  starting transfers between devices  42.1 us (19%)
  local copies, waits for them, and re-layouts  18.5 us (8%)
  other arithmetic  6.64 us (3%)
    ppermute x4, waiting for transfers between devices, sum_along_row(): outer = lax.ppermute(value, 'row', [(i + 1, i), (last - i - 1, last - i)])  33.6 us
    ppermute x17, waiting for transfers between devices, swap(): return lax.ppermute(value, axis, [(i, i ^ flip) for i in range(count)])  32 us
    pallas_call x8, Pallas kernels, input_grad(): pl.pallas_call(functools.partial(input_grad_kernel, width=width), grid_sp...  21.7 us
    pallas_call x4, Pallas kernels, weight_grad(): pl.pallas_call(functools.partial(weight_grad_kernel, groups=groups, wide=...  20.6 us
    ppermute x4, waiting for transfers between devices, sum_along_row(): lax.ppermute(value, 'row', [(i, i + 1), (last - i, last - i - 1)])  17 us
    ppermute x17, starting transfers between devices, swap(): return lax.ppermute(value, axis, [(i, i ^ flip) for i in range(count)])  14.8 us
    pallas_call x2, Pallas kernels, project(): pl.pallas_call(functools.partial(project_kernel, pieces=len(xs), count=co...  11.9 us
    ppermute x4, starting transfers between devices, sum_along_row(): lax.ppermute(value, 'row', [(i, i + 1), (last - i, last - i - 1)])  11.7 us
  transfers between devices with their start and end apart: 31, of which 14 were waited for; matrix products, arithmetic and copies ran while one was open for 5% of the time, Pallas kernels for 25%

profile of v2, /device:TPU:0, one launch (start us, length us, event | category | flops | bytes accessed | tf_op | source)
XLA Modules:
  0.0 217.8 jit_solution(123909254285911224)
XLA Ops:
  0.7 2.1 fusion
  2.8 3.0 %collective-permute-start.2 = (bf16[128,2048]{1,0:T(8,128)(2,1)S(1)}, bf16[128,2048]{1,0:T(8,128)(2,1)S(1)}, u32[]{:S(2)}, u32[]{:S(2)}) collective-permute-start(bf16[128,2048]{1,0:T(8,128)(2,1)S(1)} %get-tuple-element.25), channel_id=1, source_target_pairs={{0,4},{4,0},{1,5},{5,1},{2,6},{6,2},{3,7},{7,3},{8,12},{12,8},{9,1... | collective-permute-start | bytes 1572872 | tf_op jit(solution)/shard_map/ppermute | solution.py:19
  5.8 12.7 %collective-permute-done.2.refs_0_ = bf16[128,2048]{1,0:T(8,128)(2,1)S(1)} collective-permute-done((bf16[128,2048]{1,0:T(8,128)(2,1)S(1)}, bf16[128,2048]{1,0:T(8,128)(2,1)S(1)}, u32[]{:S(2)}, u32[]{:S(2)}) %collective-permute-start.2) | collective-permute-done | bytes 524320 | tf_op jit(solution)/shard_map/ppermute | solution.py:19
  18.5 2.1 collective-permute-start.3
  21.4 3.7 %all-to-all-start = ((bf16[96,8,128]{2,0,1:T(8,128)(2,1)}), bf16[96,8,128]{2,0,1:T(8,128)(2,1)S(1)}, u32[]{:S(2)}, u32[]{:S(2)}) async-start(bf16[96,8,128]{2,0,1:T(8,128)(2,1)} %copy_bitcast_fusion.1), calls=%async_computation | async-start | bytes 393216 | tf_op jit(solution)/shard_map/all_to_all | solution.py:359
  25.2 6.2 %all-to-all-done = bf16[96,8,128]{2,0,1:T(8,128)(2,1)S(1)} async-done(((bf16[96,8,128]{2,0,1:T(8,128)(2,1)}), bf16[96,8,128]{2,0,1:T(8,128)(2,1)S(1)}, u32[]{:S(2)}, u32[]{:S(2)}) %all-to-all-start) | async-done | bytes 196640 | tf_op jit(solution)/shard_map/all_to_all | solution.py:359
  31.3 1.4 copy-done.1
  32.7 5.9 %project.2 = (bf16[2,3,384,128]{3,2,1,0:T(8,128)(2,1)S(1)}, bf16[2,3,384,128]{3,2,1,0:T(8,128)(2,1)S(1)}) custom-call(s32[3]{0:T(128)S(1)} %pad_add_fusion.place, bf16[384,2048]{1,0:T(8,128)(2,1)S(1)} %copy-done.1, bf16[3,512,2048]{2,1,0:T(8,128)(2,1)} %bitcast.22), custom_call_target="tpu_custom_call" | custom-call | flops 2415919104 | bytes 9043968 | tf_op jit(solution)/shard_map/project/pallas_call | solution.py:75
  38.8 6.0 %project.3 = (bf16[2,3,384,128]{3,2,1,0:T(8,128)(2,1)S(1)}, bf16[2,3,384,128]{3,2,1,0:T(8,128)(2,1)S(1)}, bf16[384,2048]{1,0:T(8,128)(2,1)S(1)}) custom-call(s32[3]{0:T(128)S(1)} %pad_add_fusion.place, bf16[128,2048]{1,0:T(8,128)(2,1)S(1)} %collective-permute-done.2.refs_0_, bf16[128,2048]{1,0:T(8,128)(2,1)S(1)} %collective-permute-done.3.refs_1_, ...), custom_call_target="tpu_custom_call" | custom-call | flops 2415919104 | bytes 9043968 | tf_op jit(solution)/shard_map/project/pallas_call | solution.py:75
  45.4 0.9 add_convert_fusion.13
  46.3 1.4 collective-permute-start.1
  47.7 0.9 add_convert_fusion.12
  48.7 0.8 copy-done.7
  49.5 0.7 collective-permute-start.6
  51.0 0.8 reshape.26.taps_ref
  51.8 4.7 %collective-permute-done.1.refs_2_ = bf16[1,3,384,128]{3,2,1,0:T(8,128)(2,1)} collective-permute-done((bf16[1,3,384,128]{3,2,1,0:T(8,128)(2,1)}, bf16[1,3,384,128]{3,2,1,0:T(8,128)(2,1)}, u32[]{:S(2)}, u32[]{:S(2)}) %collective-permute-start.1) | collective-permute-done | bytes 294944 | tf_op jit(solution)/shard_map/ppermute | solution.py:19
  56.5 5.4 %collective-permute-done.6.refs_5_ = bf16[1,3,384,128]{3,2,1,0:T(8,128)(2,1)} collective-permute-done((bf16[1,3,384,128]{3,2,1,0:T(8,128)(2,1)}, bf16[1,3,384,128]{3,2,1,0:T(8,128)(2,1)}, u32[]{:S(2)}, u32[]{:S(2)}) %collective-permute-start.6) | collective-permute-done | bytes 294944 | tf_op jit(solution)/shard_map/ppermute | solution.py:19
  61.9 1.1 copy-done.4
  62.9 1.1 copy-done.6
  64.0 1.1 copy-done.8
  65.1 1.1 copy-done.10
  66.1 2.6 %middle.1 = (bf16[3,384,128]{2,1,0:T(8,128)(2,1)S(1)}, bf16[3,384,128]{2,1,0:T(8,128)(2,1)S(1)}, bf16[8,128,128]{2,1,0:T(8,128)(2,1)S(1)}) custom-call(s32[3]{0:T(128)S(1)} %pad_add_fusion.place, f32[7,128]{1,0:T(8,128)S(1)} %reshape.26.taps_ref, bf16[768,128]{1,0:T(8,128)(2,1)S(1)} %bitcast.21, bf16[2,3,384,128]{3,2,1,0:T(8,128)(2,1)S(1)} %copy-done.4, ...), custom_call_target="tpu_custom_call" | custom-call | flops 5898240 | bytes 2752512 | tf_op jit(solution)/shard_map/middle/pallas_call | solution.py:164
  70.8 4.0 %all-to-all-start.1 = ((bf16[8,128,128]{2,1,0:T(8,128)(2,1)}), bf16[8,128,128]{2,1,0:T(8,128)(2,1)}, u32[]{:S(2)}, u32[]{:S(2)}) async-start(bf16[8,128,128]{2,1,0:T(8,128)(2,1)} %copy-done.17), calls=%async_computation.1 | async-start | bytes 524288 | tf_op jit(solution)/shard_map/all_to_all | solution.py:395
  75.2 1.7 collective-permute-start.11
  77.3 1.0 copy-done.12
  78.3 1.0 copy-done.15
  79.2 4.4 %weight_grad.4.refs_0_ = f32[3,512,2048]{2,1,0:T(8,128)} custom-call(s32[3]{0:T(128)S(1)} %pad_add_fusion.place, bf16[3,384,128]{2,1,0:T(8,128)(2,1)S(1)} %copy-done.12, bf16[3,384,128]{2,1,0:T(8,128)(2,1)S(1)} %copy-done.15, bf16[384,2048]{1,0:T(8,128)(2,1)S(1)} %copy-done.2, bf16[384,2048]{1,0:T(8,128)(2,1)S(1)} %get-tuple-element.23.refs_3_.refs_4_), custom_call_target="tpu_custom_call" | custom-call | flops 1207959552 | bytes 6881280 | tf_op jit(solution)/shard_map/weight_grad/pallas_call | solution.py:294
  83.7 1.6 copy_bitcast_fusion
  85.3 0.8 slice_convert_fusion
  86.1 1.1 reshape.32
  87.2 1.3 reduce_sum.9
  89.5 4.0 %collective-permute-done.8.refs_2_.refs_1_ = bf16[3,384,128]{2,1,0:T(8,128)(2,1)} collective-permute-done((bf16[3,384,128]{2,1,0:T(8,128)(2,1)}, bf16[3,384,128]{2,1,0:T(8,128)(2,1)}, u32[]{:S(2)}, u32[]{:S(2)}) %collective-permute-start.8) | collective-permute-done | bytes 294944 | tf_op jit(solution)/shard_map/ppermute | solution.py:19
  93.5 5.4 %weight_grad.5.refs_0_ = f32[3,512,2048]{2,1,0:T(8,128)} custom-call(s32[3]{0:T(128)S(1)} %pad_add_fusion.place, f32[3,512,2048]{2,1,0:T(8,128)} %weight_grad.4.refs_0_, bf16[3,384,128]{2,1,0:T(8,128)(2,1)} %collective-permute-done.7.refs_1_, bf16[3,384,128]{2,1,0:T(8,128)(2,1)} %collective-permute-done.10.refs_1_.refs_2_, ...), custom_call_target="tpu_custom_call", output_to_operand_aliasing={{}: (1, {})} | custom-call | flops 1207959552 | bytes 6881280 | tf_op jit(solution)/shard_map/weight_grad/pallas_call | solution.py:294
  99.0 5.4 %weight_grad.6.refs_0_ = f32[3,512,2048]{2,1,0:T(8,128)} custom-call(s32[3]{0:T(128)S(1)} %pad_add_fusion.place, f32[3,512,2048]{2,1,0:T(8,128)} %weight_grad.5.refs_0_, bf16[3,384,128]{2,1,0:T(8,128)(2,1)} %collective-permute-done.8.refs_2_.refs_1_, bf16[3,384,128]{2,1,0:T(8,128)(2,1)} %collective-permute-done.11.refs_2_, ...), custom_call_target="tpu_custom_call", output_to_operand_aliasing={{}: (1, {})} | custom-call | flops 1207959552 | bytes 6881280 | tf_op jit(solution)/shard_map/weight_grad/pallas_call | solution.py:294
  104.4 1.9 assemble.3.refs_0_
  106.3 2.7 %input_grad.9 = bf16[384,512]{1,0:T(8,128)(2,1)S(1)} custom-call(s32[3]{0:T(128)S(1)} %pad_add_fusion.place, bf16[3,384,512]{2,1,0:T(8,128)(2,1)S(1)} %assemble.3.refs_0_, bf16[3,512,2048]{2,1,0:T(8,128)(2,1)} %bitcast.24), custom_call_target="tpu_custom_call" | custom-call | flops 603979776 | bytes 3145728 | tf_op jit(solution)/shard_map/input_grad/pallas_call | solution.py:232
  109.0 2.7 %input_grad.11 = bf16[384,512]{1,0:T(8,128)(2,1)S(1)} custom-call(s32[3]{0:T(128)S(1)} %pad_add_fusion.place, bf16[3,384,512]{2,1,0:T(8,128)(2,1)S(1)} %assemble.3.refs_0_, bf16[3,512,2048]{2,1,0:T(8,128)(2,1)} %bitcast.25), custom_call_target="tpu_custom_call" | custom-call | flops 603979776 | bytes 3145728 | tf_op jit(solution)/shard_map/input_grad/pallas_call | solution.py:232
  111.8 1.8 assemble.2.refs_0_
  113.6 2.7 %input_grad.8 = bf16[384,512]{1,0:T(8,128)(2,1)S(1)} custom-call(s32[3]{0:T(128)S(1)} %pad_add_fusion.place, bf16[3,384,512]{2,1,0:T(8,128)(2,1)S(1)} %assemble.2.refs_0_, bf16[3,512,2048]{2,1,0:T(8,128)(2,1)} %bitcast.26), custom_call_target="tpu_custom_call" | custom-call | flops 603979776 | bytes 3145728 | tf_op jit(solution)/shard_map/input_grad/pallas_call | solution.py:232
  116.3 1.6 collective-permute-start.13
  118.4 2.7 %input_grad.10 = bf16[384,512]{1,0:T(8,128)(2,1)S(1)} custom-call(s32[3]{0:T(128)S(1)} %pad_add_fusion.place, bf16[3,384,512]{2,1,0:T(8,128)(2,1)S(1)} %assemble.2.refs_0_, bf16[3,512,2048]{2,1,0:T(8,128)(2,1)} %bitcast.27), custom_call_target="tpu_custom_call" | custom-call | flops 603979776 | bytes 3145728 | tf_op jit(solution)/shard_map/input_grad/pallas_call | solution.py:232
  121.1 2.7 %input_grad.12 = bf16[384,512]{1,0:T(8,128)(2,1)S(1)} custom-call(s32[3]{0:T(128)S(1)} %pad_add_fusion.place, bf16[3,384,512]{2,1,0:T(8,128)(2,1)S(1)} %assemble.2.refs_0_, bf16[3,512,2048]{2,1,0:T(8,128)(2,1)} %bitcast.28), custom_call_target="tpu_custom_call" | custom-call | flops 603979776 | bytes 3145728 | tf_op jit(solution)/shard_map/input_grad/pallas_call | solution.py:232
  123.8 2.7 %input_grad.13 = bf16[384,512]{1,0:T(8,128)(2,1)S(1)} custom-call(s32[3]{0:T(128)S(1)} %pad_add_fusion.place, bf16[3,384,512]{2,1,0:T(8,128)(2,1)S(1)} %assemble.3.refs_0_, bf16[3,512,2048]{2,1,0:T(8,128)(2,1)} %bitcast.29), custom_call_target="tpu_custom_call" | custom-call | flops 603979776 | bytes 3145728 | tf_op jit(solution)/shard_map/input_grad/pallas_call | solution.py:232
  126.5 2.7 %input_grad.14 = bf16[384,512]{1,0:T(8,128)(2,1)S(1)} custom-call(s32[3]{0:T(128)S(1)} %pad_add_fusion.place, bf16[3,384,512]{2,1,0:T(8,128)(2,1)S(1)} %assemble.2.refs_0_, bf16[3,512,2048]{2,1,0:T(8,128)(2,1)} %bitcast.30), custom_call_target="tpu_custom_call" | custom-call | flops 603979776 | bytes 3145728 | tf_op jit(solution)/shard_map/input_grad/pallas_call | solution.py:232
  129.3 2.7 %input_grad.15 = bf16[384,512]{1,0:T(8,128)(2,1)S(1)} custom-call(s32[3]{0:T(128)S(1)} %pad_add_fusion.place, bf16[3,384,512]{2,1,0:T(8,128)(2,1)S(1)} %assemble.3.refs_0_, bf16[3,512,2048]{2,1,0:T(8,128)(2,1)} %bitcast.31), custom_call_target="tpu_custom_call" | custom-call | flops 603979776 | bytes 3145728 | tf_op jit(solution)/shard_map/input_grad/pallas_call | solution.py:232
  132.0 1.6 collective-permute-start.21
  134.1 5.3 %weight_grad.7 = f32[3,512,2048]{2,1,0:T(8,128)} custom-call(s32[3]{0:T(128)S(1)} %pad_add_fusion.place, f32[3,512,2048]{2,1,0:T(8,128)} %weight_grad.6.refs_0_, bf16[3,384,128]{2,1,0:T(8,128)(2,1)S(1)} %collective-permute-done.9.refs_3_.refs_1_, bf16[3,384,128]{2,1,0:T(8,128)(2,1)} %collective-permute-done.12.refs_3_.refs_2_, ...), custom_call_target="tpu_custom_call", output_to_operand_aliasing={{}: (1, {})} | custom-call | flops 1207959552 | bytes 6881280 | tf_op jit(solution)/shard_map/weight_grad/pallas_call | solution.py:294
  139.5 3.5 %collective-permute-start.14 = (bf16[384,512]{1,0:T(8,128)(2,1)S(1)}, bf16[384,512]{1,0:T(8,128)(2,1)S(1)}, u32[]{:S(2)}, u32[]{:S(2)}) collective-permute-start(bf16[384,512]{1,0:T(8,128)(2,1)S(1)} %add_convert_fusion.11), channel_id=1, source_target_pairs={{0,8},{24,16},{1,9},{25,17},{2,10},{26,18},{3,11},{27,19},{4,12},{... | collective-permute-start | bytes 1179656 | tf_op jit(solution)/shard_map/ppermute | solution.py:329
  143.1 1.3 collective-permute-start.18
  145.2 3.5 %collective-permute-start.22 = (bf16[384,512]{1,0:T(8,128)(2,1)S(1)}, bf16[384,512]{1,0:T(8,128)(2,1)S(1)}, u32[]{:S(2)}, u32[]{:S(2)}) collective-permute-start(bf16[384,512]{1,0:T(8,128)(2,1)S(1)} %add_convert_fusion.5), channel_id=1, source_target_pairs={{0,8},{24,16},{1,9},{25,17},{2,10},{26,18},{3,11},{27,19},{4,12},{... | collective-permute-start | bytes 1179656 | tf_op jit(solution)/shard_map/ppermute | solution.py:329
  148.7 4.5 %collective-permute-done.25 = bf16[384,512]{1,0:T(8,128)(2,1)S(1)} collective-permute-done((bf16[384,512]{1,0:T(8,128)(2,1)S(1)}, bf16[384,512]{1,0:T(8,128)(2,1)S(1)}, u32[]{:S(2)}, u32[]{:S(2)}) %collective-permute-start.25) | collective-permute-done | bytes 393248 | tf_op jit(solution)/shard_map/ppermute | solution.py:19
  153.2 3.4 %collective-permute-start.26 = (bf16[384,512]{1,0:T(8,128)(2,1)S(1)}, bf16[384,512]{1,0:T(8,128)(2,1)S(1)}, u32[]{:S(2)}, u32[]{:S(2)}) collective-permute-start(bf16[384,512]{1,0:T(8,128)(2,1)S(1)} %add_convert_fusion.2), channel_id=1, source_target_pairs={{0,8},{24,16},{1,9},{25,17},{2,10},{26,18},{3,11},{27,19},{4,12},{... | collective-permute-start | bytes 1179656 | tf_op jit(solution)/shard_map/ppermute | solution.py:329
  157.5 3.4 %collective-permute-done.18 = bf16[384,512]{1,0:T(8,128)(2,1)S(1)} collective-permute-done((bf16[384,512]{1,0:T(8,128)(2,1)S(1)}, bf16[384,512]{1,0:T(8,128)(2,1)S(1)}, u32[]{:S(2)}, u32[]{:S(2)}) %collective-permute-start.18) | collective-permute-done | bytes 393248 | tf_op jit(solution)/shard_map/ppermute | solution.py:329
  161.7 7.6 %collective-permute-done.22 = bf16[384,512]{1,0:T(8,128)(2,1)S(1)} collective-permute-done((bf16[384,512]{1,0:T(8,128)(2,1)S(1)}, bf16[384,512]{1,0:T(8,128)(2,1)S(1)}, u32[]{:S(2)}, u32[]{:S(2)}) %collective-permute-start.22) | collective-permute-done | bytes 393248 | tf_op jit(solution)/shard_map/ppermute | solution.py:329
  170.2 6.0 %collective-permute-done.26 = bf16[384,512]{1,0:T(8,128)(2,1)S(1)} collective-permute-done((bf16[384,512]{1,0:T(8,128)(2,1)S(1)}, bf16[384,512]{1,0:T(8,128)(2,1)S(1)}, u32[]{:S(2)}, u32[]{:S(2)}) %collective-permute-start.26) | collective-permute-done | bytes 393248 | tf_op jit(solution)/shard_map/ppermute | solution.py:329
  177.0 1.3 collective-permute-start.16
  178.5 1.3 collective-permute-start.20
  179.9 1.3 collective-permute-start.24
  181.3 1.3 collective-permute-start.28
  182.6 11.1 %collective-permute-done.16 = bf16[384,512]{1,0:T(8,128)(2,1)S(1)} collective-permute-done((bf16[384,512]{1,0:T(8,128)(2,1)S(1)}, bf16[384,512]{1,0:T(8,128)(2,1)S(1)}, u32[]{:S(2)}, u32[]{:S(2)}) %collective-permute-start.16) | collective-permute-done | bytes 393248 | tf_op jit(solution)/shard_map/ppermute | solution.py:332
  193.7 8.4 %collective-permute-done.20 = bf16[384,512]{1,0:T(8,128)(2,1)S(1)} collective-permute-done((bf16[384,512]{1,0:T(8,128)(2,1)S(1)}, bf16[384,512]{1,0:T(8,128)(2,1)S(1)}, u32[]{:S(2)}, u32[]{:S(2)}) %collective-permute-start.20) | collective-permute-done | bytes 393248 | tf_op jit(solution)/shard_map/ppermute | solution.py:332
  202.2 8.4 %collective-permute-done.24 = bf16[384,512]{1,0:T(8,128)(2,1)S(1)} collective-permute-done((bf16[384,512]{1,0:T(8,128)(2,1)S(1)}, bf16[384,512]{1,0:T(8,128)(2,1)S(1)}, u32[]{:S(2)}, u32[]{:S(2)}) %collective-permute-start.24) | collective-permute-done | bytes 393248 | tf_op jit(solution)/shard_map/ppermute | solution.py:332
  210.6 5.8 %collective-permute-done.28 = bf16[384,512]{1,0:T(8,128)(2,1)S(1)} collective-permute-done((bf16[384,512]{1,0:T(8,128)(2,1)S(1)}, bf16[384,512]{1,0:T(8,128)(2,1)S(1)}, u32[]{:S(2)}, u32[]{:S(2)}) %collective-permute-start.28) | collective-permute-done | bytes 393248 | tf_op jit(solution)/shard_map/ppermute | solution.py:332
  216.4 1.3 pad_maximum_fusion
  (85 shorter events, 12.0 us)
Async XLA Ops:
  0.6 20.0 %copy-start = (bf16[96,1024]{1,0:T(8,128)(2,1)S(1)}, bf16[96,1024]{1,0:T(8,128)(2,1)}, u32[]{:S(2)}) copy-start(bf16[96,1024]{1,0:T(8,128)(2,1)} %param.7) | copy-start | bytes 589828
  2.8 15.7 %collective-permute-start.2 = (bf16[128,2048]{1,0:T(8,128)(2,1)S(1)}, bf16[128,2048]{1,0:T(8,128)(2,1)S(1)}, u32[]{:S(2)}, u32[]{:S(2)}) collective-permute-start(bf16[128,2048]{1,0:T(8,128)(2,1)S(1)} %get-tuple-element.25), channel_id=1, source_target_pairs={{0,4},{4,0},{1,5},{5,1},{2,6},{6,2},{3,7},{7,3},{8,12},{12,8},{9,1... | collective-permute-start | bytes 1572872 | tf_op jit(solution)/shard_map/ppermute | solution.py:19
  5.8 33.0 %collective-permute-start.4 = (bf16[128,2048]{1,0:T(8,128)(2,1)}, bf16[128,2048]{1,0:T(8,128)(2,1)S(1)}, u32[]{:S(2)}, u32[]{:S(2)}) collective-permute-start(bf16[128,2048]{1,0:T(8,128)(2,1)} %get-tuple-element.24), channel_id=1, source_target_pairs={{0,4},{4,0},{1,5},{5,1},{2,6},{6,2},{3,7},{7,3},{8,12},{12,8},{9,1... | collective-permute-start | bytes 1572872 | tf_op jit(solution)/shard_map/ppermute | solution.py:19
  18.5 20.2 %collective-permute-start.3 = (bf16[128,2048]{1,0:T(8,128)(2,1)S(1)}, bf16[128,2048]{1,0:T(8,128)(2,1)S(1)}, u32[]{:S(2)}, u32[]{:S(2)}) collective-permute-start(bf16[128,2048]{1,0:T(8,128)(2,1)S(1)} %collective-permute-done.2.refs_0_), channel_id=1, source_target_pairs={{0,8},{8,0},{16,24},{24,16},{1,9},{9,1},{17,25},{25,17},{2,10},{10... | collective-permute-start | bytes 1572872 | tf_op jit(solution)/shard_map/ppermute | solution.py:19
  21.4 10.0 %all-to-all-start = ((bf16[96,8,128]{2,0,1:T(8,128)(2,1)}), bf16[96,8,128]{2,0,1:T(8,128)(2,1)S(1)}, u32[]{:S(2)}, u32[]{:S(2)}) async-start(bf16[96,8,128]{2,0,1:T(8,128)(2,1)} %copy_bitcast_fusion.1), calls=%async_computation | async-start | bytes 393216 | tf_op jit(solution)/shard_map/all_to_all | solution.py:359
  31.3 1.4 copy-start.1
  38.6 6.7 %copy-start.3 = (bf16[2,3,384,128]{3,2,1,0:T(8,128)(2,1)}, bf16[2,3,384,128]{3,2,1,0:T(8,128)(2,1)S(1)}, u32[]{:S(2)}) copy-start(bf16[2,3,384,128]{3,2,1,0:T(8,128)(2,1)S(1)} %get-tuple-element.16.refs_0_) | copy-start | bytes 1769476
  38.7 11.6 %copy-start.18 = (f32[7,64]{1,0:T(8,128)S(1)}, f32[7,64]{1,0:T(8,128)}, u32[]{:S(2)}) copy-start(f32[7,64]{1,0:T(8,128)} %param.6) | copy-start | bytes 5380
  38.7 6.7 %collective-permute-start = (bf16[2,3,384,128]{3,2,1,0:T(8,128)(2,1)S(1)}, bf16[2,3,384,128]{3,2,1,0:T(8,128)(2,1)S(1)}, u32[]{:S(2)}, u32[]{:S(2)}) collective-permute-start(bf16[2,3,384,128]{3,2,1,0:T(8,128)(2,1)S(1)} %get-tuple-element.17), channel_id=1, source_target_pairs={{0,1},{1,0},{2,3},{3,2},{4,5},{5,4},{6,7},{7,6},{8,9},{9,8},{10,11... | collective-permute-start | bytes 1769480 | tf_op jit(solution)/shard_map/ppermute | solution.py:19
  44.8 32.5 %copy-start.2 = (bf16[384,2048]{1,0:T(8,128)(2,1)S(1)}, bf16[384,2048]{1,0:T(8,128)(2,1)}, u32[]{:S(2)}) copy-start(bf16[384,2048]{1,0:T(8,128)(2,1)} %refs_3_.2) | copy-start | bytes 4718596
  44.8 2.9 %collective-permute-start.5 = (bf16[2,3,384,128]{3,2,1,0:T(8,128)(2,1)S(1)}, bf16[2,3,384,128]{3,2,1,0:T(8,128)(2,1)S(1)}, u32[]{:S(2)}, u32[]{:S(2)}) collective-permute-start(bf16[2,3,384,128]{3,2,1,0:T(8,128)(2,1)S(1)} %get-tuple-element.19), channel_id=1, source_target_pairs={{0,1},{1,0},{2,3},{3,2},{4,5},{5,4},{6,7},{7,6},{8,9},{9,8},{10,11... | collective-permute-start | bytes 1769480 | tf_op jit(solution)/shard_map/ppermute | solution.py:19
  45.4 0.9 copy-start.5
  46.3 10.2 %collective-permute-start.1 = (bf16[1,3,384,128]{3,2,1,0:T(8,128)(2,1)}, bf16[1,3,384,128]{3,2,1,0:T(8,128)(2,1)}, u32[]{:S(2)}, u32[]{:S(2)}) collective-permute-start(bf16[1,3,384,128]{3,2,1,0:T(8,128)(2,1)} %add_convert_fusion.13), channel_id=1, source_target_pairs={{0,2},{1,3},{2,0},{3,1},{4,6},{5,7},{6,4},{7,5},{8,10},{9,11},{10,... | collective-permute-start | bytes 884744 | tf_op jit(solution)/shard_map/ppermute | solution.py:19
  47.7 0.9 copy-start.9
  48.6 0.8 copy-start.7
  49.5 12.4 %collective-permute-start.6 = (bf16[1,3,384,128]{3,2,1,0:T(8,128)(2,1)}, bf16[1,3,384,128]{3,2,1,0:T(8,128)(2,1)}, u32[]{:S(2)}, u32[]{:S(2)}) collective-permute-start(bf16[1,3,384,128]{3,2,1,0:T(8,128)(2,1)} %add_convert_fusion.12), channel_id=1, source_target_pairs={{0,2},{1,3},{2,0},{3,1},{4,6},{5,7},{6,4},{7,5},{8,10},{9,11},{10,... | collective-permute-start | bytes 884744 | tf_op jit(solution)/shard_map/ppermute | solution.py:19
  61.9 1.1 copy-start.4
  62.9 1.1 copy-start.6
  64.0 1.1 copy-start.8
  65.0 1.1 copy-start.10
  68.7 0.7 copy-start.11
  69.4 0.7 copy-start.14
  70.1 0.7 copy-start.17
  70.8 12.9 %all-to-all-start.1 = ((bf16[8,128,128]{2,1,0:T(8,128)(2,1)}), bf16[8,128,128]{2,1,0:T(8,128)(2,1)}, u32[]{:S(2)}, u32[]{:S(2)}) async-start(bf16[8,128,128]{2,1,0:T(8,128)(2,1)} %copy-done.17), calls=%async_computation.1 | async-start | bytes 524288 | tf_op jit(solution)/shard_map/all_to_all | solution.py:395
  74.9 18.7 %collective-permute-start.10 = (bf16[3,384,128]{2,1,0:T(8,128)(2,1)}, bf16[3,384,128]{2,1,0:T(8,128)(2,1)}, u32[]{:S(2)}, u32[]{:S(2)}) collective-permute-start(bf16[3,384,128]{2,1,0:T(8,128)(2,1)} %copy-done.14), channel_id=1, source_target_pairs={{0,1},{1,0},{2,3},{3,2},{4,5},{5,4},{6,7},{7,6},{8,9},{9,8},{10,11... | collective-permute-start | bytes 884744 | tf_op jit(solution)/shard_map/ppermute | solution.py:19
  75.2 13.3 %collective-permute-start.11 = (bf16[3,384,128]{2,1,0:T(8,128)(2,1)}, bf16[3,384,128]{2,1,0:T(8,128)(2,1)}, u32[]{:S(2)}, u32[]{:S(2)}) collective-permute-start(bf16[3,384,128]{2,1,0:T(8,128)(2,1)} %copy-done.14), channel_id=1, source_target_pairs={{0,2},{1,3},{2,0},{3,1},{4,6},{5,7},{6,4},{7,5},{8,10},{9,11},{10,... | collective-permute-start | bytes 884744 | tf_op jit(solution)/shard_map/ppermute | solution.py:19
  76.9 16.6 %collective-permute-start.7 = (bf16[3,384,128]{2,1,0:T(8,128)(2,1)}, bf16[3,384,128]{2,1,0:T(8,128)(2,1)}, u32[]{:S(2)}, u32[]{:S(2)}) collective-permute-start(bf16[3,384,128]{2,1,0:T(8,128)(2,1)} %copy-done.11), channel_id=1, source_target_pairs={{0,1},{1,0},{2,3},{3,2},{4,5},{5,4},{6,7},{7,6},{8,9},{9,8},{10,11... | collective-permute-start | bytes 884744 | tf_op jit(solution)/shard_map/ppermute | solution.py:19
  77.0 16.5 %collective-permute-start.8 = (bf16[3,384,128]{2,1,0:T(8,128)(2,1)}, bf16[3,384,128]{2,1,0:T(8,128)(2,1)}, u32[]{:S(2)}, u32[]{:S(2)}) collective-permute-start(bf16[3,384,128]{2,1,0:T(8,128)(2,1)} %copy-done.11), channel_id=1, source_target_pairs={{0,2},{1,3},{2,0},{3,1},{4,6},{5,7},{6,4},{7,5},{8,10},{9,11},{10,... | collective-permute-start | bytes 884744 | tf_op jit(solution)/shard_map/ppermute | solution.py:19
  77.3 1.0 copy-start.12
  78.3 1.0 copy-start.15
  88.5 15.9 %collective-permute-start.12 = (bf16[3,384,128]{2,1,0:T(8,128)(2,1)}, bf16[3,384,128]{2,1,0:T(8,128)(2,1)}, u32[]{:S(2)}, u32[]{:S(2)}) collective-permute-start(bf16[3,384,128]{2,1,0:T(8,128)(2,1)} %collective-permute-done.11.refs_2_), channel_id=1, source_target_pairs={{0,1},{1,0},{2,3},{3,2},{4,5},{5,4},{6,7},{7,6},{8,9},{9,8},{10,11... | collective-permute-start | bytes 884744 | tf_op jit(solution)/shard_map/ppermute | solution.py:19
  93.5 18.2 %collective-permute-start.9 = (bf16[3,384,128]{2,1,0:T(8,128)(2,1)}, bf16[3,384,128]{2,1,0:T(8,128)(2,1)S(1)}, u32[]{:S(2)}, u32[]{:S(2)}) collective-permute-start(bf16[3,384,128]{2,1,0:T(8,128)(2,1)} %collective-permute-done.8.refs_2_.refs_1_), channel_id=1, source_target_pairs={{0,1},{1,0},{2,3},{3,2},{4,5},{5,4},{6,7},{7,6},{8,9},{9,8},{10,11... | collective-permute-start | bytes 884744 | tf_op jit(solution)/shard_map/ppermute | solution.py:19
  99.0 5.4 %copy-start.16 = (bf16[3,384,128]{2,1,0:T(8,128)(2,1)S(1)}, bf16[3,384,128]{2,1,0:T(8,128)(2,1)}, u32[]{:S(2)}) copy-start(bf16[3,384,128]{2,1,0:T(8,128)(2,1)} %copy-done.14) | copy-start | bytes 884740
  109.0 2.7 %copy-start.13 = (bf16[3,384,128]{2,1,0:T(8,128)(2,1)S(1)}, bf16[3,384,128]{2,1,0:T(8,128)(2,1)}, u32[]{:S(2)}) copy-start(bf16[3,384,128]{2,1,0:T(8,128)(2,1)} %copy-done.11) | copy-start | bytes 884740
  116.3 23.1 %collective-permute-start.13 = (bf16[384,512]{1,0:T(8,128)(2,1)S(1)}, bf16[384,512]{1,0:T(8,128)(2,1)S(1)}, u32[]{:S(2)}, u32[]{:S(2)}) collective-permute-start(bf16[384,512]{1,0:T(8,128)(2,1)S(1)} %input_grad.9), channel_id=1, source_target_pairs={{0,4},{4,0},{1,5},{5,1},{2,6},{6,2},{3,7},{7,3},{8,12},{12,8},{9,1... | collective-permute-start | bytes 1179656 | tf_op jit(solution)/shard_map/ppermute | solution.py:19
  117.8 25.2 %collective-permute-start.17 = (bf16[384,512]{1,0:T(8,128)(2,1)S(1)}, bf16[384,512]{1,0:T(8,128)(2,1)S(1)}, u32[]{:S(2)}, u32[]{:S(2)}) collective-permute-start(bf16[384,512]{1,0:T(8,128)(2,1)S(1)} %input_grad.11), channel_id=1, source_target_pairs={{0,4},{4,0},{1,5},{5,1},{2,6},{6,2},{3,7},{7,3},{8,12},{12,8},{9,1... | collective-permute-start | bytes 1179656 | tf_op jit(solution)/shard_map/ppermute | solution.py:19
  132.0 13.1 %collective-permute-start.21 = (bf16[384,512]{1,0:T(8,128)(2,1)S(1)}, bf16[384,512]{1,0:T(8,128)(2,1)S(1)}, u32[]{:S(2)}, u32[]{:S(2)}) collective-permute-start(bf16[384,512]{1,0:T(8,128)(2,1)S(1)} %input_grad.13), channel_id=1, source_target_pairs={{0,4},{4,0},{1,5},{5,1},{2,6},{6,2},{3,7},{7,3},{8,12},{12,8},{9,1... | collective-permute-start | bytes 1179656 | tf_op jit(solution)/shard_map/ppermute | solution.py:19
  133.5 19.6 %collective-permute-start.25 = (bf16[384,512]{1,0:T(8,128)(2,1)S(1)}, bf16[384,512]{1,0:T(8,128)(2,1)S(1)}, u32[]{:S(2)}, u32[]{:S(2)}) collective-permute-start(bf16[384,512]{1,0:T(8,128)(2,1)S(1)} %input_grad.15), channel_id=1, source_target_pairs={{0,4},{4,0},{1,5},{5,1},{2,6},{6,2},{3,7},{7,3},{8,12},{12,8},{9,1... | collective-permute-start | bytes 1179656 | tf_op jit(solution)/shard_map/ppermute | solution.py:19
  139.5 17.2 %collective-permute-start.14 = (bf16[384,512]{1,0:T(8,128)(2,1)S(1)}, bf16[384,512]{1,0:T(8,128)(2,1)S(1)}, u32[]{:S(2)}, u32[]{:S(2)}) collective-permute-start(bf16[384,512]{1,0:T(8,128)(2,1)S(1)} %add_convert_fusion.11), channel_id=1, source_target_pairs={{0,8},{24,16},{1,9},{25,17},{2,10},{26,18},{3,11},{27,19},{4,12},{... | collective-permute-start | bytes 1179656 | tf_op jit(solution)/shard_map/ppermute | solution.py:329
  143.1 17.8 %collective-permute-start.18 = (bf16[384,512]{1,0:T(8,128)(2,1)S(1)}, bf16[384,512]{1,0:T(8,128)(2,1)S(1)}, u32[]{:S(2)}, u32[]{:S(2)}) collective-permute-start(bf16[384,512]{1,0:T(8,128)(2,1)S(1)} %add_convert_fusion.8), channel_id=1, source_target_pairs={{0,8},{24,16},{1,9},{25,17},{2,10},{26,18},{3,11},{27,19},{4,12},{... | collective-permute-start | bytes 1179656 | tf_op jit(solution)/shard_map/ppermute | solution.py:329
  145.2 24.2 %collective-permute-start.22 = (bf16[384,512]{1,0:T(8,128)(2,1)S(1)}, bf16[384,512]{1,0:T(8,128)(2,1)S(1)}, u32[]{:S(2)}, u32[]{:S(2)}) collective-permute-start(bf16[384,512]{1,0:T(8,128)(2,1)S(1)} %add_convert_fusion.5), channel_id=1, source_target_pairs={{0,8},{24,16},{1,9},{25,17},{2,10},{26,18},{3,11},{27,19},{4,12},{... | collective-permute-start | bytes 1179656 | tf_op jit(solution)/shard_map/ppermute | solution.py:329
  153.2 22.9 %collective-permute-start.26 = (bf16[384,512]{1,0:T(8,128)(2,1)S(1)}, bf16[384,512]{1,0:T(8,128)(2,1)S(1)}, u32[]{:S(2)}, u32[]{:S(2)}) collective-permute-start(bf16[384,512]{1,0:T(8,128)(2,1)S(1)} %add_convert_fusion.2), channel_id=1, source_target_pairs={{0,8},{24,16},{1,9},{25,17},{2,10},{26,18},{3,11},{27,19},{4,12},{... | collective-permute-start | bytes 1179656 | tf_op jit(solution)/shard_map/ppermute | solution.py:329
  156.8 20.1 %collective-permute-start.15 = (bf16[384,512]{1,0:T(8,128)(2,1)S(1)}, bf16[384,512]{1,0:T(8,128)(2,1)S(1)}, u32[]{:S(2)}, u32[]{:S(2)}) collective-permute-start(bf16[384,512]{1,0:T(8,128)(2,1)S(1)} %add_convert_fusion.10), channel_id=1, source_target_pairs={{8,16},{16,8},{9,17},{17,9},{10,18},{18,10},{11,19},{19,11},{12,20... | collective-permute-start | bytes 1179656 | tf_op jit(solution)/shard_map/ppermute | solution.py:330
  161.0 17.3 %collective-permute-start.19 = (bf16[384,512]{1,0:T(8,128)(2,1)S(1)}, bf16[384,512]{1,0:T(8,128)(2,1)S(1)}, u32[]{:S(2)}, u32[]{:S(2)}) collective-permute-start(bf16[384,512]{1,0:T(8,128)(2,1)S(1)} %add_convert_fusion.7), channel_id=1, source_target_pairs={{8,16},{16,8},{9,17},{17,9},{10,18},{18,10},{11,19},{19,11},{12,20... | collective-permute-start | bytes 1179656 | tf_op jit(solution)/shard_map/ppermute | solution.py:330
  169.5 10.3 %collective-permute-start.23 = (bf16[384,512]{1,0:T(8,128)(2,1)S(1)}, bf16[384,512]{1,0:T(8,128)(2,1)S(1)}, u32[]{:S(2)}, u32[]{:S(2)}) collective-permute-start(bf16[384,512]{1,0:T(8,128)(2,1)S(1)} %add_convert_fusion.4), channel_id=1, source_target_pairs={{8,16},{16,8},{9,17},{17,9},{10,18},{18,10},{11,19},{19,11},{12,20... | collective-permute-start | bytes 1179656 | tf_op jit(solution)/shard_map/ppermute | solution.py:330
  176.2 4.9 %collective-permute-start.27 = (bf16[384,512]{1,0:T(8,128)(2,1)S(1)}, bf16[384,512]{1,0:T(8,128)(2,1)S(1)}, u32[]{:S(2)}, u32[]{:S(2)}) collective-permute-start(bf16[384,512]{1,0:T(8,128)(2,1)S(1)} %add_convert_fusion.1), channel_id=1, source_target_pairs={{8,16},{16,8},{9,17},{17,9},{10,18},{18,10},{11,19},{19,11},{12,20... | collective-permute-start | bytes 1179656 | tf_op jit(solution)/shard_map/ppermute | solution.py:330
  177.0 16.6 %collective-permute-start.16 = (bf16[384,512]{1,0:T(8,128)(2,1)S(1)}, bf16[384,512]{1,0:T(8,128)(2,1)S(1)}, u32[]{:S(2)}, u32[]{:S(2)}) collective-permute-start(bf16[384,512]{1,0:T(8,128)(2,1)S(1)} %add_convert_fusion.9), channel_id=1, source_target_pairs={{8,0},{16,24},{9,1},{17,25},{10,2},{18,26},{11,3},{19,27},{12,4},{... | collective-permute-start | bytes 1179656 | tf_op jit(solution)/shard_map/ppermute | solution.py:332
  178.5 23.6 %collective-permute-start.20 = (bf16[384,512]{1,0:T(8,128)(2,1)S(1)}, bf16[384,512]{1,0:T(8,128)(2,1)S(1)}, u32[]{:S(2)}, u32[]{:S(2)}) collective-permute-start(bf16[384,512]{1,0:T(8,128)(2,1)S(1)} %add_convert_fusion.6), channel_id=1, source_target_pairs={{8,0},{16,24},{9,1},{17,25},{10,2},{18,26},{11,3},{19,27},{12,4},{... | collective-permute-start | bytes 1179656 | tf_op jit(solution)/shard_map/ppermute | solution.py:332
  179.9 30.7 %collective-permute-start.24 = (bf16[384,512]{1,0:T(8,128)(2,1)S(1)}, bf16[384,512]{1,0:T(8,128)(2,1)S(1)}, u32[]{:S(2)}, u32[]{:S(2)}) collective-permute-start(bf16[384,512]{1,0:T(8,128)(2,1)S(1)} %add_convert_fusion.3), channel_id=1, source_target_pairs={{8,0},{16,24},{9,1},{17,25},{10,2},{18,26},{11,3},{19,27},{12,4},{... | collective-permute-start | bytes 1179656 | tf_op jit(solution)/shard_map/ppermute | solution.py:332
  181.3 35.1 %collective-permute-start.28 = (bf16[384,512]{1,0:T(8,128)(2,1)S(1)}, bf16[384,512]{1,0:T(8,128)(2,1)S(1)}, u32[]{:S(2)}, u32[]{:S(2)}) collective-permute-start(bf16[384,512]{1,0:T(8,128)(2,1)S(1)} %add_convert_fusion), channel_id=1, source_target_pairs={{8,0},{16,24},{9,1},{17,25},{10,2},{18,26},{11,3},{19,27},{12,4},{... | collective-permute-start | bytes 1179656 | tf_op jit(solution)/shard_map/ppermute | solution.py:332

commit v3 on v2

v3 whole, which is shorter than its diff:
```python
import functools

import jax
import jax.numpy as jnp
from jax import lax
from jax.experimental import pallas as pl
from jax.experimental.pallas import tpu as pltpu
from jax.sharding import PartitionSpec as P

GROUP = 16
KT = 7
PAD = 8
LANES = 128
MIB = 1024 * 1024
SMALL = pl.CostEstimate(flops=1, bytes_accessed=1, transcendentals=0)


def swap(value, axis, flip):
    count = lax.axis_size(axis)
    return lax.ppermute(value, axis, [(i, i ^ flip) for i in range(count)])


def after(value, *earlier):
    return lax.optimization_barrier((value, *earlier))[0]


def resident(shape, width):
    if width % LANES == 0:
        return pl.BlockSpec(memory_space=pltpu.VMEM)
    return pl.BlockSpec(tuple(shape), lambda *_: (0,) * len(shape))


def params(mib, width):
    return pltpu.CompilerParams(vmem_limit_bytes=(mib if width % LANES == 0 else 48) * MIB)


def project_kernel(place, *refs, pieces, count, width):
    x_refs = refs[:pieces]
    w_ref, keep_ref, send_ref = refs[pieces : pieces + 3]
    stream = pl.program_id(0)
    core = place[0] % 2
    if pieces == 1:
        x = x_refs[0][...]
    else:
        x_out = refs[pieces + 3]
        third = x_refs[0].shape[0]
        parity = place[2] % 2

        @pl.when(stream == 0)
        def _():
            x_out[pl.ds(pl.multiple_of(parity * third, third), third), :] = x_refs[0][...]
            x_out[pl.ds(pl.multiple_of((1 - parity) * third, third), third), :] = x_refs[1][...]
            x_out[2 * third :, :] = x_refs[2][...]

        x = x_out[...]
    nt = (((1,), (1,)), ((), ()))
    if width % LANES == 0:
        whole = lax.dot_general(x, w_ref[stream], nt, preferred_element_type=jnp.float32).astype(jnp.bfloat16)
        blocks = [whole[:, j * width : (j + 1) * width] for j in range(count)]
    else:
        blocks = [
            lax.dot_general(
                x, w_ref[0, j * width : (j + 1) * width, :], nt, preferred_element_type=jnp.float32
            ).astype(jnp.bfloat16)
            for j in range(count)
        ]
    for mine in range(2):

        @pl.when(core == mine)
        def _():
            for j in range(count):
                at = (j ^ place[0]) // 2
                if j % 2 == mine:
                    keep_ref[at, stream] = blocks[j]
                else:
                    send_ref[at, stream] = blocks[j]


def project(place, xs, w, count):
    tok, feat = sum(x.shape[0] for x in xs), xs[0].shape[1]
    streams, channels, _ = w.shape
    width = channels // count
    part = jax.ShapeDtypeStruct((count // 2, streams, tok, width), jnp.bfloat16)
    wide = width % LANES == 0
    spec = resident(part.shape, width)
    joined = len(xs) > 1
    outs = pl.pallas_call(
        functools.partial(project_kernel, pieces=len(xs), count=count, width=width),
        grid_spec=pltpu.PrefetchScalarGridSpec(
            num_scalar_prefetch=1,
            grid=(streams,),
            in_specs=[resident(x.shape, width) for x in xs]
            + [resident(w.shape, width) if wide else pl.BlockSpec((1, channels, feat), lambda s, _: (s, 0, 0))],
            out_specs=[spec, spec] + [resident((tok, feat), width)] * joined,
        ),
        out_shape=[part, part] + [jax.ShapeDtypeStruct((tok, feat), jnp.bfloat16)] * joined,
        compiler_params=params(24, width),
        cost_estimate=SMALL,
        name="project",
    )(place, *xs, w)
    return outs[0], outs[1], outs[2] if joined else xs[0]


def middle_kernel(place, taps_ref, up_ref, *refs, groups, terms, tile):
    part_refs = refs[: groups * terms]
    grad_refs = refs[groups * terms : groups * terms + groups]
    out_ref, q_s, k_s, v_s, mixed_s, gf_s, far_s = refs[groups * terms + groups :]
    col = place[1]
    tok = part_refs[0].shape[2]
    width = part_refs[0].shape[3]
    total = groups * tok
    mixed_s[0:PAD, :] = jnp.zeros((PAD, width), jnp.float32)
    gf_s[total : total + PAD, :] = jnp.zeros((PAD, width), jnp.float32)
    for k in range(groups):
        start = (col ^ k) * tok
        for i in range(tok // tile):
            inside = slice(i * tile, (i + 1) * tile)
            rows = pl.ds(pl.multiple_of(start + i * tile, tile), tile)
            streams = []
            for s in range(3):
                acc = None
                for ref in part_refs[k * terms : (k + 1) * terms]:
                    term = ref[0, s, inside, :].astype(jnp.float32)
                    acc = term if acc is None else acc + term
                streams.append(acc.astype(jnp.bfloat16).astype(jnp.float32))
            query, key, value = streams
            q_s[rows, :] = query
            k_s[rows, :] = key
            v_s[rows, :] = value
            mixed_s[pl.ds(pl.multiple_of(start + i * tile + PAD, PAD), tile), :] = key * value
            gf_s[rows, :] = up_ref[rows, :].astype(jnp.float32) * query
    taps = taps_ref[...]
    sums = [jnp.zeros((8, width), jnp.float32) for _ in range(KT)]
    for a in range(groups):
        for i in range(tok // tile):
            first = a * tok + i * tile
            rows = slice(first, first + tile)
            inside = slice(i * tile, (i + 1) * tile)
            gf = gf_s[rows, :]
            filtered = jnp.zeros((tile, width), jnp.float32)
            grad_mixed = jnp.zeros((tile, width), jnp.float32)
            for j in range(KT):
                shifted = mixed_s[first + PAD - j : first + PAD - j + tile, :]
                filtered = filtered + taps[j : j + 1, :] * shifted
                sums[j] = sums[j] + (gf * shifted).reshape(tile // 8, 8, width).sum(axis=0)
                grad_mixed = grad_mixed + taps[j : j + 1, :] * gf_s[first + j : first + j + tile, :]
            out_ref[first // tile, 0:tile, :] = (q_s[rows, :] * filtered).astype(jnp.bfloat16)
            at = col ^ a
            far_s[at, 0, inside, :] = (up_ref[rows, :].astype(jnp.float32) * filtered).astype(jnp.bfloat16)
            far_s[at, 1, inside, :] = (grad_mixed * v_s[rows, :]).astype(jnp.bfloat16)
            far_s[at, 2, inside, :] = (grad_mixed * k_s[rows, :]).astype(jnp.bfloat16)
    for k in range(groups):
        grad_refs[k][...] = far_s[k]
    rest = jnp.concatenate(
        [sums[j].sum(axis=0, keepdims=True) for j in range(KT)] + [jnp.zeros((1, width), jnp.float32)], axis=0
    )
    terms_of = []
    for _ in range(3):
        term = rest.astype(jnp.bfloat16).astype(jnp.float32)
        rest = rest - term
        terms_of.append(term)
    packed = jnp.concatenate(terms_of + [jnp.zeros((8, width), jnp.float32)], axis=0).astype(jnp.bfloat16)
    for i in range(out_ref.shape[0]):
        out_ref[i, tile : tile + 32, :] = packed


def middle(place, taps, up, parts, tile):
    groups, terms = len(parts), len(parts[0])
    _, _, tok, width = parts[0][0].shape
    total = groups * tok
    whole = lambda *shape: resident(shape, width)
    outs = pl.pallas_call(
        functools.partial(middle_kernel, groups=groups, terms=terms, tile=tile),
        grid_spec=pltpu.PrefetchScalarGridSpec(
            num_scalar_prefetch=1,
            grid=(1,),
            in_specs=[whole(KT, width), whole(total, width)]
            + [
                whole(1, 3, tok, width) if width % LANES == 0 else pl.BlockSpec((1, 3, tok, width), lambda *_: (0,) * 4)
            ]
            * (groups * terms),
            out_specs=[whole(3, tok, width)] * groups + [whole(total // tile, tile + 32, width)],
            scratch_shapes=[pltpu.VMEM((total, width), jnp.float32)] * 3
            + [pltpu.VMEM((total + PAD, width), jnp.float32)] * 2
            + [pltpu.VMEM((groups, 3, tok, width), jnp.bfloat16)],
        ),
        out_shape=[jax.ShapeDtypeStruct((3, tok, width), jnp.bfloat16)] * groups
        + [jax.ShapeDtypeStruct((total // tile, tile + 32, width), jnp.bfloat16)],
        compiler_params=params(16, width),
        cost_estimate=SMALL,
        name="middle",
    )(place, taps, up, *[term for terms_of in parts for term in terms_of])
    return outs[:groups], outs[groups]


def assemble_kernel(place, *refs):
    grad_refs, out_ref = refs[:-1], refs[-1]
    width = grad_refs[0].shape[2]
    for r, ref in enumerate(grad_refs):
        for s in range(3):
            at = pl.multiple_of((s * len(grad_refs) + (place[0] ^ r)) * width, width)
            out_ref[:, pl.ds(at, width)] = ref[s]


def assemble(place, grads):
    streams, tok, width = grads[0].shape
    out = jax.ShapeDtypeStruct((tok, streams * width * len(grads)), jnp.bfloat16)
    return pl.pallas_call(
        assemble_kernel,
        grid_spec=pltpu.PrefetchScalarGridSpec(
            num_scalar_prefetch=1,
            grid=(1,),
            in_specs=[resident(grads[0].shape, width)] * len(grads),
            out_specs=resident(out.shape, width),
        ),
        out_shape=out,
        compiler_params=params(12, width),
        cost_estimate=SMALL,
        name="assemble",
    )(place, *grads)


def input_grad_kernel(place, *refs, terms, width, first):
    grad_refs, w_ref, out_refs = refs[:terms], refs[terms], refs[terms + 1 :]
    step = out_refs[0].shape[1]
    if terms == 1:
        columns = pl.ds(pl.multiple_of((first + pl.program_id(0)) * step, step), step)
        acc = jnp.dot(
            grad_refs[0][...], w_ref[:, :, columns].reshape(-1, step), preferred_element_type=jnp.float32
        )
    else:
        acc = jnp.zeros(out_refs[0].shape, jnp.float32)
        for r, ref in enumerate(grad_refs):
            rows = pl.ds(pl.multiple_of((place[0] ^ r) * width, width), width)
            for s in range(3):
                acc = acc + jnp.dot(ref[s], w_ref[s, rows, :], preferred_element_type=jnp.float32)
    acc = acc.astype(jnp.bfloat16)
    for i, out_ref in enumerate(out_refs):

        @pl.when(pl.program_id(0) == i)
        def _():
            out_ref[...] = acc


def input_grad(place, grads, w, first, last, chunks):
    tok = grads[0].shape[-2]
    streams, channels, feat = w.shape
    step = feat // chunks
    width = channels if len(grads) == 1 else grads[0].shape[-1]
    return pl.pallas_call(
        functools.partial(input_grad_kernel, terms=len(grads), width=width, first=first),
        grid_spec=pltpu.PrefetchScalarGridSpec(
            num_scalar_prefetch=1,
            grid=(last - first,),
            in_specs=[resident(g.shape, width) for g in grads]
            + [
                resident(w.shape, width)
                if len(grads) == 1
                else pl.BlockSpec((streams, channels, step), lambda i, _: (0, 0, first + i))
            ],
            out_specs=[resident((tok, step), width)] * (last - first),
        ),
        out_shape=[jax.ShapeDtypeStruct((tok, step), jnp.bfloat16)] * (last - first),
        compiler_params=params(16, width),
        cost_estimate=SMALL,
        name="input_grad",
    )(place, *grads, w)


def weight_grad_kernel(place, *refs, chained, groups, wide, r):
    refs = refs[chained:]
    grad_refs = refs[: 2 * groups]
    x_refs = refs[2 * groups : 3 * groups]
    out_ref = refs[3 * groups]
    tok, step = x_refs[0].shape[0], out_ref.shape[2]
    width = grad_refs[0].shape[2]
    if wide:
        turned = refs[3 * groups + 1]

        @pl.when(pl.program_id(0) == 0)
        def _():
            for side in range(2):
                for s in range(3):
                    at = pl.multiple_of(((place[0] ^ r ^ side) % 2 + 2 * s) * width, width)
                    for k in range(groups):
                        turned[pl.ds(at, width), k * tok : (k + 1) * tok] = grad_refs[side * groups + k][s].T

        acc = None
        columns = pl.ds(pl.multiple_of(pl.program_id(0) * step, step), step)
        for k in range(groups):
            term = jnp.dot(
                turned[:, k * tok : (k + 1) * tok], x_refs[k][:, columns], preferred_element_type=jnp.float32
            )
            acc = term if acc is None else acc + term
        for s in range(3):
            out_ref[s] = acc[2 * s * width : 2 * (s + 1) * width, :]
    else:
        tn = (((0,), (0,)), ((), ()))
        for side in range(2):
            at = pl.multiple_of((place[0] ^ r ^ side) % 2 * width, width)
            for s in range(3):
                acc = None
                for k in range(groups):
                    term = lax.dot_general(
                        grad_refs[side * groups + k][s], x_refs[k][...], tn, preferred_element_type=jnp.float32
                    )
                    acc = term if acc is None else acc + term
                out_ref[s, pl.ds(at, width), :] = acc


def weight_grad(place, filled, grads, xs, r, count):
    groups = len(xs)
    streams, tok, width = grads[0].shape
    feat = xs[0].shape[1]
    channels = width * count
    step = min(512, feat)
    wide = width % LANES == 0
    chained = filled is not None
    return pl.pallas_call(
        functools.partial(weight_grad_kernel, chained=chained, groups=groups, wide=wide, r=r),
        grid_spec=pltpu.PrefetchScalarGridSpec(
            num_scalar_prefetch=1,
            grid=(feat // step,),
            in_specs=[pl.BlockSpec(memory_space=pl.ANY)] * chained
            + [resident((streams, tok, width), width)] * (2 * groups)
            + [resident((tok, feat), width) if wide else pl.BlockSpec((tok, step), lambda i, _: (0, i))] * groups,
            out_specs=pl.BlockSpec((streams, 2 * width, step), lambda i, at: (0, (at[0] ^ r) // 2, i)),
            scratch_shapes=[pltpu.VMEM((2 * streams * width, groups * tok), jnp.bfloat16)] if wide else [],
        ),
        out_shape=jax.ShapeDtypeStruct((streams, channels, feat), jnp.float32),
        input_output_aliases={1: 0} if chained else {},
        compiler_params=params(20, width),
        cost_estimate=SMALL,
        name="weight_grad",
    )(place, *([filled] if chained else []), *grads, *xs)


def added(first, second):
    return (first.astype(jnp.float32) + second.astype(jnp.float32)).astype(jnp.bfloat16)


def line_hops():
    count = lax.axis_size("row")
    half, last = count // 2, count - 1
    at = lax.axis_index("row")

    def inward(i):
        perm = [(i, i + 1), (last - i, last - i - 1)]
        return lambda value: lax.ppermute(value, "row", perm), added

    def across():
        perm = [(half - 1, half), (half, half - 1)]
        return lambda value: lax.ppermute(value, "row", perm), added

    def outward(i):
        perm = [(i + 1, i), (last - i - 1, last - i)]
        outer = (at == i) | (at == last - i)
        return lambda value: lax.ppermute(value, "row", perm), lambda value, got: jnp.where(outer, got, value)

    if count % 2:
        return [(lambda value: lax.psum(value, "row"), lambda value, got: got)]
    return [inward(i) for i in range(half - 1)] + [across()] + [outward(i) for i in reversed(range(half - 1))]


def first_pieces(tokens, k):
    tok = tokens.shape[0]
    if tok % 48 or lax.axis_size("row") % 2:
        return [swap(tokens, "col", k)]
    third = tok // 3
    parity = lax.axis_index("row") % 2
    return [swap(lax.dynamic_slice_in_dim(tokens, parity * third, third, axis=0), "col", k)]


def other_pieces(tokens, first, k):
    third = first[0].shape[0]
    if third == tokens.shape[0]:
        return first
    return first + [swap(first[0], "row", 1), swap(after(tokens[2 * third :], *first), "col", k)]


def on_device(tokens, weight, taps, upstream):
    n_col = lax.axis_size("col")
    n_depth = lax.axis_size("depth")
    both = ("col", "depth")
    local_tok = upstream.shape[0]
    depth_at = lax.axis_index("depth")
    col_at = lax.axis_index("col")
    place = jnp.stack([depth_at, col_at, lax.axis_index("row")]).astype(jnp.int32)
    w = jnp.transpose(weight, (1, 0, 2))
    width = w.shape[1] // n_depth
    own_groups = width // GROUP
    first_group = (col_at * n_depth + depth_at) * own_groups
    own_taps = jnp.repeat(lax.dynamic_slice_in_dim(taps, first_group, own_groups, axis=1), GROUP, axis=1)

    def project_and_sum(x_pieces, *earlier):
        keep, send, x = project(place, x_pieces, w, n_depth)
        near = swap(after(send, *earlier) if earlier else send, "depth", 1)
        pairs = [added(keep[r // 2], near[r // 2])[None] for r in range(2, n_depth, 2)]
        fars = [swap(pair, "depth", 2 * i + 2) for i, pair in enumerate(pairs)]
        return x, [keep, near] + fars, pairs, fars

    first = [first_pieces(tokens, k) for k in range(1, n_col)]
    x, terms, pairs, fars = project_and_sum([after(tokens, own_taps)], *[piece for of in first for piece in of])
    xs, parts = [x], [terms]
    up = lax.all_to_all(after(upstream, *pairs), both, split_axis=1, concat_axis=0, tiled=True)
    for k in range(1, n_col):
        x_pieces = other_pieces(tokens, first[k - 1], k)
        x_pieces[-1] = after(x_pieces[-1], up, *fars)
        x, terms, pairs, fars = project_and_sum(x_pieces)
        xs.append(x)
        parts.append(terms)
    own_grads, blocks = middle(place, own_taps, up, parts, local_tok)
    nears = [swap(own, "depth", 1) for own in own_grads]
    grads = [None] * n_col
    ready = []
    for k in reversed(range(n_col)):
        own = own_grads[k]
        fars = [swap(after(own, *ready) if ready else own, "depth", r) for r in range(2, n_depth, 2)]
        fars = [after(far, *nears) for far in fars]
        grads[k] = [own, nears[k]]
        for far in fars:
            grads[k] += [far, swap(far, "depth", 1)]
        ready = grads[k][2:]
    chunks = 4
    lhs = [[assemble(place, of)] if width % LANES == 0 else of for of in grads]
    sent = []
    for k in range(1, n_col):
        head = input_grad(place, lhs[k], w, 0, 1, chunks)
        behind = [after(lhs[k][0], *head)] + lhs[k][1:]
        tail = input_grad(place, behind, w, 1, chunks, chunks)
        sent.append([swap(part, "col", k) for part in list(head) + list(tail)])
        lhs[0][0] = after(lhs[0][0], tail[0])
    own_part = list(input_grad(place, lhs[0], w, 0, 1, chunks))
    hops = line_hops()
    done = [None] * chunks
    flying = [None] * chunks
    token = None
    filled = None
    for slot in range(chunks + len(hops)):
        for c in range(chunks):
            h = slot - c
            if h == 0:
                value = own_part[c] if token is None else after(own_part[c], token)
                total = value.astype(jnp.float32)
                for of in sent:
                    total = total + of[c].astype(jnp.float32)
                done[c] = total.astype(jnp.bfloat16)
            elif 0 < h <= len(hops):
                done[c] = hops[h - 1][1](after(done[c], token), flying[c])
            else:
                continue
            token = done[c]
            if h < len(hops):
                flying[c] = hops[h][0](done[c])
        if slot == 0:
            behind = [after(lhs[0][0], token)] + lhs[0][1:]
            own_part += input_grad(place, behind, w, 1, chunks, chunks)
            token = after(token, own_part[1])
        if 0 < slot <= n_depth // 2:
            r = n_depth - 2 * slot
            of = [group[i] for i in (r, r + 1) for group in grads]
            filled = weight_grad(place, filled, [after(of[0], token)] + of[1:], xs, r, n_depth)
            token = after(token, filled)
        if slot == chunks - 1:
            blocks = lax.all_to_all(after(blocks, token), both, split_axis=0, concat_axis=0, tiled=True)
    grad_tokens = jnp.concatenate(done, axis=1)
    grad_weight = jnp.transpose(filled, (1, 0, 2))
    output = jnp.transpose(blocks[:, :local_tok], (1, 0, 2)).reshape(local_tok, -1)
    sums = blocks[:, local_tok : local_tok + 24].astype(jnp.float32).reshape(-1, 3, 8, own_groups, GROUP)
    grad_taps = sums.sum(axis=(1, 4))[:, :KT].transpose(1, 0, 2).reshape(KT, -1)
    return (output, grad_tokens, grad_weight, grad_taps)


def solution(mesh):
    in_specs = (
        P("col", "depth"),
        P(("row", "col"), None, "depth"),
        P(None, "row"),
        P(("col", "depth"), "row"),
    )
    out_specs = (
        P(("col", "depth"), "row"),
        P("col", "depth"),
        P(("row", "col"), None, "depth"),
        P(None, "row"),
    )
    return jax.shard_map(
        on_device, mesh=mesh, in_specs=in_specs, out_specs=out_specs, check_vma=False
    )
```

time: 219 us -> 185 us (0.84)
  waiting for transfers between devices: 88.8 us -> 55.6 us
  Pallas kernels: 60.5 us -> 33.7 us
  starting transfers between devices: 42.1 us -> 57.4 us
  local copies, waits for them, and re-layouts: 18.5 us -> 25.9 us
  other arithmetic: 6.64 us -> 10.7 us
    ppermute x12, waiting for transfers between devices: 50.7 us -> 19.6 us  [the longest x4 17.9 us: outward(): lax.ppermute(value, 'row', perm)]
    pallas_call x12 -> x6, Pallas kernels: 42.4 us -> 21 us  [the longest x2 12.3 us: weight_grad(): pl.pallas_call(functools.partial(weight_grad_kernel, chained=chained, gro...]
    ppermute x12, starting transfers between devices: 19.6 us -> 34.4 us  [the longest x4 24.3 us: inward(): return (lambda value: lax.ppermute(value, 'row', perm), added)]
    unnamed x38 -> x78, local copies, waits for them, and re-layouts: 10.7 us -> 21.1 us
    convert_element_type x10, other arithmetic: 2.59 us -> 6.81 us  [added(): (first.astype(jnp.float32) + second.astype(jnp.float32)).astype(jnp.bfloa...]
    pallas_call x2, Pallas kernels: 11.9 us -> 7.73 us  [project(): pl.pallas_call(functools.partial(project_kernel, pieces=len(xs), count=co...]
  transfers between devices with their start and end apart: 31 -> 31, of which waited for: 14 -> 16; matrix products, arithmetic and copies ran while one was open for 5% -> 6% of each run, Pallas kernels for 25% -> 14%
where the time goes in v3:
time: 185 us; the launch traced here: 184 us
  starting transfers between devices  57.4 us (31%)
  waiting for transfers between devices  55.6 us (30%)
  Pallas kernels  33.7 us (18%)
  local copies, waits for them, and re-layouts  25.9 us (14%)
  other arithmetic  10.7 us (6%)
    ppermute x17, waiting for transfers between devices, swap(): return lax.ppermute(value, axis, [(i, i ^ flip) for i in range(count)])  30.8 us
    ppermute x4, starting transfers between devices, inward(): return (lambda value: lax.ppermute(value, 'row', perm), added)  24.3 us
    unnamed x78, local copies, waits for them, and re-layouts  21.1 us
    ppermute x4, waiting for transfers between devices, outward(): lax.ppermute(value, 'row', perm)  17.9 us
    ppermute x17, starting transfers between devices, swap(): return lax.ppermute(value, axis, [(i, i ^ flip) for i in range(count)])  16.1 us
    pallas_call x2, Pallas kernels, weight_grad(): pl.pallas_call(functools.partial(weight_grad_kernel, chained=chained, gro...  12.3 us
    pallas_call x4, Pallas kernels, input_grad(): pl.pallas_call(functools.partial(input_grad_kernel, terms=len(grads), wid...  8.67 us
    pallas_call x2, Pallas kernels, project(): pl.pallas_call(functools.partial(project_kernel, pieces=len(xs), count=co...  7.73 us
  transfers between devices with their start and end apart: 31, of which 16 were waited for; matrix products, arithmetic and copies ran while one was open for 6% of the time, Pallas kernels for 14%

profile of v3, /device:TPU:0, one launch (start us, length us, event | category | flops | bytes accessed | tf_op | source)
XLA Modules:
  0.0 184.4 jit_solution(15183296917278684208)
XLA Ops:
  0.7 2.2 %fusion = (bf16[128,2048]{1,0:T(8,128)(2,1)}, bf16[128,2048]{1,0:T(8,128)(2,1)S(1)}) fusion(bf16[384,2048]{1,0:T(8,128)(2,1)} %refs_5_, s32[]{:T(128)S(6)} %select_n.35), kind=kLoop, calls=%fused_computation.27 | loop fusion | bytes 2097156 | tf_op jit(solution)/shard_map/slice | solution.py:378
  2.9 3.0 %collective-permute-start = (bf16[128,2048]{1,0:T(8,128)(2,1)S(1)}, bf16[128,2048]{1,0:T(8,128)(2,1)S(1)}, u32[]{:S(2)}, u32[]{:S(2)}) collective-permute-start(bf16[128,2048]{1,0:T(8,128)(2,1)S(1)} %get-tuple-element.85), channel_id=1, source_target_pairs={{0,4},{4,0},{1,5},{5,1},{2,6},{6,2},{3,7},{7,3},{8,12},{12,8},{9,1... | collective-permute-start | bytes 1572872 | tf_op jit(solution)/shard_map/ppermute | solution.py:20
  6.2 2.8 %copy-done.1 = bf16[512,3,2048]{2,0,1:T(8,128)(2,1)S(1)} copy-done((bf16[512,3,2048]{2,0,1:T(8,128)(2,1)S(1)}, bf16[512,3,2048]{2,0,1:T(8,128)(2,1)}, u32[]{:S(2)}) %copy-start.1) | copy-done | bytes 6291480
  9.0 3.8 %project.2 = (bf16[2,3,384,128]{3,2,1,0:T(8,128)(2,1)S(1)}, bf16[2,3,384,128]{3,2,1,0:T(8,128)(2,1)S(1)}) custom-call(s32[3]{0:T(128)S(1)} %pad_add_fusion.place, bf16[384,2048]{1,0:T(8,128)(2,1)S(1)} %copy-done.3, bf16[3,512,2048]{2,1,0:T(8,128)(2,1)S(1)} %bitcast.21), custom_call_target="tpu_custom_call" | custom-call | flops 1 | bytes 1 | tf_op jit(solution)/shard_map/project/pallas_call | solution.py:87
  12.8 5.0 %collective-permute-done.refs_0_ = bf16[128,2048]{1,0:T(8,128)(2,1)S(1)} collective-permute-done((bf16[128,2048]{1,0:T(8,128)(2,1)S(1)}, bf16[128,2048]{1,0:T(8,128)(2,1)S(1)}, u32[]{:S(2)}, u32[]{:S(2)}) %collective-permute-start) | collective-permute-done | bytes 524320 | tf_op jit(solution)/shard_map/ppermute | solution.py:20
  17.8 1.7 collective-permute-start.4
  19.5 1.6 collective-permute-start.3
  22.0 0.9 add_convert_fusion.13
  23.7 1.5 collective-permute-start.2
  25.9 3.4 %all-to-all-start = ((bf16[96,8,128]{2,0,1:T(8,128)(2,1)}), bf16[96,8,128]{2,0,1:T(8,128)(2,1)S(1)}, u32[]{:S(2)}, u32[]{:S(2)}) async-start(bf16[96,8,128]{2,0,1:T(8,128)(2,1)} %copy_bitcast_fusion.1), calls=%async_computation | async-start | bytes 393216 | tf_op jit(solution)/shard_map/all_to_all | solution.py:405
  29.3 3.1 %collective-permute-done.4.refs_2_ = bf16[128,2048]{1,0:T(8,128)(2,1)S(1)} collective-permute-done((bf16[128,2048]{1,0:T(8,128)(2,1)}, bf16[128,2048]{1,0:T(8,128)(2,1)S(1)}, u32[]{:S(2)}, u32[]{:S(2)}) %collective-permute-start.4) | collective-permute-done | bytes 524320 | tf_op jit(solution)/shard_map/ppermute | solution.py:20
  33.1 2.3 %all-to-all-done = bf16[96,8,128]{2,0,1:T(8,128)(2,1)S(1)} async-done(((bf16[96,8,128]{2,0,1:T(8,128)(2,1)}), bf16[96,8,128]{2,0,1:T(8,128)(2,1)S(1)}, u32[]{:S(2)}, u32[]{:S(2)}) %all-to-all-start) | async-done | bytes 196640 | tf_op jit(solution)/shard_map/all_to_all | solution.py:405
  36.3 2.8 %copy-done.2 = bf16[512,3,2048]{2,0,1:T(8,128)(2,1)S(1)} copy-done((bf16[512,3,2048]{2,0,1:T(8,128)(2,1)S(1)}, bf16[512,3,2048]{2,0,1:T(8,128)(2,1)}, u32[]{:S(2)}) %copy-start.2) | copy-done | bytes 6291480
  39.0 1.0 copy-done.25
  40.1 1.0 copy-done.27
  41.1 1.0 copy-done.29
  42.2 4.0 %project.3 = (bf16[2,3,384,128]{3,2,1,0:T(8,128)(2,1)S(1)}, bf16[2,3,384,128]{3,2,1,0:T(8,128)(2,1)S(1)}, bf16[384,2048]{1,0:T(8,128)(2,1)S(1)}) custom-call(s32[3]{0:T(128)S(1)} %pad_add_fusion.place, bf16[128,2048]{1,0:T(8,128)(2,1)S(1)} %copy-done.25, bf16[128,2048]{1,0:T(8,128)(2,1)S(1)} %copy-done.29, bf16[128,2048]{1,0:T(8,128)(2,1)S(1)} %copy-done.27, ...), custom_call_target="tpu_custom_call" | custom-call | flops 1 | bytes 1 | tf_op jit(solution)/shard_map/project/pallas_call | solution.py:87
  46.2 2.0 %collective-permute-done.5.refs_4_ = bf16[2,3,384,128]{3,2,1,0:T(8,128)(2,1)S(1)} collective-permute-done((bf16[2,3,384,128]{3,2,1,0:T(8,128)(2,1)S(1)}, bf16[2,3,384,128]{3,2,1,0:T(8,128)(2,1)S(1)}, u32[]{:S(2)}, u32[]{:S(2)}) %collective-permute-start.5) | collective-permute-done | bytes 589856 | tf_op jit(solution)/shard_map/ppermute | solution.py:20
  48.3 1.0 collective-permute-start.6
  49.3 8.2 %collective-permute-done.6.refs_5_ = bf16[1,3,384,128]{3,2,1,0:T(8,128)(2,1)S(1)} collective-permute-done((bf16[1,3,384,128]{3,2,1,0:T(8,128)(2,1)S(1)}, bf16[1,3,384,128]{3,2,1,0:T(8,128)(2,1)S(1)}, u32[]{:S(2)}, u32[]{:S(2)}) %collective-permute-start.6) | collective-permute-done | bytes 294944 | tf_op jit(solution)/shard_map/ppermute | solution.py:20
  57.4 3.4 %middle.1 = (bf16[3,384,128]{2,1,0:T(8,128)(2,1)S(1)}, bf16[3,384,128]{2,1,0:T(8,128)(2,1)S(1)}, bf16[8,128,128]{2,1,0:T(8,128)(2,1)}) custom-call(s32[3]{0:T(128)S(1)} %pad_add_fusion.place, f32[7,128]{1,0:T(8,128)S(1)} %reshape.26.taps_ref, bf16[768,128]{1,0:T(8,128)(2,1)S(1)} %bitcast.29, bf16[2,3,384,128]{3,2,1,0:T(8,128)(2,1)S(1)} %copy-done.5, ...), custom_call_target="tpu_custom_call" | custom-call | flops 1 | bytes 1 | tf_op jit(solution)/shard_map/middle/pallas_call | solution.py:172
  61.3 0.9 collective-permute-start.8
  62.8 7.5 %collective-permute-done.8.refs_2_.refs_1_ = bf16[3,384,128]{2,1,0:T(8,128)(2,1)S(1)} collective-permute-done((bf16[3,384,128]{2,1,0:T(8,128)(2,1)S(1)}, bf16[3,384,128]{2,1,0:T(8,128)(2,1)S(1)}, u32[]{:S(2)}, u32[]{:S(2)}) %collective-permute-start.8) | collective-permute-done | bytes 294944 | tf_op jit(solution)/shard_map/ppermute | solution.py:20
  70.3 1.6 collective-permute-done.10.refs_3_
  71.9 0.9 collective-permute-start.11
  75.7 1.3 input_grad.4
  77.1 1.4 collective-permute-start.13
  78.5 2.5 %collective-permute-done.11.refs_2_.refs_0_ = bf16[3,384,128]{2,1,0:T(8,128)(2,1)S(1)} collective-permute-done((bf16[3,384,128]{2,1,0:T(8,128)(2,1)S(1)}, bf16[3,384,128]{2,1,0:T(8,128)(2,1)S(1)}, u32[]{:S(2)}, u32[]{:S(2)}) %collective-permute-start.11) | collective-permute-done | bytes 294944 | tf_op jit(solution)/shard_map/ppermute | solution.py:20
  81.0 3.0 %input_grad.5 = (bf16[384,512]{1,0:T(8,128)(2,1)S(1)}, bf16[384,512]{1,0:T(8,128)(2,1)S(1)}, bf16[384,512]{1,0:T(8,128)(2,1)S(1)}) custom-call(s32[3]{0:T(128)S(1)} %pad_add_fusion.place, bf16[384,1536]{1,0:T(8,128)(2,1)S(1)} %assemble.3.refs_0_, bf16[3,512,2048]{2,1,0:T(8,128)(2,1)S(1)} %bitcast.26), custom_call_target="tpu_custom_call" | custom-call | flops 1 | bytes 1 | tf_op jit(solution)/shard_map/input_grad/pallas_call | solution.py:250
  86.3 1.3 input_grad.6
  88.1 3.5 %collective-permute-start.14 = (bf16[384,512]{1,0:T(8,128)(2,1)S(1)}, bf16[384,512]{1,0:T(8,128)(2,1)S(1)}, u32[]{:S(2)}, u32[]{:S(2)}) collective-permute-start(bf16[384,512]{1,0:T(8,128)(2,1)S(1)} %add_convert_fusion.11), channel_id=1, source_target_pairs={{0,8},{24,16},{1,9},{25,17},{2,10},{26,18},{3,11},{27,19},{4,12},{... | collective-permute-start | bytes 1179656 | tf_op jit(solution)/shard_map/ppermute | solution.py:349
  91.6 1.6 collective-permute-start.15
  93.2 3.0 %input_grad.7 = (bf16[384,512]{1,0:T(8,128)(2,1)S(1)}, bf16[384,512]{1,0:T(8,128)(2,1)S(1)}, bf16[384,512]{1,0:T(8,128)(2,1)S(1)}) custom-call(s32[3]{0:T(128)S(1)} %pad_add_fusion.place, bf16[384,1536]{1,0:T(8,128)(2,1)S(1)} %assemble.2.refs_0_, bf16[3,512,2048]{2,1,0:T(8,128)(2,1)S(1)} %bitcast.28), custom_call_target="tpu_custom_call" | custom-call | flops 1 | bytes 1 | tf_op jit(solution)/shard_map/input_grad/pallas_call | solution.py:250
  97.7 1.7 collective-permute-done.14
  99.5 0.8 add_convert_fusion.10
  100.3 1.4 collective-permute-start.16
  101.8 0.8 add_convert_fusion.9
  102.6 7.9 %collective-permute-start.17 = (bf16[384,512]{1,0:T(8,128)(2,1)}, bf16[384,512]{1,0:T(8,128)(2,1)}, u32[]{:S(2)}, u32[]{:S(2)}) collective-permute-start(bf16[384,512]{1,0:T(8,128)(2,1)} %add_convert_fusion.9), channel_id=1, source_target_pairs={{0,8},{24,16},{1,9},{25,17},{2,10},{26,18},{3,11},{27,19},{4,12},{... | collective-permute-start | bytes 1179656 | tf_op jit(solution)/shard_map/ppermute | solution.py:349
  110.6 0.9 collective-permute-start.18
  111.4 1.2 collective-permute-start.22
  112.6 1.0 copy-done.9
  113.5 1.0 copy-done.11
  114.5 1.0 copy-done.13
  115.5 1.0 copy-done.15
  116.4 6.2 %weight_grad.2.refs_0_ = f32[3,512,2048]{2,1,0:T(8,128)} custom-call(s32[3]{0:T(128)S(1)} %pad_add_fusion.place, bf16[3,384,128]{2,1,0:T(8,128)(2,1)S(1)} %copy-done.13, bf16[3,384,128]{2,1,0:T(8,128)(2,1)S(1)} %copy-done.9, bf16[3,384,128]{2,1,0:T(8,128)(2,1)S(1)} %copy-done.15, bf16[3,384,128]{2,1,0:T(8,128)(2,1)S(1)} %copy-done.11, ...), custom_call_target="tpu_custom_call" | custom-call | flops 1 | bytes 1 | tf_op jit(solution)/shard_map/weight_grad/pallas_call | solution.py:319
  122.6 1.3 add_convert_fusion.8
  124.0 1.3 collective-permute-start.19
  125.3 1.2 add_convert_fusion.7
  127.3 5.8 %collective-permute-start.21 = (bf16[384,512]{1,0:T(8,128)(2,1)S(1)}, bf16[384,512]{1,0:T(8,128)(2,1)S(1)}, u32[]{:S(2)}, u32[]{:S(2)}) collective-permute-start(bf16[384,512]{1,0:T(8,128)(2,1)S(1)} %add_convert_fusion.6), channel_id=1, source_target_pairs={{0,8},{24,16},{1,9},{25,17},{2,10},{26,18},{3,11},{27,19},{4,12},{... | collective-permute-start | bytes 1179656 | tf_op jit(solution)/shard_map/ppermute | solution.py:349
  133.2 6.2 %weight_grad.3 = f32[3,512,2048]{2,1,0:T(8,128)} custom-call(s32[3]{0:T(128)S(1)} %pad_add_fusion.place, f32[3,512,2048]{2,1,0:T(8,128)} %weight_grad.2.refs_0_, bf16[3,384,128]{2,1,0:T(8,128)(2,1)S(1)} %copy-done.17, bf16[3,384,128]{2,1,0:T(8,128)(2,1)S(1)} %copy-done.19, bf16[3,384,128]{2,1,0:T(8,128)(2,1)S(1)} %copy-done.21, ...), custom_call_target="tpu_custom_call", output_to_operand_aliasing={{}: (1, {})} | custom-call | flops 1 | bytes 1 | tf_op jit(solution)/shard_map/weight_grad/pallas_call | solution.py:319
  139.5 1.3 collective-permute-start.23
  140.9 1.4 collective-permute-start.24
  142.5 7.1 %collective-permute-start.26 = (bf16[384,512]{1,0:T(8,128)(2,1)S(1)}, bf16[384,512]{1,0:T(8,128)(2,1)S(1)}, u32[]{:S(2)}, u32[]{:S(2)}) collective-permute-start(bf16[384,512]{1,0:T(8,128)(2,1)S(1)} %add_convert_fusion.3), channel_id=1, source_target_pairs={{0,8},{24,16},{1,9},{25,17},{2,10},{26,18},{3,11},{27,19},{4,12},{... | collective-permute-start | bytes 1179656 | tf_op jit(solution)/shard_map/ppermute | solution.py:349
  149.6 3.4 %all-to-all-start.1 = ((bf16[8,128,128]{2,1,0:T(8,128)(2,1)}), bf16[8,128,128]{2,1,0:T(8,128)(2,1)S(1)}, u32[]{:S(2)}, u32[]{:S(2)}) async-start(bf16[8,128,128]{2,1,0:T(8,128)(2,1)} %get-tuple-element.74), calls=%async_computation.1 | async-start | bytes 524288 | tf_op jit(solution)/shard_map/all_to_all | solution.py:465
  153.1 1.1 add_convert_fusion.2
  154.2 1.3 collective-permute-start.25
  155.6 1.4 collective-permute-start.27
  157.0 2.9 %all-to-all-done.1 = bf16[8,128,128]{2,1,0:T(8,128)(2,1)S(1)} async-done(((bf16[8,128,128]{2,1,0:T(8,128)(2,1)}), bf16[8,128,128]{2,1,0:T(8,128)(2,1)S(1)}, u32[]{:S(2)}, u32[]{:S(2)}) %all-to-all-start.1) | async-done | bytes 262176 | tf_op jit(solution)/shard_map/all_to_all | solution.py:465
  160.3 7.3 %collective-permute-done.25 = bf16[384,512]{1,0:T(8,128)(2,1)} collective-permute-done((bf16[384,512]{1,0:T(8,128)(2,1)S(1)}, bf16[384,512]{1,0:T(8,128)(2,1)}, u32[]{:S(2)}, u32[]{:S(2)}) %collective-permute-start.25) | collective-permute-done | bytes 393248 | tf_op jit(solution)/shard_map/ppermute | solution.py:358
  167.6 1.0 broadcast_select_fusion.1
  168.7 1.1 add_convert_fusion
  169.8 1.3 collective-permute-start.28
  172.5 10.6 %collective-permute-done.28 = bf16[384,512]{1,0:T(8,128)(2,1)S(1)} collective-permute-done((bf16[384,512]{1,0:T(8,128)(2,1)S(1)}, bf16[384,512]{1,0:T(8,128)(2,1)S(1)}, u32[]{:S(2)}, u32[]{:S(2)}) %collective-permute-start.28) | collective-permute-done | bytes 393248 | tf_op jit(solution)/shard_map/ppermute | solution.py:358
  183.1 1.4 pad_maximum_fusion
  (120 shorter events, 16.0 us)
Async XLA Ops:
  0.6 24.5 %copy-start = (bf16[96,1024]{1,0:T(8,128)(2,1)S(1)}, bf16[96,1024]{1,0:T(8,128)(2,1)}, u32[]{:S(2)}) copy-start(bf16[96,1024]{1,0:T(8,128)(2,1)} %param.7) | copy-start | bytes 589828
  0.6 5.5 %copy-start.3 = (bf16[384,2048]{1,0:T(8,128)(2,1)S(1)}, bf16[384,2048]{1,0:T(8,128)(2,1)}, u32[]{:S(2)}) copy-start(bf16[384,2048]{1,0:T(8,128)(2,1)} %refs_5_) | copy-start | bytes 4718596
  0.7 5.2 %copy-start.36 = (f32[7,64]{1,0:T(8,128)S(1)}, f32[7,64]{1,0:T(8,128)}, u32[]{:S(2)}) copy-start(f32[7,64]{1,0:T(8,128)} %param.6) | copy-start | bytes 5380
  2.9 14.9 %collective-permute-start = (bf16[128,2048]{1,0:T(8,128)(2,1)S(1)}, bf16[128,2048]{1,0:T(8,128)(2,1)S(1)}, u32[]{:S(2)}, u32[]{:S(2)}) collective-permute-start(bf16[128,2048]{1,0:T(8,128)(2,1)S(1)} %get-tuple-element.85), channel_id=1, source_target_pairs={{0,4},{4,0},{1,5},{5,1},{2,6},{6,2},{3,7},{7,3},{8,12},{12,8},{9,1... | collective-permute-start | bytes 1572872 | tf_op jit(solution)/shard_map/ppermute | solution.py:20
  6.2 2.8 %copy-start.1 = (bf16[512,3,2048]{2,0,1:T(8,128)(2,1)S(1)}, bf16[512,3,2048]{2,0,1:T(8,128)(2,1)}, u32[]{:S(2)}) copy-start(bf16[512,3,2048]{2,0,1:T(8,128)(2,1)} %param.5) | copy-start | bytes 18874372
  17.8 4.2 %collective-permute-start.1 = (bf16[2,3,384,128]{3,2,1,0:T(8,128)(2,1)S(1)}, bf16[2,3,384,128]{3,2,1,0:T(8,128)(2,1)S(1)}, u32[]{:S(2)}, u32[]{:S(2)}) collective-permute-start(bf16[2,3,384,128]{3,2,1,0:T(8,128)(2,1)S(1)} %get-tuple-element.47), channel_id=1, source_target_pairs={{0,1},{1,0},{2,3},{3,2},{4,5},{5,4},{6,7},{7,6},{8,9},{9,8},{10,11... | collective-permute-start | bytes 1769480 | tf_op jit(solution)/shard_map/ppermute | solution.py:20
  17.8 14.5 %collective-permute-start.4 = (bf16[128,2048]{1,0:T(8,128)(2,1)}, bf16[128,2048]{1,0:T(8,128)(2,1)S(1)}, u32[]{:S(2)}, u32[]{:S(2)}) collective-permute-start(bf16[128,2048]{1,0:T(8,128)(2,1)} %get-tuple-element.49), channel_id=1, source_target_pairs={{0,4},{4,0},{1,5},{5,1},{2,6},{6,2},{3,7},{7,3},{8,12},{12,8},{9,1... | collective-permute-start | bytes 1572872 | tf_op jit(solution)/shard_map/ppermute | solution.py:20
  19.5 15.9 %collective-permute-start.3 = (bf16[128,2048]{1,0:T(8,128)(2,1)S(1)}, bf16[128,2048]{1,0:T(8,128)(2,1)S(1)}, u32[]{:S(2)}, u32[]{:S(2)}) collective-permute-start(bf16[128,2048]{1,0:T(8,128)(2,1)S(1)} %collective-permute-done.refs_0_), channel_id=1, source_target_pairs={{0,8},{8,0},{16,24},{24,16},{1,9},{9,1},{17,25},{25,17},{2,10},{10... | collective-permute-start | bytes 1572872 | tf_op jit(solution)/shard_map/ppermute | solution.py:20
  21.1 0.8 copy-start.24
  22.0 0.9 copy-start.6
  22.9 0.8 copy-start.4
  23.7 11.8 %collective-permute-start.2 = (bf16[1,3,384,128]{3,2,1,0:T(8,128)(2,1)}, bf16[1,3,384,128]{3,2,1,0:T(8,128)(2,1)}, u32[]{:S(2)}, u32[]{:S(2)}) collective-permute-start(bf16[1,3,384,128]{3,2,1,0:T(8,128)(2,1)} %add_convert_fusion.13), channel_id=1, source_target_pairs={{0,2},{1,3},{2,0},{3,1},{4,6},{5,7},{6,4},{7,5},{8,10},{9,11},{10,... | collective-permute-start | bytes 884744 | tf_op jit(solution)/shard_map/ppermute | solution.py:20
  25.9 9.6 %all-to-all-start = ((bf16[96,8,128]{2,0,1:T(8,128)(2,1)}), bf16[96,8,128]{2,0,1:T(8,128)(2,1)S(1)}, u32[]{:S(2)}, u32[]{:S(2)}) async-start(bf16[96,8,128]{2,0,1:T(8,128)(2,1)} %copy_bitcast_fusion.1), calls=%async_computation | async-start | bytes 393216 | tf_op jit(solution)/shard_map/all_to_all | solution.py:405
  32.3 0.8 copy-start.26
  35.5 0.8 copy-start.28
  36.3 2.8 %copy-start.2 = (bf16[512,3,2048]{2,0,1:T(8,128)(2,1)S(1)}, bf16[512,3,2048]{2,0,1:T(8,128)(2,1)}, u32[]{:S(2)}) copy-start(bf16[512,3,2048]{2,0,1:T(8,128)(2,1)} %param.5) | copy-start | bytes 18874372
  39.0 1.0 copy-start.25
  40.1 1.0 copy-start.27
  41.1 1.0 copy-start.29
  42.2 15.2 %copy-start.5 = (bf16[2,3,384,128]{3,2,1,0:T(8,128)(2,1)S(1)}, bf16[2,3,384,128]{3,2,1,0:T(8,128)(2,1)}, u32[]{:S(2)}) copy-start(bf16[2,3,384,128]{3,2,1,0:T(8,128)(2,1)} %copy-done.4) | copy-start | bytes 1769476
  42.2 15.2 %copy-start.7 = (bf16[2,3,384,128]{3,2,1,0:T(8,128)(2,1)S(1)}, bf16[2,3,384,128]{3,2,1,0:T(8,128)(2,1)}, u32[]{:S(2)}) copy-start(bf16[2,3,384,128]{3,2,1,0:T(8,128)(2,1)} %copy-done.6) | copy-start | bytes 1769476
  46.1 2.1 %collective-permute-start.5 = (bf16[2,3,384,128]{3,2,1,0:T(8,128)(2,1)S(1)}, bf16[2,3,384,128]{3,2,1,0:T(8,128)(2,1)S(1)}, u32[]{:S(2)}, u32[]{:S(2)}) collective-permute-start(bf16[2,3,384,128]{3,2,1,0:T(8,128)(2,1)S(1)} %get-tuple-element.52), channel_id=1, source_target_pairs={{0,1},{1,0},{2,3},{3,2},{4,5},{5,4},{6,7},{7,6},{8,9},{9,8},{10,11... | collective-permute-start | bytes 1769480 | tf_op jit(solution)/shard_map/ppermute | solution.py:20
  48.3 9.1 %collective-permute-start.6 = (bf16[1,3,384,128]{3,2,1,0:T(8,128)(2,1)S(1)}, bf16[1,3,384,128]{3,2,1,0:T(8,128)(2,1)S(1)}, u32[]{:S(2)}, u32[]{:S(2)}) collective-permute-start(bf16[1,3,384,128]{3,2,1,0:T(8,128)(2,1)S(1)} %add_convert_fusion.12), channel_id=1, source_target_pairs={{0,2},{1,3},{2,0},{3,1},{4,6},{5,7},{6,4},{7,5},{8,10},{9,11},{10,... | collective-permute-start | bytes 884744 | tf_op jit(solution)/shard_map/ppermute | solution.py:20
  57.4 23.5 %slice-start = ((s8[6291456]{0:T(1024)(128)(4,1)}), s8[4194304]{0:T(1024)(128)(4,1)S(1)}, s32[]{:S(2)}) async-start(s8[6291456]{0:T(1024)(128)(4,1)} %bitcast.24), calls=%async_computation.2 | async-start | bytes 8388608
  60.8 16.2 %copy-start.18 = (bf16[3,384,128]{2,1,0:T(8,128)(2,1)}, bf16[3,384,128]{2,1,0:T(8,128)(2,1)S(1)}, u32[]{:S(2)}) copy-start(bf16[3,384,128]{2,1,0:T(8,128)(2,1)S(1)} %get-tuple-element.55.refs_0_.refs_2_) | copy-start | bytes 884740
  60.8 24.7 %copy-start.16 = (bf16[3,384,128]{2,1,0:T(8,128)(2,1)}, bf16[3,384,128]{2,1,0:T(8,128)(2,1)S(1)}, u32[]{:S(2)}) copy-start(bf16[3,384,128]{2,1,0:T(8,128)(2,1)S(1)} %get-tuple-element.83.refs_0_.refs_1_) | copy-start | bytes 884740
  60.8 1.6 collective-permute-start.7
  60.8 2.0 %collective-permute-start.9 = (bf16[3,384,128]{2,1,0:T(8,128)(2,1)S(1)}, bf16[3,384,128]{2,1,0:T(8,128)(2,1)S(1)}, u32[]{:S(2)}, u32[]{:S(2)}) collective-permute-start(bf16[3,384,128]{2,1,0:T(8,128)(2,1)S(1)} %get-tuple-element.55.refs_0_.refs_2_), channel_id=1, source_target_pairs={{0,1},{1,0},{2,3},{3,2},{4,5},{5,4},{6,7},{7,6},{8,9},{9,8},{10,11... | collective-permute-start | bytes 884744 | tf_op jit(solution)/shard_map/ppermute | solution.py:20
  61.3 9.0 %collective-permute-start.8 = (bf16[3,384,128]{2,1,0:T(8,128)(2,1)S(1)}, bf16[3,384,128]{2,1,0:T(8,128)(2,1)S(1)}, u32[]{:S(2)}, u32[]{:S(2)}) collective-permute-start(bf16[3,384,128]{2,1,0:T(8,128)(2,1)S(1)} %get-tuple-element.55.refs_0_.refs_2_), channel_id=1, source_target_pairs={{0,2},{1,3},{2,0},{3,1},{4,6},{5,7},{6,4},{7,5},{8,10},{9,11},{10,... | collective-permute-start | bytes 884744 | tf_op jit(solution)/shard_map/ppermute | solution.py:20
  62.4 23.1 %copy-start.20 = (bf16[3,384,128]{2,1,0:T(8,128)(2,1)}, bf16[3,384,128]{2,1,0:T(8,128)(2,1)S(1)}, u32[]{:S(2)}) copy-start(bf16[3,384,128]{2,1,0:T(8,128)(2,1)S(1)} %collective-permute-done.7.refs_1_.refs_3_) | copy-start | bytes 884740
  70.3 1.6 collective-permute-start.10
  71.9 9.1 %collective-permute-start.11 = (bf16[3,384,128]{2,1,0:T(8,128)(2,1)S(1)}, bf16[3,384,128]{2,1,0:T(8,128)(2,1)S(1)}, u32[]{:S(2)}, u32[]{:S(2)}) collective-permute-start(bf16[3,384,128]{2,1,0:T(8,128)(2,1)S(1)} %get-tuple-element.83.refs_0_.refs_1_), channel_id=1, source_target_pairs={{0,2},{1,3},{2,0},{3,1},{4,6},{5,7},{6,4},{7,5},{8,10},{9,11},{10,... | collective-permute-start | bytes 884744 | tf_op jit(solution)/shard_map/ppermute | solution.py:20
  75.7 5.2 %slice-start.1 = ((s8[6291456]{0:T(1024)(128)(4,1)}), s8[2097152]{0:T(1024)(128)(4,1)S(1)}, s32[]{:S(2)}) async-start(s8[6291456]{0:T(1024)(128)(4,1)} %bitcast.24), calls=%async_computation.3 | async-start | bytes 4194304
  77.1 10.9 %collective-permute-start.13 = (bf16[384,512]{1,0:T(8,128)(2,1)S(1)}, bf16[384,512]{1,0:T(8,128)(2,1)S(1)}, u32[]{:S(2)}, u32[]{:S(2)}) collective-permute-start(bf16[384,512]{1,0:T(8,128)(2,1)S(1)} %input_grad.4), channel_id=1, source_target_pairs={{0,4},{4,0},{1,5},{5,1},{2,6},{6,2},{3,7},{7,3},{8,12},{12,8},{9,1... | collective-permute-start | bytes 1179656 | tf_op jit(solution)/shard_map/ppermute | solution.py:20
  80.9 4.6 %copy-start.12 = (bf16[3,384,128]{2,1,0:T(8,128)(2,1)}, bf16[3,384,128]{2,1,0:T(8,128)(2,1)S(1)}, u32[]{:S(2)}) copy-start(bf16[3,384,128]{2,1,0:T(8,128)(2,1)S(1)} %collective-permute-done.11.refs_2_.refs_0_) | copy-start | bytes 884740
  81.0 4.6 %collective-permute-start.12 = (bf16[3,384,128]{2,1,0:T(8,128)(2,1)S(1)}, bf16[3,384,128]{2,1,0:T(8,128)(2,1)S(1)}, u32[]{:S(2)}, u32[]{:S(2)}) collective-permute-start(bf16[3,384,128]{2,1,0:T(8,128)(2,1)S(1)} %collective-permute-done.11.refs_2_.refs_0_), channel_id=1, source_target_pairs={{0,1},{1,0},{2,3},{3,2},{4,5},{5,4},{6,7},{7,6},{8,9},{9,8},{10,11... | collective-permute-start | bytes 884744 | tf_op jit(solution)/shard_map/ppermute | solution.py:20
  85.5 0.8 copy-start.14
  88.1 11.4 %collective-permute-start.14 = (bf16[384,512]{1,0:T(8,128)(2,1)S(1)}, bf16[384,512]{1,0:T(8,128)(2,1)S(1)}, u32[]{:S(2)}, u32[]{:S(2)}) collective-permute-start(bf16[384,512]{1,0:T(8,128)(2,1)S(1)} %add_convert_fusion.11), channel_id=1, source_target_pairs={{0,8},{24,16},{1,9},{25,17},{2,10},{26,18},{3,11},{27,19},{4,12},{... | collective-permute-start | bytes 1179656 | tf_op jit(solution)/shard_map/ppermute | solution.py:349
  91.6 10.2 %collective-permute-start.15 = (bf16[384,512]{1,0:T(8,128)(2,1)S(1)}, bf16[384,512]{1,0:T(8,128)(2,1)S(1)}, u32[]{:S(2)}, u32[]{:S(2)}) collective-permute-start(bf16[384,512]{1,0:T(8,128)(2,1)S(1)} %get-tuple-element.60), channel_id=1, source_target_pairs={{0,4},{4,0},{1,5},{5,1},{2,6},{6,2},{3,7},{7,3},{8,12},{12,8},{9,1... | collective-permute-start | bytes 1179656 | tf_op jit(solution)/shard_map/ppermute | solution.py:20
  97.0 0.8 copy-start.32
  100.3 22.3 %collective-permute-start.16 = (bf16[384,512]{1,0:T(8,128)(2,1)}, bf16[384,512]{1,0:T(8,128)(2,1)}, u32[]{:S(2)}, u32[]{:S(2)}) collective-permute-start(bf16[384,512]{1,0:T(8,128)(2,1)} %add_convert_fusion.10), channel_id=1, source_target_pairs={{8,16},{16,8},{9,17},{17,9},{10,18},{18,10},{11,19},{19,11},{12,20... | collective-permute-start | bytes 1179656 | tf_op jit(solution)/shard_map/ppermute | solution.py:353
  102.6 22.6 %collective-permute-start.17 = (bf16[384,512]{1,0:T(8,128)(2,1)}, bf16[384,512]{1,0:T(8,128)(2,1)}, u32[]{:S(2)}, u32[]{:S(2)}) collective-permute-start(bf16[384,512]{1,0:T(8,128)(2,1)} %add_convert_fusion.9), channel_id=1, source_target_pairs={{0,8},{24,16},{1,9},{25,17},{2,10},{26,18},{3,11},{27,19},{4,12},{... | collective-permute-start | bytes 1179656 | tf_op jit(solution)/shard_map/ppermute | solution.py:349
  110.6 16.6 %collective-permute-start.18 = (bf16[384,512]{1,0:T(8,128)(2,1)}, bf16[384,512]{1,0:T(8,128)(2,1)S(1)}, u32[]{:S(2)}, u32[]{:S(2)}) collective-permute-start(bf16[384,512]{1,0:T(8,128)(2,1)} %copy-done.35), channel_id=1, source_target_pairs={{0,4},{4,0},{1,5},{5,1},{2,6},{6,2},{3,7},{7,3},{8,12},{12,8},{9,1... | collective-permute-start | bytes 1179656 | tf_op jit(solution)/shard_map/ppermute | solution.py:20
  111.4 30.9 %collective-permute-start.22 = (bf16[384,512]{1,0:T(8,128)(2,1)}, bf16[384,512]{1,0:T(8,128)(2,1)S(1)}, u32[]{:S(2)}, u32[]{:S(2)}) collective-permute-start(bf16[384,512]{1,0:T(8,128)(2,1)} %copy-done.34), channel_id=1, source_target_pairs={{0,4},{4,0},{1,5},{5,1},{2,6},{6,2},{3,7},{7,3},{8,12},{12,8},{9,1... | collective-permute-start | bytes 1179656 | tf_op jit(solution)/shard_map/ppermute | solution.py:20
  112.6 1.0 copy-start.9
  113.5 1.0 copy-start.11
  114.5 1.0 copy-start.13
  115.5 1.0 copy-start.15
  122.6 4.6 %copy-start.33 = (bf16[384,512]{1,0:T(8,128)(2,1)S(1)}, bf16[384,512]{1,0:T(8,128)(2,1)}, u32[]{:S(2)}) copy-start(bf16[384,512]{1,0:T(8,128)(2,1)} %copy-done.32) | copy-start | bytes 1179652
  122.6 10.5 %copy-start.17 = (bf16[3,384,128]{2,1,0:T(8,128)(2,1)S(1)}, bf16[3,384,128]{2,1,0:T(8,128)(2,1)}, u32[]{:S(2)}) copy-start(bf16[3,384,128]{2,1,0:T(8,128)(2,1)} %copy-done.16) | copy-start | bytes 884740
  122.6 10.5 %copy-start.19 = (bf16[3,384,128]{2,1,0:T(8,128)(2,1)S(1)}, bf16[3,384,128]{2,1,0:T(8,128)(2,1)}, u32[]{:S(2)}) copy-start(bf16[3,384,128]{2,1,0:T(8,128)(2,1)} %copy-done.18) | copy-start | bytes 884740
  122.6 10.6 %copy-start.21 = (bf16[3,384,128]{2,1,0:T(8,128)(2,1)S(1)}, bf16[3,384,128]{2,1,0:T(8,128)(2,1)}, u32[]{:S(2)}) copy-start(bf16[3,384,128]{2,1,0:T(8,128)(2,1)} %copy-done.20) | copy-start | bytes 884740
  122.6 10.6 %copy-start.23 = (bf16[3,384,128]{2,1,0:T(8,128)(2,1)S(1)}, bf16[3,384,128]{2,1,0:T(8,128)(2,1)}, u32[]{:S(2)}) copy-start(bf16[3,384,128]{2,1,0:T(8,128)(2,1)} %copy-done.22) | copy-start | bytes 884740
  124.0 15.4 %collective-permute-start.19 = (bf16[384,512]{1,0:T(8,128)(2,1)S(1)}, bf16[384,512]{1,0:T(8,128)(2,1)S(1)}, u32[]{:S(2)}, u32[]{:S(2)}) collective-permute-start(bf16[384,512]{1,0:T(8,128)(2,1)S(1)} %add_convert_fusion.8), channel_id=1, source_target_pairs={{8,0},{16,24},{9,1},{17,25},{10,2},{18,26},{11,3},{19,27},{12,4},{... | collective-permute-start | bytes 1179656 | tf_op jit(solution)/shard_map/ppermute | solution.py:358
  126.5 12.9 %collective-permute-start.20 = (bf16[384,512]{1,0:T(8,128)(2,1)S(1)}, bf16[384,512]{1,0:T(8,128)(2,1)S(1)}, u32[]{:S(2)}, u32[]{:S(2)}) collective-permute-start(bf16[384,512]{1,0:T(8,128)(2,1)S(1)} %add_convert_fusion.7), channel_id=1, source_target_pairs={{8,16},{16,8},{9,17},{17,9},{10,18},{18,10},{11,19},{19,11},{12,20... | collective-permute-start | bytes 1179656 | tf_op jit(solution)/shard_map/ppermute | solution.py:353
  127.3 13.5 %collective-permute-start.21 = (bf16[384,512]{1,0:T(8,128)(2,1)S(1)}, bf16[384,512]{1,0:T(8,128)(2,1)S(1)}, u32[]{:S(2)}, u32[]{:S(2)}) collective-permute-start(bf16[384,512]{1,0:T(8,128)(2,1)S(1)} %add_convert_fusion.6), channel_id=1, source_target_pairs={{0,8},{24,16},{1,9},{25,17},{2,10},{26,18},{3,11},{27,19},{4,12},{... | collective-permute-start | bytes 1179656 | tf_op jit(solution)/shard_map/ppermute | solution.py:349
  139.4 3.0 %copy-start.31 = (bf16[384,512]{1,0:T(8,128)(2,1)S(1)}, bf16[384,512]{1,0:T(8,128)(2,1)}, u32[]{:S(2)}) copy-start(bf16[384,512]{1,0:T(8,128)(2,1)} %copy-done.30) | copy-start | bytes 1179652
  139.5 13.5 %collective-permute-start.23 = (bf16[384,512]{1,0:T(8,128)(2,1)S(1)}, bf16[384,512]{1,0:T(8,128)(2,1)S(1)}, u32[]{:S(2)}, u32[]{:S(2)}) collective-permute-start(bf16[384,512]{1,0:T(8,128)(2,1)S(1)} %add_convert_fusion.5), channel_id=1, source_target_pairs={{8,0},{16,24},{9,1},{17,25},{10,2},{18,26},{11,3},{19,27},{12,4},{... | collective-permute-start | bytes 1179656 | tf_op jit(solution)/shard_map/ppermute | solution.py:358
  140.9 12.2 %collective-permute-start.24 = (bf16[384,512]{1,0:T(8,128)(2,1)S(1)}, bf16[384,512]{1,0:T(8,128)(2,1)}, u32[]{:S(2)}, u32[]{:S(2)}) collective-permute-start(bf16[384,512]{1,0:T(8,128)(2,1)S(1)} %add_convert_fusion.4), channel_id=1, source_target_pairs={{8,16},{16,8},{9,17},{17,9},{10,18},{18,10},{11,19},{19,11},{12,20... | collective-permute-start | bytes 1179656 | tf_op jit(solution)/shard_map/ppermute | solution.py:353
  142.5 13.0 %collective-permute-start.26 = (bf16[384,512]{1,0:T(8,128)(2,1)S(1)}, bf16[384,512]{1,0:T(8,128)(2,1)S(1)}, u32[]{:S(2)}, u32[]{:S(2)}) collective-permute-start(bf16[384,512]{1,0:T(8,128)(2,1)S(1)} %add_convert_fusion.3), channel_id=1, source_target_pairs={{0,8},{24,16},{1,9},{25,17},{2,10},{26,18},{3,11},{27,19},{4,12},{... | collective-permute-start | bytes 1179656 | tf_op jit(solution)/shard_map/ppermute | solution.py:349
  149.6 10.3 %all-to-all-start.1 = ((bf16[8,128,128]{2,1,0:T(8,128)(2,1)}), bf16[8,128,128]{2,1,0:T(8,128)(2,1)S(1)}, u32[]{:S(2)}, u32[]{:S(2)}) async-start(bf16[8,128,128]{2,1,0:T(8,128)(2,1)} %get-tuple-element.74), calls=%async_computation.1 | async-start | bytes 524288 | tf_op jit(solution)/shard_map/all_to_all | solution.py:465
  154.2 13.4 %collective-permute-start.25 = (bf16[384,512]{1,0:T(8,128)(2,1)S(1)}, bf16[384,512]{1,0:T(8,128)(2,1)}, u32[]{:S(2)}, u32[]{:S(2)}) collective-permute-start(bf16[384,512]{1,0:T(8,128)(2,1)S(1)} %add_convert_fusion.2), channel_id=1, source_target_pairs={{8,0},{16,24},{9,1},{17,25},{10,2},{18,26},{11,3},{19,27},{12,4},{... | collective-permute-start | bytes 1179656 | tf_op jit(solution)/shard_map/ppermute | solution.py:358
  155.6 13.0 %collective-permute-start.27 = (bf16[384,512]{1,0:T(8,128)(2,1)S(1)}, bf16[384,512]{1,0:T(8,128)(2,1)}, u32[]{:S(2)}, u32[]{:S(2)}) collective-permute-start(bf16[384,512]{1,0:T(8,128)(2,1)S(1)} %add_convert_fusion.1), channel_id=1, source_target_pairs={{8,16},{16,8},{9,17},{17,9},{10,18},{18,10},{11,19},{19,11},{12,20... | collective-permute-start | bytes 1179656 | tf_op jit(solution)/shard_map/ppermute | solution.py:353
  169.8 13.3 %collective-permute-start.28 = (bf16[384,512]{1,0:T(8,128)(2,1)S(1)}, bf16[384,512]{1,0:T(8,128)(2,1)S(1)}, u32[]{:S(2)}, u32[]{:S(2)}) collective-permute-start(bf16[384,512]{1,0:T(8,128)(2,1)S(1)} %add_convert_fusion), channel_id=1, source_target_pairs={{8,0},{16,24},{9,1},{17,25},{10,2},{18,26},{11,3},{19,27},{12,4},{... | collective-permute-start | bytes 1179656 | tf_op jit(solution)/shard_map/ppermute | solution.py:358
  (6 other events, 4.4 us)

commit v4 on v3

--- a/solution.py
+++ b/solution.py
@@ -27,11 +27,11 @@
 def resident(shape, width):
     if width % LANES == 0:
         return pl.BlockSpec(memory_space=pltpu.VMEM)
-    return pl.BlockSpec(tuple(shape), lambda *_: (0,) * len(shape))
+    return pl.BlockSpec(tuple(shape), lambda *_: (0,) * len(shape), pipeline_mode=pl.Buffered(1))
 
 
 def params(mib, width):
-    return pltpu.CompilerParams(vmem_limit_bytes=(mib if width % LANES == 0 else 48) * MIB)
+    return pltpu.CompilerParams(vmem_limit_bytes=(mib if width % LANES == 0 else 56) * MIB)
 
 
 def project_kernel(place, *refs, pieces, count, width):
@@ -94,21 +94,107 @@
             out_specs=[spec, spec] + [resident((tok, feat), width)] * joined,
         ),
         out_shape=[part, part] + [jax.ShapeDtypeStruct((tok, feat), jnp.bfloat16)] * joined,
-        compiler_params=params(24, width),
+        compiler_params=params(10, width),
         cost_estimate=SMALL,
         name="project",
     )(place, *xs, w)
     return outs[0], outs[1], outs[2] if joined else xs[0]
 
 
-def middle_kernel(place, taps_ref, up_ref, *refs, groups, terms, tile):
+def in_three(value):
+    terms = []
+    for _ in range(3):
+        term = value.astype(jnp.bfloat16)
+        value = value - term.astype(jnp.float32)
+        terms.append(term)
+    return terms
+
+
+def split_kernel(place, up_ref, *out_refs):
+    width = out_refs[0].shape[1]
+    for r, ref in enumerate(out_refs):
+        ref[...] = up_ref[:, pl.ds(pl.multiple_of((place[3] ^ r) * width, width), width)]
+
+
+def split(place, up, count):
+    tok, width = up.shape[0], up.shape[1] // count
+    if width % LANES:
+        blocks = jnp.transpose(up.reshape(tok, count, width), (1, 0, 2))
+        return [lax.dynamic_index_in_dim(blocks, place[3] ^ r, 0, keepdims=False) for r in range(count)]
+    return pl.pallas_call(
+        split_kernel,
+        grid_spec=pltpu.PrefetchScalarGridSpec(
+            num_scalar_prefetch=1,
+            grid=(1,),
+            in_specs=[resident(up.shape, width)],
+            out_specs=[resident((tok, width), width)] * count,
+        ),
+        out_shape=[jax.ShapeDtypeStruct((tok, width), jnp.bfloat16)] * count,
+        compiler_params=params(4, width),
+        cost_estimate=SMALL,
+        name="split",
+    )(place, up)
+
+
+def join_kernel(place, _, *refs):
+    block_refs, (out_ref, grad_taps_ref) = refs[:-2], refs[-2:]
+    tok = out_ref.shape[0]
+    width = block_refs[0].shape[1]
+    groups = grad_taps_ref.shape[1]
+    lane_group = lax.broadcasted_iota(jnp.int32, (width, groups), 0) // GROUP
+    group = lax.broadcasted_iota(jnp.int32, (width, groups), 1)
+    total = jnp.zeros((24, groups), jnp.float32)
+    for r, ref in enumerate(block_refs):
+        at = place[3] ^ r
+        out_ref[:, pl.ds(pl.multiple_of(at * width, width), width)] = ref[0:tok, :]
+        spread = (lane_group + at * (width // GROUP) == group).astype(jnp.bfloat16)
+        total = total + jnp.dot(ref[tok : tok + 24, :], spread, preferred_element_type=jnp.float32)
+    grad_taps_ref[...] = (total[0:8] + total[8:16] + total[16:24])[:KT]
+
+
+def join(place, mark, blocks, tok, groups):
+    count, width = len(blocks), blocks[0].shape[1]
+    if width % LANES:
+        whole = jnp.stack(blocks)[place[3] ^ jnp.arange(count)]
+        output = jnp.transpose(whole[:, :tok], (1, 0, 2)).reshape(tok, -1)
+        sums = whole[:, tok : tok + 24].astype(jnp.float32).reshape(count, 3, 8, width // GROUP, GROUP)
+        return output, sums.sum(axis=(1, 4))[:, :KT].transpose(1, 0, 2).reshape(KT, -1)
+    return pl.pallas_call(
+        join_kernel,
+        grid_spec=pltpu.PrefetchScalarGridSpec(
+            num_scalar_prefetch=1,
+            grid=(1,),
+            in_specs=[pl.BlockSpec(memory_space=pl.ANY)] + [resident(blocks[0].shape, width)] * count,
+            out_specs=[resident((tok, width * count), width), resident((KT, groups), width)],
+        ),
+        out_shape=[
+            jax.ShapeDtypeStruct((tok, width * count), jnp.bfloat16),
+            jax.ShapeDtypeStruct((KT, groups), jnp.float32),
+        ],
+        compiler_params=params(4, width),
+        cost_estimate=SMALL,
+        name="join",
+    )(place, mark, *blocks)
+
+
+def middle_kernel(place, taps_ref, *refs, devices, groups, terms, tile):
+    up_refs, refs = refs[:devices], refs[devices:]
     part_refs = refs[: groups * terms]
     grad_refs = refs[groups * terms : groups * terms + groups]
-    out_ref, q_s, k_s, v_s, mixed_s, gf_s, far_s = refs[groups * terms + groups :]
+    out_refs = refs[groups * terms + groups : groups * terms + groups + devices]
+    up_s, out_s, q_s, k_s, v_s, mixed_s, gf_s, far_s = refs[groups * terms + groups + devices :]
     col = place[1]
     tok = part_refs[0].shape[2]
     width = part_refs[0].shape[3]
     total = groups * tok
+    tap_groups = taps_ref.shape[1]
+    for r, ref in enumerate(up_refs):
+        rows = pl.ds(pl.multiple_of((place[3] ^ r) * tile, tile), tile)
+        up_s[rows, :] = ref[...]
+    lane_group = lax.broadcasted_iota(jnp.int32, (tap_groups, width), 1) // GROUP
+    group = lax.broadcasted_iota(jnp.int32, (tap_groups, width), 0)
+    spread = (lane_group + place[3] * (width // GROUP) == group).astype(jnp.bfloat16)
+    taps = sum(jnp.dot(term, spread, preferred_element_type=jnp.float32) for term in in_three(taps_ref[...]))
     mixed_s[0:PAD, :] = jnp.zeros((PAD, width), jnp.float32)
     gf_s[total : total + PAD, :] = jnp.zeros((PAD, width), jnp.float32)
     for k in range(groups):
@@ -122,14 +208,11 @@
                 for ref in part_refs[k * terms : (k + 1) * terms]:
                     term = ref[0, s, inside, :].astype(jnp.float32)
                     acc = term if acc is None else acc + term
-                streams.append(acc.astype(jnp.bfloat16).astype(jnp.float32))
-            query, key, value = streams
-            q_s[rows, :] = query
-            k_s[rows, :] = key
-            v_s[rows, :] = value
+                streams.append(acc.astype(jnp.bfloat16))
+            q_s[rows, :], k_s[rows, :], v_s[rows, :] = streams
+            query, key, value = [stream.astype(jnp.float32) for stream in streams]
             mixed_s[pl.ds(pl.multiple_of(start + i * tile + PAD, PAD), tile), :] = key * value
-            gf_s[rows, :] = up_ref[rows, :].astype(jnp.float32) * query
-    taps = taps_ref[...]
+            gf_s[rows, :] = up_s[rows, :].astype(jnp.float32) * query
     sums = [jnp.zeros((8, width), jnp.float32) for _ in range(KT)]
     for a in range(groups):
         for i in range(tok // tile):
@@ -144,53 +227,52 @@
                 filtered = filtered + taps[j : j + 1, :] * shifted
                 sums[j] = sums[j] + (gf * shifted).reshape(tile // 8, 8, width).sum(axis=0)
                 grad_mixed = grad_mixed + taps[j : j + 1, :] * gf_s[first + j : first + j + tile, :]
-            out_ref[first // tile, 0:tile, :] = (q_s[rows, :] * filtered).astype(jnp.bfloat16)
+            out_s[first // tile] = (q_s[rows, :].astype(jnp.float32) * filtered).astype(jnp.bfloat16)
             at = col ^ a
-            far_s[at, 0, inside, :] = (up_ref[rows, :].astype(jnp.float32) * filtered).astype(jnp.bfloat16)
-            far_s[at, 1, inside, :] = (grad_mixed * v_s[rows, :]).astype(jnp.bfloat16)
-            far_s[at, 2, inside, :] = (grad_mixed * k_s[rows, :]).astype(jnp.bfloat16)
+            far_s[at, 0, inside, :] = (up_s[rows, :].astype(jnp.float32) * filtered).astype(jnp.bfloat16)
+            far_s[at, 1, inside, :] = (grad_mixed * v_s[rows, :].astype(jnp.float32)).astype(jnp.bfloat16)
+            far_s[at, 2, inside, :] = (grad_mixed * k_s[rows, :].astype(jnp.float32)).astype(jnp.bfloat16)
     for k in range(groups):
         grad_refs[k][...] = far_s[k]
     rest = jnp.concatenate(
         [sums[j].sum(axis=0, keepdims=True) for j in range(KT)] + [jnp.zeros((1, width), jnp.float32)], axis=0
     )
-    terms_of = []
-    for _ in range(3):
-        term = rest.astype(jnp.bfloat16).astype(jnp.float32)
-        rest = rest - term
-        terms_of.append(term)
+    terms_of = [term.astype(jnp.float32) for term in in_three(rest)]
     packed = jnp.concatenate(terms_of + [jnp.zeros((8, width), jnp.float32)], axis=0).astype(jnp.bfloat16)
-    for i in range(out_ref.shape[0]):
-        out_ref[i, tile : tile + 32, :] = packed
-
-
-def middle(place, taps, up, parts, tile):
-    groups, terms = len(parts), len(parts[0])
+    for r, ref in enumerate(out_refs):
+        ref[0:tile, :] = out_s[place[3] ^ r]
+        ref[tile : tile + 32, :] = packed
+
+
+def middle(place, taps, ups, parts):
+    groups, terms, devices = len(parts), len(parts[0]), len(ups)
+    tile = ups[0].shape[0]
     _, _, tok, width = parts[0][0].shape
     total = groups * tok
     whole = lambda *shape: resident(shape, width)
+    one = whole(1, 3, tok, width)
     outs = pl.pallas_call(
-        functools.partial(middle_kernel, groups=groups, terms=terms, tile=tile),
+        functools.partial(middle_kernel, devices=devices, groups=groups, terms=terms, tile=tile),
         grid_spec=pltpu.PrefetchScalarGridSpec(
             num_scalar_prefetch=1,
             grid=(1,),
-            in_specs=[whole(KT, width), whole(total, width)]
-            + [
-                whole(1, 3, tok, width) if width % LANES == 0 else pl.BlockSpec((1, 3, tok, width), lambda *_: (0,) * 4)
+            in_specs=[whole(*taps.shape)] + [whole(tile, width)] * devices + [one] * (groups * terms),
+            out_specs=[whole(3, tok, width)] * groups + [whole(tile + 32, width)] * devices,
+            scratch_shapes=[
+                pltpu.VMEM((total, width), jnp.bfloat16),
+                pltpu.VMEM((devices, tile, width), jnp.bfloat16),
             ]
-            * (groups * terms),
-            out_specs=[whole(3, tok, width)] * groups + [whole(total // tile, tile + 32, width)],
-            scratch_shapes=[pltpu.VMEM((total, width), jnp.float32)] * 3
+            + [pltpu.VMEM((total, width), jnp.bfloat16)] * 3
             + [pltpu.VMEM((total + PAD, width), jnp.float32)] * 2
             + [pltpu.VMEM((groups, 3, tok, width), jnp.bfloat16)],
         ),
         out_shape=[jax.ShapeDtypeStruct((3, tok, width), jnp.bfloat16)] * groups
-        + [jax.ShapeDtypeStruct((total // tile, tile + 32, width), jnp.bfloat16)],
-        compiler_params=params(16, width),
+        + [jax.ShapeDtypeStruct((tile + 32, width), jnp.bfloat16)] * devices,
+        compiler_params=params(10, width),
         cost_estimate=SMALL,
         name="middle",
-    )(place, taps, up, *[term for terms_of in parts for term in terms_of])
-    return outs[:groups], outs[groups]
+    )(place, taps, *ups, *[term for terms_of in parts for term in terms_of])
+    return outs[:groups], outs[groups:]
 
 
 def assemble_kernel(place, *refs):
@@ -214,7 +296,7 @@
             out_specs=resident(out.shape, width),
         ),
         out_shape=out,
-        compiler_params=params(12, width),
+        compiler_params=params(4, width),
         cost_estimate=SMALL,
         name="assemble",
     )(place, *grads)
@@ -261,21 +343,22 @@
             out_specs=[resident((tok, step), width)] * (last - first),
         ),
         out_shape=[jax.ShapeDtypeStruct((tok, step), jnp.bfloat16)] * (last - first),
-        compiler_params=params(16, width),
+        compiler_params=params(8, width),
         cost_estimate=SMALL,
         name="input_grad",
     )(place, *grads, w)
 
 
 def weight_grad_kernel(place, *refs, chained, groups, wide, r):
-    refs = refs[chained:]
+    refs = refs[2 * chained :]
     grad_refs = refs[: 2 * groups]
     x_refs = refs[2 * groups : 3 * groups]
-    out_ref = refs[3 * groups]
+    out_ref, mark_ref = refs[3 * groups : 3 * groups + 2]
+    mark_ref[...] = jnp.zeros(mark_ref.shape, jnp.float32)
     tok, step = x_refs[0].shape[0], out_ref.shape[2]
     width = grad_refs[0].shape[2]
     if wide:
-        turned = refs[3 * groups + 1]
+        turned = refs[3 * groups + 2]
 
         @pl.when(pl.program_id(0) == 0)
         def _():
@@ -321,45 +404,28 @@
         grid_spec=pltpu.PrefetchScalarGridSpec(
             num_scalar_prefetch=1,
             grid=(feat // step,),
-            in_specs=[pl.BlockSpec(memory_space=pl.ANY)] * chained
+            in_specs=[pl.BlockSpec(memory_space=pl.ANY)] * (2 * chained)
             + [resident((streams, tok, width), width)] * (2 * groups)
             + [resident((tok, feat), width) if wide else pl.BlockSpec((tok, step), lambda i, _: (0, i))] * groups,
-            out_specs=pl.BlockSpec((streams, 2 * width, step), lambda i, at: (0, (at[0] ^ r) // 2, i)),
+            out_specs=[
+                pl.BlockSpec((streams, 2 * width, step), lambda i, at: (0, (at[0] ^ r) // 2, i)),
+                resident((8, LANES), width),
+            ],
             scratch_shapes=[pltpu.VMEM((2 * streams * width, groups * tok), jnp.bfloat16)] if wide else [],
         ),
-        out_shape=jax.ShapeDtypeStruct((streams, channels, feat), jnp.float32),
+        out_shape=[
+            jax.ShapeDtypeStruct((streams, channels, feat), jnp.float32),
+            jax.ShapeDtypeStruct((8, LANES), jnp.float32),
+        ],
         input_output_aliases={1: 0} if chained else {},
-        compiler_params=params(20, width),
+        compiler_params=params(14, width),
         cost_estimate=SMALL,
         name="weight_grad",
-    )(place, *([filled] if chained else []), *grads, *xs)
+    )(place, *(filled if chained else []), *grads, *xs)
 
 
 def added(first, second):
     return (first.astype(jnp.float32) + second.astype(jnp.float32)).astype(jnp.bfloat16)
-
-
-def line_hops():
-    count = lax.axis_size("row")
-    half, last = count // 2, count - 1
-    at = lax.axis_index("row")
-
-    def inward(i):
-        perm = [(i, i + 1), (last - i, last - i - 1)]
-        return lambda value: lax.ppermute(value, "row", perm), added
-
-    def across():
-        perm = [(half - 1, half), (half, half - 1)]
-        return lambda value: lax.ppermute(value, "row", perm), added
-
-    def outward(i):
-        perm = [(i + 1, i), (last - i - 1, last - i)]
-        outer = (at == i) | (at == last - i)
-        return lambda value: lax.ppermute(value, "row", perm), lambda value, got: jnp.where(outer, got, value)
-
-    if count % 2:
-        return [(lambda value: lax.psum(value, "row"), lambda value, got: got)]
-    return [inward(i) for i in range(half - 1)] + [across()] + [outward(i) for i in reversed(range(half - 1))]
 
 
 def first_pieces(tokens, k):
@@ -375,7 +441,8 @@
     third = first[0].shape[0]
     if third == tokens.shape[0]:
         return first
-    return first + [swap(first[0], "row", 1), swap(after(tokens[2 * third :], *first), "col", k)]
+    rest = after(tokens, lax.axis_index("row"))[2 * third :]
+    return first + [swap(first[0], "row", 1), swap(after(rest, *first), "col", k)]
 
 
 def on_device(tokens, weight, taps, upstream):
@@ -385,13 +452,10 @@
     local_tok = upstream.shape[0]
     depth_at = lax.axis_index("depth")
     col_at = lax.axis_index("col")
-    place = jnp.stack([depth_at, col_at, lax.axis_index("row")]).astype(jnp.int32)
+    row_at = lax.axis_index("row")
+    place = jnp.stack([depth_at, col_at, row_at, col_at * n_depth + depth_at]).astype(jnp.int32)
     w = jnp.transpose(weight, (1, 0, 2))
     width = w.shape[1] // n_depth
-    own_groups = width // GROUP
-    first_group = (col_at * n_depth + depth_at) * own_groups
-    own_taps = jnp.repeat(lax.dynamic_slice_in_dim(taps, first_group, own_groups, axis=1), GROUP, axis=1)
-
     def project_and_sum(x_pieces, *earlier):
         keep, send, x = project(place, x_pieces, w, n_depth)
         near = swap(after(send, *earlier) if earlier else send, "depth", 1)
@@ -400,16 +464,17 @@
         return x, [keep, near] + fars, pairs, fars
 
     first = [first_pieces(tokens, k) for k in range(1, n_col)]
-    x, terms, pairs, fars = project_and_sum([after(tokens, own_taps)], *[piece for of in first for piece in of])
+    x, terms, pairs, fars = project_and_sum([tokens], *[piece for of in first for piece in of])
     xs, parts = [x], [terms]
-    up = lax.all_to_all(after(upstream, *pairs), both, split_axis=1, concat_axis=0, tiled=True)
+    ups = split(place, after(upstream, *pairs), n_col * n_depth)
+    ups = [up if r == 0 else swap(up, both, r) for r, up in enumerate(ups)]
     for k in range(1, n_col):
         x_pieces = other_pieces(tokens, first[k - 1], k)
-        x_pieces[-1] = after(x_pieces[-1], up, *fars)
+        x_pieces[-1] = after(x_pieces[-1], *ups, *fars)
         x, terms, pairs, fars = project_and_sum(x_pieces)
         xs.append(x)
         parts.append(terms)
-    own_grads, blocks = middle(place, own_taps, up, parts, local_tok)
+    own_grads, blocks = middle(place, taps, ups, parts)
     nears = [swap(own, "depth", 1) for own in own_grads]
     grads = [None] * n_col
     ready = []
@@ -431,43 +496,51 @@
         sent.append([swap(part, "col", k) for part in list(head) + list(tail)])
         lhs[0][0] = after(lhs[0][0], tail[0])
     own_part = list(input_grad(place, lhs[0], w, 0, 1, chunks))
-    hops = line_hops()
-    done = [None] * chunks
-    flying = [None] * chunks
-    token = None
-    filled = None
-    for slot in range(chunks + len(hops)):
-        for c in range(chunks):
-            h = slot - c
-            if h == 0:
-                value = own_part[c] if token is None else after(own_part[c], token)
-                total = value.astype(jnp.float32)
-                for of in sent:
-                    total = total + of[c].astype(jnp.float32)
-                done[c] = total.astype(jnp.bfloat16)
-            elif 0 < h <= len(hops):
-                done[c] = hops[h - 1][1](after(done[c], token), flying[c])
-            else:
-                continue
-            token = done[c]
-            if h < len(hops):
-                flying[c] = hops[h][0](done[c])
+    outer = (row_at == 0) | (row_at == 3)
+    inward, across, summed, done = ([None] * chunks for _ in range(4))
+    pair = cross = filled = None
+    marks = []
+    line = lax.axis_size("row") == 4
+    for slot in range(chunks + 3):
+        if slot < chunks:
+            total = after(own_part[slot], *marks).astype(jnp.float32)
+            for of in sent:
+                total = total + of[slot].astype(jnp.float32)
+            inward[slot] = total.astype(jnp.bfloat16)
+            marks = [inward[slot]]
+        if not line:
+            if slot < chunks:
+                done[slot] = lax.psum(inward[slot], "row")
+        else:
+            if 0 <= slot - 1 < chunks:
+                across[slot - 1] = added(after(inward[slot - 1], *marks), pair)
+                marks = [across[slot - 1]]
+            if 0 <= slot - 2 < chunks:
+                summed[slot - 2] = added(after(across[slot - 2], *marks), cross)
+                marks = [summed[slot - 2]]
+            if 0 <= slot - 3 < chunks:
+                done[slot - 3] = jnp.where(outer, pair, summed[slot - 3])
+            if slot < chunks + 2:
+                out = summed[slot - 2] if slot >= 2 else inward[slot]
+                pair = swap(jnp.where(outer, inward[slot], out) if slot < chunks else out, "row", 1)
+            if 0 <= slot - 1 < chunks:
+                cross = lax.ppermute(across[slot - 1], "row", [(1, 2), (2, 1)])
         if slot == 0:
-            behind = [after(lhs[0][0], token)] + lhs[0][1:]
+            behind = [after(lhs[0][0], *marks)] + lhs[0][1:]
             own_part += input_grad(place, behind, w, 1, chunks, chunks)
-            token = after(token, own_part[1])
+            marks = [own_part[1]]
         if 0 < slot <= n_depth // 2:
             r = n_depth - 2 * slot
             of = [group[i] for i in (r, r + 1) for group in grads]
-            filled = weight_grad(place, filled, [after(of[0], token)] + of[1:], xs, r, n_depth)
-            token = after(token, filled)
+            filled = weight_grad(place, filled, [after(of[0], *marks)] + of[1:], xs, r, n_depth)
+            marks = [filled[1]]
         if slot == chunks - 1:
-            blocks = lax.all_to_all(after(blocks, token), both, split_axis=0, concat_axis=0, tiled=True)
+            blocks = [
+                block if r == 0 else swap(after(block, *marks), both, r) for r, block in enumerate(blocks)
+            ]
     grad_tokens = jnp.concatenate(done, axis=1)
-    grad_weight = jnp.transpose(filled, (1, 0, 2))
-    output = jnp.transpose(blocks[:, :local_tok], (1, 0, 2)).reshape(local_tok, -1)
-    sums = blocks[:, local_tok : local_tok + 24].astype(jnp.float32).reshape(-1, 3, 8, own_groups, GROUP)
-    grad_taps = sums.sum(axis=(1, 4))[:, :KT].transpose(1, 0, 2).reshape(KT, -1)
+    grad_weight = jnp.transpose(filled[0], (1, 0, 2))
+    output, grad_taps = join(place, filled[1], blocks, local_tok, taps.shape[1])
     return (output, grad_tokens, grad_weight, grad_taps)
 
 

time: 185 us -> 162 us (0.88)
  local copies, waits for them, and re-layouts: 25.9 us -> 8.93 us
  starting transfers between devices: 57.4 us -> 52.3 us
  other arithmetic: 10.7 us -> 6.12 us
  waiting for transfers between devices: 55.6 us -> 58.8 us
    ppermute x17 -> x37, starting transfers between devices: 16.1 us -> 49.6 us  [swap(): return lax.ppermute(value, axis, [(i, i ^ flip) for i in range(count)])]
    ppermute x12 -> x4, starting transfers between devices: 34.4 us -> 2.71 us  [on_device(): cross = lax.ppermute(across[slot - 1], 'row', [(1, 2), (2, 1)])]
    ppermute x17 -> x37, waiting for transfers between devices: 30.8 us -> 58.8 us  [swap(): return lax.ppermute(value, axis, [(i, i ^ flip) for i in range(count)])]
    ppermute x12 -> x4, waiting for transfers between devices: 19.6 us -> 0.01 us  [on_device(): cross = lax.ppermute(across[slot - 1], 'row', [(1, 2), (2, 1)])]
    unnamed x78 -> x54, local copies, waits for them, and re-layouts: 21.1 us -> 7.81 us
    all_to_all x2 -> x0, starting transfers between devices: 6.81 us -> none  [the longest x1 3.42 us: on_device(): lax.all_to_all(after(blocks, token), both, split_axis=0, concat_axis=0, t...]
    all_to_all x2 -> x0, waiting for transfers between devices: 5.15 us -> none  [the longest x1 2.85 us: on_device(): lax.all_to_all(after(blocks, token), both, split_axis=0, concat_axis=0, t...]
    convert_element_type x10 -> x8, other arithmetic: 6.81 us -> 1.86 us  [added(): (first.astype(jnp.float32) + second.astype(jnp.float32)).astype(jnp.bfloa...]
  transfers between devices with their start and end apart: 31 -> 41, of which waited for: 16 -> 19; matrix products, arithmetic and copies ran while one was open for 6% -> 3% of each run, Pallas kernels for 14% -> 18%
where the time goes in v4:
time: 162 us
  waiting for transfers between devices  58.8 us (36%)
  starting transfers between devices  52.3 us (32%)
  Pallas kernels  34.5 us (21%)
  local copies, waits for them, and re-layouts  8.93 us (6%)
  other arithmetic  6.12 us (4%)
    ppermute x37, waiting for transfers between devices, swap(): return lax.ppermute(value, axis, [(i, i ^ flip) for i in range(count)])  58.8 us
    ppermute x37, starting transfers between devices, swap(): return lax.ppermute(value, axis, [(i, i ^ flip) for i in range(count)])  49.6 us
    pallas_call x2, Pallas kernels, weight_grad(): pl.pallas_call(functools.partial(weight_grad_kernel, chained=chained, gro...  12.4 us
    pallas_call x4, Pallas kernels, input_grad(): pl.pallas_call(functools.partial(input_grad_kernel, terms=len(grads), wid...  9.48 us
    unnamed x54, local copies, waits for them, and re-layouts  7.81 us
    pallas_call x2, Pallas kernels, project(): pl.pallas_call(functools.partial(project_kernel, pieces=len(xs), count=co...  7.67 us
  transfers between devices with their start and end apart: 41, of which 19 were waited for; matrix products, arithmetic and copies ran while one was open for 3% of the time, Pallas kernels for 18%

profile of v4, /device:TPU:0, one launch (start us, length us, event | category | flops | bytes accessed | tf_op | source)
XLA Modules:
  0.0 161.9 jit_solution(14887246655497526212)
XLA Ops:
  0.6 1.1 constant_dynamic-slice_fusion
  1.7 3.0 %collective-permute-start = (bf16[128,2048]{1,0:T(8,128)(2,1)S(1)}, bf16[128,2048]{1,0:T(8,128)(2,1)S(1)}, u32[]{:S(2)}, u32[]{:S(2)}) collective-permute-start(bf16[128,2048]{1,0:T(8,128)(2,1)S(1)} %constant_dynamic-slice_fusion), channel_id=1, source_target_pairs={{0,4},{4,0},{1,5},{5,1},{2,6},{6,2},{3,7},{7,3},{8,12},{12,8},{9,1... | collective-permute-start | bytes 1572872 | tf_op jit(solution)/shard_map/ppermute | solution.py:20
  4.8 2.8 %copy-done = bf16[512,3,2048]{2,0,1:T(8,128)(2,1)S(1)} copy-done((bf16[512,3,2048]{2,0,1:T(8,128)(2,1)S(1)}, bf16[512,3,2048]{2,0,1:T(8,128)(2,1)}, u32[]{:S(2)}) %copy-start) | copy-done | bytes 6291480
  7.6 1.4 copy-done.3
  9.0 3.8 %project.2 = (bf16[2,3,384,128]{3,2,1,0:T(8,128)(2,1)S(1)}, bf16[2,3,384,128]{3,2,1,0:T(8,128)(2,1)S(1)}) custom-call(s32[4]{0:T(128)S(1)} %pad_add_fusion.place, bf16[384,2048]{1,0:T(8,128)(2,1)S(1)} %copy-done.3, bf16[3,512,2048]{2,1,0:T(8,128)(2,1)S(1)} %bitcast.6), custom_call_target="tpu_custom_call" | custom-call | flops 1 | bytes 1 | tf_op jit(solution)/shard_map/project/pallas_call | solution.py:87
  12.8 3.9 %collective-permute-done.refs_0_ = bf16[128,2048]{1,0:T(8,128)(2,1)S(1)} collective-permute-done((bf16[128,2048]{1,0:T(8,128)(2,1)S(1)}, bf16[128,2048]{1,0:T(8,128)(2,1)S(1)}, u32[]{:S(2)}, u32[]{:S(2)}) %collective-permute-start) | collective-permute-done | bytes 524320 | tf_op jit(solution)/shard_map/ppermute | solution.py:20
  16.7 1.8 %collective-permute-start.11 = (bf16[128,2048]{1,0:T(8,128)(2,1)S(1)}, bf16[128,2048]{1,0:T(8,128)(2,1)S(1)}, u32[]{:S(2)}, u32[]{:S(2)}) collective-permute-start(bf16[128,2048]{1,0:T(8,128)(2,1)S(1)} %slice.17), channel_id=1, source_target_pairs={{0,4},{4,0},{1,5},{5,1},{2,6},{6,2},{3,7},{7,3},{8,12},{12,8},{9,1... | collective-permute-start | bytes 1572872 | tf_op jit(solution)/shard_map/ppermute | solution.py:20
  18.5 1.6 collective-permute-start.10
  20.2 1.6 collective-permute-start.9
  23.1 8.1 %collective-permute-done.11.refs_2_ = bf16[128,2048]{1,0:T(8,128)(2,1)S(1)} collective-permute-done((bf16[128,2048]{1,0:T(8,128)(2,1)S(1)}, bf16[128,2048]{1,0:T(8,128)(2,1)S(1)}, u32[]{:S(2)}, u32[]{:S(2)}) %collective-permute-start.11) | collective-permute-done | bytes 524320 | tf_op jit(solution)/shard_map/ppermute | solution.py:20
  31.1 1.0 collective-permute-start.4
  32.2 1.5 collective-permute-start.5
  33.7 0.6 collective-permute-start.6
  34.4 2.8 %collective-permute-start.7 = (bf16[96,128]{1,0:T(8,128)(2,1)S(1)}, bf16[96,128]{1,0:T(8,128)(2,1)S(1)}, u32[]{:S(2)}, u32[]{:S(2)}) collective-permute-start(bf16[96,128]{1,0:T(8,128)(2,1)S(1)} %get-tuple-element.79), channel_id=1, source_target_pairs={{0,6},{1,7},{2,4},{3,5},{4,2},{5,3},{6,0},{7,1},{8,14},{9,15},{10,... | collective-permute-start | bytes 73736 | tf_op jit(solution)/shard_map/ppermute | solution.py:20
  37.2 1.9 %collective-permute-done.7.refs_6_ = bf16[96,128]{1,0:T(8,128)(2,1)S(1)} collective-permute-done((bf16[96,128]{1,0:T(8,128)(2,1)S(1)}, bf16[96,128]{1,0:T(8,128)(2,1)S(1)}, u32[]{:S(2)}, u32[]{:S(2)}) %collective-permute-start.7) | collective-permute-done | bytes 24608 | tf_op jit(solution)/shard_map/ppermute | solution.py:20
  39.1 2.4 %collective-permute-done.8.refs_7_ = bf16[96,128]{1,0:T(8,128)(2,1)S(1)} collective-permute-done((bf16[96,128]{1,0:T(8,128)(2,1)S(1)}, bf16[96,128]{1,0:T(8,128)(2,1)S(1)}, u32[]{:S(2)}, u32[]{:S(2)}) %collective-permute-start.8) | collective-permute-done | bytes 24608 | tf_op jit(solution)/shard_map/ppermute | solution.py:20
  41.6 3.9 %project.3 = (bf16[2,3,384,128]{3,2,1,0:T(8,128)(2,1)S(1)}, bf16[2,3,384,128]{3,2,1,0:T(8,128)(2,1)S(1)}, bf16[384,2048]{1,0:T(8,128)(2,1)S(1)}) custom-call(s32[4]{0:T(128)S(1)} %pad_add_fusion.place, bf16[128,2048]{1,0:T(8,128)(2,1)S(1)} %collective-permute-done.refs_0_, bf16[128,2048]{1,0:T(8,128)(2,1)S(1)} %collective-permute-done.10.refs_1_, ...), custom_call_target="tpu_custom_call" | custom-call | flops 1 | bytes 1 | tf_op jit(solution)/shard_map/project/pallas_call | solution.py:87
  45.6 2.0 %collective-permute-done.12.refs_12_ = bf16[2,3,384,128]{3,2,1,0:T(8,128)(2,1)S(1)} collective-permute-done((bf16[2,3,384,128]{3,2,1,0:T(8,128)(2,1)S(1)}, bf16[2,3,384,128]{3,2,1,0:T(8,128)(2,1)S(1)}, u32[]{:S(2)}, u32[]{:S(2)}) %collective-permute-start.12) | collective-permute-done | bytes 589856 | tf_op jit(solution)/shard_map/ppermute | solution.py:20
  47.7 0.7 collective-permute-start.13
  48.4 8.4 %collective-permute-done.13.refs_13_ = bf16[1,3,384,128]{3,2,1,0:T(8,128)(2,1)S(1)} collective-permute-done((bf16[1,3,384,128]{3,2,1,0:T(8,128)(2,1)S(1)}, bf16[1,3,384,128]{3,2,1,0:T(8,128)(2,1)S(1)}, u32[]{:S(2)}, u32[]{:S(2)}) %collective-permute-start.13) | collective-permute-done | bytes 294944 | tf_op jit(solution)/shard_map/ppermute | solution.py:20
  56.8 1.6 middle.1
  59.0 0.7 collective-permute-start.14
  60.5 7.5 %collective-permute-done.14.refs_2_.refs_1_ = bf16[3,384,128]{2,1,0:T(8,128)(2,1)S(1)} collective-permute-done((bf16[3,384,128]{2,1,0:T(8,128)(2,1)S(1)}, bf16[3,384,128]{2,1,0:T(8,128)(2,1)S(1)}, u32[]{:S(2)}, u32[]{:S(2)}) %collective-permute-start.14) | collective-permute-done | bytes 294944 | tf_op jit(solution)/shard_map/ppermute | solution.py:20
  68.0 1.6 collective-permute-done.17.refs_3_
  69.5 0.7 collective-permute-start.18
  70.2 0.7 assemble.3.refs_0_
  71.0 0.7 copy-done.17
  71.7 1.3 input_grad.4
  73.0 0.7 collective-permute-start.20
  73.7 4.9 %collective-permute-done.18.refs_2_.refs_0_ = bf16[3,384,128]{2,1,0:T(8,128)(2,1)S(1)} collective-permute-done((bf16[3,384,128]{2,1,0:T(8,128)(2,1)S(1)}, bf16[3,384,128]{2,1,0:T(8,128)(2,1)S(1)}, u32[]{:S(2)}, u32[]{:S(2)}) %collective-permute-start.18) | collective-permute-done | bytes 294944 | tf_op jit(solution)/shard_map/ppermute | solution.py:20
  78.6 3.8 %input_grad.5 = (bf16[384,512]{1,0:T(8,128)(2,1)}, bf16[384,512]{1,0:T(8,128)(2,1)S(1)}, bf16[384,512]{1,0:T(8,128)(2,1)S(1)}) custom-call(s32[4]{0:T(128)S(1)} %pad_add_fusion.place, bf16[384,1536]{1,0:T(8,128)(2,1)S(1)} %assemble.3.refs_0_, bf16[3,512,2048]{2,1,0:T(8,128)(2,1)S(1)} %bitcast.9), custom_call_target="tpu_custom_call" | custom-call | flops 1 | bytes 1 | tf_op jit(solution)/shard_map/input_grad/pallas_call | solution.py:332
  83.0 0.7 assemble.2.refs_0_
  83.8 1.3 input_grad.6
  85.2 0.8 add_convert_fusion.11
  86.0 1.6 collective-permute-start.22
  87.6 1.5 collective-permute-start.23
  89.6 2.8 %copy-done.2 = bf16[512,3,2048]{2,0,1:T(8,128)(2,1)S(1)} copy-done((bf16[512,3,2048]{2,0,1:T(8,128)(2,1)S(1)}, bf16[512,3,2048]{2,0,1:T(8,128)(2,1)}, u32[]{:S(2)}) %copy-start.2) | copy-done | bytes 6291480
  92.4 3.0 %input_grad.7 = (bf16[384,512]{1,0:T(8,128)(2,1)S(1)}, bf16[384,512]{1,0:T(8,128)(2,1)S(1)}, bf16[384,512]{1,0:T(8,128)(2,1)S(1)}) custom-call(s32[4]{0:T(128)S(1)} %pad_add_fusion.place, bf16[384,1536]{1,0:T(8,128)(2,1)S(1)} %assemble.2.refs_0_, bf16[3,512,2048]{2,1,0:T(8,128)(2,1)S(1)} %bitcast.11), custom_call_target="tpu_custom_call" | custom-call | flops 1 | bytes 1 | tf_op jit(solution)/shard_map/input_grad/pallas_call | solution.py:332
  95.5 1.2 add_convert_fusion.10
  96.7 0.9 collective-permute-start.24
  97.6 1.2 add_convert_fusion.9
  98.8 0.7 collective-permute-start.25
  99.5 6.2 %weight_grad.2 = (f32[3,512,2048]{2,1,0:T(8,128)}, f32[8,128]{1,0:T(8,128)S(1)}) custom-call(s32[4]{0:T(128)S(1)} %pad_add_fusion.place, bf16[3,384,128]{2,1,0:T(8,128)(2,1)S(1)} %copy-done.8, bf16[3,384,128]{2,1,0:T(8,128)(2,1)S(1)} %collective-permute-done.14.refs_2_.refs_1_, bf16[3,384,128]{2,1,0:T(8,128)(2,1)S(1)} %copy-done.10, ...), custom_call_target="tpu_custom_call" | custom-call | flops 1 | bytes 1 | tf_op jit(solution)/shard_map/weight_grad/pallas_call | solution.py:402
  105.8 1.3 collective-permute-done.24
  107.5 5.5 %collective-permute-start.27 = (bf16[384,512]{1,0:T(8,128)(2,1)S(1)}, bf16[384,512]{1,0:T(8,128)(2,1)S(1)}, u32[]{:S(2)}, u32[]{:S(2)}) collective-permute-start(bf16[384,512]{1,0:T(8,128)(2,1)S(1)} %get-tuple-element.136), channel_id=1, source_target_pairs={{0,8},{8,0},{16,24},{24,16},{1,9},{9,1},{17,25},{25,17},{2,10},{10... | collective-permute-start | bytes 1179656 | tf_op jit(solution)/shard_map/ppermute | solution.py:20
  112.9 0.7 collective-permute-start.28
  113.6 6.2 %weight_grad.3 = (f32[3,512,2048]{2,1,0:T(8,128)}, f32[8,128]{1,0:T(8,128)S(1)}) custom-call(s32[4]{0:T(128)S(1)} %pad_add_fusion.place, f32[3,512,2048]{2,1,0:T(8,128)} %get-tuple-element.99.refs_0_, f32[8,128]{1,0:T(8,128)S(1)} %get-tuple-element.100.refs_1_, bf16[3,384,128]{2,1,0:T(8,128)(2,1)S(1)} %copy-done.12, ...), custom_call_target="tpu_custom_call", output_to_operand_aliasing={{0}: (1, {})} | custom-call | flops 1 | bytes 1 | tf_op jit(solution)/shard_map/weight_grad/pallas_call | solution.py:402
  120.0 0.7 collective-permute-done.27
  121.0 3.6 %collective-permute-start.36 = (bf16[384,512]{1,0:T(8,128)(2,1)S(1)}, bf16[384,512]{1,0:T(8,128)(2,1)S(1)}, u32[]{:S(2)}, u32[]{:S(2)}) collective-permute-start(bf16[384,512]{1,0:T(8,128)(2,1)S(1)} %get-tuple-element.134), channel_id=1, source_target_pairs={{0,8},{8,0},{16,24},{24,16},{1,9},{9,1},{17,25},{25,17},{2,10},{10... | collective-permute-start | bytes 1179656 | tf_op jit(solution)/shard_map/ppermute | solution.py:20
  124.6 0.7 collective-permute-start.37
  125.4 0.8 collective-permute-start.30
  126.1 1.1 collective-permute-start.31
  127.2 4.2 %collective-permute-done.36 = bf16[384,512]{1,0:T(8,128)(2,1)S(1)} collective-permute-done((bf16[384,512]{1,0:T(8,128)(2,1)S(1)}, bf16[384,512]{1,0:T(8,128)(2,1)S(1)}, u32[]{:S(2)}, u32[]{:S(2)}) %collective-permute-start.36) | collective-permute-done | bytes 393248 | tf_op jit(solution)/shard_map/ppermute | solution.py:20
  131.4 1.5 collective-permute-start.32
  133.1 0.8 collective-permute-start.34
  133.9 2.1 %collective-permute-start.35 = (bf16[128,128]{1,0:T(8,128)(2,1)S(1)}, bf16[128,128]{1,0:T(8,128)(2,1)S(1)}, u32[]{:S(2)}, u32[]{:S(2)}) collective-permute-start(bf16[128,128]{1,0:T(8,128)(2,1)S(1)} %get-tuple-element.127), channel_id=1, source_target_pairs={{0,7},{1,6},{2,5},{3,4},{4,3},{5,2},{6,1},{7,0},{8,15},{9,14},{10,... | collective-permute-start | bytes 98312 | tf_op jit(solution)/shard_map/ppermute | solution.py:20
  136.0 0.7 collective-permute-start.39
  136.8 1.4 collective-permute-done.34.refs_6_
  138.3 1.4 join.1
  139.8 3.1 %collective-permute-start.38 = (bf16[384,512]{1,0:T(8,128)(2,1)S(1)}, bf16[384,512]{1,0:T(8,128)(2,1)S(1)}, u32[]{:S(2)}, u32[]{:S(2)}) collective-permute-start(bf16[384,512]{1,0:T(8,128)(2,1)S(1)} %add_convert_fusion.1), channel_id=1, source_target_pairs={{0,8},{8,0},{16,24},{24,16},{1,9},{9,1},{17,25},{25,17},{2,10},{10... | collective-permute-start | bytes 1179656 | tf_op jit(solution)/shard_map/ppermute | solution.py:20
  143.0 8.1 %collective-permute-start.40 = (bf16[384,512]{1,0:T(8,128)(2,1)S(1)}, bf16[384,512]{1,0:T(8,128)(2,1)S(1)}, u32[]{:S(2)}, u32[]{:S(2)}) collective-permute-start(bf16[384,512]{1,0:T(8,128)(2,1)S(1)} %add_convert_fusion), channel_id=1, source_target_pairs={{0,8},{8,0},{16,24},{24,16},{1,9},{9,1},{17,25},{25,17},{2,10},{10... | collective-permute-start | bytes 1179656 | tf_op jit(solution)/shard_map/ppermute | solution.py:20
  151.1 1.7 %collective-permute-done.38 = bf16[384,512]{1,0:T(8,128)(2,1)S(1)} collective-permute-done((bf16[384,512]{1,0:T(8,128)(2,1)S(1)}, bf16[384,512]{1,0:T(8,128)(2,1)S(1)}, u32[]{:S(2)}, u32[]{:S(2)}) %collective-permute-start.38) | collective-permute-done | bytes 393248 | tf_op jit(solution)/shard_map/ppermute | solution.py:20
  152.8 7.6 %collective-permute-done.40 = bf16[384,512]{1,0:T(8,128)(2,1)S(1)} collective-permute-done((bf16[384,512]{1,0:T(8,128)(2,1)S(1)}, bf16[384,512]{1,0:T(8,128)(2,1)S(1)}, u32[]{:S(2)}, u32[]{:S(2)}) %collective-permute-start.40) | collective-permute-done | bytes 393248 | tf_op jit(solution)/shard_map/ppermute | solution.py:20
  160.5 1.4 pad_maximum_fusion
  (107 shorter events, 6.0 us)
Async XLA Ops:
  1.7 15.0 %collective-permute-start = (bf16[128,2048]{1,0:T(8,128)(2,1)S(1)}, bf16[128,2048]{1,0:T(8,128)(2,1)S(1)}, u32[]{:S(2)}, u32[]{:S(2)}) collective-permute-start(bf16[128,2048]{1,0:T(8,128)(2,1)S(1)} %constant_dynamic-slice_fusion), channel_id=1, source_target_pairs={{0,4},{4,0},{1,5},{5,1},{2,6},{6,2},{3,7},{7,3},{8,12},{12,8},{9,1... | collective-permute-start | bytes 1572872 | tf_op jit(solution)/shard_map/ppermute | solution.py:20
  4.8 2.8 %copy-start = (bf16[512,3,2048]{2,0,1:T(8,128)(2,1)S(1)}, bf16[512,3,2048]{2,0,1:T(8,128)(2,1)}, u32[]{:S(2)}) copy-start(bf16[512,3,2048]{2,0,1:T(8,128)(2,1)} %param.5) | copy-start | bytes 18874372
  9.0 7.7 %copy-start.4 = (bf16[384,2048]{1,0:T(8,128)(2,1)S(1)}, bf16[384,2048]{1,0:T(8,128)(2,1)}, u32[]{:S(2)}) copy-start(bf16[384,2048]{1,0:T(8,128)(2,1)} %refs_6_.1) | copy-start | bytes 4718596
  9.0 32.5 %copy-start.1 = (bf16[512,3,2048]{2,0,1:T(8,128)(2,1)S(1)}, bf16[512,3,2048]{2,0,1:T(8,128)(2,1)}, u32[]{:S(2)}) copy-start(bf16[512,3,2048]{2,0,1:T(8,128)(2,1)} %param.5) | copy-start | bytes 18874372
  12.8 9.0 %copy-start.19 = (bf16[96,1024]{1,0:T(8,128)(2,1)S(1)}, bf16[96,1024]{1,0:T(8,128)(2,1)}, u32[]{:S(2)}) copy-start(bf16[96,1024]{1,0:T(8,128)(2,1)} %up_ref) | copy-start | bytes 589828
  16.7 3.4 %collective-permute-start.1 = (bf16[2,3,384,128]{3,2,1,0:T(8,128)(2,1)S(1)}, bf16[2,3,384,128]{3,2,1,0:T(8,128)(2,1)S(1)}, u32[]{:S(2)}, u32[]{:S(2)}) collective-permute-start(bf16[2,3,384,128]{3,2,1,0:T(8,128)(2,1)S(1)} %get-tuple-element.71), channel_id=1, source_target_pairs={{0,1},{1,0},{2,3},{3,2},{4,5},{5,4},{6,7},{7,6},{8,9},{9,8},{10,11... | collective-permute-start | bytes 1769480 | tf_op jit(solution)/shard_map/ppermute | solution.py:20
  16.7 14.4 %collective-permute-start.11 = (bf16[128,2048]{1,0:T(8,128)(2,1)S(1)}, bf16[128,2048]{1,0:T(8,128)(2,1)S(1)}, u32[]{:S(2)}, u32[]{:S(2)}) collective-permute-start(bf16[128,2048]{1,0:T(8,128)(2,1)S(1)} %slice.17), channel_id=1, source_target_pairs={{0,4},{4,0},{1,5},{5,1},{2,6},{6,2},{3,7},{7,3},{8,12},{12,8},{9,1... | collective-permute-start | bytes 1572872 | tf_op jit(solution)/shard_map/ppermute | solution.py:20
  18.5 23.0 %collective-permute-start.10 = (bf16[128,2048]{1,0:T(8,128)(2,1)S(1)}, bf16[128,2048]{1,0:T(8,128)(2,1)S(1)}, u32[]{:S(2)}, u32[]{:S(2)}) collective-permute-start(bf16[128,2048]{1,0:T(8,128)(2,1)S(1)} %collective-permute-done.refs_0_), channel_id=1, source_target_pairs={{0,8},{8,0},{16,24},{24,16},{1,9},{9,1},{17,25},{25,17},{2,10},{10... | collective-permute-start | bytes 1572872 | tf_op jit(solution)/shard_map/ppermute | solution.py:20
  20.2 21.4 %collective-permute-start.9 = (bf16[1,3,384,128]{3,2,1,0:T(8,128)(2,1)S(1)}, bf16[1,3,384,128]{3,2,1,0:T(8,128)(2,1)S(1)}, u32[]{:S(2)}, u32[]{:S(2)}) collective-permute-start(bf16[1,3,384,128]{3,2,1,0:T(8,128)(2,1)S(1)} %add_convert_fusion.13), channel_id=1, source_target_pairs={{0,2},{1,3},{2,0},{3,1},{4,6},{5,7},{6,4},{7,5},{8,10},{9,11},{10,... | collective-permute-start | bytes 884744 | tf_op jit(solution)/shard_map/ppermute | solution.py:20
  22.4 9.8 %collective-permute-start.2 = (bf16[96,128]{1,0:T(8,128)(2,1)S(1)}, bf16[96,128]{1,0:T(8,128)(2,1)S(1)}, u32[]{:S(2)}, u32[]{:S(2)}) collective-permute-start(bf16[96,128]{1,0:T(8,128)(2,1)S(1)} %get-tuple-element.74), channel_id=1, source_target_pairs={{0,1},{1,0},{2,3},{3,2},{4,5},{5,4},{6,7},{7,6},{8,9},{9,8},{10,11... | collective-permute-start | bytes 73736 | tf_op jit(solution)/shard_map/ppermute | solution.py:20
  22.5 11.3 %collective-permute-start.3 = (bf16[96,128]{1,0:T(8,128)(2,1)S(1)}, bf16[96,128]{1,0:T(8,128)(2,1)S(1)}, u32[]{:S(2)}, u32[]{:S(2)}) collective-permute-start(bf16[96,128]{1,0:T(8,128)(2,1)S(1)} %get-tuple-element.75), channel_id=1, source_target_pairs={{0,2},{1,3},{2,0},{3,1},{4,6},{5,7},{6,4},{7,5},{8,10},{9,11},{10,... | collective-permute-start | bytes 73736 | tf_op jit(solution)/shard_map/ppermute | solution.py:20
  31.1 3.3 %collective-permute-start.4 = (bf16[96,128]{1,0:T(8,128)(2,1)S(1)}, bf16[96,128]{1,0:T(8,128)(2,1)S(1)}, u32[]{:S(2)}, u32[]{:S(2)}) collective-permute-start(bf16[96,128]{1,0:T(8,128)(2,1)S(1)} %get-tuple-element.76), channel_id=1, source_target_pairs={{0,3},{1,2},{2,1},{3,0},{4,7},{5,6},{6,5},{7,4},{8,11},{9,10},{10,... | collective-permute-start | bytes 73736 | tf_op jit(solution)/shard_map/ppermute | solution.py:20
  32.2 5.0 %collective-permute-start.5 = (bf16[96,128]{1,0:T(8,128)(2,1)S(1)}, bf16[96,128]{1,0:T(8,128)(2,1)S(1)}, u32[]{:S(2)}, u32[]{:S(2)}) collective-permute-start(bf16[96,128]{1,0:T(8,128)(2,1)S(1)} %get-tuple-element.77), channel_id=1, source_target_pairs={{0,4},{1,5},{2,6},{3,7},{4,0},{5,1},{6,2},{7,3},{8,12},{9,13},{10,... | collective-permute-start | bytes 73736 | tf_op jit(solution)/shard_map/ppermute | solution.py:20
  33.7 3.5 %collective-permute-start.6 = (bf16[96,128]{1,0:T(8,128)(2,1)S(1)}, bf16[96,128]{1,0:T(8,128)(2,1)S(1)}, u32[]{:S(2)}, u32[]{:S(2)}) collective-permute-start(bf16[96,128]{1,0:T(8,128)(2,1)S(1)} %get-tuple-element.78), channel_id=1, source_target_pairs={{0,5},{1,4},{2,7},{3,6},{4,1},{5,0},{6,3},{7,2},{8,13},{9,12},{10,... | collective-permute-start | bytes 73736 | tf_op jit(solution)/shard_map/ppermute | solution.py:20
  34.4 4.7 %collective-permute-start.7 = (bf16[96,128]{1,0:T(8,128)(2,1)S(1)}, bf16[96,128]{1,0:T(8,128)(2,1)S(1)}, u32[]{:S(2)}, u32[]{:S(2)}) collective-permute-start(bf16[96,128]{1,0:T(8,128)(2,1)S(1)} %get-tuple-element.79), channel_id=1, source_target_pairs={{0,6},{1,7},{2,4},{3,5},{4,2},{5,3},{6,0},{7,1},{8,14},{9,15},{10,... | collective-permute-start | bytes 73736 | tf_op jit(solution)/shard_map/ppermute | solution.py:20
  37.2 4.3 %collective-permute-start.8 = (bf16[96,128]{1,0:T(8,128)(2,1)S(1)}, bf16[96,128]{1,0:T(8,128)(2,1)S(1)}, u32[]{:S(2)}, u32[]{:S(2)}) collective-permute-start(bf16[96,128]{1,0:T(8,128)(2,1)S(1)} %get-tuple-element.80), channel_id=1, source_target_pairs={{0,7},{1,6},{2,5},{3,4},{4,3},{5,2},{6,1},{7,0},{8,15},{9,14},{10,... | collective-permute-start | bytes 73736 | tf_op jit(solution)/shard_map/ppermute | solution.py:20
  41.6 15.2 %copy-start.20 = (f32[7,64]{1,0:T(8,128)S(1)}, f32[7,64]{1,0:T(8,128)}, u32[]{:S(2)}) copy-start(f32[7,64]{1,0:T(8,128)} %taps_ref.1) | copy-start | bytes 5380
  45.5 12.8 %copy-start.5 = (bf16[384,2048]{1,0:T(8,128)(2,1)}, bf16[384,2048]{1,0:T(8,128)(2,1)S(1)}, u32[]{:S(2)}) copy-start(bf16[384,2048]{1,0:T(8,128)(2,1)S(1)} %get-tuple-element.98.refs_5_.refs_7_) | copy-start | bytes 4718596
  45.5 2.1 %collective-permute-start.12 = (bf16[2,3,384,128]{3,2,1,0:T(8,128)(2,1)S(1)}, bf16[2,3,384,128]{3,2,1,0:T(8,128)(2,1)S(1)}, u32[]{:S(2)}, u32[]{:S(2)}) collective-permute-start(bf16[2,3,384,128]{3,2,1,0:T(8,128)(2,1)S(1)} %get-tuple-element.85), channel_id=1, source_target_pairs={{0,1},{1,0},{2,3},{3,2},{4,5},{5,4},{6,7},{7,6},{8,9},{9,8},{10,11... | collective-permute-start | bytes 1769480 | tf_op jit(solution)/shard_map/ppermute | solution.py:20
  47.7 9.1 %collective-permute-start.13 = (bf16[1,3,384,128]{3,2,1,0:T(8,128)(2,1)S(1)}, bf16[1,3,384,128]{3,2,1,0:T(8,128)(2,1)S(1)}, u32[]{:S(2)}, u32[]{:S(2)}) collective-permute-start(bf16[1,3,384,128]{3,2,1,0:T(8,128)(2,1)S(1)} %add_convert_fusion.12), channel_id=1, source_target_pairs={{0,2},{1,3},{2,0},{3,1},{4,6},{5,7},{6,4},{7,5},{8,10},{9,11},{10,... | collective-permute-start | bytes 884744 | tf_op jit(solution)/shard_map/ppermute | solution.py:20
  58.4 14.7 %copy-start.13 = (bf16[3,384,128]{2,1,0:T(8,128)(2,1)}, bf16[3,384,128]{2,1,0:T(8,128)(2,1)S(1)}, u32[]{:S(2)}) copy-start(bf16[3,384,128]{2,1,0:T(8,128)(2,1)S(1)} %get-tuple-element.87.refs_0_.refs_3_) | copy-start | bytes 884740
  58.4 14.7 %copy-start.23 = (bf16[128,128]{1,0:T(8,128)(2,1)}, bf16[128,128]{1,0:T(8,128)(2,1)S(1)}, u32[]{:S(2)}) copy-start(bf16[128,128]{1,0:T(8,128)(2,1)S(1)} %get-tuple-element.117) | copy-start | bytes 98308
  58.4 14.7 %copy-start.25 = (bf16[128,128]{1,0:T(8,128)(2,1)}, bf16[128,128]{1,0:T(8,128)(2,1)S(1)}, u32[]{:S(2)}) copy-start(bf16[128,128]{1,0:T(8,128)(2,1)S(1)} %get-tuple-element.115) | copy-start | bytes 98308
  58.4 24.6 %copy-start.11 = (bf16[3,384,128]{2,1,0:T(8,128)(2,1)}, bf16[3,384,128]{2,1,0:T(8,128)(2,1)S(1)}, u32[]{:S(2)}) copy-start(bf16[3,384,128]{2,1,0:T(8,128)(2,1)S(1)} %get-tuple-element.106.refs_0_.refs_2_) | copy-start | bytes 884740
  58.4 1.6 %collective-permute-start.15 = (bf16[3,384,128]{2,1,0:T(8,128)(2,1)S(1)}, bf16[3,384,128]{2,1,0:T(8,128)(2,1)S(1)}, u32[]{:S(2)}, u32[]{:S(2)}) collective-permute-start(bf16[3,384,128]{2,1,0:T(8,128)(2,1)S(1)} %get-tuple-element.106.refs_0_.refs_2_), channel_id=1, source_target_pairs={{0,1},{1,0},{2,3},{3,2},{4,5},{5,4},{6,7},{7,6},{8,9},{9,8},{10,11... | collective-permute-start | bytes 884744 | tf_op jit(solution)/shard_map/ppermute | solution.py:20
  58.5 2.0 %collective-permute-start.16 = (bf16[3,384,128]{2,1,0:T(8,128)(2,1)S(1)}, bf16[3,384,128]{2,1,0:T(8,128)(2,1)S(1)}, u32[]{:S(2)}, u32[]{:S(2)}) collective-permute-start(bf16[3,384,128]{2,1,0:T(8,128)(2,1)S(1)} %get-tuple-element.87.refs_0_.refs_3_), channel_id=1, source_target_pairs={{0,1},{1,0},{2,3},{3,2},{4,5},{5,4},{6,7},{7,6},{8,9},{9,8},{10,11... | collective-permute-start | bytes 884744 | tf_op jit(solution)/shard_map/ppermute | solution.py:20
  59.0 9.0 %collective-permute-start.14 = (bf16[3,384,128]{2,1,0:T(8,128)(2,1)S(1)}, bf16[3,384,128]{2,1,0:T(8,128)(2,1)S(1)}, u32[]{:S(2)}, u32[]{:S(2)}) collective-permute-start(bf16[3,384,128]{2,1,0:T(8,128)(2,1)S(1)} %get-tuple-element.87.refs_0_.refs_3_), channel_id=1, source_target_pairs={{0,2},{1,3},{2,0},{3,1},{4,6},{5,7},{6,4},{7,5},{8,10},{9,11},{10,... | collective-permute-start | bytes 884744 | tf_op jit(solution)/shard_map/ppermute | solution.py:20
  60.0 23.0 %copy-start.15 = (bf16[3,384,128]{2,1,0:T(8,128)(2,1)}, bf16[3,384,128]{2,1,0:T(8,128)(2,1)S(1)}, u32[]{:S(2)}) copy-start(bf16[3,384,128]{2,1,0:T(8,128)(2,1)S(1)} %collective-permute-done.15.refs_1_.refs_4_) | copy-start | bytes 884740
  68.0 1.6 collective-permute-start.17
  69.5 9.1 %collective-permute-start.18 = (bf16[3,384,128]{2,1,0:T(8,128)(2,1)S(1)}, bf16[3,384,128]{2,1,0:T(8,128)(2,1)S(1)}, u32[]{:S(2)}, u32[]{:S(2)}) collective-permute-start(bf16[3,384,128]{2,1,0:T(8,128)(2,1)S(1)} %get-tuple-element.106.refs_0_.refs_2_), channel_id=1, source_target_pairs={{0,2},{1,3},{2,0},{3,1},{4,6},{5,7},{6,4},{7,5},{8,10},{9,11},{10,... | collective-permute-start | bytes 884744 | tf_op jit(solution)/shard_map/ppermute | solution.py:20
  73.0 12.1 %collective-permute-start.20 = (bf16[384,512]{1,0:T(8,128)(2,1)S(1)}, bf16[384,512]{1,0:T(8,128)(2,1)S(1)}, u32[]{:S(2)}, u32[]{:S(2)}) collective-permute-start(bf16[384,512]{1,0:T(8,128)(2,1)S(1)} %input_grad.4), channel_id=1, source_target_pairs={{0,4},{4,0},{1,5},{5,1},{2,6},{6,2},{3,7},{7,3},{8,12},{12,8},{9,1... | collective-permute-start | bytes 1179656 | tf_op jit(solution)/shard_map/ppermute | solution.py:20
  78.6 4.4 %copy-start.7 = (bf16[3,384,128]{2,1,0:T(8,128)(2,1)}, bf16[3,384,128]{2,1,0:T(8,128)(2,1)S(1)}, u32[]{:S(2)}) copy-start(bf16[3,384,128]{2,1,0:T(8,128)(2,1)S(1)} %collective-permute-done.18.refs_2_.refs_0_) | copy-start | bytes 884740
  78.6 4.4 %collective-permute-start.19 = (bf16[3,384,128]{2,1,0:T(8,128)(2,1)S(1)}, bf16[3,384,128]{2,1,0:T(8,128)(2,1)S(1)}, u32[]{:S(2)}, u32[]{:S(2)}) collective-permute-start(bf16[3,384,128]{2,1,0:T(8,128)(2,1)S(1)} %collective-permute-done.18.refs_2_.refs_0_), channel_id=1, source_target_pairs={{0,1},{1,0},{2,3},{3,2},{4,5},{5,4},{6,7},{7,6},{8,9},{9,8},{10,11... | collective-permute-start | bytes 884744 | tf_op jit(solution)/shard_map/ppermute | solution.py:20
  82.4 2.7 %copy-start.22 = (bf16[384,512]{1,0:T(8,128)(2,1)}, bf16[384,512]{1,0:T(8,128)(2,1)S(1)}, u32[]{:S(2)}) copy-start(bf16[384,512]{1,0:T(8,128)(2,1)S(1)} %get-tuple-element.103) | copy-start | bytes 1179652
  82.4 13.0 %collective-permute-start.21 = (bf16[384,512]{1,0:T(8,128)(2,1)}, bf16[384,512]{1,0:T(8,128)(2,1)}, u32[]{:S(2)}, u32[]{:S(2)}) collective-permute-start(bf16[384,512]{1,0:T(8,128)(2,1)} %get-tuple-element.92), channel_id=1, source_target_pairs={{0,4},{4,0},{1,5},{5,1},{2,6},{6,2},{3,7},{7,3},{8,12},{12,8},{9,1... | collective-permute-start | bytes 1179656 | tf_op jit(solution)/shard_map/ppermute | solution.py:20
  86.0 11.6 %collective-permute-start.22 = (bf16[384,512]{1,0:T(8,128)(2,1)}, bf16[384,512]{1,0:T(8,128)(2,1)}, u32[]{:S(2)}, u32[]{:S(2)}) collective-permute-start(bf16[384,512]{1,0:T(8,128)(2,1)} %add_convert_fusion.11), channel_id=1, source_target_pairs={{0,8},{8,0},{16,24},{24,16},{1,9},{9,1},{17,25},{25,17},{2,10},{10... | collective-permute-start | bytes 1179656 | tf_op jit(solution)/shard_map/ppermute | solution.py:20
  87.6 18.1 %collective-permute-start.23 = (bf16[384,512]{1,0:T(8,128)(2,1)}, bf16[384,512]{1,0:T(8,128)(2,1)S(1)}, u32[]{:S(2)}, u32[]{:S(2)}) collective-permute-start(bf16[384,512]{1,0:T(8,128)(2,1)} %copy-done.22), channel_id=1, source_target_pairs={{0,4},{4,0},{1,5},{5,1},{2,6},{6,2},{3,7},{7,3},{8,12},{12,8},{9,1... | collective-permute-start | bytes 1179656 | tf_op jit(solution)/shard_map/ppermute | solution.py:20
  89.0 30.8 %collective-permute-start.26 = (bf16[384,512]{1,0:T(8,128)(2,1)}, bf16[384,512]{1,0:T(8,128)(2,1)S(1)}, u32[]{:S(2)}, u32[]{:S(2)}) collective-permute-start(bf16[384,512]{1,0:T(8,128)(2,1)} %copy-done.21), channel_id=1, source_target_pairs={{0,4},{4,0},{1,5},{5,1},{2,6},{6,2},{3,7},{7,3},{8,12},{12,8},{9,1... | collective-permute-start | bytes 1179656 | tf_op jit(solution)/shard_map/ppermute | solution.py:20
  89.6 2.8 %copy-start.2 = (bf16[512,3,2048]{2,0,1:T(8,128)(2,1)S(1)}, bf16[512,3,2048]{2,0,1:T(8,128)(2,1)}, u32[]{:S(2)}) copy-start(bf16[512,3,2048]{2,0,1:T(8,128)(2,1)} %param.5) | copy-start | bytes 18874372
  95.4 4.1 %copy-start.6 = (bf16[384,2048]{1,0:T(8,128)(2,1)S(1)}, bf16[384,2048]{1,0:T(8,128)(2,1)}, u32[]{:S(2)}) copy-start(bf16[384,2048]{1,0:T(8,128)(2,1)} %copy-done.5) | copy-start | bytes 4718596
  95.4 4.1 %copy-start.8 = (bf16[3,384,128]{2,1,0:T(8,128)(2,1)S(1)}, bf16[3,384,128]{2,1,0:T(8,128)(2,1)}, u32[]{:S(2)}) copy-start(bf16[3,384,128]{2,1,0:T(8,128)(2,1)} %copy-done.7) | copy-start | bytes 884740
  95.4 4.1 %copy-start.10 = (bf16[3,384,128]{2,1,0:T(8,128)(2,1)S(1)}, bf16[3,384,128]{2,1,0:T(8,128)(2,1)}, u32[]{:S(2)}) copy-start(bf16[3,384,128]{2,1,0:T(8,128)(2,1)} %copy-done.9) | copy-start | bytes 884740
  96.7 10.5 %collective-permute-start.24 = (bf16[384,512]{1,0:T(8,128)(2,1)S(1)}, bf16[384,512]{1,0:T(8,128)(2,1)S(1)}, u32[]{:S(2)}, u32[]{:S(2)}) collective-permute-start(bf16[384,512]{1,0:T(8,128)(2,1)S(1)} %add_convert_fusion.10), channel_id=1, source_target_pairs={{0,8},{8,0},{16,24},{24,16},{1,9},{9,1},{17,25},{25,17},{2,10},{10... | collective-permute-start | bytes 1179656 | tf_op jit(solution)/shard_map/ppermute | solution.py:20
  98.8 8.5 %collective-permute-start.25 = (bf16[384,512]{1,0:T(8,128)(2,1)S(1)}, bf16[384,512]{1,0:T(8,128)(2,1)S(1)}, u32[]{:S(2)}, u32[]{:S(2)}) collective-permute-start(bf16[384,512]{1,0:T(8,128)(2,1)S(1)} %add_convert_fusion.9), channel_id=1, source_target_pairs={{8,16},{16,8},{9,17},{17,9},{10,18},{18,10},{11,19},{19,11},{12,20... | collective-permute-start | bytes 1179656 | tf_op jit(solution)/shard_map/ppermute | solution.py:527
  105.8 7.8 %copy-start.12 = (bf16[3,384,128]{2,1,0:T(8,128)(2,1)S(1)}, bf16[3,384,128]{2,1,0:T(8,128)(2,1)}, u32[]{:S(2)}) copy-start(bf16[3,384,128]{2,1,0:T(8,128)(2,1)} %copy-done.11) | copy-start | bytes 884740
  105.8 7.8 %copy-start.14 = (bf16[3,384,128]{2,1,0:T(8,128)(2,1)S(1)}, bf16[3,384,128]{2,1,0:T(8,128)(2,1)}, u32[]{:S(2)}) copy-start(bf16[3,384,128]{2,1,0:T(8,128)(2,1)} %copy-done.13) | copy-start | bytes 884740
  105.8 7.8 %copy-start.16 = (bf16[3,384,128]{2,1,0:T(8,128)(2,1)S(1)}, bf16[3,384,128]{2,1,0:T(8,128)(2,1)}, u32[]{:S(2)}) copy-start(bf16[3,384,128]{2,1,0:T(8,128)(2,1)} %copy-done.15) | copy-start | bytes 884740
  105.8 7.8 %copy-start.18 = (bf16[3,384,128]{2,1,0:T(8,128)(2,1)S(1)}, bf16[3,384,128]{2,1,0:T(8,128)(2,1)}, u32[]{:S(2)}) copy-start(bf16[3,384,128]{2,1,0:T(8,128)(2,1)} %copy-done.17) | copy-start | bytes 884740
  107.5 13.2 %collective-permute-start.27 = (bf16[384,512]{1,0:T(8,128)(2,1)S(1)}, bf16[384,512]{1,0:T(8,128)(2,1)S(1)}, u32[]{:S(2)}, u32[]{:S(2)}) collective-permute-start(bf16[384,512]{1,0:T(8,128)(2,1)S(1)} %get-tuple-element.136), channel_id=1, source_target_pairs={{0,8},{8,0},{16,24},{24,16},{1,9},{9,1},{17,25},{25,17},{2,10},{10... | collective-permute-start | bytes 1179656 | tf_op jit(solution)/shard_map/ppermute | solution.py:20
  112.9 7.9 %collective-permute-start.28 = (bf16[384,512]{1,0:T(8,128)(2,1)S(1)}, bf16[384,512]{1,0:T(8,128)(2,1)S(1)}, u32[]{:S(2)}, u32[]{:S(2)}) collective-permute-start(bf16[384,512]{1,0:T(8,128)(2,1)S(1)} %add_convert_fusion.7), channel_id=1, source_target_pairs={{8,16},{16,8},{9,17},{17,9},{10,18},{18,10},{11,19},{19,11},{12,20... | collective-permute-start | bytes 1179656 | tf_op jit(solution)/shard_map/ppermute | solution.py:527
  119.9 5.3 %copy-start.26 = (bf16[128,128]{1,0:T(8,128)(2,1)S(1)}, bf16[128,128]{1,0:T(8,128)(2,1)}, u32[]{:S(2)}) copy-start(bf16[128,128]{1,0:T(8,128)(2,1)} %copy-done.25) | copy-start | bytes 98308
  119.9 5.4 %copy-start.24 = (bf16[128,128]{1,0:T(8,128)(2,1)S(1)}, bf16[128,128]{1,0:T(8,128)(2,1)}, u32[]{:S(2)}) copy-start(bf16[128,128]{1,0:T(8,128)(2,1)} %copy-done.23) | copy-start | bytes 98308
  121.0 10.4 %collective-permute-start.36 = (bf16[384,512]{1,0:T(8,128)(2,1)S(1)}, bf16[384,512]{1,0:T(8,128)(2,1)S(1)}, u32[]{:S(2)}, u32[]{:S(2)}) collective-permute-start(bf16[384,512]{1,0:T(8,128)(2,1)S(1)} %get-tuple-element.134), channel_id=1, source_target_pairs={{0,8},{8,0},{16,24},{24,16},{1,9},{9,1},{17,25},{25,17},{2,10},{10... | collective-permute-start | bytes 1179656 | tf_op jit(solution)/shard_map/ppermute | solution.py:20
  124.6 15.1 %collective-permute-start.37 = (bf16[384,512]{1,0:T(8,128)(2,1)S(1)}, bf16[384,512]{1,0:T(8,128)(2,1)S(1)}, u32[]{:S(2)}, u32[]{:S(2)}) collective-permute-start(bf16[384,512]{1,0:T(8,128)(2,1)S(1)} %add_convert_fusion.4), channel_id=1, source_target_pairs={{8,16},{16,8},{9,17},{17,9},{10,18},{18,10},{11,19},{19,11},{12,20... | collective-permute-start | bytes 1179656 | tf_op jit(solution)/shard_map/ppermute | solution.py:527
  125.3 7.7 %collective-permute-start.29 = (bf16[128,128]{1,0:T(8,128)(2,1)S(1)}, bf16[128,128]{1,0:T(8,128)(2,1)S(1)}, u32[]{:S(2)}, u32[]{:S(2)}) collective-permute-start(bf16[128,128]{1,0:T(8,128)(2,1)S(1)} %copy-done.26), channel_id=1, source_target_pairs={{0,1},{1,0},{2,3},{3,2},{4,5},{5,4},{6,7},{7,6},{8,9},{9,8},{10,11... | collective-permute-start | bytes 98312 | tf_op jit(solution)/shard_map/ppermute | solution.py:20
  125.4 7.7 %collective-permute-start.30 = (bf16[128,128]{1,0:T(8,128)(2,1)S(1)}, bf16[128,128]{1,0:T(8,128)(2,1)S(1)}, u32[]{:S(2)}, u32[]{:S(2)}) collective-permute-start(bf16[128,128]{1,0:T(8,128)(2,1)S(1)} %copy-done.24), channel_id=1, source_target_pairs={{0,2},{1,3},{2,0},{3,1},{4,6},{5,7},{6,4},{7,5},{8,10},{9,11},{10,... | collective-permute-start | bytes 98312 | tf_op jit(solution)/shard_map/ppermute | solution.py:20
  126.1 7.7 %collective-permute-start.31 = (bf16[128,128]{1,0:T(8,128)(2,1)S(1)}, bf16[128,128]{1,0:T(8,128)(2,1)S(1)}, u32[]{:S(2)}, u32[]{:S(2)}) collective-permute-start(bf16[128,128]{1,0:T(8,128)(2,1)S(1)} %get-tuple-element.119), channel_id=1, source_target_pairs={{0,3},{1,2},{2,1},{3,0},{4,7},{5,6},{6,5},{7,4},{8,11},{9,10},{10,... | collective-permute-start | bytes 98312 | tf_op jit(solution)/shard_map/ppermute | solution.py:20
  131.4 4.6 %collective-permute-start.32 = (bf16[128,128]{1,0:T(8,128)(2,1)S(1)}, bf16[128,128]{1,0:T(8,128)(2,1)S(1)}, u32[]{:S(2)}, u32[]{:S(2)}) collective-permute-start(bf16[128,128]{1,0:T(8,128)(2,1)S(1)} %get-tuple-element.121), channel_id=1, source_target_pairs={{0,4},{1,5},{2,6},{3,7},{4,0},{5,1},{6,2},{7,3},{8,12},{9,13},{10,... | collective-permute-start | bytes 98312 | tf_op jit(solution)/shard_map/ppermute | solution.py:20
  133.0 3.7 %collective-permute-start.33 = (bf16[128,128]{1,0:T(8,128)(2,1)S(1)}, bf16[128,128]{1,0:T(8,128)(2,1)S(1)}, u32[]{:S(2)}, u32[]{:S(2)}) collective-permute-start(bf16[128,128]{1,0:T(8,128)(2,1)S(1)} %get-tuple-element.123), channel_id=1, source_target_pairs={{0,5},{1,4},{2,7},{3,6},{4,1},{5,0},{6,3},{7,2},{8,13},{9,12},{10,... | collective-permute-start | bytes 98312 | tf_op jit(solution)/shard_map/ppermute | solution.py:20
  133.1 5.1 %collective-permute-start.34 = (bf16[128,128]{1,0:T(8,128)(2,1)S(1)}, bf16[128,128]{1,0:T(8,128)(2,1)S(1)}, u32[]{:S(2)}, u32[]{:S(2)}) collective-permute-start(bf16[128,128]{1,0:T(8,128)(2,1)S(1)} %get-tuple-element.125), channel_id=1, source_target_pairs={{0,6},{1,7},{2,4},{3,5},{4,2},{5,3},{6,0},{7,1},{8,14},{9,15},{10,... | collective-permute-start | bytes 98312 | tf_op jit(solution)/shard_map/ppermute | solution.py:20
  133.9 4.5 %collective-permute-start.35 = (bf16[128,128]{1,0:T(8,128)(2,1)S(1)}, bf16[128,128]{1,0:T(8,128)(2,1)S(1)}, u32[]{:S(2)}, u32[]{:S(2)}) collective-permute-start(bf16[128,128]{1,0:T(8,128)(2,1)S(1)} %get-tuple-element.127), channel_id=1, source_target_pairs={{0,7},{1,6},{2,5},{3,4},{4,3},{5,2},{6,1},{7,0},{8,15},{9,14},{10,... | collective-permute-start | bytes 98312 | tf_op jit(solution)/shard_map/ppermute | solution.py:20
  136.0 6.8 %collective-permute-start.39 = (bf16[384,512]{1,0:T(8,128)(2,1)S(1)}, bf16[384,512]{1,0:T(8,128)(2,1)S(1)}, u32[]{:S(2)}, u32[]{:S(2)}) collective-permute-start(bf16[384,512]{1,0:T(8,128)(2,1)S(1)} %add_convert_fusion.2), channel_id=1, source_target_pairs={{8,16},{16,8},{9,17},{17,9},{10,18},{18,10},{11,19},{19,11},{12,20... | collective-permute-start | bytes 1179656 | tf_op jit(solution)/shard_map/ppermute | solution.py:527
  139.8 13.0 %collective-permute-start.38 = (bf16[384,512]{1,0:T(8,128)(2,1)S(1)}, bf16[384,512]{1,0:T(8,128)(2,1)S(1)}, u32[]{:S(2)}, u32[]{:S(2)}) collective-permute-start(bf16[384,512]{1,0:T(8,128)(2,1)S(1)} %add_convert_fusion.1), channel_id=1, source_target_pairs={{0,8},{8,0},{16,24},{24,16},{1,9},{9,1},{17,25},{25,17},{2,10},{10... | collective-permute-start | bytes 1179656 | tf_op jit(solution)/shard_map/ppermute | solution.py:20
  143.0 17.5 %collective-permute-start.40 = (bf16[384,512]{1,0:T(8,128)(2,1)S(1)}, bf16[384,512]{1,0:T(8,128)(2,1)S(1)}, u32[]{:S(2)}, u32[]{:S(2)}) collective-permute-start(bf16[384,512]{1,0:T(8,128)(2,1)S(1)} %add_convert_fusion), channel_id=1, source_target_pairs={{0,8},{8,0},{16,24},{24,16},{1,9},{9,1},{17,25},{25,17},{2,10},{10... | collective-permute-start | bytes 1179656 | tf_op jit(solution)/shard_map/ppermute | solution.py:20
  (4 other events, 7.0 us)

commit v5 on v4

--- a/solution.py
+++ b/solution.py
@@ -306,10 +306,8 @@
     grad_refs, w_ref, out_refs = refs[:terms], refs[terms], refs[terms + 1 :]
     step = out_refs[0].shape[1]
     if terms == 1:
-        columns = pl.ds(pl.multiple_of((first + pl.program_id(0)) * step, step), step)
-        acc = jnp.dot(
-            grad_refs[0][...], w_ref[:, :, columns].reshape(-1, step), preferred_element_type=jnp.float32
-        )
+        own = slice(first * step, (first + 1) * step) if len(out_refs) == 1 else slice(None)
+        acc = jnp.dot(grad_refs[0][...], w_ref[:, :, own].reshape(-1, step), preferred_element_type=jnp.float32)
     else:
         acc = jnp.zeros(out_refs[0].shape, jnp.float32)
         for r, ref in enumerate(grad_refs):
@@ -337,13 +335,13 @@
             in_specs=[resident(g.shape, width) for g in grads]
             + [
                 resident(w.shape, width)
-                if len(grads) == 1
+                if len(grads) == 1 and last - first == 1
                 else pl.BlockSpec((streams, channels, step), lambda i, _: (0, 0, first + i))
             ],
             out_specs=[resident((tok, step), width)] * (last - first),
         ),
         out_shape=[jax.ShapeDtypeStruct((tok, step), jnp.bfloat16)] * (last - first),
-        compiler_params=params(8, width),
+        compiler_params=params(12, width),
         cost_estimate=SMALL,
         name="input_grad",
     )(place, *grads, w)
@@ -466,36 +464,43 @@
     first = [first_pieces(tokens, k) for k in range(1, n_col)]
     x, terms, pairs, fars = project_and_sum([tokens], *[piece for of in first for piece in of])
     xs, parts = [x], [terms]
-    ups = split(place, after(upstream, *pairs), n_col * n_depth)
-    ups = [up if r == 0 else swap(up, both, r) for r, up in enumerate(ups)]
     for k in range(1, n_col):
         x_pieces = other_pieces(tokens, first[k - 1], k)
-        x_pieces[-1] = after(x_pieces[-1], *ups, *fars)
+        x_pieces[-1] = after(x_pieces[-1], *fars)
         x, terms, pairs, fars = project_and_sum(x_pieces)
         xs.append(x)
         parts.append(terms)
+    ups = split(place, after(upstream, *pairs), n_col * n_depth)
+    ups = [up if r == 0 else swap(up, both, r) for r, up in enumerate(ups)]
     own_grads, blocks = middle(place, taps, ups, parts)
+    near_blocks = [r for r in range(1, len(blocks)) if r % n_depth < 2]
+    blocks = [swap(block, both, r) if r in near_blocks else block for r, block in enumerate(blocks)]
     nears = [swap(own, "depth", 1) for own in own_grads]
+    beside = nears + [blocks[r] for r in near_blocks]
+    chunks = 4
     grads = [None] * n_col
     ready = []
+    sent = []
     for k in reversed(range(n_col)):
-        own = own_grads[k]
-        fars = [swap(after(own, *ready) if ready else own, "depth", r) for r in range(2, n_depth, 2)]
-        fars = [after(far, *nears) for far in fars]
-        grads[k] = [own, nears[k]]
+        fars = [swap(after(own_grads[k], *ready) if ready else own_grads[k], "depth", r) for r in range(2, n_depth, 2)]
+        ready = fars
+        if k > 0:
+            fars = [after(far, *beside) for far in fars]
+        elif sent:
+            fars = [after(far, sent[-1][1][-1]) for far in fars]
+        grads[k] = [own_grads[k], nears[k]]
         for far in fars:
             grads[k] += [far, swap(far, "depth", 1)]
         ready = grads[k][2:]
-    chunks = 4
-    lhs = [[assemble(place, of)] if width % LANES == 0 else of for of in grads]
-    sent = []
-    for k in range(1, n_col):
-        head = input_grad(place, lhs[k], w, 0, 1, chunks)
-        behind = [after(lhs[k][0], *head)] + lhs[k][1:]
-        tail = input_grad(place, behind, w, 1, chunks, chunks)
-        sent.append([swap(part, "col", k) for part in list(head) + list(tail)])
-        lhs[0][0] = after(lhs[0][0], tail[0])
-    own_part = list(input_grad(place, lhs[0], w, 0, 1, chunks))
+        lhs = [assemble(place, grads[k])] if width % LANES == 0 else grads[k]
+        if k > 0:
+            head = input_grad(place, lhs, w, 0, 1, chunks)
+            behind = [after(lhs[0], *head)] + lhs[1:]
+            tail = input_grad(place, behind, w, 1, chunks, chunks)
+            parts_of = list(head) + list(tail)
+            sent.append(([swap(part, "col", k) for part in parts_of], parts_of))
+    sent = [of for of, _ in sent]
+    own_part = list(input_grad(place, lhs, w, 0, 1, chunks))
     outer = (row_at == 0) | (row_at == 3)
     inward, across, summed, done = ([None] * chunks for _ in range(4))
     pair = cross = filled = None
@@ -524,9 +529,9 @@
                 out = summed[slot - 2] if slot >= 2 else inward[slot]
                 pair = swap(jnp.where(outer, inward[slot], out) if slot < chunks else out, "row", 1)
             if 0 <= slot - 1 < chunks:
-                cross = lax.ppermute(across[slot - 1], "row", [(1, 2), (2, 1)])
+                cross = lax.ppermute(across[slot - 1], "row", [(0, 0), (1, 2), (2, 1), (3, 3)])
         if slot == 0:
-            behind = [after(lhs[0][0], *marks)] + lhs[0][1:]
+            behind = [after(lhs[0], *marks)] + lhs[1:]
             own_part += input_grad(place, behind, w, 1, chunks, chunks)
             marks = [own_part[1]]
         if 0 < slot <= n_depth // 2:
@@ -534,9 +539,10 @@
             of = [group[i] for i in (r, r + 1) for group in grads]
             filled = weight_grad(place, filled, [after(of[0], *marks)] + of[1:], xs, r, n_depth)
             marks = [filled[1]]
-        if slot == chunks - 1:
+        if slot == chunks + 1:
             blocks = [
-                block if r == 0 else swap(after(block, *marks), both, r) for r, block in enumerate(blocks)
+                block if r == 0 or r in near_blocks else swap(after(block, *marks), both, r)
+                for r, block in enumerate(blocks)
             ]
     grad_tokens = jnp.concatenate(done, axis=1)
     grad_weight = jnp.transpose(filled[0], (1, 0, 2))

time: 162 us -> 155 us (0.957)
  waiting for transfers between devices: 58.8 us -> 49.2 us
  local copies, waits for them, and re-layouts: 8.93 us -> 11.5 us
  starting transfers between devices: 52.3 us -> 50.1 us
    ppermute x37, waiting for transfers between devices: 58.8 us -> 49.2 us  [swap(): return lax.ppermute(value, axis, [(i, i ^ flip) for i in range(count)])]
    unnamed x54, local copies, waits for them, and re-layouts: 7.81 us -> 10.4 us
    ppermute x37, starting transfers between devices: 49.6 us -> 47.4 us  [swap(): return lax.ppermute(value, axis, [(i, i ^ flip) for i in range(count)])]
  transfers between devices with their start and end apart: 41 -> 41, of which waited for: 19 -> 19; matrix products, arithmetic and copies ran while one was open for 3% -> 3% of each run, Pallas kernels for 18% -> 19%
where the time goes in v5:
time: 155 us; the launch traced here: 153 us
  starting transfers between devices  50.1 us (32%)
  waiting for transfers between devices  49.2 us (32%)
  Pallas kernels  35.3 us (23%)
  local copies, waits for them, and re-layouts  11.5 us (7%)
  other arithmetic  6.12 us (4%)
    ppermute x37, waiting for transfers between devices, swap(): return lax.ppermute(value, axis, [(i, i ^ flip) for i in range(count)])  49.2 us
    ppermute x37, starting transfers between devices, swap(): return lax.ppermute(value, axis, [(i, i ^ flip) for i in range(count)])  47.4 us
    pallas_call x2, Pallas kernels, weight_grad(): pl.pallas_call(functools.partial(weight_grad_kernel, chained=chained, gro...  12.4 us
    unnamed x54, local copies, waits for them, and re-layouts  10.4 us
    pallas_call x4, Pallas kernels, input_grad(): pl.pallas_call(functools.partial(input_grad_kernel, terms=len(grads), wid...  10.2 us
    pallas_call x2, Pallas kernels, project(): pl.pallas_call(functools.partial(project_kernel, pieces=len(xs), count=co...  7.73 us
  transfers between devices with their start and end apart: 41, of which 19 were waited for; matrix products, arithmetic and copies ran while one was open for 3% of the time, Pallas kernels for 19%

profile of v5, /device:TPU:0, one launch (start us, length us, event | category | flops | bytes accessed | tf_op | source)
XLA Modules:
  0.0 153.4 jit_solution(9931557308399118618)
XLA Ops:
  0.6 1.1 constant_dynamic-slice_fusion
  1.7 3.0 %collective-permute-start = (bf16[128,2048]{1,0:T(8,128)(2,1)S(1)}, bf16[128,2048]{1,0:T(8,128)(2,1)S(1)}, u32[]{:S(2)}, u32[]{:S(2)}) collective-permute-start(bf16[128,2048]{1,0:T(8,128)(2,1)S(1)} %constant_dynamic-slice_fusion), channel_id=1, source_target_pairs={{0,4},{4,0},{1,5},{5,1},{2,6},{6,2},{3,7},{7,3},{8,12},{12,8},{9,1... | collective-permute-start | bytes 1572872 | tf_op jit(solution)/shard_map/ppermute | solution.py:20
  4.8 2.8 %copy-done = bf16[512,3,2048]{2,0,1:T(8,128)(2,1)S(1)} copy-done((bf16[512,3,2048]{2,0,1:T(8,128)(2,1)S(1)}, bf16[512,3,2048]{2,0,1:T(8,128)(2,1)}, u32[]{:S(2)}) %copy-start) | copy-done | bytes 6291480
  7.6 1.4 copy-done.3
  9.0 3.8 %project.2 = (bf16[2,3,384,128]{3,2,1,0:T(8,128)(2,1)S(1)}, bf16[2,3,384,128]{3,2,1,0:T(8,128)(2,1)S(1)}) custom-call(s32[4]{0:T(128)S(1)} %pad_add_fusion.place, bf16[384,2048]{1,0:T(8,128)(2,1)S(1)} %copy-done.3, bf16[3,512,2048]{2,1,0:T(8,128)(2,1)S(1)} %bitcast.6), custom_call_target="tpu_custom_call" | custom-call | flops 1 | bytes 1 | tf_op jit(solution)/shard_map/project/pallas_call | solution.py:87
  12.8 3.9 %collective-permute-done.refs_0_ = bf16[128,2048]{1,0:T(8,128)(2,1)S(1)} collective-permute-done((bf16[128,2048]{1,0:T(8,128)(2,1)S(1)}, bf16[128,2048]{1,0:T(8,128)(2,1)S(1)}, u32[]{:S(2)}, u32[]{:S(2)}) %collective-permute-start) | collective-permute-done | bytes 524320 | tf_op jit(solution)/shard_map/ppermute | solution.py:20
  16.7 1.8 %collective-permute-start.2 = (bf16[128,2048]{1,0:T(8,128)(2,1)S(1)}, bf16[128,2048]{1,0:T(8,128)(2,1)S(1)}, u32[]{:S(2)}, u32[]{:S(2)}) collective-permute-start(bf16[128,2048]{1,0:T(8,128)(2,1)S(1)} %slice.15), channel_id=1, source_target_pairs={{0,4},{4,0},{1,5},{5,1},{2,6},{6,2},{3,7},{7,3},{8,12},{12,8},{9,1... | collective-permute-start | bytes 1572872 | tf_op jit(solution)/shard_map/ppermute | solution.py:20
  18.5 1.6 %collective-permute-start.1 = (bf16[128,2048]{1,0:T(8,128)(2,1)S(1)}, bf16[128,2048]{1,0:T(8,128)(2,1)S(1)}, u32[]{:S(2)}, u32[]{:S(2)}) collective-permute-start(bf16[128,2048]{1,0:T(8,128)(2,1)S(1)} %collective-permute-done.refs_0_), channel_id=1, source_target_pairs={{0,8},{8,0},{16,24},{24,16},{1,9},{9,1},{17,25},{25,17},{2,10},{10... | collective-permute-start | bytes 1572872 | tf_op jit(solution)/shard_map/ppermute | solution.py:20
  20.2 1.6 %collective-permute-start.4 = (bf16[1,3,384,128]{3,2,1,0:T(8,128)(2,1)S(1)}, bf16[1,3,384,128]{3,2,1,0:T(8,128)(2,1)S(1)}, u32[]{:S(2)}, u32[]{:S(2)}) collective-permute-start(bf16[1,3,384,128]{3,2,1,0:T(8,128)(2,1)S(1)} %add_convert_fusion.13), channel_id=1, source_target_pairs={{0,2},{1,3},{2,0},{3,1},{4,6},{5,7},{6,4},{7,5},{8,10},{9,11},{10,... | collective-permute-start | bytes 884744 | tf_op jit(solution)/shard_map/ppermute | solution.py:20
  21.8 9.3 %collective-permute-done.2.refs_2_ = bf16[128,2048]{1,0:T(8,128)(2,1)S(1)} collective-permute-done((bf16[128,2048]{1,0:T(8,128)(2,1)S(1)}, bf16[128,2048]{1,0:T(8,128)(2,1)S(1)}, u32[]{:S(2)}, u32[]{:S(2)}) %collective-permute-start.2) | collective-permute-done | bytes 524320 | tf_op jit(solution)/shard_map/ppermute | solution.py:20
  31.1 1.5 collective-permute-done.1.refs_1_
  32.6 4.0 %project.3 = (bf16[2,3,384,128]{3,2,1,0:T(8,128)(2,1)S(1)}, bf16[2,3,384,128]{3,2,1,0:T(8,128)(2,1)S(1)}, bf16[384,2048]{1,0:T(8,128)(2,1)S(1)}) custom-call(s32[4]{0:T(128)S(1)} %pad_add_fusion.place, bf16[128,2048]{1,0:T(8,128)(2,1)S(1)} %collective-permute-done.refs_0_, bf16[128,2048]{1,0:T(8,128)(2,1)S(1)} %collective-permute-done.1.refs_1_, ...), custom_call_target="tpu_custom_call" | custom-call | flops 1 | bytes 1 | tf_op jit(solution)/shard_map/project/pallas_call | solution.py:87
  36.7 2.0 %collective-permute-done.5.refs_12_ = bf16[2,3,384,128]{3,2,1,0:T(8,128)(2,1)S(1)} collective-permute-done((bf16[2,3,384,128]{3,2,1,0:T(8,128)(2,1)S(1)}, bf16[2,3,384,128]{3,2,1,0:T(8,128)(2,1)S(1)}, u32[]{:S(2)}, u32[]{:S(2)}) %collective-permute-start.5) | collective-permute-done | bytes 589856 | tf_op jit(solution)/shard_map/ppermute | solution.py:20
  38.7 1.6 %collective-permute-start.13 = (bf16[1,3,384,128]{3,2,1,0:T(8,128)(2,1)S(1)}, bf16[1,3,384,128]{3,2,1,0:T(8,128)(2,1)S(1)}, u32[]{:S(2)}, u32[]{:S(2)}) collective-permute-start(bf16[1,3,384,128]{3,2,1,0:T(8,128)(2,1)S(1)} %add_convert_fusion.12), channel_id=1, source_target_pairs={{0,2},{1,3},{2,0},{3,1},{4,6},{5,7},{6,4},{7,5},{8,10},{9,11},{10,... | collective-permute-start | bytes 884744 | tf_op jit(solution)/shard_map/ppermute | solution.py:20
  41.6 1.3 collective-permute-start.8
  43.3 1.2 collective-permute-start.10
  44.5 4.1 %collective-permute-done.7.refs_2_ = bf16[96,128]{1,0:T(8,128)(2,1)S(1)} collective-permute-done((bf16[96,128]{1,0:T(8,128)(2,1)S(1)}, bf16[96,128]{1,0:T(8,128)(2,1)S(1)}, u32[]{:S(2)}, u32[]{:S(2)}) %collective-permute-start.7) | collective-permute-done | bytes 24608 | tf_op jit(solution)/shard_map/ppermute | solution.py:20
  48.6 1.4 collective-permute-start.11
  50.1 3.3 %collective-permute-done.11.refs_6_ = bf16[96,128]{1,0:T(8,128)(2,1)S(1)} collective-permute-done((bf16[96,128]{1,0:T(8,128)(2,1)S(1)}, bf16[96,128]{1,0:T(8,128)(2,1)S(1)}, u32[]{:S(2)}, u32[]{:S(2)}) %collective-permute-start.11) | collective-permute-done | bytes 24608 | tf_op jit(solution)/shard_map/ppermute | solution.py:20
  53.4 0.9 collective-permute-done.12.refs_7_
  54.2 1.6 %middle.1 = (bf16[3,384,128]{2,1,0:T(8,128)(2,1)S(1)}, bf16[3,384,128]{2,1,0:T(8,128)(2,1)S(1)}, bf16[128,128]{1,0:T(8,128)(2,1)S(1)}, bf16[128,128]{1,0:T(8,128...) custom-call(s32[4]{0:T(128)S(1)} %pad_add_fusion.place, ...), custom_call_target="tpu_custom_call" | custom-call | flops 1 | bytes 1 | tf_op jit(solution)/shard_map/middle/pallas_call | solution.py:254
  58.2 1.4 collective-permute-start.18
  59.6 1.0 collective-permute-start.19
  60.6 1.6 %collective-permute-done.18.refs_4_ = bf16[128,128]{1,0:T(8,128)(2,1)S(1)} collective-permute-done((bf16[128,128]{1,0:T(8,128)(2,1)S(1)}, bf16[128,128]{1,0:T(8,128)(2,1)S(1)}, u32[]{:S(2)}, u32[]{:S(2)}) %collective-permute-start.18) | collective-permute-done | bytes 32800 | tf_op jit(solution)/shard_map/ppermute | solution.py:20
  62.1 0.8 collective-permute-done.19.refs_5_
  63.0 3.5 %collective-permute-done.14.refs_2_.refs_1_ = bf16[3,384,128]{2,1,0:T(8,128)(2,1)S(1)} collective-permute-done((bf16[3,384,128]{2,1,0:T(8,128)(2,1)S(1)}, bf16[3,384,128]{2,1,0:T(8,128)(2,1)S(1)}, u32[]{:S(2)}, u32[]{:S(2)}) %collective-permute-start.14) | collective-permute-done | bytes 294944 | tf_op jit(solution)/shard_map/ppermute | solution.py:20
  66.5 1.6 %collective-permute-done.20.refs_3_ = bf16[3,384,128]{2,1,0:T(8,128)(2,1)S(1)} collective-permute-done((bf16[3,384,128]{2,1,0:T(8,128)(2,1)S(1)}, bf16[3,384,128]{2,1,0:T(8,128)(2,1)S(1)}, u32[]{:S(2)}, u32[]{:S(2)}) %collective-permute-start.20) | collective-permute-done | bytes 294944 | tf_op jit(solution)/shard_map/ppermute | solution.py:20
  68.0 0.8 collective-permute-start.21
  68.8 0.7 assemble.2.refs_0_
  69.6 0.7 copy-done.13
  70.3 0.7 copy-done.17
  71.0 1.3 input_grad.4
  72.3 1.4 collective-permute-start.23
  73.7 4.1 %input_grad.5 = (bf16[384,512]{1,0:T(8,128)(2,1)}, bf16[384,512]{1,0:T(8,128)(2,1)S(1)}, bf16[384,512]{1,0:T(8,128)(2,1)S(1)}) custom-call(s32[4]{0:T(128)S(1)} %pad_add_fusion.place, bf16[384,1536]{1,0:T(8,128)(2,1)S(1)} %assemble.2.refs_0_, bf16[3,512,2048]{2,1,0:T(8,128)(2,1)S(1)} %bitcast.9), custom_call_target="tpu_custom_call" | custom-call | flops 1 | bytes 1 | tf_op jit(solution)/shard_map/input_grad/pallas_call | solution.py:330
  77.9 0.8 collective-permute-start.24
  78.7 0.8 collective-permute-done.22.refs_3_.refs_2_
  79.5 0.7 assemble.3.refs_0_
  80.2 0.7 copy-done.9
  80.9 1.3 input_grad.6
  82.3 2.1 %collective-permute-done.23 = bf16[384,512]{1,0:T(8,128)(2,1)S(1)} collective-permute-done((bf16[384,512]{1,0:T(8,128)(2,1)S(1)}, bf16[384,512]{1,0:T(8,128)(2,1)S(1)}, u32[]{:S(2)}, u32[]{:S(2)}) %collective-permute-start.23) | collective-permute-done | bytes 393248 | tf_op jit(solution)/shard_map/ppermute | solution.py:20
  84.4 0.8 add_convert_fusion.11
  85.2 1.7 %collective-permute-start.25 = (bf16[384,512]{1,0:T(8,128)(2,1)}, bf16[384,512]{1,0:T(8,128)(2,1)}, u32[]{:S(2)}, u32[]{:S(2)}) collective-permute-start(bf16[384,512]{1,0:T(8,128)(2,1)} %add_convert_fusion.11), channel_id=1, source_target_pairs={{0,8},{8,0},{16,24},{24,16},{1,9},{9,1},{17,25},{25,17},{2,10},{10... | collective-permute-start | bytes 1179656 | tf_op jit(solution)/shard_map/ppermute | solution.py:20
  86.9 1.1 collective-permute-start.29
  88.1 0.9 collective-permute-start.26
  89.0 2.8 %copy-done.2 = bf16[512,3,2048]{2,0,1:T(8,128)(2,1)S(1)} copy-done((bf16[512,3,2048]{2,0,1:T(8,128)(2,1)S(1)}, bf16[512,3,2048]{2,0,1:T(8,128)(2,1)}, u32[]{:S(2)}) %copy-start.2) | copy-done | bytes 6291480
  91.8 3.4 %input_grad.7 = (bf16[384,512]{1,0:T(8,128)(2,1)S(1)}, bf16[384,512]{1,0:T(8,128)(2,1)S(1)}, bf16[384,512]{1,0:T(8,128)(2,1)S(1)}) custom-call(s32[4]{0:T(128)S(1)} %pad_add_fusion.place, bf16[384,1536]{1,0:T(8,128)(2,1)S(1)} %assemble.3.refs_0_, bf16[3,512,2048]{2,1,0:T(8,128)(2,1)S(1)} %bitcast.11), custom_call_target="tpu_custom_call" | custom-call | flops 1 | bytes 1 | tf_op jit(solution)/shard_map/input_grad/pallas_call | solution.py:330
  95.2 1.2 add_convert_fusion.10
  96.8 1.2 add_convert_fusion.9
  98.8 6.2 %weight_grad.2 = (f32[3,512,2048]{2,1,0:T(8,128)}, f32[8,128]{1,0:T(8,128)S(1)}) custom-call(s32[4]{0:T(128)S(1)} %pad_add_fusion.place, bf16[3,384,128]{2,1,0:T(8,128)(2,1)S(1)} %copy-done.8, bf16[3,384,128]{2,1,0:T(8,128)(2,1)S(1)} %collective-permute-done.14.refs_2_.refs_1_, bf16[3,384,128]{2,1,0:T(8,128)(2,1)S(1)} %copy-done.10, ...), custom_call_target="tpu_custom_call" | custom-call | flops 1 | bytes 1 | tf_op jit(solution)/shard_map/weight_grad/pallas_call | solution.py:400
  105.0 3.6 %collective-permute-done.26 = bf16[384,512]{1,0:T(8,128)(2,1)S(1)} collective-permute-done((bf16[384,512]{1,0:T(8,128)(2,1)}, bf16[384,512]{1,0:T(8,128)(2,1)S(1)}, u32[]{:S(2)}, u32[]{:S(2)}) %collective-permute-start.26) | collective-permute-done | bytes 393248 | tf_op jit(solution)/shard_map/ppermute | solution.py:20
  109.0 1.8 %collective-permute-start.30 = (bf16[384,512]{1,0:T(8,128)(2,1)S(1)}, bf16[384,512]{1,0:T(8,128)(2,1)S(1)}, u32[]{:S(2)}, u32[]{:S(2)}) collective-permute-start(bf16[384,512]{1,0:T(8,128)(2,1)S(1)} %get-tuple-element.128), channel_id=1, source_target_pairs={{0,8},{8,0},{16,24},{24,16},{1,9},{9,1},{17,25},{25,17},{2,10},{10... | collective-permute-start | bytes 1179656 | tf_op jit(solution)/shard_map/ppermute | solution.py:20
  111.5 6.2 %weight_grad.3 = (f32[3,512,2048]{2,1,0:T(8,128)}, f32[8,128]{1,0:T(8,128)S(1)}) custom-call(s32[4]{0:T(128)S(1)} %pad_add_fusion.place, f32[3,512,2048]{2,1,0:T(8,128)} %get-tuple-element.98.refs_0_, f32[8,128]{1,0:T(8,128)S(1)} %get-tuple-element.99.refs_1_, bf16[3,384,128]{2,1,0:T(8,128)(2,1)S(1)} %copy-done.12, ...), custom_call_target="tpu_custom_call", output_to_operand_aliasing={{0}: (1, {})} | custom-call | flops 1 | bytes 1 | tf_op jit(solution)/shard_map/weight_grad/pallas_call | solution.py:400
  117.8 1.3 collective-permute-done.30
  119.4 4.7 %collective-permute-start.32 = (bf16[384,512]{1,0:T(8,128)(2,1)S(1)}, bf16[384,512]{1,0:T(8,128)(2,1)S(1)}, u32[]{:S(2)}, u32[]{:S(2)}) collective-permute-start(bf16[384,512]{1,0:T(8,128)(2,1)S(1)} %get-tuple-element.126), channel_id=1, source_target_pairs={{0,8},{8,0},{16,24},{24,16},{1,9},{9,1},{17,25},{25,17},{2,10},{10... | collective-permute-start | bytes 1179656 | tf_op jit(solution)/shard_map/ppermute | solution.py:20
  124.7 6.7 %collective-permute-done.32 = bf16[384,512]{1,0:T(8,128)(2,1)S(1)} collective-permute-done((bf16[384,512]{1,0:T(8,128)(2,1)S(1)}, bf16[384,512]{1,0:T(8,128)(2,1)S(1)}, u32[]{:S(2)}, u32[]{:S(2)}) %collective-permute-start.32) | collective-permute-done | bytes 393248 | tf_op jit(solution)/shard_map/ppermute | solution.py:20
  131.5 0.7 collective-permute-start.34
  132.4 4.5 %collective-permute-start.39 = (bf16[384,512]{1,0:T(8,128)(2,1)S(1)}, bf16[384,512]{1,0:T(8,128)(2,1)S(1)}, u32[]{:S(2)}, u32[]{:S(2)}) collective-permute-start(bf16[384,512]{1,0:T(8,128)(2,1)S(1)} %add_convert_fusion.1), channel_id=1, source_target_pairs={{0,8},{8,0},{16,24},{24,16},{1,9},{9,1},{17,25},{25,17},{2,10},{10... | collective-permute-start | bytes 1179656 | tf_op jit(solution)/shard_map/ppermute | solution.py:20
  137.0 6.7 %collective-permute-start.40 = (bf16[384,512]{1,0:T(8,128)(2,1)S(1)}, bf16[384,512]{1,0:T(8,128)(2,1)S(1)}, u32[]{:S(2)}, u32[]{:S(2)}) collective-permute-start(bf16[384,512]{1,0:T(8,128)(2,1)S(1)} %add_convert_fusion), channel_id=1, source_target_pairs={{0,8},{8,0},{16,24},{24,16},{1,9},{9,1},{17,25},{25,17},{2,10},{10... | collective-permute-start | bytes 1179656 | tf_op jit(solution)/shard_map/ppermute | solution.py:20
  143.7 1.2 collective-permute-start.35
  144.9 1.5 collective-permute-start.37
  146.4 1.8 %collective-permute-start.38 = (bf16[128,128]{1,0:T(8,128)(2,1)S(1)}, bf16[128,128]{1,0:T(8,128)(2,1)S(1)}, u32[]{:S(2)}, u32[]{:S(2)}) collective-permute-start(bf16[128,128]{1,0:T(8,128)(2,1)S(1)} %get-tuple-element.122), channel_id=1, source_target_pairs={{0,7},{1,6},{2,5},{3,4},{4,3},{5,2},{6,1},{7,0},{8,15},{9,14},{10,... | collective-permute-start | bytes 98312 | tf_op jit(solution)/shard_map/ppermute | solution.py:20
  148.4 1.6 %collective-permute-done.37.refs_6_ = bf16[128,128]{1,0:T(8,128)(2,1)S(1)} collective-permute-done((bf16[128,128]{1,0:T(8,128)(2,1)S(1)}, bf16[128,128]{1,0:T(8,128)(2,1)S(1)}, u32[]{:S(2)}, u32[]{:S(2)}) %collective-permute-start.37) | collective-permute-done | bytes 32800 | tf_op jit(solution)/shard_map/ppermute | solution.py:20
  150.6 1.4 join.1
  152.0 1.4 pad_maximum_fusion
  (107 shorter events, 9.2 us)
Async XLA Ops:
  1.7 15.0 %collective-permute-start = (bf16[128,2048]{1,0:T(8,128)(2,1)S(1)}, bf16[128,2048]{1,0:T(8,128)(2,1)S(1)}, u32[]{:S(2)}, u32[]{:S(2)}) collective-permute-start(bf16[128,2048]{1,0:T(8,128)(2,1)S(1)} %constant_dynamic-slice_fusion), channel_id=1, source_target_pairs={{0,4},{4,0},{1,5},{5,1},{2,6},{6,2},{3,7},{7,3},{8,12},{12,8},{9,1... | collective-permute-start | bytes 1572872 | tf_op jit(solution)/shard_map/ppermute | solution.py:20
  4.8 2.8 %copy-start = (bf16[512,3,2048]{2,0,1:T(8,128)(2,1)S(1)}, bf16[512,3,2048]{2,0,1:T(8,128)(2,1)}, u32[]{:S(2)}) copy-start(bf16[512,3,2048]{2,0,1:T(8,128)(2,1)} %param.5) | copy-start | bytes 18874372
  7.6 1.4 copy-start.3
  9.0 7.7 %copy-start.4 = (bf16[384,2048]{1,0:T(8,128)(2,1)S(1)}, bf16[384,2048]{1,0:T(8,128)(2,1)}, u32[]{:S(2)}) copy-start(bf16[384,2048]{1,0:T(8,128)(2,1)} %refs_6_.1) | copy-start | bytes 4718596
  9.0 23.6 %copy-start.1 = (bf16[512,3,2048]{2,0,1:T(8,128)(2,1)S(1)}, bf16[512,3,2048]{2,0,1:T(8,128)(2,1)}, u32[]{:S(2)}) copy-start(bf16[512,3,2048]{2,0,1:T(8,128)(2,1)} %param.5) | copy-start | bytes 18874372
  16.7 3.4 %collective-permute-start.3 = (bf16[2,3,384,128]{3,2,1,0:T(8,128)(2,1)S(1)}, bf16[2,3,384,128]{3,2,1,0:T(8,128)(2,1)S(1)}, u32[]{:S(2)}, u32[]{:S(2)}) collective-permute-start(bf16[2,3,384,128]{3,2,1,0:T(8,128)(2,1)S(1)} %get-tuple-element.69), channel_id=1, source_target_pairs={{0,1},{1,0},{2,3},{3,2},{4,5},{5,4},{6,7},{7,6},{8,9},{9,8},{10,11... | collective-permute-start | bytes 1769480 | tf_op jit(solution)/shard_map/ppermute | solution.py:20
  16.7 14.4 %collective-permute-start.2 = (bf16[128,2048]{1,0:T(8,128)(2,1)S(1)}, bf16[128,2048]{1,0:T(8,128)(2,1)S(1)}, u32[]{:S(2)}, u32[]{:S(2)}) collective-permute-start(bf16[128,2048]{1,0:T(8,128)(2,1)S(1)} %slice.15), channel_id=1, source_target_pairs={{0,4},{4,0},{1,5},{5,1},{2,6},{6,2},{3,7},{7,3},{8,12},{12,8},{9,1... | collective-permute-start | bytes 1572872 | tf_op jit(solution)/shard_map/ppermute | solution.py:20
  18.5 14.1 %collective-permute-start.1 = (bf16[128,2048]{1,0:T(8,128)(2,1)S(1)}, bf16[128,2048]{1,0:T(8,128)(2,1)S(1)}, u32[]{:S(2)}, u32[]{:S(2)}) collective-permute-start(bf16[128,2048]{1,0:T(8,128)(2,1)S(1)} %collective-permute-done.refs_0_), channel_id=1, source_target_pairs={{0,8},{8,0},{16,24},{24,16},{1,9},{9,1},{17,25},{25,17},{2,10},{10... | collective-permute-start | bytes 1572872 | tf_op jit(solution)/shard_map/ppermute | solution.py:20
  20.2 20.1 %copy-start.19 = (bf16[96,1024]{1,0:T(8,128)(2,1)S(1)}, bf16[96,1024]{1,0:T(8,128)(2,1)}, u32[]{:S(2)}) copy-start(bf16[96,1024]{1,0:T(8,128)(2,1)} %up_ref) | copy-start | bytes 589828
  20.2 34.0 %copy-start.20 = (f32[7,64]{1,0:T(8,128)S(1)}, f32[7,64]{1,0:T(8,128)}, u32[]{:S(2)}) copy-start(f32[7,64]{1,0:T(8,128)} %taps_ref.1) | copy-start | bytes 5380
  20.2 10.9 %collective-permute-start.4 = (bf16[1,3,384,128]{3,2,1,0:T(8,128)(2,1)S(1)}, bf16[1,3,384,128]{3,2,1,0:T(8,128)(2,1)S(1)}, u32[]{:S(2)}, u32[]{:S(2)}) collective-permute-start(bf16[1,3,384,128]{3,2,1,0:T(8,128)(2,1)S(1)} %add_convert_fusion.13), channel_id=1, source_target_pairs={{0,2},{1,3},{2,0},{3,1},{4,6},{5,7},{6,4},{7,5},{8,10},{9,11},{10,... | collective-permute-start | bytes 884744 | tf_op jit(solution)/shard_map/ppermute | solution.py:20
  36.6 19.2 %copy-start.5 = (bf16[384,2048]{1,0:T(8,128)(2,1)}, bf16[384,2048]{1,0:T(8,128)(2,1)S(1)}, u32[]{:S(2)}) copy-start(bf16[384,2048]{1,0:T(8,128)(2,1)S(1)} %get-tuple-element.97.refs_5_.refs_7_) | copy-start | bytes 4718596
  36.6 2.1 %collective-permute-start.5 = (bf16[2,3,384,128]{3,2,1,0:T(8,128)(2,1)S(1)}, bf16[2,3,384,128]{3,2,1,0:T(8,128)(2,1)S(1)}, u32[]{:S(2)}, u32[]{:S(2)}) collective-permute-start(bf16[2,3,384,128]{3,2,1,0:T(8,128)(2,1)S(1)} %get-tuple-element.72), channel_id=1, source_target_pairs={{0,1},{1,0},{2,3},{3,2},{4,5},{5,4},{6,7},{7,6},{8,9},{9,8},{10,11... | collective-permute-start | bytes 1769480 | tf_op jit(solution)/shard_map/ppermute | solution.py:20
  38.7 15.5 %collective-permute-start.13 = (bf16[1,3,384,128]{3,2,1,0:T(8,128)(2,1)S(1)}, bf16[1,3,384,128]{3,2,1,0:T(8,128)(2,1)S(1)}, u32[]{:S(2)}, u32[]{:S(2)}) collective-permute-start(bf16[1,3,384,128]{3,2,1,0:T(8,128)(2,1)S(1)} %add_convert_fusion.12), channel_id=1, source_target_pairs={{0,2},{1,3},{2,0},{3,1},{4,6},{5,7},{6,4},{7,5},{8,10},{9,11},{10,... | collective-permute-start | bytes 884744 | tf_op jit(solution)/shard_map/ppermute | solution.py:20
  40.9 2.5 %collective-permute-start.6 = (bf16[96,128]{1,0:T(8,128)(2,1)S(1)}, bf16[96,128]{1,0:T(8,128)(2,1)S(1)}, u32[]{:S(2)}, u32[]{:S(2)}) collective-permute-start(bf16[96,128]{1,0:T(8,128)(2,1)S(1)} %get-tuple-element.75), channel_id=1, source_target_pairs={{0,1},{1,0},{2,3},{3,2},{4,5},{5,4},{6,7},{7,6},{8,9},{9,8},{10,11... | collective-permute-start | bytes 73736 | tf_op jit(solution)/shard_map/ppermute | solution.py:20
  41.0 7.7 %collective-permute-start.7 = (bf16[96,128]{1,0:T(8,128)(2,1)S(1)}, bf16[96,128]{1,0:T(8,128)(2,1)S(1)}, u32[]{:S(2)}, u32[]{:S(2)}) collective-permute-start(bf16[96,128]{1,0:T(8,128)(2,1)S(1)} %get-tuple-element.76), channel_id=1, source_target_pairs={{0,2},{1,3},{2,0},{3,1},{4,6},{5,7},{6,4},{7,5},{8,10},{9,11},{10,... | collective-permute-start | bytes 73736 | tf_op jit(solution)/shard_map/ppermute | solution.py:20
  41.6 8.5 %collective-permute-start.8 = (bf16[96,128]{1,0:T(8,128)(2,1)S(1)}, bf16[96,128]{1,0:T(8,128)(2,1)S(1)}, u32[]{:S(2)}, u32[]{:S(2)}) collective-permute-start(bf16[96,128]{1,0:T(8,128)(2,1)S(1)} %get-tuple-element.77), channel_id=1, source_target_pairs={{0,3},{1,2},{2,1},{3,0},{4,7},{5,6},{6,5},{7,4},{8,11},{9,10},{10,... | collective-permute-start | bytes 73736 | tf_op jit(solution)/shard_map/ppermute | solution.py:20
  42.8 7.2 %collective-permute-start.9 = (bf16[96,128]{1,0:T(8,128)(2,1)S(1)}, bf16[96,128]{1,0:T(8,128)(2,1)S(1)}, u32[]{:S(2)}, u32[]{:S(2)}) collective-permute-start(bf16[96,128]{1,0:T(8,128)(2,1)S(1)} %get-tuple-element.78), channel_id=1, source_target_pairs={{0,4},{1,5},{2,6},{3,7},{4,0},{5,1},{6,2},{7,3},{8,12},{9,13},{10,... | collective-permute-start | bytes 73736 | tf_op jit(solution)/shard_map/ppermute | solution.py:20
  43.3 6.7 %collective-permute-start.10 = (bf16[96,128]{1,0:T(8,128)(2,1)S(1)}, bf16[96,128]{1,0:T(8,128)(2,1)S(1)}, u32[]{:S(2)}, u32[]{:S(2)}) collective-permute-start(bf16[96,128]{1,0:T(8,128)(2,1)S(1)} %get-tuple-element.79), channel_id=1, source_target_pairs={{0,5},{1,4},{2,7},{3,6},{4,1},{5,0},{6,3},{7,2},{8,13},{9,12},{10,... | collective-permute-start | bytes 73736 | tf_op jit(solution)/shard_map/ppermute | solution.py:20
  48.6 4.7 %collective-permute-start.11 = (bf16[96,128]{1,0:T(8,128)(2,1)S(1)}, bf16[96,128]{1,0:T(8,128)(2,1)S(1)}, u32[]{:S(2)}, u32[]{:S(2)}) collective-permute-start(bf16[96,128]{1,0:T(8,128)(2,1)S(1)} %get-tuple-element.80), channel_id=1, source_target_pairs={{0,6},{1,7},{2,4},{3,5},{4,2},{5,3},{6,0},{7,1},{8,14},{9,15},{10,... | collective-permute-start | bytes 73736 | tf_op jit(solution)/shard_map/ppermute | solution.py:20
  50.1 4.2 %collective-permute-start.12 = (bf16[96,128]{1,0:T(8,128)(2,1)S(1)}, bf16[96,128]{1,0:T(8,128)(2,1)S(1)}, u32[]{:S(2)}, u32[]{:S(2)}) collective-permute-start(bf16[96,128]{1,0:T(8,128)(2,1)S(1)} %get-tuple-element.81), channel_id=1, source_target_pairs={{0,7},{1,6},{2,5},{3,4},{4,3},{5,2},{6,1},{7,0},{8,15},{9,14},{10,... | collective-permute-start | bytes 73736 | tf_op jit(solution)/shard_map/ppermute | solution.py:20
  57.0 22.4 %copy-start.11 = (bf16[3,384,128]{2,1,0:T(8,128)(2,1)}, bf16[3,384,128]{2,1,0:T(8,128)(2,1)S(1)}, u32[]{:S(2)}) copy-start(bf16[3,384,128]{2,1,0:T(8,128)(2,1)S(1)} %get-tuple-element.105.refs_0_.refs_2_) | copy-start | bytes 884740
  57.0 5.9 %collective-permute-start.15 = (bf16[3,384,128]{2,1,0:T(8,128)(2,1)S(1)}, bf16[3,384,128]{2,1,0:T(8,128)(2,1)S(1)}, u32[]{:S(2)}, u32[]{:S(2)}) collective-permute-start(bf16[3,384,128]{2,1,0:T(8,128)(2,1)S(1)} %get-tuple-element.105.refs_0_.refs_2_), channel_id=1, source_target_pairs={{0,1},{1,0},{2,3},{3,2},{4,5},{5,4},{6,7},{7,6},{8,9},{9,8},{10,11... | collective-permute-start | bytes 884744 | tf_op jit(solution)/shard_map/ppermute | solution.py:20
  57.0 5.9 %collective-permute-start.16 = (bf16[3,384,128]{2,1,0:T(8,128)(2,1)S(1)}, bf16[3,384,128]{2,1,0:T(8,128)(2,1)S(1)}, u32[]{:S(2)}, u32[]{:S(2)}) collective-permute-start(bf16[3,384,128]{2,1,0:T(8,128)(2,1)S(1)} %get-tuple-element.83.refs_0_.refs_3_), channel_id=1, source_target_pairs={{0,1},{1,0},{2,3},{3,2},{4,5},{5,4},{6,7},{7,6},{8,9},{9,8},{10,11... | collective-permute-start | bytes 884744 | tf_op jit(solution)/shard_map/ppermute | solution.py:20
  57.5 8.9 %collective-permute-start.14 = (bf16[3,384,128]{2,1,0:T(8,128)(2,1)S(1)}, bf16[3,384,128]{2,1,0:T(8,128)(2,1)S(1)}, u32[]{:S(2)}, u32[]{:S(2)}) collective-permute-start(bf16[3,384,128]{2,1,0:T(8,128)(2,1)S(1)} %get-tuple-element.83.refs_0_.refs_3_), channel_id=1, source_target_pairs={{0,2},{1,3},{2,0},{3,1},{4,6},{5,7},{6,4},{7,5},{8,10},{9,11},{10,... | collective-permute-start | bytes 884744 | tf_op jit(solution)/shard_map/ppermute | solution.py:20
  58.2 1.4 collective-permute-start.17
  58.2 3.9 %collective-permute-start.18 = (bf16[128,128]{1,0:T(8,128)(2,1)S(1)}, bf16[128,128]{1,0:T(8,128)(2,1)S(1)}, u32[]{:S(2)}, u32[]{:S(2)}) collective-permute-start(bf16[128,128]{1,0:T(8,128)(2,1)S(1)} %get-tuple-element.85), channel_id=1, source_target_pairs={{0,4},{1,5},{2,6},{3,7},{4,0},{5,1},{6,2},{7,3},{8,12},{9,13},{10,... | collective-permute-start | bytes 98312 | tf_op jit(solution)/shard_map/ppermute | solution.py:20
  59.6 3.3 %collective-permute-start.19 = (bf16[128,128]{1,0:T(8,128)(2,1)S(1)}, bf16[128,128]{1,0:T(8,128)(2,1)S(1)}, u32[]{:S(2)}, u32[]{:S(2)}) collective-permute-start(bf16[128,128]{1,0:T(8,128)(2,1)S(1)} %get-tuple-element.86), channel_id=1, source_target_pairs={{0,5},{1,4},{2,7},{3,6},{4,1},{5,0},{6,3},{7,2},{8,13},{9,12},{10,... | collective-permute-start | bytes 98312 | tf_op jit(solution)/shard_map/ppermute | solution.py:20
  63.0 16.5 %copy-start.15 = (bf16[3,384,128]{2,1,0:T(8,128)(2,1)}, bf16[3,384,128]{2,1,0:T(8,128)(2,1)S(1)}, u32[]{:S(2)}) copy-start(bf16[3,384,128]{2,1,0:T(8,128)(2,1)S(1)} %collective-permute-done.15.refs_1_.refs_4_) | copy-start | bytes 884740
  66.5 1.6 %collective-permute-start.20 = (bf16[3,384,128]{2,1,0:T(8,128)(2,1)S(1)}, bf16[3,384,128]{2,1,0:T(8,128)(2,1)S(1)}, u32[]{:S(2)}, u32[]{:S(2)}) collective-permute-start(bf16[3,384,128]{2,1,0:T(8,128)(2,1)S(1)} %collective-permute-done.14.refs_2_.refs_1_), channel_id=1, source_target_pairs={{0,1},{1,0},{2,3},{3,2},{4,5},{5,4},{6,7},{7,6},{8,9},{9,8},{10,11... | collective-permute-start | bytes 884744 | tf_op jit(solution)/shard_map/ppermute | solution.py:20
  68.0 9.8 %collective-permute-start.21 = (bf16[3,384,128]{2,1,0:T(8,128)(2,1)S(1)}, bf16[3,384,128]{2,1,0:T(8,128)(2,1)S(1)}, u32[]{:S(2)}, u32[]{:S(2)}) collective-permute-start(bf16[3,384,128]{2,1,0:T(8,128)(2,1)S(1)} %get-tuple-element.105.refs_0_.refs_2_), channel_id=1, source_target_pairs={{0,2},{1,3},{2,0},{3,1},{4,6},{5,7},{6,4},{7,5},{8,10},{9,11},{10,... | collective-permute-start | bytes 884744 | tf_op jit(solution)/shard_map/ppermute | solution.py:20
  70.3 0.7 copy-start.17
  72.3 12.1 %collective-permute-start.23 = (bf16[384,512]{1,0:T(8,128)(2,1)S(1)}, bf16[384,512]{1,0:T(8,128)(2,1)S(1)}, u32[]{:S(2)}, u32[]{:S(2)}) collective-permute-start(bf16[384,512]{1,0:T(8,128)(2,1)S(1)} %input_grad.4), channel_id=1, source_target_pairs={{0,4},{4,0},{1,5},{5,1},{2,6},{6,2},{3,7},{7,3},{8,12},{12,8},{9,1... | collective-permute-start | bytes 1179656 | tf_op jit(solution)/shard_map/ppermute | solution.py:20
  77.8 4.5 %copy-start.21 = (bf16[384,512]{1,0:T(8,128)(2,1)}, bf16[384,512]{1,0:T(8,128)(2,1)S(1)}, u32[]{:S(2)}) copy-start(bf16[384,512]{1,0:T(8,128)(2,1)S(1)} %get-tuple-element.90) | copy-start | bytes 1179652
  77.8 4.5 %copy-start.22 = (bf16[384,512]{1,0:T(8,128)(2,1)}, bf16[384,512]{1,0:T(8,128)(2,1)S(1)}, u32[]{:S(2)}) copy-start(bf16[384,512]{1,0:T(8,128)(2,1)S(1)} %get-tuple-element.102) | copy-start | bytes 1179652
  77.8 4.5 %copy-start.7 = (bf16[3,384,128]{2,1,0:T(8,128)(2,1)}, bf16[3,384,128]{2,1,0:T(8,128)(2,1)S(1)}, u32[]{:S(2)}) copy-start(bf16[3,384,128]{2,1,0:T(8,128)(2,1)S(1)} %collective-permute-done.21.refs_2_.refs_0_) | copy-start | bytes 884740
  77.8 1.6 %collective-permute-start.22 = (bf16[3,384,128]{2,1,0:T(8,128)(2,1)S(1)}, bf16[3,384,128]{2,1,0:T(8,128)(2,1)S(1)}, u32[]{:S(2)}, u32[]{:S(2)}) collective-permute-start(bf16[3,384,128]{2,1,0:T(8,128)(2,1)S(1)} %collective-permute-done.21.refs_2_.refs_0_), channel_id=1, source_target_pairs={{0,1},{1,0},{2,3},{3,2},{4,5},{5,4},{6,7},{7,6},{8,9},{9,8},{10,11... | collective-permute-start | bytes 884744 | tf_op jit(solution)/shard_map/ppermute | solution.py:20
  77.9 17.3 %collective-permute-start.24 = (bf16[384,512]{1,0:T(8,128)(2,1)}, bf16[384,512]{1,0:T(8,128)(2,1)}, u32[]{:S(2)}, u32[]{:S(2)}) collective-permute-start(bf16[384,512]{1,0:T(8,128)(2,1)} %get-tuple-element.94), channel_id=1, source_target_pairs={{0,4},{4,0},{1,5},{5,1},{2,6},{6,2},{3,7},{7,3},{8,12},{12,8},{9,1... | collective-permute-start | bytes 1179656 | tf_op jit(solution)/shard_map/ppermute | solution.py:20
  85.2 11.6 %collective-permute-start.25 = (bf16[384,512]{1,0:T(8,128)(2,1)}, bf16[384,512]{1,0:T(8,128)(2,1)}, u32[]{:S(2)}, u32[]{:S(2)}) collective-permute-start(bf16[384,512]{1,0:T(8,128)(2,1)} %add_convert_fusion.11), channel_id=1, source_target_pairs={{0,8},{8,0},{16,24},{24,16},{1,9},{9,1},{17,25},{25,17},{2,10},{10... | collective-permute-start | bytes 1179656 | tf_op jit(solution)/shard_map/ppermute | solution.py:20
  86.9 30.7 %collective-permute-start.29 = (bf16[384,512]{1,0:T(8,128)(2,1)}, bf16[384,512]{1,0:T(8,128)(2,1)S(1)}, u32[]{:S(2)}, u32[]{:S(2)}) collective-permute-start(bf16[384,512]{1,0:T(8,128)(2,1)} %copy-done.21), channel_id=1, source_target_pairs={{0,4},{4,0},{1,5},{5,1},{2,6},{6,2},{3,7},{7,3},{8,12},{12,8},{9,1... | collective-permute-start | bytes 1179656 | tf_op jit(solution)/shard_map/ppermute | solution.py:20
  88.1 20.4 %collective-permute-start.26 = (bf16[384,512]{1,0:T(8,128)(2,1)}, bf16[384,512]{1,0:T(8,128)(2,1)S(1)}, u32[]{:S(2)}, u32[]{:S(2)}) collective-permute-start(bf16[384,512]{1,0:T(8,128)(2,1)} %copy-done.22), channel_id=1, source_target_pairs={{0,4},{4,0},{1,5},{5,1},{2,6},{6,2},{3,7},{7,3},{8,12},{12,8},{9,1... | collective-permute-start | bytes 1179656 | tf_op jit(solution)/shard_map/ppermute | solution.py:20
  89.0 2.8 %copy-start.2 = (bf16[512,3,2048]{2,0,1:T(8,128)(2,1)S(1)}, bf16[512,3,2048]{2,0,1:T(8,128)(2,1)}, u32[]{:S(2)}) copy-start(bf16[512,3,2048]{2,0,1:T(8,128)(2,1)} %param.5) | copy-start | bytes 18874372
  95.2 3.6 %copy-start.6 = (bf16[384,2048]{1,0:T(8,128)(2,1)S(1)}, bf16[384,2048]{1,0:T(8,128)(2,1)}, u32[]{:S(2)}) copy-start(bf16[384,2048]{1,0:T(8,128)(2,1)} %copy-done.5) | copy-start | bytes 4718596
  95.2 3.6 %copy-start.8 = (bf16[3,384,128]{2,1,0:T(8,128)(2,1)S(1)}, bf16[3,384,128]{2,1,0:T(8,128)(2,1)}, u32[]{:S(2)}) copy-start(bf16[3,384,128]{2,1,0:T(8,128)(2,1)} %copy-done.7) | copy-start | bytes 884740
  95.2 3.6 %copy-start.10 = (bf16[3,384,128]{2,1,0:T(8,128)(2,1)S(1)}, bf16[3,384,128]{2,1,0:T(8,128)(2,1)}, u32[]{:S(2)}) copy-start(bf16[3,384,128]{2,1,0:T(8,128)(2,1)} %copy-done.9) | copy-start | bytes 884740
  96.5 12.2 %collective-permute-start.27 = (bf16[384,512]{1,0:T(8,128)(2,1)S(1)}, bf16[384,512]{1,0:T(8,128)(2,1)S(1)}, u32[]{:S(2)}, u32[]{:S(2)}) collective-permute-start(bf16[384,512]{1,0:T(8,128)(2,1)S(1)} %add_convert_fusion.10), channel_id=1, source_target_pairs={{0,8},{8,0},{16,24},{24,16},{1,9},{9,1},{17,25},{25,17},{2,10},{10... | collective-permute-start | bytes 1179656 | tf_op jit(solution)/shard_map/ppermute | solution.py:20
  98.0 10.8 %collective-permute-start.28 = (bf16[384,512]{1,0:T(8,128)(2,1)S(1)}, bf16[384,512]{1,0:T(8,128)(2,1)S(1)}, u32[]{:S(2)}, u32[]{:S(2)}) collective-permute-start(bf16[384,512]{1,0:T(8,128)(2,1)S(1)} %add_convert_fusion.9), channel_id=1, source_target_pairs={{0,0},{8,16},{16,8},{24,24},{1,1},{9,17},{17,9},{25,25},{2,2},{10,... | collective-permute-start | bytes 1179656 | tf_op jit(solution)/shard_map/ppermute | solution.py:532
  108.6 2.8 %copy-start.12 = (bf16[3,384,128]{2,1,0:T(8,128)(2,1)S(1)}, bf16[3,384,128]{2,1,0:T(8,128)(2,1)}, u32[]{:S(2)}) copy-start(bf16[3,384,128]{2,1,0:T(8,128)(2,1)} %copy-done.11) | copy-start | bytes 884740
  108.6 2.8 %copy-start.14 = (bf16[3,384,128]{2,1,0:T(8,128)(2,1)S(1)}, bf16[3,384,128]{2,1,0:T(8,128)(2,1)}, u32[]{:S(2)}) copy-start(bf16[3,384,128]{2,1,0:T(8,128)(2,1)} %copy-done.13) | copy-start | bytes 884740
  108.7 2.8 %copy-start.16 = (bf16[3,384,128]{2,1,0:T(8,128)(2,1)S(1)}, bf16[3,384,128]{2,1,0:T(8,128)(2,1)}, u32[]{:S(2)}) copy-start(bf16[3,384,128]{2,1,0:T(8,128)(2,1)} %copy-done.15) | copy-start | bytes 884740
  108.7 2.8 %copy-start.18 = (bf16[3,384,128]{2,1,0:T(8,128)(2,1)S(1)}, bf16[3,384,128]{2,1,0:T(8,128)(2,1)}, u32[]{:S(2)}) copy-start(bf16[3,384,128]{2,1,0:T(8,128)(2,1)} %copy-done.17) | copy-start | bytes 884740
  109.0 10.1 %collective-permute-start.30 = (bf16[384,512]{1,0:T(8,128)(2,1)S(1)}, bf16[384,512]{1,0:T(8,128)(2,1)S(1)}, u32[]{:S(2)}, u32[]{:S(2)}) collective-permute-start(bf16[384,512]{1,0:T(8,128)(2,1)S(1)} %get-tuple-element.128), channel_id=1, source_target_pairs={{0,8},{8,0},{16,24},{24,16},{1,9},{9,1},{17,25},{25,17},{2,10},{10... | collective-permute-start | bytes 1179656 | tf_op jit(solution)/shard_map/ppermute | solution.py:20
  110.8 8.4 %collective-permute-start.31 = (bf16[384,512]{1,0:T(8,128)(2,1)S(1)}, bf16[384,512]{1,0:T(8,128)(2,1)S(1)}, u32[]{:S(2)}, u32[]{:S(2)}) collective-permute-start(bf16[384,512]{1,0:T(8,128)(2,1)S(1)} %add_convert_fusion.7), channel_id=1, source_target_pairs={{0,0},{8,16},{16,8},{24,24},{1,1},{9,17},{17,9},{25,25},{2,2},{10,... | collective-permute-start | bytes 1179656 | tf_op jit(solution)/shard_map/ppermute | solution.py:532
  119.4 12.0 %collective-permute-start.32 = (bf16[384,512]{1,0:T(8,128)(2,1)S(1)}, bf16[384,512]{1,0:T(8,128)(2,1)S(1)}, u32[]{:S(2)}, u32[]{:S(2)}) collective-permute-start(bf16[384,512]{1,0:T(8,128)(2,1)S(1)} %get-tuple-element.126), channel_id=1, source_target_pairs={{0,8},{8,0},{16,24},{24,16},{1,9},{9,1},{17,25},{25,17},{2,10},{10... | collective-permute-start | bytes 1179656 | tf_op jit(solution)/shard_map/ppermute | solution.py:20
  124.1 8.2 %collective-permute-start.33 = (bf16[384,512]{1,0:T(8,128)(2,1)S(1)}, bf16[384,512]{1,0:T(8,128)(2,1)S(1)}, u32[]{:S(2)}, u32[]{:S(2)}) collective-permute-start(bf16[384,512]{1,0:T(8,128)(2,1)S(1)} %add_convert_fusion.4), channel_id=1, source_target_pairs={{0,0},{8,16},{16,8},{24,24},{1,1},{9,17},{17,9},{25,25},{2,2},{10,... | collective-permute-start | bytes 1179656 | tf_op jit(solution)/shard_map/ppermute | solution.py:532
  131.5 5.4 %collective-permute-start.34 = (bf16[384,512]{1,0:T(8,128)(2,1)S(1)}, bf16[384,512]{1,0:T(8,128)(2,1)S(1)}, u32[]{:S(2)}, u32[]{:S(2)}) collective-permute-start(bf16[384,512]{1,0:T(8,128)(2,1)S(1)} %add_convert_fusion.2), channel_id=1, source_target_pairs={{0,0},{8,16},{16,8},{24,24},{1,1},{9,17},{17,9},{25,25},{2,2},{10,... | collective-permute-start | bytes 1179656 | tf_op jit(solution)/shard_map/ppermute | solution.py:532
  132.3 11.4 %copy-start.26 = (bf16[128,128]{1,0:T(8,128)(2,1)S(1)}, bf16[128,128]{1,0:T(8,128)(2,1)}, u32[]{:S(2)}) copy-start(bf16[128,128]{1,0:T(8,128)(2,1)} %copy-done.25) | copy-start | bytes 98308
  132.3 12.6 %copy-start.24 = (bf16[128,128]{1,0:T(8,128)(2,1)S(1)}, bf16[128,128]{1,0:T(8,128)(2,1)}, u32[]{:S(2)}) copy-start(bf16[128,128]{1,0:T(8,128)(2,1)} %copy-done.23) | copy-start | bytes 98308
  132.4 14.0 %collective-permute-start.39 = (bf16[384,512]{1,0:T(8,128)(2,1)S(1)}, bf16[384,512]{1,0:T(8,128)(2,1)S(1)}, u32[]{:S(2)}, u32[]{:S(2)}) collective-permute-start(bf16[384,512]{1,0:T(8,128)(2,1)S(1)} %add_convert_fusion.1), channel_id=1, source_target_pairs={{0,8},{8,0},{16,24},{24,16},{1,9},{9,1},{17,25},{25,17},{2,10},{10... | collective-permute-start | bytes 1179656 | tf_op jit(solution)/shard_map/ppermute | solution.py:20
  137.0 15.0 %collective-permute-start.40 = (bf16[384,512]{1,0:T(8,128)(2,1)S(1)}, bf16[384,512]{1,0:T(8,128)(2,1)S(1)}, u32[]{:S(2)}, u32[]{:S(2)}) collective-permute-start(bf16[384,512]{1,0:T(8,128)(2,1)S(1)} %add_convert_fusion), channel_id=1, source_target_pairs={{0,8},{8,0},{16,24},{24,16},{1,9},{9,1},{17,25},{25,17},{2,10},{10... | collective-permute-start | bytes 1179656 | tf_op jit(solution)/shard_map/ppermute | solution.py:20
  143.7 4.5 %collective-permute-start.35 = (bf16[128,128]{1,0:T(8,128)(2,1)S(1)}, bf16[128,128]{1,0:T(8,128)(2,1)S(1)}, u32[]{:S(2)}, u32[]{:S(2)}) collective-permute-start(bf16[128,128]{1,0:T(8,128)(2,1)S(1)} %copy-done.26), channel_id=1, source_target_pairs={{0,2},{1,3},{2,0},{3,1},{4,6},{5,7},{6,4},{7,5},{8,10},{9,11},{10,... | collective-permute-start | bytes 98312 | tf_op jit(solution)/shard_map/ppermute | solution.py:20
  144.9 3.5 %collective-permute-start.36 = (bf16[128,128]{1,0:T(8,128)(2,1)S(1)}, bf16[128,128]{1,0:T(8,128)(2,1)S(1)}, u32[]{:S(2)}, u32[]{:S(2)}) collective-permute-start(bf16[128,128]{1,0:T(8,128)(2,1)S(1)} %copy-done.24), channel_id=1, source_target_pairs={{0,3},{1,2},{2,1},{3,0},{4,7},{5,6},{6,5},{7,4},{8,11},{9,10},{10,... | collective-permute-start | bytes 98312 | tf_op jit(solution)/shard_map/ppermute | solution.py:20
  144.9 5.1 %collective-permute-start.37 = (bf16[128,128]{1,0:T(8,128)(2,1)S(1)}, bf16[128,128]{1,0:T(8,128)(2,1)S(1)}, u32[]{:S(2)}, u32[]{:S(2)}) collective-permute-start(bf16[128,128]{1,0:T(8,128)(2,1)S(1)} %get-tuple-element.120), channel_id=1, source_target_pairs={{0,6},{1,7},{2,4},{3,5},{4,2},{5,3},{6,0},{7,1},{8,14},{9,15},{10,... | collective-permute-start | bytes 98312 | tf_op jit(solution)/shard_map/ppermute | solution.py:20
  146.4 4.2 %collective-permute-start.38 = (bf16[128,128]{1,0:T(8,128)(2,1)S(1)}, bf16[128,128]{1,0:T(8,128)(2,1)S(1)}, u32[]{:S(2)}, u32[]{:S(2)}) collective-permute-start(bf16[128,128]{1,0:T(8,128)(2,1)S(1)} %get-tuple-element.122), channel_id=1, source_target_pairs={{0,7},{1,6},{2,5},{3,4},{4,3},{5,2},{6,1},{7,0},{8,15},{9,14},{10,... | collective-permute-start | bytes 98312 | tf_op jit(solution)/shard_map/ppermute | solution.py:20
  (4 other events, 2.6 us)

commit v6 on v5

--- a/solution.py
+++ b/solution.py
@@ -110,87 +110,94 @@
     return terms
 
 
-def split_kernel(place, up_ref, *out_refs):
+def split_kernel(place, up_ref, *out_refs, n_depth):
     width = out_refs[0].shape[1]
-    for r, ref in enumerate(out_refs):
-        ref[...] = up_ref[:, pl.ds(pl.multiple_of((place[3] ^ r) * width, width), width)]
-
-
-def split(place, up, count):
-    tok, width = up.shape[0], up.shape[1] // count
+    for k, ref in enumerate(out_refs):
+        at = ((place[1] ^ k) * n_depth + place[0]) * width
+        ref[...] = up_ref[:, pl.ds(pl.multiple_of(at, width), width)]
+
+
+def split(place, up, n_col, n_depth):
+    tok, width = up.shape[0], up.shape[1] // (n_col * n_depth)
     if width % LANES:
-        blocks = jnp.transpose(up.reshape(tok, count, width), (1, 0, 2))
-        return [lax.dynamic_index_in_dim(blocks, place[3] ^ r, 0, keepdims=False) for r in range(count)]
+        blocks = up.reshape(tok, n_col * n_depth, width)
+        at = [(place[1] ^ k) * n_depth + place[0] for k in range(n_col)]
+        return [lax.dynamic_index_in_dim(blocks, i, 1, keepdims=False) for i in at]
     return pl.pallas_call(
-        split_kernel,
+        functools.partial(split_kernel, n_depth=n_depth),
         grid_spec=pltpu.PrefetchScalarGridSpec(
             num_scalar_prefetch=1,
             grid=(1,),
             in_specs=[resident(up.shape, width)],
-            out_specs=[resident((tok, width), width)] * count,
-        ),
-        out_shape=[jax.ShapeDtypeStruct((tok, width), jnp.bfloat16)] * count,
+            out_specs=[resident((tok, width), width)] * n_col,
+        ),
+        out_shape=[jax.ShapeDtypeStruct((tok, width), jnp.bfloat16)] * n_col,
         compiler_params=params(4, width),
         cost_estimate=SMALL,
         name="split",
     )(place, up)
 
 
-def join_kernel(place, _, *refs):
-    block_refs, (out_ref, grad_taps_ref) = refs[:-2], refs[-2:]
-    tok = out_ref.shape[0]
-    width = block_refs[0].shape[1]
-    groups = grad_taps_ref.shape[1]
+def join_kernel(place, _, blocks_ref, out_ref, grad_taps_ref):
+    n_depth, n_col, rows, width = blocks_ref.shape
+    local, groups = out_ref.shape[0], grad_taps_ref.shape[1]
     lane_group = lax.broadcasted_iota(jnp.int32, (width, groups), 0) // GROUP
     group = lax.broadcasted_iota(jnp.int32, (width, groups), 1)
     total = jnp.zeros((24, groups), jnp.float32)
-    for r, ref in enumerate(block_refs):
-        at = place[3] ^ r
-        out_ref[:, pl.ds(pl.multiple_of(at * width, width), width)] = ref[0:tok, :]
-        spread = (lane_group + at * (width // GROUP) == group).astype(jnp.bfloat16)
-        total = total + jnp.dot(ref[tok : tok + 24, :], spread, preferred_element_type=jnp.float32)
+    mine = pl.ds(pl.multiple_of(place[0] * local, 16), local)
+    for p in range(n_depth):
+        for k in range(n_col):
+            at = (place[1] ^ k) * n_depth + p
+            out_ref[:, pl.ds(pl.multiple_of(at * width, width), width)] = blocks_ref[p, k, mine, :]
+            spread = (lane_group + at * (width // GROUP) == group).astype(jnp.bfloat16)
+            sums = blocks_ref[p, k, rows - 32 : rows - 8, :]
+            total = total + jnp.dot(sums, spread, preferred_element_type=jnp.float32)
     grad_taps_ref[...] = (total[0:8] + total[8:16] + total[16:24])[:KT]
 
 
-def join(place, mark, blocks, tok, groups):
-    count, width = len(blocks), blocks[0].shape[1]
+def join(place, mark, blocks, local, groups):
+    n_depth, n_col, rows, width = blocks.shape
     if width % LANES:
-        whole = jnp.stack(blocks)[place[3] ^ jnp.arange(count)]
-        output = jnp.transpose(whole[:, :tok], (1, 0, 2)).reshape(tok, -1)
-        sums = whole[:, tok : tok + 24].astype(jnp.float32).reshape(count, 3, 8, width // GROUP, GROUP)
-        return output, sums.sum(axis=(1, 4))[:, :KT].transpose(1, 0, 2).reshape(KT, -1)
+        blocks = blocks[:, place[1] ^ jnp.arange(n_col)]
+        mine = lax.dynamic_slice_in_dim(blocks, place[0] * local, local, axis=2)
+        sums = blocks[:, :, rows - 32 : rows - 8].astype(jnp.float32)
+        sums = sums.reshape(n_depth, n_col, 3, 8, width // GROUP, GROUP).sum(axis=(2, 5))[:, :, :KT]
+        return (
+            jnp.transpose(mine, (2, 1, 0, 3)).reshape(local, -1),
+            jnp.transpose(sums, (2, 1, 0, 3)).reshape(KT, -1),
+        )
+    channels = n_depth * n_col * width
     return pl.pallas_call(
         join_kernel,
         grid_spec=pltpu.PrefetchScalarGridSpec(
             num_scalar_prefetch=1,
             grid=(1,),
-            in_specs=[pl.BlockSpec(memory_space=pl.ANY)] + [resident(blocks[0].shape, width)] * count,
-            out_specs=[resident((tok, width * count), width), resident((KT, groups), width)],
+            in_specs=[pl.BlockSpec(memory_space=pl.ANY), resident(blocks.shape, width)],
+            out_specs=[resident((local, channels), width), resident((KT, groups), width)],
         ),
         out_shape=[
-            jax.ShapeDtypeStruct((tok, width * count), jnp.bfloat16),
+            jax.ShapeDtypeStruct((local, channels), jnp.bfloat16),
             jax.ShapeDtypeStruct((KT, groups), jnp.float32),
         ],
         compiler_params=params(4, width),
         cost_estimate=SMALL,
         name="join",
-    )(place, mark, *blocks)
-
-
-def middle_kernel(place, taps_ref, *refs, devices, groups, terms, tile):
-    up_refs, refs = refs[:devices], refs[devices:]
+    )(place, mark, blocks)
+
+
+def middle_kernel(place, taps_ref, *refs, groups, terms, tile):
+    up_refs, refs = refs[:groups], refs[groups:]
     part_refs = refs[: groups * terms]
     grad_refs = refs[groups * terms : groups * terms + groups]
-    out_refs = refs[groups * terms + groups : groups * terms + groups + devices]
-    up_s, out_s, q_s, k_s, v_s, mixed_s, gf_s, far_s = refs[groups * terms + groups + devices :]
+    out_refs = refs[groups * terms + groups : groups * terms + 2 * groups]
+    up_s, out_s, q_s, k_s, v_s, mixed_s, gf_s, far_s = refs[groups * terms + 2 * groups :]
     col = place[1]
     tok = part_refs[0].shape[2]
     width = part_refs[0].shape[3]
     total = groups * tok
     tap_groups = taps_ref.shape[1]
-    for r, ref in enumerate(up_refs):
-        rows = pl.ds(pl.multiple_of((place[3] ^ r) * tile, tile), tile)
-        up_s[rows, :] = ref[...]
+    for k, ref in enumerate(up_refs):
+        up_s[pl.ds(pl.multiple_of((col ^ k) * tok, tok), tok), :] = ref[...]
     lane_group = lax.broadcasted_iota(jnp.int32, (tap_groups, width), 1) // GROUP
     group = lax.broadcasted_iota(jnp.int32, (tap_groups, width), 0)
     spread = (lane_group + place[3] * (width // GROUP) == group).astype(jnp.bfloat16)
@@ -227,7 +234,7 @@
                 filtered = filtered + taps[j : j + 1, :] * shifted
                 sums[j] = sums[j] + (gf * shifted).reshape(tile // 8, 8, width).sum(axis=0)
                 grad_mixed = grad_mixed + taps[j : j + 1, :] * gf_s[first + j : first + j + tile, :]
-            out_s[first // tile] = (q_s[rows, :].astype(jnp.float32) * filtered).astype(jnp.bfloat16)
+            out_s[a, inside, :] = (q_s[rows, :].astype(jnp.float32) * filtered).astype(jnp.bfloat16)
             at = col ^ a
             far_s[at, 0, inside, :] = (up_s[rows, :].astype(jnp.float32) * filtered).astype(jnp.bfloat16)
             far_s[at, 1, inside, :] = (grad_mixed * v_s[rows, :].astype(jnp.float32)).astype(jnp.bfloat16)
@@ -239,35 +246,34 @@
     )
     terms_of = [term.astype(jnp.float32) for term in in_three(rest)]
     packed = jnp.concatenate(terms_of + [jnp.zeros((8, width), jnp.float32)], axis=0).astype(jnp.bfloat16)
-    for r, ref in enumerate(out_refs):
-        ref[0:tile, :] = out_s[place[3] ^ r]
-        ref[tile : tile + 32, :] = packed
-
-
-def middle(place, taps, ups, parts):
-    groups, terms, devices = len(parts), len(parts[0]), len(ups)
-    tile = ups[0].shape[0]
+    for k, ref in enumerate(out_refs):
+        ref[0:tok, :] = out_s[col ^ k]
+        ref[tok : tok + 32, :] = packed
+
+
+def middle(place, taps, ups, parts, tile):
+    groups, terms = len(parts), len(parts[0])
     _, _, tok, width = parts[0][0].shape
     total = groups * tok
     whole = lambda *shape: resident(shape, width)
     one = whole(1, 3, tok, width)
     outs = pl.pallas_call(
-        functools.partial(middle_kernel, devices=devices, groups=groups, terms=terms, tile=tile),
+        functools.partial(middle_kernel, groups=groups, terms=terms, tile=tile),
         grid_spec=pltpu.PrefetchScalarGridSpec(
             num_scalar_prefetch=1,
             grid=(1,),
-            in_specs=[whole(*taps.shape)] + [whole(tile, width)] * devices + [one] * (groups * terms),
-            out_specs=[whole(3, tok, width)] * groups + [whole(tile + 32, width)] * devices,
+            in_specs=[whole(*taps.shape)] + [whole(tok, width)] * groups + [one] * (groups * terms),
+            out_specs=[whole(3, tok, width)] * groups + [whole(tok + 32, width)] * groups,
             scratch_shapes=[
                 pltpu.VMEM((total, width), jnp.bfloat16),
-                pltpu.VMEM((devices, tile, width), jnp.bfloat16),
+                pltpu.VMEM((groups, tok, width), jnp.bfloat16),
             ]
             + [pltpu.VMEM((total, width), jnp.bfloat16)] * 3
             + [pltpu.VMEM((total + PAD, width), jnp.float32)] * 2
             + [pltpu.VMEM((groups, 3, tok, width), jnp.bfloat16)],
         ),
         out_shape=[jax.ShapeDtypeStruct((3, tok, width), jnp.bfloat16)] * groups
-        + [jax.ShapeDtypeStruct((tile + 32, width), jnp.bfloat16)] * devices,
+        + [jax.ShapeDtypeStruct((tok + 32, width), jnp.bfloat16)] * groups,
         compiler_params=params(10, width),
         cost_estimate=SMALL,
         name="middle",
@@ -446,7 +452,6 @@
 def on_device(tokens, weight, taps, upstream):
     n_col = lax.axis_size("col")
     n_depth = lax.axis_size("depth")
-    both = ("col", "depth")
     local_tok = upstream.shape[0]
     depth_at = lax.axis_index("depth")
     col_at = lax.axis_index("col")
@@ -464,19 +469,19 @@
     first = [first_pieces(tokens, k) for k in range(1, n_col)]
     x, terms, pairs, fars = project_and_sum([tokens], *[piece for of in first for piece in of])
     xs, parts = [x], [terms]
+    group_up = lax.all_gather(upstream, "depth", axis=0, tiled=True)
+    ups = split(place, after(group_up, *pairs), n_col, n_depth)
     for k in range(1, n_col):
         x_pieces = other_pieces(tokens, first[k - 1], k)
-        x_pieces[-1] = after(x_pieces[-1], *fars)
+        x_pieces[-1] = after(x_pieces[-1], *fars, *ups)
         x, terms, pairs, fars = project_and_sum(x_pieces)
         xs.append(x)
         parts.append(terms)
-    ups = split(place, after(upstream, *pairs), n_col * n_depth)
-    ups = [up if r == 0 else swap(up, both, r) for r, up in enumerate(ups)]
-    own_grads, blocks = middle(place, taps, ups, parts)
-    near_blocks = [r for r in range(1, len(blocks)) if r % n_depth < 2]
-    blocks = [swap(block, both, r) if r in near_blocks else block for r, block in enumerate(blocks)]
+    ups = [up if k == 0 else swap(up, "col", k) for k, up in enumerate(ups)]
+    own_grads, blocks = middle(place, taps, ups, parts, local_tok)
     nears = [swap(own, "depth", 1) for own in own_grads]
-    beside = nears + [blocks[r] for r in near_blocks]
+    blocks = [block if k == 0 else swap(block, "col", k) for k, block in enumerate(blocks)]
+    beside = nears + blocks[1:]
     chunks = 4
     grads = [None] * n_col
     ready = []
@@ -498,10 +503,14 @@
             behind = [after(lhs[0], *head)] + lhs[1:]
             tail = input_grad(place, behind, w, 1, chunks, chunks)
             parts_of = list(head) + list(tail)
-            sent.append(([swap(part, "col", k) for part in parts_of], parts_of))
+            got = []
+            for c, part in enumerate(parts_of):
+                got.append(swap(part if c < 3 else after(part, got[c - 2]), "col", k))
+            sent.append((got, parts_of))
     sent = [of for of, _ in sent]
     own_part = list(input_grad(place, lhs, w, 0, 1, chunks))
     outer = (row_at == 0) | (row_at == 3)
+    blocks = lax.all_gather(after(jnp.stack(blocks), own_part[0]), "depth", axis=0)
     inward, across, summed, done = ([None] * chunks for _ in range(4))
     pair = cross = filled = None
     marks = []
@@ -539,14 +548,11 @@
             of = [group[i] for i in (r, r + 1) for group in grads]
             filled = weight_grad(place, filled, [after(of[0], *marks)] + of[1:], xs, r, n_depth)
             marks = [filled[1]]
-        if slot == chunks + 1:
-            blocks = [
-                block if r == 0 or r in near_blocks else swap(after(block, *marks), both, r)
-                for r, block in enumerate(blocks)
-            ]
+        if slot == chunks:
+            marks.append(blocks)
     grad_tokens = jnp.concatenate(done, axis=1)
     grad_weight = jnp.transpose(filled[0], (1, 0, 2))
-    output, grad_taps = join(place, filled[1], blocks, local_tok, taps.shape[1])
+    output, grad_taps = join(place, filled[1], after(blocks, *marks), local_tok, taps.shape[1])
     return (output, grad_tokens, grad_weight, grad_taps)
 
 

time: 155 us -> 163 us (1.052)
  blocking collectives: 0 us -> 20.5 us
  waiting for transfers between devices: 49.2 us -> 37.2 us
  starting transfers between devices: 50.1 us -> 51.8 us
    all_gather x0 -> x2, blocking collectives: none -> 20.5 us  [the longest x1 12.5 us: on_device(): group_up = lax.all_gather(upstream, 'depth', axis=0, tiled=True)]
    ppermute x37 -> x25, waiting for transfers between devices: 49.2 us -> 37.2 us  [swap(): return lax.ppermute(value, axis, [(i, i ^ flip) for i in range(count)])]
    ppermute x37 -> x25, starting transfers between devices: 47.4 us -> 49.1 us  [swap(): return lax.ppermute(value, axis, [(i, i ^ flip) for i in range(count)])]
    unnamed x54 -> x50, local copies, waits for them, and re-layouts: 10.4 us -> 9.23 us
  transfers between devices with their start and end apart: 41 -> 29, of which waited for: 19 -> 10; matrix products, arithmetic and copies ran while one was open for 3% -> 3% of each run, Pallas kernels for 19% -> 18%
where the time goes in v6:
time: 163 us; the launch traced here: 162 us
  starting transfers between devices  51.8 us (32%)
  waiting for transfers between devices  37.2 us (23%)
  Pallas kernels  35.2 us (22%)
  blocking collectives  20.5 us (13%)
  local copies, waits for them, and re-layouts  10.3 us (6%)
  other arithmetic  6.14 us (4%)
    ppermute x25, starting transfers between devices, swap(): return lax.ppermute(value, axis, [(i, i ^ flip) for i in range(count)])  49.1 us
    ppermute x25, waiting for transfers between devices, swap(): return lax.ppermute(value, axis, [(i, i ^ flip) for i in range(count)])  37.2 us
    all_gather x1, blocking collectives, on_device(): group_up = lax.all_gather(upstream, 'depth', axis=0, tiled=True)  12.5 us
    pallas_call x2, Pallas kernels, weight_grad(): pl.pallas_call(functools.partial(weight_grad_kernel, chained=chained, gro...  12.4 us
    pallas_call x4, Pallas kernels, input_grad(): pl.pallas_call(functools.partial(input_grad_kernel, terms=len(grads), wid...  10.2 us
    unnamed x50, local copies, waits for them, and re-layouts  9.23 us
    all_gather x1, blocking collectives, on_device(): lax.all_gather(after(jnp.stack(blocks), own_part[0]), 'depth', axis=0)  8 us
    pallas_call x2, Pallas kernels, project(): pl.pallas_call(functools.partial(project_kernel, pieces=len(xs), count=co...  7.67 us
  transfers between devices with their start and end apart: 29, of which 10 were waited for; matrix products, arithmetic and copies ran while one was open for 3% of the time, Pallas kernels for 18%

profile of v6, /device:TPU:0, one launch (start us, length us, event | category | flops | bytes accessed | tf_op | source)
XLA Modules:
  0.0 162.3 jit_solution(4042422336697713091)
XLA Ops:
  0.6 1.1 constant_dynamic-slice_fusion
  1.7 3.0 %collective-permute-start = (bf16[128,2048]{1,0:T(8,128)(2,1)S(1)}, bf16[128,2048]{1,0:T(8,128)(2,1)S(1)}, u32[]{:S(2)}, u32[]{:S(2)}) collective-permute-start(bf16[128,2048]{1,0:T(8,128)(2,1)S(1)} %constant_dynamic-slice_fusion), channel_id=1, source_target_pairs={{0,4},{4,0},{1,5},{5,1},{2,6},{6,2},{3,7},{7,3},{8,12},{12,8},{9,1... | collective-permute-start | bytes 1572872 | tf_op jit(solution)/shard_map/ppermute | solution.py:20
  4.8 2.8 %copy-done = bf16[512,3,2048]{2,0,1:T(8,128)(2,1)S(1)} copy-done((bf16[512,3,2048]{2,0,1:T(8,128)(2,1)S(1)}, bf16[512,3,2048]{2,0,1:T(8,128)(2,1)}, u32[]{:S(2)}) %copy-start) | copy-done | bytes 6291480
  7.6 1.4 copy-done.3
  9.0 3.8 %project.2 = (bf16[2,3,384,128]{3,2,1,0:T(8,128)(2,1)S(1)}, bf16[2,3,384,128]{3,2,1,0:T(8,128)(2,1)S(1)}) custom-call(s32[4]{0:T(128)S(1)} %pad_add_fusion.place, bf16[384,2048]{1,0:T(8,128)(2,1)S(1)} %copy-done.3, bf16[3,512,2048]{2,1,0:T(8,128)(2,1)S(1)} %bitcast.9), custom_call_target="tpu_custom_call" | custom-call | flops 1 | bytes 1 | tf_op jit(solution)/shard_map/project/pallas_call | solution.py:87
  12.8 3.9 %collective-permute-done.refs_0_ = bf16[128,2048]{1,0:T(8,128)(2,1)S(1)} collective-permute-done((bf16[128,2048]{1,0:T(8,128)(2,1)S(1)}, bf16[128,2048]{1,0:T(8,128)(2,1)S(1)}, u32[]{:S(2)}, u32[]{:S(2)}) %collective-permute-start) | collective-permute-done | bytes 524320 | tf_op jit(solution)/shard_map/ppermute | solution.py:20
  16.7 1.8 %collective-permute-start.5 = (bf16[128,2048]{1,0:T(8,128)(2,1)S(1)}, bf16[128,2048]{1,0:T(8,128)(2,1)S(1)}, u32[]{:S(2)}, u32[]{:S(2)}) collective-permute-start(bf16[128,2048]{1,0:T(8,128)(2,1)S(1)} %slice.17), channel_id=1, source_target_pairs={{0,4},{4,0},{1,5},{5,1},{2,6},{6,2},{3,7},{7,3},{8,12},{12,8},{9,1... | collective-permute-start | bytes 1572872 | tf_op jit(solution)/shard_map/ppermute | solution.py:20
  18.5 1.6 collective-permute-start.4
  20.2 1.6 collective-permute-start.3
  21.8 12.5 %all_gather.9.up_ref = bf16[384,1024]{1,0:T(8,128)(2,1)S(1)} all-gather(bf16[96,1024]{1,0:T(8,128)(2,1)S(1)} %copy-done.22), channel_id=1, replica_groups=mesh['row'=4,'col'=2,'depth'=4] {'depth'}, dimensions={0}, use_global_device_ids=true | all-gather | bytes 983040 | tf_op jit(solution)/shard_map/all_gather | solution.py:472
  34.2 0.6 split.1
  34.9 3.9 %project.3 = (bf16[2,3,384,128]{3,2,1,0:T(8,128)(2,1)S(1)}, bf16[2,3,384,128]{3,2,1,0:T(8,128)(2,1)S(1)}, bf16[384,2048]{1,0:T(8,128)(2,1)S(1)}) custom-call(s32[4]{0:T(128)S(1)} %pad_add_fusion.place, bf16[128,2048]{1,0:T(8,128)(2,1)S(1)} %collective-permute-done.refs_0_, bf16[128,2048]{1,0:T(8,128)(2,1)S(1)} %collective-permute-done.4.refs_1_, ...), custom_call_target="tpu_custom_call" | custom-call | flops 1 | bytes 1 | tf_op jit(solution)/shard_map/project/pallas_call | solution.py:87
  38.8 0.4 collective-permute-start.6
  39.2 1.7 %collective-permute-done.6.refs_6_ = bf16[2,3,384,128]{3,2,1,0:T(8,128)(2,1)S(1)} collective-permute-done((bf16[2,3,384,128]{3,2,1,0:T(8,128)(2,1)S(1)}, bf16[2,3,384,128]{3,2,1,0:T(8,128)(2,1)S(1)}, u32[]{:S(2)}, u32[]{:S(2)}) %collective-permute-start.6) | collective-permute-done | bytes 589856 | tf_op jit(solution)/shard_map/ppermute | solution.py:20
  41.0 1.6 collective-permute-start.7
  42.5 0.5 collective-permute-start.2
  43.0 4.3 %collective-permute-done.2.refs_1_ = bf16[384,128]{1,0:T(8,128)(2,1)S(1)} collective-permute-done((bf16[384,128]{1,0:T(8,128)(2,1)S(1)}, bf16[384,128]{1,0:T(8,128)(2,1)S(1)}, u32[]{:S(2)}, u32[]{:S(2)}) %collective-permute-start.2) | collective-permute-done | bytes 98336 | tf_op jit(solution)/shard_map/ppermute | solution.py:20
  47.3 3.0 %collective-permute-done.7.refs_7_ = bf16[1,3,384,128]{3,2,1,0:T(8,128)(2,1)S(1)} collective-permute-done((bf16[1,3,384,128]{3,2,1,0:T(8,128)(2,1)S(1)}, bf16[1,3,384,128]{3,2,1,0:T(8,128)(2,1)S(1)}, u32[]{:S(2)}, u32[]{:S(2)}) %collective-permute-start.7) | collective-permute-done | bytes 294944 | tf_op jit(solution)/shard_map/ppermute | solution.py:20
  50.3 1.6 middle.1
  52.0 0.5 collective-permute-start.10
  52.5 1.5 collective-permute-start.8
  53.9 0.5 collective-permute-start.11
  54.4 4.2 %collective-permute-done.11 = bf16[416,128]{1,0:T(8,128)(2,1)S(1)} collective-permute-done((bf16[416,128]{1,0:T(8,128)(2,1)S(1)}, bf16[416,128]{1,0:T(8,128)(2,1)S(1)}, u32[]{:S(2)}, u32[]{:S(2)}) %collective-permute-start.11) | collective-permute-done | bytes 106528 | tf_op jit(solution)/shard_map/ppermute | solution.py:20
  58.7 2.8 %collective-permute-done.8.refs_2_.refs_1_ = bf16[3,384,128]{2,1,0:T(8,128)(2,1)S(1)} collective-permute-done((bf16[3,384,128]{2,1,0:T(8,128)(2,1)S(1)}, bf16[3,384,128]{2,1,0:T(8,128)(2,1)S(1)}, u32[]{:S(2)}, u32[]{:S(2)}) %collective-permute-start.8) | collective-permute-done | bytes 294944 | tf_op jit(solution)/shard_map/ppermute | solution.py:20
  61.4 1.6 collective-permute-done.12.refs_3_
  63.0 1.5 collective-permute-start.13
  64.5 0.7 assemble.2.refs_0_
  65.3 0.7 copy-done.13
  66.0 0.7 copy-done.17
  66.7 1.3 input_grad.4
  68.0 0.6 collective-permute-start.15
  68.6 4.1 %input_grad.5 = (bf16[384,512]{1,0:T(8,128)(2,1)}, bf16[384,512]{1,0:T(8,128)(2,1)S(1)}, bf16[384,512]{1,0:T(8,128)(2,1)S(1)}) custom-call(s32[4]{0:T(128)S(1)} %pad_add_fusion.place, bf16[384,1536]{1,0:T(8,128)(2,1)S(1)} %assemble.2.refs_0_, bf16[3,512,2048]{2,1,0:T(8,128)(2,1)S(1)} %bitcast.12), custom_call_target="tpu_custom_call" | custom-call | flops 1 | bytes 1 | tf_op jit(solution)/shard_map/input_grad/pallas_call | solution.py:336
  72.8 1.6 collective-permute-start.16
  74.4 0.7 assemble.3.refs_0_
  75.2 0.7 copy-done.9
  75.9 1.3 input_grad.6
  77.3 2.8 %collective-permute-done.15 = bf16[384,512]{1,0:T(8,128)(2,1)S(1)} collective-permute-done((bf16[384,512]{1,0:T(8,128)(2,1)S(1)}, bf16[384,512]{1,0:T(8,128)(2,1)S(1)}, u32[]{:S(2)}, u32[]{:S(2)}) %collective-permute-start.15) | collective-permute-done | bytes 393248 | tf_op jit(solution)/shard_map/ppermute | solution.py:20
  80.1 0.9 add_convert_fusion.11
  80.9 0.6 collective-permute-start.17
  81.5 1.5 collective-permute-start.18
  83.0 5.6 %collective-permute-done.16 = bf16[384,512]{1,0:T(8,128)(2,1)} collective-permute-done((bf16[384,512]{1,0:T(8,128)(2,1)}, bf16[384,512]{1,0:T(8,128)(2,1)}, u32[]{:S(2)}, u32[]{:S(2)}) %collective-permute-start.16) | collective-permute-done | bytes 393248 | tf_op jit(solution)/shard_map/ppermute | solution.py:20
  88.6 0.5 collective-permute-start.21
  89.1 2.8 %copy-done.2 = bf16[512,3,2048]{2,0,1:T(8,128)(2,1)S(1)} copy-done((bf16[512,3,2048]{2,0,1:T(8,128)(2,1)S(1)}, bf16[512,3,2048]{2,0,1:T(8,128)(2,1)}, u32[]{:S(2)}) %copy-start.2) | copy-done | bytes 6291480
  91.9 3.4 %input_grad.7 = (bf16[384,512]{1,0:T(8,128)(2,1)S(1)}, bf16[384,512]{1,0:T(8,128)(2,1)S(1)}, bf16[384,512]{1,0:T(8,128)(2,1)S(1)}) custom-call(s32[4]{0:T(128)S(1)} %pad_add_fusion.place, bf16[384,1536]{1,0:T(8,128)(2,1)S(1)} %assemble.3.refs_0_, bf16[3,512,2048]{2,1,0:T(8,128)(2,1)S(1)} %bitcast.14), custom_call_target="tpu_custom_call" | custom-call | flops 1 | bytes 1 | tf_op jit(solution)/shard_map/input_grad/pallas_call | solution.py:336
  95.4 1.2 add_convert_fusion.10
  96.6 1.6 %collective-permute-start.19 = (bf16[384,512]{1,0:T(8,128)(2,1)S(1)}, bf16[384,512]{1,0:T(8,128)(2,1)S(1)}, u32[]{:S(2)}, u32[]{:S(2)}) collective-permute-start(bf16[384,512]{1,0:T(8,128)(2,1)S(1)} %add_convert_fusion.10), channel_id=1, source_target_pairs={{0,8},{8,0},{16,24},{24,16},{1,9},{9,1},{17,25},{25,17},{2,10},{10... | collective-permute-start | bytes 1179656 | tf_op jit(solution)/shard_map/ppermute | solution.py:20
  98.2 1.2 add_convert_fusion.9
  99.5 0.7 collective-permute-start.20
  100.2 6.2 %weight_grad.2 = (f32[3,512,2048]{2,1,0:T(8,128)}, f32[8,128]{1,0:T(8,128)S(1)}) custom-call(s32[4]{0:T(128)S(1)} %pad_add_fusion.place, bf16[3,384,128]{2,1,0:T(8,128)(2,1)S(1)} %copy-done.8, bf16[3,384,128]{2,1,0:T(8,128)(2,1)S(1)} %collective-permute-done.8.refs_2_.refs_1_, bf16[3,384,128]{2,1,0:T(8,128)(2,1)S(1)} %copy-done.10, ...), custom_call_target="tpu_custom_call" | custom-call | flops 1 | bytes 1 | tf_op jit(solution)/shard_map/weight_grad/pallas_call | solution.py:406
  106.5 0.1 add_convert_fusion.7
  106.6 0.2 broadcast_select_fusion.5
  106.8 4.5 %collective-permute-start.22 = (bf16[384,512]{1,0:T(8,128)(2,1)S(1)}, bf16[384,512]{1,0:T(8,128)(2,1)S(1)}, u32[]{:S(2)}, u32[]{:S(2)}) collective-permute-start(bf16[384,512]{1,0:T(8,128)(2,1)S(1)} %get-tuple-element.102), channel_id=1, source_target_pairs={{0,8},{8,0},{16,24},{24,16},{1,9},{9,1},{17,25},{25,17},{2,10},{10... | collective-permute-start | bytes 1179656 | tf_op jit(solution)/shard_map/ppermute | solution.py:20
  111.3 0.7 collective-permute-start.23
  112.1 6.2 %weight_grad.3 = (f32[3,512,2048]{2,1,0:T(8,128)}, f32[8,128]{1,0:T(8,128)S(1)}) custom-call(s32[4]{0:T(128)S(1)} %pad_add_fusion.place, f32[3,512,2048]{2,1,0:T(8,128)} %get-tuple-element.77.refs_0_, f32[8,128]{1,0:T(8,128)S(1)} %get-tuple-element.78.refs_1_, bf16[3,384,128]{2,1,0:T(8,128)(2,1)S(1)} %copy-done.12, ...), custom_call_target="tpu_custom_call", output_to_operand_aliasing={{0}: (1, {})} | custom-call | flops 1 | bytes 1 | tf_op jit(solution)/shard_map/weight_grad/pallas_call | solution.py:406
  118.5 0.2 broadcast_select_fusion.4
  118.7 3.0 %collective-permute-start.24 = (bf16[384,512]{1,0:T(8,128)(2,1)S(1)}, bf16[384,512]{1,0:T(8,128)(2,1)S(1)}, u32[]{:S(2)}, u32[]{:S(2)}) collective-permute-start(bf16[384,512]{1,0:T(8,128)(2,1)S(1)} %get-tuple-element.100), channel_id=1, source_target_pairs={{0,8},{8,0},{16,24},{24,16},{1,9},{9,1},{17,25},{25,17},{2,10},{10... | collective-permute-start | bytes 1179656 | tf_op jit(solution)/shard_map/ppermute | solution.py:20
  121.8 8.0 %all-gather = bf16[8,416,128]{2,1,0:T(8,128)(2,1)S(1)} all-gather(bf16[2,416,128]{2,1,0:T(8,128)(2,1)S(1)} %pad_maximum_fusion.1), channel_id=2, replica_groups=mesh['row'=4,'col'=2,'depth'=4] {'depth'}, dimensions={0}, use_global_device_ids=true | all-gather | bytes 1064960 | tf_op jit(solution)/shard_map/all_gather | solution.py:513
  129.8 0.7 collective-permute-start.25
  130.6 0.7 collective-permute-start.26
  131.4 12.8 %collective-permute-start.27 = (bf16[384,512]{1,0:T(8,128)(2,1)S(1)}, bf16[384,512]{1,0:T(8,128)(2,1)S(1)}, u32[]{:S(2)}, u32[]{:S(2)}) collective-permute-start(bf16[384,512]{1,0:T(8,128)(2,1)S(1)} %add_convert_fusion.1), channel_id=1, source_target_pairs={{0,8},{8,0},{16,24},{24,16},{1,9},{9,1},{17,25},{25,17},{2,10},{10... | collective-permute-start | bytes 1179656 | tf_op jit(solution)/shard_map/ppermute | solution.py:20
  144.4 7.8 %collective-permute-start.28 = (bf16[384,512]{1,0:T(8,128)(2,1)S(1)}, bf16[384,512]{1,0:T(8,128)(2,1)S(1)}, u32[]{:S(2)}, u32[]{:S(2)}) collective-permute-start(bf16[384,512]{1,0:T(8,128)(2,1)S(1)} %add_convert_fusion), channel_id=1, source_target_pairs={{0,8},{8,0},{16,24},{24,16},{1,9},{9,1},{17,25},{25,17},{2,10},{10... | collective-permute-start | bytes 1179656 | tf_op jit(solution)/shard_map/ppermute | solution.py:20
  152.2 1.4 join.1
  153.6 7.4 %collective-permute-done.28 = bf16[384,512]{1,0:T(8,128)(2,1)S(1)} collective-permute-done((bf16[384,512]{1,0:T(8,128)(2,1)S(1)}, bf16[384,512]{1,0:T(8,128)(2,1)S(1)}, u32[]{:S(2)}, u32[]{:S(2)}) %collective-permute-start.28) | collective-permute-done | bytes 393248 | tf_op jit(solution)/shard_map/ppermute | solution.py:20
  161.0 1.3 pad_maximum_fusion
  (82 shorter events, 1.3 us)
Async XLA Ops:
  1.7 15.0 %collective-permute-start = (bf16[128,2048]{1,0:T(8,128)(2,1)S(1)}, bf16[128,2048]{1,0:T(8,128)(2,1)S(1)}, u32[]{:S(2)}, u32[]{:S(2)}) collective-permute-start(bf16[128,2048]{1,0:T(8,128)(2,1)S(1)} %constant_dynamic-slice_fusion), channel_id=1, source_target_pairs={{0,4},{4,0},{1,5},{5,1},{2,6},{6,2},{3,7},{7,3},{8,12},{12,8},{9,1... | collective-permute-start | bytes 1572872 | tf_op jit(solution)/shard_map/ppermute | solution.py:20
  4.8 2.8 %copy-start = (bf16[512,3,2048]{2,0,1:T(8,128)(2,1)S(1)}, bf16[512,3,2048]{2,0,1:T(8,128)(2,1)}, u32[]{:S(2)}) copy-start(bf16[512,3,2048]{2,0,1:T(8,128)(2,1)} %param.5) | copy-start | bytes 18874372
  7.6 1.4 copy-start.3
  9.0 7.7 %copy-start.4 = (bf16[384,2048]{1,0:T(8,128)(2,1)S(1)}, bf16[384,2048]{1,0:T(8,128)(2,1)}, u32[]{:S(2)}) copy-start(bf16[384,2048]{1,0:T(8,128)(2,1)} %refs_6_.1) | copy-start | bytes 4718596
  9.0 25.8 %copy-start.1 = (bf16[512,3,2048]{2,0,1:T(8,128)(2,1)S(1)}, bf16[512,3,2048]{2,0,1:T(8,128)(2,1)}, u32[]{:S(2)}) copy-start(bf16[512,3,2048]{2,0,1:T(8,128)(2,1)} %param.5) | copy-start | bytes 18874372
  12.8 8.9 %copy-start.22 = (bf16[96,1024]{1,0:T(8,128)(2,1)S(1)}, bf16[96,1024]{1,0:T(8,128)(2,1)}, u32[]{:S(2)}) copy-start(bf16[96,1024]{1,0:T(8,128)(2,1)} %param.7) | copy-start | bytes 589828
  16.7 3.4 %collective-permute-start.1 = (bf16[2,3,384,128]{3,2,1,0:T(8,128)(2,1)S(1)}, bf16[2,3,384,128]{3,2,1,0:T(8,128)(2,1)S(1)}, u32[]{:S(2)}, u32[]{:S(2)}) collective-permute-start(bf16[2,3,384,128]{3,2,1,0:T(8,128)(2,1)S(1)} %get-tuple-element.54), channel_id=1, source_target_pairs={{0,1},{1,0},{2,3},{3,2},{4,5},{5,4},{6,7},{7,6},{8,9},{9,8},{10,11... | collective-permute-start | bytes 1769480 | tf_op jit(solution)/shard_map/ppermute | solution.py:20
  16.7 18.1 %collective-permute-start.5 = (bf16[128,2048]{1,0:T(8,128)(2,1)S(1)}, bf16[128,2048]{1,0:T(8,128)(2,1)S(1)}, u32[]{:S(2)}, u32[]{:S(2)}) collective-permute-start(bf16[128,2048]{1,0:T(8,128)(2,1)S(1)} %slice.17), channel_id=1, source_target_pairs={{0,4},{4,0},{1,5},{5,1},{2,6},{6,2},{3,7},{7,3},{8,12},{12,8},{9,1... | collective-permute-start | bytes 1572872 | tf_op jit(solution)/shard_map/ppermute | solution.py:20
  18.5 16.3 %collective-permute-start.4 = (bf16[128,2048]{1,0:T(8,128)(2,1)S(1)}, bf16[128,2048]{1,0:T(8,128)(2,1)S(1)}, u32[]{:S(2)}, u32[]{:S(2)}) collective-permute-start(bf16[128,2048]{1,0:T(8,128)(2,1)S(1)} %collective-permute-done.refs_0_), channel_id=1, source_target_pairs={{0,8},{8,0},{16,24},{24,16},{1,9},{9,1},{17,25},{25,17},{2,10},{10... | collective-permute-start | bytes 1572872 | tf_op jit(solution)/shard_map/ppermute | solution.py:20
  20.2 14.6 %collective-permute-start.3 = (bf16[1,3,384,128]{3,2,1,0:T(8,128)(2,1)S(1)}, bf16[1,3,384,128]{3,2,1,0:T(8,128)(2,1)S(1)}, u32[]{:S(2)}, u32[]{:S(2)}) collective-permute-start(bf16[1,3,384,128]{3,2,1,0:T(8,128)(2,1)S(1)} %add_convert_fusion.13), channel_id=1, source_target_pairs={{0,2},{1,3},{2,0},{3,1},{4,6},{5,7},{6,4},{7,5},{8,10},{9,11},{10,... | collective-permute-start | bytes 884744 | tf_op jit(solution)/shard_map/ppermute | solution.py:20
  34.8 15.4 %copy-start.19 = (f32[7,64]{1,0:T(8,128)S(1)}, f32[7,64]{1,0:T(8,128)}, u32[]{:S(2)}) copy-start(f32[7,64]{1,0:T(8,128)} %taps_ref.1) | copy-start | bytes 5380
  38.8 13.1 %copy-start.5 = (bf16[384,2048]{1,0:T(8,128)(2,1)}, bf16[384,2048]{1,0:T(8,128)(2,1)S(1)}, u32[]{:S(2)}) copy-start(bf16[384,2048]{1,0:T(8,128)(2,1)S(1)} %get-tuple-element.76.refs_5_.refs_7_) | copy-start | bytes 4718596
  38.8 2.1 %collective-permute-start.6 = (bf16[2,3,384,128]{3,2,1,0:T(8,128)(2,1)S(1)}, bf16[2,3,384,128]{3,2,1,0:T(8,128)(2,1)S(1)}, u32[]{:S(2)}, u32[]{:S(2)}) collective-permute-start(bf16[2,3,384,128]{3,2,1,0:T(8,128)(2,1)S(1)} %get-tuple-element.62), channel_id=1, source_target_pairs={{0,1},{1,0},{2,3},{3,2},{4,5},{5,4},{6,7},{7,6},{8,9},{9,8},{10,11... | collective-permute-start | bytes 1769480 | tf_op jit(solution)/shard_map/ppermute | solution.py:20
  41.0 9.3 %collective-permute-start.7 = (bf16[1,3,384,128]{3,2,1,0:T(8,128)(2,1)S(1)}, bf16[1,3,384,128]{3,2,1,0:T(8,128)(2,1)S(1)}, u32[]{:S(2)}, u32[]{:S(2)}) collective-permute-start(bf16[1,3,384,128]{3,2,1,0:T(8,128)(2,1)S(1)} %add_convert_fusion.12), channel_id=1, source_target_pairs={{0,2},{1,3},{2,0},{3,1},{4,6},{5,7},{6,4},{7,5},{8,10},{9,11},{10,... | collective-permute-start | bytes 884744 | tf_op jit(solution)/shard_map/ppermute | solution.py:20
  42.5 4.8 %collective-permute-start.2 = (bf16[384,128]{1,0:T(8,128)(2,1)S(1)}, bf16[384,128]{1,0:T(8,128)(2,1)S(1)}, u32[]{:S(2)}, u32[]{:S(2)}) collective-permute-start(bf16[384,128]{1,0:T(8,128)(2,1)S(1)} %get-tuple-element.57), channel_id=1, source_target_pairs={{0,4},{4,0},{1,5},{5,1},{2,6},{6,2},{3,7},{7,3},{8,12},{12,8},{9,1... | collective-permute-start | bytes 294920 | tf_op jit(solution)/shard_map/ppermute | solution.py:20
  51.9 22.5 %copy-start.11 = (bf16[3,384,128]{2,1,0:T(8,128)(2,1)}, bf16[3,384,128]{2,1,0:T(8,128)(2,1)S(1)}, u32[]{:S(2)}) copy-start(bf16[3,384,128]{2,1,0:T(8,128)(2,1)S(1)} %get-tuple-element.84.refs_0_.refs_2_) | copy-start | bytes 884740
  51.9 6.8 %collective-permute-start.9 = (bf16[3,384,128]{2,1,0:T(8,128)(2,1)S(1)}, bf16[3,384,128]{2,1,0:T(8,128)(2,1)S(1)}, u32[]{:S(2)}, u32[]{:S(2)}) collective-permute-start(bf16[3,384,128]{2,1,0:T(8,128)(2,1)S(1)} %get-tuple-element.84.refs_0_.refs_2_), channel_id=1, source_target_pairs={{0,1},{1,0},{2,3},{3,2},{4,5},{5,4},{6,7},{7,6},{8,9},{9,8},{10,11... | collective-permute-start | bytes 884744 | tf_op jit(solution)/shard_map/ppermute | solution.py:20
  52.0 6.7 %collective-permute-start.10 = (bf16[3,384,128]{2,1,0:T(8,128)(2,1)S(1)}, bf16[3,384,128]{2,1,0:T(8,128)(2,1)S(1)}, u32[]{:S(2)}, u32[]{:S(2)}) collective-permute-start(bf16[3,384,128]{2,1,0:T(8,128)(2,1)S(1)} %get-tuple-element.64.refs_0_.refs_3_), channel_id=1, source_target_pairs={{0,1},{1,0},{2,3},{3,2},{4,5},{5,4},{6,7},{7,6},{8,9},{9,8},{10,11... | collective-permute-start | bytes 884744 | tf_op jit(solution)/shard_map/ppermute | solution.py:20
  52.5 9.0 %collective-permute-start.8 = (bf16[3,384,128]{2,1,0:T(8,128)(2,1)S(1)}, bf16[3,384,128]{2,1,0:T(8,128)(2,1)S(1)}, u32[]{:S(2)}, u32[]{:S(2)}) collective-permute-start(bf16[3,384,128]{2,1,0:T(8,128)(2,1)S(1)} %get-tuple-element.64.refs_0_.refs_3_), channel_id=1, source_target_pairs={{0,2},{1,3},{2,0},{3,1},{4,6},{5,7},{6,4},{7,5},{8,10},{9,11},{10,... | collective-permute-start | bytes 884744 | tf_op jit(solution)/shard_map/ppermute | solution.py:20
  53.9 4.7 %collective-permute-start.11 = (bf16[416,128]{1,0:T(8,128)(2,1)S(1)}, bf16[416,128]{1,0:T(8,128)(2,1)S(1)}, u32[]{:S(2)}, u32[]{:S(2)}) collective-permute-start(bf16[416,128]{1,0:T(8,128)(2,1)S(1)} %get-tuple-element.65), channel_id=1, source_target_pairs={{0,4},{4,0},{1,5},{5,1},{2,6},{6,2},{3,7},{7,3},{8,12},{12,8},{9,1... | collective-permute-start | bytes 319496 | tf_op jit(solution)/shard_map/ppermute | solution.py:20
  58.6 2.8 %copy-start.23 = (bf16[416,128]{1,0:T(8,128)(2,1)}, bf16[416,128]{1,0:T(8,128)(2,1)S(1)}, u32[]{:S(2)}) copy-start(bf16[416,128]{1,0:T(8,128)(2,1)S(1)} %collective-permute-done.11) | copy-start | bytes 319492
  58.6 15.8 %copy-start.15 = (bf16[3,384,128]{2,1,0:T(8,128)(2,1)}, bf16[3,384,128]{2,1,0:T(8,128)(2,1)S(1)}, u32[]{:S(2)}) copy-start(bf16[3,384,128]{2,1,0:T(8,128)(2,1)S(1)} %collective-permute-done.9.refs_1_.refs_4_) | copy-start | bytes 884740
  61.4 1.6 collective-permute-start.12
  63.0 9.7 %collective-permute-start.13 = (bf16[3,384,128]{2,1,0:T(8,128)(2,1)S(1)}, bf16[3,384,128]{2,1,0:T(8,128)(2,1)S(1)}, u32[]{:S(2)}, u32[]{:S(2)}) collective-permute-start(bf16[3,384,128]{2,1,0:T(8,128)(2,1)S(1)} %get-tuple-element.84.refs_0_.refs_2_), channel_id=1, source_target_pairs={{0,2},{1,3},{2,0},{3,1},{4,6},{5,7},{6,4},{7,5},{8,10},{9,11},{10,... | collective-permute-start | bytes 884744 | tf_op jit(solution)/shard_map/ppermute | solution.py:20
  65.3 0.7 copy-start.13
  66.0 0.7 copy-start.17
  68.0 12.1 %collective-permute-start.15 = (bf16[384,512]{1,0:T(8,128)(2,1)S(1)}, bf16[384,512]{1,0:T(8,128)(2,1)S(1)}, u32[]{:S(2)}, u32[]{:S(2)}) collective-permute-start(bf16[384,512]{1,0:T(8,128)(2,1)S(1)} %input_grad.4), channel_id=1, source_target_pairs={{0,4},{4,0},{1,5},{5,1},{2,6},{6,2},{3,7},{7,3},{8,12},{12,8},{9,1... | collective-permute-start | bytes 1179656 | tf_op jit(solution)/shard_map/ppermute | solution.py:20
  72.7 4.5 %copy-start.20 = (bf16[384,512]{1,0:T(8,128)(2,1)}, bf16[384,512]{1,0:T(8,128)(2,1)S(1)}, u32[]{:S(2)}) copy-start(bf16[384,512]{1,0:T(8,128)(2,1)S(1)} %get-tuple-element.90) | copy-start | bytes 1179652
  72.7 4.5 %copy-start.21 = (bf16[384,512]{1,0:T(8,128)(2,1)}, bf16[384,512]{1,0:T(8,128)(2,1)S(1)}, u32[]{:S(2)}) copy-start(bf16[384,512]{1,0:T(8,128)(2,1)S(1)} %get-tuple-element.81) | copy-start | bytes 1179652
  72.7 4.5 %copy-start.7 = (bf16[3,384,128]{2,1,0:T(8,128)(2,1)}, bf16[3,384,128]{2,1,0:T(8,128)(2,1)S(1)}, u32[]{:S(2)}) copy-start(bf16[3,384,128]{2,1,0:T(8,128)(2,1)S(1)} %collective-permute-done.13.refs_2_.refs_0_) | copy-start | bytes 884740
  72.7 1.7 %collective-permute-start.14 = (bf16[3,384,128]{2,1,0:T(8,128)(2,1)S(1)}, bf16[3,384,128]{2,1,0:T(8,128)(2,1)S(1)}, u32[]{:S(2)}, u32[]{:S(2)}) collective-permute-start(bf16[3,384,128]{2,1,0:T(8,128)(2,1)S(1)} %collective-permute-done.13.refs_2_.refs_0_), channel_id=1, source_target_pairs={{0,1},{1,0},{2,3},{3,2},{4,5},{5,4},{6,7},{7,6},{8,9},{9,8},{10,11... | collective-permute-start | bytes 884744 | tf_op jit(solution)/shard_map/ppermute | solution.py:20
  72.8 15.8 %collective-permute-start.16 = (bf16[384,512]{1,0:T(8,128)(2,1)}, bf16[384,512]{1,0:T(8,128)(2,1)}, u32[]{:S(2)}, u32[]{:S(2)}) collective-permute-start(bf16[384,512]{1,0:T(8,128)(2,1)} %get-tuple-element.73), channel_id=1, source_target_pairs={{0,4},{4,0},{1,5},{5,1},{2,6},{6,2},{3,7},{7,3},{8,12},{12,8},{9,1... | collective-permute-start | bytes 1179656 | tf_op jit(solution)/shard_map/ppermute | solution.py:20
  75.2 0.7 copy-start.9
  80.9 17.3 %collective-permute-start.17 = (bf16[384,512]{1,0:T(8,128)(2,1)}, bf16[384,512]{1,0:T(8,128)(2,1)}, u32[]{:S(2)}, u32[]{:S(2)}) collective-permute-start(bf16[384,512]{1,0:T(8,128)(2,1)} %add_convert_fusion.11), channel_id=1, source_target_pairs={{0,8},{8,0},{16,24},{24,16},{1,9},{9,1},{17,25},{25,17},{2,10},{10... | collective-permute-start | bytes 1179656 | tf_op jit(solution)/shard_map/ppermute | solution.py:20
  81.5 24.9 %collective-permute-start.18 = (bf16[384,512]{1,0:T(8,128)(2,1)}, bf16[384,512]{1,0:T(8,128)(2,1)S(1)}, u32[]{:S(2)}, u32[]{:S(2)}) collective-permute-start(bf16[384,512]{1,0:T(8,128)(2,1)} %copy-done.21), channel_id=1, source_target_pairs={{0,4},{4,0},{1,5},{5,1},{2,6},{6,2},{3,7},{7,3},{8,12},{12,8},{9,1... | collective-permute-start | bytes 1179656 | tf_op jit(solution)/shard_map/ppermute | solution.py:20
  88.6 29.6 %collective-permute-start.21 = (bf16[384,512]{1,0:T(8,128)(2,1)}, bf16[384,512]{1,0:T(8,128)(2,1)S(1)}, u32[]{:S(2)}, u32[]{:S(2)}) collective-permute-start(bf16[384,512]{1,0:T(8,128)(2,1)} %copy-done.20), channel_id=1, source_target_pairs={{0,4},{4,0},{1,5},{5,1},{2,6},{6,2},{3,7},{7,3},{8,12},{12,8},{9,1... | collective-permute-start | bytes 1179656 | tf_op jit(solution)/shard_map/ppermute | solution.py:20
  89.1 2.8 %copy-start.2 = (bf16[512,3,2048]{2,0,1:T(8,128)(2,1)S(1)}, bf16[512,3,2048]{2,0,1:T(8,128)(2,1)}, u32[]{:S(2)}) copy-start(bf16[512,3,2048]{2,0,1:T(8,128)(2,1)} %param.5) | copy-start | bytes 18874372
  95.3 4.8 %copy-start.6 = (bf16[384,2048]{1,0:T(8,128)(2,1)S(1)}, bf16[384,2048]{1,0:T(8,128)(2,1)}, u32[]{:S(2)}) copy-start(bf16[384,2048]{1,0:T(8,128)(2,1)} %copy-done.5) | copy-start | bytes 4718596
  95.3 4.8 %copy-start.8 = (bf16[3,384,128]{2,1,0:T(8,128)(2,1)S(1)}, bf16[3,384,128]{2,1,0:T(8,128)(2,1)}, u32[]{:S(2)}) copy-start(bf16[3,384,128]{2,1,0:T(8,128)(2,1)} %copy-done.7) | copy-start | bytes 884740
  95.3 4.8 %copy-start.10 = (bf16[3,384,128]{2,1,0:T(8,128)(2,1)S(1)}, bf16[3,384,128]{2,1,0:T(8,128)(2,1)}, u32[]{:S(2)}) copy-start(bf16[3,384,128]{2,1,0:T(8,128)(2,1)} %copy-done.9) | copy-start | bytes 884740
  96.6 9.9 %collective-permute-start.19 = (bf16[384,512]{1,0:T(8,128)(2,1)S(1)}, bf16[384,512]{1,0:T(8,128)(2,1)S(1)}, u32[]{:S(2)}, u32[]{:S(2)}) collective-permute-start(bf16[384,512]{1,0:T(8,128)(2,1)S(1)} %add_convert_fusion.10), channel_id=1, source_target_pairs={{0,8},{8,0},{16,24},{24,16},{1,9},{9,1},{17,25},{25,17},{2,10},{10... | collective-permute-start | bytes 1179656 | tf_op jit(solution)/shard_map/ppermute | solution.py:20
  99.5 7.2 %collective-permute-start.20 = (bf16[384,512]{1,0:T(8,128)(2,1)S(1)}, bf16[384,512]{1,0:T(8,128)(2,1)S(1)}, u32[]{:S(2)}, u32[]{:S(2)}) collective-permute-start(bf16[384,512]{1,0:T(8,128)(2,1)S(1)} %add_convert_fusion.9), channel_id=1, source_target_pairs={{0,0},{8,16},{16,8},{24,24},{1,1},{9,17},{17,9},{25,25},{2,2},{10,... | collective-permute-start | bytes 1179656 | tf_op jit(solution)/shard_map/ppermute | solution.py:541
  106.5 5.6 %copy-start.12 = (bf16[3,384,128]{2,1,0:T(8,128)(2,1)S(1)}, bf16[3,384,128]{2,1,0:T(8,128)(2,1)}, u32[]{:S(2)}) copy-start(bf16[3,384,128]{2,1,0:T(8,128)(2,1)} %copy-done.11) | copy-start | bytes 884740
  106.5 5.6 %copy-start.14 = (bf16[3,384,128]{2,1,0:T(8,128)(2,1)S(1)}, bf16[3,384,128]{2,1,0:T(8,128)(2,1)}, u32[]{:S(2)}) copy-start(bf16[3,384,128]{2,1,0:T(8,128)(2,1)} %copy-done.13) | copy-start | bytes 884740
  106.5 5.6 %copy-start.16 = (bf16[3,384,128]{2,1,0:T(8,128)(2,1)S(1)}, bf16[3,384,128]{2,1,0:T(8,128)(2,1)}, u32[]{:S(2)}) copy-start(bf16[3,384,128]{2,1,0:T(8,128)(2,1)} %copy-done.15) | copy-start | bytes 884740
  106.5 5.6 %copy-start.18 = (bf16[3,384,128]{2,1,0:T(8,128)(2,1)S(1)}, bf16[3,384,128]{2,1,0:T(8,128)(2,1)}, u32[]{:S(2)}) copy-start(bf16[3,384,128]{2,1,0:T(8,128)(2,1)} %copy-done.17) | copy-start | bytes 884740
  106.8 11.6 %collective-permute-start.22 = (bf16[384,512]{1,0:T(8,128)(2,1)S(1)}, bf16[384,512]{1,0:T(8,128)(2,1)S(1)}, u32[]{:S(2)}, u32[]{:S(2)}) collective-permute-start(bf16[384,512]{1,0:T(8,128)(2,1)S(1)} %get-tuple-element.102), channel_id=1, source_target_pairs={{0,8},{8,0},{16,24},{24,16},{1,9},{9,1},{17,25},{25,17},{2,10},{10... | collective-permute-start | bytes 1179656 | tf_op jit(solution)/shard_map/ppermute | solution.py:20
  111.3 7.2 %collective-permute-start.23 = (bf16[384,512]{1,0:T(8,128)(2,1)S(1)}, bf16[384,512]{1,0:T(8,128)(2,1)S(1)}, u32[]{:S(2)}, u32[]{:S(2)}) collective-permute-start(bf16[384,512]{1,0:T(8,128)(2,1)S(1)} %add_convert_fusion.7), channel_id=1, source_target_pairs={{0,0},{8,16},{16,8},{24,24},{1,1},{9,17},{17,9},{25,25},{2,2},{10,... | collective-permute-start | bytes 1179656 | tf_op jit(solution)/shard_map/ppermute | solution.py:541
  118.4 3.4 %copy-start.24 = (bf16[416,128]{1,0:T(8,128)(2,1)S(1)}, bf16[416,128]{1,0:T(8,128)(2,1)}, u32[]{:S(2)}) copy-start(bf16[416,128]{1,0:T(8,128)(2,1)} %copy-done.23) | copy-start | bytes 319492
  118.7 11.8 %collective-permute-start.24 = (bf16[384,512]{1,0:T(8,128)(2,1)S(1)}, bf16[384,512]{1,0:T(8,128)(2,1)S(1)}, u32[]{:S(2)}, u32[]{:S(2)}) collective-permute-start(bf16[384,512]{1,0:T(8,128)(2,1)S(1)} %get-tuple-element.100), channel_id=1, source_target_pairs={{0,8},{8,0},{16,24},{24,16},{1,9},{9,1},{17,25},{25,17},{2,10},{10... | collective-permute-start | bytes 1179656 | tf_op jit(solution)/shard_map/ppermute | solution.py:20
  129.8 1.5 collective-permute-start.25
  130.6 13.7 %collective-permute-start.26 = (bf16[384,512]{1,0:T(8,128)(2,1)S(1)}, bf16[384,512]{1,0:T(8,128)(2,1)S(1)}, u32[]{:S(2)}, u32[]{:S(2)}) collective-permute-start(bf16[384,512]{1,0:T(8,128)(2,1)S(1)} %add_convert_fusion.2), channel_id=1, source_target_pairs={{0,0},{8,16},{16,8},{24,24},{1,1},{9,17},{17,9},{25,25},{2,2},{10,... | collective-permute-start | bytes 1179656 | tf_op jit(solution)/shard_map/ppermute | solution.py:541
  131.4 22.1 %collective-permute-start.27 = (bf16[384,512]{1,0:T(8,128)(2,1)S(1)}, bf16[384,512]{1,0:T(8,128)(2,1)S(1)}, u32[]{:S(2)}, u32[]{:S(2)}) collective-permute-start(bf16[384,512]{1,0:T(8,128)(2,1)S(1)} %add_convert_fusion.1), channel_id=1, source_target_pairs={{0,8},{8,0},{16,24},{24,16},{1,9},{9,1},{17,25},{25,17},{2,10},{10... | collective-permute-start | bytes 1179656 | tf_op jit(solution)/shard_map/ppermute | solution.py:20
  144.4 16.6 %collective-permute-start.28 = (bf16[384,512]{1,0:T(8,128)(2,1)S(1)}, bf16[384,512]{1,0:T(8,128)(2,1)S(1)}, u32[]{:S(2)}, u32[]{:S(2)}) collective-permute-start(bf16[384,512]{1,0:T(8,128)(2,1)S(1)} %add_convert_fusion), channel_id=1, source_target_pairs={{0,8},{8,0},{16,24},{24,16},{1,9},{9,1},{17,25},{25,17},{2,10},{10... | collective-permute-start | bytes 1179656 | tf_op jit(solution)/shard_map/ppermute | solution.py:20

commit v7 on v6

--- a/solution.py
+++ b/solution.py
@@ -110,60 +110,90 @@
     return terms
 
 
-def split_kernel(place, up_ref, *out_refs, n_depth):
-    width = out_refs[0].shape[1]
-    for k, ref in enumerate(out_refs):
-        at = ((place[1] ^ k) * n_depth + place[0]) * width
-        ref[...] = up_ref[:, pl.ds(pl.multiple_of(at, width), width)]
-
-
-def split(place, up, n_col, n_depth):
-    tok, width = up.shape[0], up.shape[1] // (n_col * n_depth)
-    if width % LANES:
-        blocks = up.reshape(tok, n_col * n_depth, width)
-        at = [(place[1] ^ k) * n_depth + place[0] for k in range(n_col)]
-        return [lax.dynamic_index_in_dim(blocks, i, 1, keepdims=False) for i in at]
+def split_lanes_kernel(place, *refs, n_col):
+    in_refs, out_refs = refs[:n_col], refs[n_col:]
+    width = out_refs[0].shape[2]
+    for r, ref in enumerate(out_refs):
+        lanes = pl.ds(pl.multiple_of((place[0] ^ r) * width, width), width)
+        for k in range(n_col):
+            ref[k] = in_refs[k][:, lanes]
+
+
+def split_rows_kernel(place, *refs, n_col):
+    in_refs, out_refs = refs[:n_col], refs[n_col:]
+    local = out_refs[0].shape[1] - 32
+    for r, ref in enumerate(out_refs):
+        rows = pl.ds(pl.multiple_of((place[0] ^ r) * local, 16), local)
+        for k in range(n_col):
+            ref[k, 0:local] = in_refs[k][rows, :]
+            ref[k, local:] = in_refs[k][-32:, :]
+
+
+def split(kernel, place, arrays, n_depth, shape):
+    whole = (len(arrays),) + shape
     return pl.pallas_call(
-        functools.partial(split_kernel, n_depth=n_depth),
+        functools.partial(kernel, n_col=len(arrays)),
         grid_spec=pltpu.PrefetchScalarGridSpec(
             num_scalar_prefetch=1,
             grid=(1,),
-            in_specs=[resident(up.shape, width)],
-            out_specs=[resident((tok, width), width)] * n_col,
+            in_specs=[resident(value.shape, shape[1]) for value in arrays],
+            out_specs=[resident(whole, shape[1])] * n_depth,
         ),
-        out_shape=[jax.ShapeDtypeStruct((tok, width), jnp.bfloat16)] * n_col,
-        compiler_params=params(4, width),
+        out_shape=[jax.ShapeDtypeStruct(whole, jnp.bfloat16)] * n_depth,
+        compiler_params=params(4, shape[1]),
         cost_estimate=SMALL,
         name="split",
-    )(place, up)
-
-
-def join_kernel(place, _, blocks_ref, out_ref, grad_taps_ref):
-    n_depth, n_col, rows, width = blocks_ref.shape
+    )(place, *arrays)
+
+
+def split_lanes(place, arrays, n_depth):
+    local, width = arrays[0].shape[0], arrays[0].shape[1] // n_depth
+    if width % LANES:
+        whole = jnp.stack(arrays)
+        return [lax.dynamic_slice_in_dim(whole, (place[0] ^ r) * width, width, axis=2) for r in range(n_depth)]
+    return split(split_lanes_kernel, place, arrays, n_depth, (local, width))
+
+
+def split_rows(place, arrays, n_depth):
+    local, width = (arrays[0].shape[0] - 32) // n_depth, arrays[0].shape[1]
+    if width % LANES:
+        whole = jnp.stack(arrays)
+        return [
+            jnp.concatenate(
+                [lax.dynamic_slice_in_dim(whole, (place[0] ^ r) * local, local, axis=1), whole[:, -32:]], axis=1
+            )
+            for r in range(n_depth)
+        ]
+    return split(split_rows_kernel, place, arrays, n_depth, (local + 32, width))
+
+
+def join_kernel(place, _, *refs):
+    block_refs, (out_ref, grad_taps_ref) = refs[:-2], refs[-2:]
+    n_depth = len(block_refs)
+    n_col, _, width = block_refs[0].shape
     local, groups = out_ref.shape[0], grad_taps_ref.shape[1]
     lane_group = lax.broadcasted_iota(jnp.int32, (width, groups), 0) // GROUP
     group = lax.broadcasted_iota(jnp.int32, (width, groups), 1)
     total = jnp.zeros((24, groups), jnp.float32)
-    mine = pl.ds(pl.multiple_of(place[0] * local, 16), local)
-    for p in range(n_depth):
+    for r, ref in enumerate(block_refs):
         for k in range(n_col):
-            at = (place[1] ^ k) * n_depth + p
-            out_ref[:, pl.ds(pl.multiple_of(at * width, width), width)] = blocks_ref[p, k, mine, :]
+            at = (place[1] ^ k) * n_depth + (place[0] ^ r)
+            out_ref[:, pl.ds(pl.multiple_of(at * width, width), width)] = ref[k, 0:local, :]
             spread = (lane_group + at * (width // GROUP) == group).astype(jnp.bfloat16)
-            sums = blocks_ref[p, k, rows - 32 : rows - 8, :]
-            total = total + jnp.dot(sums, spread, preferred_element_type=jnp.float32)
+            total = total + jnp.dot(ref[k, local : local + 24, :], spread, preferred_element_type=jnp.float32)
     grad_taps_ref[...] = (total[0:8] + total[8:16] + total[16:24])[:KT]
 
 
-def join(place, mark, blocks, local, groups):
-    n_depth, n_col, rows, width = blocks.shape
+def join(place, mark, blocks, groups):
+    n_depth = len(blocks)
+    n_col, rows, width = blocks[0].shape
+    local = rows - 32
     if width % LANES:
-        blocks = blocks[:, place[1] ^ jnp.arange(n_col)]
-        mine = lax.dynamic_slice_in_dim(blocks, place[0] * local, local, axis=2)
-        sums = blocks[:, :, rows - 32 : rows - 8].astype(jnp.float32)
+        whole = jnp.stack(blocks)[place[0] ^ jnp.arange(n_depth)][:, place[1] ^ jnp.arange(n_col)]
+        sums = whole[:, :, local : local + 24].astype(jnp.float32)
         sums = sums.reshape(n_depth, n_col, 3, 8, width // GROUP, GROUP).sum(axis=(2, 5))[:, :, :KT]
         return (
-            jnp.transpose(mine, (2, 1, 0, 3)).reshape(local, -1),
+            jnp.transpose(whole[:, :, :local], (2, 1, 0, 3)).reshape(local, -1),
             jnp.transpose(sums, (2, 1, 0, 3)).reshape(KT, -1),
         )
     channels = n_depth * n_col * width
@@ -172,7 +202,7 @@
         grid_spec=pltpu.PrefetchScalarGridSpec(
             num_scalar_prefetch=1,
             grid=(1,),
-            in_specs=[pl.BlockSpec(memory_space=pl.ANY), resident(blocks.shape, width)],
+            in_specs=[pl.BlockSpec(memory_space=pl.ANY)] + [resident(blocks[0].shape, width)] * n_depth,
             out_specs=[resident((local, channels), width), resident((KT, groups), width)],
         ),
         out_shape=[
@@ -182,11 +212,11 @@
         compiler_params=params(4, width),
         cost_estimate=SMALL,
         name="join",
-    )(place, mark, blocks)
-
-
-def middle_kernel(place, taps_ref, *refs, groups, terms, tile):
-    up_refs, refs = refs[:groups], refs[groups:]
+    )(place, mark, *blocks)
+
+
+def middle_kernel(place, taps_ref, *refs, devices, groups, terms, tile):
+    up_refs, refs = refs[:devices], refs[devices:]
     part_refs = refs[: groups * terms]
     grad_refs = refs[groups * terms : groups * terms + groups]
     out_refs = refs[groups * terms + groups : groups * terms + 2 * groups]
@@ -196,8 +226,10 @@
     width = part_refs[0].shape[3]
     total = groups * tok
     tap_groups = taps_ref.shape[1]
-    for k, ref in enumerate(up_refs):
-        up_s[pl.ds(pl.multiple_of((col ^ k) * tok, tok), tok), :] = ref[...]
+    for r, ref in enumerate(up_refs):
+        for k in range(groups):
+            at = (col ^ k) * tok + (place[0] ^ r) * tile
+            up_s[pl.ds(pl.multiple_of(at, tile), tile), :] = ref[k]
     lane_group = lax.broadcasted_iota(jnp.int32, (tap_groups, width), 1) // GROUP
     group = lax.broadcasted_iota(jnp.int32, (tap_groups, width), 0)
     spread = (lane_group + place[3] * (width // GROUP) == group).astype(jnp.bfloat16)
@@ -251,18 +283,19 @@
         ref[tok : tok + 32, :] = packed
 
 
-def middle(place, taps, ups, parts, tile):
-    groups, terms = len(parts), len(parts[0])
+def middle(place, taps, ups, parts):
+    groups, terms, devices = len(parts), len(parts[0]), len(ups)
+    tile = ups[0].shape[1]
     _, _, tok, width = parts[0][0].shape
     total = groups * tok
     whole = lambda *shape: resident(shape, width)
     one = whole(1, 3, tok, width)
     outs = pl.pallas_call(
-        functools.partial(middle_kernel, groups=groups, terms=terms, tile=tile),
+        functools.partial(middle_kernel, devices=devices, groups=groups, terms=terms, tile=tile),
         grid_spec=pltpu.PrefetchScalarGridSpec(
             num_scalar_prefetch=1,
             grid=(1,),
-            in_specs=[whole(*taps.shape)] + [whole(tok, width)] * groups + [one] * (groups * terms),
+            in_specs=[whole(*taps.shape)] + [whole(*ups[0].shape)] * devices + [one] * (groups * terms),
             out_specs=[whole(3, tok, width)] * groups + [whole(tok + 32, width)] * groups,
             scratch_shapes=[
                 pltpu.VMEM((total, width), jnp.bfloat16),
@@ -467,18 +500,20 @@
         return x, [keep, near] + fars, pairs, fars
 
     first = [first_pieces(tokens, k) for k in range(1, n_col)]
-    x, terms, pairs, fars = project_and_sum([tokens], *[piece for of in first for piece in of])
+    span = width * n_depth
+    col_ups = [lax.dynamic_slice_in_dim(upstream, (col_at ^ k) * span, span, axis=1) for k in range(n_col)]
+    col_ups = [up if k == 0 else swap(up, "col", k) for k, up in enumerate(col_ups)]
+    x, terms, pairs, fars = project_and_sum([tokens], *[piece for of in first for piece in of], *col_ups[1:])
     xs, parts = [x], [terms]
-    group_up = lax.all_gather(upstream, "depth", axis=0, tiled=True)
-    ups = split(place, after(group_up, *pairs), n_col, n_depth)
+    ups = split_lanes(place, [after(col_ups[0], *pairs)] + col_ups[1:], n_depth)
+    ups = [up if r == 0 else swap(up, "depth", r) for r, up in enumerate(ups)]
     for k in range(1, n_col):
         x_pieces = other_pieces(tokens, first[k - 1], k)
-        x_pieces[-1] = after(x_pieces[-1], *fars, *ups)
+        x_pieces[-1] = after(x_pieces[-1], *fars, *ups[1:])
         x, terms, pairs, fars = project_and_sum(x_pieces)
         xs.append(x)
         parts.append(terms)
-    ups = [up if k == 0 else swap(up, "col", k) for k, up in enumerate(ups)]
-    own_grads, blocks = middle(place, taps, ups, parts, local_tok)
+    own_grads, blocks = middle(place, taps, ups, parts)
     nears = [swap(own, "depth", 1) for own in own_grads]
     blocks = [block if k == 0 else swap(block, "col", k) for k, block in enumerate(blocks)]
     beside = nears + blocks[1:]
@@ -503,14 +538,11 @@
             behind = [after(lhs[0], *head)] + lhs[1:]
             tail = input_grad(place, behind, w, 1, chunks, chunks)
             parts_of = list(head) + list(tail)
-            got = []
-            for c, part in enumerate(parts_of):
-                got.append(swap(part if c < 3 else after(part, got[c - 2]), "col", k))
-            sent.append((got, parts_of))
+            sent.append(([swap(part, "col", k) for part in parts_of[:3]], parts_of))
+    held = [parts_of[3:] for _, parts_of in sent]
     sent = [of for of, _ in sent]
     own_part = list(input_grad(place, lhs, w, 0, 1, chunks))
     outer = (row_at == 0) | (row_at == 3)
-    blocks = lax.all_gather(after(jnp.stack(blocks), own_part[0]), "depth", axis=0)
     inward, across, summed, done = ([None] * chunks for _ in range(4))
     pair = cross = filled = None
     marks = []
@@ -525,10 +557,16 @@
         if not line:
             if slot < chunks:
                 done[slot] = lax.psum(inward[slot], "row")
+                if slot + 3 < chunks:
+                    for k, parts_of in enumerate(held):
+                        sent[k].append(swap(parts_of[slot], "col", k + 1))
         else:
             if 0 <= slot - 1 < chunks:
                 across[slot - 1] = added(after(inward[slot - 1], *marks), pair)
                 marks = [across[slot - 1]]
+                if slot + 2 < chunks:
+                    for k, parts_of in enumerate(held):
+                        sent[k].append(swap(after(parts_of[slot - 1], *marks), "col", k + 1))
             if 0 <= slot - 2 < chunks:
                 summed[slot - 2] = added(after(across[slot - 2], *marks), cross)
                 marks = [summed[slot - 2]]
@@ -548,11 +586,15 @@
             of = [group[i] for i in (r, r + 1) for group in grads]
             filled = weight_grad(place, filled, [after(of[0], *marks)] + of[1:], xs, r, n_depth)
             marks = [filled[1]]
+        if slot == chunks - 1:
+            blocks = split_rows(place, [after(blocks[0], *marks)] + blocks[1:], n_depth)
+            blocks = [block if r == 0 else swap(block, "depth", r) for r, block in enumerate(blocks)]
+            late = blocks[1:]
         if slot == chunks:
-            marks.append(blocks)
+            marks += late
     grad_tokens = jnp.concatenate(done, axis=1)
     grad_weight = jnp.transpose(filled[0], (1, 0, 2))
-    output, grad_taps = join(place, filled[1], after(blocks, *marks), local_tok, taps.shape[1])
+    output, grad_taps = join(place, filled[1], [after(blocks[0], *marks)] + blocks[1:], taps.shape[1])
     return (output, grad_tokens, grad_weight, grad_taps)
 
 

time: 163 us -> 147 us (0.902)
  blocking collectives: 20.5 us -> 0 us
  waiting for transfers between devices: 37.2 us -> 43.5 us
  starting transfers between devices: 51.8 us -> 47.9 us
    all_gather x2 -> x0, blocking collectives: 20.5 us -> none  [the longest x1 12.5 us: on_device(): group_up = lax.all_gather(upstream, 'depth', axis=0, tiled=True)]
    ppermute x25 -> x31, waiting for transfers between devices: 37.2 us -> 43.5 us  [swap(): return lax.ppermute(value, axis, [(i, i ^ flip) for i in range(count)])]
    ppermute x25 -> x31, starting transfers between devices: 49.1 us -> 45.2 us  [swap(): return lax.ppermute(value, axis, [(i, i ^ flip) for i in range(count)])]
  transfers between devices with their start and end apart: 29 -> 35, of which waited for: 10 -> 12; matrix products, arithmetic and copies ran while one was open for 3% -> 4% of each run, Pallas kernels for 18% -> 21%
where the time goes in v7:
time: 147 us; the launch traced here: 146 us
  starting transfers between devices  47.9 us (33%)
  waiting for transfers between devices  43.5 us (30%)
  Pallas kernels  35.8 us (24%)
  local copies, waits for them, and re-layouts  11.9 us (8%)
  other arithmetic  6.08 us (4%)
    ppermute x31, starting transfers between devices, swap(): return lax.ppermute(value, axis, [(i, i ^ flip) for i in range(count)])  45.2 us
    ppermute x31, waiting for transfers between devices, swap(): return lax.ppermute(value, axis, [(i, i ^ flip) for i in range(count)])  43.5 us
    pallas_call x2, Pallas kernels, weight_grad(): pl.pallas_call(functools.partial(weight_grad_kernel, chained=chained, gro...  12.4 us
    pallas_call x4, Pallas kernels, input_grad(): pl.pallas_call(functools.partial(input_grad_kernel, terms=len(grads), wid...  10.2 us
    unnamed x50, local copies, waits for them, and re-layouts  9.81 us
    pallas_call x2, Pallas kernels, project(): pl.pallas_call(functools.partial(project_kernel, pieces=len(xs), count=co...  7.73 us
  transfers between devices with their start and end apart: 35, of which 12 were waited for; matrix products, arithmetic and copies ran while one was open for 4% of the time, Pallas kernels for 21%

profile of v7, /device:TPU:0, one launch (start us, length us, event | category | flops | bytes accessed | tf_op | source)
XLA Modules:
  0.0 146.4 jit_solution(7685468308636230823)
XLA Ops:
  0.6 1.1 constant_dynamic-slice_fusion.1
  1.7 3.0 %collective-permute-start = (bf16[128,2048]{1,0:T(8,128)(2,1)S(1)}, bf16[128,2048]{1,0:T(8,128)(2,1)S(1)}, u32[]{:S(2)}, u32[]{:S(2)}) collective-permute-start(bf16[128,2048]{1,0:T(8,128)(2,1)S(1)} %constant_dynamic-slice_fusion.1), channel_id=1, source_target_pairs={{0,4},{4,0},{1,5},{5,1},{2,6},{6,2},{3,7},{7,3},{8,12},{12,8},{9,1... | collective-permute-start | bytes 1572872 | tf_op jit(solution)/shard_map/ppermute | solution.py:20
  4.8 1.0 constant_dynamic-slice_fusion
  5.9 2.8 %copy-done = bf16[512,3,2048]{2,0,1:T(8,128)(2,1)S(1)} copy-done((bf16[512,3,2048]{2,0,1:T(8,128)(2,1)S(1)}, bf16[512,3,2048]{2,0,1:T(8,128)(2,1)}, u32[]{:S(2)}) %copy-start) | copy-done | bytes 6291480
  8.7 1.4 copy-done.3
  10.1 3.8 %project.2 = (bf16[2,3,384,128]{3,2,1,0:T(8,128)(2,1)S(1)}, bf16[2,3,384,128]{3,2,1,0:T(8,128)(2,1)S(1)}) custom-call(s32[4]{0:T(128)S(1)} %pad_add_fusion.place, bf16[384,2048]{1,0:T(8,128)(2,1)S(1)} %copy-done.3, bf16[3,512,2048]{2,1,0:T(8,128)(2,1)S(1)} %bitcast.6), custom_call_target="tpu_custom_call" | custom-call | flops 1 | bytes 1 | tf_op jit(solution)/shard_map/project/pallas_call | solution.py:87
  13.9 4.9 %collective-permute-done.1.refs_1_ = bf16[96,512]{1,0:T(8,128)(2,1)S(1)} collective-permute-done((bf16[96,512]{1,0:T(8,128)(2,1)S(1)}, bf16[96,512]{1,0:T(8,128)(2,1)S(1)}, u32[]{:S(2)}, u32[]{:S(2)}) %collective-permute-start.1) | collective-permute-done | bytes 98336 | tf_op jit(solution)/shard_map/ppermute | solution.py:20
  18.8 1.8 %collective-permute-start.8 = (bf16[128,2048]{1,0:T(8,128)(2,1)S(1)}, bf16[128,2048]{1,0:T(8,128)(2,1)S(1)}, u32[]{:S(2)}, u32[]{:S(2)}) collective-permute-start(bf16[128,2048]{1,0:T(8,128)(2,1)S(1)} %slice.17), channel_id=1, source_target_pairs={{0,4},{4,0},{1,5},{5,1},{2,6},{6,2},{3,7},{7,3},{8,12},{12,8},{9,1... | collective-permute-start | bytes 1572872 | tf_op jit(solution)/shard_map/ppermute | solution.py:20
  20.7 1.6 %collective-permute-start.7 = (bf16[128,2048]{1,0:T(8,128)(2,1)S(1)}, bf16[128,2048]{1,0:T(8,128)(2,1)S(1)}, u32[]{:S(2)}, u32[]{:S(2)}) collective-permute-start(bf16[128,2048]{1,0:T(8,128)(2,1)S(1)} %collective-permute-done.refs_0_), channel_id=1, source_target_pairs={{0,8},{8,0},{16,24},{24,16},{1,9},{9,1},{17,25},{25,17},{2,10},{10... | collective-permute-start | bytes 1572872 | tf_op jit(solution)/shard_map/ppermute | solution.py:20
  22.3 1.6 %collective-permute-start.6 = (bf16[1,3,384,128]{3,2,1,0:T(8,128)(2,1)S(1)}, bf16[1,3,384,128]{3,2,1,0:T(8,128)(2,1)S(1)}, u32[]{:S(2)}, u32[]{:S(2)}) collective-permute-start(bf16[1,3,384,128]{3,2,1,0:T(8,128)(2,1)S(1)} %add_convert_fusion.13), channel_id=1, source_target_pairs={{0,2},{1,3},{2,0},{3,1},{4,6},{5,7},{6,4},{7,5},{8,10},{9,11},{10,... | collective-permute-start | bytes 884744 | tf_op jit(solution)/shard_map/ppermute | solution.py:20
  23.9 0.6 split.2
  24.5 0.6 collective-permute-start.4
  25.1 8.1 %collective-permute-done.8.refs_2_ = bf16[128,2048]{1,0:T(8,128)(2,1)S(1)} collective-permute-done((bf16[128,2048]{1,0:T(8,128)(2,1)S(1)}, bf16[128,2048]{1,0:T(8,128)(2,1)S(1)}, u32[]{:S(2)}, u32[]{:S(2)}) %collective-permute-start.8) | collective-permute-done | bytes 524320 | tf_op jit(solution)/shard_map/ppermute | solution.py:20
  33.2 1.0 collective-permute-start.5
  34.3 2.7 %collective-permute-done.5.refs_3_ = bf16[2,96,128]{2,1,0:T(8,128)(2,1)S(1)} collective-permute-done((bf16[2,96,128]{2,1,0:T(8,128)(2,1)S(1)}, bf16[2,96,128]{2,1,0:T(8,128)(2,1)S(1)}, u32[]{:S(2)}, u32[]{:S(2)}) %collective-permute-start.5) | collective-permute-done | bytes 49184 | tf_op jit(solution)/shard_map/ppermute | solution.py:20
  37.0 4.0 %project.3 = (bf16[2,3,384,128]{3,2,1,0:T(8,128)(2,1)S(1)}, bf16[2,3,384,128]{3,2,1,0:T(8,128)(2,1)S(1)}, bf16[384,2048]{1,0:T(8,128)(2,1)S(1)}) custom-call(s32[4]{0:T(128)S(1)} %pad_add_fusion.place, bf16[128,2048]{1,0:T(8,128)(2,1)S(1)} %collective-permute-done.refs_0_, bf16[128,2048]{1,0:T(8,128)(2,1)S(1)} %collective-permute-done.7.refs_1_, ...), custom_call_target="tpu_custom_call" | custom-call | flops 1 | bytes 1 | tf_op jit(solution)/shard_map/project/pallas_call | solution.py:87
  41.2 1.9 %collective-permute-done.9.refs_8_ = bf16[2,3,384,128]{3,2,1,0:T(8,128)(2,1)S(1)} collective-permute-done((bf16[2,3,384,128]{3,2,1,0:T(8,128)(2,1)S(1)}, bf16[2,3,384,128]{3,2,1,0:T(8,128)(2,1)S(1)}, u32[]{:S(2)}, u32[]{:S(2)}) %collective-permute-start.9) | collective-permute-done | bytes 589856 | tf_op jit(solution)/shard_map/ppermute | solution.py:20
  43.2 1.9 %collective-permute-start.10 = (bf16[1,3,384,128]{3,2,1,0:T(8,128)(2,1)S(1)}, bf16[1,3,384,128]{3,2,1,0:T(8,128)(2,1)S(1)}, u32[]{:S(2)}, u32[]{:S(2)}) collective-permute-start(bf16[1,3,384,128]{3,2,1,0:T(8,128)(2,1)S(1)} %add_convert_fusion.12), channel_id=1, source_target_pairs={{0,2},{1,3},{2,0},{3,1},{4,6},{5,7},{6,4},{7,5},{8,10},{9,11},{10,... | collective-permute-start | bytes 884744 | tf_op jit(solution)/shard_map/ppermute | solution.py:20
  45.1 7.3 %collective-permute-done.10.refs_9_ = bf16[1,3,384,128]{3,2,1,0:T(8,128)(2,1)S(1)} collective-permute-done((bf16[1,3,384,128]{3,2,1,0:T(8,128)(2,1)S(1)}, bf16[1,3,384,128]{3,2,1,0:T(8,128)(2,1)S(1)}, u32[]{:S(2)}, u32[]{:S(2)}) %collective-permute-start.10) | collective-permute-done | bytes 294944 | tf_op jit(solution)/shard_map/ppermute | solution.py:20
  52.4 1.5 %middle.1 = (bf16[3,384,128]{2,1,0:T(8,128)(2,1)S(1)}, bf16[3,384,128]{2,1,0:T(8,128)(2,1)S(1)}, bf16[416,128]{1,0:T(8,128)(2,1)S(1)}, bf16[416,128]{1,0:T(8,128)(2,1)S(1)}) custom-call(s32[4]{0:T(128)S(1)} %pad_add_fusion.place, f32[7,64]{1,0:T(8,128)S(1)} %copy-done.21, bf16[2,96,128]{2,1,0:T(8,128)(2,1)S(1)} %get-tuple-element.62.refs_0_, ...), custom_call_target="tpu_custom_call" | custom-call | flops 1 | bytes 1 | tf_op jit(solution)/shard_map/middle/pallas_call | solution.py:293
  54.6 1.7 %collective-permute-start.11 = (bf16[3,384,128]{2,1,0:T(8,128)(2,1)S(1)}, bf16[3,384,128]{2,1,0:T(8,128)(2,1)S(1)}, u32[]{:S(2)}, u32[]{:S(2)}) collective-permute-start(bf16[3,384,128]{2,1,0:T(8,128)(2,1)S(1)} %get-tuple-element.72.refs_0_.refs_3_), channel_id=1, source_target_pairs={{0,2},{1,3},{2,0},{3,1},{4,6},{5,7},{6,4},{7,5},{8,10},{9,11},{10,... | collective-permute-start | bytes 884744 | tf_op jit(solution)/shard_map/ppermute | solution.py:20
  56.3 1.5 %collective-permute-start.14 = (bf16[416,128]{1,0:T(8,128)(2,1)S(1)}, bf16[416,128]{1,0:T(8,128)(2,1)S(1)}, u32[]{:S(2)}, u32[]{:S(2)}) collective-permute-start(bf16[416,128]{1,0:T(8,128)(2,1)S(1)} %get-tuple-element.73), channel_id=1, source_target_pairs={{0,4},{4,0},{1,5},{5,1},{2,6},{6,2},{3,7},{7,3},{8,12},{12,8},{9,1... | collective-permute-start | bytes 319496 | tf_op jit(solution)/shard_map/ppermute | solution.py:20
  57.8 3.2 %collective-permute-done.14.refs_1_ = bf16[416,128]{1,0:T(8,128)(2,1)S(1)} collective-permute-done((bf16[416,128]{1,0:T(8,128)(2,1)S(1)}, bf16[416,128]{1,0:T(8,128)(2,1)S(1)}, u32[]{:S(2)}, u32[]{:S(2)}) %collective-permute-start.14) | collective-permute-done | bytes 106528 | tf_op jit(solution)/shard_map/ppermute | solution.py:20
  61.0 0.6 copy-done.19
  61.7 1.9 %collective-permute-done.11.refs_2_.refs_1_ = bf16[3,384,128]{2,1,0:T(8,128)(2,1)S(1)} collective-permute-done((bf16[3,384,128]{2,1,0:T(8,128)(2,1)S(1)}, bf16[3,384,128]{2,1,0:T(8,128)(2,1)S(1)}, u32[]{:S(2)}, u32[]{:S(2)}) %collective-permute-start.11) | collective-permute-done | bytes 294944 | tf_op jit(solution)/shard_map/ppermute | solution.py:20
  63.6 1.6 %collective-permute-done.15.refs_3_ = bf16[3,384,128]{2,1,0:T(8,128)(2,1)S(1)} collective-permute-done((bf16[3,384,128]{2,1,0:T(8,128)(2,1)S(1)}, bf16[3,384,128]{2,1,0:T(8,128)(2,1)S(1)}, u32[]{:S(2)}, u32[]{:S(2)}) %collective-permute-start.15) | collective-permute-done | bytes 294944 | tf_op jit(solution)/shard_map/ppermute | solution.py:20
  65.1 1.7 %collective-permute-start.16 = (bf16[3,384,128]{2,1,0:T(8,128)(2,1)S(1)}, bf16[3,384,128]{2,1,0:T(8,128)(2,1)S(1)}, u32[]{:S(2)}, u32[]{:S(2)}) collective-permute-start(bf16[3,384,128]{2,1,0:T(8,128)(2,1)S(1)} %get-tuple-element.92.refs_0_.refs_2_), channel_id=1, source_target_pairs={{0,2},{1,3},{2,0},{3,1},{4,6},{5,7},{6,4},{7,5},{8,10},{9,11},{10,... | collective-permute-start | bytes 884744 | tf_op jit(solution)/shard_map/ppermute | solution.py:20
  66.9 0.7 assemble.2.refs_0_
  67.7 0.7 copy-done.13
  68.3 0.7 copy-done.17
  69.1 1.3 input_grad.4
  70.4 1.6 %collective-permute-start.18 = (bf16[384,512]{1,0:T(8,128)(2,1)S(1)}, bf16[384,512]{1,0:T(8,128)(2,1)S(1)}, u32[]{:S(2)}, u32[]{:S(2)}) collective-permute-start(bf16[384,512]{1,0:T(8,128)(2,1)S(1)} %input_grad.4), channel_id=1, source_target_pairs={{0,4},{4,0},{1,5},{5,1},{2,6},{6,2},{3,7},{7,3},{8,12},{12,8},{9,1... | collective-permute-start | bytes 1179656 | tf_op jit(solution)/shard_map/ppermute | solution.py:20
  72.0 4.1 %input_grad.5 = (bf16[384,512]{1,0:T(8,128)(2,1)}, bf16[384,512]{1,0:T(8,128)(2,1)S(1)}, bf16[384,512]{1,0:T(8,128)(2,1)S(1)}) custom-call(s32[4]{0:T(128)S(1)} %pad_add_fusion.place, bf16[384,1536]{1,0:T(8,128)(2,1)S(1)} %assemble.2.refs_0_, bf16[3,512,2048]{2,1,0:T(8,128)(2,1)S(1)} %bitcast.9), custom_call_target="tpu_custom_call" | custom-call | flops 1 | bytes 1 | tf_op jit(solution)/shard_map/input_grad/pallas_call | solution.py:369
  76.2 0.6 collective-permute-start.19
  76.8 1.0 collective-permute-done.17.refs_3_.refs_2_
  77.8 0.7 assemble.3.refs_0_
  78.5 0.7 copy-done.9
  79.2 1.3 input_grad.6
  80.6 1.8 %collective-permute-done.18 = bf16[384,512]{1,0:T(8,128)(2,1)S(1)} collective-permute-done((bf16[384,512]{1,0:T(8,128)(2,1)S(1)}, bf16[384,512]{1,0:T(8,128)(2,1)S(1)}, u32[]{:S(2)}, u32[]{:S(2)}) %collective-permute-start.18) | collective-permute-done | bytes 393248 | tf_op jit(solution)/shard_map/ppermute | solution.py:20
  82.4 0.8 add_convert_fusion.11
  83.3 1.6 %collective-permute-start.20 = (bf16[384,512]{1,0:T(8,128)(2,1)}, bf16[384,512]{1,0:T(8,128)(2,1)}, u32[]{:S(2)}, u32[]{:S(2)}) collective-permute-start(bf16[384,512]{1,0:T(8,128)(2,1)} %add_convert_fusion.11), channel_id=1, source_target_pairs={{0,8},{8,0},{16,24},{24,16},{1,9},{9,1},{17,25},{25,17},{2,10},{10... | collective-permute-start | bytes 1179656 | tf_op jit(solution)/shard_map/ppermute | solution.py:20
  84.9 1.5 %collective-permute-start.21 = (bf16[384,512]{1,0:T(8,128)(2,1)}, bf16[384,512]{1,0:T(8,128)(2,1)S(1)}, u32[]{:S(2)}, u32[]{:S(2)}) collective-permute-start(bf16[384,512]{1,0:T(8,128)(2,1)} %copy-done.24), channel_id=1, source_target_pairs={{0,4},{4,0},{1,5},{5,1},{2,6},{6,2},{3,7},{7,3},{8,12},{12,8},{9,1... | collective-permute-start | bytes 1179656 | tf_op jit(solution)/shard_map/ppermute | solution.py:20
  86.4 2.8 %copy-done.2 = bf16[512,3,2048]{2,0,1:T(8,128)(2,1)S(1)} copy-done((bf16[512,3,2048]{2,0,1:T(8,128)(2,1)S(1)}, bf16[512,3,2048]{2,0,1:T(8,128)(2,1)}, u32[]{:S(2)}) %copy-start.2) | copy-done | bytes 6291480
  89.2 3.4 %input_grad.7 = (bf16[384,512]{1,0:T(8,128)(2,1)S(1)}, bf16[384,512]{1,0:T(8,128)(2,1)S(1)}, bf16[384,512]{1,0:T(8,128)(2,1)S(1)}) custom-call(s32[4]{0:T(128)S(1)} %pad_add_fusion.place, bf16[384,1536]{1,0:T(8,128)(2,1)S(1)} %assemble.3.refs_0_, bf16[3,512,2048]{2,1,0:T(8,128)(2,1)S(1)} %bitcast.11), custom_call_target="tpu_custom_call" | custom-call | flops 1 | bytes 1 | tf_op jit(solution)/shard_map/input_grad/pallas_call | solution.py:369
  92.6 1.2 add_convert_fusion.10
  94.4 1.2 add_convert_fusion.9
  95.6 0.7 collective-permute-start.23
  96.3 1.0 collective-permute-start.24
  97.3 6.2 %weight_grad.2 = (f32[3,512,2048]{2,1,0:T(8,128)}, f32[8,128]{1,0:T(8,128)S(1)}) custom-call(s32[4]{0:T(128)S(1)} %pad_add_fusion.place, bf16[3,384,128]{2,1,0:T(8,128)(2,1)S(1)} %copy-done.8, bf16[3,384,128]{2,1,0:T(8,128)(2,1)S(1)} %collective-permute-done.11.refs_2_.refs_1_, bf16[3,384,128]{2,1,0:T(8,128)(2,1)S(1)} %copy-done.10, ...), custom_call_target="tpu_custom_call" | custom-call | flops 1 | bytes 1 | tf_op jit(solution)/shard_map/weight_grad/pallas_call | solution.py:439
  104.0 4.4 %collective-permute-start.25 = (bf16[384,512]{1,0:T(8,128)(2,1)S(1)}, bf16[384,512]{1,0:T(8,128)(2,1)S(1)}, u32[]{:S(2)}, u32[]{:S(2)}) collective-permute-start(bf16[384,512]{1,0:T(8,128)(2,1)S(1)} %get-tuple-element.114), channel_id=1, source_target_pairs={{0,8},{8,0},{16,24},{24,16},{1,9},{9,1},{17,25},{25,17},{2,10},{10... | collective-permute-start | bytes 1179656 | tf_op jit(solution)/shard_map/ppermute | solution.py:20
  108.4 0.7 collective-permute-start.26
  109.1 6.2 %weight_grad.3 = (f32[3,512,2048]{2,1,0:T(8,128)}, f32[8,128]{1,0:T(8,128)S(1)}) custom-call(s32[4]{0:T(128)S(1)} %pad_add_fusion.place, f32[3,512,2048]{2,1,0:T(8,128)} %get-tuple-element.85.refs_0_, f32[8,128]{1,0:T(8,128)S(1)} %get-tuple-element.86.refs_1_, bf16[3,384,128]{2,1,0:T(8,128)(2,1)S(1)} %copy-done.12, ...), custom_call_target="tpu_custom_call", output_to_operand_aliasing={{0}: (1, {})} | custom-call | flops 1 | bytes 1 | tf_op jit(solution)/shard_map/weight_grad/pallas_call | solution.py:439
  115.7 2.7 %collective-permute-start.27 = (bf16[384,512]{1,0:T(8,128)(2,1)S(1)}, bf16[384,512]{1,0:T(8,128)(2,1)S(1)}, u32[]{:S(2)}, u32[]{:S(2)}) collective-permute-start(bf16[384,512]{1,0:T(8,128)(2,1)S(1)} %get-tuple-element.112), channel_id=1, source_target_pairs={{0,8},{8,0},{16,24},{24,16},{1,9},{9,1},{17,25},{25,17},{2,10},{10... | collective-permute-start | bytes 1179656 | tf_op jit(solution)/shard_map/ppermute | solution.py:20
  118.5 0.7 collective-permute-start.28
  119.2 0.6 split.3
  119.8 0.7 collective-permute-start.30
  120.5 1.2 collective-permute-start.31
  121.7 2.6 %collective-permute-done.27 = bf16[384,512]{1,0:T(8,128)(2,1)S(1)} collective-permute-done((bf16[384,512]{1,0:T(8,128)(2,1)S(1)}, bf16[384,512]{1,0:T(8,128)(2,1)S(1)}, u32[]{:S(2)}, u32[]{:S(2)}) %collective-permute-start.27) | collective-permute-done | bytes 393248 | tf_op jit(solution)/shard_map/ppermute | solution.py:20
  124.3 0.7 collective-permute-start.32
  125.2 3.9 %collective-permute-start.33 = (bf16[384,512]{1,0:T(8,128)(2,1)S(1)}, bf16[384,512]{1,0:T(8,128)(2,1)S(1)}, u32[]{:S(2)}, u32[]{:S(2)}) collective-permute-start(bf16[384,512]{1,0:T(8,128)(2,1)S(1)} %add_convert_fusion.1), channel_id=1, source_target_pairs={{0,8},{8,0},{16,24},{24,16},{1,9},{9,1},{17,25},{25,17},{2,10},{10... | collective-permute-start | bytes 1179656 | tf_op jit(solution)/shard_map/ppermute | solution.py:20
  129.2 7.8 %collective-permute-start.34 = (bf16[384,512]{1,0:T(8,128)(2,1)S(1)}, bf16[384,512]{1,0:T(8,128)(2,1)S(1)}, u32[]{:S(2)}, u32[]{:S(2)}) collective-permute-start(bf16[384,512]{1,0:T(8,128)(2,1)S(1)} %add_convert_fusion), channel_id=1, source_target_pairs={{0,8},{8,0},{16,24},{24,16},{1,9},{9,1},{17,25},{25,17},{2,10},{10... | collective-permute-start | bytes 1179656 | tf_op jit(solution)/shard_map/ppermute | solution.py:20
  137.1 1.4 join.1
  138.5 6.5 %collective-permute-done.34 = bf16[384,512]{1,0:T(8,128)(2,1)S(1)} collective-permute-done((bf16[384,512]{1,0:T(8,128)(2,1)S(1)}, bf16[384,512]{1,0:T(8,128)(2,1)S(1)}, u32[]{:S(2)}, u32[]{:S(2)}) %collective-permute-start.34) | collective-permute-done | bytes 393248 | tf_op jit(solution)/shard_map/ppermute | solution.py:20
  145.0 1.3 pad_maximum_fusion
  (93 shorter events, 3.2 us)
Async XLA Ops:
  1.7 17.1 %collective-permute-start = (bf16[128,2048]{1,0:T(8,128)(2,1)S(1)}, bf16[128,2048]{1,0:T(8,128)(2,1)S(1)}, u32[]{:S(2)}, u32[]{:S(2)}) collective-permute-start(bf16[128,2048]{1,0:T(8,128)(2,1)S(1)} %constant_dynamic-slice_fusion.1), channel_id=1, source_target_pairs={{0,4},{4,0},{1,5},{5,1},{2,6},{6,2},{3,7},{7,3},{8,12},{12,8},{9,1... | collective-permute-start | bytes 1572872 | tf_op jit(solution)/shard_map/ppermute | solution.py:20
  5.7 13.1 %collective-permute-start.1 = (bf16[96,512]{1,0:T(8,128)(2,1)S(1)}, bf16[96,512]{1,0:T(8,128)(2,1)S(1)}, u32[]{:S(2)}, u32[]{:S(2)}) collective-permute-start(bf16[96,512]{1,0:T(8,128)(2,1)S(1)} %get-tuple-element.116), channel_id=1, source_target_pairs={{0,4},{4,0},{1,5},{5,1},{2,6},{6,2},{3,7},{7,3},{8,12},{12,8},{9,1... | collective-permute-start | bytes 294920 | tf_op jit(solution)/shard_map/ppermute | solution.py:20
  5.9 2.8 %copy-start = (bf16[512,3,2048]{2,0,1:T(8,128)(2,1)S(1)}, bf16[512,3,2048]{2,0,1:T(8,128)(2,1)}, u32[]{:S(2)}) copy-start(bf16[512,3,2048]{2,0,1:T(8,128)(2,1)} %param.5) | copy-start | bytes 18874372
  8.7 1.4 copy-start.3
  10.1 8.7 %copy-start.4 = (bf16[384,2048]{1,0:T(8,128)(2,1)S(1)}, bf16[384,2048]{1,0:T(8,128)(2,1)}, u32[]{:S(2)}) copy-start(bf16[384,2048]{1,0:T(8,128)(2,1)} %refs_6_.1) | copy-start | bytes 4718596
  10.1 26.9 %copy-start.1 = (bf16[512,3,2048]{2,0,1:T(8,128)(2,1)S(1)}, bf16[512,3,2048]{2,0,1:T(8,128)(2,1)}, u32[]{:S(2)}) copy-start(bf16[512,3,2048]{2,0,1:T(8,128)(2,1)} %param.5) | copy-start | bytes 18874372
  18.8 3.4 %collective-permute-start.2 = (bf16[2,3,384,128]{3,2,1,0:T(8,128)(2,1)S(1)}, bf16[2,3,384,128]{3,2,1,0:T(8,128)(2,1)S(1)}, u32[]{:S(2)}, u32[]{:S(2)}) collective-permute-start(bf16[2,3,384,128]{3,2,1,0:T(8,128)(2,1)S(1)} %get-tuple-element.60), channel_id=1, source_target_pairs={{0,1},{1,0},{2,3},{3,2},{4,5},{5,4},{6,7},{7,6},{8,9},{9,8},{10,11... | collective-permute-start | bytes 1769480 | tf_op jit(solution)/shard_map/ppermute | solution.py:20
  18.8 14.4 %collective-permute-start.8 = (bf16[128,2048]{1,0:T(8,128)(2,1)S(1)}, bf16[128,2048]{1,0:T(8,128)(2,1)S(1)}, u32[]{:S(2)}, u32[]{:S(2)}) collective-permute-start(bf16[128,2048]{1,0:T(8,128)(2,1)S(1)} %slice.17), channel_id=1, source_target_pairs={{0,4},{4,0},{1,5},{5,1},{2,6},{6,2},{3,7},{7,3},{8,12},{12,8},{9,1... | collective-permute-start | bytes 1572872 | tf_op jit(solution)/shard_map/ppermute | solution.py:20
  20.7 16.4 %collective-permute-start.7 = (bf16[128,2048]{1,0:T(8,128)(2,1)S(1)}, bf16[128,2048]{1,0:T(8,128)(2,1)S(1)}, u32[]{:S(2)}, u32[]{:S(2)}) collective-permute-start(bf16[128,2048]{1,0:T(8,128)(2,1)S(1)} %collective-permute-done.refs_0_), channel_id=1, source_target_pairs={{0,8},{8,0},{16,24},{24,16},{1,9},{9,1},{17,25},{25,17},{2,10},{10... | collective-permute-start | bytes 1572872 | tf_op jit(solution)/shard_map/ppermute | solution.py:20
  22.3 14.7 %collective-permute-start.6 = (bf16[1,3,384,128]{3,2,1,0:T(8,128)(2,1)S(1)}, bf16[1,3,384,128]{3,2,1,0:T(8,128)(2,1)S(1)}, u32[]{:S(2)}, u32[]{:S(2)}) collective-permute-start(bf16[1,3,384,128]{3,2,1,0:T(8,128)(2,1)S(1)} %add_convert_fusion.13), channel_id=1, source_target_pairs={{0,2},{1,3},{2,0},{3,1},{4,6},{5,7},{6,4},{7,5},{8,10},{9,11},{10,... | collective-permute-start | bytes 884744 | tf_op jit(solution)/shard_map/ppermute | solution.py:20
  24.5 9.8 %collective-permute-start.3 = (bf16[2,96,128]{2,1,0:T(8,128)(2,1)S(1)}, bf16[2,96,128]{2,1,0:T(8,128)(2,1)S(1)}, u32[]{:S(2)}, u32[]{:S(2)}) collective-permute-start(bf16[2,96,128]{2,1,0:T(8,128)(2,1)S(1)} %get-tuple-element.63), channel_id=1, source_target_pairs={{0,1},{1,0},{2,3},{3,2},{4,5},{5,4},{6,7},{7,6},{8,9},{9,8},{10,11... | collective-permute-start | bytes 147464 | tf_op jit(solution)/shard_map/ppermute | solution.py:20
  24.5 9.7 %collective-permute-start.4 = (bf16[2,96,128]{2,1,0:T(8,128)(2,1)S(1)}, bf16[2,96,128]{2,1,0:T(8,128)(2,1)S(1)}, u32[]{:S(2)}, u32[]{:S(2)}) collective-permute-start(bf16[2,96,128]{2,1,0:T(8,128)(2,1)S(1)} %get-tuple-element.64), channel_id=1, source_target_pairs={{0,2},{1,3},{2,0},{3,1},{4,6},{5,7},{6,4},{7,5},{8,10},{9,11},{10,... | collective-permute-start | bytes 147464 | tf_op jit(solution)/shard_map/ppermute | solution.py:20
  33.2 19.2 %copy-start.21 = (f32[7,64]{1,0:T(8,128)S(1)}, f32[7,64]{1,0:T(8,128)}, u32[]{:S(2)}) copy-start(f32[7,64]{1,0:T(8,128)} %taps_ref.1) | copy-start | bytes 5380
  33.2 3.8 %collective-permute-start.5 = (bf16[2,96,128]{2,1,0:T(8,128)(2,1)S(1)}, bf16[2,96,128]{2,1,0:T(8,128)(2,1)S(1)}, u32[]{:S(2)}, u32[]{:S(2)}) collective-permute-start(bf16[2,96,128]{2,1,0:T(8,128)(2,1)S(1)} %get-tuple-element.65), channel_id=1, source_target_pairs={{0,3},{1,2},{2,1},{3,0},{4,7},{5,6},{6,5},{7,4},{8,11},{9,10},{10,... | collective-permute-start | bytes 147464 | tf_op jit(solution)/shard_map/ppermute | solution.py:20
  41.0 13.0 %copy-start.5 = (bf16[384,2048]{1,0:T(8,128)(2,1)}, bf16[384,2048]{1,0:T(8,128)(2,1)S(1)}, u32[]{:S(2)}) copy-start(bf16[384,2048]{1,0:T(8,128)(2,1)S(1)} %get-tuple-element.84.refs_5_.refs_7_) | copy-start | bytes 4718596
  41.0 2.1 %collective-permute-start.9 = (bf16[2,3,384,128]{3,2,1,0:T(8,128)(2,1)S(1)}, bf16[2,3,384,128]{3,2,1,0:T(8,128)(2,1)S(1)}, u32[]{:S(2)}, u32[]{:S(2)}) collective-permute-start(bf16[2,3,384,128]{3,2,1,0:T(8,128)(2,1)S(1)} %get-tuple-element.70), channel_id=1, source_target_pairs={{0,1},{1,0},{2,3},{3,2},{4,5},{5,4},{6,7},{7,6},{8,9},{9,8},{10,11... | collective-permute-start | bytes 1769480 | tf_op jit(solution)/shard_map/ppermute | solution.py:20
  43.2 9.3 %collective-permute-start.10 = (bf16[1,3,384,128]{3,2,1,0:T(8,128)(2,1)S(1)}, bf16[1,3,384,128]{3,2,1,0:T(8,128)(2,1)S(1)}, u32[]{:S(2)}, u32[]{:S(2)}) collective-permute-start(bf16[1,3,384,128]{3,2,1,0:T(8,128)(2,1)S(1)} %add_convert_fusion.12), channel_id=1, source_target_pairs={{0,2},{1,3},{2,0},{3,1},{4,6},{5,7},{6,4},{7,5},{8,10},{9,11},{10,... | collective-permute-start | bytes 884744 | tf_op jit(solution)/shard_map/ppermute | solution.py:20
  54.0 23.8 %copy-start.11 = (bf16[3,384,128]{2,1,0:T(8,128)(2,1)}, bf16[3,384,128]{2,1,0:T(8,128)(2,1)S(1)}, u32[]{:S(2)}) copy-start(bf16[3,384,128]{2,1,0:T(8,128)(2,1)S(1)} %get-tuple-element.92.refs_0_.refs_2_) | copy-start | bytes 884740
  54.0 7.7 %collective-permute-start.12 = (bf16[3,384,128]{2,1,0:T(8,128)(2,1)S(1)}, bf16[3,384,128]{2,1,0:T(8,128)(2,1)S(1)}, u32[]{:S(2)}, u32[]{:S(2)}) collective-permute-start(bf16[3,384,128]{2,1,0:T(8,128)(2,1)S(1)} %get-tuple-element.92.refs_0_.refs_2_), channel_id=1, source_target_pairs={{0,1},{1,0},{2,3},{3,2},{4,5},{5,4},{6,7},{7,6},{8,9},{9,8},{10,11... | collective-permute-start | bytes 884744 | tf_op jit(solution)/shard_map/ppermute | solution.py:20
  54.1 7.6 %collective-permute-start.13 = (bf16[3,384,128]{2,1,0:T(8,128)(2,1)S(1)}, bf16[3,384,128]{2,1,0:T(8,128)(2,1)S(1)}, u32[]{:S(2)}, u32[]{:S(2)}) collective-permute-start(bf16[3,384,128]{2,1,0:T(8,128)(2,1)S(1)} %get-tuple-element.72.refs_0_.refs_3_), channel_id=1, source_target_pairs={{0,1},{1,0},{2,3},{3,2},{4,5},{5,4},{6,7},{7,6},{8,9},{9,8},{10,11... | collective-permute-start | bytes 884744 | tf_op jit(solution)/shard_map/ppermute | solution.py:20
  54.6 9.0 %collective-permute-start.11 = (bf16[3,384,128]{2,1,0:T(8,128)(2,1)S(1)}, bf16[3,384,128]{2,1,0:T(8,128)(2,1)S(1)}, u32[]{:S(2)}, u32[]{:S(2)}) collective-permute-start(bf16[3,384,128]{2,1,0:T(8,128)(2,1)S(1)} %get-tuple-element.72.refs_0_.refs_3_), channel_id=1, source_target_pairs={{0,2},{1,3},{2,0},{3,1},{4,6},{5,7},{6,4},{7,5},{8,10},{9,11},{10,... | collective-permute-start | bytes 884744 | tf_op jit(solution)/shard_map/ppermute | solution.py:20
  56.3 4.7 %collective-permute-start.14 = (bf16[416,128]{1,0:T(8,128)(2,1)S(1)}, bf16[416,128]{1,0:T(8,128)(2,1)S(1)}, u32[]{:S(2)}, u32[]{:S(2)}) collective-permute-start(bf16[416,128]{1,0:T(8,128)(2,1)S(1)} %get-tuple-element.73), channel_id=1, source_target_pairs={{0,4},{4,0},{1,5},{5,1},{2,6},{6,2},{3,7},{7,3},{8,12},{12,8},{9,1... | collective-permute-start | bytes 319496 | tf_op jit(solution)/shard_map/ppermute | solution.py:20
  61.0 0.6 copy-start.19
  61.7 16.1 %copy-start.15 = (bf16[3,384,128]{2,1,0:T(8,128)(2,1)}, bf16[3,384,128]{2,1,0:T(8,128)(2,1)S(1)}, u32[]{:S(2)}) copy-start(bf16[3,384,128]{2,1,0:T(8,128)(2,1)S(1)} %collective-permute-done.12.refs_1_.refs_4_) | copy-start | bytes 884740
  63.6 1.6 %collective-permute-start.15 = (bf16[3,384,128]{2,1,0:T(8,128)(2,1)S(1)}, bf16[3,384,128]{2,1,0:T(8,128)(2,1)S(1)}, u32[]{:S(2)}, u32[]{:S(2)}) collective-permute-start(bf16[3,384,128]{2,1,0:T(8,128)(2,1)S(1)} %collective-permute-done.11.refs_2_.refs_1_), channel_id=1, source_target_pairs={{0,1},{1,0},{2,3},{3,2},{4,5},{5,4},{6,7},{7,6},{8,9},{9,8},{10,11... | collective-permute-start | bytes 884744 | tf_op jit(solution)/shard_map/ppermute | solution.py:20
  65.1 10.9 %collective-permute-start.16 = (bf16[3,384,128]{2,1,0:T(8,128)(2,1)S(1)}, bf16[3,384,128]{2,1,0:T(8,128)(2,1)S(1)}, u32[]{:S(2)}, u32[]{:S(2)}) collective-permute-start(bf16[3,384,128]{2,1,0:T(8,128)(2,1)S(1)} %get-tuple-element.92.refs_0_.refs_2_), channel_id=1, source_target_pairs={{0,2},{1,3},{2,0},{3,1},{4,6},{5,7},{6,4},{7,5},{8,10},{9,11},{10,... | collective-permute-start | bytes 884744 | tf_op jit(solution)/shard_map/ppermute | solution.py:20
  67.6 0.7 copy-start.13
  68.3 0.7 copy-start.17
  70.4 12.1 %collective-permute-start.18 = (bf16[384,512]{1,0:T(8,128)(2,1)S(1)}, bf16[384,512]{1,0:T(8,128)(2,1)S(1)}, u32[]{:S(2)}, u32[]{:S(2)}) collective-permute-start(bf16[384,512]{1,0:T(8,128)(2,1)S(1)} %input_grad.4), channel_id=1, source_target_pairs={{0,4},{4,0},{1,5},{5,1},{2,6},{6,2},{3,7},{7,3},{8,12},{12,8},{9,1... | collective-permute-start | bytes 1179656 | tf_op jit(solution)/shard_map/ppermute | solution.py:20
  76.1 4.5 %copy-start.22 = (bf16[384,512]{1,0:T(8,128)(2,1)}, bf16[384,512]{1,0:T(8,128)(2,1)S(1)}, u32[]{:S(2)}) copy-start(bf16[384,512]{1,0:T(8,128)(2,1)S(1)} %get-tuple-element.97) | copy-start | bytes 1179652
  76.1 4.5 %copy-start.24 = (bf16[384,512]{1,0:T(8,128)(2,1)}, bf16[384,512]{1,0:T(8,128)(2,1)S(1)}, u32[]{:S(2)}) copy-start(bf16[384,512]{1,0:T(8,128)(2,1)S(1)} %get-tuple-element.89) | copy-start | bytes 1179652
  76.1 4.5 %copy-start.7 = (bf16[3,384,128]{2,1,0:T(8,128)(2,1)}, bf16[3,384,128]{2,1,0:T(8,128)(2,1)S(1)}, u32[]{:S(2)}) copy-start(bf16[3,384,128]{2,1,0:T(8,128)(2,1)S(1)} %collective-permute-done.16.refs_2_.refs_0_) | copy-start | bytes 884740
  76.1 1.6 %collective-permute-start.17 = (bf16[3,384,128]{2,1,0:T(8,128)(2,1)S(1)}, bf16[3,384,128]{2,1,0:T(8,128)(2,1)S(1)}, u32[]{:S(2)}, u32[]{:S(2)}) collective-permute-start(bf16[3,384,128]{2,1,0:T(8,128)(2,1)S(1)} %collective-permute-done.16.refs_2_.refs_0_), channel_id=1, source_target_pairs={{0,1},{1,0},{2,3},{3,2},{4,5},{5,4},{6,7},{7,6},{8,9},{9,8},{10,11... | collective-permute-start | bytes 884744 | tf_op jit(solution)/shard_map/ppermute | solution.py:20
  76.2 16.4 %collective-permute-start.19 = (bf16[384,512]{1,0:T(8,128)(2,1)}, bf16[384,512]{1,0:T(8,128)(2,1)}, u32[]{:S(2)}, u32[]{:S(2)}) collective-permute-start(bf16[384,512]{1,0:T(8,128)(2,1)} %get-tuple-element.81), channel_id=1, source_target_pairs={{0,4},{4,0},{1,5},{5,1},{2,6},{6,2},{3,7},{7,3},{8,12},{12,8},{9,1... | collective-permute-start | bytes 1179656 | tf_op jit(solution)/shard_map/ppermute | solution.py:20
  78.5 0.7 copy-start.9
  83.3 11.1 %collective-permute-start.20 = (bf16[384,512]{1,0:T(8,128)(2,1)}, bf16[384,512]{1,0:T(8,128)(2,1)}, u32[]{:S(2)}, u32[]{:S(2)}) collective-permute-start(bf16[384,512]{1,0:T(8,128)(2,1)} %add_convert_fusion.11), channel_id=1, source_target_pairs={{0,8},{8,0},{16,24},{24,16},{1,9},{9,1},{17,25},{25,17},{2,10},{10... | collective-permute-start | bytes 1179656 | tf_op jit(solution)/shard_map/ppermute | solution.py:20
  84.9 18.7 %collective-permute-start.21 = (bf16[384,512]{1,0:T(8,128)(2,1)}, bf16[384,512]{1,0:T(8,128)(2,1)S(1)}, u32[]{:S(2)}, u32[]{:S(2)}) collective-permute-start(bf16[384,512]{1,0:T(8,128)(2,1)} %copy-done.24), channel_id=1, source_target_pairs={{0,4},{4,0},{1,5},{5,1},{2,6},{6,2},{3,7},{7,3},{8,12},{12,8},{9,1... | collective-permute-start | bytes 1179656 | tf_op jit(solution)/shard_map/ppermute | solution.py:20
  86.4 2.8 %copy-start.2 = (bf16[512,3,2048]{2,0,1:T(8,128)(2,1)S(1)}, bf16[512,3,2048]{2,0,1:T(8,128)(2,1)}, u32[]{:S(2)}) copy-start(bf16[512,3,2048]{2,0,1:T(8,128)(2,1)} %param.5) | copy-start | bytes 18874372
  89.2 7.1 %copy-start.23 = (bf16[384,512]{1,0:T(8,128)(2,1)S(1)}, bf16[384,512]{1,0:T(8,128)(2,1)}, u32[]{:S(2)}) copy-start(bf16[384,512]{1,0:T(8,128)(2,1)} %copy-done.22) | copy-start | bytes 1179652
  92.6 4.8 %copy-start.6 = (bf16[384,2048]{1,0:T(8,128)(2,1)S(1)}, bf16[384,2048]{1,0:T(8,128)(2,1)}, u32[]{:S(2)}) copy-start(bf16[384,2048]{1,0:T(8,128)(2,1)} %copy-done.5) | copy-start | bytes 4718596
  92.6 4.7 %copy-start.8 = (bf16[3,384,128]{2,1,0:T(8,128)(2,1)S(1)}, bf16[3,384,128]{2,1,0:T(8,128)(2,1)}, u32[]{:S(2)}) copy-start(bf16[3,384,128]{2,1,0:T(8,128)(2,1)} %copy-done.7) | copy-start | bytes 884740
  92.6 4.7 %copy-start.10 = (bf16[3,384,128]{2,1,0:T(8,128)(2,1)S(1)}, bf16[3,384,128]{2,1,0:T(8,128)(2,1)}, u32[]{:S(2)}) copy-start(bf16[3,384,128]{2,1,0:T(8,128)(2,1)} %copy-done.9) | copy-start | bytes 884740
  93.9 9.8 %collective-permute-start.22 = (bf16[384,512]{1,0:T(8,128)(2,1)S(1)}, bf16[384,512]{1,0:T(8,128)(2,1)S(1)}, u32[]{:S(2)}, u32[]{:S(2)}) collective-permute-start(bf16[384,512]{1,0:T(8,128)(2,1)S(1)} %add_convert_fusion.10), channel_id=1, source_target_pairs={{0,8},{8,0},{16,24},{24,16},{1,9},{9,1},{17,25},{25,17},{2,10},{10... | collective-permute-start | bytes 1179656 | tf_op jit(solution)/shard_map/ppermute | solution.py:20
  95.6 8.2 %collective-permute-start.23 = (bf16[384,512]{1,0:T(8,128)(2,1)S(1)}, bf16[384,512]{1,0:T(8,128)(2,1)S(1)}, u32[]{:S(2)}, u32[]{:S(2)}) collective-permute-start(bf16[384,512]{1,0:T(8,128)(2,1)S(1)} %add_convert_fusion.9), channel_id=1, source_target_pairs={{0,0},{8,16},{16,8},{24,24},{1,1},{9,17},{17,9},{25,25},{2,2},{10,... | collective-permute-start | bytes 1179656 | tf_op jit(solution)/shard_map/ppermute | solution.py:579
  96.3 19.0 %collective-permute-start.24 = (bf16[384,512]{1,0:T(8,128)(2,1)S(1)}, bf16[384,512]{1,0:T(8,128)(2,1)S(1)}, u32[]{:S(2)}, u32[]{:S(2)}) collective-permute-start(bf16[384,512]{1,0:T(8,128)(2,1)S(1)} %copy-done.23), channel_id=1, source_target_pairs={{0,4},{4,0},{1,5},{5,1},{2,6},{6,2},{3,7},{7,3},{8,12},{12,8},{9,1... | collective-permute-start | bytes 1179656 | tf_op jit(solution)/shard_map/ppermute | solution.py:20
  103.6 5.5 %copy-start.12 = (bf16[3,384,128]{2,1,0:T(8,128)(2,1)S(1)}, bf16[3,384,128]{2,1,0:T(8,128)(2,1)}, u32[]{:S(2)}) copy-start(bf16[3,384,128]{2,1,0:T(8,128)(2,1)} %copy-done.11) | copy-start | bytes 884740
  103.6 5.5 %copy-start.14 = (bf16[3,384,128]{2,1,0:T(8,128)(2,1)S(1)}, bf16[3,384,128]{2,1,0:T(8,128)(2,1)}, u32[]{:S(2)}) copy-start(bf16[3,384,128]{2,1,0:T(8,128)(2,1)} %copy-done.13) | copy-start | bytes 884740
  103.6 5.5 %copy-start.16 = (bf16[3,384,128]{2,1,0:T(8,128)(2,1)S(1)}, bf16[3,384,128]{2,1,0:T(8,128)(2,1)}, u32[]{:S(2)}) copy-start(bf16[3,384,128]{2,1,0:T(8,128)(2,1)} %copy-done.15) | copy-start | bytes 884740
  103.7 5.5 %copy-start.18 = (bf16[3,384,128]{2,1,0:T(8,128)(2,1)S(1)}, bf16[3,384,128]{2,1,0:T(8,128)(2,1)}, u32[]{:S(2)}) copy-start(bf16[3,384,128]{2,1,0:T(8,128)(2,1)} %copy-done.17) | copy-start | bytes 884740
  104.0 11.5 %collective-permute-start.25 = (bf16[384,512]{1,0:T(8,128)(2,1)S(1)}, bf16[384,512]{1,0:T(8,128)(2,1)S(1)}, u32[]{:S(2)}, u32[]{:S(2)}) collective-permute-start(bf16[384,512]{1,0:T(8,128)(2,1)S(1)} %get-tuple-element.114), channel_id=1, source_target_pairs={{0,8},{8,0},{16,24},{24,16},{1,9},{9,1},{17,25},{25,17},{2,10},{10... | collective-permute-start | bytes 1179656 | tf_op jit(solution)/shard_map/ppermute | solution.py:20
  108.4 7.1 %collective-permute-start.26 = (bf16[384,512]{1,0:T(8,128)(2,1)S(1)}, bf16[384,512]{1,0:T(8,128)(2,1)S(1)}, u32[]{:S(2)}, u32[]{:S(2)}) collective-permute-start(bf16[384,512]{1,0:T(8,128)(2,1)S(1)} %add_convert_fusion.7), channel_id=1, source_target_pairs={{0,0},{8,16},{16,8},{24,24},{1,1},{9,17},{17,9},{25,25},{2,2},{10,... | collective-permute-start | bytes 1179656 | tf_op jit(solution)/shard_map/ppermute | solution.py:579
  115.4 3.7 %copy-start.20 = (bf16[416,128]{1,0:T(8,128)(2,1)S(1)}, bf16[416,128]{1,0:T(8,128)(2,1)}, u32[]{:S(2)}) copy-start(bf16[416,128]{1,0:T(8,128)(2,1)} %copy-done.19) | copy-start | bytes 319492
  115.7 8.5 %collective-permute-start.27 = (bf16[384,512]{1,0:T(8,128)(2,1)S(1)}, bf16[384,512]{1,0:T(8,128)(2,1)S(1)}, u32[]{:S(2)}, u32[]{:S(2)}) collective-permute-start(bf16[384,512]{1,0:T(8,128)(2,1)S(1)} %get-tuple-element.112), channel_id=1, source_target_pairs={{0,8},{8,0},{16,24},{24,16},{1,9},{9,1},{17,25},{25,17},{2,10},{10... | collective-permute-start | bytes 1179656 | tf_op jit(solution)/shard_map/ppermute | solution.py:20
  118.5 6.6 %collective-permute-start.28 = (bf16[384,512]{1,0:T(8,128)(2,1)S(1)}, bf16[384,512]{1,0:T(8,128)(2,1)S(1)}, u32[]{:S(2)}, u32[]{:S(2)}) collective-permute-start(bf16[384,512]{1,0:T(8,128)(2,1)S(1)} %add_convert_fusion.4), channel_id=1, source_target_pairs={{0,0},{8,16},{16,8},{24,24},{1,1},{9,17},{17,9},{25,25},{2,2},{10,... | collective-permute-start | bytes 1179656 | tf_op jit(solution)/shard_map/ppermute | solution.py:579
  119.8 9.4 %collective-permute-start.29 = (bf16[2,128,128]{2,1,0:T(8,128)(2,1)S(1)}, bf16[2,128,128]{2,1,0:T(8,128)(2,1)S(1)}, u32[]{:S(2)}, u32[]{:S(2)}) collective-permute-start(bf16[2,128,128]{2,1,0:T(8,128)(2,1)S(1)} %get-tuple-element.104), channel_id=1, source_target_pairs={{0,1},{1,0},{2,3},{3,2},{4,5},{5,4},{6,7},{7,6},{8,9},{9,8},{10,11... | collective-permute-start | bytes 196616 | tf_op jit(solution)/shard_map/ppermute | solution.py:20
  119.8 9.3 %collective-permute-start.30 = (bf16[2,128,128]{2,1,0:T(8,128)(2,1)S(1)}, bf16[2,128,128]{2,1,0:T(8,128)(2,1)S(1)}, u32[]{:S(2)}, u32[]{:S(2)}) collective-permute-start(bf16[2,128,128]{2,1,0:T(8,128)(2,1)S(1)} %get-tuple-element.105), channel_id=1, source_target_pairs={{0,2},{1,3},{2,0},{3,1},{4,6},{5,7},{6,4},{7,5},{8,10},{9,11},{10,... | collective-permute-start | bytes 196616 | tf_op jit(solution)/shard_map/ppermute | solution.py:20
  120.5 8.6 %collective-permute-start.31 = (bf16[2,128,128]{2,1,0:T(8,128)(2,1)S(1)}, bf16[2,128,128]{2,1,0:T(8,128)(2,1)S(1)}, u32[]{:S(2)}, u32[]{:S(2)}) collective-permute-start(bf16[2,128,128]{2,1,0:T(8,128)(2,1)S(1)} %get-tuple-element.106), channel_id=1, source_target_pairs={{0,3},{1,2},{2,1},{3,0},{4,7},{5,6},{6,5},{7,4},{8,11},{9,10},{10,... | collective-permute-start | bytes 196616 | tf_op jit(solution)/shard_map/ppermute | solution.py:20
  124.3 4.8 %collective-permute-start.32 = (bf16[384,512]{1,0:T(8,128)(2,1)S(1)}, bf16[384,512]{1,0:T(8,128)(2,1)S(1)}, u32[]{:S(2)}, u32[]{:S(2)}) collective-permute-start(bf16[384,512]{1,0:T(8,128)(2,1)S(1)} %add_convert_fusion.2), channel_id=1, source_target_pairs={{0,0},{8,16},{16,8},{24,24},{1,1},{9,17},{17,9},{25,25},{2,2},{10,... | collective-permute-start | bytes 1179656 | tf_op jit(solution)/shard_map/ppermute | solution.py:579
  125.2 13.3 %collective-permute-start.33 = (bf16[384,512]{1,0:T(8,128)(2,1)S(1)}, bf16[384,512]{1,0:T(8,128)(2,1)S(1)}, u32[]{:S(2)}, u32[]{:S(2)}) collective-permute-start(bf16[384,512]{1,0:T(8,128)(2,1)S(1)} %add_convert_fusion.1), channel_id=1, source_target_pairs={{0,8},{8,0},{16,24},{24,16},{1,9},{9,1},{17,25},{25,17},{2,10},{10... | collective-permute-start | bytes 1179656 | tf_op jit(solution)/shard_map/ppermute | solution.py:20
  129.2 15.8 %collective-permute-start.34 = (bf16[384,512]{1,0:T(8,128)(2,1)S(1)}, bf16[384,512]{1,0:T(8,128)(2,1)S(1)}, u32[]{:S(2)}, u32[]{:S(2)}) collective-permute-start(bf16[384,512]{1,0:T(8,128)(2,1)S(1)} %add_convert_fusion), channel_id=1, source_target_pairs={{0,8},{8,0},{16,24},{24,16},{1,9},{9,1},{17,25},{25,17},{2,10},{10... | collective-permute-start | bytes 1179656 | tf_op jit(solution)/shard_map/ppermute | solution.py:20

commit v8 on v7

--- a/solution.py
+++ b/solution.py
@@ -110,13 +110,20 @@
     return terms
 
 
-def split_lanes_kernel(place, *refs, n_col):
-    in_refs, out_refs = refs[:n_col], refs[n_col:]
-    width = out_refs[0].shape[2]
+def split_lanes_kernel(place, up_ref, *out_refs):
+    n_depth, width = len(out_refs), out_refs[0].shape[2]
     for r, ref in enumerate(out_refs):
-        lanes = pl.ds(pl.multiple_of((place[0] ^ r) * width, width), width)
-        for k in range(n_col):
-            ref[k] = in_refs[k][:, lanes]
+        for k in range(ref.shape[0]):
+            at = ((place[1] ^ k) * n_depth + (place[0] ^ r)) * width
+            ref[k] = up_ref[:, pl.ds(pl.multiple_of(at, width), width)]
+
+
+def merge_rows_kernel(place, *refs, n_depth):
+    in_refs, out_refs = refs[:n_depth], refs[n_depth:]
+    local = in_refs[0].shape[1]
+    for r, ref in enumerate(in_refs):
+        for k, out_ref in enumerate(out_refs):
+            out_ref[pl.ds(pl.multiple_of((place[0] ^ r) * local, 16), local), :] = ref[k]
 
 
 def split_rows_kernel(place, *refs, n_col):
@@ -129,29 +136,42 @@
             ref[k, local:] = in_refs[k][-32:, :]
 
 
-def split(kernel, place, arrays, n_depth, shape):
-    whole = (len(arrays),) + shape
+def rearrange(kernel, place, arrays, count, shape, name):
+    width = shape[-1]
     return pl.pallas_call(
-        functools.partial(kernel, n_col=len(arrays)),
+        kernel,
         grid_spec=pltpu.PrefetchScalarGridSpec(
             num_scalar_prefetch=1,
             grid=(1,),
-            in_specs=[resident(value.shape, shape[1]) for value in arrays],
-            out_specs=[resident(whole, shape[1])] * n_depth,
+            in_specs=[resident(value.shape, width) for value in arrays],
+            out_specs=[resident(shape, width)] * count,
         ),
-        out_shape=[jax.ShapeDtypeStruct(whole, jnp.bfloat16)] * n_depth,
-        compiler_params=params(4, shape[1]),
+        out_shape=[jax.ShapeDtypeStruct(shape, jnp.bfloat16)] * count,
+        compiler_params=params(4, width),
         cost_estimate=SMALL,
-        name="split",
+        name=name,
     )(place, *arrays)
 
 
-def split_lanes(place, arrays, n_depth):
-    local, width = arrays[0].shape[0], arrays[0].shape[1] // n_depth
+def split_lanes(place, up, n_col, n_depth):
+    local, width = up.shape[0], up.shape[1] // (n_col * n_depth)
     if width % LANES:
-        whole = jnp.stack(arrays)
-        return [lax.dynamic_slice_in_dim(whole, (place[0] ^ r) * width, width, axis=2) for r in range(n_depth)]
-    return split(split_lanes_kernel, place, arrays, n_depth, (local, width))
+        blocks = up.reshape(local, n_col, n_depth, width)[:, place[1] ^ jnp.arange(n_col)]
+        return [
+            jnp.transpose(lax.dynamic_index_in_dim(blocks, place[0] ^ r, 2, keepdims=False), (1, 0, 2))
+            for r in range(n_depth)
+        ]
+    return rearrange(split_lanes_kernel, place, [up], n_depth, (n_col, local, width), "split")
+
+
+def merge_rows(place, pieces):
+    n_depth = len(pieces)
+    n_col, local, width = pieces[0].shape
+    if width % LANES:
+        whole = jnp.stack(pieces)[place[0] ^ jnp.arange(n_depth)]
+        return list(jnp.transpose(whole, (1, 0, 2, 3)).reshape(n_col, n_depth * local, width))
+    kernel = functools.partial(merge_rows_kernel, n_depth=n_depth)
+    return list(rearrange(kernel, place, pieces, n_col, (n_depth * local, width), "merge"))
 
 
 def split_rows(place, arrays, n_depth):
@@ -164,7 +184,8 @@
             )
             for r in range(n_depth)
         ]
-    return split(split_rows_kernel, place, arrays, n_depth, (local + 32, width))
+    kernel = functools.partial(split_rows_kernel, n_col=len(arrays))
+    return rearrange(kernel, place, arrays, n_depth, (len(arrays), local + 32, width), "split")
 
 
 def join_kernel(place, _, *refs):
@@ -215,8 +236,8 @@
     )(place, mark, *blocks)
 
 
-def middle_kernel(place, taps_ref, *refs, devices, groups, terms, tile):
-    up_refs, refs = refs[:devices], refs[devices:]
+def middle_kernel(place, taps_ref, *refs, groups, terms, tile):
+    up_refs, refs = refs[:groups], refs[groups:]
     part_refs = refs[: groups * terms]
     grad_refs = refs[groups * terms : groups * terms + groups]
     out_refs = refs[groups * terms + groups : groups * terms + 2 * groups]
@@ -226,10 +247,8 @@
     width = part_refs[0].shape[3]
     total = groups * tok
     tap_groups = taps_ref.shape[1]
-    for r, ref in enumerate(up_refs):
-        for k in range(groups):
-            at = (col ^ k) * tok + (place[0] ^ r) * tile
-            up_s[pl.ds(pl.multiple_of(at, tile), tile), :] = ref[k]
+    for k, ref in enumerate(up_refs):
+        up_s[pl.ds(pl.multiple_of((col ^ k) * tok, tok), tok), :] = ref[...]
     lane_group = lax.broadcasted_iota(jnp.int32, (tap_groups, width), 1) // GROUP
     group = lax.broadcasted_iota(jnp.int32, (tap_groups, width), 0)
     spread = (lane_group + place[3] * (width // GROUP) == group).astype(jnp.bfloat16)
@@ -283,19 +302,18 @@
         ref[tok : tok + 32, :] = packed
 
 
-def middle(place, taps, ups, parts):
-    groups, terms, devices = len(parts), len(parts[0]), len(ups)
-    tile = ups[0].shape[1]
+def middle(place, taps, ups, parts, tile):
+    groups, terms = len(parts), len(parts[0])
     _, _, tok, width = parts[0][0].shape
     total = groups * tok
     whole = lambda *shape: resident(shape, width)
     one = whole(1, 3, tok, width)
     outs = pl.pallas_call(
-        functools.partial(middle_kernel, devices=devices, groups=groups, terms=terms, tile=tile),
+        functools.partial(middle_kernel, groups=groups, terms=terms, tile=tile),
         grid_spec=pltpu.PrefetchScalarGridSpec(
             num_scalar_prefetch=1,
             grid=(1,),
-            in_specs=[whole(*taps.shape)] + [whole(*ups[0].shape)] * devices + [one] * (groups * terms),
+            in_specs=[whole(*taps.shape)] + [whole(tok, width)] * groups + [one] * (groups * terms),
             out_specs=[whole(3, tok, width)] * groups + [whole(tok + 32, width)] * groups,
             scratch_shapes=[
                 pltpu.VMEM((total, width), jnp.bfloat16),
@@ -326,6 +344,9 @@
 def assemble(place, grads):
     streams, tok, width = grads[0].shape
     out = jax.ShapeDtypeStruct((tok, streams * width * len(grads)), jnp.bfloat16)
+    if width % LANES:
+        whole = jnp.stack(grads)[place[0] ^ jnp.arange(len(grads))]
+        return jnp.transpose(whole, (2, 1, 0, 3)).reshape(out.shape)
     return pl.pallas_call(
         assemble_kernel,
         grid_spec=pltpu.PrefetchScalarGridSpec(
@@ -341,18 +362,10 @@
     )(place, *grads)
 
 
-def input_grad_kernel(place, *refs, terms, width, first):
-    grad_refs, w_ref, out_refs = refs[:terms], refs[terms], refs[terms + 1 :]
+def input_grad_kernel(grad_ref, w_ref, *out_refs, first):
     step = out_refs[0].shape[1]
-    if terms == 1:
-        own = slice(first * step, (first + 1) * step) if len(out_refs) == 1 else slice(None)
-        acc = jnp.dot(grad_refs[0][...], w_ref[:, :, own].reshape(-1, step), preferred_element_type=jnp.float32)
-    else:
-        acc = jnp.zeros(out_refs[0].shape, jnp.float32)
-        for r, ref in enumerate(grad_refs):
-            rows = pl.ds(pl.multiple_of((place[0] ^ r) * width, width), width)
-            for s in range(3):
-                acc = acc + jnp.dot(ref[s], w_ref[s, rows, :], preferred_element_type=jnp.float32)
+    own = slice(first * step, (first + 1) * step) if len(out_refs) == 1 else slice(None)
+    acc = jnp.dot(grad_ref[...], w_ref[:, :, own].reshape(-1, step), preferred_element_type=jnp.float32)
     acc = acc.astype(jnp.bfloat16)
     for i, out_ref in enumerate(out_refs):
 
@@ -361,104 +374,93 @@
             out_ref[...] = acc
 
 
-def input_grad(place, grads, w, first, last, chunks):
-    tok = grads[0].shape[-2]
+def input_grad(grad, w, first, last, chunks, width):
+    tok = grad.shape[0]
     streams, channels, feat = w.shape
     step = feat // chunks
-    width = channels if len(grads) == 1 else grads[0].shape[-1]
+    count = last - first
+    if width % LANES:
+        rows = w[:, :, first * step : last * step].reshape(streams * channels, count * step)
+        whole = jnp.dot(grad, rows, preferred_element_type=jnp.float32).astype(jnp.bfloat16)
+        return [whole[:, i * step : (i + 1) * step] for i in range(count)]
+    return list(
+        pl.pallas_call(
+            functools.partial(input_grad_kernel, first=first),
+            grid=(count,),
+            in_specs=[
+                resident(grad.shape, width),
+                resident(w.shape, width)
+                if count == 1
+                else pl.BlockSpec((streams, channels, step), lambda i: (0, 0, first + i)),
+            ],
+            out_specs=[resident((tok, step), width)] * count,
+            out_shape=[jax.ShapeDtypeStruct((tok, step), jnp.bfloat16)] * count,
+            compiler_params=params(12, width),
+            cost_estimate=SMALL,
+            name="input_grad",
+        )(grad, w)
+    )
+
+
+def weight_grad_kernel(*refs, chained, groups, half):
+    refs = refs[2 * chained :]
+    grad_refs, x_refs = refs[:groups], refs[groups : 2 * groups]
+    out_ref, mark_ref, turned = refs[2 * groups :]
+    mark_ref[...] = jnp.zeros(mark_ref.shape, jnp.float32)
+    streams, channels, step = out_ref.shape
+    tok = x_refs[0].shape[0]
+
+    @pl.when(pl.program_id(0) == 0)
+    def _():
+        for k in range(groups):
+            for s in range(streams):
+                at = (2 * s + half) * channels
+                block = grad_refs[k][:, at : at + channels]
+                turned[s * channels : (s + 1) * channels, k * tok : (k + 1) * tok] = block.T
+
+    columns = pl.ds(pl.multiple_of(pl.program_id(0) * step, step), step)
+    acc = None
+    for k in range(groups):
+        term = jnp.dot(turned[:, k * tok : (k + 1) * tok], x_refs[k][:, columns], preferred_element_type=jnp.float32)
+        acc = term if acc is None else acc + term
+    for s in range(streams):
+        out_ref[s] = acc[s * channels : (s + 1) * channels, :]
+
+
+def weight_grad(filled, grads, xs, half, streams, width):
+    groups = len(xs)
+    tok, feat = xs[0].shape
+    channels = grads[0].shape[1] // streams
+    chained = filled is not None
+    if width % LANES:
+        if chained:
+            return filled
+        terms = [
+            lax.dot_general(grad, x, (((0,), (0,)), ((), ())), preferred_element_type=jnp.float32)
+            for grad, x in zip(grads, xs)
+        ]
+        return sum(terms).reshape(streams, channels, feat), jnp.zeros((8, LANES), jnp.float32)
+    step = min(512, feat)
     return pl.pallas_call(
-        functools.partial(input_grad_kernel, terms=len(grads), width=width, first=first),
-        grid_spec=pltpu.PrefetchScalarGridSpec(
-            num_scalar_prefetch=1,
-            grid=(last - first,),
-            in_specs=[resident(g.shape, width) for g in grads]
-            + [
-                resident(w.shape, width)
-                if len(grads) == 1 and last - first == 1
-                else pl.BlockSpec((streams, channels, step), lambda i, _: (0, 0, first + i))
-            ],
-            out_specs=[resident((tok, step), width)] * (last - first),
-        ),
-        out_shape=[jax.ShapeDtypeStruct((tok, step), jnp.bfloat16)] * (last - first),
-        compiler_params=params(12, width),
-        cost_estimate=SMALL,
-        name="input_grad",
-    )(place, *grads, w)
-
-
-def weight_grad_kernel(place, *refs, chained, groups, wide, r):
-    refs = refs[2 * chained :]
-    grad_refs = refs[: 2 * groups]
-    x_refs = refs[2 * groups : 3 * groups]
-    out_ref, mark_ref = refs[3 * groups : 3 * groups + 2]
-    mark_ref[...] = jnp.zeros(mark_ref.shape, jnp.float32)
-    tok, step = x_refs[0].shape[0], out_ref.shape[2]
-    width = grad_refs[0].shape[2]
-    if wide:
-        turned = refs[3 * groups + 2]
-
-        @pl.when(pl.program_id(0) == 0)
-        def _():
-            for side in range(2):
-                for s in range(3):
-                    at = pl.multiple_of(((place[0] ^ r ^ side) % 2 + 2 * s) * width, width)
-                    for k in range(groups):
-                        turned[pl.ds(at, width), k * tok : (k + 1) * tok] = grad_refs[side * groups + k][s].T
-
-        acc = None
-        columns = pl.ds(pl.multiple_of(pl.program_id(0) * step, step), step)
-        for k in range(groups):
-            term = jnp.dot(
-                turned[:, k * tok : (k + 1) * tok], x_refs[k][:, columns], preferred_element_type=jnp.float32
-            )
-            acc = term if acc is None else acc + term
-        for s in range(3):
-            out_ref[s] = acc[2 * s * width : 2 * (s + 1) * width, :]
-    else:
-        tn = (((0,), (0,)), ((), ()))
-        for side in range(2):
-            at = pl.multiple_of((place[0] ^ r ^ side) % 2 * width, width)
-            for s in range(3):
-                acc = None
-                for k in range(groups):
-                    term = lax.dot_general(
-                        grad_refs[side * groups + k][s], x_refs[k][...], tn, preferred_element_type=jnp.float32
-                    )
-                    acc = term if acc is None else acc + term
-                out_ref[s, pl.ds(at, width), :] = acc
-
-
-def weight_grad(place, filled, grads, xs, r, count):
-    groups = len(xs)
-    streams, tok, width = grads[0].shape
-    feat = xs[0].shape[1]
-    channels = width * count
-    step = min(512, feat)
-    wide = width % LANES == 0
-    chained = filled is not None
-    return pl.pallas_call(
-        functools.partial(weight_grad_kernel, chained=chained, groups=groups, wide=wide, r=r),
-        grid_spec=pltpu.PrefetchScalarGridSpec(
-            num_scalar_prefetch=1,
-            grid=(feat // step,),
-            in_specs=[pl.BlockSpec(memory_space=pl.ANY)] * (2 * chained)
-            + [resident((streams, tok, width), width)] * (2 * groups)
-            + [resident((tok, feat), width) if wide else pl.BlockSpec((tok, step), lambda i, _: (0, i))] * groups,
-            out_specs=[
-                pl.BlockSpec((streams, 2 * width, step), lambda i, at: (0, (at[0] ^ r) // 2, i)),
-                resident((8, LANES), width),
-            ],
-            scratch_shapes=[pltpu.VMEM((2 * streams * width, groups * tok), jnp.bfloat16)] if wide else [],
-        ),
+        functools.partial(weight_grad_kernel, chained=chained, groups=groups, half=half),
+        grid=(feat // step,),
+        in_specs=[pl.BlockSpec(memory_space=pl.ANY)] * (2 * chained)
+        + [resident(grads[0].shape, width)] * groups
+        + [resident((tok, feat), width)] * groups,
+        out_specs=[
+            pl.BlockSpec((streams, channels // 2, step), lambda i: (0, half, i)),
+            resident((8, LANES), width),
+        ],
+        scratch_shapes=[pltpu.VMEM((streams * channels // 2, groups * tok), jnp.bfloat16)],
         out_shape=[
             jax.ShapeDtypeStruct((streams, channels, feat), jnp.float32),
             jax.ShapeDtypeStruct((8, LANES), jnp.float32),
         ],
-        input_output_aliases={1: 0} if chained else {},
+        input_output_aliases={0: 0} if chained else {},
         compiler_params=params(14, width),
         cost_estimate=SMALL,
         name="weight_grad",
-    )(place, *(filled if chained else []), *grads, *xs)
+    )(*(filled if chained else []), *grads, *xs)
 
 
 def added(first, second):
@@ -500,20 +502,19 @@
         return x, [keep, near] + fars, pairs, fars
 
     first = [first_pieces(tokens, k) for k in range(1, n_col)]
-    span = width * n_depth
-    col_ups = [lax.dynamic_slice_in_dim(upstream, (col_at ^ k) * span, span, axis=1) for k in range(n_col)]
-    col_ups = [up if k == 0 else swap(up, "col", k) for k, up in enumerate(col_ups)]
-    x, terms, pairs, fars = project_and_sum([tokens], *[piece for of in first for piece in of], *col_ups[1:])
+    ups = split_lanes(place, upstream, n_col, n_depth)
+    ups = [up if r == 0 else swap(up, "depth", r) for r, up in enumerate(ups)]
+    x, terms, pairs, fars = project_and_sum([tokens], *[piece for of in first for piece in of], *ups[1:])
     xs, parts = [x], [terms]
-    ups = split_lanes(place, [after(col_ups[0], *pairs)] + col_ups[1:], n_depth)
-    ups = [up if r == 0 else swap(up, "depth", r) for r, up in enumerate(ups)]
     for k in range(1, n_col):
         x_pieces = other_pieces(tokens, first[k - 1], k)
-        x_pieces[-1] = after(x_pieces[-1], *fars, *ups[1:])
+        x_pieces[-1] = after(x_pieces[-1], *fars)
         x, terms, pairs, fars = project_and_sum(x_pieces)
         xs.append(x)
         parts.append(terms)
-    own_grads, blocks = middle(place, taps, ups, parts)
+    ups = merge_rows(place, [after(ups[0], *pairs)] + ups[1:])
+    ups = [up if k == 0 else swap(up, "col", k) for k, up in enumerate(ups)]
+    own_grads, blocks = middle(place, taps, ups, parts, local_tok)
     nears = [swap(own, "depth", 1) for own in own_grads]
     blocks = [block if k == 0 else swap(block, "col", k) for k, block in enumerate(blocks)]
     beside = nears + blocks[1:]
@@ -521,6 +522,7 @@
     grads = [None] * n_col
     ready = []
     sent = []
+    lhs = [None] * n_col
     for k in reversed(range(n_col)):
         fars = [swap(after(own_grads[k], *ready) if ready else own_grads[k], "depth", r) for r in range(2, n_depth, 2)]
         ready = fars
@@ -532,69 +534,69 @@
         for far in fars:
             grads[k] += [far, swap(far, "depth", 1)]
         ready = grads[k][2:]
-        lhs = [assemble(place, grads[k])] if width % LANES == 0 else grads[k]
+        lhs[k] = assemble(place, grads[k])
         if k > 0:
-            head = input_grad(place, lhs, w, 0, 1, chunks)
-            behind = [after(lhs[0], *head)] + lhs[1:]
-            tail = input_grad(place, behind, w, 1, chunks, chunks)
-            parts_of = list(head) + list(tail)
+            parts_of = input_grad(lhs[k], w, 0, 1, chunks, width)
+            parts_of += input_grad(after(lhs[k], *parts_of), w, 1, chunks, chunks, width)
             sent.append(([swap(part, "col", k) for part in parts_of[:3]], parts_of))
     held = [parts_of[3:] for _, parts_of in sent]
     sent = [of for of, _ in sent]
-    own_part = list(input_grad(place, lhs, w, 0, 1, chunks))
+    own_part = input_grad(lhs[0], w, 0, 1, chunks, width)
     outer = (row_at == 0) | (row_at == 3)
+    line = lax.axis_size("row") == 4
+    hopping = chunks - 1
     inward, across, summed, done = ([None] * chunks for _ in range(4))
     pair = cross = filled = None
     marks = []
-    line = lax.axis_size("row") == 4
-    for slot in range(chunks + 3):
-        if slot < chunks:
-            total = after(own_part[slot], *marks).astype(jnp.float32)
-            for of in sent:
-                total = total + of[slot].astype(jnp.float32)
-            inward[slot] = total.astype(jnp.bfloat16)
+
+    def with_sent(c):
+        total = after(own_part[c], *marks).astype(jnp.float32)
+        for of in sent:
+            total = total + of[c].astype(jnp.float32)
+        return total.astype(jnp.bfloat16)
+
+    for slot in range(hopping + 3):
+        if slot < hopping:
+            inward[slot] = with_sent(slot)
             marks = [inward[slot]]
         if not line:
-            if slot < chunks:
+            if slot < hopping:
                 done[slot] = lax.psum(inward[slot], "row")
-                if slot + 3 < chunks:
-                    for k, parts_of in enumerate(held):
-                        sent[k].append(swap(parts_of[slot], "col", k + 1))
         else:
-            if 0 <= slot - 1 < chunks:
+            if 0 <= slot - 1 < hopping:
                 across[slot - 1] = added(after(inward[slot - 1], *marks), pair)
                 marks = [across[slot - 1]]
-                if slot + 2 < chunks:
-                    for k, parts_of in enumerate(held):
-                        sent[k].append(swap(after(parts_of[slot - 1], *marks), "col", k + 1))
-            if 0 <= slot - 2 < chunks:
+            if 0 <= slot - 2 < hopping:
                 summed[slot - 2] = added(after(across[slot - 2], *marks), cross)
                 marks = [summed[slot - 2]]
-            if 0 <= slot - 3 < chunks:
+            if 0 <= slot - 3 < hopping:
                 done[slot - 3] = jnp.where(outer, pair, summed[slot - 3])
-            if slot < chunks + 2:
+            if slot < hopping + 2:
                 out = summed[slot - 2] if slot >= 2 else inward[slot]
-                pair = swap(jnp.where(outer, inward[slot], out) if slot < chunks else out, "row", 1)
-            if 0 <= slot - 1 < chunks:
+                pair = swap(jnp.where(outer, inward[slot], out) if slot < hopping else out, "row", 1)
+            if 0 <= slot - 1 < hopping:
                 cross = lax.ppermute(across[slot - 1], "row", [(0, 0), (1, 2), (2, 1), (3, 3)])
         if slot == 0:
-            behind = [after(lhs[0], *marks)] + lhs[1:]
-            own_part += input_grad(place, behind, w, 1, chunks, chunks)
+            own_part += input_grad(after(lhs[0], *marks), w, 1, chunks, chunks, width)
             marks = [own_part[1]]
-        if 0 < slot <= n_depth // 2:
-            r = n_depth - 2 * slot
-            of = [group[i] for i in (r, r + 1) for group in grads]
-            filled = weight_grad(place, filled, [after(of[0], *marks)] + of[1:], xs, r, n_depth)
-            marks = [filled[1]]
-        if slot == chunks - 1:
+        if slot == 1:
+            for k, parts_of in enumerate(held):
+                sent[k] += [swap(after(part, *marks), "col", k + 1) for part in parts_of]
             blocks = split_rows(place, [after(blocks[0], *marks)] + blocks[1:], n_depth)
             blocks = [block if r == 0 else swap(block, "depth", r) for r, block in enumerate(blocks)]
-            late = blocks[1:]
-        if slot == chunks:
-            marks += late
+            marks += blocks[1:]
+        if slot == 2:
+            last = with_sent(hopping)
+            done[hopping] = lax.psum(last, "row")
+            marks = [last]
+        if slot >= hopping and slot < hopping + 2:
+            filled = weight_grad(filled, [after(lhs[0], *marks)] + lhs[1:], xs, slot - hopping, 3, width)
+            marks = [filled[1]]
+    output, grad_taps = join(
+        place, filled[1], [after(blocks[0], *marks, done[hopping])] + blocks[1:], taps.shape[1]
+    )
     grad_tokens = jnp.concatenate(done, axis=1)
     grad_weight = jnp.transpose(filled[0], (1, 0, 2))
-    output, grad_taps = join(place, filled[1], [after(blocks[0], *marks)] + blocks[1:], taps.shape[1])
     return (output, grad_tokens, grad_weight, grad_taps)
 
 

time: 147 us -> 178 us (1.21)
  waiting for transfers between devices: 43.5 us -> 56.7 us
  between operations: 1.17 us -> 14.3 us
  other arithmetic: 6.08 us -> 16.6 us
  starting transfers between devices: 47.9 us -> 44.4 us
  Pallas kernels: 35.8 us -> 33.7 us
    psum x0 -> x1, waiting for transfers between devices: none -> 14.7 us  [on_device(): done[hopping] = lax.psum(last, 'row')]
    ppermute x31 -> x30, starting transfers between devices: 45.2 us -> 36.7 us  [swap(): return lax.ppermute(value, axis, [(i, i ^ flip) for i in range(count)])]
    convert_element_type x8 -> x7, other arithmetic: 1.86 us -> 8.18 us  [added(): (first.astype(jnp.float32) + second.astype(jnp.float32)).astype(jnp.bfloa...]
    ppermute x4 -> x3, starting transfers between devices: 2.72 us -> 7.65 us  [on_device(): lax.ppermute(across[slot - 1], 'row', [(0, 0), (1, 2), (2, 1), (3, 3)])]
    select_n x4 -> x3, other arithmetic: 0.17 us -> 3.15 us  [on_device(): done[slot - 3] = jnp.where(outer, pair, summed[slot - 3])]
    ppermute x31 -> x30, waiting for transfers between devices: 43.5 us -> 42 us  [swap(): return lax.ppermute(value, axis, [(i, i ^ flip) for i in range(count)])]
    unnamed x50 -> x24, local copies, waits for them, and re-layouts: 9.81 us -> 8.73 us
    pallas_call x7 -> x8, Pallas kernels: 12.9 us -> 11.9 us  [the longest x4 8.03 us: input_grad(): pl.pallas_call(functools.partial(input_grad_kernel, first=first), grid=(c...]
  transfers between devices with their start and end apart: 35 -> 34, of which waited for: 12 -> 17; matrix products, arithmetic and copies ran while one was open for 4% -> 9% of each run, Pallas kernels for 21% -> 16%
where the time goes in v8:
time: 178 us; the launch traced here: 177 us
  waiting for transfers between devices  56.7 us (32%)
  starting transfers between devices  44.4 us (25%)
  Pallas kernels  33.7 us (19%)
  other arithmetic  16.6 us (9%)
  between operations  14.3 us (8%)
  local copies, waits for them, and re-layouts  10.9 us (6%)
    ppermute x30, waiting for transfers between devices, swap(): return lax.ppermute(value, axis, [(i, i ^ flip) for i in range(count)])  42 us
    ppermute x30, starting transfers between devices, swap(): return lax.ppermute(value, axis, [(i, i ^ flip) for i in range(count)])  36.7 us
    psum x1, waiting for transfers between devices, on_device(): done[hopping] = lax.psum(last, 'row')  14.7 us
    pallas_call x2, Pallas kernels, weight_grad(): pl.pallas_call(functools.partial(weight_grad_kernel, chained=chained, gro...  11.2 us
    unnamed x24, local copies, waits for them, and re-layouts  8.73 us
    convert_element_type x7, other arithmetic, added(): (first.astype(jnp.float32) + second.astype(jnp.float32)).astype(jnp.bfloa...  8.18 us
    pallas_call x4, Pallas kernels, input_grad(): pl.pallas_call(functools.partial(input_grad_kernel, first=first), grid=(c...  8.03 us
    pallas_call x2, Pallas kernels, project(): pl.pallas_call(functools.partial(project_kernel, pieces=len(xs), count=co...  7.73 us
  transfers between devices with their start and end apart: 34, of which 17 were waited for; matrix products, arithmetic and copies ran while one was open for 9% of the time, Pallas kernels for 16%

profile of v8, /device:TPU:0, one launch (start us, length us, event | category | flops | bytes accessed | tf_op | source)
XLA Modules:
  0.0 176.6 jit_solution(8853317155281967591)
XLA Ops:
  7.2 1.1 constant_dynamic-slice_fusion
  8.3 3.0 %collective-permute-start = (bf16[128,2048]{1,0:T(8,128)(2,1)S(1)}, bf16[128,2048]{1,0:T(8,128)(2,1)S(1)}, u32[]{:S(2)}, u32[]{:S(2)}) collective-permute-start(bf16[128,2048]{1,0:T(8,128)(2,1)S(1)} %constant_dynamic-slice_fusion), channel_id=1, source_target_pairs={{0,4},{4,0},{1,5},{5,1},{2,6},{6,2},{3,7},{7,3},{8,12},{12,8},{9,1... | collective-permute-start | bytes 1572872 | tf_op jit(solution)/shard_map/ppermute | solution.py:20
  11.4 0.9 copy-done.6
  13.0 1.6 collective-permute-start.4
  14.9 2.8 %copy-done = bf16[512,3,2048]{2,0,1:T(8,128)(2,1)S(1)} copy-done((bf16[512,3,2048]{2,0,1:T(8,128)(2,1)S(1)}, bf16[512,3,2048]{2,0,1:T(8,128)(2,1)}, u32[]{:S(2)}) %copy-start) | copy-done | bytes 6291480
  17.7 1.4 copy-done.2
  19.1 3.8 %project.2 = (bf16[2,3,384,128]{3,2,1,0:T(8,128)(2,1)S(1)}, bf16[2,3,384,128]{3,2,1,0:T(8,128)(2,1)S(1)}) custom-call(s32[4]{0:T(128)S(1)} %pad_add_fusion.place, bf16[384,2048]{1,0:T(8,128)(2,1)S(1)} %copy-done.2, bf16[3,512,2048]{2,1,0:T(8,128)(2,1)S(1)} %bitcast.6), custom_call_target="tpu_custom_call" | custom-call | flops 1 | bytes 1 | tf_op jit(solution)/shard_map/project/pallas_call | solution.py:87
  23.4 1.1 slice.15
  24.5 1.7 collective-permute-start.2
  26.2 1.6 collective-permute-start.1
  27.8 1.6 collective-permute-start.7
  29.4 9.4 %collective-permute-done.2.refs_2_ = bf16[128,2048]{1,0:T(8,128)(2,1)S(1)} collective-permute-done((bf16[128,2048]{1,0:T(8,128)(2,1)S(1)}, bf16[128,2048]{1,0:T(8,128)(2,1)S(1)}, u32[]{:S(2)}, u32[]{:S(2)}) %collective-permute-start.2) | collective-permute-done | bytes 524320 | tf_op jit(solution)/shard_map/ppermute | solution.py:20
  38.8 1.4 collective-permute-done.1.refs_1_
  40.2 3.9 %project.3 = (bf16[2,3,384,128]{3,2,1,0:T(8,128)(2,1)S(1)}, bf16[2,3,384,128]{3,2,1,0:T(8,128)(2,1)S(1)}, bf16[384,2048]{1,0:T(8,128)(2,1)S(1)}) custom-call(s32[4]{0:T(128)S(1)} %pad_add_fusion.place, bf16[128,2048]{1,0:T(8,128)(2,1)S(1)} %collective-permute-done.refs_0_, bf16[128,2048]{1,0:T(8,128)(2,1)S(1)} %collective-permute-done.1.refs_1_, ...), custom_call_target="tpu_custom_call" | custom-call | flops 1 | bytes 1 | tf_op jit(solution)/shard_map/project/pallas_call | solution.py:87
  44.2 2.0 %collective-permute-done.8.refs_6_ = bf16[2,3,384,128]{3,2,1,0:T(8,128)(2,1)S(1)} collective-permute-done((bf16[2,3,384,128]{3,2,1,0:T(8,128)(2,1)S(1)}, bf16[2,3,384,128]{3,2,1,0:T(8,128)(2,1)S(1)}, u32[]{:S(2)}, u32[]{:S(2)}) %collective-permute-start.8) | collective-permute-done | bytes 589856 | tf_op jit(solution)/shard_map/ppermute | solution.py:20
  46.3 1.6 collective-permute-start.10
  49.0 4.1 %collective-permute-done.9.refs_1_ = bf16[384,128]{1,0:T(8,128)(2,1)S(1)} collective-permute-done((bf16[384,128]{1,0:T(8,128)(2,1)S(1)}, bf16[384,128]{1,0:T(8,128)(2,1)S(1)}, u32[]{:S(2)}, u32[]{:S(2)}) %collective-permute-start.9) | collective-permute-done | bytes 98336 | tf_op jit(solution)/shard_map/ppermute | solution.py:20
  53.1 2.3 %collective-permute-done.10.refs_7_ = bf16[1,3,384,128]{3,2,1,0:T(8,128)(2,1)S(1)} collective-permute-done((bf16[1,3,384,128]{3,2,1,0:T(8,128)(2,1)S(1)}, bf16[1,3,384,128]{3,2,1,0:T(8,128)(2,1)S(1)}, u32[]{:S(2)}, u32[]{:S(2)}) %collective-permute-start.10) | collective-permute-done | bytes 294944 | tf_op jit(solution)/shard_map/ppermute | solution.py:20
  55.4 1.6 middle.1
  57.6 1.5 collective-permute-start.12
  59.6 4.2 %collective-permute-done.14.refs_1_ = bf16[416,128]{1,0:T(8,128)(2,1)S(1)} collective-permute-done((bf16[416,128]{1,0:T(8,128)(2,1)S(1)}, bf16[416,128]{1,0:T(8,128)(2,1)S(1)}, u32[]{:S(2)}, u32[]{:S(2)}) %collective-permute-start.14) | collective-permute-done | bytes 106528 | tf_op jit(solution)/shard_map/ppermute | solution.py:20
  63.8 2.8 %collective-permute-done.12.refs_2_ = bf16[3,384,128]{2,1,0:T(8,128)(2,1)S(1)} collective-permute-done((bf16[3,384,128]{2,1,0:T(8,128)(2,1)S(1)}, bf16[3,384,128]{2,1,0:T(8,128)(2,1)S(1)}, u32[]{:S(2)}, u32[]{:S(2)}) %collective-permute-start.12) | collective-permute-done | bytes 294944 | tf_op jit(solution)/shard_map/ppermute | solution.py:20
  66.6 1.6 collective-permute-done.15.refs_3_
  68.1 1.5 collective-permute-start.16
  70.4 0.8 input_grad.4
  71.7 3.6 %input_grad.5 = (bf16[384,512]{1,0:T(8,128)(2,1)S(1)}, bf16[384,512]{1,0:T(8,128)(2,1)}, bf16[384,512]{1,0:T(8,128)(2,1)S(1)}) custom-call(bf16[384,1536]{1,0:T(8,128)(2,1)S(1)} %assemble.2.grad_ref.refs_1_.refs_3_, bf16[3,512,2048]{2,1,0:T(8,128)(2,1)S(1)} %bitcast.9), custom_call_target="tpu_custom_call" | custom-call | flops 1 | bytes 1 | tf_op jit(solution)/shard_map/input_grad/pallas_call | solution.py:387
  75.3 0.8 copy-done.8
  76.1 1.1 collective-permute-done.16.refs_2_
  77.6 1.1 collective-permute-done.17.refs_3_
  79.5 0.8 input_grad.6
  80.3 2.9 %collective-permute-done.18 = bf16[384,512]{1,0:T(8,128)(2,1)S(1)} collective-permute-done((bf16[384,512]{1,0:T(8,128)(2,1)S(1)}, bf16[384,512]{1,0:T(8,128)(2,1)S(1)}, u32[]{:S(2)}, u32[]{:S(2)}) %collective-permute-start.18) | collective-permute-done | bytes 393248 | tf_op jit(solution)/shard_map/ppermute | solution.py:20
  83.3 1.6 collective-permute-start.20
  85.5 2.9 %input_grad.7 = (bf16[384,512]{1,0:T(8,128)(2,1)S(1)}, bf16[384,512]{1,0:T(8,128)(2,1)S(1)}, bf16[384,512]{1,0:T(8,128)(2,1)S(1)}) custom-call(bf16[384,1536]{1,0:T(8,128)(2,1)S(1)} %assemble.3.grad_ref.refs_0_.refs_2_, bf16[3,512,2048]{2,1,0:T(8,128)(2,1)S(1)} %bitcast.11), custom_call_target="tpu_custom_call" | custom-call | flops 1 | bytes 1 | tf_op jit(solution)/shard_map/input_grad/pallas_call | solution.py:387
  88.4 3.3 %collective-permute-done.19 = bf16[384,512]{1,0:T(8,128)(2,1)S(1)} collective-permute-done((bf16[384,512]{1,0:T(8,128)(2,1)S(1)}, bf16[384,512]{1,0:T(8,128)(2,1)S(1)}, u32[]{:S(2)}, u32[]{:S(2)}) %collective-permute-start.19) | collective-permute-done | bytes 393248 | tf_op jit(solution)/shard_map/ppermute | solution.py:20
  91.7 0.9 add_convert_fusion.8
  92.5 1.6 collective-permute-start.25
  94.1 0.9 add_convert_fusion.7
  95.0 1.2 split.3
  96.4 1.6 collective-permute-start.23
  98.0 1.8 %collective-permute-start.26 = (bf16[384,512]{1,0:T(8,128)(2,1)}, bf16[384,512]{1,0:T(8,128)(2,1)S(1)}, u32[]{:S(2)}, u32[]{:S(2)}) collective-permute-start(bf16[384,512]{1,0:T(8,128)(2,1)} %add_convert_fusion.7), channel_id=1, source_target_pairs={{0,0},{8,16},{16,8},{24,24},{1,1},{9,17},{17,9},{25,25},{2,2},{10,... | collective-permute-start | bytes 1179656 | tf_op jit(solution)/shard_map/ppermute | solution.py:578
  99.8 1.3 collective-permute-done.22.refs_2_
  101.7 1.1 add_convert_fusion.6
  102.8 2.1 %add_convert_fusion.5 = bf16[384,512]{1,0:T(8,128)(2,1)} fusion(bf16[384,512]{1,0:T(8,128)(2,1)} %collective-permute-done.25, bf16[384,512]{1,0:T(8,128)(2,1)} %add_convert_fusion.8), kind=kLoop, calls=%fused_computation.6 | loop fusion | flops 786432 | bytes 1179648 | tf_op jit(solution)/shard_map/convert_element_type | solution.py:467
  104.9 0.9 broadcast_select_fusion.3
  105.9 8.0 %collective-permute-start.28 = (bf16[384,512]{1,0:T(8,128)(2,1)}, bf16[384,512]{1,0:T(8,128)(2,1)}, u32[]{:S(2)}, u32[]{:S(2)}) collective-permute-start(bf16[384,512]{1,0:T(8,128)(2,1)} %get-tuple-element.112), channel_id=1, source_target_pairs={{0,8},{8,0},{16,24},{24,16},{1,9},{9,1},{17,25},{25,17},{2,10},{10... | collective-permute-start | bytes 1179656 | tf_op jit(solution)/shard_map/ppermute | solution.py:20
  113.9 4.5 %collective-permute-start.29 = (bf16[384,512]{1,0:T(8,128)(2,1)}, bf16[384,512]{1,0:T(8,128)(2,1)}, u32[]{:S(2)}, u32[]{:S(2)}) collective-permute-start(bf16[384,512]{1,0:T(8,128)(2,1)} %add_convert_fusion.5), channel_id=1, source_target_pairs={{0,0},{8,16},{16,8},{24,24},{1,1},{9,17},{17,9},{25,25},{2,2},{10,... | collective-permute-start | bytes 1179656 | tf_op jit(solution)/shard_map/ppermute | solution.py:578
  118.4 0.8 add_convert_fusion.3
  119.2 4.1 %collective-permute-done.28 = bf16[384,512]{1,0:T(8,128)(2,1)} collective-permute-done((bf16[384,512]{1,0:T(8,128)(2,1)}, bf16[384,512]{1,0:T(8,128)(2,1)}, u32[]{:S(2)}, u32[]{:S(2)}) %collective-permute-start.28) | collective-permute-done | bytes 393248 | tf_op jit(solution)/shard_map/ppermute | solution.py:20
  123.3 1.2 add_convert_fusion.2
  124.5 1.4 collective-permute-start.30
  126.0 2.0 %add_convert_fusion.1 = bf16[384,512]{1,0:T(8,128)(2,1)} fusion(bf16[384,512]{1,0:T(8,128)(2,1)} %collective-permute-done.29, bf16[384,512]{1,0:T(8,128)(2,1)} %add_convert_fusion.5), kind=kLoop, calls=%fused_computation.2 | loop fusion | flops 786432 | bytes 1179648 | tf_op jit(solution)/shard_map/convert_element_type | solution.py:467
  127.9 3.7 %collective-permute-start.31 = (bf16[384,512]{1,0:T(8,128)(2,1)}, bf16[384,512]{1,0:T(8,128)(2,1)}, u32[]{:S(2)}, u32[]{:S(2)}) collective-permute-start(bf16[384,512]{1,0:T(8,128)(2,1)} %add_convert_fusion.1), channel_id=1, source_target_pairs={{0,8},{8,0},{16,24},{24,16},{1,9},{9,1},{17,25},{25,17},{2,10},{10... | collective-permute-start | bytes 1179656 | tf_op jit(solution)/shard_map/ppermute | solution.py:20
  131.6 1.4 copy-done.3
  133.0 1.4 copy-done.5
  134.4 5.6 %weight_grad.2 = (f32[3,512,2048]{2,1,0:T(8,128)}, f32[8,128]{1,0:T(8,128)S(1)}) custom-call(bf16[384,1536]{1,0:T(8,128)(2,1)S(1)} %assemble.3.grad_ref.refs_0_.refs_2_, bf16[384,1536]{1,0:T(8,128)(2,1)S(1)} %assemble.2.grad_ref.refs_1_.refs_3_, bf16[384,2048]{1,0:T(8,128)(2,1)S(1)} %copy-done.3, bf16[384,2048]{1,0:T(8,128)(2,1)S(1)} %copy-done.5), custom_call_target="tpu_custom_call" | custom-call | flops 1 | bytes 1 | tf_op jit(solution)/shard_map/weight_grad/pallas_call | solution.py:444
  140.0 1.9 %add_convert_fusion = bf16[384,512]{1,0:T(8,128)(2,1)} fusion(bf16[384,512]{1,0:T(8,128)(2,1)} %collective-permute-done.30, bf16[384,512]{1,0:T(8,128)(2,1)S(1)} %add_convert_fusion.2), kind=kLoop, calls=%fused_computation.1 | loop fusion | flops 786432 | bytes 1179648 | tf_op jit(solution)/shard_map/convert_element_type | solution.py:467
  141.9 1.7 collective-permute-start.32
  143.6 1.1 broadcast_select_fusion.2
  144.7 5.6 %weight_grad.3 = (f32[3,512,2048]{2,1,0:T(8,128)}, f32[8,128]{1,0:T(8,128)S(1)}) custom-call(f32[3,512,2048]{2,1,0:T(8,128)} %get-tuple-element.102.refs_0_, f32[8,128]{1,0:T(8,128)S(1)} %get-tuple-element.103.refs_1_, bf16[384,1536]{1,0:T(8,128)(2,1)S(1)} %assemble.3.grad_ref.refs_0_.refs_2_, ...), custom_call_target="tpu_custom_call", output_to_operand_aliasing={{0}: (0, {})} | custom-call | flops 1 | bytes 1 | tf_op jit(solution)/shard_map/weight_grad/pallas_call | solution.py:444
  150.3 14.7 %all-reduce.2.cloned.1.call-done = bf16[384,512]{1,0:T(8,128)(2,1)} async-done(((bf16[384,512]{1,0:T(8,128)(2,1)}), bf16[384,512]{1,0:T(8,128)(2,1)}) %all-reduce.2.cloned.1.call-update) | async-done | bytes 393232 | tf_op jit(solution)/shard_map/psum | solution.py:590
  165.0 1.4 join.1
  166.3 1.0 broadcast_select_fusion.1
  167.4 1.1 broadcast_select_fusion
  168.4 1.3 pad_maximum_fusion
  (63 shorter events, 8.0 us)
Async XLA Ops:
  7.2 157.8 %all-reduce.2.cloned.1.call-start = ((), (), s32[]{:S(2)}) async-start(), calls=%async_computation | async-start | bytes 786432 | tf_op jit(solution)/shard_map/psum | solution.py:590
  8.3 15.0 %collective-permute-start = (bf16[128,2048]{1,0:T(8,128)(2,1)S(1)}, bf16[128,2048]{1,0:T(8,128)(2,1)S(1)}, u32[]{:S(2)}, u32[]{:S(2)}) collective-permute-start(bf16[128,2048]{1,0:T(8,128)(2,1)S(1)} %constant_dynamic-slice_fusion), channel_id=1, source_target_pairs={{0,4},{4,0},{1,5},{5,1},{2,6},{6,2},{3,7},{7,3},{8,12},{12,8},{9,1... | collective-permute-start | bytes 1572872 | tf_op jit(solution)/shard_map/ppermute | solution.py:20
  11.4 0.9 copy-start.6
  13.0 10.0 %collective-permute-start.3 = (bf16[2,96,128]{2,1,0:T(8,128)(2,1)S(1)}, bf16[2,96,128]{2,1,0:T(8,128)(2,1)S(1)}, u32[]{:S(2)}, u32[]{:S(2)}) collective-permute-start(bf16[2,96,128]{2,1,0:T(8,128)(2,1)S(1)} %get-tuple-element.63), channel_id=1, source_target_pairs={{0,1},{1,0},{2,3},{3,2},{4,5},{5,4},{6,7},{7,6},{8,9},{9,8},{10,11... | collective-permute-start | bytes 147464 | tf_op jit(solution)/shard_map/ppermute | solution.py:20
  13.0 9.9 %collective-permute-start.4 = (bf16[2,96,128]{2,1,0:T(8,128)(2,1)S(1)}, bf16[2,96,128]{2,1,0:T(8,128)(2,1)S(1)}, u32[]{:S(2)}, u32[]{:S(2)}) collective-permute-start(bf16[2,96,128]{2,1,0:T(8,128)(2,1)S(1)} %get-tuple-element.64), channel_id=1, source_target_pairs={{0,2},{1,3},{2,0},{3,1},{4,6},{5,7},{6,4},{7,5},{8,10},{9,11},{10,... | collective-permute-start | bytes 147464 | tf_op jit(solution)/shard_map/ppermute | solution.py:20
  14.6 8.4 %collective-permute-start.5 = (bf16[2,96,128]{2,1,0:T(8,128)(2,1)S(1)}, bf16[2,96,128]{2,1,0:T(8,128)(2,1)S(1)}, u32[]{:S(2)}, u32[]{:S(2)}) collective-permute-start(bf16[2,96,128]{2,1,0:T(8,128)(2,1)S(1)} %get-tuple-element.65), channel_id=1, source_target_pairs={{0,3},{1,2},{2,1},{3,0},{4,7},{5,6},{6,5},{7,4},{8,11},{9,10},{10,... | collective-permute-start | bytes 147464 | tf_op jit(solution)/shard_map/ppermute | solution.py:20
  14.9 2.8 %copy-start = (bf16[512,3,2048]{2,0,1:T(8,128)(2,1)S(1)}, bf16[512,3,2048]{2,0,1:T(8,128)(2,1)}, u32[]{:S(2)}) copy-start(bf16[512,3,2048]{2,0,1:T(8,128)(2,1)} %param.5) | copy-start | bytes 18874372
  17.7 1.4 copy-start.2
  19.1 21.1 %copy-start.1 = (bf16[512,3,2048]{2,0,1:T(8,128)(2,1)S(1)}, bf16[512,3,2048]{2,0,1:T(8,128)(2,1)}, u32[]{:S(2)}) copy-start(bf16[512,3,2048]{2,0,1:T(8,128)(2,1)} %param.5) | copy-start | bytes 18874372
  23.3 4.5 %collective-permute-start.6 = (bf16[2,3,384,128]{3,2,1,0:T(8,128)(2,1)S(1)}, bf16[2,3,384,128]{3,2,1,0:T(8,128)(2,1)S(1)}, u32[]{:S(2)}, u32[]{:S(2)}) collective-permute-start(bf16[2,3,384,128]{3,2,1,0:T(8,128)(2,1)S(1)} %get-tuple-element.66), channel_id=1, source_target_pairs={{0,1},{1,0},{2,3},{3,2},{4,5},{5,4},{6,7},{7,6},{8,9},{9,8},{10,11... | collective-permute-start | bytes 1769480 | tf_op jit(solution)/shard_map/ppermute | solution.py:20
  24.5 14.3 %collective-permute-start.2 = (bf16[128,2048]{1,0:T(8,128)(2,1)S(1)}, bf16[128,2048]{1,0:T(8,128)(2,1)S(1)}, u32[]{:S(2)}, u32[]{:S(2)}) collective-permute-start(bf16[128,2048]{1,0:T(8,128)(2,1)S(1)} %slice.15), channel_id=1, source_target_pairs={{0,4},{4,0},{1,5},{5,1},{2,6},{6,2},{3,7},{7,3},{8,12},{12,8},{9,1... | collective-permute-start | bytes 1572872 | tf_op jit(solution)/shard_map/ppermute | solution.py:20
  26.2 14.1 %collective-permute-start.1 = (bf16[128,2048]{1,0:T(8,128)(2,1)S(1)}, bf16[128,2048]{1,0:T(8,128)(2,1)S(1)}, u32[]{:S(2)}, u32[]{:S(2)}) collective-permute-start(bf16[128,2048]{1,0:T(8,128)(2,1)S(1)} %collective-permute-done.refs_0_), channel_id=1, source_target_pairs={{0,8},{8,0},{16,24},{24,16},{1,9},{9,1},{17,25},{25,17},{2,10},{10... | collective-permute-start | bytes 1572872 | tf_op jit(solution)/shard_map/ppermute | solution.py:20
  27.8 27.6 %copy-start.7 = (f32[7,64]{1,0:T(8,128)S(1)}, f32[7,64]{1,0:T(8,128)}, u32[]{:S(2)}) copy-start(f32[7,64]{1,0:T(8,128)} %taps_ref.1) | copy-start | bytes 5380
  27.8 10.9 %collective-permute-start.7 = (bf16[1,3,384,128]{3,2,1,0:T(8,128)(2,1)S(1)}, bf16[1,3,384,128]{3,2,1,0:T(8,128)(2,1)S(1)}, u32[]{:S(2)}, u32[]{:S(2)}) collective-permute-start(bf16[1,3,384,128]{3,2,1,0:T(8,128)(2,1)S(1)} %add_convert_fusion.11), channel_id=1, source_target_pairs={{0,2},{1,3},{2,0},{3,1},{4,6},{5,7},{6,4},{7,5},{8,10},{9,11},{10,... | collective-permute-start | bytes 884744 | tf_op jit(solution)/shard_map/ppermute | solution.py:20
  44.1 12.8 %copy-start.4 = (bf16[384,2048]{1,0:T(8,128)(2,1)}, bf16[384,2048]{1,0:T(8,128)(2,1)S(1)}, u32[]{:S(2)}) copy-start(bf16[384,2048]{1,0:T(8,128)(2,1)S(1)} %get-tuple-element.101.refs_3_.refs_5_) | copy-start | bytes 4718596
  44.1 2.1 %collective-permute-start.8 = (bf16[2,3,384,128]{3,2,1,0:T(8,128)(2,1)S(1)}, bf16[2,3,384,128]{3,2,1,0:T(8,128)(2,1)S(1)}, u32[]{:S(2)}, u32[]{:S(2)}) collective-permute-start(bf16[2,3,384,128]{3,2,1,0:T(8,128)(2,1)S(1)} %get-tuple-element.69), channel_id=1, source_target_pairs={{0,1},{1,0},{2,3},{3,2},{4,5},{5,4},{6,7},{7,6},{8,9},{9,8},{10,11... | collective-permute-start | bytes 1769480 | tf_op jit(solution)/shard_map/ppermute | solution.py:20
  46.3 9.1 %collective-permute-start.10 = (bf16[1,3,384,128]{3,2,1,0:T(8,128)(2,1)S(1)}, bf16[1,3,384,128]{3,2,1,0:T(8,128)(2,1)S(1)}, u32[]{:S(2)}, u32[]{:S(2)}) collective-permute-start(bf16[1,3,384,128]{3,2,1,0:T(8,128)(2,1)S(1)} %add_convert_fusion.10), channel_id=1, source_target_pairs={{0,2},{1,3},{2,0},{3,1},{4,6},{5,7},{6,4},{7,5},{8,10},{9,11},{10,... | collective-permute-start | bytes 884744 | tf_op jit(solution)/shard_map/ppermute | solution.py:20
  48.4 4.7 %collective-permute-start.9 = (bf16[384,128]{1,0:T(8,128)(2,1)S(1)}, bf16[384,128]{1,0:T(8,128)(2,1)S(1)}, u32[]{:S(2)}, u32[]{:S(2)}) collective-permute-start(bf16[384,128]{1,0:T(8,128)(2,1)S(1)} %get-tuple-element.72), channel_id=1, source_target_pairs={{0,4},{4,0},{1,5},{5,1},{2,6},{6,2},{3,7},{7,3},{8,12},{12,8},{9,1... | collective-permute-start | bytes 294920 | tf_op jit(solution)/shard_map/ppermute | solution.py:20
  57.0 6.8 %collective-permute-start.11 = (bf16[3,384,128]{2,1,0:T(8,128)(2,1)S(1)}, bf16[3,384,128]{2,1,0:T(8,128)(2,1)S(1)}, u32[]{:S(2)}, u32[]{:S(2)}) collective-permute-start(bf16[3,384,128]{2,1,0:T(8,128)(2,1)S(1)} %get-tuple-element.77.refs_0_), channel_id=1, source_target_pairs={{0,1},{1,0},{2,3},{3,2},{4,5},{5,4},{6,7},{7,6},{8,9},{9,8},{10,11... | collective-permute-start | bytes 884744 | tf_op jit(solution)/shard_map/ppermute | solution.py:20
  57.1 6.7 %collective-permute-start.13 = (bf16[3,384,128]{2,1,0:T(8,128)(2,1)S(1)}, bf16[3,384,128]{2,1,0:T(8,128)(2,1)S(1)}, u32[]{:S(2)}, u32[]{:S(2)}) collective-permute-start(bf16[3,384,128]{2,1,0:T(8,128)(2,1)S(1)} %get-tuple-element.74.refs_0_), channel_id=1, source_target_pairs={{0,1},{1,0},{2,3},{3,2},{4,5},{5,4},{6,7},{7,6},{8,9},{9,8},{10,11... | collective-permute-start | bytes 884744 | tf_op jit(solution)/shard_map/ppermute | solution.py:20
  57.6 9.0 %collective-permute-start.12 = (bf16[3,384,128]{2,1,0:T(8,128)(2,1)S(1)}, bf16[3,384,128]{2,1,0:T(8,128)(2,1)S(1)}, u32[]{:S(2)}, u32[]{:S(2)}) collective-permute-start(bf16[3,384,128]{2,1,0:T(8,128)(2,1)S(1)} %get-tuple-element.74.refs_0_), channel_id=1, source_target_pairs={{0,2},{1,3},{2,0},{3,1},{4,6},{5,7},{6,4},{7,5},{8,10},{9,11},{10,... | collective-permute-start | bytes 884744 | tf_op jit(solution)/shard_map/ppermute | solution.py:20
  59.1 4.7 %collective-permute-start.14 = (bf16[416,128]{1,0:T(8,128)(2,1)S(1)}, bf16[416,128]{1,0:T(8,128)(2,1)S(1)}, u32[]{:S(2)}, u32[]{:S(2)}) collective-permute-start(bf16[416,128]{1,0:T(8,128)(2,1)S(1)} %get-tuple-element.75), channel_id=1, source_target_pairs={{0,4},{4,0},{1,5},{5,1},{2,6},{6,2},{3,7},{7,3},{8,12},{12,8},{9,1... | collective-permute-start | bytes 319496 | tf_op jit(solution)/shard_map/ppermute | solution.py:20
  66.6 1.6 collective-permute-start.15
  68.1 9.1 %collective-permute-start.16 = (bf16[3,384,128]{2,1,0:T(8,128)(2,1)S(1)}, bf16[3,384,128]{2,1,0:T(8,128)(2,1)S(1)}, u32[]{:S(2)}, u32[]{:S(2)}) collective-permute-start(bf16[3,384,128]{2,1,0:T(8,128)(2,1)S(1)} %get-tuple-element.77.refs_0_), channel_id=1, source_target_pairs={{0,2},{1,3},{2,0},{3,1},{4,6},{5,7},{6,4},{7,5},{8,10},{9,11},{10,... | collective-permute-start | bytes 884744 | tf_op jit(solution)/shard_map/ppermute | solution.py:20
  71.2 12.1 %collective-permute-start.18 = (bf16[384,512]{1,0:T(8,128)(2,1)S(1)}, bf16[384,512]{1,0:T(8,128)(2,1)S(1)}, u32[]{:S(2)}, u32[]{:S(2)}) collective-permute-start(bf16[384,512]{1,0:T(8,128)(2,1)S(1)} %input_grad.4), channel_id=1, source_target_pairs={{0,4},{4,0},{1,5},{5,1},{2,6},{6,2},{3,7},{7,3},{8,12},{12,8},{9,1... | collective-permute-start | bytes 1179656 | tf_op jit(solution)/shard_map/ppermute | solution.py:20
  75.3 0.8 copy-start.8
  77.2 1.6 collective-permute-start.17
  77.2 14.5 %collective-permute-start.19 = (bf16[384,512]{1,0:T(8,128)(2,1)S(1)}, bf16[384,512]{1,0:T(8,128)(2,1)S(1)}, u32[]{:S(2)}, u32[]{:S(2)}) collective-permute-start(bf16[384,512]{1,0:T(8,128)(2,1)S(1)} %get-tuple-element.83), channel_id=1, source_target_pairs={{0,4},{4,0},{1,5},{5,1},{2,6},{6,2},{3,7},{7,3},{8,12},{12,8},{9,1... | collective-permute-start | bytes 1179656 | tf_op jit(solution)/shard_map/ppermute | solution.py:20
  83.3 10.8 %collective-permute-start.20 = (bf16[384,512]{1,0:T(8,128)(2,1)S(1)}, bf16[384,512]{1,0:T(8,128)(2,1)S(1)}, u32[]{:S(2)}, u32[]{:S(2)}) collective-permute-start(bf16[384,512]{1,0:T(8,128)(2,1)S(1)} %add_convert_fusion.9), channel_id=1, source_target_pairs={{0,8},{8,0},{16,24},{24,16},{1,9},{9,1},{17,25},{25,17},{2,10},{10... | collective-permute-start | bytes 1179656 | tf_op jit(solution)/shard_map/ppermute | solution.py:20
  85.0 16.7 %collective-permute-start.24 = (bf16[384,512]{1,0:T(8,128)(2,1)}, bf16[384,512]{1,0:T(8,128)(2,1)}, u32[]{:S(2)}, u32[]{:S(2)}) collective-permute-start(bf16[384,512]{1,0:T(8,128)(2,1)} %get-tuple-element.92), channel_id=1, source_target_pairs={{0,4},{4,0},{1,5},{5,1},{2,6},{6,2},{3,7},{7,3},{8,12},{12,8},{9,1... | collective-permute-start | bytes 1179656 | tf_op jit(solution)/shard_map/ppermute | solution.py:20
  92.5 10.3 %collective-permute-start.25 = (bf16[384,512]{1,0:T(8,128)(2,1)}, bf16[384,512]{1,0:T(8,128)(2,1)}, u32[]{:S(2)}, u32[]{:S(2)}) collective-permute-start(bf16[384,512]{1,0:T(8,128)(2,1)} %add_convert_fusion.8), channel_id=1, source_target_pairs={{0,8},{8,0},{16,24},{24,16},{1,9},{9,1},{17,25},{25,17},{2,10},{10... | collective-permute-start | bytes 1179656 | tf_op jit(solution)/shard_map/ppermute | solution.py:20
  96.2 1.9 %collective-permute-start.21 = (bf16[2,128,128]{2,1,0:T(8,128)(2,1)}, bf16[2,128,128]{2,1,0:T(8,128)(2,1)S(1)}, u32[]{:S(2)}, u32[]{:S(2)}) collective-permute-start(bf16[2,128,128]{2,1,0:T(8,128)(2,1)} %get-tuple-element.88), channel_id=1, source_target_pairs={{0,1},{1,0},{2,3},{3,2},{4,5},{5,4},{6,7},{7,6},{8,9},{9,8},{10,11... | collective-permute-start | bytes 196616 | tf_op jit(solution)/shard_map/ppermute | solution.py:20
  96.2 4.9 %collective-permute-start.22 = (bf16[2,128,128]{2,1,0:T(8,128)(2,1)S(1)}, bf16[2,128,128]{2,1,0:T(8,128)(2,1)S(1)}, u32[]{:S(2)}, u32[]{:S(2)}) collective-permute-start(bf16[2,128,128]{2,1,0:T(8,128)(2,1)S(1)} %get-tuple-element.89), channel_id=1, source_target_pairs={{0,2},{1,3},{2,0},{3,1},{4,6},{5,7},{6,4},{7,5},{8,10},{9,11},{10,... | collective-permute-start | bytes 196616 | tf_op jit(solution)/shard_map/ppermute | solution.py:20
  96.4 5.3 %collective-permute-start.23 = (bf16[2,128,128]{2,1,0:T(8,128)(2,1)S(1)}, bf16[2,128,128]{2,1,0:T(8,128)(2,1)S(1)}, u32[]{:S(2)}, u32[]{:S(2)}) collective-permute-start(bf16[2,128,128]{2,1,0:T(8,128)(2,1)S(1)} %get-tuple-element.90), channel_id=1, source_target_pairs={{0,3},{1,2},{2,1},{3,0},{4,7},{5,6},{6,5},{7,4},{8,11},{9,10},{10,... | collective-permute-start | bytes 196616 | tf_op jit(solution)/shard_map/ppermute | solution.py:20
  98.0 6.9 %copy-start.10 = (bf16[384,512]{1,0:T(8,128)(2,1)S(1)}, bf16[384,512]{1,0:T(8,128)(2,1)}, u32[]{:S(2)}) copy-start(bf16[384,512]{1,0:T(8,128)(2,1)} %add_convert_fusion.7) | copy-start | bytes 1179652
  98.0 6.9 %collective-permute-start.26 = (bf16[384,512]{1,0:T(8,128)(2,1)}, bf16[384,512]{1,0:T(8,128)(2,1)S(1)}, u32[]{:S(2)}, u32[]{:S(2)}) collective-permute-start(bf16[384,512]{1,0:T(8,128)(2,1)} %add_convert_fusion.7), channel_id=1, source_target_pairs={{0,0},{8,16},{16,8},{24,24},{1,1},{9,17},{17,9},{25,25},{2,2},{10,... | collective-permute-start | bytes 1179656 | tf_op jit(solution)/shard_map/ppermute | solution.py:578
  101.1 17.3 %collective-permute-start.27 = (bf16[384,512]{1,0:T(8,128)(2,1)}, bf16[384,512]{1,0:T(8,128)(2,1)S(1)}, u32[]{:S(2)}, u32[]{:S(2)}) collective-permute-start(bf16[384,512]{1,0:T(8,128)(2,1)} %copy-done.8), channel_id=1, source_target_pairs={{0,4},{4,0},{1,5},{5,1},{2,6},{6,2},{3,7},{7,3},{8,12},{12,8},{9,1... | collective-permute-start | bytes 1179656 | tf_op jit(solution)/shard_map/ppermute | solution.py:20
  102.8 3.1 %copy-start.9 = (bf16[384,512]{1,0:T(8,128)(2,1)}, bf16[384,512]{1,0:T(8,128)(2,1)S(1)}, u32[]{:S(2)}) copy-start(bf16[384,512]{1,0:T(8,128)(2,1)S(1)} %add_convert_fusion.6) | copy-start | bytes 1179652
  105.9 17.4 %collective-permute-start.28 = (bf16[384,512]{1,0:T(8,128)(2,1)}, bf16[384,512]{1,0:T(8,128)(2,1)}, u32[]{:S(2)}, u32[]{:S(2)}) collective-permute-start(bf16[384,512]{1,0:T(8,128)(2,1)} %get-tuple-element.112), channel_id=1, source_target_pairs={{0,8},{8,0},{16,24},{24,16},{1,9},{9,1},{17,25},{25,17},{2,10},{10... | collective-permute-start | bytes 1179656 | tf_op jit(solution)/shard_map/ppermute | solution.py:20
  113.9 12.0 %collective-permute-start.29 = (bf16[384,512]{1,0:T(8,128)(2,1)}, bf16[384,512]{1,0:T(8,128)(2,1)}, u32[]{:S(2)}, u32[]{:S(2)}) collective-permute-start(bf16[384,512]{1,0:T(8,128)(2,1)} %add_convert_fusion.5), channel_id=1, source_target_pairs={{0,0},{8,16},{16,8},{24,24},{1,1},{9,17},{17,9},{25,25},{2,2},{10,... | collective-permute-start | bytes 1179656 | tf_op jit(solution)/shard_map/ppermute | solution.py:578
  124.5 15.5 %collective-permute-start.30 = (bf16[384,512]{1,0:T(8,128)(2,1)S(1)}, bf16[384,512]{1,0:T(8,128)(2,1)}, u32[]{:S(2)}, u32[]{:S(2)}) collective-permute-start(bf16[384,512]{1,0:T(8,128)(2,1)S(1)} %add_convert_fusion.2), channel_id=1, source_target_pairs={{0,0},{8,16},{16,8},{24,24},{1,1},{9,17},{17,9},{25,25},{2,2},{10,... | collective-permute-start | bytes 1179656 | tf_op jit(solution)/shard_map/ppermute | solution.py:578
  127.9 38.4 %collective-permute-start.31 = (bf16[384,512]{1,0:T(8,128)(2,1)}, bf16[384,512]{1,0:T(8,128)(2,1)}, u32[]{:S(2)}, u32[]{:S(2)}) collective-permute-start(bf16[384,512]{1,0:T(8,128)(2,1)} %add_convert_fusion.1), channel_id=1, source_target_pairs={{0,8},{8,0},{16,24},{24,16},{1,9},{9,1},{17,25},{25,17},{2,10},{10... | collective-permute-start | bytes 1179656 | tf_op jit(solution)/shard_map/ppermute | solution.py:20
  131.6 1.4 copy-start.3
  133.0 1.4 copy-start.5
  141.9 25.5 %collective-permute-start.32 = (bf16[384,512]{1,0:T(8,128)(2,1)}, bf16[384,512]{1,0:T(8,128)(2,1)}, u32[]{:S(2)}, u32[]{:S(2)}) collective-permute-start(bf16[384,512]{1,0:T(8,128)(2,1)} %add_convert_fusion), channel_id=1, source_target_pairs={{0,8},{8,0},{16,24},{24,16},{1,9},{9,1},{17,25},{25,17},{2,10},{10... | collective-permute-start | bytes 1179656 | tf_op jit(solution)/shard_map/ppermute | solution.py:20
  165.0 3.5 %copy-start.11 = (bf16[384,512]{1,0:T(8,128)(2,1)S(1)}, bf16[384,512]{1,0:T(8,128)(2,1)}, u32[]{:S(2)}) copy-start(bf16[384,512]{1,0:T(8,128)(2,1)} %all-reduce.2.cloned.1.call-done) | copy-start | bytes 1179652
Sparse Core Ops, SparseCore 0:
  126.1 38.8 all-reduce.1

commit v9 on v8

--- a/solution.py
+++ b/solution.py
@@ -467,21 +467,65 @@
     return (first.astype(jnp.float32) + second.astype(jnp.float32)).astype(jnp.bfloat16)
 
 
-def first_pieces(tokens, k):
-    tok = tokens.shape[0]
+def cut_kernel(_, own_ref, last_ref, own_out, last_out):
+    own_out[...] = own_ref[...]
+    last_out[...] = last_ref[...]
+
+
+def cut(place, tokens):
+    tok, feat = tokens.shape
     if tok % 48 or lax.axis_size("row") % 2:
-        return [swap(tokens, "col", k)]
+        return None
     third = tok // 3
-    parity = lax.axis_index("row") % 2
-    return [swap(lax.dynamic_slice_in_dim(tokens, parity * third, third, axis=0), "col", k)]
-
-
-def other_pieces(tokens, first, k):
-    third = first[0].shape[0]
-    if third == tokens.shape[0]:
-        return first
-    rest = after(tokens, lax.axis_index("row"))[2 * third :]
-    return first + [swap(first[0], "row", 1), swap(after(rest, *first), "col", k)]
+    out = jax.ShapeDtypeStruct((third, feat), jnp.bfloat16)
+    return pl.pallas_call(
+        cut_kernel,
+        grid_spec=pltpu.PrefetchScalarGridSpec(
+            num_scalar_prefetch=1,
+            grid=(1,),
+            in_specs=[
+                pl.BlockSpec((third, feat), lambda i, at: (at[2] % 2, 0)),
+                pl.BlockSpec((third, feat), lambda i, at: (2, 0)),
+            ],
+            out_specs=[pl.BlockSpec(memory_space=pltpu.VMEM)] * 2,
+        ),
+        out_shape=[out, out],
+        compiler_params=params(10, LANES),
+        cost_estimate=SMALL,
+        name="cut",
+    )(place, tokens, tokens)
+
+
+def put_kernel(place, *refs):
+    pair_ref, summed_ref, out_ref = refs[-3:]
+    outer = (place[2] == 0) | (place[2] == 3)
+
+    @pl.when(outer)
+    def _():
+        out_ref[...] = pair_ref[...]
+
+    @pl.when(jnp.logical_not(outer))
+    def _():
+        out_ref[...] = summed_ref[...]
+
+
+def put(place, filled, pair, summed, chunk, feat):
+    tok, step = pair.shape
+    chained = filled is not None
+    return pl.pallas_call(
+        put_kernel,
+        grid_spec=pltpu.PrefetchScalarGridSpec(
+            num_scalar_prefetch=1,
+            grid=(1,),
+            in_specs=[pl.BlockSpec(memory_space=pl.ANY)] * chained + [resident((tok, step), LANES)] * 2,
+            out_specs=pl.BlockSpec((tok, step), lambda i, _: (0, chunk)),
+        ),
+        out_shape=jax.ShapeDtypeStruct((tok, feat), jnp.bfloat16),
+        input_output_aliases={1: 0} if chained else {},
+        compiler_params=params(6, LANES),
+        cost_estimate=SMALL,
+        name="put",
+    )(place, *([filled] if chained else []), pair, summed)
 
 
 def on_device(tokens, weight, taps, upstream):
@@ -501,13 +545,16 @@
         fars = [swap(pair, "depth", 2 * i + 2) for i, pair in enumerate(pairs)]
         return x, [keep, near] + fars, pairs, fars
 
-    first = [first_pieces(tokens, k) for k in range(1, n_col)]
+    thirds = cut(place, tokens)
+    first = [[swap(tokens if thirds is None else thirds[0], "col", k)] for k in range(1, n_col)]
     ups = split_lanes(place, upstream, n_col, n_depth)
     ups = [up if r == 0 else swap(up, "depth", r) for r, up in enumerate(ups)]
     x, terms, pairs, fars = project_and_sum([tokens], *[piece for of in first for piece in of], *ups[1:])
     xs, parts = [x], [terms]
     for k in range(1, n_col):
-        x_pieces = other_pieces(tokens, first[k - 1], k)
+        x_pieces = first[k - 1]
+        if thirds is not None:
+            x_pieces += [swap(x_pieces[0], "row", 1), swap(after(thirds[1], *x_pieces), "col", k)]
         x_pieces[-1] = after(x_pieces[-1], *fars)
         x, terms, pairs, fars = project_and_sum(x_pieces)
         xs.append(x)
@@ -544,37 +591,32 @@
     own_part = input_grad(lhs[0], w, 0, 1, chunks, width)
     outer = (row_at == 0) | (row_at == 3)
     line = lax.axis_size("row") == 4
-    hopping = chunks - 1
     inward, across, summed, done = ([None] * chunks for _ in range(4))
-    pair = cross = filled = None
+    pair = cross = filled = grad_tokens = None
     marks = []
-
-    def with_sent(c):
-        total = after(own_part[c], *marks).astype(jnp.float32)
-        for of in sent:
-            total = total + of[c].astype(jnp.float32)
-        return total.astype(jnp.bfloat16)
-
-    for slot in range(hopping + 3):
-        if slot < hopping:
-            inward[slot] = with_sent(slot)
+    for slot in range(chunks + 3):
+        if slot < chunks:
+            total = after(own_part[slot], *marks).astype(jnp.float32)
+            for of in sent:
+                total = total + of[slot].astype(jnp.float32)
+            inward[slot] = total.astype(jnp.bfloat16)
             marks = [inward[slot]]
         if not line:
-            if slot < hopping:
+            if slot < chunks:
                 done[slot] = lax.psum(inward[slot], "row")
         else:
-            if 0 <= slot - 1 < hopping:
+            if 0 <= slot - 1 < chunks:
                 across[slot - 1] = added(after(inward[slot - 1], *marks), pair)
                 marks = [across[slot - 1]]
-            if 0 <= slot - 2 < hopping:
+            if 0 <= slot - 2 < chunks:
                 summed[slot - 2] = added(after(across[slot - 2], *marks), cross)
                 marks = [summed[slot - 2]]
-            if 0 <= slot - 3 < hopping:
-                done[slot - 3] = jnp.where(outer, pair, summed[slot - 3])
-            if slot < hopping + 2:
+            if 0 <= slot - 3 < chunks:
+                grad_tokens = put(place, grad_tokens, pair, summed[slot - 3], slot - 3, tokens.shape[1])
+            if slot < chunks + 2:
                 out = summed[slot - 2] if slot >= 2 else inward[slot]
-                pair = swap(jnp.where(outer, inward[slot], out) if slot < hopping else out, "row", 1)
-            if 0 <= slot - 1 < hopping:
+                pair = swap(jnp.where(outer, inward[slot], out) if slot < chunks else out, "row", 1)
+            if 0 <= slot - 1 < chunks:
                 cross = lax.ppermute(across[slot - 1], "row", [(0, 0), (1, 2), (2, 1), (3, 3)])
         if slot == 0:
             own_part += input_grad(after(lhs[0], *marks), w, 1, chunks, chunks, width)
@@ -582,20 +624,18 @@
         if slot == 1:
             for k, parts_of in enumerate(held):
                 sent[k] += [swap(after(part, *marks), "col", k + 1) for part in parts_of]
+        if slot == 2:
+            marks += [of[-1] for of in sent]
+        if slot in (2, 3):
+            filled = weight_grad(filled, [after(lhs[0], *marks)] + lhs[1:], xs, slot - 2, 3, width)
+            marks = [filled[1]]
+        if slot == chunks:
             blocks = split_rows(place, [after(blocks[0], *marks)] + blocks[1:], n_depth)
             blocks = [block if r == 0 else swap(block, "depth", r) for r, block in enumerate(blocks)]
             marks += blocks[1:]
-        if slot == 2:
-            last = with_sent(hopping)
-            done[hopping] = lax.psum(last, "row")
-            marks = [last]
-        if slot >= hopping and slot < hopping + 2:
-            filled = weight_grad(filled, [after(lhs[0], *marks)] + lhs[1:], xs, slot - hopping, 3, width)
-            marks = [filled[1]]
-    output, grad_taps = join(
-        place, filled[1], [after(blocks[0], *marks, done[hopping])] + blocks[1:], taps.shape[1]
-    )
-    grad_tokens = jnp.concatenate(done, axis=1)
+    if not line:
+        grad_tokens = jnp.concatenate(done, axis=1)
+    output, grad_taps = join(place, filled[1], [after(blocks[0], *marks)] + blocks[1:], taps.shape[1])
     grad_weight = jnp.transpose(filled[0], (1, 0, 2))
     return (output, grad_tokens, grad_weight, grad_taps)
 

time: 178 us -> 146 us (0.82)
  between operations: 14.3 us -> 1 us
  other arithmetic: 16.6 us -> 4.41 us
  waiting for transfers between devices: 56.7 us -> 51.2 us
  Pallas kernels: 33.7 us -> 38.9 us
  local copies, waits for them, and re-layouts: 10.9 us -> 7.01 us
    psum x1 -> x0, waiting for transfers between devices: 14.7 us -> none  [on_device(): done[hopping] = lax.psum(last, 'row')]
    ppermute x30 -> x31, waiting for transfers between devices: 42 us -> 51.2 us  [swap(): return lax.ppermute(value, axis, [(i, i ^ flip) for i in range(count)])]
    convert_element_type x7 -> x8, other arithmetic: 8.18 us -> 1.86 us  [added(): (first.astype(jnp.float32) + second.astype(jnp.float32)).astype(jnp.bfloa...]
    pallas_call x0 -> x5, Pallas kernels: none -> 5.88 us  [the longest x4 5.27 us: put(): pl.pallas_call(put_kernel, grid_spec=pltpu.PrefetchScalarGridSpec(num_sca...]
    ppermute x3 -> x4, starting transfers between devices: 7.65 us -> 2.72 us  [on_device(): lax.ppermute(across[slot - 1], 'row', [(0, 0), (1, 2), (2, 1), (3, 3)])]
    ppermute x30 -> x31, starting transfers between devices: 36.7 us -> 40.6 us  [swap(): return lax.ppermute(value, axis, [(i, i ^ flip) for i in range(count)])]
    select_n x3 -> x0, other arithmetic: 3.15 us -> none  [on_device(): done[slot - 3] = jnp.where(outer, pair, summed[slot - 3])]
    unnamed x24 -> x18, local copies, waits for them, and re-layouts: 8.73 us -> 7.01 us
  transfers between devices with their start and end apart: 34 -> 35, of which waited for: 17 -> 17; matrix products, arithmetic and copies ran while one was open for 9% -> 3% of each run, Pallas kernels for 16% -> 22%
where the time goes in v9:
time: 146 us
  waiting for transfers between devices  51.2 us (35%)
  starting transfers between devices  43.3 us (30%)
  Pallas kernels  38.9 us (27%)
  local copies, waits for them, and re-layouts  7.01 us (5%)
  other arithmetic  4.41 us (3%)
    ppermute x31, waiting for transfers between devices, swap(): return lax.ppermute(value, axis, [(i, i ^ flip) for i in range(count)])  51.2 us
    ppermute x31, starting transfers between devices, swap(): return lax.ppermute(value, axis, [(i, i ^ flip) for i in range(count)])  40.6 us
    pallas_call x2, Pallas kernels, weight_grad(): pl.pallas_call(functools.partial(weight_grad_kernel, chained=chained, gro...  11.2 us
    pallas_call x4, Pallas kernels, input_grad(): pl.pallas_call(functools.partial(input_grad_kernel, first=first), grid=(c...  7.98 us
    pallas_call x2, Pallas kernels, project(): pl.pallas_call(functools.partial(project_kernel, pieces=len(xs), count=co...  7.72 us
    unnamed x18, local copies, waits for them, and re-layouts  7.01 us
    pallas_call x4, Pallas kernels, put(): pl.pallas_call(put_kernel, grid_spec=pltpu.PrefetchScalarGridSpec(num_sca...  5.27 us
  transfers between devices with their start and end apart: 35, of which 17 were waited for; matrix products, arithmetic and copies ran while one was open for 3% of the time, Pallas kernels for 22%

profile of v9, /device:TPU:0, one launch (start us, length us, event | category | flops | bytes accessed | tf_op | source)
XLA Modules:
  0.0 145.8 jit_solution(8469151035394871500)
XLA Ops:
  0.7 1.4 copy-done.3
  2.1 0.6 cut.1
  2.7 3.0 %collective-permute-start = (bf16[128,2048]{1,0:T(8,128)(2,1)S(1)}, bf16[128,2048]{1,0:T(8,128)(2,1)S(1)}, u32[]{:S(2)}, u32[]{:S(2)}) collective-permute-start(bf16[128,2048]{1,0:T(8,128)(2,1)S(1)} %get-tuple-element.62), channel_id=1, source_target_pairs={{0,4},{4,0},{1,5},{5,1},{2,6},{6,2},{3,7},{7,3},{8,12},{12,8},{9,1... | collective-permute-start | bytes 1572872 | tf_op jit(solution)/shard_map/ppermute | solution.py:20
  5.8 0.6 split.2
  6.5 1.6 %collective-permute-start.4 = (bf16[2,96,128]{2,1,0:T(8,128)(2,1)S(1)}, bf16[2,96,128]{2,1,0:T(8,128)(2,1)S(1)}, u32[]{:S(2)}, u32[]{:S(2)}) collective-permute-start(bf16[2,96,128]{2,1,0:T(8,128)(2,1)S(1)} %get-tuple-element.68), channel_id=1, source_target_pairs={{0,2},{1,3},{2,0},{3,1},{4,6},{5,7},{6,4},{7,5},{8,10},{9,11},{10,... | collective-permute-start | bytes 147464 | tf_op jit(solution)/shard_map/ppermute | solution.py:20
  8.3 2.8 %copy-done = bf16[512,3,2048]{2,0,1:T(8,128)(2,1)S(1)} copy-done((bf16[512,3,2048]{2,0,1:T(8,128)(2,1)S(1)}, bf16[512,3,2048]{2,0,1:T(8,128)(2,1)}, u32[]{:S(2)}) %copy-start) | copy-done | bytes 6291480
  11.1 3.8 %project.2 = (bf16[2,3,384,128]{3,2,1,0:T(8,128)(2,1)S(1)}, bf16[2,3,384,128]{3,2,1,0:T(8,128)(2,1)S(1)}) custom-call(s32[4]{0:T(128)S(1)} %pad_add_fusion.place._, bf16[384,2048]{1,0:T(8,128)(2,1)S(1)} %copy-done.3, bf16[3,512,2048]{2,1,0:T(8,128)(2,1)S(1)} %bitcast.6), custom_call_target="tpu_custom_call" | custom-call | flops 1 | bytes 1 | tf_op jit(solution)/shard_map/project/pallas_call | solution.py:87
  14.9 2.8 %collective-permute-done.refs_0_ = bf16[128,2048]{1,0:T(8,128)(2,1)S(1)} collective-permute-done((bf16[128,2048]{1,0:T(8,128)(2,1)S(1)}, bf16[128,2048]{1,0:T(8,128)(2,1)S(1)}, u32[]{:S(2)}, u32[]{:S(2)}) %collective-permute-start) | collective-permute-done | bytes 524320 | tf_op jit(solution)/shard_map/ppermute | solution.py:20
  17.7 1.7 %collective-permute-start.2 = (bf16[128,2048]{1,0:T(8,128)(2,1)S(1)}, bf16[128,2048]{1,0:T(8,128)(2,1)S(1)}, u32[]{:S(2)}, u32[]{:S(2)}) collective-permute-start(bf16[128,2048]{1,0:T(8,128)(2,1)S(1)} %get-tuple-element.64), channel_id=1, source_target_pairs={{0,4},{4,0},{1,5},{5,1},{2,6},{6,2},{3,7},{7,3},{8,12},{12,8},{9,1... | collective-permute-start | bytes 1572872 | tf_op jit(solution)/shard_map/ppermute | solution.py:20
  19.4 1.6 %collective-permute-start.1 = (bf16[128,2048]{1,0:T(8,128)(2,1)S(1)}, bf16[128,2048]{1,0:T(8,128)(2,1)S(1)}, u32[]{:S(2)}, u32[]{:S(2)}) collective-permute-start(bf16[128,2048]{1,0:T(8,128)(2,1)S(1)} %collective-permute-done.refs_0_), channel_id=1, source_target_pairs={{0,8},{8,0},{16,24},{24,16},{1,9},{9,1},{17,25},{25,17},{2,10},{10... | collective-permute-start | bytes 1572872 | tf_op jit(solution)/shard_map/ppermute | solution.py:20
  21.1 1.6 %collective-permute-start.7 = (bf16[1,3,384,128]{3,2,1,0:T(8,128)(2,1)S(1)}, bf16[1,3,384,128]{3,2,1,0:T(8,128)(2,1)S(1)}, u32[]{:S(2)}, u32[]{:S(2)}) collective-permute-start(bf16[1,3,384,128]{3,2,1,0:T(8,128)(2,1)S(1)} %add_convert_fusion.13), channel_id=1, source_target_pairs={{0,2},{1,3},{2,0},{3,1},{4,6},{5,7},{6,4},{7,5},{8,10},{9,11},{10,... | collective-permute-start | bytes 884744 | tf_op jit(solution)/shard_map/ppermute | solution.py:20
  22.7 9.4 %collective-permute-done.2.refs_2_ = bf16[128,2048]{1,0:T(8,128)(2,1)S(1)} collective-permute-done((bf16[128,2048]{1,0:T(8,128)(2,1)S(1)}, bf16[128,2048]{1,0:T(8,128)(2,1)S(1)}, u32[]{:S(2)}, u32[]{:S(2)}) %collective-permute-start.2) | collective-permute-done | bytes 524320 | tf_op jit(solution)/shard_map/ppermute | solution.py:20
  32.0 1.5 collective-permute-done.1.refs_1_
  33.5 4.0 %project.3 = (bf16[2,3,384,128]{3,2,1,0:T(8,128)(2,1)S(1)}, bf16[2,3,384,128]{3,2,1,0:T(8,128)(2,1)S(1)}, bf16[384,2048]{1,0:T(8,128)(2,1)S(1)}) custom-call(s32[4]{0:T(128)S(1)} %pad_add_fusion.place._, bf16[128,2048]{1,0:T(8,128)(2,1)S(1)} %collective-permute-done.refs_0_, bf16[128,2048]{1,0:T(8,128)(2,1)S(1)} %collective-permute-done.1.refs_1_, ...), custom_call_target="tpu_custom_call" | custom-call | flops 1 | bytes 1 | tf_op jit(solution)/shard_map/project/pallas_call | solution.py:87
  37.6 2.0 %collective-permute-done.8.refs_6_ = bf16[2,3,384,128]{3,2,1,0:T(8,128)(2,1)S(1)} collective-permute-done((bf16[2,3,384,128]{3,2,1,0:T(8,128)(2,1)S(1)}, bf16[2,3,384,128]{3,2,1,0:T(8,128)(2,1)S(1)}, u32[]{:S(2)}, u32[]{:S(2)}) %collective-permute-start.8) | collective-permute-done | bytes 589856 | tf_op jit(solution)/shard_map/ppermute | solution.py:20
  39.6 1.6 %collective-permute-start.10 = (bf16[1,3,384,128]{3,2,1,0:T(8,128)(2,1)S(1)}, bf16[1,3,384,128]{3,2,1,0:T(8,128)(2,1)S(1)}, u32[]{:S(2)}, u32[]{:S(2)}) collective-permute-start(bf16[1,3,384,128]{3,2,1,0:T(8,128)(2,1)S(1)} %add_convert_fusion.12), channel_id=1, source_target_pairs={{0,2},{1,3},{2,0},{3,1},{4,6},{5,7},{6,4},{7,5},{8,10},{9,11},{10,... | collective-permute-start | bytes 884744 | tf_op jit(solution)/shard_map/ppermute | solution.py:20
  41.8 0.6 collective-permute-start.9
  42.3 4.1 %collective-permute-done.9.refs_1_ = bf16[384,128]{1,0:T(8,128)(2,1)S(1)} collective-permute-done((bf16[384,128]{1,0:T(8,128)(2,1)S(1)}, bf16[384,128]{1,0:T(8,128)(2,1)S(1)}, u32[]{:S(2)}, u32[]{:S(2)}) %collective-permute-start.9) | collective-permute-done | bytes 98336 | tf_op jit(solution)/shard_map/ppermute | solution.py:20
  46.4 2.3 %collective-permute-done.10.refs_7_ = bf16[1,3,384,128]{3,2,1,0:T(8,128)(2,1)S(1)} collective-permute-done((bf16[1,3,384,128]{3,2,1,0:T(8,128)(2,1)S(1)}, bf16[1,3,384,128]{3,2,1,0:T(8,128)(2,1)S(1)}, u32[]{:S(2)}, u32[]{:S(2)}) %collective-permute-start.10) | collective-permute-done | bytes 294944 | tf_op jit(solution)/shard_map/ppermute | solution.py:20
  48.7 1.6 %middle.1 = (bf16[3,384,128]{2,1,0:T(8,128)(2,1)S(1)}, bf16[3,384,128]{2,1,0:T(8,128)(2,1)S(1)}, bf16[416,128]{1,0:T(8,128)(2,1)S(1)}, bf16[416,128]{1,0:T(8,128)(2,1)S(1)}) custom-call(s32[4]{0:T(128)S(1)} %pad_add_fusion.place._, f32[7,64]{1,0:T(8,128)S(1)} %copy-done.8, bf16[384,128]{1,0:T(8,128)(2,1)S(1)} %get-tuple-element.75.refs_0_, ...), custom_call_target="tpu_custom_call" | custom-call | flops 1 | bytes 1 | tf_op jit(solution)/shard_map/middle/pallas_call | solution.py:311
  50.4 1.6 %collective-permute-start.12 = (bf16[3,384,128]{2,1,0:T(8,128)(2,1)S(1)}, bf16[3,384,128]{2,1,0:T(8,128)(2,1)S(1)}, u32[]{:S(2)}, u32[]{:S(2)}) collective-permute-start(bf16[3,384,128]{2,1,0:T(8,128)(2,1)S(1)} %get-tuple-element.78.refs_0_), channel_id=1, source_target_pairs={{0,2},{1,3},{2,0},{3,1},{4,6},{5,7},{6,4},{7,5},{8,10},{9,11},{10,... | collective-permute-start | bytes 884744 | tf_op jit(solution)/shard_map/ppermute | solution.py:20
  52.6 4.7 %collective-permute-done.14.refs_1_ = bf16[416,128]{1,0:T(8,128)(2,1)S(1)} collective-permute-done((bf16[416,128]{1,0:T(8,128)(2,1)S(1)}, bf16[416,128]{1,0:T(8,128)(2,1)S(1)}, u32[]{:S(2)}, u32[]{:S(2)}) %collective-permute-start.14) | collective-permute-done | bytes 106528 | tf_op jit(solution)/shard_map/ppermute | solution.py:20
  57.3 2.5 %collective-permute-done.12.refs_2_ = bf16[3,384,128]{2,1,0:T(8,128)(2,1)S(1)} collective-permute-done((bf16[3,384,128]{2,1,0:T(8,128)(2,1)S(1)}, bf16[3,384,128]{2,1,0:T(8,128)(2,1)S(1)}, u32[]{:S(2)}, u32[]{:S(2)}) %collective-permute-start.12) | collective-permute-done | bytes 294944 | tf_op jit(solution)/shard_map/ppermute | solution.py:20
  59.8 1.6 %collective-permute-done.15.refs_3_ = bf16[3,384,128]{2,1,0:T(8,128)(2,1)S(1)} collective-permute-done((bf16[3,384,128]{2,1,0:T(8,128)(2,1)S(1)}, bf16[3,384,128]{2,1,0:T(8,128)(2,1)S(1)}, u32[]{:S(2)}, u32[]{:S(2)}) %collective-permute-start.15) | collective-permute-done | bytes 294944 | tf_op jit(solution)/shard_map/ppermute | solution.py:20
  61.4 1.5 %collective-permute-start.16 = (bf16[3,384,128]{2,1,0:T(8,128)(2,1)S(1)}, bf16[3,384,128]{2,1,0:T(8,128)(2,1)S(1)}, u32[]{:S(2)}, u32[]{:S(2)}) collective-permute-start(bf16[3,384,128]{2,1,0:T(8,128)(2,1)S(1)} %get-tuple-element.81.refs_0_), channel_id=1, source_target_pairs={{0,2},{1,3},{2,0},{3,1},{4,6},{5,7},{6,4},{7,5},{8,10},{9,11},{10,... | collective-permute-start | bytes 884744 | tf_op jit(solution)/shard_map/ppermute | solution.py:20
  62.9 0.7 assemble.2.grad_ref.refs_1_.refs_3_
  63.7 0.8 input_grad.4
  64.4 0.6 collective-permute-start.18
  65.0 3.6 %input_grad.5 = (bf16[384,512]{1,0:T(8,128)(2,1)}, bf16[384,512]{1,0:T(8,128)(2,1)S(1)}, bf16[384,512]{1,0:T(8,128)(2,1)S(1)}) custom-call(bf16[384,1536]{1,0:T(8,128)(2,1)S(1)} %assemble.2.grad_ref.refs_1_.refs_3_, bf16[3,512,2048]{2,1,0:T(8,128)(2,1)S(1)} %bitcast.9), custom_call_target="tpu_custom_call" | custom-call | flops 1 | bytes 1 | tf_op jit(solution)/shard_map/input_grad/pallas_call | solution.py:387
  68.6 1.9 %collective-permute-done.16.refs_2_ = bf16[3,384,128]{2,1,0:T(8,128)(2,1)S(1)} collective-permute-done((bf16[3,384,128]{2,1,0:T(8,128)(2,1)S(1)}, bf16[3,384,128]{2,1,0:T(8,128)(2,1)S(1)}, u32[]{:S(2)}, u32[]{:S(2)}) %collective-permute-start.16) | collective-permute-done | bytes 294944 | tf_op jit(solution)/shard_map/ppermute | solution.py:20
  70.8 1.2 collective-permute-done.17.refs_3_
  72.0 0.7 assemble.3.grad_ref.refs_0_.refs_2_
  72.8 0.8 input_grad.6
  73.6 2.9 %collective-permute-done.18 = bf16[384,512]{1,0:T(8,128)(2,1)S(1)} collective-permute-done((bf16[384,512]{1,0:T(8,128)(2,1)S(1)}, bf16[384,512]{1,0:T(8,128)(2,1)S(1)}, u32[]{:S(2)}, u32[]{:S(2)}) %collective-permute-start.18) | collective-permute-done | bytes 393248 | tf_op jit(solution)/shard_map/ppermute | solution.py:20
  76.5 0.9 add_convert_fusion.11
  77.4 1.6 %collective-permute-start.20 = (bf16[384,512]{1,0:T(8,128)(2,1)}, bf16[384,512]{1,0:T(8,128)(2,1)}, u32[]{:S(2)}, u32[]{:S(2)}) collective-permute-start(bf16[384,512]{1,0:T(8,128)(2,1)} %add_convert_fusion.11), channel_id=1, source_target_pairs={{0,8},{8,0},{16,24},{24,16},{1,9},{9,1},{17,25},{25,17},{2,10},{10... | collective-permute-start | bytes 1179656 | tf_op jit(solution)/shard_map/ppermute | solution.py:20
  79.5 2.8 %copy-done.2 = bf16[512,3,2048]{2,0,1:T(8,128)(2,1)S(1)} copy-done((bf16[512,3,2048]{2,0,1:T(8,128)(2,1)S(1)}, bf16[512,3,2048]{2,0,1:T(8,128)(2,1)}, u32[]{:S(2)}) %copy-start.2) | copy-done | bytes 6291480
  82.2 2.9 %input_grad.7 = (bf16[384,512]{1,0:T(8,128)(2,1)S(1)}, bf16[384,512]{1,0:T(8,128)(2,1)S(1)}, bf16[384,512]{1,0:T(8,128)(2,1)S(1)}) custom-call(bf16[384,1536]{1,0:T(8,128)(2,1)S(1)} %assemble.3.grad_ref.refs_0_.refs_2_, bf16[3,512,2048]{2,1,0:T(8,128)(2,1)S(1)} %bitcast.11), custom_call_target="tpu_custom_call" | custom-call | flops 1 | bytes 1 | tf_op jit(solution)/shard_map/input_grad/pallas_call | solution.py:387
  85.1 1.1 add_convert_fusion.10
  86.2 1.6 %collective-permute-start.22 = (bf16[384,512]{1,0:T(8,128)(2,1)S(1)}, bf16[384,512]{1,0:T(8,128)(2,1)S(1)}, u32[]{:S(2)}, u32[]{:S(2)}) collective-permute-start(bf16[384,512]{1,0:T(8,128)(2,1)S(1)} %add_convert_fusion.10), channel_id=1, source_target_pairs={{0,8},{8,0},{16,24},{24,16},{1,9},{9,1},{17,25},{25,17},{2,10},{10... | collective-permute-start | bytes 1179656 | tf_op jit(solution)/shard_map/ppermute | solution.py:20
  87.8 1.2 add_convert_fusion.9
  89.0 0.7 collective-permute-start.23
  89.7 2.6 %collective-permute-done.21 = bf16[384,512]{1,0:T(8,128)(2,1)S(1)} collective-permute-done((bf16[384,512]{1,0:T(8,128)(2,1)S(1)}, bf16[384,512]{1,0:T(8,128)(2,1)S(1)}, u32[]{:S(2)}, u32[]{:S(2)}) %collective-permute-start.21) | collective-permute-done | bytes 393248 | tf_op jit(solution)/shard_map/ppermute | solution.py:20
  92.4 2.7 %collective-permute-done.22 = bf16[384,512]{1,0:T(8,128)(2,1)S(1)} collective-permute-done((bf16[384,512]{1,0:T(8,128)(2,1)S(1)}, bf16[384,512]{1,0:T(8,128)(2,1)S(1)}, u32[]{:S(2)}, u32[]{:S(2)}) %collective-permute-start.22) | collective-permute-done | bytes 393248 | tf_op jit(solution)/shard_map/ppermute | solution.py:20
  95.2 1.1 collective-permute-start.24
  96.5 4.7 %collective-permute-start.25 = (bf16[384,512]{1,0:T(8,128)(2,1)S(1)}, bf16[384,512]{1,0:T(8,128)(2,1)S(1)}, u32[]{:S(2)}, u32[]{:S(2)}) collective-permute-start(bf16[384,512]{1,0:T(8,128)(2,1)S(1)} %get-tuple-element.120), channel_id=1, source_target_pairs={{0,8},{8,0},{16,24},{24,16},{1,9},{9,1},{17,25},{25,17},{2,10},{10... | collective-permute-start | bytes 1179656 | tf_op jit(solution)/shard_map/ppermute | solution.py:20
  101.1 0.7 collective-permute-start.26
  101.8 1.3 collective-permute-done.24
  103.1 5.6 %weight_grad.2 = (f32[3,512,2048]{2,1,0:T(8,128)}, f32[8,128]{1,0:T(8,128)S(1)}) custom-call(bf16[384,1536]{1,0:T(8,128)(2,1)S(1)} %assemble.3.grad_ref.refs_0_.refs_2_, bf16[384,1536]{1,0:T(8,128)(2,1)S(1)} %assemble.2.grad_ref.refs_1_.refs_3_, bf16[384,2048]{1,0:T(8,128)(2,1)S(1)} %copy-done.4, bf16[384,2048]{1,0:T(8,128)(2,1)S(1)} %copy-done.6), custom_call_target="tpu_custom_call" | custom-call | flops 1 | bytes 1 | tf_op jit(solution)/shard_map/weight_grad/pallas_call | solution.py:444
  109.2 2.1 %collective-permute-start.27 = (bf16[384,512]{1,0:T(8,128)(2,1)S(1)}, bf16[384,512]{1,0:T(8,128)(2,1)S(1)}, u32[]{:S(2)}, u32[]{:S(2)}) collective-permute-start(bf16[384,512]{1,0:T(8,128)(2,1)S(1)} %get-tuple-element.118), channel_id=1, source_target_pairs={{0,8},{8,0},{16,24},{24,16},{1,9},{9,1},{17,25},{25,17},{2,10},{10... | collective-permute-start | bytes 1179656 | tf_op jit(solution)/shard_map/ppermute | solution.py:20
  111.2 0.7 collective-permute-start.28
  111.9 5.6 %weight_grad.3 = (f32[3,512,2048]{2,1,0:T(8,128)}, f32[8,128]{1,0:T(8,128)S(1)}) custom-call(f32[3,512,2048]{2,1,0:T(8,128)} %get-tuple-element.97.refs_0_, f32[8,128]{1,0:T(8,128)S(1)} %get-tuple-element.98.refs_1_, bf16[384,1536]{1,0:T(8,128)(2,1)S(1)} %assemble.3.grad_ref.refs_0_.refs_2_, ...), custom_call_target="tpu_custom_call", output_to_operand_aliasing={{0}: (0, {})} | custom-call | flops 1 | bytes 1 | tf_op jit(solution)/shard_map/weight_grad/pallas_call | solution.py:444
  117.6 0.7 collective-permute-start.32
  118.5 0.6 split.3
  119.1 2.2 %collective-permute-start.30 = (bf16[2,128,128]{2,1,0:T(8,128)(2,1)S(1)}, bf16[2,128,128]{2,1,0:T(8,128)(2,1)S(1)}, u32[]{:S(2)}, u32[]{:S(2)}) collective-permute-start(bf16[2,128,128]{2,1,0:T(8,128)(2,1)S(1)} %get-tuple-element.111), channel_id=1, source_target_pairs={{0,2},{1,3},{2,0},{3,1},{4,6},{5,7},{6,4},{7,5},{8,10},{9,11},{10,... | collective-permute-start | bytes 196616 | tf_op jit(solution)/shard_map/ppermute | solution.py:20
  121.3 5.3 %collective-permute-start.33 = (bf16[384,512]{1,0:T(8,128)(2,1)S(1)}, bf16[384,512]{1,0:T(8,128)(2,1)S(1)}, u32[]{:S(2)}, u32[]{:S(2)}) collective-permute-start(bf16[384,512]{1,0:T(8,128)(2,1)S(1)} %add_convert_fusion.1.refs_2_), channel_id=1, source_target_pairs={{0,8},{8,0},{16,24},{24,16},{1,9},{9,1},{17,25},{25,17},{2,10},{10... | collective-permute-start | bytes 1179656 | tf_op jit(solution)/shard_map/ppermute | solution.py:20
  126.8 4.7 %collective-permute-start.34 = (bf16[384,512]{1,0:T(8,128)(2,1)S(1)}, bf16[384,512]{1,0:T(8,128)(2,1)S(1)}, u32[]{:S(2)}, u32[]{:S(2)}) collective-permute-start(bf16[384,512]{1,0:T(8,128)(2,1)S(1)} %add_convert_fusion.refs_2_), channel_id=1, source_target_pairs={{0,8},{8,0},{16,24},{24,16},{1,9},{9,1},{17,25},{25,17},{2,10},{10... | collective-permute-start | bytes 1179656 | tf_op jit(solution)/shard_map/ppermute | solution.py:20
  131.5 1.3 put.4.refs_0_
  132.8 1.3 put.5.refs_0_
  134.1 1.4 join.1
  135.5 1.1 collective-permute-done.33.refs_1_
  136.6 1.3 put.6.refs_0_
  137.9 6.6 %collective-permute-done.34.refs_1_ = bf16[384,512]{1,0:T(8,128)(2,1)S(1)} collective-permute-done((bf16[384,512]{1,0:T(8,128)(2,1)S(1)}, bf16[384,512]{1,0:T(8,128)(2,1)S(1)}, u32[]{:S(2)}, u32[]{:S(2)}) %collective-permute-start.34) | collective-permute-done | bytes 393248 | tf_op jit(solution)/shard_map/ppermute | solution.py:20
  144.5 1.3 put.7
  (59 shorter events, 4.1 us)
Async XLA Ops:
  0.7 1.4 copy-start.3
  2.1 3.7 %copy-start.7 = (bf16[96,1024]{1,0:T(8,128)(2,1)S(1)}, bf16[96,1024]{1,0:T(8,128)(2,1)}, u32[]{:S(2)}) copy-start(bf16[96,1024]{1,0:T(8,128)(2,1)} %up_ref.1) | copy-start | bytes 589828
  2.7 15.0 %collective-permute-start = (bf16[128,2048]{1,0:T(8,128)(2,1)S(1)}, bf16[128,2048]{1,0:T(8,128)(2,1)S(1)}, u32[]{:S(2)}, u32[]{:S(2)}) collective-permute-start(bf16[128,2048]{1,0:T(8,128)(2,1)S(1)} %get-tuple-element.62), channel_id=1, source_target_pairs={{0,4},{4,0},{1,5},{5,1},{2,6},{6,2},{3,7},{7,3},{8,12},{12,8},{9,1... | collective-permute-start | bytes 1572872 | tf_op jit(solution)/shard_map/ppermute | solution.py:20
  6.4 8.5 %collective-permute-start.3 = (bf16[2,96,128]{2,1,0:T(8,128)(2,1)S(1)}, bf16[2,96,128]{2,1,0:T(8,128)(2,1)S(1)}, u32[]{:S(2)}, u32[]{:S(2)}) collective-permute-start(bf16[2,96,128]{2,1,0:T(8,128)(2,1)S(1)} %get-tuple-element.67), channel_id=1, source_target_pairs={{0,1},{1,0},{2,3},{3,2},{4,5},{5,4},{6,7},{7,6},{8,9},{9,8},{10,11... | collective-permute-start | bytes 147464 | tf_op jit(solution)/shard_map/ppermute | solution.py:20
  6.5 8.4 %collective-permute-start.4 = (bf16[2,96,128]{2,1,0:T(8,128)(2,1)S(1)}, bf16[2,96,128]{2,1,0:T(8,128)(2,1)S(1)}, u32[]{:S(2)}, u32[]{:S(2)}) collective-permute-start(bf16[2,96,128]{2,1,0:T(8,128)(2,1)S(1)} %get-tuple-element.68), channel_id=1, source_target_pairs={{0,2},{1,3},{2,0},{3,1},{4,6},{5,7},{6,4},{7,5},{8,10},{9,11},{10,... | collective-permute-start | bytes 147464 | tf_op jit(solution)/shard_map/ppermute | solution.py:20
  8.0 6.9 %collective-permute-start.5 = (bf16[2,96,128]{2,1,0:T(8,128)(2,1)S(1)}, bf16[2,96,128]{2,1,0:T(8,128)(2,1)S(1)}, u32[]{:S(2)}, u32[]{:S(2)}) collective-permute-start(bf16[2,96,128]{2,1,0:T(8,128)(2,1)S(1)} %get-tuple-element.69), channel_id=1, source_target_pairs={{0,3},{1,2},{2,1},{3,0},{4,7},{5,6},{6,5},{7,4},{8,11},{9,10},{10,... | collective-permute-start | bytes 147464 | tf_op jit(solution)/shard_map/ppermute | solution.py:20
  8.3 2.8 %copy-start = (bf16[512,3,2048]{2,0,1:T(8,128)(2,1)S(1)}, bf16[512,3,2048]{2,0,1:T(8,128)(2,1)}, u32[]{:S(2)}) copy-start(bf16[512,3,2048]{2,0,1:T(8,128)(2,1)} %param.5) | copy-start | bytes 18874372
  11.1 22.4 %copy-start.1 = (bf16[512,3,2048]{2,0,1:T(8,128)(2,1)S(1)}, bf16[512,3,2048]{2,0,1:T(8,128)(2,1)}, u32[]{:S(2)}) copy-start(bf16[512,3,2048]{2,0,1:T(8,128)(2,1)} %param.5) | copy-start | bytes 18874372
  17.7 3.3 %collective-permute-start.6 = (bf16[2,3,384,128]{3,2,1,0:T(8,128)(2,1)S(1)}, bf16[2,3,384,128]{3,2,1,0:T(8,128)(2,1)S(1)}, u32[]{:S(2)}, u32[]{:S(2)}) collective-permute-start(bf16[2,3,384,128]{3,2,1,0:T(8,128)(2,1)S(1)} %get-tuple-element.70), channel_id=1, source_target_pairs={{0,1},{1,0},{2,3},{3,2},{4,5},{5,4},{6,7},{7,6},{8,9},{9,8},{10,11... | collective-permute-start | bytes 1769480 | tf_op jit(solution)/shard_map/ppermute | solution.py:20
  17.7 14.3 %collective-permute-start.2 = (bf16[128,2048]{1,0:T(8,128)(2,1)S(1)}, bf16[128,2048]{1,0:T(8,128)(2,1)S(1)}, u32[]{:S(2)}, u32[]{:S(2)}) collective-permute-start(bf16[128,2048]{1,0:T(8,128)(2,1)S(1)} %get-tuple-element.64), channel_id=1, source_target_pairs={{0,4},{4,0},{1,5},{5,1},{2,6},{6,2},{3,7},{7,3},{8,12},{12,8},{9,1... | collective-permute-start | bytes 1572872 | tf_op jit(solution)/shard_map/ppermute | solution.py:20
  19.4 14.1 %collective-permute-start.1 = (bf16[128,2048]{1,0:T(8,128)(2,1)S(1)}, bf16[128,2048]{1,0:T(8,128)(2,1)S(1)}, u32[]{:S(2)}, u32[]{:S(2)}) collective-permute-start(bf16[128,2048]{1,0:T(8,128)(2,1)S(1)} %collective-permute-done.refs_0_), channel_id=1, source_target_pairs={{0,8},{8,0},{16,24},{24,16},{1,9},{9,1},{17,25},{25,17},{2,10},{10... | collective-permute-start | bytes 1572872 | tf_op jit(solution)/shard_map/ppermute | solution.py:20
  21.1 27.6 %copy-start.8 = (f32[7,64]{1,0:T(8,128)S(1)}, f32[7,64]{1,0:T(8,128)}, u32[]{:S(2)}) copy-start(f32[7,64]{1,0:T(8,128)} %taps_ref.1) | copy-start | bytes 5380
  21.1 10.9 %collective-permute-start.7 = (bf16[1,3,384,128]{3,2,1,0:T(8,128)(2,1)S(1)}, bf16[1,3,384,128]{3,2,1,0:T(8,128)(2,1)S(1)}, u32[]{:S(2)}, u32[]{:S(2)}) collective-permute-start(bf16[1,3,384,128]{3,2,1,0:T(8,128)(2,1)S(1)} %add_convert_fusion.13), channel_id=1, source_target_pairs={{0,2},{1,3},{2,0},{3,1},{4,6},{5,7},{6,4},{7,5},{8,10},{9,11},{10,... | collective-permute-start | bytes 884744 | tf_op jit(solution)/shard_map/ppermute | solution.py:20
  37.5 12.8 %copy-start.5 = (bf16[384,2048]{1,0:T(8,128)(2,1)}, bf16[384,2048]{1,0:T(8,128)(2,1)S(1)}, u32[]{:S(2)}) copy-start(bf16[384,2048]{1,0:T(8,128)(2,1)S(1)} %get-tuple-element.96.refs_3_.refs_5_) | copy-start | bytes 4718596
  37.5 2.1 %collective-permute-start.8 = (bf16[2,3,384,128]{3,2,1,0:T(8,128)(2,1)S(1)}, bf16[2,3,384,128]{3,2,1,0:T(8,128)(2,1)S(1)}, u32[]{:S(2)}, u32[]{:S(2)}) collective-permute-start(bf16[2,3,384,128]{3,2,1,0:T(8,128)(2,1)S(1)} %get-tuple-element.73), channel_id=1, source_target_pairs={{0,1},{1,0},{2,3},{3,2},{4,5},{5,4},{6,7},{7,6},{8,9},{9,8},{10,11... | collective-permute-start | bytes 1769480 | tf_op jit(solution)/shard_map/ppermute | solution.py:20
  39.6 9.1 %collective-permute-start.10 = (bf16[1,3,384,128]{3,2,1,0:T(8,128)(2,1)S(1)}, bf16[1,3,384,128]{3,2,1,0:T(8,128)(2,1)S(1)}, u32[]{:S(2)}, u32[]{:S(2)}) collective-permute-start(bf16[1,3,384,128]{3,2,1,0:T(8,128)(2,1)S(1)} %add_convert_fusion.12), channel_id=1, source_target_pairs={{0,2},{1,3},{2,0},{3,1},{4,6},{5,7},{6,4},{7,5},{8,10},{9,11},{10,... | collective-permute-start | bytes 884744 | tf_op jit(solution)/shard_map/ppermute | solution.py:20
  41.8 4.7 %collective-permute-start.9 = (bf16[384,128]{1,0:T(8,128)(2,1)S(1)}, bf16[384,128]{1,0:T(8,128)(2,1)S(1)}, u32[]{:S(2)}, u32[]{:S(2)}) collective-permute-start(bf16[384,128]{1,0:T(8,128)(2,1)S(1)} %get-tuple-element.76), channel_id=1, source_target_pairs={{0,4},{4,0},{1,5},{5,1},{2,6},{6,2},{3,7},{7,3},{8,12},{12,8},{9,1... | collective-permute-start | bytes 294920 | tf_op jit(solution)/shard_map/ppermute | solution.py:20
  50.3 7.0 %collective-permute-start.11 = (bf16[3,384,128]{2,1,0:T(8,128)(2,1)S(1)}, bf16[3,384,128]{2,1,0:T(8,128)(2,1)S(1)}, u32[]{:S(2)}, u32[]{:S(2)}) collective-permute-start(bf16[3,384,128]{2,1,0:T(8,128)(2,1)S(1)} %get-tuple-element.81.refs_0_), channel_id=1, source_target_pairs={{0,1},{1,0},{2,3},{3,2},{4,5},{5,4},{6,7},{7,6},{8,9},{9,8},{10,11... | collective-permute-start | bytes 884744 | tf_op jit(solution)/shard_map/ppermute | solution.py:20
  50.4 9.4 %collective-permute-start.12 = (bf16[3,384,128]{2,1,0:T(8,128)(2,1)S(1)}, bf16[3,384,128]{2,1,0:T(8,128)(2,1)S(1)}, u32[]{:S(2)}, u32[]{:S(2)}) collective-permute-start(bf16[3,384,128]{2,1,0:T(8,128)(2,1)S(1)} %get-tuple-element.78.refs_0_), channel_id=1, source_target_pairs={{0,2},{1,3},{2,0},{3,1},{4,6},{5,7},{6,4},{7,5},{8,10},{9,11},{10,... | collective-permute-start | bytes 884744 | tf_op jit(solution)/shard_map/ppermute | solution.py:20
  52.0 7.9 %collective-permute-start.13 = (bf16[3,384,128]{2,1,0:T(8,128)(2,1)S(1)}, bf16[3,384,128]{2,1,0:T(8,128)(2,1)S(1)}, u32[]{:S(2)}, u32[]{:S(2)}) collective-permute-start(bf16[3,384,128]{2,1,0:T(8,128)(2,1)S(1)} %get-tuple-element.78.refs_0_), channel_id=1, source_target_pairs={{0,1},{1,0},{2,3},{3,2},{4,5},{5,4},{6,7},{7,6},{8,9},{9,8},{10,11... | collective-permute-start | bytes 884744 | tf_op jit(solution)/shard_map/ppermute | solution.py:20
  52.1 5.2 %collective-permute-start.14 = (bf16[416,128]{1,0:T(8,128)(2,1)S(1)}, bf16[416,128]{1,0:T(8,128)(2,1)S(1)}, u32[]{:S(2)}, u32[]{:S(2)}) collective-permute-start(bf16[416,128]{1,0:T(8,128)(2,1)S(1)} %get-tuple-element.79), channel_id=1, source_target_pairs={{0,4},{4,0},{1,5},{5,1},{2,6},{6,2},{3,7},{7,3},{8,12},{12,8},{9,1... | collective-permute-start | bytes 319496 | tf_op jit(solution)/shard_map/ppermute | solution.py:20
  59.8 1.6 %collective-permute-start.15 = (bf16[3,384,128]{2,1,0:T(8,128)(2,1)S(1)}, bf16[3,384,128]{2,1,0:T(8,128)(2,1)S(1)}, u32[]{:S(2)}, u32[]{:S(2)}) collective-permute-start(bf16[3,384,128]{2,1,0:T(8,128)(2,1)S(1)} %collective-permute-done.12.refs_2_), channel_id=1, source_target_pairs={{0,1},{1,0},{2,3},{3,2},{4,5},{5,4},{6,7},{7,6},{8,9},{9,8},{10,11... | collective-permute-start | bytes 884744 | tf_op jit(solution)/shard_map/ppermute | solution.py:20
  61.4 9.1 %collective-permute-start.16 = (bf16[3,384,128]{2,1,0:T(8,128)(2,1)S(1)}, bf16[3,384,128]{2,1,0:T(8,128)(2,1)S(1)}, u32[]{:S(2)}, u32[]{:S(2)}) collective-permute-start(bf16[3,384,128]{2,1,0:T(8,128)(2,1)S(1)} %get-tuple-element.81.refs_0_), channel_id=1, source_target_pairs={{0,2},{1,3},{2,0},{3,1},{4,6},{5,7},{6,4},{7,5},{8,10},{9,11},{10,... | collective-permute-start | bytes 884744 | tf_op jit(solution)/shard_map/ppermute | solution.py:20
  64.4 12.1 %collective-permute-start.18 = (bf16[384,512]{1,0:T(8,128)(2,1)S(1)}, bf16[384,512]{1,0:T(8,128)(2,1)S(1)}, u32[]{:S(2)}, u32[]{:S(2)}) collective-permute-start(bf16[384,512]{1,0:T(8,128)(2,1)S(1)} %input_grad.4), channel_id=1, source_target_pairs={{0,4},{4,0},{1,5},{5,1},{2,6},{6,2},{3,7},{7,3},{8,12},{12,8},{9,1... | collective-permute-start | bytes 1179656 | tf_op jit(solution)/shard_map/ppermute | solution.py:20
  70.5 1.6 %collective-permute-start.17 = (bf16[3,384,128]{2,1,0:T(8,128)(2,1)S(1)}, bf16[3,384,128]{2,1,0:T(8,128)(2,1)S(1)}, u32[]{:S(2)}, u32[]{:S(2)}) collective-permute-start(bf16[3,384,128]{2,1,0:T(8,128)(2,1)S(1)} %collective-permute-done.16.refs_2_), channel_id=1, source_target_pairs={{0,1},{1,0},{2,3},{3,2},{4,5},{5,4},{6,7},{7,6},{8,9},{9,8},{10,11... | collective-permute-start | bytes 884744 | tf_op jit(solution)/shard_map/ppermute | solution.py:20
  70.5 14.6 %collective-permute-start.19 = (bf16[384,512]{1,0:T(8,128)(2,1)}, bf16[384,512]{1,0:T(8,128)(2,1)}, u32[]{:S(2)}, u32[]{:S(2)}) collective-permute-start(bf16[384,512]{1,0:T(8,128)(2,1)} %get-tuple-element.87), channel_id=1, source_target_pairs={{0,4},{4,0},{1,5},{5,1},{2,6},{6,2},{3,7},{7,3},{8,12},{12,8},{9,1... | collective-permute-start | bytes 1179656 | tf_op jit(solution)/shard_map/ppermute | solution.py:20
  77.4 10.4 %collective-permute-start.20 = (bf16[384,512]{1,0:T(8,128)(2,1)}, bf16[384,512]{1,0:T(8,128)(2,1)}, u32[]{:S(2)}, u32[]{:S(2)}) collective-permute-start(bf16[384,512]{1,0:T(8,128)(2,1)} %add_convert_fusion.11), channel_id=1, source_target_pairs={{0,8},{8,0},{16,24},{24,16},{1,9},{9,1},{17,25},{25,17},{2,10},{10... | collective-permute-start | bytes 1179656 | tf_op jit(solution)/shard_map/ppermute | solution.py:20
  78.9 13.3 %collective-permute-start.21 = (bf16[384,512]{1,0:T(8,128)(2,1)S(1)}, bf16[384,512]{1,0:T(8,128)(2,1)S(1)}, u32[]{:S(2)}, u32[]{:S(2)}) collective-permute-start(bf16[384,512]{1,0:T(8,128)(2,1)S(1)} %get-tuple-element.91), channel_id=1, source_target_pairs={{0,4},{4,0},{1,5},{5,1},{2,6},{6,2},{3,7},{7,3},{8,12},{12,8},{9,1... | collective-permute-start | bytes 1179656 | tf_op jit(solution)/shard_map/ppermute | solution.py:20
  79.4 2.8 %copy-start.2 = (bf16[512,3,2048]{2,0,1:T(8,128)(2,1)S(1)}, bf16[512,3,2048]{2,0,1:T(8,128)(2,1)}, u32[]{:S(2)}) copy-start(bf16[512,3,2048]{2,0,1:T(8,128)(2,1)} %param.5) | copy-start | bytes 18874372
  86.2 8.9 %collective-permute-start.22 = (bf16[384,512]{1,0:T(8,128)(2,1)S(1)}, bf16[384,512]{1,0:T(8,128)(2,1)S(1)}, u32[]{:S(2)}, u32[]{:S(2)}) collective-permute-start(bf16[384,512]{1,0:T(8,128)(2,1)S(1)} %add_convert_fusion.10), channel_id=1, source_target_pairs={{0,8},{8,0},{16,24},{24,16},{1,9},{9,1},{17,25},{25,17},{2,10},{10... | collective-permute-start | bytes 1179656 | tf_op jit(solution)/shard_map/ppermute | solution.py:20
  89.0 7.3 %collective-permute-start.23 = (bf16[384,512]{1,0:T(8,128)(2,1)S(1)}, bf16[384,512]{1,0:T(8,128)(2,1)S(1)}, u32[]{:S(2)}, u32[]{:S(2)}) collective-permute-start(bf16[384,512]{1,0:T(8,128)(2,1)S(1)} %add_convert_fusion.9), channel_id=1, source_target_pairs={{0,0},{8,16},{16,8},{24,24},{1,1},{9,17},{17,9},{25,25},{2,2},{10,... | collective-permute-start | bytes 1179656 | tf_op jit(solution)/shard_map/ppermute | solution.py:620
  92.3 10.8 %copy-start.4 = (bf16[384,2048]{1,0:T(8,128)(2,1)S(1)}, bf16[384,2048]{1,0:T(8,128)(2,1)}, u32[]{:S(2)}) copy-start(bf16[384,2048]{1,0:T(8,128)(2,1)} %refs_4_.1) | copy-start | bytes 4718596
  92.3 10.8 %copy-start.6 = (bf16[384,2048]{1,0:T(8,128)(2,1)S(1)}, bf16[384,2048]{1,0:T(8,128)(2,1)}, u32[]{:S(2)}) copy-start(bf16[384,2048]{1,0:T(8,128)(2,1)} %copy-done.5) | copy-start | bytes 4718596
  95.2 8.0 %collective-permute-start.24 = (bf16[384,512]{1,0:T(8,128)(2,1)S(1)}, bf16[384,512]{1,0:T(8,128)(2,1)S(1)}, u32[]{:S(2)}, u32[]{:S(2)}) collective-permute-start(bf16[384,512]{1,0:T(8,128)(2,1)S(1)} %get-tuple-element.94), channel_id=1, source_target_pairs={{0,4},{4,0},{1,5},{5,1},{2,6},{6,2},{3,7},{7,3},{8,12},{12,8},{9,1... | collective-permute-start | bytes 1179656 | tf_op jit(solution)/shard_map/ppermute | solution.py:20
  96.5 12.4 %collective-permute-start.25 = (bf16[384,512]{1,0:T(8,128)(2,1)S(1)}, bf16[384,512]{1,0:T(8,128)(2,1)S(1)}, u32[]{:S(2)}, u32[]{:S(2)}) collective-permute-start(bf16[384,512]{1,0:T(8,128)(2,1)S(1)} %get-tuple-element.120), channel_id=1, source_target_pairs={{0,8},{8,0},{16,24},{24,16},{1,9},{9,1},{17,25},{25,17},{2,10},{10... | collective-permute-start | bytes 1179656 | tf_op jit(solution)/shard_map/ppermute | solution.py:20
  101.1 7.8 %collective-permute-start.26 = (bf16[384,512]{1,0:T(8,128)(2,1)S(1)}, bf16[384,512]{1,0:T(8,128)(2,1)S(1)}, u32[]{:S(2)}, u32[]{:S(2)}) collective-permute-start(bf16[384,512]{1,0:T(8,128)(2,1)S(1)} %add_convert_fusion.7), channel_id=1, source_target_pairs={{0,0},{8,16},{16,8},{24,24},{1,1},{9,17},{17,9},{25,25},{2,2},{10,... | collective-permute-start | bytes 1179656 | tf_op jit(solution)/shard_map/ppermute | solution.py:620
  109.2 8.4 %collective-permute-start.27 = (bf16[384,512]{1,0:T(8,128)(2,1)S(1)}, bf16[384,512]{1,0:T(8,128)(2,1)S(1)}, u32[]{:S(2)}, u32[]{:S(2)}) collective-permute-start(bf16[384,512]{1,0:T(8,128)(2,1)S(1)} %get-tuple-element.118), channel_id=1, source_target_pairs={{0,8},{8,0},{16,24},{24,16},{1,9},{9,1},{17,25},{25,17},{2,10},{10... | collective-permute-start | bytes 1179656 | tf_op jit(solution)/shard_map/ppermute | solution.py:20
  111.2 7.1 %collective-permute-start.28 = (bf16[384,512]{1,0:T(8,128)(2,1)S(1)}, bf16[384,512]{1,0:T(8,128)(2,1)S(1)}, u32[]{:S(2)}, u32[]{:S(2)}) collective-permute-start(bf16[384,512]{1,0:T(8,128)(2,1)S(1)} %add_convert_fusion.4), channel_id=1, source_target_pairs={{0,0},{8,16},{16,8},{24,24},{1,1},{9,17},{17,9},{25,25},{2,2},{10,... | collective-permute-start | bytes 1179656 | tf_op jit(solution)/shard_map/ppermute | solution.py:620
  117.6 9.0 %collective-permute-start.32 = (bf16[384,512]{1,0:T(8,128)(2,1)S(1)}, bf16[384,512]{1,0:T(8,128)(2,1)S(1)}, u32[]{:S(2)}, u32[]{:S(2)}) collective-permute-start(bf16[384,512]{1,0:T(8,128)(2,1)S(1)} %add_convert_fusion.2), channel_id=1, source_target_pairs={{0,0},{8,16},{16,8},{24,24},{1,1},{9,17},{17,9},{25,25},{2,2},{10,... | collective-permute-start | bytes 1179656 | tf_op jit(solution)/shard_map/ppermute | solution.py:620
  119.0 7.6 %collective-permute-start.29 = (bf16[2,128,128]{2,1,0:T(8,128)(2,1)S(1)}, bf16[2,128,128]{2,1,0:T(8,128)(2,1)S(1)}, u32[]{:S(2)}, u32[]{:S(2)}) collective-permute-start(bf16[2,128,128]{2,1,0:T(8,128)(2,1)S(1)} %get-tuple-element.110), channel_id=1, source_target_pairs={{0,1},{1,0},{2,3},{3,2},{4,5},{5,4},{6,7},{7,6},{8,9},{9,8},{10,11... | collective-permute-start | bytes 196616 | tf_op jit(solution)/shard_map/ppermute | solution.py:20
  119.1 7.6 %collective-permute-start.30 = (bf16[2,128,128]{2,1,0:T(8,128)(2,1)S(1)}, bf16[2,128,128]{2,1,0:T(8,128)(2,1)S(1)}, u32[]{:S(2)}, u32[]{:S(2)}) collective-permute-start(bf16[2,128,128]{2,1,0:T(8,128)(2,1)S(1)} %get-tuple-element.111), channel_id=1, source_target_pairs={{0,2},{1,3},{2,0},{3,1},{4,6},{5,7},{6,4},{7,5},{8,10},{9,11},{10,... | collective-permute-start | bytes 196616 | tf_op jit(solution)/shard_map/ppermute | solution.py:20
  121.3 5.4 %collective-permute-start.31 = (bf16[2,128,128]{2,1,0:T(8,128)(2,1)S(1)}, bf16[2,128,128]{2,1,0:T(8,128)(2,1)S(1)}, u32[]{:S(2)}, u32[]{:S(2)}) collective-permute-start(bf16[2,128,128]{2,1,0:T(8,128)(2,1)S(1)} %get-tuple-element.112), channel_id=1, source_target_pairs={{0,3},{1,2},{2,1},{3,0},{4,7},{5,6},{6,5},{7,4},{8,11},{9,10},{10,... | collective-permute-start | bytes 196616 | tf_op jit(solution)/shard_map/ppermute | solution.py:20
  121.3 15.2 %collective-permute-start.33 = (bf16[384,512]{1,0:T(8,128)(2,1)S(1)}, bf16[384,512]{1,0:T(8,128)(2,1)S(1)}, u32[]{:S(2)}, u32[]{:S(2)}) collective-permute-start(bf16[384,512]{1,0:T(8,128)(2,1)S(1)} %add_convert_fusion.1.refs_2_), channel_id=1, source_target_pairs={{0,8},{8,0},{16,24},{24,16},{1,9},{9,1},{17,25},{25,17},{2,10},{10... | collective-permute-start | bytes 1179656 | tf_op jit(solution)/shard_map/ppermute | solution.py:20
  126.8 17.7 %collective-permute-start.34 = (bf16[384,512]{1,0:T(8,128)(2,1)S(1)}, bf16[384,512]{1,0:T(8,128)(2,1)S(1)}, u32[]{:S(2)}, u32[]{:S(2)}) collective-permute-start(bf16[384,512]{1,0:T(8,128)(2,1)S(1)} %add_convert_fusion.refs_2_), channel_id=1, source_target_pairs={{0,8},{8,0},{16,24},{24,16},{1,9},{9,1},{17,25},{25,17},{2,10},{10... | collective-permute-start | bytes 1179656 | tf_op jit(solution)/shard_map/ppermute | solution.py:20

commit v10 on v9

--- a/solution.py
+++ b/solution.py
@@ -362,16 +362,27 @@
     )(place, *grads)
 
 
-def input_grad_kernel(grad_ref, w_ref, *out_refs, first):
+def input_grad_kernel(grad_ref, w_ref, out_ref, *, first):
+    step = out_ref.shape[1]
+    rows = w_ref[:, :, first * step : (first + 1) * step].reshape(-1, step)
+    out_ref[...] = jnp.dot(grad_ref[...], rows, preferred_element_type=jnp.float32).astype(jnp.bfloat16)
+
+
+def input_grads_kernel(grad_ref, w_ref, *refs, first):
+    out_refs, (slots, sems) = refs[:-2], refs[-2:]
     step = out_refs[0].shape[1]
-    own = slice(first * step, (first + 1) * step) if len(out_refs) == 1 else slice(None)
-    acc = jnp.dot(grad_ref[...], w_ref[:, :, own].reshape(-1, step), preferred_element_type=jnp.float32)
-    acc = acc.astype(jnp.bfloat16)
+
+    def fetch(i):
+        columns = pl.ds((first + i) * step, step)
+        return pltpu.make_async_copy(w_ref.at[:, :, columns], slots.at[i % 2], sems.at[i % 2])
+
+    fetch(0).start()
     for i, out_ref in enumerate(out_refs):
-
-        @pl.when(pl.program_id(0) == i)
-        def _():
-            out_ref[...] = acc
+        if i + 1 < len(out_refs):
+            fetch(i + 1).start()
+        fetch(i).wait()
+        rows = slots[i % 2].reshape(-1, step)
+        out_ref[...] = jnp.dot(grad_ref[...], rows, preferred_element_type=jnp.float32).astype(jnp.bfloat16)
 
 
 def input_grad(grad, w, first, last, chunks, width):
@@ -383,19 +394,20 @@
         rows = w[:, :, first * step : last * step].reshape(streams * channels, count * step)
         whole = jnp.dot(grad, rows, preferred_element_type=jnp.float32).astype(jnp.bfloat16)
         return [whole[:, i * step : (i + 1) * step] for i in range(count)]
+    single = count == 1
     return list(
         pl.pallas_call(
-            functools.partial(input_grad_kernel, first=first),
-            grid=(count,),
+            functools.partial(input_grad_kernel if single else input_grads_kernel, first=first),
             in_specs=[
                 resident(grad.shape, width),
-                resident(w.shape, width)
-                if count == 1
-                else pl.BlockSpec((streams, channels, step), lambda i: (0, 0, first + i)),
+                pl.BlockSpec(memory_space=pltpu.VMEM if single else pltpu.HBM),
             ],
             out_specs=[resident((tok, step), width)] * count,
             out_shape=[jax.ShapeDtypeStruct((tok, step), jnp.bfloat16)] * count,
-            compiler_params=params(12, width),
+            scratch_shapes=[]
+            if single
+            else [pltpu.VMEM((2, streams, channels, step), jnp.bfloat16), pltpu.SemaphoreType.DMA((2,))],
+            compiler_params=params(8, width),
             cost_estimate=SMALL,
             name="input_grad",
         )(grad, w)
@@ -494,38 +506,6 @@
         cost_estimate=SMALL,
         name="cut",
     )(place, tokens, tokens)
-
-
-def put_kernel(place, *refs):
-    pair_ref, summed_ref, out_ref = refs[-3:]
-    outer = (place[2] == 0) | (place[2] == 3)
-
-    @pl.when(outer)
-    def _():
-        out_ref[...] = pair_ref[...]
-
-    @pl.when(jnp.logical_not(outer))
-    def _():
-        out_ref[...] = summed_ref[...]
-
-
-def put(place, filled, pair, summed, chunk, feat):
-    tok, step = pair.shape
-    chained = filled is not None
-    return pl.pallas_call(
-        put_kernel,
-        grid_spec=pltpu.PrefetchScalarGridSpec(
-            num_scalar_prefetch=1,
-            grid=(1,),
-            in_specs=[pl.BlockSpec(memory_space=pl.ANY)] * chained + [resident((tok, step), LANES)] * 2,
-            out_specs=pl.BlockSpec((tok, step), lambda i, _: (0, chunk)),
-        ),
-        out_shape=jax.ShapeDtypeStruct((tok, feat), jnp.bfloat16),
-        input_output_aliases={1: 0} if chained else {},
-        compiler_params=params(6, LANES),
-        cost_estimate=SMALL,
-        name="put",
-    )(place, *([filled] if chained else []), pair, summed)
 
 
 def on_device(tokens, weight, taps, upstream):
@@ -592,7 +572,7 @@
     outer = (row_at == 0) | (row_at == 3)
     line = lax.axis_size("row") == 4
     inward, across, summed, done = ([None] * chunks for _ in range(4))
-    pair = cross = filled = grad_tokens = None
+    pair = cross = filled = None
     marks = []
     for slot in range(chunks + 3):
         if slot < chunks:
@@ -612,7 +592,7 @@
                 summed[slot - 2] = added(after(across[slot - 2], *marks), cross)
                 marks = [summed[slot - 2]]
             if 0 <= slot - 3 < chunks:
-                grad_tokens = put(place, grad_tokens, pair, summed[slot - 3], slot - 3, tokens.shape[1])
+                done[slot - 3] = jnp.where(outer, pair, summed[slot - 3])
             if slot < chunks + 2:
                 out = summed[slot - 2] if slot >= 2 else inward[slot]
                 pair = swap(jnp.where(outer, inward[slot], out) if slot < chunks else out, "row", 1)
@@ -621,20 +601,15 @@
         if slot == 0:
             own_part += input_grad(after(lhs[0], *marks), w, 1, chunks, chunks, width)
             marks = [own_part[1]]
-        if slot == 1:
             for k, parts_of in enumerate(held):
                 sent[k] += [swap(after(part, *marks), "col", k + 1) for part in parts_of]
-        if slot == 2:
-            marks += [of[-1] for of in sent]
         if slot in (2, 3):
             filled = weight_grad(filled, [after(lhs[0], *marks)] + lhs[1:], xs, slot - 2, 3, width)
             marks = [filled[1]]
-        if slot == chunks:
+        if slot == chunks + 1:
             blocks = split_rows(place, [after(blocks[0], *marks)] + blocks[1:], n_depth)
             blocks = [block if r == 0 else swap(block, "depth", r) for r, block in enumerate(blocks)]
-            marks += blocks[1:]
-    if not line:
-        grad_tokens = jnp.concatenate(done, axis=1)
+    grad_tokens = jnp.concatenate(done, axis=1)
     output, grad_taps = join(place, filled[1], [after(blocks[0], *marks)] + blocks[1:], taps.shape[1])
     grad_weight = jnp.transpose(filled[0], (1, 0, 2))
     return (output, grad_tokens, grad_weight, grad_taps)

time: 146 us -> 140 us (0.959)
  Pallas kernels: 38.9 us -> 33.3 us
  waiting for transfers between devices: 51.2 us -> 45.7 us
  starting transfers between devices: 43.3 us -> 46.9 us
  other arithmetic: 4.41 us -> 6.08 us
    pallas_call x8 -> x4, Pallas kernels: 13.3 us -> 7.63 us  [input_grad(): pl.pallas_call(functools.partial(input_grad_kernel if single else input_g...]
    ppermute x31, waiting for transfers between devices: 51.2 us -> 45.7 us  [swap(): return lax.ppermute(value, axis, [(i, i ^ flip) for i in range(count)])]
    ppermute x31, starting transfers between devices: 40.6 us -> 44.1 us  [swap(): return lax.ppermute(value, axis, [(i, i ^ flip) for i in range(count)])]
  transfers between devices with their start and end apart: 35 -> 35, of which waited for: 17 -> 16; matrix products, arithmetic and copies ran while one was open for 3% -> 3% of each run, Pallas kernels for 22% -> 19%
where the time goes in v10:
time: 140 us
  starting transfers between devices  46.9 us (34%)
  waiting for transfers between devices  45.7 us (33%)
  Pallas kernels  33.3 us (24%)
  local copies, waits for them, and re-layouts  7.01 us (5%)
  other arithmetic  6.08 us (4%)
    ppermute x31, waiting for transfers between devices, swap(): return lax.ppermute(value, axis, [(i, i ^ flip) for i in range(count)])  45.7 us
    ppermute x31, starting transfers between devices, swap(): return lax.ppermute(value, axis, [(i, i ^ flip) for i in range(count)])  44.1 us
    pallas_call x2, Pallas kernels, weight_grad(): pl.pallas_call(functools.partial(weight_grad_kernel, chained=chained, gro...  11.3 us
    pallas_call x2, Pallas kernels, project(): pl.pallas_call(functools.partial(project_kernel, pieces=len(xs), count=co...  7.67 us
    pallas_call x4, Pallas kernels, input_grad(): pl.pallas_call(functools.partial(input_grad_kernel if single else input_g...  7.63 us
    unnamed x18, local copies, waits for them, and re-layouts  7.01 us
  transfers between devices with their start and end apart: 35, of which 16 were waited for; matrix products, arithmetic and copies ran while one was open for 3% of the time, Pallas kernels for 19%

profile of v10, /device:TPU:0, one launch (start us, length us, event | category | flops | bytes accessed | tf_op | source)
XLA Modules:
  0.0 140.0 jit_solution(17355715728989997964)
XLA Ops:
  0.7 1.4 %copy-done.3 = bf16[384,2048]{1,0:T(8,128)(2,1)S(1)} copy-done((bf16[384,2048]{1,0:T(8,128)(2,1)S(1)}, bf16[384,2048]{1,0:T(8,128)(2,1)}, u32[]{:S(2)}) %copy-start.3) | copy-done | bytes 1572888
  2.1 0.6 cut.1
  2.7 3.0 %collective-permute-start = (bf16[128,2048]{1,0:T(8,128)(2,1)S(1)}, bf16[128,2048]{1,0:T(8,128)(2,1)S(1)}, u32[]{:S(2)}, u32[]{:S(2)}) collective-permute-start(bf16[128,2048]{1,0:T(8,128)(2,1)S(1)} %get-tuple-element.63), channel_id=1, source_target_pairs={{0,4},{4,0},{1,5},{5,1},{2,6},{6,2},{3,7},{7,3},{8,12},{12,8},{9,1... | collective-permute-start | bytes 1572872 | tf_op jit(solution)/shard_map/ppermute | solution.py:20
  5.8 0.6 split.2
  6.5 1.6 %collective-permute-start.4 = (bf16[2,96,128]{2,1,0:T(8,128)(2,1)S(1)}, bf16[2,96,128]{2,1,0:T(8,128)(2,1)S(1)}, u32[]{:S(2)}, u32[]{:S(2)}) collective-permute-start(bf16[2,96,128]{2,1,0:T(8,128)(2,1)S(1)} %get-tuple-element.69), channel_id=1, source_target_pairs={{0,2},{1,3},{2,0},{3,1},{4,6},{5,7},{6,4},{7,5},{8,10},{9,11},{10,... | collective-permute-start | bytes 147464 | tf_op jit(solution)/shard_map/ppermute | solution.py:20
  8.3 2.8 %copy-done = bf16[512,3,2048]{2,0,1:T(8,128)(2,1)S(1)} copy-done((bf16[512,3,2048]{2,0,1:T(8,128)(2,1)S(1)}, bf16[512,3,2048]{2,0,1:T(8,128)(2,1)}, u32[]{:S(2)}) %copy-start) | copy-done | bytes 6291480
  11.1 3.8 %project.2 = (bf16[2,3,384,128]{3,2,1,0:T(8,128)(2,1)S(1)}, bf16[2,3,384,128]{3,2,1,0:T(8,128)(2,1)S(1)}) custom-call(s32[4]{0:T(128)S(1)} %pad_add_fusion.place._, bf16[384,2048]{1,0:T(8,128)(2,1)S(1)} %copy-done.3, bf16[3,512,2048]{2,1,0:T(8,128)(2,1)S(1)} %bitcast.6), custom_call_target="tpu_custom_call" | custom-call | flops 1 | bytes 1 | tf_op jit(solution)/shard_map/project/pallas_call | solution.py:87
  14.9 2.8 %collective-permute-done.refs_0_ = bf16[128,2048]{1,0:T(8,128)(2,1)S(1)} collective-permute-done((bf16[128,2048]{1,0:T(8,128)(2,1)S(1)}, bf16[128,2048]{1,0:T(8,128)(2,1)S(1)}, u32[]{:S(2)}, u32[]{:S(2)}) %collective-permute-start) | collective-permute-done | bytes 524320 | tf_op jit(solution)/shard_map/ppermute | solution.py:20
  17.7 1.7 %collective-permute-start.2 = (bf16[128,2048]{1,0:T(8,128)(2,1)S(1)}, bf16[128,2048]{1,0:T(8,128)(2,1)S(1)}, u32[]{:S(2)}, u32[]{:S(2)}) collective-permute-start(bf16[128,2048]{1,0:T(8,128)(2,1)S(1)} %get-tuple-element.65), channel_id=1, source_target_pairs={{0,4},{4,0},{1,5},{5,1},{2,6},{6,2},{3,7},{7,3},{8,12},{12,8},{9,1... | collective-permute-start | bytes 1572872 | tf_op jit(solution)/shard_map/ppermute | solution.py:20
  19.4 1.6 %collective-permute-start.1 = (bf16[128,2048]{1,0:T(8,128)(2,1)S(1)}, bf16[128,2048]{1,0:T(8,128)(2,1)S(1)}, u32[]{:S(2)}, u32[]{:S(2)}) collective-permute-start(bf16[128,2048]{1,0:T(8,128)(2,1)S(1)} %collective-permute-done.refs_0_), channel_id=1, source_target_pairs={{0,8},{8,0},{16,24},{24,16},{1,9},{9,1},{17,25},{25,17},{2,10},{10... | collective-permute-start | bytes 1572872 | tf_op jit(solution)/shard_map/ppermute | solution.py:20
  21.1 1.6 %collective-permute-start.7 = (bf16[1,3,384,128]{3,2,1,0:T(8,128)(2,1)S(1)}, bf16[1,3,384,128]{3,2,1,0:T(8,128)(2,1)S(1)}, u32[]{:S(2)}, u32[]{:S(2)}) collective-permute-start(bf16[1,3,384,128]{3,2,1,0:T(8,128)(2,1)S(1)} %add_convert_fusion.13), channel_id=1, source_target_pairs={{0,2},{1,3},{2,0},{3,1},{4,6},{5,7},{6,4},{7,5},{8,10},{9,11},{10,... | collective-permute-start | bytes 884744 | tf_op jit(solution)/shard_map/ppermute | solution.py:20
  22.7 9.4 %collective-permute-done.2.refs_2_ = bf16[128,2048]{1,0:T(8,128)(2,1)S(1)} collective-permute-done((bf16[128,2048]{1,0:T(8,128)(2,1)S(1)}, bf16[128,2048]{1,0:T(8,128)(2,1)S(1)}, u32[]{:S(2)}, u32[]{:S(2)}) %collective-permute-start.2) | collective-permute-done | bytes 524320 | tf_op jit(solution)/shard_map/ppermute | solution.py:20
  32.0 1.5 %collective-permute-done.1.refs_1_ = bf16[128,2048]{1,0:T(8,128)(2,1)S(1)} collective-permute-done((bf16[128,2048]{1,0:T(8,128)(2,1)S(1)}, bf16[128,2048]{1,0:T(8,128)(2,1)S(1)}, u32[]{:S(2)}, u32[]{:S(2)}) %collective-permute-start.1) | collective-permute-done | bytes 524320 | tf_op jit(solution)/shard_map/ppermute | solution.py:20
  33.5 3.9 %project.3 = (bf16[2,3,384,128]{3,2,1,0:T(8,128)(2,1)S(1)}, bf16[2,3,384,128]{3,2,1,0:T(8,128)(2,1)S(1)}, bf16[384,2048]{1,0:T(8,128)(2,1)S(1)}) custom-call(s32[4]{0:T(128)S(1)} %pad_add_fusion.place._, bf16[128,2048]{1,0:T(8,128)(2,1)S(1)} %collective-permute-done.refs_0_, bf16[128,2048]{1,0:T(8,128)(2,1)S(1)} %collective-permute-done.1.refs_1_, ...), custom_call_target="tpu_custom_call" | custom-call | flops 1 | bytes 1 | tf_op jit(solution)/shard_map/project/pallas_call | solution.py:87
  37.5 2.0 %collective-permute-done.8.refs_6_ = bf16[2,3,384,128]{3,2,1,0:T(8,128)(2,1)S(1)} collective-permute-done((bf16[2,3,384,128]{3,2,1,0:T(8,128)(2,1)S(1)}, bf16[2,3,384,128]{3,2,1,0:T(8,128)(2,1)S(1)}, u32[]{:S(2)}, u32[]{:S(2)}) %collective-permute-start.8) | collective-permute-done | bytes 589856 | tf_op jit(solution)/shard_map/ppermute | solution.py:20
  39.6 1.6 %collective-permute-start.10 = (bf16[1,3,384,128]{3,2,1,0:T(8,128)(2,1)S(1)}, bf16[1,3,384,128]{3,2,1,0:T(8,128)(2,1)S(1)}, u32[]{:S(2)}, u32[]{:S(2)}) collective-permute-start(bf16[1,3,384,128]{3,2,1,0:T(8,128)(2,1)S(1)} %add_convert_fusion.12), channel_id=1, source_target_pairs={{0,2},{1,3},{2,0},{3,1},{4,6},{5,7},{6,4},{7,5},{8,10},{9,11},{10,... | collective-permute-start | bytes 884744 | tf_op jit(solution)/shard_map/ppermute | solution.py:20
  41.1 0.6 merge.1
  41.7 0.6 collective-permute-start.9
  42.3 4.1 %collective-permute-done.9.refs_1_ = bf16[384,128]{1,0:T(8,128)(2,1)S(1)} collective-permute-done((bf16[384,128]{1,0:T(8,128)(2,1)S(1)}, bf16[384,128]{1,0:T(8,128)(2,1)S(1)}, u32[]{:S(2)}, u32[]{:S(2)}) %collective-permute-start.9) | collective-permute-done | bytes 98336 | tf_op jit(solution)/shard_map/ppermute | solution.py:20
  46.4 2.3 %collective-permute-done.10.refs_7_ = bf16[1,3,384,128]{3,2,1,0:T(8,128)(2,1)S(1)} collective-permute-done((bf16[1,3,384,128]{3,2,1,0:T(8,128)(2,1)S(1)}, bf16[1,3,384,128]{3,2,1,0:T(8,128)(2,1)S(1)}, u32[]{:S(2)}, u32[]{:S(2)}) %collective-permute-start.10) | collective-permute-done | bytes 294944 | tf_op jit(solution)/shard_map/ppermute | solution.py:20
  48.7 1.6 %middle.1 = (bf16[3,384,128]{2,1,0:T(8,128)(2,1)S(1)}, bf16[3,384,128]{2,1,0:T(8,128)(2,1)S(1)}, bf16[416,128]{1,0:T(8,128)(2,1)S(1)}, bf16[416,128]{1,0:T(8,128)(2,1)S(1)}) custom-call(s32[4]{0:T(128)S(1)} %pad_add_fusion.place._, f32[7,64]{1,0:T(8,128)S(1)} %copy-done.8, bf16[384,128]{1,0:T(8,128)(2,1)S(1)} %get-tuple-element.76.refs_0_, ...), custom_call_target="tpu_custom_call" | custom-call | flops 1 | bytes 1 | tf_op jit(solution)/shard_map/middle/pallas_call | solution.py:311
  50.3 0.5 collective-permute-start.13
  50.8 1.5 %collective-permute-start.12 = (bf16[3,384,128]{2,1,0:T(8,128)(2,1)S(1)}, bf16[3,384,128]{2,1,0:T(8,128)(2,1)S(1)}, u32[]{:S(2)}, u32[]{:S(2)}) collective-permute-start(bf16[3,384,128]{2,1,0:T(8,128)(2,1)S(1)} %get-tuple-element.79.refs_0_), channel_id=1, source_target_pairs={{0,2},{1,3},{2,0},{3,1},{4,6},{5,7},{6,4},{7,5},{8,10},{9,11},{10,... | collective-permute-start | bytes 884744 | tf_op jit(solution)/shard_map/ppermute | solution.py:20
  52.3 0.5 collective-permute-start.14
  52.8 4.2 %collective-permute-done.14.refs_1_ = bf16[416,128]{1,0:T(8,128)(2,1)S(1)} collective-permute-done((bf16[416,128]{1,0:T(8,128)(2,1)S(1)}, bf16[416,128]{1,0:T(8,128)(2,1)S(1)}, u32[]{:S(2)}, u32[]{:S(2)}) %collective-permute-start.14) | collective-permute-done | bytes 106528 | tf_op jit(solution)/shard_map/ppermute | solution.py:20
  57.0 2.8 %collective-permute-done.12.refs_2_ = bf16[3,384,128]{2,1,0:T(8,128)(2,1)S(1)} collective-permute-done((bf16[3,384,128]{2,1,0:T(8,128)(2,1)S(1)}, bf16[3,384,128]{2,1,0:T(8,128)(2,1)S(1)}, u32[]{:S(2)}, u32[]{:S(2)}) %collective-permute-start.12) | collective-permute-done | bytes 294944 | tf_op jit(solution)/shard_map/ppermute | solution.py:20
  59.8 1.6 %collective-permute-done.15.refs_3_ = bf16[3,384,128]{2,1,0:T(8,128)(2,1)S(1)} collective-permute-done((bf16[3,384,128]{2,1,0:T(8,128)(2,1)S(1)}, bf16[3,384,128]{2,1,0:T(8,128)(2,1)S(1)}, u32[]{:S(2)}, u32[]{:S(2)}) %collective-permute-start.15) | collective-permute-done | bytes 294944 | tf_op jit(solution)/shard_map/ppermute | solution.py:20
  61.4 1.5 %collective-permute-start.16 = (bf16[3,384,128]{2,1,0:T(8,128)(2,1)S(1)}, bf16[3,384,128]{2,1,0:T(8,128)(2,1)S(1)}, u32[]{:S(2)}, u32[]{:S(2)}) collective-permute-start(bf16[3,384,128]{2,1,0:T(8,128)(2,1)S(1)} %get-tuple-element.82.refs_0_), channel_id=1, source_target_pairs={{0,2},{1,3},{2,0},{3,1},{4,6},{5,7},{6,4},{7,5},{8,10},{9,11},{10,... | collective-permute-start | bytes 884744 | tf_op jit(solution)/shard_map/ppermute | solution.py:20
  62.9 0.7 assemble.2.grad_ref.refs_1_.refs_3_
  63.7 0.8 input_grad.4
  64.5 0.6 collective-permute-start.18
  65.0 3.0 %input_grad.5 = (bf16[384,512]{1,0:T(8,128)(2,1)}, bf16[384,512]{1,0:T(8,128)(2,1)S(1)}, bf16[384,512]{1,0:T(8,128)(2,1)S(1)}) custom-call(bf16[384,1536]{1,0:T(8,128)(2,1)S(1)} %assemble.2.grad_ref.refs_1_.refs_3_, bf16[3,512,2048]{2,1,0:T(8,128)(2,1)S(1)} %bitcast.9), custom_call_target="tpu_custom_call" | custom-call | flops 1 | bytes 1 | tf_op jit(solution)/shard_map/input_grad/pallas_call | solution.py:399
  68.0 2.5 %collective-permute-done.16.refs_2_ = bf16[3,384,128]{2,1,0:T(8,128)(2,1)S(1)} collective-permute-done((bf16[3,384,128]{2,1,0:T(8,128)(2,1)S(1)}, bf16[3,384,128]{2,1,0:T(8,128)(2,1)S(1)}, u32[]{:S(2)}, u32[]{:S(2)}) %collective-permute-start.16) | collective-permute-done | bytes 294944 | tf_op jit(solution)/shard_map/ppermute | solution.py:20
  70.8 1.2 collective-permute-done.17.refs_3_
  72.0 0.7 assemble.3.grad_ref.refs_0_.refs_2_
  72.8 0.8 input_grad.6
  73.6 2.9 %collective-permute-done.18 = bf16[384,512]{1,0:T(8,128)(2,1)S(1)} collective-permute-done((bf16[384,512]{1,0:T(8,128)(2,1)S(1)}, bf16[384,512]{1,0:T(8,128)(2,1)S(1)}, u32[]{:S(2)}, u32[]{:S(2)}) %collective-permute-start.18) | collective-permute-done | bytes 393248 | tf_op jit(solution)/shard_map/ppermute | solution.py:20
  76.5 0.9 add_convert_fusion.11
  77.4 1.6 %collective-permute-start.20 = (bf16[384,512]{1,0:T(8,128)(2,1)}, bf16[384,512]{1,0:T(8,128)(2,1)}, u32[]{:S(2)}, u32[]{:S(2)}) collective-permute-start(bf16[384,512]{1,0:T(8,128)(2,1)} %add_convert_fusion.11), channel_id=1, source_target_pairs={{0,8},{8,0},{16,24},{24,16},{1,9},{9,1},{17,25},{25,17},{2,10},{10... | collective-permute-start | bytes 1179656 | tf_op jit(solution)/shard_map/ppermute | solution.py:20
  79.0 0.5 collective-permute-start.21
  79.5 2.8 %copy-done.2 = bf16[512,3,2048]{2,0,1:T(8,128)(2,1)S(1)} copy-done((bf16[512,3,2048]{2,0,1:T(8,128)(2,1)S(1)}, bf16[512,3,2048]{2,0,1:T(8,128)(2,1)}, u32[]{:S(2)}) %copy-start.2) | copy-done | bytes 6291480
  82.3 3.1 %input_grad.7 = (bf16[384,512]{1,0:T(8,128)(2,1)S(1)}, bf16[384,512]{1,0:T(8,128)(2,1)S(1)}, bf16[384,512]{1,0:T(8,128)(2,1)S(1)}) custom-call(bf16[384,1536]{1,0:T(8,128)(2,1)S(1)} %assemble.3.grad_ref.refs_0_.refs_2_, bf16[3,512,2048]{2,1,0:T(8,128)(2,1)S(1)} %bitcast.11), custom_call_target="tpu_custom_call" | custom-call | flops 1 | bytes 1 | tf_op jit(solution)/shard_map/input_grad/pallas_call | solution.py:399
  85.4 1.2 add_convert_fusion.10
  86.6 1.3 collective-permute-start.22
  87.9 0.8 collective-permute-start.24
  88.7 1.2 add_convert_fusion.9
  89.9 0.7 collective-permute-start.23
  90.6 2.8 %collective-permute-done.21 = bf16[384,512]{1,0:T(8,128)(2,1)S(1)} collective-permute-done((bf16[384,512]{1,0:T(8,128)(2,1)S(1)}, bf16[384,512]{1,0:T(8,128)(2,1)S(1)}, u32[]{:S(2)}, u32[]{:S(2)}) %collective-permute-start.21) | collective-permute-done | bytes 393248 | tf_op jit(solution)/shard_map/ppermute | solution.py:20
  93.5 1.8 %collective-permute-done.22 = bf16[384,512]{1,0:T(8,128)(2,1)S(1)} collective-permute-done((bf16[384,512]{1,0:T(8,128)(2,1)S(1)}, bf16[384,512]{1,0:T(8,128)(2,1)S(1)}, u32[]{:S(2)}, u32[]{:S(2)}) %collective-permute-start.22) | collective-permute-done | bytes 393248 | tf_op jit(solution)/shard_map/ppermute | solution.py:20
  95.5 6.0 %collective-permute-start.25 = (bf16[384,512]{1,0:T(8,128)(2,1)S(1)}, bf16[384,512]{1,0:T(8,128)(2,1)S(1)}, u32[]{:S(2)}, u32[]{:S(2)}) collective-permute-start(bf16[384,512]{1,0:T(8,128)(2,1)S(1)} %get-tuple-element.122), channel_id=1, source_target_pairs={{0,8},{8,0},{16,24},{24,16},{1,9},{9,1},{17,25},{25,17},{2,10},{10... | collective-permute-start | bytes 1179656 | tf_op jit(solution)/shard_map/ppermute | solution.py:20
  101.6 0.7 collective-permute-start.26
  102.3 5.6 %weight_grad.2 = (f32[3,512,2048]{2,1,0:T(8,128)}, f32[8,128]{1,0:T(8,128)S(1)}) custom-call(bf16[384,1536]{1,0:T(8,128)(2,1)S(1)} %assemble.3.grad_ref.refs_0_.refs_2_, bf16[384,1536]{1,0:T(8,128)(2,1)S(1)} %assemble.2.grad_ref.refs_1_.refs_3_, bf16[384,2048]{1,0:T(8,128)(2,1)S(1)} %copy-done.4, bf16[384,2048]{1,0:T(8,128)(2,1)S(1)} %copy-done.6), custom_call_target="tpu_custom_call" | custom-call | flops 1 | bytes 1 | tf_op jit(solution)/shard_map/weight_grad/pallas_call | solution.py:456
  108.3 3.2 %collective-permute-start.27 = (bf16[384,512]{1,0:T(8,128)(2,1)S(1)}, bf16[384,512]{1,0:T(8,128)(2,1)S(1)}, u32[]{:S(2)}, u32[]{:S(2)}) collective-permute-start(bf16[384,512]{1,0:T(8,128)(2,1)S(1)} %get-tuple-element.120), channel_id=1, source_target_pairs={{0,8},{8,0},{16,24},{24,16},{1,9},{9,1},{17,25},{25,17},{2,10},{10... | collective-permute-start | bytes 1179656 | tf_op jit(solution)/shard_map/ppermute | solution.py:20
  111.5 0.7 collective-permute-start.28
  112.2 5.6 %weight_grad.3 = (f32[3,512,2048]{2,1,0:T(8,128)}, f32[8,128]{1,0:T(8,128)S(1)}) custom-call(f32[3,512,2048]{2,1,0:T(8,128)} %get-tuple-element.98.refs_0_, f32[8,128]{1,0:T(8,128)S(1)} %get-tuple-element.99.refs_1_, bf16[384,1536]{1,0:T(8,128)(2,1)S(1)} %assemble.3.grad_ref.refs_0_.refs_2_, ...), custom_call_target="tpu_custom_call", output_to_operand_aliasing={{0}: (0, {})} | custom-call | flops 1 | bytes 1 | tf_op jit(solution)/shard_map/weight_grad/pallas_call | solution.py:456
  117.9 0.7 collective-permute-start.29
  118.8 4.6 %collective-permute-start.33 = (bf16[384,512]{1,0:T(8,128)(2,1)S(1)}, bf16[384,512]{1,0:T(8,128)(2,1)S(1)}, u32[]{:S(2)}, u32[]{:S(2)}) collective-permute-start(bf16[384,512]{1,0:T(8,128)(2,1)S(1)} %add_convert_fusion.1), channel_id=1, source_target_pairs={{0,8},{8,0},{16,24},{24,16},{1,9},{9,1},{17,25},{25,17},{2,10},{10... | collective-permute-start | bytes 1179656 | tf_op jit(solution)/shard_map/ppermute | solution.py:20
  123.4 7.3 %collective-permute-start.34 = (bf16[384,512]{1,0:T(8,128)(2,1)S(1)}, bf16[384,512]{1,0:T(8,128)(2,1)S(1)}, u32[]{:S(2)}, u32[]{:S(2)}) collective-permute-start(bf16[384,512]{1,0:T(8,128)(2,1)S(1)} %add_convert_fusion), channel_id=1, source_target_pairs={{0,8},{8,0},{16,24},{24,16},{1,9},{9,1},{17,25},{25,17},{2,10},{10... | collective-permute-start | bytes 1179656 | tf_op jit(solution)/shard_map/ppermute | solution.py:20
  130.8 0.6 split.3
  131.4 1.8 %collective-permute-start.31 = (bf16[2,128,128]{2,1,0:T(8,128)(2,1)S(1)}, bf16[2,128,128]{2,1,0:T(8,128)(2,1)S(1)}, u32[]{:S(2)}, u32[]{:S(2)}) collective-permute-start(bf16[2,128,128]{2,1,0:T(8,128)(2,1)S(1)} %get-tuple-element.115), channel_id=1, source_target_pairs={{0,2},{1,3},{2,0},{3,1},{4,6},{5,7},{6,4},{7,5},{8,10},{9,11},{10,... | collective-permute-start | bytes 196616 | tf_op jit(solution)/shard_map/ppermute | solution.py:20
  133.4 2.6 %collective-permute-done.31.refs_2_ = bf16[2,128,128]{2,1,0:T(8,128)(2,1)S(1)} collective-permute-done((bf16[2,128,128]{2,1,0:T(8,128)(2,1)S(1)}, bf16[2,128,128]{2,1,0:T(8,128)(2,1)S(1)}, u32[]{:S(2)}, u32[]{:S(2)}) %collective-permute-start.31) | collective-permute-done | bytes 65568 | tf_op jit(solution)/shard_map/ppermute | solution.py:20
  135.9 1.3 collective-permute-done.32.refs_3_
  137.3 1.4 join.1
  138.7 1.3 pad_maximum_fusion
  (60 shorter events, 2.5 us)
Async XLA Ops:
  0.7 1.4 %copy-start.3 = (bf16[384,2048]{1,0:T(8,128)(2,1)S(1)}, bf16[384,2048]{1,0:T(8,128)(2,1)}, u32[]{:S(2)}) copy-start(bf16[384,2048]{1,0:T(8,128)(2,1)} %refs_4_.1) | copy-start | bytes 4718596
  2.1 3.7 %copy-start.7 = (bf16[96,1024]{1,0:T(8,128)(2,1)S(1)}, bf16[96,1024]{1,0:T(8,128)(2,1)}, u32[]{:S(2)}) copy-start(bf16[96,1024]{1,0:T(8,128)(2,1)} %up_ref.1) | copy-start | bytes 589828
  2.7 15.0 %collective-permute-start = (bf16[128,2048]{1,0:T(8,128)(2,1)S(1)}, bf16[128,2048]{1,0:T(8,128)(2,1)S(1)}, u32[]{:S(2)}, u32[]{:S(2)}) collective-permute-start(bf16[128,2048]{1,0:T(8,128)(2,1)S(1)} %get-tuple-element.63), channel_id=1, source_target_pairs={{0,4},{4,0},{1,5},{5,1},{2,6},{6,2},{3,7},{7,3},{8,12},{12,8},{9,1... | collective-permute-start | bytes 1572872 | tf_op jit(solution)/shard_map/ppermute | solution.py:20
  6.4 8.5 %collective-permute-start.3 = (bf16[2,96,128]{2,1,0:T(8,128)(2,1)S(1)}, bf16[2,96,128]{2,1,0:T(8,128)(2,1)S(1)}, u32[]{:S(2)}, u32[]{:S(2)}) collective-permute-start(bf16[2,96,128]{2,1,0:T(8,128)(2,1)S(1)} %get-tuple-element.68), channel_id=1, source_target_pairs={{0,1},{1,0},{2,3},{3,2},{4,5},{5,4},{6,7},{7,6},{8,9},{9,8},{10,11... | collective-permute-start | bytes 147464 | tf_op jit(solution)/shard_map/ppermute | solution.py:20
  6.5 8.4 %collective-permute-start.4 = (bf16[2,96,128]{2,1,0:T(8,128)(2,1)S(1)}, bf16[2,96,128]{2,1,0:T(8,128)(2,1)S(1)}, u32[]{:S(2)}, u32[]{:S(2)}) collective-permute-start(bf16[2,96,128]{2,1,0:T(8,128)(2,1)S(1)} %get-tuple-element.69), channel_id=1, source_target_pairs={{0,2},{1,3},{2,0},{3,1},{4,6},{5,7},{6,4},{7,5},{8,10},{9,11},{10,... | collective-permute-start | bytes 147464 | tf_op jit(solution)/shard_map/ppermute | solution.py:20
  8.0 6.9 %collective-permute-start.5 = (bf16[2,96,128]{2,1,0:T(8,128)(2,1)S(1)}, bf16[2,96,128]{2,1,0:T(8,128)(2,1)S(1)}, u32[]{:S(2)}, u32[]{:S(2)}) collective-permute-start(bf16[2,96,128]{2,1,0:T(8,128)(2,1)S(1)} %get-tuple-element.70), channel_id=1, source_target_pairs={{0,3},{1,2},{2,1},{3,0},{4,7},{5,6},{6,5},{7,4},{8,11},{9,10},{10,... | collective-permute-start | bytes 147464 | tf_op jit(solution)/shard_map/ppermute | solution.py:20
  8.3 2.8 %copy-start = (bf16[512,3,2048]{2,0,1:T(8,128)(2,1)S(1)}, bf16[512,3,2048]{2,0,1:T(8,128)(2,1)}, u32[]{:S(2)}) copy-start(bf16[512,3,2048]{2,0,1:T(8,128)(2,1)} %param.5) | copy-start | bytes 18874372
  11.1 22.4 %copy-start.1 = (bf16[512,3,2048]{2,0,1:T(8,128)(2,1)S(1)}, bf16[512,3,2048]{2,0,1:T(8,128)(2,1)}, u32[]{:S(2)}) copy-start(bf16[512,3,2048]{2,0,1:T(8,128)(2,1)} %param.5) | copy-start | bytes 18874372
  17.7 3.3 %collective-permute-start.6 = (bf16[2,3,384,128]{3,2,1,0:T(8,128)(2,1)S(1)}, bf16[2,3,384,128]{3,2,1,0:T(8,128)(2,1)S(1)}, u32[]{:S(2)}, u32[]{:S(2)}) collective-permute-start(bf16[2,3,384,128]{3,2,1,0:T(8,128)(2,1)S(1)} %get-tuple-element.71), channel_id=1, source_target_pairs={{0,1},{1,0},{2,3},{3,2},{4,5},{5,4},{6,7},{7,6},{8,9},{9,8},{10,11... | collective-permute-start | bytes 1769480 | tf_op jit(solution)/shard_map/ppermute | solution.py:20
  17.7 14.3 %collective-permute-start.2 = (bf16[128,2048]{1,0:T(8,128)(2,1)S(1)}, bf16[128,2048]{1,0:T(8,128)(2,1)S(1)}, u32[]{:S(2)}, u32[]{:S(2)}) collective-permute-start(bf16[128,2048]{1,0:T(8,128)(2,1)S(1)} %get-tuple-element.65), channel_id=1, source_target_pairs={{0,4},{4,0},{1,5},{5,1},{2,6},{6,2},{3,7},{7,3},{8,12},{12,8},{9,1... | collective-permute-start | bytes 1572872 | tf_op jit(solution)/shard_map/ppermute | solution.py:20
  19.4 14.1 %collective-permute-start.1 = (bf16[128,2048]{1,0:T(8,128)(2,1)S(1)}, bf16[128,2048]{1,0:T(8,128)(2,1)S(1)}, u32[]{:S(2)}, u32[]{:S(2)}) collective-permute-start(bf16[128,2048]{1,0:T(8,128)(2,1)S(1)} %collective-permute-done.refs_0_), channel_id=1, source_target_pairs={{0,8},{8,0},{16,24},{24,16},{1,9},{9,1},{17,25},{25,17},{2,10},{10... | collective-permute-start | bytes 1572872 | tf_op jit(solution)/shard_map/ppermute | solution.py:20
  21.1 27.6 %copy-start.8 = (f32[7,64]{1,0:T(8,128)S(1)}, f32[7,64]{1,0:T(8,128)}, u32[]{:S(2)}) copy-start(f32[7,64]{1,0:T(8,128)} %taps_ref.1) | copy-start | bytes 5380
  21.1 10.9 %collective-permute-start.7 = (bf16[1,3,384,128]{3,2,1,0:T(8,128)(2,1)S(1)}, bf16[1,3,384,128]{3,2,1,0:T(8,128)(2,1)S(1)}, u32[]{:S(2)}, u32[]{:S(2)}) collective-permute-start(bf16[1,3,384,128]{3,2,1,0:T(8,128)(2,1)S(1)} %add_convert_fusion.13), channel_id=1, source_target_pairs={{0,2},{1,3},{2,0},{3,1},{4,6},{5,7},{6,4},{7,5},{8,10},{9,11},{10,... | collective-permute-start | bytes 884744 | tf_op jit(solution)/shard_map/ppermute | solution.py:20
  37.4 26.2 %copy-start.5 = (bf16[384,2048]{1,0:T(8,128)(2,1)}, bf16[384,2048]{1,0:T(8,128)(2,1)S(1)}, u32[]{:S(2)}) copy-start(bf16[384,2048]{1,0:T(8,128)(2,1)S(1)} %get-tuple-element.97.refs_3_.refs_5_) | copy-start | bytes 4718596
  37.4 2.1 %collective-permute-start.8 = (bf16[2,3,384,128]{3,2,1,0:T(8,128)(2,1)S(1)}, bf16[2,3,384,128]{3,2,1,0:T(8,128)(2,1)S(1)}, u32[]{:S(2)}, u32[]{:S(2)}) collective-permute-start(bf16[2,3,384,128]{3,2,1,0:T(8,128)(2,1)S(1)} %get-tuple-element.74), channel_id=1, source_target_pairs={{0,1},{1,0},{2,3},{3,2},{4,5},{5,4},{6,7},{7,6},{8,9},{9,8},{10,11... | collective-permute-start | bytes 1769480 | tf_op jit(solution)/shard_map/ppermute | solution.py:20
  39.6 9.1 %collective-permute-start.10 = (bf16[1,3,384,128]{3,2,1,0:T(8,128)(2,1)S(1)}, bf16[1,3,384,128]{3,2,1,0:T(8,128)(2,1)S(1)}, u32[]{:S(2)}, u32[]{:S(2)}) collective-permute-start(bf16[1,3,384,128]{3,2,1,0:T(8,128)(2,1)S(1)} %add_convert_fusion.12), channel_id=1, source_target_pairs={{0,2},{1,3},{2,0},{3,1},{4,6},{5,7},{6,4},{7,5},{8,10},{9,11},{10,... | collective-permute-start | bytes 884744 | tf_op jit(solution)/shard_map/ppermute | solution.py:20
  41.7 4.7 %collective-permute-start.9 = (bf16[384,128]{1,0:T(8,128)(2,1)S(1)}, bf16[384,128]{1,0:T(8,128)(2,1)S(1)}, u32[]{:S(2)}, u32[]{:S(2)}) collective-permute-start(bf16[384,128]{1,0:T(8,128)(2,1)S(1)} %get-tuple-element.77), channel_id=1, source_target_pairs={{0,4},{4,0},{1,5},{5,1},{2,6},{6,2},{3,7},{7,3},{8,12},{12,8},{9,1... | collective-permute-start | bytes 294920 | tf_op jit(solution)/shard_map/ppermute | solution.py:20
  50.3 6.8 %collective-permute-start.11 = (bf16[3,384,128]{2,1,0:T(8,128)(2,1)S(1)}, bf16[3,384,128]{2,1,0:T(8,128)(2,1)S(1)}, u32[]{:S(2)}, u32[]{:S(2)}) collective-permute-start(bf16[3,384,128]{2,1,0:T(8,128)(2,1)S(1)} %get-tuple-element.82.refs_0_), channel_id=1, source_target_pairs={{0,1},{1,0},{2,3},{3,2},{4,5},{5,4},{6,7},{7,6},{8,9},{9,8},{10,11... | collective-permute-start | bytes 884744 | tf_op jit(solution)/shard_map/ppermute | solution.py:20
  50.3 6.7 %collective-permute-start.13 = (bf16[3,384,128]{2,1,0:T(8,128)(2,1)S(1)}, bf16[3,384,128]{2,1,0:T(8,128)(2,1)S(1)}, u32[]{:S(2)}, u32[]{:S(2)}) collective-permute-start(bf16[3,384,128]{2,1,0:T(8,128)(2,1)S(1)} %get-tuple-element.79.refs_0_), channel_id=1, source_target_pairs={{0,1},{1,0},{2,3},{3,2},{4,5},{5,4},{6,7},{7,6},{8,9},{9,8},{10,11... | collective-permute-start | bytes 884744 | tf_op jit(solution)/shard_map/ppermute | solution.py:20
  50.8 9.0 %collective-permute-start.12 = (bf16[3,384,128]{2,1,0:T(8,128)(2,1)S(1)}, bf16[3,384,128]{2,1,0:T(8,128)(2,1)S(1)}, u32[]{:S(2)}, u32[]{:S(2)}) collective-permute-start(bf16[3,384,128]{2,1,0:T(8,128)(2,1)S(1)} %get-tuple-element.79.refs_0_), channel_id=1, source_target_pairs={{0,2},{1,3},{2,0},{3,1},{4,6},{5,7},{6,4},{7,5},{8,10},{9,11},{10,... | collective-permute-start | bytes 884744 | tf_op jit(solution)/shard_map/ppermute | solution.py:20
  52.3 4.7 %collective-permute-start.14 = (bf16[416,128]{1,0:T(8,128)(2,1)S(1)}, bf16[416,128]{1,0:T(8,128)(2,1)S(1)}, u32[]{:S(2)}, u32[]{:S(2)}) collective-permute-start(bf16[416,128]{1,0:T(8,128)(2,1)S(1)} %get-tuple-element.80), channel_id=1, source_target_pairs={{0,4},{4,0},{1,5},{5,1},{2,6},{6,2},{3,7},{7,3},{8,12},{12,8},{9,1... | collective-permute-start | bytes 319496 | tf_op jit(solution)/shard_map/ppermute | solution.py:20
  59.8 1.6 %collective-permute-start.15 = (bf16[3,384,128]{2,1,0:T(8,128)(2,1)S(1)}, bf16[3,384,128]{2,1,0:T(8,128)(2,1)S(1)}, u32[]{:S(2)}, u32[]{:S(2)}) collective-permute-start(bf16[3,384,128]{2,1,0:T(8,128)(2,1)S(1)} %collective-permute-done.12.refs_2_), channel_id=1, source_target_pairs={{0,1},{1,0},{2,3},{3,2},{4,5},{5,4},{6,7},{7,6},{8,9},{9,8},{10,11... | collective-permute-start | bytes 884744 | tf_op jit(solution)/shard_map/ppermute | solution.py:20
  61.4 9.1 %collective-permute-start.16 = (bf16[3,384,128]{2,1,0:T(8,128)(2,1)S(1)}, bf16[3,384,128]{2,1,0:T(8,128)(2,1)S(1)}, u32[]{:S(2)}, u32[]{:S(2)}) collective-permute-start(bf16[3,384,128]{2,1,0:T(8,128)(2,1)S(1)} %get-tuple-element.82.refs_0_), channel_id=1, source_target_pairs={{0,2},{1,3},{2,0},{3,1},{4,6},{5,7},{6,4},{7,5},{8,10},{9,11},{10,... | collective-permute-start | bytes 884744 | tf_op jit(solution)/shard_map/ppermute | solution.py:20
  64.5 12.1 %collective-permute-start.18 = (bf16[384,512]{1,0:T(8,128)(2,1)S(1)}, bf16[384,512]{1,0:T(8,128)(2,1)S(1)}, u32[]{:S(2)}, u32[]{:S(2)}) collective-permute-start(bf16[384,512]{1,0:T(8,128)(2,1)S(1)} %input_grad.4), channel_id=1, source_target_pairs={{0,4},{4,0},{1,5},{5,1},{2,6},{6,2},{3,7},{7,3},{8,12},{12,8},{9,1... | collective-permute-start | bytes 1179656 | tf_op jit(solution)/shard_map/ppermute | solution.py:20
  70.5 1.6 %collective-permute-start.17 = (bf16[3,384,128]{2,1,0:T(8,128)(2,1)S(1)}, bf16[3,384,128]{2,1,0:T(8,128)(2,1)S(1)}, u32[]{:S(2)}, u32[]{:S(2)}) collective-permute-start(bf16[3,384,128]{2,1,0:T(8,128)(2,1)S(1)} %collective-permute-done.16.refs_2_), channel_id=1, source_target_pairs={{0,1},{1,0},{2,3},{3,2},{4,5},{5,4},{6,7},{7,6},{8,9},{9,8},{10,11... | collective-permute-start | bytes 884744 | tf_op jit(solution)/shard_map/ppermute | solution.py:20
  70.5 14.9 %collective-permute-start.19 = (bf16[384,512]{1,0:T(8,128)(2,1)}, bf16[384,512]{1,0:T(8,128)(2,1)}, u32[]{:S(2)}, u32[]{:S(2)}) collective-permute-start(bf16[384,512]{1,0:T(8,128)(2,1)} %get-tuple-element.89), channel_id=1, source_target_pairs={{0,4},{4,0},{1,5},{5,1},{2,6},{6,2},{3,7},{7,3},{8,12},{12,8},{9,1... | collective-permute-start | bytes 1179656 | tf_op jit(solution)/shard_map/ppermute | solution.py:20
  77.4 11.3 %collective-permute-start.20 = (bf16[384,512]{1,0:T(8,128)(2,1)}, bf16[384,512]{1,0:T(8,128)(2,1)}, u32[]{:S(2)}, u32[]{:S(2)}) collective-permute-start(bf16[384,512]{1,0:T(8,128)(2,1)} %add_convert_fusion.11), channel_id=1, source_target_pairs={{0,8},{8,0},{16,24},{24,16},{1,9},{9,1},{17,25},{25,17},{2,10},{10... | collective-permute-start | bytes 1179656 | tf_op jit(solution)/shard_map/ppermute | solution.py:20
  79.0 14.4 %collective-permute-start.21 = (bf16[384,512]{1,0:T(8,128)(2,1)S(1)}, bf16[384,512]{1,0:T(8,128)(2,1)S(1)}, u32[]{:S(2)}, u32[]{:S(2)}) collective-permute-start(bf16[384,512]{1,0:T(8,128)(2,1)S(1)} %get-tuple-element.93), channel_id=1, source_target_pairs={{0,4},{4,0},{1,5},{5,1},{2,6},{6,2},{3,7},{7,3},{8,12},{12,8},{9,1... | collective-permute-start | bytes 1179656 | tf_op jit(solution)/shard_map/ppermute | solution.py:20
  79.5 2.8 %copy-start.2 = (bf16[512,3,2048]{2,0,1:T(8,128)(2,1)S(1)}, bf16[512,3,2048]{2,0,1:T(8,128)(2,1)}, u32[]{:S(2)}) copy-start(bf16[512,3,2048]{2,0,1:T(8,128)(2,1)} %param.5) | copy-start | bytes 18874372
  85.4 16.9 %copy-start.4 = (bf16[384,2048]{1,0:T(8,128)(2,1)S(1)}, bf16[384,2048]{1,0:T(8,128)(2,1)}, u32[]{:S(2)}) copy-start(bf16[384,2048]{1,0:T(8,128)(2,1)} %refs_4_.1) | copy-start | bytes 4718596
  85.4 16.9 %copy-start.6 = (bf16[384,2048]{1,0:T(8,128)(2,1)S(1)}, bf16[384,2048]{1,0:T(8,128)(2,1)}, u32[]{:S(2)}) copy-start(bf16[384,2048]{1,0:T(8,128)(2,1)} %copy-done.5) | copy-start | bytes 4718596
  86.6 8.6 %collective-permute-start.22 = (bf16[384,512]{1,0:T(8,128)(2,1)S(1)}, bf16[384,512]{1,0:T(8,128)(2,1)S(1)}, u32[]{:S(2)}, u32[]{:S(2)}) collective-permute-start(bf16[384,512]{1,0:T(8,128)(2,1)S(1)} %add_convert_fusion.10), channel_id=1, source_target_pairs={{0,8},{8,0},{16,24},{24,16},{1,9},{9,1},{17,25},{25,17},{2,10},{10... | collective-permute-start | bytes 1179656 | tf_op jit(solution)/shard_map/ppermute | solution.py:20
  87.9 20.0 %collective-permute-start.24 = (bf16[384,512]{1,0:T(8,128)(2,1)S(1)}, bf16[384,512]{1,0:T(8,128)(2,1)S(1)}, u32[]{:S(2)}, u32[]{:S(2)}) collective-permute-start(bf16[384,512]{1,0:T(8,128)(2,1)S(1)} %get-tuple-element.102), channel_id=1, source_target_pairs={{0,4},{4,0},{1,5},{5,1},{2,6},{6,2},{3,7},{7,3},{8,12},{12,8},{9,1... | collective-permute-start | bytes 1179656 | tf_op jit(solution)/shard_map/ppermute | solution.py:20
  89.9 5.5 %collective-permute-start.23 = (bf16[384,512]{1,0:T(8,128)(2,1)S(1)}, bf16[384,512]{1,0:T(8,128)(2,1)S(1)}, u32[]{:S(2)}, u32[]{:S(2)}) collective-permute-start(bf16[384,512]{1,0:T(8,128)(2,1)S(1)} %add_convert_fusion.9), channel_id=1, source_target_pairs={{0,0},{8,16},{16,8},{24,24},{1,1},{9,17},{17,9},{25,25},{2,2},{10,... | collective-permute-start | bytes 1179656 | tf_op jit(solution)/shard_map/ppermute | solution.py:600
  95.5 12.5 %collective-permute-start.25 = (bf16[384,512]{1,0:T(8,128)(2,1)S(1)}, bf16[384,512]{1,0:T(8,128)(2,1)S(1)}, u32[]{:S(2)}, u32[]{:S(2)}) collective-permute-start(bf16[384,512]{1,0:T(8,128)(2,1)S(1)} %get-tuple-element.122), channel_id=1, source_target_pairs={{0,8},{8,0},{16,24},{24,16},{1,9},{9,1},{17,25},{25,17},{2,10},{10... | collective-permute-start | bytes 1179656 | tf_op jit(solution)/shard_map/ppermute | solution.py:20
  101.6 6.6 %collective-permute-start.26 = (bf16[384,512]{1,0:T(8,128)(2,1)S(1)}, bf16[384,512]{1,0:T(8,128)(2,1)S(1)}, u32[]{:S(2)}, u32[]{:S(2)}) collective-permute-start(bf16[384,512]{1,0:T(8,128)(2,1)S(1)} %add_convert_fusion.7), channel_id=1, source_target_pairs={{0,0},{8,16},{16,8},{24,24},{1,1},{9,17},{17,9},{25,25},{2,2},{10,... | collective-permute-start | bytes 1179656 | tf_op jit(solution)/shard_map/ppermute | solution.py:600
  108.3 9.5 %collective-permute-start.27 = (bf16[384,512]{1,0:T(8,128)(2,1)S(1)}, bf16[384,512]{1,0:T(8,128)(2,1)S(1)}, u32[]{:S(2)}, u32[]{:S(2)}) collective-permute-start(bf16[384,512]{1,0:T(8,128)(2,1)S(1)} %get-tuple-element.120), channel_id=1, source_target_pairs={{0,8},{8,0},{16,24},{24,16},{1,9},{9,1},{17,25},{25,17},{2,10},{10... | collective-permute-start | bytes 1179656 | tf_op jit(solution)/shard_map/ppermute | solution.py:20
  111.5 7.2 %collective-permute-start.28 = (bf16[384,512]{1,0:T(8,128)(2,1)S(1)}, bf16[384,512]{1,0:T(8,128)(2,1)S(1)}, u32[]{:S(2)}, u32[]{:S(2)}) collective-permute-start(bf16[384,512]{1,0:T(8,128)(2,1)S(1)} %add_convert_fusion.4), channel_id=1, source_target_pairs={{0,0},{8,16},{16,8},{24,24},{1,1},{9,17},{17,9},{25,25},{2,2},{10,... | collective-permute-start | bytes 1179656 | tf_op jit(solution)/shard_map/ppermute | solution.py:600
  117.9 5.4 %collective-permute-start.29 = (bf16[384,512]{1,0:T(8,128)(2,1)S(1)}, bf16[384,512]{1,0:T(8,128)(2,1)S(1)}, u32[]{:S(2)}, u32[]{:S(2)}) collective-permute-start(bf16[384,512]{1,0:T(8,128)(2,1)S(1)} %add_convert_fusion.2), channel_id=1, source_target_pairs={{0,0},{8,16},{16,8},{24,24},{1,1},{9,17},{17,9},{25,25},{2,2},{10,... | collective-permute-start | bytes 1179656 | tf_op jit(solution)/shard_map/ppermute | solution.py:600
  118.8 14.5 %collective-permute-start.33 = (bf16[384,512]{1,0:T(8,128)(2,1)S(1)}, bf16[384,512]{1,0:T(8,128)(2,1)S(1)}, u32[]{:S(2)}, u32[]{:S(2)}) collective-permute-start(bf16[384,512]{1,0:T(8,128)(2,1)S(1)} %add_convert_fusion.1), channel_id=1, source_target_pairs={{0,8},{8,0},{16,24},{24,16},{1,9},{9,1},{17,25},{25,17},{2,10},{10... | collective-permute-start | bytes 1179656 | tf_op jit(solution)/shard_map/ppermute | solution.py:20
  123.4 15.2 %collective-permute-start.34 = (bf16[384,512]{1,0:T(8,128)(2,1)S(1)}, bf16[384,512]{1,0:T(8,128)(2,1)S(1)}, u32[]{:S(2)}, u32[]{:S(2)}) collective-permute-start(bf16[384,512]{1,0:T(8,128)(2,1)S(1)} %add_convert_fusion), channel_id=1, source_target_pairs={{0,8},{8,0},{16,24},{24,16},{1,9},{9,1},{17,25},{25,17},{2,10},{10... | collective-permute-start | bytes 1179656 | tf_op jit(solution)/shard_map/ppermute | solution.py:20
  131.3 2.0 %collective-permute-start.30 = (bf16[2,128,128]{2,1,0:T(8,128)(2,1)S(1)}, bf16[2,128,128]{2,1,0:T(8,128)(2,1)S(1)}, u32[]{:S(2)}, u32[]{:S(2)}) collective-permute-start(bf16[2,128,128]{2,1,0:T(8,128)(2,1)S(1)} %get-tuple-element.114), channel_id=1, source_target_pairs={{0,1},{1,0},{2,3},{3,2},{4,5},{5,4},{6,7},{7,6},{8,9},{9,8},{10,11... | collective-permute-start | bytes 196616 | tf_op jit(solution)/shard_map/ppermute | solution.py:20
  131.4 4.5 %collective-permute-start.31 = (bf16[2,128,128]{2,1,0:T(8,128)(2,1)S(1)}, bf16[2,128,128]{2,1,0:T(8,128)(2,1)S(1)}, u32[]{:S(2)}, u32[]{:S(2)}) collective-permute-start(bf16[2,128,128]{2,1,0:T(8,128)(2,1)S(1)} %get-tuple-element.115), channel_id=1, source_target_pairs={{0,2},{1,3},{2,0},{3,1},{4,6},{5,7},{6,4},{7,5},{8,10},{9,11},{10,... | collective-permute-start | bytes 196616 | tf_op jit(solution)/shard_map/ppermute | solution.py:20
  133.2 4.0 %collective-permute-start.32 = (bf16[2,128,128]{2,1,0:T(8,128)(2,1)S(1)}, bf16[2,128,128]{2,1,0:T(8,128)(2,1)S(1)}, u32[]{:S(2)}, u32[]{:S(2)}) collective-permute-start(bf16[2,128,128]{2,1,0:T(8,128)(2,1)S(1)} %get-tuple-element.116), channel_id=1, source_target_pairs={{0,3},{1,2},{2,1},{3,0},{4,7},{5,6},{6,5},{7,4},{8,11},{9,10},{10,... | collective-permute-start | bytes 196616 | tf_op jit(solution)/shard_map/ppermute | solution.py:20

commit v11 on v10

--- a/solution.py
+++ b/solution.py
@@ -560,7 +560,6 @@
         grads[k] = [own_grads[k], nears[k]]
         for far in fars:
             grads[k] += [far, swap(far, "depth", 1)]
-        ready = grads[k][2:]
         lhs[k] = assemble(place, grads[k])
         if k > 0:
             parts_of = input_grad(lhs[k], w, 0, 1, chunks, width)
@@ -568,7 +567,7 @@
             sent.append(([swap(part, "col", k) for part in parts_of[:3]], parts_of))
     held = [parts_of[3:] for _, parts_of in sent]
     sent = [of for of, _ in sent]
-    own_part = input_grad(lhs[0], w, 0, 1, chunks, width)
+    own_part = input_grad(lhs[0], w, 0, chunks, chunks, width)
     outer = (row_at == 0) | (row_at == 3)
     line = lax.axis_size("row") == 4
     inward, across, summed, done = ([None] * chunks for _ in range(4))
@@ -599,16 +598,17 @@
             if 0 <= slot - 1 < chunks:
                 cross = lax.ppermute(across[slot - 1], "row", [(0, 0), (1, 2), (2, 1), (3, 3)])
         if slot == 0:
-            own_part += input_grad(after(lhs[0], *marks), w, 1, chunks, chunks, width)
-            marks = [own_part[1]]
             for k, parts_of in enumerate(held):
                 sent[k] += [swap(after(part, *marks), "col", k + 1) for part in parts_of]
-        if slot in (2, 3):
-            filled = weight_grad(filled, [after(lhs[0], *marks)] + lhs[1:], xs, slot - 2, 3, width)
+        if slot in (2, 4):
+            filled = weight_grad(filled, [after(lhs[0], *marks)] + lhs[1:], xs, slot // 2 - 1, 3, width)
             marks = [filled[1]]
-        if slot == chunks + 1:
+        if slot == 4:
+            marks += late
+        if slot == 3:
             blocks = split_rows(place, [after(blocks[0], *marks)] + blocks[1:], n_depth)
             blocks = [block if r == 0 else swap(block, "depth", r) for r, block in enumerate(blocks)]
+            late = blocks[1:]
     grad_tokens = jnp.concatenate(done, axis=1)
     output, grad_taps = join(place, filled[1], [after(blocks[0], *marks)] + blocks[1:], taps.shape[1])
     grad_weight = jnp.transpose(filled[0], (1, 0, 2))

time: 140 us -> 142 us (1.014)
  waiting for transfers between devices: 45.7 us -> 53.6 us
  starting transfers between devices: 46.9 us -> 43 us
  local copies, waits for them, and re-layouts: 7.01 us -> 4.88 us
    ppermute x31, waiting for transfers between devices: 45.7 us -> 53.6 us  [swap(): return lax.ppermute(value, axis, [(i, i ^ flip) for i in range(count)])]
    ppermute x31, starting transfers between devices: 44.1 us -> 40.3 us  [swap(): return lax.ppermute(value, axis, [(i, i ^ flip) for i in range(count)])]
    unnamed x18 -> x28, local copies, waits for them, and re-layouts: 7.01 us -> 4.88 us
    pallas_call x4 -> x3, Pallas kernels: 7.63 us -> 7.71 us  [input_grad(): pl.pallas_call(functools.partial(input_grad_kernel if single else input_g...]
  transfers between devices with their start and end apart: 35 -> 35, of which waited for: 16 -> 18; matrix products, arithmetic and copies ran while one was open for 3% -> 3% of each run, Pallas kernels for 19% -> 19%
where the time goes in v11:
time: 142 us
  waiting for transfers between devices  53.6 us (38%)
  starting transfers between devices  43 us (30%)
  Pallas kernels  33.4 us (24%)
  other arithmetic  5.97 us (4%)
  local copies, waits for them, and re-layouts  4.88 us (3%)
    ppermute x31, waiting for transfers between devices, swap(): return lax.ppermute(value, axis, [(i, i ^ flip) for i in range(count)])  53.6 us
    ppermute x31, starting transfers between devices, swap(): return lax.ppermute(value, axis, [(i, i ^ flip) for i in range(count)])  40.3 us
    pallas_call x2, Pallas kernels, weight_grad(): pl.pallas_call(functools.partial(weight_grad_kernel, chained=chained, gro...  11.3 us
    pallas_call x3, Pallas kernels, input_grad(): pl.pallas_call(functools.partial(input_grad_kernel if single else input_g...  7.71 us
    pallas_call x2, Pallas kernels, project(): pl.pallas_call(functools.partial(project_kernel, pieces=len(xs), count=co...  7.67 us
    unnamed x28, local copies, waits for them, and re-layouts  4.88 us
  transfers between devices with their start and end apart: 35, of which 18 were waited for; matrix products, arithmetic and copies ran while one was open for 3% of the time, Pallas kernels for 19%

profile of v11, /device:TPU:0, one launch (start us, length us, event | category | flops | bytes accessed | tf_op | source)
XLA Modules:
  0.0 141.9 jit_solution(2523098320781295556)
XLA Ops:
  0.7 1.4 copy-done.2
  2.1 0.6 cut.1
  2.7 3.0 %collective-permute-start = (bf16[128,2048]{1,0:T(8,128)(2,1)S(1)}, bf16[128,2048]{1,0:T(8,128)(2,1)S(1)}, u32[]{:S(2)}, u32[]{:S(2)}) collective-permute-start(bf16[128,2048]{1,0:T(8,128)(2,1)S(1)} %get-tuple-element.63), channel_id=1, source_target_pairs={{0,4},{4,0},{1,5},{5,1},{2,6},{6,2},{3,7},{7,3},{8,12},{12,8},{9,1... | collective-permute-start | bytes 1572872 | tf_op jit(solution)/shard_map/ppermute | solution.py:20
  5.8 0.6 split.2
  6.5 1.6 %collective-permute-start.4 = (bf16[2,96,128]{2,1,0:T(8,128)(2,1)S(1)}, bf16[2,96,128]{2,1,0:T(8,128)(2,1)S(1)}, u32[]{:S(2)}, u32[]{:S(2)}) collective-permute-start(bf16[2,96,128]{2,1,0:T(8,128)(2,1)S(1)} %get-tuple-element.69), channel_id=1, source_target_pairs={{0,2},{1,3},{2,0},{3,1},{4,6},{5,7},{6,4},{7,5},{8,10},{9,11},{10,... | collective-permute-start | bytes 147464 | tf_op jit(solution)/shard_map/ppermute | solution.py:20
  8.3 2.8 %copy-done = bf16[512,3,2048]{2,0,1:T(8,128)(2,1)S(1)} copy-done((bf16[512,3,2048]{2,0,1:T(8,128)(2,1)S(1)}, bf16[512,3,2048]{2,0,1:T(8,128)(2,1)}, u32[]{:S(2)}) %copy-start) | copy-done | bytes 6291480
  11.1 3.8 %project.2 = (bf16[2,3,384,128]{3,2,1,0:T(8,128)(2,1)S(1)}, bf16[2,3,384,128]{3,2,1,0:T(8,128)(2,1)S(1)}) custom-call(s32[4]{0:T(128)S(1)} %pad_add_fusion.place._, bf16[384,2048]{1,0:T(8,128)(2,1)S(1)} %copy-done.2, bf16[3,512,2048]{2,1,0:T(8,128)(2,1)S(1)} %bitcast.6), custom_call_target="tpu_custom_call" | custom-call | flops 1 | bytes 1 | tf_op jit(solution)/shard_map/project/pallas_call | solution.py:87
  14.9 2.8 %collective-permute-done.refs_0_ = bf16[128,2048]{1,0:T(8,128)(2,1)S(1)} collective-permute-done((bf16[128,2048]{1,0:T(8,128)(2,1)S(1)}, bf16[128,2048]{1,0:T(8,128)(2,1)S(1)}, u32[]{:S(2)}, u32[]{:S(2)}) %collective-permute-start) | collective-permute-done | bytes 524320 | tf_op jit(solution)/shard_map/ppermute | solution.py:20
  17.7 1.7 %collective-permute-start.2 = (bf16[128,2048]{1,0:T(8,128)(2,1)S(1)}, bf16[128,2048]{1,0:T(8,128)(2,1)S(1)}, u32[]{:S(2)}, u32[]{:S(2)}) collective-permute-start(bf16[128,2048]{1,0:T(8,128)(2,1)S(1)} %get-tuple-element.65), channel_id=1, source_target_pairs={{0,4},{4,0},{1,5},{5,1},{2,6},{6,2},{3,7},{7,3},{8,12},{12,8},{9,1... | collective-permute-start | bytes 1572872 | tf_op jit(solution)/shard_map/ppermute | solution.py:20
  19.4 1.6 %collective-permute-start.1 = (bf16[128,2048]{1,0:T(8,128)(2,1)S(1)}, bf16[128,2048]{1,0:T(8,128)(2,1)S(1)}, u32[]{:S(2)}, u32[]{:S(2)}) collective-permute-start(bf16[128,2048]{1,0:T(8,128)(2,1)S(1)} %collective-permute-done.refs_0_), channel_id=1, source_target_pairs={{0,8},{8,0},{16,24},{24,16},{1,9},{9,1},{17,25},{25,17},{2,10},{10... | collective-permute-start | bytes 1572872 | tf_op jit(solution)/shard_map/ppermute | solution.py:20
  21.1 1.6 %collective-permute-start.7 = (bf16[1,3,384,128]{3,2,1,0:T(8,128)(2,1)S(1)}, bf16[1,3,384,128]{3,2,1,0:T(8,128)(2,1)S(1)}, u32[]{:S(2)}, u32[]{:S(2)}) collective-permute-start(bf16[1,3,384,128]{3,2,1,0:T(8,128)(2,1)S(1)} %add_convert_fusion.13), channel_id=1, source_target_pairs={{0,2},{1,3},{2,0},{3,1},{4,6},{5,7},{6,4},{7,5},{8,10},{9,11},{10,... | collective-permute-start | bytes 884744 | tf_op jit(solution)/shard_map/ppermute | solution.py:20
  22.7 9.4 %collective-permute-done.2.refs_2_ = bf16[128,2048]{1,0:T(8,128)(2,1)S(1)} collective-permute-done((bf16[128,2048]{1,0:T(8,128)(2,1)S(1)}, bf16[128,2048]{1,0:T(8,128)(2,1)S(1)}, u32[]{:S(2)}, u32[]{:S(2)}) %collective-permute-start.2) | collective-permute-done | bytes 524320 | tf_op jit(solution)/shard_map/ppermute | solution.py:20
  32.0 1.5 %collective-permute-done.1.refs_1_ = bf16[128,2048]{1,0:T(8,128)(2,1)S(1)} collective-permute-done((bf16[128,2048]{1,0:T(8,128)(2,1)S(1)}, bf16[128,2048]{1,0:T(8,128)(2,1)S(1)}, u32[]{:S(2)}, u32[]{:S(2)}) %collective-permute-start.1) | collective-permute-done | bytes 524320 | tf_op jit(solution)/shard_map/ppermute | solution.py:20
  33.5 3.9 %project.3 = (bf16[2,3,384,128]{3,2,1,0:T(8,128)(2,1)S(1)}, bf16[2,3,384,128]{3,2,1,0:T(8,128)(2,1)S(1)}, bf16[384,2048]{1,0:T(8,128)(2,1)S(1)}) custom-call(s32[4]{0:T(128)S(1)} %pad_add_fusion.place._, bf16[128,2048]{1,0:T(8,128)(2,1)S(1)} %collective-permute-done.refs_0_, bf16[128,2048]{1,0:T(8,128)(2,1)S(1)} %collective-permute-done.1.refs_1_, ...), custom_call_target="tpu_custom_call" | custom-call | flops 1 | bytes 1 | tf_op jit(solution)/shard_map/project/pallas_call | solution.py:87
  37.5 2.0 %collective-permute-done.8.refs_6_ = bf16[2,3,384,128]{3,2,1,0:T(8,128)(2,1)S(1)} collective-permute-done((bf16[2,3,384,128]{3,2,1,0:T(8,128)(2,1)S(1)}, bf16[2,3,384,128]{3,2,1,0:T(8,128)(2,1)S(1)}, u32[]{:S(2)}, u32[]{:S(2)}) %collective-permute-start.8) | collective-permute-done | bytes 589856 | tf_op jit(solution)/shard_map/ppermute | solution.py:20
  39.6 1.6 %collective-permute-start.10 = (bf16[1,3,384,128]{3,2,1,0:T(8,128)(2,1)S(1)}, bf16[1,3,384,128]{3,2,1,0:T(8,128)(2,1)S(1)}, u32[]{:S(2)}, u32[]{:S(2)}) collective-permute-start(bf16[1,3,384,128]{3,2,1,0:T(8,128)(2,1)S(1)} %add_convert_fusion.12), channel_id=1, source_target_pairs={{0,2},{1,3},{2,0},{3,1},{4,6},{5,7},{6,4},{7,5},{8,10},{9,11},{10,... | collective-permute-start | bytes 884744 | tf_op jit(solution)/shard_map/ppermute | solution.py:20
  41.1 0.6 merge.1
  41.7 0.6 collective-permute-start.9
  42.3 4.1 %collective-permute-done.9.refs_1_ = bf16[384,128]{1,0:T(8,128)(2,1)S(1)} collective-permute-done((bf16[384,128]{1,0:T(8,128)(2,1)S(1)}, bf16[384,128]{1,0:T(8,128)(2,1)S(1)}, u32[]{:S(2)}, u32[]{:S(2)}) %collective-permute-start.9) | collective-permute-done | bytes 98336 | tf_op jit(solution)/shard_map/ppermute | solution.py:20
  46.4 2.3 %collective-permute-done.10.refs_7_ = bf16[1,3,384,128]{3,2,1,0:T(8,128)(2,1)S(1)} collective-permute-done((bf16[1,3,384,128]{3,2,1,0:T(8,128)(2,1)S(1)}, bf16[1,3,384,128]{3,2,1,0:T(8,128)(2,1)S(1)}, u32[]{:S(2)}, u32[]{:S(2)}) %collective-permute-start.10) | collective-permute-done | bytes 294944 | tf_op jit(solution)/shard_map/ppermute | solution.py:20
  48.7 1.6 %middle.1 = (bf16[3,384,128]{2,1,0:T(8,128)(2,1)S(1)}, bf16[3,384,128]{2,1,0:T(8,128)(2,1)S(1)}, bf16[416,128]{1,0:T(8,128)(2,1)S(1)}, bf16[416,128]{1,0:T(8,128)(2,1)S(1)}) custom-call(s32[4]{0:T(128)S(1)} %pad_add_fusion.place._, f32[7,64]{1,0:T(8,128)S(1)} %copy-done.11, bf16[384,128]{1,0:T(8,128)(2,1)S(1)} %get-tuple-element.76.refs_0_, ...), custom_call_target="tpu_custom_call" | custom-call | flops 1 | bytes 1 | tf_op jit(solution)/shard_map/middle/pallas_call | solution.py:311
  50.4 0.5 collective-permute-start.14
  50.8 1.5 %collective-permute-start.12 = (bf16[3,384,128]{2,1,0:T(8,128)(2,1)S(1)}, bf16[3,384,128]{2,1,0:T(8,128)(2,1)S(1)}, u32[]{:S(2)}, u32[]{:S(2)}) collective-permute-start(bf16[3,384,128]{2,1,0:T(8,128)(2,1)S(1)} %get-tuple-element.79.refs_0_), channel_id=1, source_target_pairs={{0,2},{1,3},{2,0},{3,1},{4,6},{5,7},{6,4},{7,5},{8,10},{9,11},{10,... | collective-permute-start | bytes 884744 | tf_op jit(solution)/shard_map/ppermute | solution.py:20
  52.3 0.5 collective-permute-start.15
  52.8 4.2 %collective-permute-done.15.refs_1_ = bf16[416,128]{1,0:T(8,128)(2,1)S(1)} collective-permute-done((bf16[416,128]{1,0:T(8,128)(2,1)S(1)}, bf16[416,128]{1,0:T(8,128)(2,1)S(1)}, u32[]{:S(2)}, u32[]{:S(2)}) %collective-permute-start.15) | collective-permute-done | bytes 106528 | tf_op jit(solution)/shard_map/ppermute | solution.py:20
  57.0 0.6 copy-done.9
  57.7 2.1 %collective-permute-done.12.refs_2_ = bf16[3,384,128]{2,1,0:T(8,128)(2,1)S(1)} collective-permute-done((bf16[3,384,128]{2,1,0:T(8,128)(2,1)S(1)}, bf16[3,384,128]{2,1,0:T(8,128)(2,1)S(1)}, u32[]{:S(2)}, u32[]{:S(2)}) %collective-permute-start.12) | collective-permute-done | bytes 294944 | tf_op jit(solution)/shard_map/ppermute | solution.py:20
  59.8 1.5 %collective-permute-start.13 = (bf16[3,384,128]{2,1,0:T(8,128)(2,1)S(1)}, bf16[3,384,128]{2,1,0:T(8,128)(2,1)S(1)}, u32[]{:S(2)}, u32[]{:S(2)}) collective-permute-start(bf16[3,384,128]{2,1,0:T(8,128)(2,1)S(1)} %get-tuple-element.80.refs_0_), channel_id=1, source_target_pairs={{0,2},{1,3},{2,0},{3,1},{4,6},{5,7},{6,4},{7,5},{8,10},{9,11},{10,... | collective-permute-start | bytes 884744 | tf_op jit(solution)/shard_map/ppermute | solution.py:20
  61.4 0.7 assemble.2.grad_ref.refs_1_.refs_3_
  62.2 0.8 input_grad.3
  63.0 0.5 collective-permute-start.18
  63.5 3.0 %input_grad.4 = (bf16[384,512]{1,0:T(8,128)(2,1)}, bf16[384,512]{1,0:T(8,128)(2,1)S(1)}, bf16[384,512]{1,0:T(8,128)(2,1)S(1)}) custom-call(bf16[384,1536]{1,0:T(8,128)(2,1)S(1)} %assemble.2.grad_ref.refs_1_.refs_3_, bf16[3,512,2048]{2,1,0:T(8,128)(2,1)S(1)} %bitcast.9), custom_call_target="tpu_custom_call" | custom-call | flops 1 | bytes 1 | tf_op jit(solution)/shard_map/input_grad/pallas_call | solution.py:399
  66.5 2.8 %collective-permute-done.13.refs_2_ = bf16[3,384,128]{2,1,0:T(8,128)(2,1)S(1)} collective-permute-done((bf16[3,384,128]{2,1,0:T(8,128)(2,1)S(1)}, bf16[3,384,128]{2,1,0:T(8,128)(2,1)S(1)}, u32[]{:S(2)}, u32[]{:S(2)}) %collective-permute-start.13) | collective-permute-done | bytes 294944 | tf_op jit(solution)/shard_map/ppermute | solution.py:20
  69.6 1.2 collective-permute-done.17.refs_3_
  70.8 0.7 assemble.3.grad_ref.refs_0_.refs_2_
  71.6 4.0 %input_grad.5 = (bf16[384,512]{1,0:T(8,128)(2,1)S(1)}, bf16[384,512]{1,0:T(8,128)(2,1)S(1)}, bf16[384,512]{1,0:T(8,128)(2,1)S(1)}, bf16[384,512]{1,0:T(8,128)(2,1)S(1)}) custom-call(bf16[384,1536]{1,0:T(8,128)(2,1)S(1)} %assemble.3.grad_ref.refs_0_.refs_2_, bf16[3,512,2048]{2,1,0:T(8,128)(2,1)S(1)} %bitcast.10), custom_call_target="tpu_custom_call" | custom-call | flops 1 | bytes 1 | tf_op jit(solution)/shard_map/input_grad/pallas_call | solution.py:399
  75.6 0.8 add_convert_fusion.11
  76.4 1.6 %collective-permute-start.20 = (bf16[384,512]{1,0:T(8,128)(2,1)}, bf16[384,512]{1,0:T(8,128)(2,1)}, u32[]{:S(2)}, u32[]{:S(2)}) collective-permute-start(bf16[384,512]{1,0:T(8,128)(2,1)} %add_convert_fusion.11), channel_id=1, source_target_pairs={{0,8},{8,0},{16,24},{24,16},{1,9},{9,1},{17,25},{25,17},{2,10},{10... | collective-permute-start | bytes 1179656 | tf_op jit(solution)/shard_map/ppermute | solution.py:20
  78.0 0.5 collective-permute-start.21
  78.5 5.0 %collective-permute-done.19 = bf16[384,512]{1,0:T(8,128)(2,1)} collective-permute-done((bf16[384,512]{1,0:T(8,128)(2,1)}, bf16[384,512]{1,0:T(8,128)(2,1)}, u32[]{:S(2)}, u32[]{:S(2)}) %collective-permute-start.19) | collective-permute-done | bytes 393248 | tf_op jit(solution)/shard_map/ppermute | solution.py:20
  83.5 1.1 add_convert_fusion.10
  84.7 1.6 %collective-permute-start.22 = (bf16[384,512]{1,0:T(8,128)(2,1)S(1)}, bf16[384,512]{1,0:T(8,128)(2,1)S(1)}, u32[]{:S(2)}, u32[]{:S(2)}) collective-permute-start(bf16[384,512]{1,0:T(8,128)(2,1)S(1)} %add_convert_fusion.10), channel_id=1, source_target_pairs={{0,8},{8,0},{16,24},{24,16},{1,9},{9,1},{17,25},{25,17},{2,10},{10... | collective-permute-start | bytes 1179656 | tf_op jit(solution)/shard_map/ppermute | solution.py:20
  86.3 0.5 collective-permute-start.24
  86.8 1.9 %collective-permute-done.20 = bf16[384,512]{1,0:T(8,128)(2,1)} collective-permute-done((bf16[384,512]{1,0:T(8,128)(2,1)}, bf16[384,512]{1,0:T(8,128)(2,1)}, u32[]{:S(2)}, u32[]{:S(2)}) %collective-permute-start.20) | collective-permute-done | bytes 393248 | tf_op jit(solution)/shard_map/ppermute | solution.py:20
  88.7 1.2 add_convert_fusion.9
  89.9 0.7 collective-permute-start.23
  90.6 1.2 collective-permute-done.21
  92.0 4.3 %collective-permute-done.22 = bf16[384,512]{1,0:T(8,128)(2,1)S(1)} collective-permute-done((bf16[384,512]{1,0:T(8,128)(2,1)S(1)}, bf16[384,512]{1,0:T(8,128)(2,1)S(1)}, u32[]{:S(2)}, u32[]{:S(2)}) %collective-permute-start.22) | collective-permute-done | bytes 393248 | tf_op jit(solution)/shard_map/ppermute | solution.py:20
  96.5 6.6 %collective-permute-start.25 = (bf16[384,512]{1,0:T(8,128)(2,1)S(1)}, bf16[384,512]{1,0:T(8,128)(2,1)S(1)}, u32[]{:S(2)}, u32[]{:S(2)}) collective-permute-start(bf16[384,512]{1,0:T(8,128)(2,1)S(1)} %get-tuple-element.122), channel_id=1, source_target_pairs={{0,8},{8,0},{16,24},{24,16},{1,9},{9,1},{17,25},{25,17},{2,10},{10... | collective-permute-start | bytes 1179656 | tf_op jit(solution)/shard_map/ppermute | solution.py:20
  103.2 0.7 collective-permute-start.26
  103.9 5.6 %weight_grad.2 = (f32[3,512,2048]{2,1,0:T(8,128)}, f32[8,128]{1,0:T(8,128)S(1)}) custom-call(bf16[384,1536]{1,0:T(8,128)(2,1)S(1)} %assemble.3.grad_ref.refs_0_.refs_2_, bf16[384,1536]{1,0:T(8,128)(2,1)S(1)} %assemble.2.grad_ref.refs_1_.refs_3_, bf16[384,2048]{1,0:T(8,128)(2,1)S(1)} %copy-done.3, bf16[384,2048]{1,0:T(8,128)(2,1)S(1)} %copy-done.5), custom_call_target="tpu_custom_call" | custom-call | flops 1 | bytes 1 | tf_op jit(solution)/shard_map/weight_grad/pallas_call | solution.py:456
  109.6 0.4 collective-permute-done.25
  110.3 3.6 %collective-permute-start.27 = (bf16[384,512]{1,0:T(8,128)(2,1)S(1)}, bf16[384,512]{1,0:T(8,128)(2,1)S(1)}, u32[]{:S(2)}, u32[]{:S(2)}) collective-permute-start(bf16[384,512]{1,0:T(8,128)(2,1)S(1)} %get-tuple-element.120), channel_id=1, source_target_pairs={{0,8},{8,0},{16,24},{24,16},{1,9},{9,1},{17,25},{25,17},{2,10},{10... | collective-permute-start | bytes 1179656 | tf_op jit(solution)/shard_map/ppermute | solution.py:20
  113.9 0.7 collective-permute-start.28
  114.6 0.6 split.3
  115.3 1.6 %collective-permute-start.30 = (bf16[2,128,128]{2,1,0:T(8,128)(2,1)S(1)}, bf16[2,128,128]{2,1,0:T(8,128)(2,1)S(1)}, u32[]{:S(2)}, u32[]{:S(2)}) collective-permute-start(bf16[2,128,128]{2,1,0:T(8,128)(2,1)S(1)} %get-tuple-element.113), channel_id=1, source_target_pairs={{0,2},{1,3},{2,0},{3,1},{4,6},{5,7},{6,4},{7,5},{8,10},{9,11},{10,... | collective-permute-start | bytes 196616 | tf_op jit(solution)/shard_map/ppermute | solution.py:20
  117.2 2.7 %collective-permute-done.27 = bf16[384,512]{1,0:T(8,128)(2,1)S(1)} collective-permute-done((bf16[384,512]{1,0:T(8,128)(2,1)S(1)}, bf16[384,512]{1,0:T(8,128)(2,1)S(1)}, u32[]{:S(2)}, u32[]{:S(2)}) %collective-permute-start.27) | collective-permute-done | bytes 393248 | tf_op jit(solution)/shard_map/ppermute | solution.py:20
  120.0 0.7 collective-permute-start.32
  120.8 4.7 %collective-permute-start.33 = (bf16[384,512]{1,0:T(8,128)(2,1)S(1)}, bf16[384,512]{1,0:T(8,128)(2,1)S(1)}, u32[]{:S(2)}, u32[]{:S(2)}) collective-permute-start(bf16[384,512]{1,0:T(8,128)(2,1)S(1)} %add_convert_fusion.1), channel_id=1, source_target_pairs={{0,8},{8,0},{16,24},{24,16},{1,9},{9,1},{17,25},{25,17},{2,10},{10... | collective-permute-start | bytes 1179656 | tf_op jit(solution)/shard_map/ppermute | solution.py:20
  125.5 5.6 %weight_grad.3 = (f32[3,512,2048]{2,1,0:T(8,128)}, f32[8,128]{1,0:T(8,128)S(1)}) custom-call(f32[3,512,2048]{2,1,0:T(8,128)} %get-tuple-element.98.refs_0_, f32[8,128]{1,0:T(8,128)S(1)} %get-tuple-element.99.refs_1_, bf16[384,1536]{1,0:T(8,128)(2,1)S(1)} %assemble.3.grad_ref.refs_0_.refs_2_, ...), custom_call_target="tpu_custom_call", output_to_operand_aliasing={{0}: (0, {})} | custom-call | flops 1 | bytes 1 | tf_op jit(solution)/shard_map/weight_grad/pallas_call | solution.py:456
  131.3 2.2 %collective-permute-start.34 = (bf16[384,512]{1,0:T(8,128)(2,1)S(1)}, bf16[384,512]{1,0:T(8,128)(2,1)S(1)}, u32[]{:S(2)}, u32[]{:S(2)}) collective-permute-start(bf16[384,512]{1,0:T(8,128)(2,1)S(1)} %add_convert_fusion), channel_id=1, source_target_pairs={{0,8},{8,0},{16,24},{24,16},{1,9},{9,1},{17,25},{25,17},{2,10},{10... | collective-permute-start | bytes 1179656 | tf_op jit(solution)/shard_map/ppermute | solution.py:20
  133.6 1.4 join.1
  135.0 5.5 %collective-permute-done.34 = bf16[384,512]{1,0:T(8,128)(2,1)S(1)} collective-permute-done((bf16[384,512]{1,0:T(8,128)(2,1)S(1)}, bf16[384,512]{1,0:T(8,128)(2,1)S(1)}, u32[]{:S(2)}, u32[]{:S(2)}) %collective-permute-start.34) | collective-permute-done | bytes 393248 | tf_op jit(solution)/shard_map/ppermute | solution.py:20
  140.5 1.3 pad_maximum_fusion
  (69 shorter events, 2.9 us)
Async XLA Ops:
  0.7 1.4 copy-start.2
  2.1 3.7 %copy-start.6 = (bf16[96,1024]{1,0:T(8,128)(2,1)S(1)}, bf16[96,1024]{1,0:T(8,128)(2,1)}, u32[]{:S(2)}) copy-start(bf16[96,1024]{1,0:T(8,128)(2,1)} %up_ref.1) | copy-start | bytes 589828
  2.7 15.0 %collective-permute-start = (bf16[128,2048]{1,0:T(8,128)(2,1)S(1)}, bf16[128,2048]{1,0:T(8,128)(2,1)S(1)}, u32[]{:S(2)}, u32[]{:S(2)}) collective-permute-start(bf16[128,2048]{1,0:T(8,128)(2,1)S(1)} %get-tuple-element.63), channel_id=1, source_target_pairs={{0,4},{4,0},{1,5},{5,1},{2,6},{6,2},{3,7},{7,3},{8,12},{12,8},{9,1... | collective-permute-start | bytes 1572872 | tf_op jit(solution)/shard_map/ppermute | solution.py:20
  6.4 8.5 %collective-permute-start.3 = (bf16[2,96,128]{2,1,0:T(8,128)(2,1)S(1)}, bf16[2,96,128]{2,1,0:T(8,128)(2,1)S(1)}, u32[]{:S(2)}, u32[]{:S(2)}) collective-permute-start(bf16[2,96,128]{2,1,0:T(8,128)(2,1)S(1)} %get-tuple-element.68), channel_id=1, source_target_pairs={{0,1},{1,0},{2,3},{3,2},{4,5},{5,4},{6,7},{7,6},{8,9},{9,8},{10,11... | collective-permute-start | bytes 147464 | tf_op jit(solution)/shard_map/ppermute | solution.py:20
  6.5 8.4 %collective-permute-start.4 = (bf16[2,96,128]{2,1,0:T(8,128)(2,1)S(1)}, bf16[2,96,128]{2,1,0:T(8,128)(2,1)S(1)}, u32[]{:S(2)}, u32[]{:S(2)}) collective-permute-start(bf16[2,96,128]{2,1,0:T(8,128)(2,1)S(1)} %get-tuple-element.69), channel_id=1, source_target_pairs={{0,2},{1,3},{2,0},{3,1},{4,6},{5,7},{6,4},{7,5},{8,10},{9,11},{10,... | collective-permute-start | bytes 147464 | tf_op jit(solution)/shard_map/ppermute | solution.py:20
  8.0 6.9 %collective-permute-start.5 = (bf16[2,96,128]{2,1,0:T(8,128)(2,1)S(1)}, bf16[2,96,128]{2,1,0:T(8,128)(2,1)S(1)}, u32[]{:S(2)}, u32[]{:S(2)}) collective-permute-start(bf16[2,96,128]{2,1,0:T(8,128)(2,1)S(1)} %get-tuple-element.70), channel_id=1, source_target_pairs={{0,3},{1,2},{2,1},{3,0},{4,7},{5,6},{6,5},{7,4},{8,11},{9,10},{10,... | collective-permute-start | bytes 147464 | tf_op jit(solution)/shard_map/ppermute | solution.py:20
  8.3 2.8 %copy-start = (bf16[512,3,2048]{2,0,1:T(8,128)(2,1)S(1)}, bf16[512,3,2048]{2,0,1:T(8,128)(2,1)}, u32[]{:S(2)}) copy-start(bf16[512,3,2048]{2,0,1:T(8,128)(2,1)} %param.5) | copy-start | bytes 18874372
  11.1 22.4 %copy-start.1 = (bf16[512,3,2048]{2,0,1:T(8,128)(2,1)S(1)}, bf16[512,3,2048]{2,0,1:T(8,128)(2,1)}, u32[]{:S(2)}) copy-start(bf16[512,3,2048]{2,0,1:T(8,128)(2,1)} %param.5) | copy-start | bytes 18874372
  17.7 3.3 %collective-permute-start.6 = (bf16[2,3,384,128]{3,2,1,0:T(8,128)(2,1)S(1)}, bf16[2,3,384,128]{3,2,1,0:T(8,128)(2,1)S(1)}, u32[]{:S(2)}, u32[]{:S(2)}) collective-permute-start(bf16[2,3,384,128]{3,2,1,0:T(8,128)(2,1)S(1)} %get-tuple-element.71), channel_id=1, source_target_pairs={{0,1},{1,0},{2,3},{3,2},{4,5},{5,4},{6,7},{7,6},{8,9},{9,8},{10,11... | collective-permute-start | bytes 1769480 | tf_op jit(solution)/shard_map/ppermute | solution.py:20
  17.7 14.3 %collective-permute-start.2 = (bf16[128,2048]{1,0:T(8,128)(2,1)S(1)}, bf16[128,2048]{1,0:T(8,128)(2,1)S(1)}, u32[]{:S(2)}, u32[]{:S(2)}) collective-permute-start(bf16[128,2048]{1,0:T(8,128)(2,1)S(1)} %get-tuple-element.65), channel_id=1, source_target_pairs={{0,4},{4,0},{1,5},{5,1},{2,6},{6,2},{3,7},{7,3},{8,12},{12,8},{9,1... | collective-permute-start | bytes 1572872 | tf_op jit(solution)/shard_map/ppermute | solution.py:20
  19.4 14.1 %collective-permute-start.1 = (bf16[128,2048]{1,0:T(8,128)(2,1)S(1)}, bf16[128,2048]{1,0:T(8,128)(2,1)S(1)}, u32[]{:S(2)}, u32[]{:S(2)}) collective-permute-start(bf16[128,2048]{1,0:T(8,128)(2,1)S(1)} %collective-permute-done.refs_0_), channel_id=1, source_target_pairs={{0,8},{8,0},{16,24},{24,16},{1,9},{9,1},{17,25},{25,17},{2,10},{10... | collective-permute-start | bytes 1572872 | tf_op jit(solution)/shard_map/ppermute | solution.py:20
  21.1 27.6 %copy-start.11 = (f32[7,64]{1,0:T(8,128)S(1)}, f32[7,64]{1,0:T(8,128)}, u32[]{:S(2)}) copy-start(f32[7,64]{1,0:T(8,128)} %taps_ref.1) | copy-start | bytes 5380
  21.1 10.9 %collective-permute-start.7 = (bf16[1,3,384,128]{3,2,1,0:T(8,128)(2,1)S(1)}, bf16[1,3,384,128]{3,2,1,0:T(8,128)(2,1)S(1)}, u32[]{:S(2)}, u32[]{:S(2)}) collective-permute-start(bf16[1,3,384,128]{3,2,1,0:T(8,128)(2,1)S(1)} %add_convert_fusion.13), channel_id=1, source_target_pairs={{0,2},{1,3},{2,0},{3,1},{4,6},{5,7},{6,4},{7,5},{8,10},{9,11},{10,... | collective-permute-start | bytes 884744 | tf_op jit(solution)/shard_map/ppermute | solution.py:20
  37.4 24.8 %copy-start.4 = (bf16[384,2048]{1,0:T(8,128)(2,1)}, bf16[384,2048]{1,0:T(8,128)(2,1)S(1)}, u32[]{:S(2)}) copy-start(bf16[384,2048]{1,0:T(8,128)(2,1)S(1)} %get-tuple-element.97.refs_3_.refs_5_) | copy-start | bytes 4718596
  37.4 2.1 %collective-permute-start.8 = (bf16[2,3,384,128]{3,2,1,0:T(8,128)(2,1)S(1)}, bf16[2,3,384,128]{3,2,1,0:T(8,128)(2,1)S(1)}, u32[]{:S(2)}, u32[]{:S(2)}) collective-permute-start(bf16[2,3,384,128]{3,2,1,0:T(8,128)(2,1)S(1)} %get-tuple-element.74), channel_id=1, source_target_pairs={{0,1},{1,0},{2,3},{3,2},{4,5},{5,4},{6,7},{7,6},{8,9},{9,8},{10,11... | collective-permute-start | bytes 1769480 | tf_op jit(solution)/shard_map/ppermute | solution.py:20
  39.6 9.1 %collective-permute-start.10 = (bf16[1,3,384,128]{3,2,1,0:T(8,128)(2,1)S(1)}, bf16[1,3,384,128]{3,2,1,0:T(8,128)(2,1)S(1)}, u32[]{:S(2)}, u32[]{:S(2)}) collective-permute-start(bf16[1,3,384,128]{3,2,1,0:T(8,128)(2,1)S(1)} %add_convert_fusion.12), channel_id=1, source_target_pairs={{0,2},{1,3},{2,0},{3,1},{4,6},{5,7},{6,4},{7,5},{8,10},{9,11},{10,... | collective-permute-start | bytes 884744 | tf_op jit(solution)/shard_map/ppermute | solution.py:20
  41.7 4.7 %collective-permute-start.9 = (bf16[384,128]{1,0:T(8,128)(2,1)S(1)}, bf16[384,128]{1,0:T(8,128)(2,1)S(1)}, u32[]{:S(2)}, u32[]{:S(2)}) collective-permute-start(bf16[384,128]{1,0:T(8,128)(2,1)S(1)} %get-tuple-element.77), channel_id=1, source_target_pairs={{0,4},{4,0},{1,5},{5,1},{2,6},{6,2},{3,7},{7,3},{8,12},{12,8},{9,1... | collective-permute-start | bytes 294920 | tf_op jit(solution)/shard_map/ppermute | solution.py:20
  50.3 12.7 %copy-start.7 = (bf16[416,128]{1,0:T(8,128)(2,1)}, bf16[416,128]{1,0:T(8,128)(2,1)S(1)}, u32[]{:S(2)}) copy-start(bf16[416,128]{1,0:T(8,128)(2,1)S(1)} %get-tuple-element.110.refs_0_) | copy-start | bytes 319492
  50.3 7.4 %collective-permute-start.11 = (bf16[3,384,128]{2,1,0:T(8,128)(2,1)S(1)}, bf16[3,384,128]{2,1,0:T(8,128)(2,1)S(1)}, u32[]{:S(2)}, u32[]{:S(2)}) collective-permute-start(bf16[3,384,128]{2,1,0:T(8,128)(2,1)S(1)} %get-tuple-element.80.refs_0_), channel_id=1, source_target_pairs={{0,1},{1,0},{2,3},{3,2},{4,5},{5,4},{6,7},{7,6},{8,9},{9,8},{10,11... | collective-permute-start | bytes 884744 | tf_op jit(solution)/shard_map/ppermute | solution.py:20
  50.4 7.3 %collective-permute-start.14 = (bf16[3,384,128]{2,1,0:T(8,128)(2,1)S(1)}, bf16[3,384,128]{2,1,0:T(8,128)(2,1)S(1)}, u32[]{:S(2)}, u32[]{:S(2)}) collective-permute-start(bf16[3,384,128]{2,1,0:T(8,128)(2,1)S(1)} %get-tuple-element.79.refs_0_), channel_id=1, source_target_pairs={{0,1},{1,0},{2,3},{3,2},{4,5},{5,4},{6,7},{7,6},{8,9},{9,8},{10,11... | collective-permute-start | bytes 884744 | tf_op jit(solution)/shard_map/ppermute | solution.py:20
  50.8 9.0 %collective-permute-start.12 = (bf16[3,384,128]{2,1,0:T(8,128)(2,1)S(1)}, bf16[3,384,128]{2,1,0:T(8,128)(2,1)S(1)}, u32[]{:S(2)}, u32[]{:S(2)}) collective-permute-start(bf16[3,384,128]{2,1,0:T(8,128)(2,1)S(1)} %get-tuple-element.79.refs_0_), channel_id=1, source_target_pairs={{0,2},{1,3},{2,0},{3,1},{4,6},{5,7},{6,4},{7,5},{8,10},{9,11},{10,... | collective-permute-start | bytes 884744 | tf_op jit(solution)/shard_map/ppermute | solution.py:20
  52.3 4.7 %collective-permute-start.15 = (bf16[416,128]{1,0:T(8,128)(2,1)S(1)}, bf16[416,128]{1,0:T(8,128)(2,1)S(1)}, u32[]{:S(2)}, u32[]{:S(2)}) collective-permute-start(bf16[416,128]{1,0:T(8,128)(2,1)S(1)} %get-tuple-element.81), channel_id=1, source_target_pairs={{0,4},{4,0},{1,5},{5,1},{2,6},{6,2},{3,7},{7,3},{8,12},{12,8},{9,1... | collective-permute-start | bytes 319496 | tf_op jit(solution)/shard_map/ppermute | solution.py:20
  57.0 0.6 copy-start.9
  59.8 1.6 %collective-permute-start.16 = (bf16[3,384,128]{2,1,0:T(8,128)(2,1)S(1)}, bf16[3,384,128]{2,1,0:T(8,128)(2,1)S(1)}, u32[]{:S(2)}, u32[]{:S(2)}) collective-permute-start(bf16[3,384,128]{2,1,0:T(8,128)(2,1)S(1)} %collective-permute-done.12.refs_2_), channel_id=1, source_target_pairs={{0,1},{1,0},{2,3},{3,2},{4,5},{5,4},{6,7},{7,6},{8,9},{9,8},{10,11... | collective-permute-start | bytes 884744 | tf_op jit(solution)/shard_map/ppermute | solution.py:20
  59.8 9.4 %collective-permute-start.13 = (bf16[3,384,128]{2,1,0:T(8,128)(2,1)S(1)}, bf16[3,384,128]{2,1,0:T(8,128)(2,1)S(1)}, u32[]{:S(2)}, u32[]{:S(2)}) collective-permute-start(bf16[3,384,128]{2,1,0:T(8,128)(2,1)S(1)} %get-tuple-element.80.refs_0_), channel_id=1, source_target_pairs={{0,2},{1,3},{2,0},{3,1},{4,6},{5,7},{6,4},{7,5},{8,10},{9,11},{10,... | collective-permute-start | bytes 884744 | tf_op jit(solution)/shard_map/ppermute | solution.py:20
  63.0 12.6 %collective-permute-start.18 = (bf16[384,512]{1,0:T(8,128)(2,1)S(1)}, bf16[384,512]{1,0:T(8,128)(2,1)S(1)}, u32[]{:S(2)}, u32[]{:S(2)}) collective-permute-start(bf16[384,512]{1,0:T(8,128)(2,1)S(1)} %input_grad.3), channel_id=1, source_target_pairs={{0,4},{4,0},{1,5},{5,1},{2,6},{6,2},{3,7},{7,3},{8,12},{12,8},{9,1... | collective-permute-start | bytes 1179656 | tf_op jit(solution)/shard_map/ppermute | solution.py:20
  66.5 9.1 %copy-start.12 = (bf16[384,512]{1,0:T(8,128)(2,1)}, bf16[384,512]{1,0:T(8,128)(2,1)S(1)}, u32[]{:S(2)}) copy-start(bf16[384,512]{1,0:T(8,128)(2,1)S(1)} %get-tuple-element.102) | copy-start | bytes 1179652
  66.5 9.1 %copy-start.13 = (bf16[384,512]{1,0:T(8,128)(2,1)}, bf16[384,512]{1,0:T(8,128)(2,1)S(1)}, u32[]{:S(2)}) copy-start(bf16[384,512]{1,0:T(8,128)(2,1)S(1)} %get-tuple-element.93) | copy-start | bytes 1179652
  69.3 1.6 %collective-permute-start.17 = (bf16[3,384,128]{2,1,0:T(8,128)(2,1)S(1)}, bf16[3,384,128]{2,1,0:T(8,128)(2,1)S(1)}, u32[]{:S(2)}, u32[]{:S(2)}) collective-permute-start(bf16[3,384,128]{2,1,0:T(8,128)(2,1)S(1)} %collective-permute-done.13.refs_2_), channel_id=1, source_target_pairs={{0,1},{1,0},{2,3},{3,2},{4,5},{5,4},{6,7},{7,6},{8,9},{9,8},{10,11... | collective-permute-start | bytes 884744 | tf_op jit(solution)/shard_map/ppermute | solution.py:20
  69.3 14.3 %collective-permute-start.19 = (bf16[384,512]{1,0:T(8,128)(2,1)}, bf16[384,512]{1,0:T(8,128)(2,1)}, u32[]{:S(2)}, u32[]{:S(2)}) collective-permute-start(bf16[384,512]{1,0:T(8,128)(2,1)} %get-tuple-element.89), channel_id=1, source_target_pairs={{0,4},{4,0},{1,5},{5,1},{2,6},{6,2},{3,7},{7,3},{8,12},{12,8},{9,1... | collective-permute-start | bytes 1179656 | tf_op jit(solution)/shard_map/ppermute | solution.py:20
  76.4 12.3 %collective-permute-start.20 = (bf16[384,512]{1,0:T(8,128)(2,1)}, bf16[384,512]{1,0:T(8,128)(2,1)}, u32[]{:S(2)}, u32[]{:S(2)}) collective-permute-start(bf16[384,512]{1,0:T(8,128)(2,1)} %add_convert_fusion.11), channel_id=1, source_target_pairs={{0,8},{8,0},{16,24},{24,16},{1,9},{9,1},{17,25},{25,17},{2,10},{10... | collective-permute-start | bytes 1179656 | tf_op jit(solution)/shard_map/ppermute | solution.py:20
  78.0 13.8 %collective-permute-start.21 = (bf16[384,512]{1,0:T(8,128)(2,1)}, bf16[384,512]{1,0:T(8,128)(2,1)S(1)}, u32[]{:S(2)}, u32[]{:S(2)}) collective-permute-start(bf16[384,512]{1,0:T(8,128)(2,1)} %copy-done.13), channel_id=1, source_target_pairs={{0,4},{4,0},{1,5},{5,1},{2,6},{6,2},{3,7},{7,3},{8,12},{12,8},{9,1... | collective-permute-start | bytes 1179656 | tf_op jit(solution)/shard_map/ppermute | solution.py:20
  78.5 25.3 %copy-start.3 = (bf16[384,2048]{1,0:T(8,128)(2,1)S(1)}, bf16[384,2048]{1,0:T(8,128)(2,1)}, u32[]{:S(2)}) copy-start(bf16[384,2048]{1,0:T(8,128)(2,1)} %refs_4_.1) | copy-start | bytes 4718596
  78.5 25.3 %copy-start.5 = (bf16[384,2048]{1,0:T(8,128)(2,1)S(1)}, bf16[384,2048]{1,0:T(8,128)(2,1)}, u32[]{:S(2)}) copy-start(bf16[384,2048]{1,0:T(8,128)(2,1)} %copy-done.4) | copy-start | bytes 4718596
  84.7 11.6 %collective-permute-start.22 = (bf16[384,512]{1,0:T(8,128)(2,1)S(1)}, bf16[384,512]{1,0:T(8,128)(2,1)S(1)}, u32[]{:S(2)}, u32[]{:S(2)}) collective-permute-start(bf16[384,512]{1,0:T(8,128)(2,1)S(1)} %add_convert_fusion.10), channel_id=1, source_target_pairs={{0,8},{8,0},{16,24},{24,16},{1,9},{9,1},{17,25},{25,17},{2,10},{10... | collective-permute-start | bytes 1179656 | tf_op jit(solution)/shard_map/ppermute | solution.py:20
  86.3 23.2 %collective-permute-start.24 = (bf16[384,512]{1,0:T(8,128)(2,1)}, bf16[384,512]{1,0:T(8,128)(2,1)S(1)}, u32[]{:S(2)}, u32[]{:S(2)}) collective-permute-start(bf16[384,512]{1,0:T(8,128)(2,1)} %copy-done.12), channel_id=1, source_target_pairs={{0,4},{4,0},{1,5},{5,1},{2,6},{6,2},{3,7},{7,3},{8,12},{12,8},{9,1... | collective-permute-start | bytes 1179656 | tf_op jit(solution)/shard_map/ppermute | solution.py:20
  89.9 6.4 %collective-permute-start.23 = (bf16[384,512]{1,0:T(8,128)(2,1)S(1)}, bf16[384,512]{1,0:T(8,128)(2,1)S(1)}, u32[]{:S(2)}, u32[]{:S(2)}) collective-permute-start(bf16[384,512]{1,0:T(8,128)(2,1)S(1)} %add_convert_fusion.9), channel_id=1, source_target_pairs={{0,0},{8,16},{16,8},{24,24},{1,1},{9,17},{17,9},{25,25},{2,2},{10,... | collective-permute-start | bytes 1179656 | tf_op jit(solution)/shard_map/ppermute | solution.py:599
  96.5 13.5 %collective-permute-start.25 = (bf16[384,512]{1,0:T(8,128)(2,1)S(1)}, bf16[384,512]{1,0:T(8,128)(2,1)S(1)}, u32[]{:S(2)}, u32[]{:S(2)}) collective-permute-start(bf16[384,512]{1,0:T(8,128)(2,1)S(1)} %get-tuple-element.122), channel_id=1, source_target_pairs={{0,8},{8,0},{16,24},{24,16},{1,9},{9,1},{17,25},{25,17},{2,10},{10... | collective-permute-start | bytes 1179656 | tf_op jit(solution)/shard_map/ppermute | solution.py:20
  103.2 7.0 %collective-permute-start.26 = (bf16[384,512]{1,0:T(8,128)(2,1)S(1)}, bf16[384,512]{1,0:T(8,128)(2,1)S(1)}, u32[]{:S(2)}, u32[]{:S(2)}) collective-permute-start(bf16[384,512]{1,0:T(8,128)(2,1)S(1)} %add_convert_fusion.7), channel_id=1, source_target_pairs={{0,0},{8,16},{16,8},{24,24},{1,1},{9,17},{17,9},{25,25},{2,2},{10,... | collective-permute-start | bytes 1179656 | tf_op jit(solution)/shard_map/ppermute | solution.py:599
  109.5 5.1 %copy-start.8 = (bf16[416,128]{1,0:T(8,128)(2,1)S(1)}, bf16[416,128]{1,0:T(8,128)(2,1)}, u32[]{:S(2)}) copy-start(bf16[416,128]{1,0:T(8,128)(2,1)} %copy-done.7) | copy-start | bytes 319492
  109.5 5.1 %copy-start.10 = (bf16[416,128]{1,0:T(8,128)(2,1)S(1)}, bf16[416,128]{1,0:T(8,128)(2,1)}, u32[]{:S(2)}) copy-start(bf16[416,128]{1,0:T(8,128)(2,1)} %copy-done.9) | copy-start | bytes 319492
  110.3 9.5 %collective-permute-start.27 = (bf16[384,512]{1,0:T(8,128)(2,1)S(1)}, bf16[384,512]{1,0:T(8,128)(2,1)S(1)}, u32[]{:S(2)}, u32[]{:S(2)}) collective-permute-start(bf16[384,512]{1,0:T(8,128)(2,1)S(1)} %get-tuple-element.120), channel_id=1, source_target_pairs={{0,8},{8,0},{16,24},{24,16},{1,9},{9,1},{17,25},{25,17},{2,10},{10... | collective-permute-start | bytes 1179656 | tf_op jit(solution)/shard_map/ppermute | solution.py:20
  113.9 6.8 %collective-permute-start.28 = (bf16[384,512]{1,0:T(8,128)(2,1)S(1)}, bf16[384,512]{1,0:T(8,128)(2,1)S(1)}, u32[]{:S(2)}, u32[]{:S(2)}) collective-permute-start(bf16[384,512]{1,0:T(8,128)(2,1)S(1)} %add_convert_fusion.4), channel_id=1, source_target_pairs={{0,0},{8,16},{16,8},{24,24},{1,1},{9,17},{17,9},{25,25},{2,2},{10,... | collective-permute-start | bytes 1179656 | tf_op jit(solution)/shard_map/ppermute | solution.py:599
  115.2 16.0 %collective-permute-start.29 = (bf16[2,128,128]{2,1,0:T(8,128)(2,1)S(1)}, bf16[2,128,128]{2,1,0:T(8,128)(2,1)S(1)}, u32[]{:S(2)}, u32[]{:S(2)}) collective-permute-start(bf16[2,128,128]{2,1,0:T(8,128)(2,1)S(1)} %get-tuple-element.112), channel_id=1, source_target_pairs={{0,1},{1,0},{2,3},{3,2},{4,5},{5,4},{6,7},{7,6},{8,9},{9,8},{10,11... | collective-permute-start | bytes 196616 | tf_op jit(solution)/shard_map/ppermute | solution.py:20
  115.3 15.9 %collective-permute-start.30 = (bf16[2,128,128]{2,1,0:T(8,128)(2,1)S(1)}, bf16[2,128,128]{2,1,0:T(8,128)(2,1)S(1)}, u32[]{:S(2)}, u32[]{:S(2)}) collective-permute-start(bf16[2,128,128]{2,1,0:T(8,128)(2,1)S(1)} %get-tuple-element.113), channel_id=1, source_target_pairs={{0,2},{1,3},{2,0},{3,1},{4,6},{5,7},{6,4},{7,5},{8,10},{9,11},{10,... | collective-permute-start | bytes 196616 | tf_op jit(solution)/shard_map/ppermute | solution.py:20
  116.8 14.3 %collective-permute-start.31 = (bf16[2,128,128]{2,1,0:T(8,128)(2,1)S(1)}, bf16[2,128,128]{2,1,0:T(8,128)(2,1)S(1)}, u32[]{:S(2)}, u32[]{:S(2)}) collective-permute-start(bf16[2,128,128]{2,1,0:T(8,128)(2,1)S(1)} %get-tuple-element.114), channel_id=1, source_target_pairs={{0,3},{1,2},{2,1},{3,0},{4,7},{5,6},{6,5},{7,4},{8,11},{9,10},{10,... | collective-permute-start | bytes 196616 | tf_op jit(solution)/shard_map/ppermute | solution.py:20
  120.0 11.2 %collective-permute-start.32 = (bf16[384,512]{1,0:T(8,128)(2,1)S(1)}, bf16[384,512]{1,0:T(8,128)(2,1)S(1)}, u32[]{:S(2)}, u32[]{:S(2)}) collective-permute-start(bf16[384,512]{1,0:T(8,128)(2,1)S(1)} %add_convert_fusion.2), channel_id=1, source_target_pairs={{0,0},{8,16},{16,8},{24,24},{1,1},{9,17},{17,9},{25,25},{2,2},{10,... | collective-permute-start | bytes 1179656 | tf_op jit(solution)/shard_map/ppermute | solution.py:599
  120.8 14.1 %collective-permute-start.33 = (bf16[384,512]{1,0:T(8,128)(2,1)S(1)}, bf16[384,512]{1,0:T(8,128)(2,1)S(1)}, u32[]{:S(2)}, u32[]{:S(2)}) collective-permute-start(bf16[384,512]{1,0:T(8,128)(2,1)S(1)} %add_convert_fusion.1), channel_id=1, source_target_pairs={{0,8},{8,0},{16,24},{24,16},{1,9},{9,1},{17,25},{25,17},{2,10},{10... | collective-permute-start | bytes 1179656 | tf_op jit(solution)/shard_map/ppermute | solution.py:20
  131.3 9.2 %collective-permute-start.34 = (bf16[384,512]{1,0:T(8,128)(2,1)S(1)}, bf16[384,512]{1,0:T(8,128)(2,1)S(1)}, u32[]{:S(2)}, u32[]{:S(2)}) collective-permute-start(bf16[384,512]{1,0:T(8,128)(2,1)S(1)} %add_convert_fusion), channel_id=1, source_target_pairs={{0,8},{8,0},{16,24},{24,16},{1,9},{9,1},{17,25},{25,17},{2,10},{10... | collective-permute-start | bytes 1179656 | tf_op jit(solution)/shard_map/ppermute | solution.py:20

commit v12 on v11

--- a/solution.py
+++ b/solution.py
@@ -34,25 +34,33 @@
     return pltpu.CompilerParams(vmem_limit_bytes=(mib if width % LANES == 0 else 56) * MIB)
 
 
-def project_kernel(place, *refs, pieces, count, width):
+def project_kernel(place, *refs, pieces, mode, count, width):
     x_refs = refs[:pieces]
     w_ref, keep_ref, send_ref = refs[pieces : pieces + 3]
     stream = pl.program_id(0)
     core = place[0] % 2
-    if pieces == 1:
-        x = x_refs[0][...]
-    else:
-        x_out = refs[pieces + 3]
-        third = x_refs[0].shape[0]
-        parity = place[2] % 2
+    x = x_refs[0][...]
+    if mode == "cut":
+        last_ref = refs[pieces + 3]
 
         @pl.when(stream == 0)
         def _():
-            x_out[pl.ds(pl.multiple_of(parity * third, third), third), :] = x_refs[0][...]
-            x_out[pl.ds(pl.multiple_of((1 - parity) * third, third), third), :] = x_refs[1][...]
-            x_out[2 * third :, :] = x_refs[2][...]
-
-        x = x_out[...]
+            last_ref[...] = x_refs[0][x.shape[0] - last_ref.shape[0] :, :]
+
+    if mode == "join":
+        joined, rest = refs[pieces + 3 :]
+        third = x.shape[0]
+        parity = place[2] % 2
+
+        @pl.when(stream == 0)
+        def _():
+            joined[pl.ds(pl.multiple_of(parity * third, third), third), :] = x_refs[0][...]
+            joined[pl.ds(pl.multiple_of((1 - parity) * third, third), third), :] = x_refs[1][...]
+            joined[2 * third :, :] = x_refs[2][...]
+            rest[0:third, :] = x_refs[1][...]
+            rest[third:, :] = x_refs[2][...]
+
+        x = rest[...]
     nt = (((1,), (1,)), ((), ()))
     if width % LANES == 0:
         whole = lax.dot_general(x, w_ref[stream], nt, preferred_element_type=jnp.float32).astype(jnp.bfloat16)
@@ -76,29 +84,31 @@
                     send_ref[at, stream] = blocks[j]
 
 
-def project(place, xs, w, count):
-    tok, feat = sum(x.shape[0] for x in xs), xs[0].shape[1]
+def project(place, xs, w, count, mode="plain"):
+    feat = xs[0].shape[1]
+    all_tok = sum(x.shape[0] for x in xs)
+    tok = all_tok - xs[0].shape[0] if mode == "join" else all_tok
     streams, channels, _ = w.shape
     width = channels // count
     part = jax.ShapeDtypeStruct((count // 2, streams, tok, width), jnp.bfloat16)
     wide = width % LANES == 0
     spec = resident(part.shape, width)
-    joined = len(xs) > 1
-    outs = pl.pallas_call(
-        functools.partial(project_kernel, pieces=len(xs), count=count, width=width),
+    more = {"plain": [], "cut": [(tok // 3, feat)], "join": [(all_tok, feat)]}[mode]
+    return pl.pallas_call(
+        functools.partial(project_kernel, pieces=len(xs), mode=mode, count=count, width=width),
         grid_spec=pltpu.PrefetchScalarGridSpec(
             num_scalar_prefetch=1,
             grid=(streams,),
             in_specs=[resident(x.shape, width) for x in xs]
             + [resident(w.shape, width) if wide else pl.BlockSpec((1, channels, feat), lambda s, _: (s, 0, 0))],
-            out_specs=[spec, spec] + [resident((tok, feat), width)] * joined,
+            out_specs=[spec, spec] + [resident(shape, width) for shape in more],
+            scratch_shapes=[pltpu.VMEM((tok, feat), jnp.bfloat16)] if mode == "join" else [],
         ),
-        out_shape=[part, part] + [jax.ShapeDtypeStruct((tok, feat), jnp.bfloat16)] * joined,
+        out_shape=[part, part] + [jax.ShapeDtypeStruct(shape, jnp.bfloat16) for shape in more],
         compiler_params=params(10, width),
         cost_estimate=SMALL,
         name="project",
     )(place, *xs, w)
-    return outs[0], outs[1], outs[2] if joined else xs[0]
 
 
 def in_three(value):
@@ -236,15 +246,14 @@
     )(place, mark, *blocks)
 
 
-def middle_kernel(place, taps_ref, *refs, groups, terms, tile):
+def middle_kernel(place, taps_ref, *refs, pieces, groups, terms, tile):
     up_refs, refs = refs[:groups], refs[groups:]
-    part_refs = refs[: groups * terms]
-    grad_refs = refs[groups * terms : groups * terms + groups]
-    out_refs = refs[groups * terms + groups : groups * terms + 2 * groups]
-    up_s, out_s, q_s, k_s, v_s, mixed_s, gf_s, far_s = refs[groups * terms + 2 * groups :]
+    part_refs, refs = refs[: len(pieces) * terms], refs[len(pieces) * terms :]
+    grad_refs, out_refs = refs[:groups], refs[groups : 2 * groups]
+    up_s, out_s, q_s, k_s, v_s, mixed_s, gf_s, far_s = refs[2 * groups :]
     col = place[1]
-    tok = part_refs[0].shape[2]
-    width = part_refs[0].shape[3]
+    tok, width = up_refs[0].shape
+    parity = place[2] % 2
     total = groups * tok
     tap_groups = taps_ref.shape[1]
     for k, ref in enumerate(up_refs):
@@ -255,21 +264,27 @@
     taps = sum(jnp.dot(term, spread, preferred_element_type=jnp.float32) for term in in_three(taps_ref[...]))
     mixed_s[0:PAD, :] = jnp.zeros((PAD, width), jnp.float32)
     gf_s[total : total + PAD, :] = jnp.zeros((PAD, width), jnp.float32)
-    for k in range(groups):
-        start = (col ^ k) * tok
-        for i in range(tok // tile):
-            inside = slice(i * tile, (i + 1) * tile)
-            rows = pl.ds(pl.multiple_of(start + i * tile, tile), tile)
+    step = 64
+    for piece, (k, thirds) in enumerate(pieces):
+        refs_of = part_refs[piece * terms : (piece + 1) * terms]
+        rows_of = refs_of[0].shape[2]
+        length = rows_of // len(thirds)
+        for i in range(rows_of // step):
+            third = thirds[i * step // length]
+            at = {"own": parity, "other": 1 - parity, "last": 2, "all": 0}[third] * length
+            start = (col ^ k) * tok + at + i * step % length
+            inside = slice(i * step, (i + 1) * step)
+            rows = pl.ds(pl.multiple_of(start, step), step)
             streams = []
             for s in range(3):
                 acc = None
-                for ref in part_refs[k * terms : (k + 1) * terms]:
+                for ref in refs_of:
                     term = ref[0, s, inside, :].astype(jnp.float32)
                     acc = term if acc is None else acc + term
                 streams.append(acc.astype(jnp.bfloat16))
             q_s[rows, :], k_s[rows, :], v_s[rows, :] = streams
             query, key, value = [stream.astype(jnp.float32) for stream in streams]
-            mixed_s[pl.ds(pl.multiple_of(start + i * tile + PAD, PAD), tile), :] = key * value
+            mixed_s[pl.ds(pl.multiple_of(start + PAD, PAD), step), :] = key * value
             gf_s[rows, :] = up_s[rows, :].astype(jnp.float32) * query
     sums = [jnp.zeros((8, width), jnp.float32) for _ in range(KT)]
     for a in range(groups):
@@ -302,18 +317,18 @@
         ref[tok : tok + 32, :] = packed
 
 
-def middle(place, taps, ups, parts, tile):
-    groups, terms = len(parts), len(parts[0])
-    _, _, tok, width = parts[0][0].shape
+def middle(place, taps, ups, pieces, parts, tile):
+    groups, terms = len(ups), len(parts[0])
+    tok, width = ups[0].shape
     total = groups * tok
     whole = lambda *shape: resident(shape, width)
-    one = whole(1, 3, tok, width)
+    ones = [whole(1, 3, terms_of[0].shape[2], width) for terms_of in parts for _ in terms_of]
     outs = pl.pallas_call(
-        functools.partial(middle_kernel, groups=groups, terms=terms, tile=tile),
+        functools.partial(middle_kernel, pieces=pieces, groups=groups, terms=terms, tile=tile),
         grid_spec=pltpu.PrefetchScalarGridSpec(
             num_scalar_prefetch=1,
             grid=(1,),
-            in_specs=[whole(*taps.shape)] + [whole(tok, width)] * groups + [one] * (groups * terms),
+            in_specs=[whole(*taps.shape)] + [whole(tok, width)] * groups + ones,
             out_specs=[whole(3, tok, width)] * groups + [whole(tok + 32, width)] * groups,
             scratch_shapes=[
                 pltpu.VMEM((total, width), jnp.bfloat16),
@@ -479,35 +494,6 @@
     return (first.astype(jnp.float32) + second.astype(jnp.float32)).astype(jnp.bfloat16)
 
 
-def cut_kernel(_, own_ref, last_ref, own_out, last_out):
-    own_out[...] = own_ref[...]
-    last_out[...] = last_ref[...]
-
-
-def cut(place, tokens):
-    tok, feat = tokens.shape
-    if tok % 48 or lax.axis_size("row") % 2:
-        return None
-    third = tok // 3
-    out = jax.ShapeDtypeStruct((third, feat), jnp.bfloat16)
-    return pl.pallas_call(
-        cut_kernel,
-        grid_spec=pltpu.PrefetchScalarGridSpec(
-            num_scalar_prefetch=1,
-            grid=(1,),
-            in_specs=[
-                pl.BlockSpec((third, feat), lambda i, at: (at[2] % 2, 0)),
-                pl.BlockSpec((third, feat), lambda i, at: (2, 0)),
-            ],
-            out_specs=[pl.BlockSpec(memory_space=pltpu.VMEM)] * 2,
-        ),
-        out_shape=[out, out],
-        compiler_params=params(10, LANES),
-        cost_estimate=SMALL,
-        name="cut",
-    )(place, tokens, tokens)
-
-
 def on_device(tokens, weight, taps, upstream):
     n_col = lax.axis_size("col")
     n_depth = lax.axis_size("depth")
@@ -518,30 +504,46 @@
     place = jnp.stack([depth_at, col_at, row_at, col_at * n_depth + depth_at]).astype(jnp.int32)
     w = jnp.transpose(weight, (1, 0, 2))
     width = w.shape[1] // n_depth
-    def project_and_sum(x_pieces, *earlier):
-        keep, send, x = project(place, x_pieces, w, n_depth)
-        near = swap(after(send, *earlier) if earlier else send, "depth", 1)
+    def sum_over_depth(keep, send, near_after=(), far_after=()):
+        near = swap(after(send, *near_after) if near_after else send, "depth", 1)
         pairs = [added(keep[r // 2], near[r // 2])[None] for r in range(2, n_depth, 2)]
-        fars = [swap(pair, "depth", 2 * i + 2) for i, pair in enumerate(pairs)]
-        return x, [keep, near] + fars, pairs, fars
-
-    thirds = cut(place, tokens)
-    first = [[swap(tokens if thirds is None else thirds[0], "col", k)] for k in range(1, n_col)]
+        held = [after(pair, *far_after) if far_after else pair for pair in pairs]
+        fars = [swap(pair, "depth", 2 * i + 2) for i, pair in enumerate(held)]
+        return [keep, near] + fars, pairs, fars
+
+    tok = tokens.shape[0]
+    third = tok // 3
+    cut = tok % 192 == 0 and lax.axis_size("row") % 2 == 0
+    sent_first = lax.dynamic_slice_in_dim(tokens, row_at % 2 * third, third, axis=0) if cut else tokens
+    first = [swap(sent_first, "col", k) for k in range(1, n_col)]
     ups = split_lanes(place, upstream, n_col, n_depth)
     ups = [up if r == 0 else swap(up, "depth", r) for r, up in enumerate(ups)]
-    x, terms, pairs, fars = project_and_sum([tokens], *[piece for of in first for piece in of], *ups[1:])
-    xs, parts = [x], [terms]
+    keep, send, *last = project(place, [tokens], w, n_depth, "cut" if cut else "plain")
+    terms, pairs, fars = sum_over_depth(keep, send, first + ups[1:])
+    xs, pieces, parts = [tokens], [(0, ("all",))], [terms]
     for k in range(1, n_col):
-        x_pieces = first[k - 1]
-        if thirds is not None:
-            x_pieces += [swap(x_pieces[0], "row", 1), swap(after(thirds[1], *x_pieces), "col", k)]
-        x_pieces[-1] = after(x_pieces[-1], *fars)
-        x, terms, pairs, fars = project_and_sum(x_pieces)
+        mine = first[k - 1]
+        if not cut:
+            keep, send = project(place, [after(mine, *fars)], w, n_depth)
+            terms, pairs, fars = sum_over_depth(keep, send)
+            xs.append(mine)
+            pieces.append((k, ("all",)))
+            parts.append(terms)
+            continue
+        other = swap(mine, "row", 1)
+        rest = swap(after(last[0], mine), "col", k)
+        keep, send = project(place, [after(mine, *pairs)], w, n_depth)
+        terms, ahead, ahead_fars = sum_over_depth(keep, send)
+        pieces.append((k, ("own",)))
+        parts.append(terms)
+        keep, send, x = project(place, [mine, other, after(rest, *fars, *ahead)], w, n_depth, "join")
+        terms, pairs, fars = sum_over_depth(keep, send, (), ahead_fars)
+        pieces.append((k, ("other", "last")))
+        parts.append(terms)
         xs.append(x)
-        parts.append(terms)
     ups = merge_rows(place, [after(ups[0], *pairs)] + ups[1:])
     ups = [up if k == 0 else swap(up, "col", k) for k, up in enumerate(ups)]
-    own_grads, blocks = middle(place, taps, ups, parts, local_tok)
+    own_grads, blocks = middle(place, taps, ups, pieces, parts, local_tok)
     nears = [swap(own, "depth", 1) for own in own_grads]
     blocks = [block if k == 0 else swap(block, "col", k) for k, block in enumerate(blocks)]
     beside = nears + blocks[1:]
@@ -567,7 +569,7 @@
             sent.append(([swap(part, "col", k) for part in parts_of[:3]], parts_of))
     held = [parts_of[3:] for _, parts_of in sent]
     sent = [of for of, _ in sent]
-    own_part = input_grad(lhs[0], w, 0, chunks, chunks, width)
+    own_part = input_grad(lhs[0], w, 0, 1, chunks, width)
     outer = (row_at == 0) | (row_at == 3)
     line = lax.axis_size("row") == 4
     inward, across, summed, done = ([None] * chunks for _ in range(4))
@@ -598,6 +600,8 @@
             if 0 <= slot - 1 < chunks:
                 cross = lax.ppermute(across[slot - 1], "row", [(0, 0), (1, 2), (2, 1), (3, 3)])
         if slot == 0:
+            own_part += input_grad(after(lhs[0], *marks), w, 1, chunks, chunks, width)
+            marks = [own_part[1]]
             for k, parts_of in enumerate(held):
                 sent[k] += [swap(after(part, *marks), "col", k + 1) for part in parts_of]
         if slot in (2, 4):

time: 142 us -> 138 us (0.972)
  waiting for transfers between devices: 53.6 us -> 42.4 us
  local copies, waits for them, and re-layouts: 4.88 us -> 9.01 us
  Pallas kernels: 33.4 us -> 35.3 us
    ppermute x31 -> x33, waiting for transfers between devices: 53.6 us -> 42.4 us  [swap(): return lax.ppermute(value, axis, [(i, i ^ flip) for i in range(count)])]
    unnamed x28 -> x18, local copies, waits for them, and re-layouts: 4.88 us -> 7.93 us
    pallas_call x4, Pallas kernels: 9.83 us -> 11.9 us  [the longest x3 10.3 us: project(): pl.pallas_call(functools.partial(project_kernel, pieces=len(xs), mode=mod...]
    ppermute x31 -> x33, starting transfers between devices: 40.3 us -> 41 us  [swap(): return lax.ppermute(value, axis, [(i, i ^ flip) for i in range(count)])]
    pallas_call x3 -> x4, Pallas kernels: 7.71 us -> 7.63 us  [input_grad(): pl.pallas_call(functools.partial(input_grad_kernel if single else input_g...]
  transfers between devices with their start and end apart: 35 -> 37, of which waited for: 18 -> 16; matrix products, arithmetic and copies ran while one was open for 3% -> 3% of each run, Pallas kernels for 19% -> 22%
where the time goes in v12:
time: 138 us
  starting transfers between devices  43.9 us (32%)
  waiting for transfers between devices  42.4 us (31%)
  Pallas kernels  35.3 us (26%)
  local copies, waits for them, and re-layouts  9.01 us (7%)
  other arithmetic  5.98 us (4%)
    ppermute x33, waiting for transfers between devices, swap(): return lax.ppermute(value, axis, [(i, i ^ flip) for i in range(count)])  42.4 us
    ppermute x33, starting transfers between devices, swap(): return lax.ppermute(value, axis, [(i, i ^ flip) for i in range(count)])  41 us
    pallas_call x2, Pallas kernels, weight_grad(): pl.pallas_call(functools.partial(weight_grad_kernel, chained=chained, gro...  11.2 us
    pallas_call x3, Pallas kernels, project(): pl.pallas_call(functools.partial(project_kernel, pieces=len(xs), mode=mod...  10.3 us
    unnamed x18, local copies, waits for them, and re-layouts  7.93 us
    pallas_call x4, Pallas kernels, input_grad(): pl.pallas_call(functools.partial(input_grad_kernel if single else input_g...  7.63 us
    ppermute x4, starting transfers between devices, on_device(): lax.ppermute(across[slot - 1], 'row', [(0, 0), (1, 2), (2, 1), (3, 3)])  2.9 us
  transfers between devices with their start and end apart: 37, of which 16 were waited for; matrix products, arithmetic and copies ran while one was open for 3% of the time, Pallas kernels for 22%

profile of v12, /device:TPU:0, one launch (start us, length us, event | category | flops | bytes accessed | tf_op | source)
XLA Modules:
  0.0 137.7 jit_solution(1437154777869905286)
XLA Ops:
  0.6 1.1 constant_dynamic-slice_fusion
  1.7 3.0 %collective-permute-start = (bf16[128,2048]{1,0:T(8,128)(2,1)S(1)}, bf16[128,2048]{1,0:T(8,128)(2,1)S(1)}, u32[]{:S(2)}, u32[]{:S(2)}) collective-permute-start(bf16[128,2048]{1,0:T(8,128)(2,1)S(1)} %constant_dynamic-slice_fusion), channel_id=1, source_target_pairs={{0,4},{4,0},{1,5},{5,1},{2,6},{6,2},{3,7},{7,3},{8,12},{12,8},{9,1... | collective-permute-start | bytes 1572872 | tf_op jit(solution)/shard_map/ppermute | solution.py:20
  4.8 0.9 copy-done.7
  5.8 0.6 split.2
  6.5 1.6 %collective-permute-start.4 = (bf16[2,96,128]{2,1,0:T(8,128)(2,1)S(1)}, bf16[2,96,128]{2,1,0:T(8,128)(2,1)S(1)}, u32[]{:S(2)}, u32[]{:S(2)}) collective-permute-start(bf16[2,96,128]{2,1,0:T(8,128)(2,1)S(1)} %get-tuple-element.71), channel_id=1, source_target_pairs={{0,2},{1,3},{2,0},{3,1},{4,6},{5,7},{6,4},{7,5},{8,10},{9,11},{10,... | collective-permute-start | bytes 147464 | tf_op jit(solution)/shard_map/ppermute | solution.py:20
  8.3 2.8 %copy-done = bf16[512,3,2048]{2,0,1:T(8,128)(2,1)S(1)} copy-done((bf16[512,3,2048]{2,0,1:T(8,128)(2,1)S(1)}, bf16[512,3,2048]{2,0,1:T(8,128)(2,1)}, u32[]{:S(2)}) %copy-start) | copy-done | bytes 6291480
  11.1 1.4 %copy-done.3 = bf16[384,2048]{1,0:T(8,128)(2,1)S(1)} copy-done((bf16[384,2048]{1,0:T(8,128)(2,1)S(1)}, bf16[384,2048]{1,0:T(8,128)(2,1)}, u32[]{:S(2)}) %copy-start.3) | copy-done | bytes 1572888
  12.5 4.1 %project.3 = (bf16[2,3,384,128]{3,2,1,0:T(8,128)(2,1)S(1)}, bf16[2,3,384,128]{3,2,1,0:T(8,128)(2,1)S(1)}, bf16[128,2048]{1,0:T(8,128)(2,1)S(1)}) custom-call(s32[4]{0:T(128)S(1)} %pad_add_fusion.place, bf16[384,2048]{1,0:T(8,128)(2,1)S(1)} %copy-done.3, bf16[3,512,2048]{2,1,0:T(8,128)(2,1)S(1)} %bitcast.6), custom_call_target="tpu_custom_call" | custom-call | flops 1 | bytes 1 | tf_op jit(solution)/shard_map/project/pallas_call | solution.py:97
  17.0 1.4 %collective-permute-start.2 = (bf16[128,2048]{1,0:T(8,128)(2,1)S(1)}, bf16[128,2048]{1,0:T(8,128)(2,1)S(1)}, u32[]{:S(2)}, u32[]{:S(2)}) collective-permute-start(bf16[128,2048]{1,0:T(8,128)(2,1)S(1)} %get-tuple-element.67), channel_id=1, source_target_pairs={{0,4},{4,0},{1,5},{5,1},{2,6},{6,2},{3,7},{7,3},{8,12},{12,8},{9,1... | collective-permute-start | bytes 1572872 | tf_op jit(solution)/shard_map/ppermute | solution.py:20
  18.4 1.6 %collective-permute-start.1 = (bf16[128,2048]{1,0:T(8,128)(2,1)S(1)}, bf16[128,2048]{1,0:T(8,128)(2,1)S(1)}, u32[]{:S(2)}, u32[]{:S(2)}) collective-permute-start(bf16[128,2048]{1,0:T(8,128)(2,1)S(1)} %collective-permute-done.refs_0_), channel_id=1, source_target_pairs={{0,8},{8,0},{16,24},{24,16},{1,9},{9,1},{17,25},{25,17},{2,10},{10... | collective-permute-start | bytes 1572872 | tf_op jit(solution)/shard_map/ppermute | solution.py:20
  20.1 3.1 %project.4 = (bf16[2,3,128,128]{3,2,1,0:T(8,128)(2,1)S(1)}, bf16[2,3,128,128]{3,2,1,0:T(8,128)(2,1)S(1)}) custom-call(s32[4]{0:T(128)S(1)} %pad_add_fusion.place, bf16[128,2048]{1,0:T(8,128)(2,1)S(1)} %collective-permute-done.refs_0_, bf16[3,512,2048]{2,1,0:T(8,128)(2,1)S(1)} %bitcast.7), custom_call_target="tpu_custom_call" | custom-call | flops 1 | bytes 1 | tf_op jit(solution)/shard_map/project/pallas_call | solution.py:97
  23.3 1.6 %collective-permute-start.7 = (bf16[1,3,384,128]{3,2,1,0:T(8,128)(2,1)S(1)}, bf16[1,3,384,128]{3,2,1,0:T(8,128)(2,1)S(1)}, u32[]{:S(2)}, u32[]{:S(2)}) collective-permute-start(bf16[1,3,384,128]{3,2,1,0:T(8,128)(2,1)S(1)} %add_convert_fusion.12), channel_id=1, source_target_pairs={{0,2},{1,3},{2,0},{3,1},{4,6},{5,7},{6,4},{7,5},{8,10},{9,11},{10,... | collective-permute-start | bytes 884744 | tf_op jit(solution)/shard_map/ppermute | solution.py:20
  24.9 6.1 %collective-permute-done.2.refs_2_ = bf16[128,2048]{1,0:T(8,128)(2,1)S(1)} collective-permute-done((bf16[128,2048]{1,0:T(8,128)(2,1)S(1)}, bf16[128,2048]{1,0:T(8,128)(2,1)S(1)}, u32[]{:S(2)}, u32[]{:S(2)}) %collective-permute-start.2) | collective-permute-done | bytes 524320 | tf_op jit(solution)/shard_map/ppermute | solution.py:20
  31.0 1.7 %collective-permute-done.7.refs_4_ = bf16[1,3,384,128]{3,2,1,0:T(8,128)(2,1)S(1)} collective-permute-done((bf16[1,3,384,128]{3,2,1,0:T(8,128)(2,1)S(1)}, bf16[1,3,384,128]{3,2,1,0:T(8,128)(2,1)S(1)}, u32[]{:S(2)}, u32[]{:S(2)}) %collective-permute-start.7) | collective-permute-done | bytes 294944 | tf_op jit(solution)/shard_map/ppermute | solution.py:20
  32.8 3.1 %project.5 = (bf16[2,3,256,128]{3,2,1,0:T(8,128)(2,1)S(1)}, bf16[2,3,256,128]{3,2,1,0:T(8,128)(2,1)S(1)}, bf16[384,2048]{1,0:T(8,128)(2,1)S(1)}) custom-call(s32[4]{0:T(128)S(1)} %pad_add_fusion.place, bf16[128,2048]{1,0:T(8,128)(2,1)S(1)} %collective-permute-done.refs_0_, bf16[128,2048]{1,0:T(8,128)(2,1)S(1)} %collective-permute-done.1.refs_1_, ...), custom_call_target="tpu_custom_call" | custom-call | flops 1 | bytes 1 | tf_op jit(solution)/shard_map/project/pallas_call | solution.py:97
  36.0 1.6 %collective-permute-start.11 = (bf16[1,3,128,128]{3,2,1,0:T(8,128)(2,1)S(1)}, bf16[1,3,128,128]{3,2,1,0:T(8,128)(2,1)S(1)}, u32[]{:S(2)}, u32[]{:S(2)}) collective-permute-start(bf16[1,3,128,128]{3,2,1,0:T(8,128)(2,1)S(1)} %add_convert_fusion.14), channel_id=1, source_target_pairs={{0,2},{1,3},{2,0},{3,1},{4,6},{5,7},{6,4},{7,5},{8,10},{9,11},{10,... | collective-permute-start | bytes 294920 | tf_op jit(solution)/shard_map/ppermute | solution.py:20
  37.7 3.4 %collective-permute-done.11.refs_7_ = bf16[1,3,128,128]{3,2,1,0:T(8,128)(2,1)S(1)} collective-permute-done((bf16[1,3,128,128]{3,2,1,0:T(8,128)(2,1)S(1)}, bf16[1,3,128,128]{3,2,1,0:T(8,128)(2,1)S(1)}, u32[]{:S(2)}, u32[]{:S(2)}) %collective-permute-start.11) | collective-permute-done | bytes 98336 | tf_op jit(solution)/shard_map/ppermute | solution.py:20
  41.2 1.5 %collective-permute-start.12 = (bf16[1,3,256,128]{3,2,1,0:T(8,128)(2,1)S(1)}, bf16[1,3,256,128]{3,2,1,0:T(8,128)(2,1)S(1)}, u32[]{:S(2)}, u32[]{:S(2)}) collective-permute-start(bf16[1,3,256,128]{3,2,1,0:T(8,128)(2,1)S(1)} %add_convert_fusion.13), channel_id=1, source_target_pairs={{0,2},{1,3},{2,0},{3,1},{4,6},{5,7},{6,4},{7,5},{8,10},{9,11},{10,... | collective-permute-start | bytes 589832 | tf_op jit(solution)/shard_map/ppermute | solution.py:20
  43.2 0.7 collective-permute-start.10
  44.0 4.0 %collective-permute-done.10.refs_1_ = bf16[384,128]{1,0:T(8,128)(2,1)S(1)} collective-permute-done((bf16[384,128]{1,0:T(8,128)(2,1)S(1)}, bf16[384,128]{1,0:T(8,128)(2,1)S(1)}, u32[]{:S(2)}, u32[]{:S(2)}) %collective-permute-start.10) | collective-permute-done | bytes 98336 | tf_op jit(solution)/shard_map/ppermute | solution.py:20
  47.9 1.5 %middle.1 = (bf16[3,384,128]{2,1,0:T(8,128)(2,1)S(1)}, bf16[3,384,128]{2,1,0:T(8,128)(2,1)S(1)}, bf16[416,128]{1,0:T(8,128)(2,1)S(1)}, bf16[416,128]{1,0:T(8,128)(2,1)S(1)}) custom-call(s32[4]{0:T(128)S(1)} %pad_add_fusion.place, f32[7,64]{1,0:T(8,128)S(1)} %copy-done.8, bf16[384,128]{1,0:T(8,128)(2,1)S(1)} %get-tuple-element.81.refs_0_, ...), custom_call_target="tpu_custom_call" | custom-call | flops 1 | bytes 1 | tf_op jit(solution)/shard_map/middle/pallas_call | solution.py:326
  50.1 1.2 collective-permute-start.14
  51.3 0.7 collective-permute-start.17
  51.9 4.0 %collective-permute-done.17.refs_1_ = bf16[416,128]{1,0:T(8,128)(2,1)S(1)} collective-permute-done((bf16[416,128]{1,0:T(8,128)(2,1)S(1)}, bf16[416,128]{1,0:T(8,128)(2,1)S(1)}, u32[]{:S(2)}, u32[]{:S(2)}) %collective-permute-start.17) | collective-permute-done | bytes 106528 | tf_op jit(solution)/shard_map/ppermute | solution.py:20
  56.0 3.1 %collective-permute-done.14.refs_2_ = bf16[3,384,128]{2,1,0:T(8,128)(2,1)S(1)} collective-permute-done((bf16[3,384,128]{2,1,0:T(8,128)(2,1)S(1)}, bf16[3,384,128]{2,1,0:T(8,128)(2,1)S(1)}, u32[]{:S(2)}, u32[]{:S(2)}) %collective-permute-start.14) | collective-permute-done | bytes 294944 | tf_op jit(solution)/shard_map/ppermute | solution.py:20
  59.1 1.2 collective-permute-start.15
  60.6 0.7 assemble.2.grad_ref.refs_1_.refs_3_
  61.4 0.8 input_grad.4
  62.2 0.7 collective-permute-start.20
  62.9 3.0 %input_grad.5 = (bf16[384,512]{1,0:T(8,128)(2,1)}, bf16[384,512]{1,0:T(8,128)(2,1)S(1)}, bf16[384,512]{1,0:T(8,128)(2,1)S(1)}) custom-call(bf16[384,1536]{1,0:T(8,128)(2,1)S(1)} %assemble.2.grad_ref.refs_1_.refs_3_, bf16[3,512,2048]{2,1,0:T(8,128)(2,1)S(1)} %bitcast.10), custom_call_target="tpu_custom_call" | custom-call | flops 1 | bytes 1 | tf_op jit(solution)/shard_map/input_grad/pallas_call | solution.py:414
  65.9 2.6 %collective-permute-done.15.refs_2_ = bf16[3,384,128]{2,1,0:T(8,128)(2,1)S(1)} collective-permute-done((bf16[3,384,128]{2,1,0:T(8,128)(2,1)S(1)}, bf16[3,384,128]{2,1,0:T(8,128)(2,1)S(1)}, u32[]{:S(2)}, u32[]{:S(2)}) %collective-permute-start.15) | collective-permute-done | bytes 294944 | tf_op jit(solution)/shard_map/ppermute | solution.py:20
  68.5 0.7 collective-permute-start.21
  69.1 0.9 collective-permute-done.19.refs_3_
  70.1 0.7 assemble.3.grad_ref.refs_0_.refs_2_
  70.8 0.8 input_grad.6
  71.6 2.6 %collective-permute-done.20 = bf16[384,512]{1,0:T(8,128)(2,1)S(1)} collective-permute-done((bf16[384,512]{1,0:T(8,128)(2,1)S(1)}, bf16[384,512]{1,0:T(8,128)(2,1)S(1)}, u32[]{:S(2)}, u32[]{:S(2)}) %collective-permute-start.20) | collective-permute-done | bytes 393248 | tf_op jit(solution)/shard_map/ppermute | solution.py:20
  74.2 0.9 add_convert_fusion.11
  75.1 1.3 collective-permute-start.22
  76.4 0.7 collective-permute-start.23
  77.1 2.8 %copy-done.2 = bf16[512,3,2048]{2,0,1:T(8,128)(2,1)S(1)} copy-done((bf16[512,3,2048]{2,0,1:T(8,128)(2,1)S(1)}, bf16[512,3,2048]{2,0,1:T(8,128)(2,1)}, u32[]{:S(2)}) %copy-start.2) | copy-done | bytes 6291480
  79.9 3.1 %input_grad.7 = (bf16[384,512]{1,0:T(8,128)(2,1)S(1)}, bf16[384,512]{1,0:T(8,128)(2,1)S(1)}, bf16[384,512]{1,0:T(8,128)(2,1)S(1)}) custom-call(bf16[384,1536]{1,0:T(8,128)(2,1)S(1)} %assemble.3.grad_ref.refs_0_.refs_2_, bf16[3,512,2048]{2,1,0:T(8,128)(2,1)S(1)} %bitcast.12), custom_call_target="tpu_custom_call" | custom-call | flops 1 | bytes 1 | tf_op jit(solution)/shard_map/input_grad/pallas_call | solution.py:414
  83.0 1.1 add_convert_fusion.10
  84.1 1.1 collective-permute-start.24
  85.2 1.0 collective-permute-start.26
  86.2 1.2 add_convert_fusion.9
  87.4 0.7 collective-permute-start.25
  88.1 3.0 %collective-permute-done.23 = bf16[384,512]{1,0:T(8,128)(2,1)S(1)} collective-permute-done((bf16[384,512]{1,0:T(8,128)(2,1)S(1)}, bf16[384,512]{1,0:T(8,128)(2,1)S(1)}, u32[]{:S(2)}, u32[]{:S(2)}) %collective-permute-start.23) | collective-permute-done | bytes 393248 | tf_op jit(solution)/shard_map/ppermute | solution.py:20
  91.2 2.2 %collective-permute-done.24 = bf16[384,512]{1,0:T(8,128)(2,1)S(1)} collective-permute-done((bf16[384,512]{1,0:T(8,128)(2,1)S(1)}, bf16[384,512]{1,0:T(8,128)(2,1)S(1)}, u32[]{:S(2)}, u32[]{:S(2)}) %collective-permute-start.24) | collective-permute-done | bytes 393248 | tf_op jit(solution)/shard_map/ppermute | solution.py:20
  93.7 5.9 %collective-permute-start.27 = (bf16[384,512]{1,0:T(8,128)(2,1)S(1)}, bf16[384,512]{1,0:T(8,128)(2,1)S(1)}, u32[]{:S(2)}, u32[]{:S(2)}) collective-permute-start(bf16[384,512]{1,0:T(8,128)(2,1)S(1)} %get-tuple-element.128), channel_id=1, source_target_pairs={{0,8},{8,0},{16,24},{24,16},{1,9},{9,1},{17,25},{25,17},{2,10},{10... | collective-permute-start | bytes 1179656 | tf_op jit(solution)/shard_map/ppermute | solution.py:20
  99.6 0.9 collective-permute-start.28
  100.5 5.6 %weight_grad.2 = (f32[3,512,2048]{2,1,0:T(8,128)}, f32[8,128]{1,0:T(8,128)S(1)}) custom-call(bf16[384,1536]{1,0:T(8,128)(2,1)S(1)} %assemble.3.grad_ref.refs_0_.refs_2_, bf16[384,1536]{1,0:T(8,128)(2,1)S(1)} %assemble.2.grad_ref.refs_1_.refs_3_, bf16[384,2048]{1,0:T(8,128)(2,1)S(1)} %copy-done.4, bf16[384,2048]{1,0:T(8,128)(2,1)S(1)} %copy-done.6), custom_call_target="tpu_custom_call" | custom-call | flops 1 | bytes 1 | tf_op jit(solution)/shard_map/weight_grad/pallas_call | solution.py:471
  106.5 3.1 %collective-permute-start.29 = (bf16[384,512]{1,0:T(8,128)(2,1)S(1)}, bf16[384,512]{1,0:T(8,128)(2,1)S(1)}, u32[]{:S(2)}, u32[]{:S(2)}) collective-permute-start(bf16[384,512]{1,0:T(8,128)(2,1)S(1)} %get-tuple-element.126), channel_id=1, source_target_pairs={{0,8},{8,0},{16,24},{24,16},{1,9},{9,1},{17,25},{25,17},{2,10},{10... | collective-permute-start | bytes 1179656 | tf_op jit(solution)/shard_map/ppermute | solution.py:20
  109.6 0.7 collective-permute-start.30
  110.3 0.6 split.3
  111.0 1.3 collective-permute-start.32
  112.3 0.6 collective-permute-start.33
  112.8 2.6 %collective-permute-done.29 = bf16[384,512]{1,0:T(8,128)(2,1)S(1)} collective-permute-done((bf16[384,512]{1,0:T(8,128)(2,1)S(1)}, bf16[384,512]{1,0:T(8,128)(2,1)S(1)}, u32[]{:S(2)}, u32[]{:S(2)}) %collective-permute-start.29) | collective-permute-done | bytes 393248 | tf_op jit(solution)/shard_map/ppermute | solution.py:20
  115.5 0.7 collective-permute-start.34
  116.4 4.9 %collective-permute-start.35 = (bf16[384,512]{1,0:T(8,128)(2,1)S(1)}, bf16[384,512]{1,0:T(8,128)(2,1)S(1)}, u32[]{:S(2)}, u32[]{:S(2)}) collective-permute-start(bf16[384,512]{1,0:T(8,128)(2,1)S(1)} %add_convert_fusion.1), channel_id=1, source_target_pairs={{0,8},{8,0},{16,24},{24,16},{1,9},{9,1},{17,25},{25,17},{2,10},{10... | collective-permute-start | bytes 1179656 | tf_op jit(solution)/shard_map/ppermute | solution.py:20
  121.3 5.6 %weight_grad.3 = (f32[3,512,2048]{2,1,0:T(8,128)}, f32[8,128]{1,0:T(8,128)S(1)}) custom-call(f32[3,512,2048]{2,1,0:T(8,128)} %get-tuple-element.104.refs_0_, f32[8,128]{1,0:T(8,128)S(1)} %get-tuple-element.105.refs_1_, bf16[384,1536]{1,0:T(8,128)(2,1)S(1)} %assemble.3.grad_ref.refs_0_.refs_2_, ...), custom_call_target="tpu_custom_call", output_to_operand_aliasing={{0}: (0, {})} | custom-call | flops 1 | bytes 1 | tf_op jit(solution)/shard_map/weight_grad/pallas_call | solution.py:471
  127.0 2.2 %collective-permute-start.36 = (bf16[384,512]{1,0:T(8,128)(2,1)S(1)}, bf16[384,512]{1,0:T(8,128)(2,1)S(1)}, u32[]{:S(2)}, u32[]{:S(2)}) collective-permute-start(bf16[384,512]{1,0:T(8,128)(2,1)S(1)} %add_convert_fusion), channel_id=1, source_target_pairs={{0,8},{8,0},{16,24},{24,16},{1,9},{9,1},{17,25},{25,17},{2,10},{10... | collective-permute-start | bytes 1179656 | tf_op jit(solution)/shard_map/ppermute | solution.py:20
  129.3 1.4 join.1
  130.7 5.5 %collective-permute-done.36 = bf16[384,512]{1,0:T(8,128)(2,1)S(1)} collective-permute-done((bf16[384,512]{1,0:T(8,128)(2,1)S(1)}, bf16[384,512]{1,0:T(8,128)(2,1)S(1)}, u32[]{:S(2)}, u32[]{:S(2)}) %collective-permute-start.36) | collective-permute-done | bytes 393248 | tf_op jit(solution)/shard_map/ppermute | solution.py:20
  136.3 1.3 pad_maximum_fusion
  (66 shorter events, 4.2 us)
Async XLA Ops:
  1.7 15.0 %collective-permute-start = (bf16[128,2048]{1,0:T(8,128)(2,1)S(1)}, bf16[128,2048]{1,0:T(8,128)(2,1)S(1)}, u32[]{:S(2)}, u32[]{:S(2)}) collective-permute-start(bf16[128,2048]{1,0:T(8,128)(2,1)S(1)} %constant_dynamic-slice_fusion), channel_id=1, source_target_pairs={{0,4},{4,0},{1,5},{5,1},{2,6},{6,2},{3,7},{7,3},{8,12},{12,8},{9,1... | collective-permute-start | bytes 1572872 | tf_op jit(solution)/shard_map/ppermute | solution.py:20
  4.8 0.9 copy-start.7
  6.4 10.2 %collective-permute-start.3 = (bf16[2,96,128]{2,1,0:T(8,128)(2,1)S(1)}, bf16[2,96,128]{2,1,0:T(8,128)(2,1)S(1)}, u32[]{:S(2)}, u32[]{:S(2)}) collective-permute-start(bf16[2,96,128]{2,1,0:T(8,128)(2,1)S(1)} %get-tuple-element.70), channel_id=1, source_target_pairs={{0,1},{1,0},{2,3},{3,2},{4,5},{5,4},{6,7},{7,6},{8,9},{9,8},{10,11... | collective-permute-start | bytes 147464 | tf_op jit(solution)/shard_map/ppermute | solution.py:20
  6.5 10.1 %collective-permute-start.4 = (bf16[2,96,128]{2,1,0:T(8,128)(2,1)S(1)}, bf16[2,96,128]{2,1,0:T(8,128)(2,1)S(1)}, u32[]{:S(2)}, u32[]{:S(2)}) collective-permute-start(bf16[2,96,128]{2,1,0:T(8,128)(2,1)S(1)} %get-tuple-element.71), channel_id=1, source_target_pairs={{0,2},{1,3},{2,0},{3,1},{4,6},{5,7},{6,4},{7,5},{8,10},{9,11},{10,... | collective-permute-start | bytes 147464 | tf_op jit(solution)/shard_map/ppermute | solution.py:20
  8.0 8.6 %collective-permute-start.5 = (bf16[2,96,128]{2,1,0:T(8,128)(2,1)S(1)}, bf16[2,96,128]{2,1,0:T(8,128)(2,1)S(1)}, u32[]{:S(2)}, u32[]{:S(2)}) collective-permute-start(bf16[2,96,128]{2,1,0:T(8,128)(2,1)S(1)} %get-tuple-element.72), channel_id=1, source_target_pairs={{0,3},{1,2},{2,1},{3,0},{4,7},{5,6},{6,5},{7,4},{8,11},{9,10},{10,... | collective-permute-start | bytes 147464 | tf_op jit(solution)/shard_map/ppermute | solution.py:20
  8.3 2.8 %copy-start = (bf16[512,3,2048]{2,0,1:T(8,128)(2,1)S(1)}, bf16[512,3,2048]{2,0,1:T(8,128)(2,1)}, u32[]{:S(2)}) copy-start(bf16[512,3,2048]{2,0,1:T(8,128)(2,1)} %param.5) | copy-start | bytes 18874372
  11.1 1.4 %copy-start.3 = (bf16[384,2048]{1,0:T(8,128)(2,1)S(1)}, bf16[384,2048]{1,0:T(8,128)(2,1)}, u32[]{:S(2)}) copy-start(bf16[384,2048]{1,0:T(8,128)(2,1)} %refs_4_.1) | copy-start | bytes 4718596
  12.5 7.6 %copy-start.1 = (bf16[512,3,2048]{2,0,1:T(8,128)(2,1)S(1)}, bf16[512,3,2048]{2,0,1:T(8,128)(2,1)}, u32[]{:S(2)}) copy-start(bf16[512,3,2048]{2,0,1:T(8,128)(2,1)} %param.5) | copy-start | bytes 18874372
  16.7 3.3 %collective-permute-start.6 = (bf16[2,3,384,128]{3,2,1,0:T(8,128)(2,1)S(1)}, bf16[2,3,384,128]{3,2,1,0:T(8,128)(2,1)S(1)}, u32[]{:S(2)}, u32[]{:S(2)}) collective-permute-start(bf16[2,3,384,128]{3,2,1,0:T(8,128)(2,1)S(1)} %get-tuple-element.73), channel_id=1, source_target_pairs={{0,1},{1,0},{2,3},{3,2},{4,5},{5,4},{6,7},{7,6},{8,9},{9,8},{10,11... | collective-permute-start | bytes 1769480 | tf_op jit(solution)/shard_map/ppermute | solution.py:20
  17.0 14.0 %collective-permute-start.2 = (bf16[128,2048]{1,0:T(8,128)(2,1)S(1)}, bf16[128,2048]{1,0:T(8,128)(2,1)S(1)}, u32[]{:S(2)}, u32[]{:S(2)}) collective-permute-start(bf16[128,2048]{1,0:T(8,128)(2,1)S(1)} %get-tuple-element.67), channel_id=1, source_target_pairs={{0,4},{4,0},{1,5},{5,1},{2,6},{6,2},{3,7},{7,3},{8,12},{12,8},{9,1... | collective-permute-start | bytes 1572872 | tf_op jit(solution)/shard_map/ppermute | solution.py:20
  18.4 14.3 %collective-permute-start.1 = (bf16[128,2048]{1,0:T(8,128)(2,1)S(1)}, bf16[128,2048]{1,0:T(8,128)(2,1)S(1)}, u32[]{:S(2)}, u32[]{:S(2)}) collective-permute-start(bf16[128,2048]{1,0:T(8,128)(2,1)S(1)} %collective-permute-done.refs_0_), channel_id=1, source_target_pairs={{0,8},{8,0},{16,24},{24,16},{1,9},{9,1},{17,25},{25,17},{2,10},{10... | collective-permute-start | bytes 1572872 | tf_op jit(solution)/shard_map/ppermute | solution.py:20
  23.3 1.6 %collective-permute-start.8 = (bf16[2,3,128,128]{3,2,1,0:T(8,128)(2,1)S(1)}, bf16[2,3,128,128]{3,2,1,0:T(8,128)(2,1)S(1)}, u32[]{:S(2)}, u32[]{:S(2)}) collective-permute-start(bf16[2,3,128,128]{3,2,1,0:T(8,128)(2,1)S(1)} %get-tuple-element.76), channel_id=1, source_target_pairs={{0,1},{1,0},{2,3},{3,2},{4,5},{5,4},{6,7},{7,6},{8,9},{9,8},{10,11... | collective-permute-start | bytes 589832 | tf_op jit(solution)/shard_map/ppermute | solution.py:20
  23.3 9.4 %collective-permute-start.7 = (bf16[1,3,384,128]{3,2,1,0:T(8,128)(2,1)S(1)}, bf16[1,3,384,128]{3,2,1,0:T(8,128)(2,1)S(1)}, u32[]{:S(2)}, u32[]{:S(2)}) collective-permute-start(bf16[1,3,384,128]{3,2,1,0:T(8,128)(2,1)S(1)} %add_convert_fusion.12), channel_id=1, source_target_pairs={{0,2},{1,3},{2,0},{3,1},{4,6},{5,7},{6,4},{7,5},{8,10},{9,11},{10,... | collective-permute-start | bytes 884744 | tf_op jit(solution)/shard_map/ppermute | solution.py:20
  24.9 23.0 %copy-start.8 = (f32[7,64]{1,0:T(8,128)S(1)}, f32[7,64]{1,0:T(8,128)}, u32[]{:S(2)}) copy-start(f32[7,64]{1,0:T(8,128)} %taps_ref.1) | copy-start | bytes 5380
  35.9 13.6 %copy-start.5 = (bf16[384,2048]{1,0:T(8,128)(2,1)}, bf16[384,2048]{1,0:T(8,128)(2,1)S(1)}, u32[]{:S(2)}) copy-start(bf16[384,2048]{1,0:T(8,128)(2,1)S(1)} %get-tuple-element.103.refs_3_.refs_5_) | copy-start | bytes 4718596
  35.9 1.8 %collective-permute-start.9 = (bf16[2,3,256,128]{3,2,1,0:T(8,128)(2,1)S(1)}, bf16[2,3,256,128]{3,2,1,0:T(8,128)(2,1)S(1)}, u32[]{:S(2)}, u32[]{:S(2)}) collective-permute-start(bf16[2,3,256,128]{3,2,1,0:T(8,128)(2,1)S(1)} %get-tuple-element.79), channel_id=1, source_target_pairs={{0,1},{1,0},{2,3},{3,2},{4,5},{5,4},{6,7},{7,6},{8,9},{9,8},{10,11... | collective-permute-start | bytes 1179656 | tf_op jit(solution)/shard_map/ppermute | solution.py:20
  36.0 5.2 %collective-permute-start.11 = (bf16[1,3,128,128]{3,2,1,0:T(8,128)(2,1)S(1)}, bf16[1,3,128,128]{3,2,1,0:T(8,128)(2,1)S(1)}, u32[]{:S(2)}, u32[]{:S(2)}) collective-permute-start(bf16[1,3,128,128]{3,2,1,0:T(8,128)(2,1)S(1)} %add_convert_fusion.14), channel_id=1, source_target_pairs={{0,2},{1,3},{2,0},{3,1},{4,6},{5,7},{6,4},{7,5},{8,10},{9,11},{10,... | collective-permute-start | bytes 294920 | tf_op jit(solution)/shard_map/ppermute | solution.py:20
  41.2 6.7 %collective-permute-start.12 = (bf16[1,3,256,128]{3,2,1,0:T(8,128)(2,1)S(1)}, bf16[1,3,256,128]{3,2,1,0:T(8,128)(2,1)S(1)}, u32[]{:S(2)}, u32[]{:S(2)}) collective-permute-start(bf16[1,3,256,128]{3,2,1,0:T(8,128)(2,1)S(1)} %add_convert_fusion.13), channel_id=1, source_target_pairs={{0,2},{1,3},{2,0},{3,1},{4,6},{5,7},{6,4},{7,5},{8,10},{9,11},{10,... | collective-permute-start | bytes 589832 | tf_op jit(solution)/shard_map/ppermute | solution.py:20
  43.2 4.7 %collective-permute-start.10 = (bf16[384,128]{1,0:T(8,128)(2,1)S(1)}, bf16[384,128]{1,0:T(8,128)(2,1)S(1)}, u32[]{:S(2)}, u32[]{:S(2)}) collective-permute-start(bf16[384,128]{1,0:T(8,128)(2,1)S(1)} %get-tuple-element.82), channel_id=1, source_target_pairs={{0,4},{4,0},{1,5},{5,1},{2,6},{6,2},{3,7},{7,3},{8,12},{12,8},{9,1... | collective-permute-start | bytes 294920 | tf_op jit(solution)/shard_map/ppermute | solution.py:20
  49.5 6.5 %collective-permute-start.13 = (bf16[3,384,128]{2,1,0:T(8,128)(2,1)S(1)}, bf16[3,384,128]{2,1,0:T(8,128)(2,1)S(1)}, u32[]{:S(2)}, u32[]{:S(2)}) collective-permute-start(bf16[3,384,128]{2,1,0:T(8,128)(2,1)S(1)} %get-tuple-element.86.refs_0_), channel_id=1, source_target_pairs={{0,1},{1,0},{2,3},{3,2},{4,5},{5,4},{6,7},{7,6},{8,9},{9,8},{10,11... | collective-permute-start | bytes 884744 | tf_op jit(solution)/shard_map/ppermute | solution.py:20
  49.6 6.4 %collective-permute-start.16 = (bf16[3,384,128]{2,1,0:T(8,128)(2,1)S(1)}, bf16[3,384,128]{2,1,0:T(8,128)(2,1)S(1)}, u32[]{:S(2)}, u32[]{:S(2)}) collective-permute-start(bf16[3,384,128]{2,1,0:T(8,128)(2,1)S(1)} %get-tuple-element.85.refs_0_), channel_id=1, source_target_pairs={{0,1},{1,0},{2,3},{3,2},{4,5},{5,4},{6,7},{7,6},{8,9},{9,8},{10,11... | collective-permute-start | bytes 884744 | tf_op jit(solution)/shard_map/ppermute | solution.py:20
  50.1 9.0 %collective-permute-start.14 = (bf16[3,384,128]{2,1,0:T(8,128)(2,1)S(1)}, bf16[3,384,128]{2,1,0:T(8,128)(2,1)S(1)}, u32[]{:S(2)}, u32[]{:S(2)}) collective-permute-start(bf16[3,384,128]{2,1,0:T(8,128)(2,1)S(1)} %get-tuple-element.85.refs_0_), channel_id=1, source_target_pairs={{0,2},{1,3},{2,0},{3,1},{4,6},{5,7},{6,4},{7,5},{8,10},{9,11},{10,... | collective-permute-start | bytes 884744 | tf_op jit(solution)/shard_map/ppermute | solution.py:20
  51.3 4.7 %collective-permute-start.17 = (bf16[416,128]{1,0:T(8,128)(2,1)S(1)}, bf16[416,128]{1,0:T(8,128)(2,1)S(1)}, u32[]{:S(2)}, u32[]{:S(2)}) collective-permute-start(bf16[416,128]{1,0:T(8,128)(2,1)S(1)} %get-tuple-element.87), channel_id=1, source_target_pairs={{0,4},{4,0},{1,5},{5,1},{2,6},{6,2},{3,7},{7,3},{8,12},{12,8},{9,1... | collective-permute-start | bytes 319496 | tf_op jit(solution)/shard_map/ppermute | solution.py:20
  59.1 1.6 %collective-permute-start.18 = (bf16[3,384,128]{2,1,0:T(8,128)(2,1)S(1)}, bf16[3,384,128]{2,1,0:T(8,128)(2,1)S(1)}, u32[]{:S(2)}, u32[]{:S(2)}) collective-permute-start(bf16[3,384,128]{2,1,0:T(8,128)(2,1)S(1)} %collective-permute-done.14.refs_2_), channel_id=1, source_target_pairs={{0,1},{1,0},{2,3},{3,2},{4,5},{5,4},{6,7},{7,6},{8,9},{9,8},{10,11... | collective-permute-start | bytes 884744 | tf_op jit(solution)/shard_map/ppermute | solution.py:20
  59.1 9.4 %collective-permute-start.15 = (bf16[3,384,128]{2,1,0:T(8,128)(2,1)S(1)}, bf16[3,384,128]{2,1,0:T(8,128)(2,1)S(1)}, u32[]{:S(2)}, u32[]{:S(2)}) collective-permute-start(bf16[3,384,128]{2,1,0:T(8,128)(2,1)S(1)} %get-tuple-element.86.refs_0_), channel_id=1, source_target_pairs={{0,2},{1,3},{2,0},{3,1},{4,6},{5,7},{6,4},{7,5},{8,10},{9,11},{10,... | collective-permute-start | bytes 884744 | tf_op jit(solution)/shard_map/ppermute | solution.py:20
  62.2 12.0 %collective-permute-start.20 = (bf16[384,512]{1,0:T(8,128)(2,1)S(1)}, bf16[384,512]{1,0:T(8,128)(2,1)S(1)}, u32[]{:S(2)}, u32[]{:S(2)}) collective-permute-start(bf16[384,512]{1,0:T(8,128)(2,1)S(1)} %input_grad.4), channel_id=1, source_target_pairs={{0,4},{4,0},{1,5},{5,1},{2,6},{6,2},{3,7},{7,3},{8,12},{12,8},{9,1... | collective-permute-start | bytes 1179656 | tf_op jit(solution)/shard_map/ppermute | solution.py:20
  68.5 1.6 %collective-permute-start.19 = (bf16[3,384,128]{2,1,0:T(8,128)(2,1)S(1)}, bf16[3,384,128]{2,1,0:T(8,128)(2,1)S(1)}, u32[]{:S(2)}, u32[]{:S(2)}) collective-permute-start(bf16[3,384,128]{2,1,0:T(8,128)(2,1)S(1)} %collective-permute-done.15.refs_2_), channel_id=1, source_target_pairs={{0,1},{1,0},{2,3},{3,2},{4,5},{5,4},{6,7},{7,6},{8,9},{9,8},{10,11... | collective-permute-start | bytes 884744 | tf_op jit(solution)/shard_map/ppermute | solution.py:20
  68.5 14.5 %collective-permute-start.21 = (bf16[384,512]{1,0:T(8,128)(2,1)}, bf16[384,512]{1,0:T(8,128)(2,1)}, u32[]{:S(2)}, u32[]{:S(2)}) collective-permute-start(bf16[384,512]{1,0:T(8,128)(2,1)} %get-tuple-element.95), channel_id=1, source_target_pairs={{0,4},{4,0},{1,5},{5,1},{2,6},{6,2},{3,7},{7,3},{8,12},{12,8},{9,1... | collective-permute-start | bytes 1179656 | tf_op jit(solution)/shard_map/ppermute | solution.py:20
  75.1 11.1 %collective-permute-start.22 = (bf16[384,512]{1,0:T(8,128)(2,1)}, bf16[384,512]{1,0:T(8,128)(2,1)}, u32[]{:S(2)}, u32[]{:S(2)}) collective-permute-start(bf16[384,512]{1,0:T(8,128)(2,1)} %add_convert_fusion.11), channel_id=1, source_target_pairs={{0,8},{8,0},{16,24},{24,16},{1,9},{9,1},{17,25},{25,17},{2,10},{10... | collective-permute-start | bytes 1179656 | tf_op jit(solution)/shard_map/ppermute | solution.py:20
  76.4 14.7 %collective-permute-start.23 = (bf16[384,512]{1,0:T(8,128)(2,1)S(1)}, bf16[384,512]{1,0:T(8,128)(2,1)S(1)}, u32[]{:S(2)}, u32[]{:S(2)}) collective-permute-start(bf16[384,512]{1,0:T(8,128)(2,1)S(1)} %get-tuple-element.99), channel_id=1, source_target_pairs={{0,4},{4,0},{1,5},{5,1},{2,6},{6,2},{3,7},{7,3},{8,12},{12,8},{9,1... | collective-permute-start | bytes 1179656 | tf_op jit(solution)/shard_map/ppermute | solution.py:20
  77.1 2.8 %copy-start.2 = (bf16[512,3,2048]{2,0,1:T(8,128)(2,1)S(1)}, bf16[512,3,2048]{2,0,1:T(8,128)(2,1)}, u32[]{:S(2)}) copy-start(bf16[512,3,2048]{2,0,1:T(8,128)(2,1)} %param.5) | copy-start | bytes 18874372
  84.1 9.4 %collective-permute-start.24 = (bf16[384,512]{1,0:T(8,128)(2,1)S(1)}, bf16[384,512]{1,0:T(8,128)(2,1)S(1)}, u32[]{:S(2)}, u32[]{:S(2)}) collective-permute-start(bf16[384,512]{1,0:T(8,128)(2,1)S(1)} %add_convert_fusion.10), channel_id=1, source_target_pairs={{0,8},{8,0},{16,24},{24,16},{1,9},{9,1},{17,25},{25,17},{2,10},{10... | collective-permute-start | bytes 1179656 | tf_op jit(solution)/shard_map/ppermute | solution.py:20
  85.2 20.9 %collective-permute-start.26 = (bf16[384,512]{1,0:T(8,128)(2,1)S(1)}, bf16[384,512]{1,0:T(8,128)(2,1)S(1)}, u32[]{:S(2)}, u32[]{:S(2)}) collective-permute-start(bf16[384,512]{1,0:T(8,128)(2,1)S(1)} %get-tuple-element.108), channel_id=1, source_target_pairs={{0,4},{4,0},{1,5},{5,1},{2,6},{6,2},{3,7},{7,3},{8,12},{12,8},{9,1... | collective-permute-start | bytes 1179656 | tf_op jit(solution)/shard_map/ppermute | solution.py:20
  87.4 6.1 %collective-permute-start.25 = (bf16[384,512]{1,0:T(8,128)(2,1)S(1)}, bf16[384,512]{1,0:T(8,128)(2,1)S(1)}, u32[]{:S(2)}, u32[]{:S(2)}) collective-permute-start(bf16[384,512]{1,0:T(8,128)(2,1)S(1)} %add_convert_fusion.9), channel_id=1, source_target_pairs={{0,0},{8,16},{16,8},{24,24},{1,1},{9,17},{17,9},{25,25},{2,2},{10,... | collective-permute-start | bytes 1179656 | tf_op jit(solution)/shard_map/ppermute | solution.py:601
  91.2 9.3 %copy-start.4 = (bf16[384,2048]{1,0:T(8,128)(2,1)S(1)}, bf16[384,2048]{1,0:T(8,128)(2,1)}, u32[]{:S(2)}) copy-start(bf16[384,2048]{1,0:T(8,128)(2,1)} %refs_4_.1) | copy-start | bytes 4718596
  91.2 9.3 %copy-start.6 = (bf16[384,2048]{1,0:T(8,128)(2,1)S(1)}, bf16[384,2048]{1,0:T(8,128)(2,1)}, u32[]{:S(2)}) copy-start(bf16[384,2048]{1,0:T(8,128)(2,1)} %copy-done.5) | copy-start | bytes 4718596
  93.7 12.5 %collective-permute-start.27 = (bf16[384,512]{1,0:T(8,128)(2,1)S(1)}, bf16[384,512]{1,0:T(8,128)(2,1)S(1)}, u32[]{:S(2)}, u32[]{:S(2)}) collective-permute-start(bf16[384,512]{1,0:T(8,128)(2,1)S(1)} %get-tuple-element.128), channel_id=1, source_target_pairs={{0,8},{8,0},{16,24},{24,16},{1,9},{9,1},{17,25},{25,17},{2,10},{10... | collective-permute-start | bytes 1179656 | tf_op jit(solution)/shard_map/ppermute | solution.py:20
  99.6 6.7 %collective-permute-start.28 = (bf16[384,512]{1,0:T(8,128)(2,1)S(1)}, bf16[384,512]{1,0:T(8,128)(2,1)S(1)}, u32[]{:S(2)}, u32[]{:S(2)}) collective-permute-start(bf16[384,512]{1,0:T(8,128)(2,1)S(1)} %add_convert_fusion.7), channel_id=1, source_target_pairs={{0,0},{8,16},{16,8},{24,24},{1,1},{9,17},{17,9},{25,25},{2,2},{10,... | collective-permute-start | bytes 1179656 | tf_op jit(solution)/shard_map/ppermute | solution.py:601
  106.5 8.9 %collective-permute-start.29 = (bf16[384,512]{1,0:T(8,128)(2,1)S(1)}, bf16[384,512]{1,0:T(8,128)(2,1)S(1)}, u32[]{:S(2)}, u32[]{:S(2)}) collective-permute-start(bf16[384,512]{1,0:T(8,128)(2,1)S(1)} %get-tuple-element.126), channel_id=1, source_target_pairs={{0,8},{8,0},{16,24},{24,16},{1,9},{9,1},{17,25},{25,17},{2,10},{10... | collective-permute-start | bytes 1179656 | tf_op jit(solution)/shard_map/ppermute | solution.py:20
  109.6 6.6 %collective-permute-start.30 = (bf16[384,512]{1,0:T(8,128)(2,1)S(1)}, bf16[384,512]{1,0:T(8,128)(2,1)S(1)}, u32[]{:S(2)}, u32[]{:S(2)}) collective-permute-start(bf16[384,512]{1,0:T(8,128)(2,1)S(1)} %add_convert_fusion.4), channel_id=1, source_target_pairs={{0,0},{8,16},{16,8},{24,24},{1,1},{9,17},{17,9},{25,25},{2,2},{10,... | collective-permute-start | bytes 1179656 | tf_op jit(solution)/shard_map/ppermute | solution.py:601
  110.9 16.0 %collective-permute-start.31 = (bf16[2,128,128]{2,1,0:T(8,128)(2,1)S(1)}, bf16[2,128,128]{2,1,0:T(8,128)(2,1)S(1)}, u32[]{:S(2)}, u32[]{:S(2)}) collective-permute-start(bf16[2,128,128]{2,1,0:T(8,128)(2,1)S(1)} %get-tuple-element.118), channel_id=1, source_target_pairs={{0,1},{1,0},{2,3},{3,2},{4,5},{5,4},{6,7},{7,6},{8,9},{9,8},{10,11... | collective-permute-start | bytes 196616 | tf_op jit(solution)/shard_map/ppermute | solution.py:20
  111.0 15.9 %collective-permute-start.32 = (bf16[2,128,128]{2,1,0:T(8,128)(2,1)S(1)}, bf16[2,128,128]{2,1,0:T(8,128)(2,1)S(1)}, u32[]{:S(2)}, u32[]{:S(2)}) collective-permute-start(bf16[2,128,128]{2,1,0:T(8,128)(2,1)S(1)} %get-tuple-element.119), channel_id=1, source_target_pairs={{0,2},{1,3},{2,0},{3,1},{4,6},{5,7},{6,4},{7,5},{8,10},{9,11},{10,... | collective-permute-start | bytes 196616 | tf_op jit(solution)/shard_map/ppermute | solution.py:20
  112.3 14.7 %collective-permute-start.33 = (bf16[2,128,128]{2,1,0:T(8,128)(2,1)S(1)}, bf16[2,128,128]{2,1,0:T(8,128)(2,1)S(1)}, u32[]{:S(2)}, u32[]{:S(2)}) collective-permute-start(bf16[2,128,128]{2,1,0:T(8,128)(2,1)S(1)} %get-tuple-element.120), channel_id=1, source_target_pairs={{0,3},{1,2},{2,1},{3,0},{4,7},{5,6},{6,5},{7,4},{8,11},{9,10},{10,... | collective-permute-start | bytes 196616 | tf_op jit(solution)/shard_map/ppermute | solution.py:20
  115.5 11.4 %collective-permute-start.34 = (bf16[384,512]{1,0:T(8,128)(2,1)S(1)}, bf16[384,512]{1,0:T(8,128)(2,1)S(1)}, u32[]{:S(2)}, u32[]{:S(2)}) collective-permute-start(bf16[384,512]{1,0:T(8,128)(2,1)S(1)} %add_convert_fusion.2), channel_id=1, source_target_pairs={{0,0},{8,16},{16,8},{24,24},{1,1},{9,17},{17,9},{25,25},{2,2},{10,... | collective-permute-start | bytes 1179656 | tf_op jit(solution)/shard_map/ppermute | solution.py:601
  116.4 14.3 %collective-permute-start.35 = (bf16[384,512]{1,0:T(8,128)(2,1)S(1)}, bf16[384,512]{1,0:T(8,128)(2,1)S(1)}, u32[]{:S(2)}, u32[]{:S(2)}) collective-permute-start(bf16[384,512]{1,0:T(8,128)(2,1)S(1)} %add_convert_fusion.1), channel_id=1, source_target_pairs={{0,8},{8,0},{16,24},{24,16},{1,9},{9,1},{17,25},{25,17},{2,10},{10... | collective-permute-start | bytes 1179656 | tf_op jit(solution)/shard_map/ppermute | solution.py:20
  127.0 9.2 %collective-permute-start.36 = (bf16[384,512]{1,0:T(8,128)(2,1)S(1)}, bf16[384,512]{1,0:T(8,128)(2,1)S(1)}, u32[]{:S(2)}, u32[]{:S(2)}) collective-permute-start(bf16[384,512]{1,0:T(8,128)(2,1)S(1)} %add_convert_fusion), channel_id=1, source_target_pairs={{0,8},{8,0},{16,24},{24,16},{1,9},{9,1},{17,25},{25,17},{2,10},{10... | collective-permute-start | bytes 1179656 | tf_op jit(solution)/shard_map/ppermute | solution.py:20

commit v13 on v12

--- a/solution.py
+++ b/solution.py
@@ -518,7 +518,8 @@
     first = [swap(sent_first, "col", k) for k in range(1, n_col)]
     ups = split_lanes(place, upstream, n_col, n_depth)
     ups = [up if r == 0 else swap(up, "depth", r) for r, up in enumerate(ups)]
-    keep, send, *last = project(place, [tokens], w, n_depth, "cut" if cut else "plain")
+    outer = (row_at == 0) | (row_at == 3)
+    keep, send, *last = project(place, [after(tokens, outer)], w, n_depth, "cut" if cut else "plain")
     terms, pairs, fars = sum_over_depth(keep, send, first + ups[1:])
     xs, pieces, parts = [tokens], [(0, ("all",))], [terms]
     for k in range(1, n_col):
@@ -570,7 +571,6 @@
     held = [parts_of[3:] for _, parts_of in sent]
     sent = [of for of, _ in sent]
     own_part = input_grad(lhs[0], w, 0, 1, chunks, width)
-    outer = (row_at == 0) | (row_at == 3)
     line = lax.axis_size("row") == 4
     inward, across, summed, done = ([None] * chunks for _ in range(4))
     pair = cross = filled = None

time: 138 us -> 136 us (0.986)
  waiting for transfers between devices: 42.4 us -> 47.2 us
  other arithmetic: 5.98 us -> 3.07 us
  local copies, waits for them, and re-layouts: 9.01 us -> 6.22 us
    ppermute x33, waiting for transfers between devices: 42.4 us -> 47.2 us  [swap(): return lax.ppermute(value, axis, [(i, i ^ flip) for i in range(count)])]
    unnamed x18 -> x12, local copies, waits for them, and re-layouts: 7.93 us -> 5.14 us
    convert_element_type x4, other arithmetic: 2.15 us -> 0.39 us  [on_device(): inward[slot] = total.astype(jnp.bfloat16)]
  transfers between devices with their start and end apart: 37 -> 37, of which waited for: 16 -> 17; matrix products, arithmetic and copies ran while one was open for 3% -> 1% of each run, Pallas kernels for 22% -> 22%
where the time goes in v13:
time: 136 us
  waiting for transfers between devices  47.2 us (35%)
  starting transfers between devices  43 us (32%)
  Pallas kernels  35.1 us (26%)
  local copies, waits for them, and re-layouts  6.22 us (5%)
  other arithmetic  3.07 us (2%)
    ppermute x33, waiting for transfers between devices, swap(): return lax.ppermute(value, axis, [(i, i ^ flip) for i in range(count)])  47.2 us
    ppermute x33, starting transfers between devices, swap(): return lax.ppermute(value, axis, [(i, i ^ flip) for i in range(count)])  40.1 us
    pallas_call x2, Pallas kernels, weight_grad(): pl.pallas_call(functools.partial(weight_grad_kernel, chained=chained, gro...  11.2 us
    pallas_call x3, Pallas kernels, project(): pl.pallas_call(functools.partial(project_kernel, pieces=len(xs), mode=mod...  10.3 us
    pallas_call x4, Pallas kernels, input_grad(): pl.pallas_call(functools.partial(input_grad_kernel if single else input_g...  7.49 us
    unnamed x12, local copies, waits for them, and re-layouts  5.14 us
    ppermute x4, starting transfers between devices, on_device(): lax.ppermute(across[slot - 1], 'row', [(0, 0), (1, 2), (2, 1), (3, 3)])  2.9 us
  transfers between devices with their start and end apart: 37, of which 17 were waited for; matrix products, arithmetic and copies ran while one was open for 1% of the time, Pallas kernels for 22%

profile of v13, /device:TPU:0, one launch (start us, length us, event | category | flops | bytes accessed | tf_op | source)
XLA Modules:
  0.0 135.7 jit_solution(13552668750234016617)
XLA Ops:
  0.6 1.1 constant_dynamic-slice_fusion
  1.7 3.0 %collective-permute-start = (bf16[128,2048]{1,0:T(8,128)(2,1)S(1)}, bf16[128,2048]{1,0:T(8,128)(2,1)S(1)}, u32[]{:S(2)}, u32[]{:S(2)}) collective-permute-start(bf16[128,2048]{1,0:T(8,128)(2,1)S(1)} %constant_dynamic-slice_fusion), channel_id=1, source_target_pairs={{0,4},{4,0},{1,5},{5,1},{2,6},{6,2},{3,7},{7,3},{8,12},{12,8},{9,1... | collective-permute-start | bytes 1572872 | tf_op jit(solution)/shard_map/ppermute | solution.py:20
  4.9 0.9 copy-done.4
  5.8 0.6 split.2
  6.5 1.6 %collective-permute-start.4 = (bf16[2,96,128]{2,1,0:T(8,128)(2,1)S(1)}, bf16[2,96,128]{2,1,0:T(8,128)(2,1)S(1)}, u32[]{:S(2)}, u32[]{:S(2)}) collective-permute-start(bf16[2,96,128]{2,1,0:T(8,128)(2,1)S(1)} %get-tuple-element.73), channel_id=1, source_target_pairs={{0,2},{1,3},{2,0},{3,1},{4,6},{5,7},{6,4},{7,5},{8,10},{9,11},{10,... | collective-permute-start | bytes 147464 | tf_op jit(solution)/shard_map/ppermute | solution.py:20
  8.3 2.8 %copy-done = bf16[512,3,2048]{2,0,1:T(8,128)(2,1)S(1)} copy-done((bf16[512,3,2048]{2,0,1:T(8,128)(2,1)S(1)}, bf16[512,3,2048]{2,0,1:T(8,128)(2,1)}, u32[]{:S(2)}) %copy-start) | copy-done | bytes 6291480
  11.1 1.4 %copy-done.2 = bf16[384,2048]{1,0:T(8,128)(2,1)S(1)} copy-done((bf16[384,2048]{1,0:T(8,128)(2,1)S(1)}, bf16[384,2048]{1,0:T(8,128)(2,1)}, u32[]{:S(2)}) %copy-start.2) | copy-done | bytes 1572888
  12.5 4.1 %project.3 = (bf16[2,3,384,128]{3,2,1,0:T(8,128)(2,1)S(1)}, bf16[2,3,384,128]{3,2,1,0:T(8,128)(2,1)S(1)}, bf16[128,2048]{1,0:T(8,128)(2,1)S(1)}) custom-call(s32[4]{0:T(128)S(1)} %pad_add_fusion.place, bf16[384,2048]{1,0:T(8,128)(2,1)S(1)} %copy-done.2, bf16[3,512,2048]{2,1,0:T(8,128)(2,1)S(1)} %bitcast.6), custom_call_target="tpu_custom_call" | custom-call | flops 1 | bytes 1 | tf_op jit(solution)/shard_map/project/pallas_call | solution.py:97
  17.0 1.4 %collective-permute-start.2 = (bf16[128,2048]{1,0:T(8,128)(2,1)S(1)}, bf16[128,2048]{1,0:T(8,128)(2,1)S(1)}, u32[]{:S(2)}, u32[]{:S(2)}) collective-permute-start(bf16[128,2048]{1,0:T(8,128)(2,1)S(1)} %get-tuple-element.69), channel_id=1, source_target_pairs={{0,4},{4,0},{1,5},{5,1},{2,6},{6,2},{3,7},{7,3},{8,12},{12,8},{9,1... | collective-permute-start | bytes 1572872 | tf_op jit(solution)/shard_map/ppermute | solution.py:20
  18.4 1.6 %collective-permute-start.1 = (bf16[128,2048]{1,0:T(8,128)(2,1)S(1)}, bf16[128,2048]{1,0:T(8,128)(2,1)S(1)}, u32[]{:S(2)}, u32[]{:S(2)}) collective-permute-start(bf16[128,2048]{1,0:T(8,128)(2,1)S(1)} %collective-permute-done.refs_0_), channel_id=1, source_target_pairs={{0,8},{8,0},{16,24},{24,16},{1,9},{9,1},{17,25},{25,17},{2,10},{10... | collective-permute-start | bytes 1572872 | tf_op jit(solution)/shard_map/ppermute | solution.py:20
  20.1 3.1 %project.4 = (bf16[2,3,128,128]{3,2,1,0:T(8,128)(2,1)S(1)}, bf16[2,3,128,128]{3,2,1,0:T(8,128)(2,1)S(1)}) custom-call(s32[4]{0:T(128)S(1)} %pad_add_fusion.place, bf16[128,2048]{1,0:T(8,128)(2,1)S(1)} %collective-permute-done.refs_0_, bf16[3,512,2048]{2,1,0:T(8,128)(2,1)S(1)} %bitcast.7), custom_call_target="tpu_custom_call" | custom-call | flops 1 | bytes 1 | tf_op jit(solution)/shard_map/project/pallas_call | solution.py:97
  23.4 1.6 %collective-permute-start.7 = (bf16[1,3,384,128]{3,2,1,0:T(8,128)(2,1)S(1)}, bf16[1,3,384,128]{3,2,1,0:T(8,128)(2,1)S(1)}, u32[]{:S(2)}, u32[]{:S(2)}) collective-permute-start(bf16[1,3,384,128]{3,2,1,0:T(8,128)(2,1)S(1)} %add_convert_fusion.12), channel_id=1, source_target_pairs={{0,2},{1,3},{2,0},{3,1},{4,6},{5,7},{6,4},{7,5},{8,10},{9,11},{10,... | collective-permute-start | bytes 884744 | tf_op jit(solution)/shard_map/ppermute | solution.py:20
  25.0 6.1 %collective-permute-done.2.refs_2_ = bf16[128,2048]{1,0:T(8,128)(2,1)S(1)} collective-permute-done((bf16[128,2048]{1,0:T(8,128)(2,1)S(1)}, bf16[128,2048]{1,0:T(8,128)(2,1)S(1)}, u32[]{:S(2)}, u32[]{:S(2)}) %collective-permute-start.2) | collective-permute-done | bytes 524320 | tf_op jit(solution)/shard_map/ppermute | solution.py:20
  31.0 1.7 %collective-permute-done.7.refs_4_ = bf16[1,3,384,128]{3,2,1,0:T(8,128)(2,1)S(1)} collective-permute-done((bf16[1,3,384,128]{3,2,1,0:T(8,128)(2,1)S(1)}, bf16[1,3,384,128]{3,2,1,0:T(8,128)(2,1)S(1)}, u32[]{:S(2)}, u32[]{:S(2)}) %collective-permute-start.7) | collective-permute-done | bytes 294944 | tf_op jit(solution)/shard_map/ppermute | solution.py:20
  32.8 3.1 %project.5 = (bf16[2,3,256,128]{3,2,1,0:T(8,128)(2,1)S(1)}, bf16[2,3,256,128]{3,2,1,0:T(8,128)(2,1)S(1)}, bf16[384,2048]{1,0:T(8,128)(2,1)S(1)}) custom-call(s32[4]{0:T(128)S(1)} %pad_add_fusion.place, bf16[128,2048]{1,0:T(8,128)(2,1)S(1)} %collective-permute-done.refs_0_, bf16[128,2048]{1,0:T(8,128)(2,1)S(1)} %collective-permute-done.1.refs_1_, ...), custom_call_target="tpu_custom_call" | custom-call | flops 1 | bytes 1 | tf_op jit(solution)/shard_map/project/pallas_call | solution.py:97
  36.0 1.6 %collective-permute-start.11 = (bf16[1,3,128,128]{3,2,1,0:T(8,128)(2,1)S(1)}, bf16[1,3,128,128]{3,2,1,0:T(8,128)(2,1)S(1)}, u32[]{:S(2)}, u32[]{:S(2)}) collective-permute-start(bf16[1,3,128,128]{3,2,1,0:T(8,128)(2,1)S(1)} %add_convert_fusion.14), channel_id=1, source_target_pairs={{0,2},{1,3},{2,0},{3,1},{4,6},{5,7},{6,4},{7,5},{8,10},{9,11},{10,... | collective-permute-start | bytes 294920 | tf_op jit(solution)/shard_map/ppermute | solution.py:20
  37.7 3.4 %collective-permute-done.11.refs_7_ = bf16[1,3,128,128]{3,2,1,0:T(8,128)(2,1)S(1)} collective-permute-done((bf16[1,3,128,128]{3,2,1,0:T(8,128)(2,1)S(1)}, bf16[1,3,128,128]{3,2,1,0:T(8,128)(2,1)S(1)}, u32[]{:S(2)}, u32[]{:S(2)}) %collective-permute-start.11) | collective-permute-done | bytes 98336 | tf_op jit(solution)/shard_map/ppermute | solution.py:20
  41.2 1.5 %collective-permute-start.12 = (bf16[1,3,256,128]{3,2,1,0:T(8,128)(2,1)S(1)}, bf16[1,3,256,128]{3,2,1,0:T(8,128)(2,1)S(1)}, u32[]{:S(2)}, u32[]{:S(2)}) collective-permute-start(bf16[1,3,256,128]{3,2,1,0:T(8,128)(2,1)S(1)} %add_convert_fusion.13), channel_id=1, source_target_pairs={{0,2},{1,3},{2,0},{3,1},{4,6},{5,7},{6,4},{7,5},{8,10},{9,11},{10,... | collective-permute-start | bytes 589832 | tf_op jit(solution)/shard_map/ppermute | solution.py:20
  42.7 0.6 merge.1
  43.2 0.7 collective-permute-start.10
  44.0 4.0 %collective-permute-done.10.refs_1_ = bf16[384,128]{1,0:T(8,128)(2,1)S(1)} collective-permute-done((bf16[384,128]{1,0:T(8,128)(2,1)S(1)}, bf16[384,128]{1,0:T(8,128)(2,1)S(1)}, u32[]{:S(2)}, u32[]{:S(2)}) %collective-permute-start.10) | collective-permute-done | bytes 98336 | tf_op jit(solution)/shard_map/ppermute | solution.py:20
  47.9 1.5 %middle.1 = (bf16[3,384,128]{2,1,0:T(8,128)(2,1)S(1)}, bf16[3,384,128]{2,1,0:T(8,128)(2,1)S(1)}, bf16[416,128]{1,0:T(8,128)(2,1)S(1)}, bf16[416,128]{1,0:T(8,128)(2,1)S(1)}) custom-call(s32[4]{0:T(128)S(1)} %pad_add_fusion.place, f32[7,64]{1,0:T(8,128)S(1)} %copy-done.5, bf16[384,128]{1,0:T(8,128)(2,1)S(1)} %get-tuple-element.83.refs_0_, ...), custom_call_target="tpu_custom_call" | custom-call | flops 1 | bytes 1 | tf_op jit(solution)/shard_map/middle/pallas_call | solution.py:326
  49.6 0.5 collective-permute-start.16
  50.1 1.2 collective-permute-start.14
  51.3 0.7 collective-permute-start.17
  51.9 4.1 %collective-permute-done.17.refs_1_ = bf16[416,128]{1,0:T(8,128)(2,1)S(1)} collective-permute-done((bf16[416,128]{1,0:T(8,128)(2,1)S(1)}, bf16[416,128]{1,0:T(8,128)(2,1)S(1)}, u32[]{:S(2)}, u32[]{:S(2)}) %collective-permute-start.17) | collective-permute-done | bytes 106528 | tf_op jit(solution)/shard_map/ppermute | solution.py:20
  56.0 3.1 %collective-permute-done.14.refs_2_ = bf16[3,384,128]{2,1,0:T(8,128)(2,1)S(1)} collective-permute-done((bf16[3,384,128]{2,1,0:T(8,128)(2,1)S(1)}, bf16[3,384,128]{2,1,0:T(8,128)(2,1)S(1)}, u32[]{:S(2)}, u32[]{:S(2)}) %collective-permute-start.14) | collective-permute-done | bytes 294944 | tf_op jit(solution)/shard_map/ppermute | solution.py:20
  59.1 1.2 collective-permute-start.15
  60.3 0.4 collective-permute-done.18.refs_3_
  60.6 0.7 assemble.2.grad_ref.refs_1_.refs_3_
  61.4 0.8 input_grad.4
  62.2 0.7 collective-permute-start.20
  62.9 3.0 %input_grad.5 = (bf16[384,512]{1,0:T(8,128)(2,1)S(1)}, bf16[384,512]{1,0:T(8,128)(2,1)S(1)}, bf16[384,512]{1,0:T(8,128)(2,1)S(1)}) custom-call(bf16[384,1536]{1,0:T(8,128)(2,1)S(1)} %assemble.2.grad_ref.refs_1_.refs_3_, bf16[3,512,2048]{2,1,0:T(8,128)(2,1)S(1)} %bitcast.10), custom_call_target="tpu_custom_call" | custom-call | flops 1 | bytes 1 | tf_op jit(solution)/shard_map/input_grad/pallas_call | solution.py:414
  65.9 2.6 %collective-permute-done.15.refs_2_ = bf16[3,384,128]{2,1,0:T(8,128)(2,1)S(1)} collective-permute-done((bf16[3,384,128]{2,1,0:T(8,128)(2,1)S(1)}, bf16[3,384,128]{2,1,0:T(8,128)(2,1)S(1)}, u32[]{:S(2)}, u32[]{:S(2)}) %collective-permute-start.15) | collective-permute-done | bytes 294944 | tf_op jit(solution)/shard_map/ppermute | solution.py:20
  68.5 0.7 collective-permute-start.21
  69.1 0.9 collective-permute-done.19.refs_3_
  70.1 0.7 assemble.3.grad_ref.refs_0_.refs_2_
  70.8 0.8 input_grad.6
  71.6 2.6 %collective-permute-done.20 = bf16[384,512]{1,0:T(8,128)(2,1)S(1)} collective-permute-done((bf16[384,512]{1,0:T(8,128)(2,1)S(1)}, bf16[384,512]{1,0:T(8,128)(2,1)S(1)}, u32[]{:S(2)}, u32[]{:S(2)}) %collective-permute-start.20) | collective-permute-done | bytes 393248 | tf_op jit(solution)/shard_map/ppermute | solution.py:20
  74.3 1.4 collective-permute-start.22
  75.7 0.7 collective-permute-start.23
  76.3 3.0 %input_grad.7 = (bf16[384,512]{1,0:T(8,128)(2,1)S(1)}, bf16[384,512]{1,0:T(8,128)(2,1)S(1)}, bf16[384,512]{1,0:T(8,128)(2,1)S(1)}) custom-call(bf16[384,1536]{1,0:T(8,128)(2,1)S(1)} %assemble.3.grad_ref.refs_0_.refs_2_, bf16[3,512,2048]{2,1,0:T(8,128)(2,1)S(1)} %bitcast.12), custom_call_target="tpu_custom_call" | custom-call | flops 1 | bytes 1 | tf_op jit(solution)/shard_map/input_grad/pallas_call | solution.py:414
  79.3 3.3 %collective-permute-done.21 = bf16[384,512]{1,0:T(8,128)(2,1)S(1)} collective-permute-done((bf16[384,512]{1,0:T(8,128)(2,1)S(1)}, bf16[384,512]{1,0:T(8,128)(2,1)S(1)}, u32[]{:S(2)}, u32[]{:S(2)}) %collective-permute-start.21) | collective-permute-done | bytes 393248 | tf_op jit(solution)/shard_map/ppermute | solution.py:20
  82.7 1.4 collective-permute-start.24
  84.1 0.7 collective-permute-start.26
  84.9 0.7 collective-permute-start.25
  85.6 5.5 %collective-permute-done.23 = bf16[384,512]{1,0:T(8,128)(2,1)S(1)} collective-permute-done((bf16[384,512]{1,0:T(8,128)(2,1)S(1)}, bf16[384,512]{1,0:T(8,128)(2,1)S(1)}, u32[]{:S(2)}, u32[]{:S(2)}) %collective-permute-start.23) | collective-permute-done | bytes 393248 | tf_op jit(solution)/shard_map/ppermute | solution.py:20
  91.2 1.2 collective-permute-done.24
  92.6 4.8 %collective-permute-start.27 = (bf16[384,512]{1,0:T(8,128)(2,1)S(1)}, bf16[384,512]{1,0:T(8,128)(2,1)S(1)}, u32[]{:S(2)}, u32[]{:S(2)}) collective-permute-start(bf16[384,512]{1,0:T(8,128)(2,1)S(1)} %get-tuple-element.130), channel_id=1, source_target_pairs={{0,8},{8,0},{16,24},{24,16},{1,9},{9,1},{17,25},{25,17},{2,10},{10... | collective-permute-start | bytes 1179656 | tf_op jit(solution)/shard_map/ppermute | solution.py:20
  97.4 0.9 collective-permute-start.28
  98.3 5.6 %weight_grad.2 = (f32[3,512,2048]{2,1,0:T(8,128)}, f32[8,128]{1,0:T(8,128)S(1)}) custom-call(bf16[384,1536]{1,0:T(8,128)(2,1)S(1)} %assemble.3.grad_ref.refs_0_.refs_2_, bf16[384,1536]{1,0:T(8,128)(2,1)S(1)} %assemble.2.grad_ref.refs_1_.refs_3_, bf16[384,2048]{1,0:T(8,128)(2,1)S(1)} %copy-done.3, bf16[384,2048]{1,0:T(8,128)(2,1)S(1)} %get-tuple-element.105.refs_3_.refs_5_), custom_call_target="tpu_custom_call" | custom-call | flops 1 | bytes 1 | tf_op jit(solution)/shard_map/weight_grad/pallas_call | solution.py:471
  104.3 3.6 %collective-permute-start.29 = (bf16[384,512]{1,0:T(8,128)(2,1)S(1)}, bf16[384,512]{1,0:T(8,128)(2,1)S(1)}, u32[]{:S(2)}, u32[]{:S(2)}) collective-permute-start(bf16[384,512]{1,0:T(8,128)(2,1)S(1)} %get-tuple-element.128), channel_id=1, source_target_pairs={{0,8},{8,0},{16,24},{24,16},{1,9},{9,1},{17,25},{25,17},{2,10},{10... | collective-permute-start | bytes 1179656 | tf_op jit(solution)/shard_map/ppermute | solution.py:20
  107.9 0.7 collective-permute-start.30
  108.5 0.6 split.3
  109.2 1.3 collective-permute-start.32
  110.5 0.6 collective-permute-start.33
  111.0 2.6 %collective-permute-done.29 = bf16[384,512]{1,0:T(8,128)(2,1)S(1)} collective-permute-done((bf16[384,512]{1,0:T(8,128)(2,1)S(1)}, bf16[384,512]{1,0:T(8,128)(2,1)S(1)}, u32[]{:S(2)}, u32[]{:S(2)}) %collective-permute-start.29) | collective-permute-done | bytes 393248 | tf_op jit(solution)/shard_map/ppermute | solution.py:20
  113.7 0.7 collective-permute-start.34
  114.6 4.8 %collective-permute-start.35 = (bf16[384,512]{1,0:T(8,128)(2,1)S(1)}, bf16[384,512]{1,0:T(8,128)(2,1)S(1)}, u32[]{:S(2)}, u32[]{:S(2)}) collective-permute-start(bf16[384,512]{1,0:T(8,128)(2,1)S(1)} %add_convert_fusion.1), channel_id=1, source_target_pairs={{0,8},{8,0},{16,24},{24,16},{1,9},{9,1},{17,25},{25,17},{2,10},{10... | collective-permute-start | bytes 1179656 | tf_op jit(solution)/shard_map/ppermute | solution.py:20
  119.3 5.6 %weight_grad.3 = (f32[3,512,2048]{2,1,0:T(8,128)}, f32[8,128]{1,0:T(8,128)S(1)}) custom-call(f32[3,512,2048]{2,1,0:T(8,128)} %get-tuple-element.106.refs_0_, f32[8,128]{1,0:T(8,128)S(1)} %get-tuple-element.107.refs_1_, bf16[384,1536]{1,0:T(8,128)(2,1)S(1)} %assemble.3.grad_ref.refs_0_.refs_2_, ...), custom_call_target="tpu_custom_call", output_to_operand_aliasing={{0}: (0, {})} | custom-call | flops 1 | bytes 1 | tf_op jit(solution)/shard_map/weight_grad/pallas_call | solution.py:471
  125.1 2.2 %collective-permute-start.36 = (bf16[384,512]{1,0:T(8,128)(2,1)S(1)}, bf16[384,512]{1,0:T(8,128)(2,1)S(1)}, u32[]{:S(2)}, u32[]{:S(2)}) collective-permute-start(bf16[384,512]{1,0:T(8,128)(2,1)S(1)} %add_convert_fusion), channel_id=1, source_target_pairs={{0,8},{8,0},{16,24},{24,16},{1,9},{9,1},{17,25},{25,17},{2,10},{10... | collective-permute-start | bytes 1179656 | tf_op jit(solution)/shard_map/ppermute | solution.py:20
  127.3 1.4 join.1
  128.7 5.6 %collective-permute-done.36 = bf16[384,512]{1,0:T(8,128)(2,1)S(1)} collective-permute-done((bf16[384,512]{1,0:T(8,128)(2,1)S(1)}, bf16[384,512]{1,0:T(8,128)(2,1)S(1)}, u32[]{:S(2)}, u32[]{:S(2)}) %collective-permute-start.36) | collective-permute-done | bytes 393248 | tf_op jit(solution)/shard_map/ppermute | solution.py:20
  134.4 1.3 pad_maximum_fusion
  (60 shorter events, 3.1 us)
Async XLA Ops:
  1.7 15.0 %collective-permute-start = (bf16[128,2048]{1,0:T(8,128)(2,1)S(1)}, bf16[128,2048]{1,0:T(8,128)(2,1)S(1)}, u32[]{:S(2)}, u32[]{:S(2)}) collective-permute-start(bf16[128,2048]{1,0:T(8,128)(2,1)S(1)} %constant_dynamic-slice_fusion), channel_id=1, source_target_pairs={{0,4},{4,0},{1,5},{5,1},{2,6},{6,2},{3,7},{7,3},{8,12},{12,8},{9,1... | collective-permute-start | bytes 1572872 | tf_op jit(solution)/shard_map/ppermute | solution.py:20
  4.8 0.9 copy-start.4
  6.4 10.2 %collective-permute-start.3 = (bf16[2,96,128]{2,1,0:T(8,128)(2,1)S(1)}, bf16[2,96,128]{2,1,0:T(8,128)(2,1)S(1)}, u32[]{:S(2)}, u32[]{:S(2)}) collective-permute-start(bf16[2,96,128]{2,1,0:T(8,128)(2,1)S(1)} %get-tuple-element.72), channel_id=1, source_target_pairs={{0,1},{1,0},{2,3},{3,2},{4,5},{5,4},{6,7},{7,6},{8,9},{9,8},{10,11... | collective-permute-start | bytes 147464 | tf_op jit(solution)/shard_map/ppermute | solution.py:20
  6.5 10.1 %collective-permute-start.4 = (bf16[2,96,128]{2,1,0:T(8,128)(2,1)S(1)}, bf16[2,96,128]{2,1,0:T(8,128)(2,1)S(1)}, u32[]{:S(2)}, u32[]{:S(2)}) collective-permute-start(bf16[2,96,128]{2,1,0:T(8,128)(2,1)S(1)} %get-tuple-element.73), channel_id=1, source_target_pairs={{0,2},{1,3},{2,0},{3,1},{4,6},{5,7},{6,4},{7,5},{8,10},{9,11},{10,... | collective-permute-start | bytes 147464 | tf_op jit(solution)/shard_map/ppermute | solution.py:20
  8.0 8.6 %collective-permute-start.5 = (bf16[2,96,128]{2,1,0:T(8,128)(2,1)S(1)}, bf16[2,96,128]{2,1,0:T(8,128)(2,1)S(1)}, u32[]{:S(2)}, u32[]{:S(2)}) collective-permute-start(bf16[2,96,128]{2,1,0:T(8,128)(2,1)S(1)} %get-tuple-element.74), channel_id=1, source_target_pairs={{0,3},{1,2},{2,1},{3,0},{4,7},{5,6},{6,5},{7,4},{8,11},{9,10},{10,... | collective-permute-start | bytes 147464 | tf_op jit(solution)/shard_map/ppermute | solution.py:20
  8.3 2.8 %copy-start = (bf16[512,3,2048]{2,0,1:T(8,128)(2,1)S(1)}, bf16[512,3,2048]{2,0,1:T(8,128)(2,1)}, u32[]{:S(2)}) copy-start(bf16[512,3,2048]{2,0,1:T(8,128)(2,1)} %param.5) | copy-start | bytes 18874372
  11.1 1.4 %copy-start.2 = (bf16[384,2048]{1,0:T(8,128)(2,1)S(1)}, bf16[384,2048]{1,0:T(8,128)(2,1)}, u32[]{:S(2)}) copy-start(bf16[384,2048]{1,0:T(8,128)(2,1)} %refs_4_.1) | copy-start | bytes 4718596
  12.5 7.6 %copy-start.1 = (bf16[512,3,2048]{2,0,1:T(8,128)(2,1)S(1)}, bf16[512,3,2048]{2,0,1:T(8,128)(2,1)}, u32[]{:S(2)}) copy-start(bf16[512,3,2048]{2,0,1:T(8,128)(2,1)} %param.5) | copy-start | bytes 18874372
  16.7 3.3 %collective-permute-start.6 = (bf16[2,3,384,128]{3,2,1,0:T(8,128)(2,1)S(1)}, bf16[2,3,384,128]{3,2,1,0:T(8,128)(2,1)S(1)}, u32[]{:S(2)}, u32[]{:S(2)}) collective-permute-start(bf16[2,3,384,128]{3,2,1,0:T(8,128)(2,1)S(1)} %get-tuple-element.75), channel_id=1, source_target_pairs={{0,1},{1,0},{2,3},{3,2},{4,5},{5,4},{6,7},{7,6},{8,9},{9,8},{10,11... | collective-permute-start | bytes 1769480 | tf_op jit(solution)/shard_map/ppermute | solution.py:20
  17.0 14.0 %collective-permute-start.2 = (bf16[128,2048]{1,0:T(8,128)(2,1)S(1)}, bf16[128,2048]{1,0:T(8,128)(2,1)S(1)}, u32[]{:S(2)}, u32[]{:S(2)}) collective-permute-start(bf16[128,2048]{1,0:T(8,128)(2,1)S(1)} %get-tuple-element.69), channel_id=1, source_target_pairs={{0,4},{4,0},{1,5},{5,1},{2,6},{6,2},{3,7},{7,3},{8,12},{12,8},{9,1... | collective-permute-start | bytes 1572872 | tf_op jit(solution)/shard_map/ppermute | solution.py:20
  18.4 14.3 %collective-permute-start.1 = (bf16[128,2048]{1,0:T(8,128)(2,1)S(1)}, bf16[128,2048]{1,0:T(8,128)(2,1)S(1)}, u32[]{:S(2)}, u32[]{:S(2)}) collective-permute-start(bf16[128,2048]{1,0:T(8,128)(2,1)S(1)} %collective-permute-done.refs_0_), channel_id=1, source_target_pairs={{0,8},{8,0},{16,24},{24,16},{1,9},{9,1},{17,25},{25,17},{2,10},{10... | collective-permute-start | bytes 1572872 | tf_op jit(solution)/shard_map/ppermute | solution.py:20
  23.3 1.6 %collective-permute-start.8 = (bf16[2,3,128,128]{3,2,1,0:T(8,128)(2,1)S(1)}, bf16[2,3,128,128]{3,2,1,0:T(8,128)(2,1)S(1)}, u32[]{:S(2)}, u32[]{:S(2)}) collective-permute-start(bf16[2,3,128,128]{3,2,1,0:T(8,128)(2,1)S(1)} %get-tuple-element.78), channel_id=1, source_target_pairs={{0,1},{1,0},{2,3},{3,2},{4,5},{5,4},{6,7},{7,6},{8,9},{9,8},{10,11... | collective-permute-start | bytes 589832 | tf_op jit(solution)/shard_map/ppermute | solution.py:20
  23.4 9.4 %collective-permute-start.7 = (bf16[1,3,384,128]{3,2,1,0:T(8,128)(2,1)S(1)}, bf16[1,3,384,128]{3,2,1,0:T(8,128)(2,1)S(1)}, u32[]{:S(2)}, u32[]{:S(2)}) collective-permute-start(bf16[1,3,384,128]{3,2,1,0:T(8,128)(2,1)S(1)} %add_convert_fusion.12), channel_id=1, source_target_pairs={{0,2},{1,3},{2,0},{3,1},{4,6},{5,7},{6,4},{7,5},{8,10},{9,11},{10,... | collective-permute-start | bytes 884744 | tf_op jit(solution)/shard_map/ppermute | solution.py:20
  24.9 23.0 %copy-start.5 = (f32[7,64]{1,0:T(8,128)S(1)}, f32[7,64]{1,0:T(8,128)}, u32[]{:S(2)}) copy-start(f32[7,64]{1,0:T(8,128)} %taps_ref.1) | copy-start | bytes 5380
  35.9 1.8 %collective-permute-start.9 = (bf16[2,3,256,128]{3,2,1,0:T(8,128)(2,1)S(1)}, bf16[2,3,256,128]{3,2,1,0:T(8,128)(2,1)S(1)}, u32[]{:S(2)}, u32[]{:S(2)}) collective-permute-start(bf16[2,3,256,128]{3,2,1,0:T(8,128)(2,1)S(1)} %get-tuple-element.81), channel_id=1, source_target_pairs={{0,1},{1,0},{2,3},{3,2},{4,5},{5,4},{6,7},{7,6},{8,9},{9,8},{10,11... | collective-permute-start | bytes 1179656 | tf_op jit(solution)/shard_map/ppermute | solution.py:20
  36.0 5.2 %collective-permute-start.11 = (bf16[1,3,128,128]{3,2,1,0:T(8,128)(2,1)S(1)}, bf16[1,3,128,128]{3,2,1,0:T(8,128)(2,1)S(1)}, u32[]{:S(2)}, u32[]{:S(2)}) collective-permute-start(bf16[1,3,128,128]{3,2,1,0:T(8,128)(2,1)S(1)} %add_convert_fusion.14), channel_id=1, source_target_pairs={{0,2},{1,3},{2,0},{3,1},{4,6},{5,7},{6,4},{7,5},{8,10},{9,11},{10,... | collective-permute-start | bytes 294920 | tf_op jit(solution)/shard_map/ppermute | solution.py:20
  41.2 6.7 %collective-permute-start.12 = (bf16[1,3,256,128]{3,2,1,0:T(8,128)(2,1)S(1)}, bf16[1,3,256,128]{3,2,1,0:T(8,128)(2,1)S(1)}, u32[]{:S(2)}, u32[]{:S(2)}) collective-permute-start(bf16[1,3,256,128]{3,2,1,0:T(8,128)(2,1)S(1)} %add_convert_fusion.13), channel_id=1, source_target_pairs={{0,2},{1,3},{2,0},{3,1},{4,6},{5,7},{6,4},{7,5},{8,10},{9,11},{10,... | collective-permute-start | bytes 589832 | tf_op jit(solution)/shard_map/ppermute | solution.py:20
  43.2 4.7 %collective-permute-start.10 = (bf16[384,128]{1,0:T(8,128)(2,1)S(1)}, bf16[384,128]{1,0:T(8,128)(2,1)S(1)}, u32[]{:S(2)}, u32[]{:S(2)}) collective-permute-start(bf16[384,128]{1,0:T(8,128)(2,1)S(1)} %get-tuple-element.84), channel_id=1, source_target_pairs={{0,4},{4,0},{1,5},{5,1},{2,6},{6,2},{3,7},{7,3},{8,12},{12,8},{9,1... | collective-permute-start | bytes 294920 | tf_op jit(solution)/shard_map/ppermute | solution.py:20
  49.5 6.5 %collective-permute-start.13 = (bf16[3,384,128]{2,1,0:T(8,128)(2,1)S(1)}, bf16[3,384,128]{2,1,0:T(8,128)(2,1)S(1)}, u32[]{:S(2)}, u32[]{:S(2)}) collective-permute-start(bf16[3,384,128]{2,1,0:T(8,128)(2,1)S(1)} %get-tuple-element.88.refs_0_), channel_id=1, source_target_pairs={{0,1},{1,0},{2,3},{3,2},{4,5},{5,4},{6,7},{7,6},{8,9},{9,8},{10,11... | collective-permute-start | bytes 884744 | tf_op jit(solution)/shard_map/ppermute | solution.py:20
  49.6 6.4 %collective-permute-start.16 = (bf16[3,384,128]{2,1,0:T(8,128)(2,1)S(1)}, bf16[3,384,128]{2,1,0:T(8,128)(2,1)S(1)}, u32[]{:S(2)}, u32[]{:S(2)}) collective-permute-start(bf16[3,384,128]{2,1,0:T(8,128)(2,1)S(1)} %get-tuple-element.87.refs_0_), channel_id=1, source_target_pairs={{0,1},{1,0},{2,3},{3,2},{4,5},{5,4},{6,7},{7,6},{8,9},{9,8},{10,11... | collective-permute-start | bytes 884744 | tf_op jit(solution)/shard_map/ppermute | solution.py:20
  50.1 9.0 %collective-permute-start.14 = (bf16[3,384,128]{2,1,0:T(8,128)(2,1)S(1)}, bf16[3,384,128]{2,1,0:T(8,128)(2,1)S(1)}, u32[]{:S(2)}, u32[]{:S(2)}) collective-permute-start(bf16[3,384,128]{2,1,0:T(8,128)(2,1)S(1)} %get-tuple-element.87.refs_0_), channel_id=1, source_target_pairs={{0,2},{1,3},{2,0},{3,1},{4,6},{5,7},{6,4},{7,5},{8,10},{9,11},{10,... | collective-permute-start | bytes 884744 | tf_op jit(solution)/shard_map/ppermute | solution.py:20
  51.3 4.7 %collective-permute-start.17 = (bf16[416,128]{1,0:T(8,128)(2,1)S(1)}, bf16[416,128]{1,0:T(8,128)(2,1)S(1)}, u32[]{:S(2)}, u32[]{:S(2)}) collective-permute-start(bf16[416,128]{1,0:T(8,128)(2,1)S(1)} %get-tuple-element.89), channel_id=1, source_target_pairs={{0,4},{4,0},{1,5},{5,1},{2,6},{6,2},{3,7},{7,3},{8,12},{12,8},{9,1... | collective-permute-start | bytes 319496 | tf_op jit(solution)/shard_map/ppermute | solution.py:20
  59.1 1.6 %collective-permute-start.18 = (bf16[3,384,128]{2,1,0:T(8,128)(2,1)S(1)}, bf16[3,384,128]{2,1,0:T(8,128)(2,1)S(1)}, u32[]{:S(2)}, u32[]{:S(2)}) collective-permute-start(bf16[3,384,128]{2,1,0:T(8,128)(2,1)S(1)} %collective-permute-done.14.refs_2_), channel_id=1, source_target_pairs={{0,1},{1,0},{2,3},{3,2},{4,5},{5,4},{6,7},{7,6},{8,9},{9,8},{10,11... | collective-permute-start | bytes 884744 | tf_op jit(solution)/shard_map/ppermute | solution.py:20
  59.1 9.4 %collective-permute-start.15 = (bf16[3,384,128]{2,1,0:T(8,128)(2,1)S(1)}, bf16[3,384,128]{2,1,0:T(8,128)(2,1)S(1)}, u32[]{:S(2)}, u32[]{:S(2)}) collective-permute-start(bf16[3,384,128]{2,1,0:T(8,128)(2,1)S(1)} %get-tuple-element.88.refs_0_), channel_id=1, source_target_pairs={{0,2},{1,3},{2,0},{3,1},{4,6},{5,7},{6,4},{7,5},{8,10},{9,11},{10,... | collective-permute-start | bytes 884744 | tf_op jit(solution)/shard_map/ppermute | solution.py:20
  62.2 12.0 %collective-permute-start.20 = (bf16[384,512]{1,0:T(8,128)(2,1)S(1)}, bf16[384,512]{1,0:T(8,128)(2,1)S(1)}, u32[]{:S(2)}, u32[]{:S(2)}) collective-permute-start(bf16[384,512]{1,0:T(8,128)(2,1)S(1)} %input_grad.4), channel_id=1, source_target_pairs={{0,4},{4,0},{1,5},{5,1},{2,6},{6,2},{3,7},{7,3},{8,12},{12,8},{9,1... | collective-permute-start | bytes 1179656 | tf_op jit(solution)/shard_map/ppermute | solution.py:20
  68.5 1.6 %collective-permute-start.19 = (bf16[3,384,128]{2,1,0:T(8,128)(2,1)S(1)}, bf16[3,384,128]{2,1,0:T(8,128)(2,1)S(1)}, u32[]{:S(2)}, u32[]{:S(2)}) collective-permute-start(bf16[3,384,128]{2,1,0:T(8,128)(2,1)S(1)} %collective-permute-done.15.refs_2_), channel_id=1, source_target_pairs={{0,1},{1,0},{2,3},{3,2},{4,5},{5,4},{6,7},{7,6},{8,9},{9,8},{10,11... | collective-permute-start | bytes 884744 | tf_op jit(solution)/shard_map/ppermute | solution.py:20
  68.5 14.1 %collective-permute-start.21 = (bf16[384,512]{1,0:T(8,128)(2,1)S(1)}, bf16[384,512]{1,0:T(8,128)(2,1)S(1)}, u32[]{:S(2)}, u32[]{:S(2)}) collective-permute-start(bf16[384,512]{1,0:T(8,128)(2,1)S(1)} %get-tuple-element.97), channel_id=1, source_target_pairs={{0,4},{4,0},{1,5},{5,1},{2,6},{6,2},{3,7},{7,3},{8,12},{12,8},{9,1... | collective-permute-start | bytes 1179656 | tf_op jit(solution)/shard_map/ppermute | solution.py:20
  74.3 10.5 %collective-permute-start.22 = (bf16[384,512]{1,0:T(8,128)(2,1)S(1)}, bf16[384,512]{1,0:T(8,128)(2,1)S(1)}, u32[]{:S(2)}, u32[]{:S(2)}) collective-permute-start(bf16[384,512]{1,0:T(8,128)(2,1)S(1)} %add_convert_fusion.11), channel_id=1, source_target_pairs={{0,8},{8,0},{16,24},{24,16},{1,9},{9,1},{17,25},{25,17},{2,10},{10... | collective-permute-start | bytes 1179656 | tf_op jit(solution)/shard_map/ppermute | solution.py:20
  75.7 15.4 %collective-permute-start.23 = (bf16[384,512]{1,0:T(8,128)(2,1)S(1)}, bf16[384,512]{1,0:T(8,128)(2,1)S(1)}, u32[]{:S(2)}, u32[]{:S(2)}) collective-permute-start(bf16[384,512]{1,0:T(8,128)(2,1)S(1)} %get-tuple-element.101), channel_id=1, source_target_pairs={{0,4},{4,0},{1,5},{5,1},{2,6},{6,2},{3,7},{7,3},{8,12},{12,8},{9,1... | collective-permute-start | bytes 1179656 | tf_op jit(solution)/shard_map/ppermute | solution.py:20
  82.7 9.6 %collective-permute-start.24 = (bf16[384,512]{1,0:T(8,128)(2,1)S(1)}, bf16[384,512]{1,0:T(8,128)(2,1)S(1)}, u32[]{:S(2)}, u32[]{:S(2)}) collective-permute-start(bf16[384,512]{1,0:T(8,128)(2,1)S(1)} %add_convert_fusion.10), channel_id=1, source_target_pairs={{0,8},{8,0},{16,24},{24,16},{1,9},{9,1},{17,25},{25,17},{2,10},{10... | collective-permute-start | bytes 1179656 | tf_op jit(solution)/shard_map/ppermute | solution.py:20
  84.1 19.8 %collective-permute-start.26 = (bf16[384,512]{1,0:T(8,128)(2,1)S(1)}, bf16[384,512]{1,0:T(8,128)(2,1)S(1)}, u32[]{:S(2)}, u32[]{:S(2)}) collective-permute-start(bf16[384,512]{1,0:T(8,128)(2,1)S(1)} %get-tuple-element.110), channel_id=1, source_target_pairs={{0,4},{4,0},{1,5},{5,1},{2,6},{6,2},{3,7},{7,3},{8,12},{12,8},{9,1... | collective-permute-start | bytes 1179656 | tf_op jit(solution)/shard_map/ppermute | solution.py:20
  84.9 7.5 %collective-permute-start.25 = (bf16[384,512]{1,0:T(8,128)(2,1)S(1)}, bf16[384,512]{1,0:T(8,128)(2,1)S(1)}, u32[]{:S(2)}, u32[]{:S(2)}) collective-permute-start(bf16[384,512]{1,0:T(8,128)(2,1)S(1)} %add_convert_fusion.9), channel_id=1, source_target_pairs={{0,0},{8,16},{16,8},{24,24},{1,1},{9,17},{17,9},{25,25},{2,2},{10,... | collective-permute-start | bytes 1179656 | tf_op jit(solution)/shard_map/ppermute | solution.py:601
  91.1 7.1 %copy-start.3 = (bf16[384,2048]{1,0:T(8,128)(2,1)S(1)}, bf16[384,2048]{1,0:T(8,128)(2,1)}, u32[]{:S(2)}) copy-start(bf16[384,2048]{1,0:T(8,128)(2,1)} %refs_4_.1) | copy-start | bytes 4718596
  92.6 11.4 %collective-permute-start.27 = (bf16[384,512]{1,0:T(8,128)(2,1)S(1)}, bf16[384,512]{1,0:T(8,128)(2,1)S(1)}, u32[]{:S(2)}, u32[]{:S(2)}) collective-permute-start(bf16[384,512]{1,0:T(8,128)(2,1)S(1)} %get-tuple-element.130), channel_id=1, source_target_pairs={{0,8},{8,0},{16,24},{24,16},{1,9},{9,1},{17,25},{25,17},{2,10},{10... | collective-permute-start | bytes 1179656 | tf_op jit(solution)/shard_map/ppermute | solution.py:20
  97.4 6.7 %collective-permute-start.28 = (bf16[384,512]{1,0:T(8,128)(2,1)S(1)}, bf16[384,512]{1,0:T(8,128)(2,1)S(1)}, u32[]{:S(2)}, u32[]{:S(2)}) collective-permute-start(bf16[384,512]{1,0:T(8,128)(2,1)S(1)} %add_convert_fusion.7), channel_id=1, source_target_pairs={{0,0},{8,16},{16,8},{24,24},{1,1},{9,17},{17,9},{25,25},{2,2},{10,... | collective-permute-start | bytes 1179656 | tf_op jit(solution)/shard_map/ppermute | solution.py:601
  104.3 9.3 %collective-permute-start.29 = (bf16[384,512]{1,0:T(8,128)(2,1)S(1)}, bf16[384,512]{1,0:T(8,128)(2,1)S(1)}, u32[]{:S(2)}, u32[]{:S(2)}) collective-permute-start(bf16[384,512]{1,0:T(8,128)(2,1)S(1)} %get-tuple-element.128), channel_id=1, source_target_pairs={{0,8},{8,0},{16,24},{24,16},{1,9},{9,1},{17,25},{25,17},{2,10},{10... | collective-permute-start | bytes 1179656 | tf_op jit(solution)/shard_map/ppermute | solution.py:20
  107.9 6.6 %collective-permute-start.30 = (bf16[384,512]{1,0:T(8,128)(2,1)S(1)}, bf16[384,512]{1,0:T(8,128)(2,1)S(1)}, u32[]{:S(2)}, u32[]{:S(2)}) collective-permute-start(bf16[384,512]{1,0:T(8,128)(2,1)S(1)} %add_convert_fusion.4), channel_id=1, source_target_pairs={{0,0},{8,16},{16,8},{24,24},{1,1},{9,17},{17,9},{25,25},{2,2},{10,... | collective-permute-start | bytes 1179656 | tf_op jit(solution)/shard_map/ppermute | solution.py:601
  109.1 15.8 %collective-permute-start.31 = (bf16[2,128,128]{2,1,0:T(8,128)(2,1)S(1)}, bf16[2,128,128]{2,1,0:T(8,128)(2,1)S(1)}, u32[]{:S(2)}, u32[]{:S(2)}) collective-permute-start(bf16[2,128,128]{2,1,0:T(8,128)(2,1)S(1)} %get-tuple-element.120), channel_id=1, source_target_pairs={{0,1},{1,0},{2,3},{3,2},{4,5},{5,4},{6,7},{7,6},{8,9},{9,8},{10,11... | collective-permute-start | bytes 196616 | tf_op jit(solution)/shard_map/ppermute | solution.py:20
  109.2 15.7 %collective-permute-start.32 = (bf16[2,128,128]{2,1,0:T(8,128)(2,1)S(1)}, bf16[2,128,128]{2,1,0:T(8,128)(2,1)S(1)}, u32[]{:S(2)}, u32[]{:S(2)}) collective-permute-start(bf16[2,128,128]{2,1,0:T(8,128)(2,1)S(1)} %get-tuple-element.121), channel_id=1, source_target_pairs={{0,2},{1,3},{2,0},{3,1},{4,6},{5,7},{6,4},{7,5},{8,10},{9,11},{10,... | collective-permute-start | bytes 196616 | tf_op jit(solution)/shard_map/ppermute | solution.py:20
  110.5 14.5 %collective-permute-start.33 = (bf16[2,128,128]{2,1,0:T(8,128)(2,1)S(1)}, bf16[2,128,128]{2,1,0:T(8,128)(2,1)S(1)}, u32[]{:S(2)}, u32[]{:S(2)}) collective-permute-start(bf16[2,128,128]{2,1,0:T(8,128)(2,1)S(1)} %get-tuple-element.122), channel_id=1, source_target_pairs={{0,3},{1,2},{2,1},{3,0},{4,7},{5,6},{6,5},{7,4},{8,11},{9,10},{10,... | collective-permute-start | bytes 196616 | tf_op jit(solution)/shard_map/ppermute | solution.py:20
  113.7 11.2 %collective-permute-start.34 = (bf16[384,512]{1,0:T(8,128)(2,1)S(1)}, bf16[384,512]{1,0:T(8,128)(2,1)S(1)}, u32[]{:S(2)}, u32[]{:S(2)}) collective-permute-start(bf16[384,512]{1,0:T(8,128)(2,1)S(1)} %add_convert_fusion.2), channel_id=1, source_target_pairs={{0,0},{8,16},{16,8},{24,24},{1,1},{9,17},{17,9},{25,25},{2,2},{10,... | collective-permute-start | bytes 1179656 | tf_op jit(solution)/shard_map/ppermute | solution.py:601
  114.6 14.1 %collective-permute-start.35 = (bf16[384,512]{1,0:T(8,128)(2,1)S(1)}, bf16[384,512]{1,0:T(8,128)(2,1)S(1)}, u32[]{:S(2)}, u32[]{:S(2)}) collective-permute-start(bf16[384,512]{1,0:T(8,128)(2,1)S(1)} %add_convert_fusion.1), channel_id=1, source_target_pairs={{0,8},{8,0},{16,24},{24,16},{1,9},{9,1},{17,25},{25,17},{2,10},{10... | collective-permute-start | bytes 1179656 | tf_op jit(solution)/shard_map/ppermute | solution.py:20
  125.1 9.3 %collective-permute-start.36 = (bf16[384,512]{1,0:T(8,128)(2,1)S(1)}, bf16[384,512]{1,0:T(8,128)(2,1)S(1)}, u32[]{:S(2)}, u32[]{:S(2)}) collective-permute-start(bf16[384,512]{1,0:T(8,128)(2,1)S(1)} %add_convert_fusion), channel_id=1, source_target_pairs={{0,8},{8,0},{16,24},{24,16},{1,9},{9,1},{17,25},{25,17},{2,10},{10... | collective-permute-start | bytes 1179656 | tf_op jit(solution)/shard_map/ppermute | solution.py:20

commit v14 on v13

--- a/solution.py
+++ b/solution.py
@@ -574,24 +574,25 @@
     line = lax.axis_size("row") == 4
     inward, across, summed, done = ([None] * chunks for _ in range(4))
     pair = cross = filled = None
-    marks = []
+    marks, late = [], []
     for slot in range(chunks + 3):
         if slot < chunks:
             total = after(own_part[slot], *marks).astype(jnp.float32)
             for of in sent:
                 total = total + of[slot].astype(jnp.float32)
             inward[slot] = total.astype(jnp.bfloat16)
-            marks = [inward[slot]]
+            marks = [inward[slot]] + late
+            late = []
         if not line:
             if slot < chunks:
                 done[slot] = lax.psum(inward[slot], "row")
         else:
+            if 0 <= slot - 2 < chunks:
+                summed[slot - 2] = added(after(across[slot - 2], *marks), cross)
+                marks = [summed[slot - 2]]
             if 0 <= slot - 1 < chunks:
                 across[slot - 1] = added(after(inward[slot - 1], *marks), pair)
                 marks = [across[slot - 1]]
-            if 0 <= slot - 2 < chunks:
-                summed[slot - 2] = added(after(across[slot - 2], *marks), cross)
-                marks = [summed[slot - 2]]
             if 0 <= slot - 3 < chunks:
                 done[slot - 3] = jnp.where(outer, pair, summed[slot - 3])
             if slot < chunks + 2:
@@ -604,12 +605,10 @@
             marks = [own_part[1]]
             for k, parts_of in enumerate(held):
                 sent[k] += [swap(after(part, *marks), "col", k + 1) for part in parts_of]
-        if slot in (2, 4):
-            filled = weight_grad(filled, [after(lhs[0], *marks)] + lhs[1:], xs, slot // 2 - 1, 3, width)
+        if slot in (2, 3):
+            filled = weight_grad(filled, [after(lhs[0], *marks)] + lhs[1:], xs, slot - 2, 3, width)
             marks = [filled[1]]
-        if slot == 4:
-            marks += late
-        if slot == 3:
+        if slot == 1:
             blocks = split_rows(place, [after(blocks[0], *marks)] + blocks[1:], n_depth)
             blocks = [block if r == 0 else swap(block, "depth", r) for r, block in enumerate(blocks)]
             late = blocks[1:]

time: 136 us -> 143 us (1.051)
  starting transfers between devices: 43 us -> 49.1 us
    ppermute x33, starting transfers between devices: 40.1 us -> 46.2 us  [swap(): return lax.ppermute(value, axis, [(i, i ^ flip) for i in range(count)])]
  transfers between devices with their start and end apart: 37 -> 37, of which waited for: 17 -> 20; matrix products, arithmetic and copies ran while one was open for 1% -> 1% of each run, Pallas kernels for 22% -> 21%
where the time goes in v14:
time: 143 us; the launch traced here: 142 us
  starting transfers between devices  49.1 us (34%)
  waiting for transfers between devices  47.9 us (33%)
  Pallas kernels  35.1 us (25%)
  local copies, waits for them, and re-layouts  6.22 us (4%)
  other arithmetic  3.05 us (2%)
    ppermute x33, waiting for transfers between devices, swap(): return lax.ppermute(value, axis, [(i, i ^ flip) for i in range(count)])  47.9 us
    ppermute x33, starting transfers between devices, swap(): return lax.ppermute(value, axis, [(i, i ^ flip) for i in range(count)])  46.2 us
    pallas_call x2, Pallas kernels, weight_grad(): pl.pallas_call(functools.partial(weight_grad_kernel, chained=chained, gro...  11.2 us
    pallas_call x3, Pallas kernels, project(): pl.pallas_call(functools.partial(project_kernel, pieces=len(xs), mode=mod...  10.3 us
    pallas_call x4, Pallas kernels, input_grad(): pl.pallas_call(functools.partial(input_grad_kernel if single else input_g...  7.49 us
    unnamed x12, local copies, waits for them, and re-layouts  5.14 us
    ppermute x4, starting transfers between devices, on_device(): lax.ppermute(across[slot - 1], 'row', [(0, 0), (1, 2), (2, 1), (3, 3)])  2.92 us
  transfers between devices with their start and end apart: 37, of which 20 were waited for; matrix products, arithmetic and copies ran while one was open for 1% of the time, Pallas kernels for 21%

profile of v14, /device:TPU:0, one launch (start us, length us, event | category | flops | bytes accessed | tf_op | source)
XLA Modules:
  0.0 142.4 jit_solution(7090964981720940600)
XLA Ops:
  0.6 1.1 constant_dynamic-slice_fusion
  1.7 3.0 %collective-permute-start = (bf16[128,2048]{1,0:T(8,128)(2,1)S(1)}, bf16[128,2048]{1,0:T(8,128)(2,1)S(1)}, u32[]{:S(2)}, u32[]{:S(2)}) collective-permute-start(bf16[128,2048]{1,0:T(8,128)(2,1)S(1)} %constant_dynamic-slice_fusion), channel_id=1, source_target_pairs={{0,4},{4,0},{1,5},{5,1},{2,6},{6,2},{3,7},{7,3},{8,12},{12,8},{9,1... | collective-permute-start | bytes 1572872 | tf_op jit(solution)/shard_map/ppermute | solution.py:20
  4.9 0.9 copy-done.4
  5.8 0.6 split.2
  6.5 1.6 %collective-permute-start.4 = (bf16[2,96,128]{2,1,0:T(8,128)(2,1)S(1)}, bf16[2,96,128]{2,1,0:T(8,128)(2,1)S(1)}, u32[]{:S(2)}, u32[]{:S(2)}) collective-permute-start(bf16[2,96,128]{2,1,0:T(8,128)(2,1)S(1)} %get-tuple-element.73), channel_id=1, source_target_pairs={{0,2},{1,3},{2,0},{3,1},{4,6},{5,7},{6,4},{7,5},{8,10},{9,11},{10,... | collective-permute-start | bytes 147464 | tf_op jit(solution)/shard_map/ppermute | solution.py:20
  8.3 2.8 %copy-done = bf16[512,3,2048]{2,0,1:T(8,128)(2,1)S(1)} copy-done((bf16[512,3,2048]{2,0,1:T(8,128)(2,1)S(1)}, bf16[512,3,2048]{2,0,1:T(8,128)(2,1)}, u32[]{:S(2)}) %copy-start) | copy-done | bytes 6291480
  11.1 1.4 copy-done.2
  12.5 4.1 %project.3 = (bf16[2,3,384,128]{3,2,1,0:T(8,128)(2,1)S(1)}, bf16[2,3,384,128]{3,2,1,0:T(8,128)(2,1)S(1)}, bf16[128,2048]{1,0:T(8,128)(2,1)S(1)}) custom-call(s32[4]{0:T(128)S(1)} %pad_add_fusion.place, bf16[384,2048]{1,0:T(8,128)(2,1)S(1)} %copy-done.2, bf16[3,512,2048]{2,1,0:T(8,128)(2,1)S(1)} %bitcast.6), custom_call_target="tpu_custom_call" | custom-call | flops 1 | bytes 1 | tf_op jit(solution)/shard_map/project/pallas_call | solution.py:97
  17.0 1.4 collective-permute-start.2
  18.4 1.6 %collective-permute-start.1 = (bf16[128,2048]{1,0:T(8,128)(2,1)S(1)}, bf16[128,2048]{1,0:T(8,128)(2,1)S(1)}, u32[]{:S(2)}, u32[]{:S(2)}) collective-permute-start(bf16[128,2048]{1,0:T(8,128)(2,1)S(1)} %collective-permute-done.refs_0_), channel_id=1, source_target_pairs={{0,8},{8,0},{16,24},{24,16},{1,9},{9,1},{17,25},{25,17},{2,10},{10... | collective-permute-start | bytes 1572872 | tf_op jit(solution)/shard_map/ppermute | solution.py:20
  20.1 3.1 %project.4 = (bf16[2,3,128,128]{3,2,1,0:T(8,128)(2,1)S(1)}, bf16[2,3,128,128]{3,2,1,0:T(8,128)(2,1)S(1)}) custom-call(s32[4]{0:T(128)S(1)} %pad_add_fusion.place, bf16[128,2048]{1,0:T(8,128)(2,1)S(1)} %collective-permute-done.refs_0_, bf16[3,512,2048]{2,1,0:T(8,128)(2,1)S(1)} %bitcast.7), custom_call_target="tpu_custom_call" | custom-call | flops 1 | bytes 1 | tf_op jit(solution)/shard_map/project/pallas_call | solution.py:97
  23.4 1.6 %collective-permute-start.7 = (bf16[1,3,384,128]{3,2,1,0:T(8,128)(2,1)S(1)}, bf16[1,3,384,128]{3,2,1,0:T(8,128)(2,1)S(1)}, u32[]{:S(2)}, u32[]{:S(2)}) collective-permute-start(bf16[1,3,384,128]{3,2,1,0:T(8,128)(2,1)S(1)} %add_convert_fusion.12), channel_id=1, source_target_pairs={{0,2},{1,3},{2,0},{3,1},{4,6},{5,7},{6,4},{7,5},{8,10},{9,11},{10,... | collective-permute-start | bytes 884744 | tf_op jit(solution)/shard_map/ppermute | solution.py:20
  25.0 6.1 %collective-permute-done.2.refs_2_ = bf16[128,2048]{1,0:T(8,128)(2,1)S(1)} collective-permute-done((bf16[128,2048]{1,0:T(8,128)(2,1)S(1)}, bf16[128,2048]{1,0:T(8,128)(2,1)S(1)}, u32[]{:S(2)}, u32[]{:S(2)}) %collective-permute-start.2) | collective-permute-done | bytes 524320 | tf_op jit(solution)/shard_map/ppermute | solution.py:20
  31.0 1.7 %collective-permute-done.7.refs_4_ = bf16[1,3,384,128]{3,2,1,0:T(8,128)(2,1)S(1)} collective-permute-done((bf16[1,3,384,128]{3,2,1,0:T(8,128)(2,1)S(1)}, bf16[1,3,384,128]{3,2,1,0:T(8,128)(2,1)S(1)}, u32[]{:S(2)}, u32[]{:S(2)}) %collective-permute-start.7) | collective-permute-done | bytes 294944 | tf_op jit(solution)/shard_map/ppermute | solution.py:20
  32.8 3.1 %project.5 = (bf16[2,3,256,128]{3,2,1,0:T(8,128)(2,1)S(1)}, bf16[2,3,256,128]{3,2,1,0:T(8,128)(2,1)S(1)}, bf16[384,2048]{1,0:T(8,128)(2,1)S(1)}) custom-call(s32[4]{0:T(128)S(1)} %pad_add_fusion.place, bf16[128,2048]{1,0:T(8,128)(2,1)S(1)} %collective-permute-done.refs_0_, bf16[128,2048]{1,0:T(8,128)(2,1)S(1)} %collective-permute-done.1.refs_1_, ...), custom_call_target="tpu_custom_call" | custom-call | flops 1 | bytes 1 | tf_op jit(solution)/shard_map/project/pallas_call | solution.py:97
  36.0 1.6 %collective-permute-start.11 = (bf16[1,3,128,128]{3,2,1,0:T(8,128)(2,1)S(1)}, bf16[1,3,128,128]{3,2,1,0:T(8,128)(2,1)S(1)}, u32[]{:S(2)}, u32[]{:S(2)}) collective-permute-start(bf16[1,3,128,128]{3,2,1,0:T(8,128)(2,1)S(1)} %add_convert_fusion.14), channel_id=1, source_target_pairs={{0,2},{1,3},{2,0},{3,1},{4,6},{5,7},{6,4},{7,5},{8,10},{9,11},{10,... | collective-permute-start | bytes 294920 | tf_op jit(solution)/shard_map/ppermute | solution.py:20
  37.7 3.4 %collective-permute-done.11.refs_7_ = bf16[1,3,128,128]{3,2,1,0:T(8,128)(2,1)S(1)} collective-permute-done((bf16[1,3,128,128]{3,2,1,0:T(8,128)(2,1)S(1)}, bf16[1,3,128,128]{3,2,1,0:T(8,128)(2,1)S(1)}, u32[]{:S(2)}, u32[]{:S(2)}) %collective-permute-start.11) | collective-permute-done | bytes 98336 | tf_op jit(solution)/shard_map/ppermute | solution.py:20
  41.2 1.5 %collective-permute-start.12 = (bf16[1,3,256,128]{3,2,1,0:T(8,128)(2,1)S(1)}, bf16[1,3,256,128]{3,2,1,0:T(8,128)(2,1)S(1)}, u32[]{:S(2)}, u32[]{:S(2)}) collective-permute-start(bf16[1,3,256,128]{3,2,1,0:T(8,128)(2,1)S(1)} %add_convert_fusion.13), channel_id=1, source_target_pairs={{0,2},{1,3},{2,0},{3,1},{4,6},{5,7},{6,4},{7,5},{8,10},{9,11},{10,... | collective-permute-start | bytes 589832 | tf_op jit(solution)/shard_map/ppermute | solution.py:20
  42.7 0.6 merge.1
  43.2 0.7 collective-permute-start.10
  44.0 4.0 %collective-permute-done.10.refs_1_ = bf16[384,128]{1,0:T(8,128)(2,1)S(1)} collective-permute-done((bf16[384,128]{1,0:T(8,128)(2,1)S(1)}, bf16[384,128]{1,0:T(8,128)(2,1)S(1)}, u32[]{:S(2)}, u32[]{:S(2)}) %collective-permute-start.10) | collective-permute-done | bytes 98336 | tf_op jit(solution)/shard_map/ppermute | solution.py:20
  47.9 1.5 %middle.1 = (bf16[3,384,128]{2,1,0:T(8,128)(2,1)S(1)}, bf16[3,384,128]{2,1,0:T(8,128)(2,1)S(1)}, bf16[416,128]{1,0:T(8,128)(2,1)S(1)}, bf16[416,128]{1,0:T(8,128)(2,1)S(1)}) custom-call(s32[4]{0:T(128)S(1)} %pad_add_fusion.place, f32[7,64]{1,0:T(8,128)S(1)} %copy-done.5, bf16[384,128]{1,0:T(8,128)(2,1)S(1)} %get-tuple-element.83.refs_0_, ...), custom_call_target="tpu_custom_call" | custom-call | flops 1 | bytes 1 | tf_op jit(solution)/shard_map/middle/pallas_call | solution.py:326
  50.1 1.2 collective-permute-start.14
  51.3 0.7 collective-permute-start.17
  51.9 4.1 %collective-permute-done.17.refs_1_ = bf16[416,128]{1,0:T(8,128)(2,1)S(1)} collective-permute-done((bf16[416,128]{1,0:T(8,128)(2,1)S(1)}, bf16[416,128]{1,0:T(8,128)(2,1)S(1)}, u32[]{:S(2)}, u32[]{:S(2)}) %collective-permute-start.17) | collective-permute-done | bytes 106528 | tf_op jit(solution)/shard_map/ppermute | solution.py:20
  56.0 3.1 %collective-permute-done.14.refs_2_ = bf16[3,384,128]{2,1,0:T(8,128)(2,1)S(1)} collective-permute-done((bf16[3,384,128]{2,1,0:T(8,128)(2,1)S(1)}, bf16[3,384,128]{2,1,0:T(8,128)(2,1)S(1)}, u32[]{:S(2)}, u32[]{:S(2)}) %collective-permute-start.14) | collective-permute-done | bytes 294944 | tf_op jit(solution)/shard_map/ppermute | solution.py:20
  59.1 1.2 collective-permute-start.15
  60.6 0.7 assemble.2.grad_ref.refs_1_.refs_3_
  61.4 0.8 input_grad.4
  62.2 0.7 collective-permute-start.20
  62.9 3.0 %input_grad.5 = (bf16[384,512]{1,0:T(8,128)(2,1)S(1)}, bf16[384,512]{1,0:T(8,128)(2,1)S(1)}, bf16[384,512]{1,0:T(8,128)(2,1)S(1)}) custom-call(bf16[384,1536]{1,0:T(8,128)(2,1)S(1)} %assemble.2.grad_ref.refs_1_.refs_3_, bf16[3,512,2048]{2,1,0:T(8,128)(2,1)S(1)} %bitcast.10), custom_call_target="tpu_custom_call" | custom-call | flops 1 | bytes 1 | tf_op jit(solution)/shard_map/input_grad/pallas_call | solution.py:414
  65.9 2.6 %collective-permute-done.15.refs_2_ = bf16[3,384,128]{2,1,0:T(8,128)(2,1)S(1)} collective-permute-done((bf16[3,384,128]{2,1,0:T(8,128)(2,1)S(1)}, bf16[3,384,128]{2,1,0:T(8,128)(2,1)S(1)}, u32[]{:S(2)}, u32[]{:S(2)}) %collective-permute-start.15) | collective-permute-done | bytes 294944 | tf_op jit(solution)/shard_map/ppermute | solution.py:20
  68.5 0.7 collective-permute-start.21
  69.1 0.9 collective-permute-done.19.refs_3_
  70.1 0.7 assemble.3.grad_ref.refs_0_.refs_2_
  70.8 0.8 input_grad.6
  71.6 2.6 %collective-permute-done.20 = bf16[384,512]{1,0:T(8,128)(2,1)S(1)} collective-permute-done((bf16[384,512]{1,0:T(8,128)(2,1)S(1)}, bf16[384,512]{1,0:T(8,128)(2,1)S(1)}, u32[]{:S(2)}, u32[]{:S(2)}) %collective-permute-start.20) | collective-permute-done | bytes 393248 | tf_op jit(solution)/shard_map/ppermute | solution.py:20
  74.3 1.4 collective-permute-start.22
  75.7 0.7 collective-permute-start.23
  76.3 3.0 %input_grad.7 = (bf16[384,512]{1,0:T(8,128)(2,1)S(1)}, bf16[384,512]{1,0:T(8,128)(2,1)S(1)}, bf16[384,512]{1,0:T(8,128)(2,1)S(1)}) custom-call(bf16[384,1536]{1,0:T(8,128)(2,1)S(1)} %assemble.3.grad_ref.refs_0_.refs_2_, bf16[3,512,2048]{2,1,0:T(8,128)(2,1)S(1)} %bitcast.12), custom_call_target="tpu_custom_call" | custom-call | flops 1 | bytes 1 | tf_op jit(solution)/shard_map/input_grad/pallas_call | solution.py:414
  79.3 3.3 %collective-permute-done.21 = bf16[384,512]{1,0:T(8,128)(2,1)S(1)} collective-permute-done((bf16[384,512]{1,0:T(8,128)(2,1)S(1)}, bf16[384,512]{1,0:T(8,128)(2,1)S(1)}, u32[]{:S(2)}, u32[]{:S(2)}) %collective-permute-start.21) | collective-permute-done | bytes 393248 | tf_op jit(solution)/shard_map/ppermute | solution.py:20
  82.7 1.2 collective-permute-done.22
  84.0 0.7 collective-permute-start.27
  84.7 4.4 %collective-permute-start.28 = (bf16[384,512]{1,0:T(8,128)(2,1)S(1)}, bf16[384,512]{1,0:T(8,128)(2,1)S(1)}, u32[]{:S(2)}, u32[]{:S(2)}) collective-permute-start(bf16[384,512]{1,0:T(8,128)(2,1)S(1)} %add_convert_fusion.10), channel_id=1, source_target_pairs={{0,8},{8,0},{16,24},{24,16},{1,9},{9,1},{17,25},{25,17},{2,10},{10... | collective-permute-start | bytes 1179656 | tf_op jit(solution)/shard_map/ppermute | solution.py:20
  89.1 0.6 split.3
  89.8 1.3 collective-permute-start.25
  91.1 0.6 collective-permute-start.26
  91.8 0.7 collective-permute-start.29
  92.5 2.1 %collective-permute-done.25.refs_2_ = bf16[2,128,128]{2,1,0:T(8,128)(2,1)S(1)} collective-permute-done((bf16[2,128,128]{2,1,0:T(8,128)(2,1)S(1)}, bf16[2,128,128]{2,1,0:T(8,128)(2,1)S(1)}, u32[]{:S(2)}, u32[]{:S(2)}) %collective-permute-start.25) | collective-permute-done | bytes 65568 | tf_op jit(solution)/shard_map/ppermute | solution.py:20
  94.6 0.8 collective-permute-done.26.refs_3_
  95.8 0.9 collective-permute-start.30
  96.7 3.4 %collective-permute-start.31 = (bf16[384,512]{1,0:T(8,128)(2,1)S(1)}, bf16[384,512]{1,0:T(8,128)(2,1)S(1)}, u32[]{:S(2)}, u32[]{:S(2)}) collective-permute-start(bf16[384,512]{1,0:T(8,128)(2,1)S(1)} %get-tuple-element.130), channel_id=1, source_target_pairs={{0,8},{8,0},{16,24},{24,16},{1,9},{9,1},{17,25},{25,17},{2,10},{10... | collective-permute-start | bytes 1179656 | tf_op jit(solution)/shard_map/ppermute | solution.py:20
  100.1 5.6 %weight_grad.2 = (f32[3,512,2048]{2,1,0:T(8,128)}, f32[8,128]{1,0:T(8,128)S(1)}) custom-call(bf16[384,1536]{1,0:T(8,128)(2,1)S(1)} %assemble.3.grad_ref.refs_0_.refs_2_, bf16[384,1536]{1,0:T(8,128)(2,1)S(1)} %assemble.2.grad_ref.refs_1_.refs_3_, bf16[384,2048]{1,0:T(8,128)(2,1)S(1)} %copy-done.3, bf16[384,2048]{1,0:T(8,128)(2,1)S(1)} %get-tuple-element.110.refs_3_.refs_5_), custom_call_target="tpu_custom_call" | custom-call | flops 1 | bytes 1 | tf_op jit(solution)/shard_map/weight_grad/pallas_call | solution.py:471
  106.0 2.9 %collective-permute-done.31 = bf16[384,512]{1,0:T(8,128)(2,1)S(1)} collective-permute-done((bf16[384,512]{1,0:T(8,128)(2,1)S(1)}, bf16[384,512]{1,0:T(8,128)(2,1)S(1)}, u32[]{:S(2)}, u32[]{:S(2)}) %collective-permute-start.31) | collective-permute-done | bytes 393248 | tf_op jit(solution)/shard_map/ppermute | solution.py:20
  109.0 0.7 collective-permute-start.32
  109.7 3.4 %collective-permute-start.33 = (bf16[384,512]{1,0:T(8,128)(2,1)S(1)}, bf16[384,512]{1,0:T(8,128)(2,1)S(1)}, u32[]{:S(2)}, u32[]{:S(2)}) collective-permute-start(bf16[384,512]{1,0:T(8,128)(2,1)S(1)} %get-tuple-element.128), channel_id=1, source_target_pairs={{0,8},{8,0},{16,24},{24,16},{1,9},{9,1},{17,25},{25,17},{2,10},{10... | collective-permute-start | bytes 1179656 | tf_op jit(solution)/shard_map/ppermute | solution.py:20
  113.1 5.6 %weight_grad.3 = (f32[3,512,2048]{2,1,0:T(8,128)}, f32[8,128]{1,0:T(8,128)S(1)}) custom-call(f32[3,512,2048]{2,1,0:T(8,128)} %get-tuple-element.111.refs_0_, f32[8,128]{1,0:T(8,128)S(1)} %get-tuple-element.112.refs_1_, bf16[384,1536]{1,0:T(8,128)(2,1)S(1)} %assemble.3.grad_ref.refs_0_.refs_2_, ...), custom_call_target="tpu_custom_call", output_to_operand_aliasing={{0}: (0, {})} | custom-call | flops 1 | bytes 1 | tf_op jit(solution)/shard_map/weight_grad/pallas_call | solution.py:471
  118.8 2.0 %collective-permute-done.33 = bf16[384,512]{1,0:T(8,128)(2,1)S(1)} collective-permute-done((bf16[384,512]{1,0:T(8,128)(2,1)S(1)}, bf16[384,512]{1,0:T(8,128)(2,1)S(1)}, u32[]{:S(2)}, u32[]{:S(2)}) %collective-permute-start.33) | collective-permute-done | bytes 393248 | tf_op jit(solution)/shard_map/ppermute | solution.py:20
  120.9 0.7 collective-permute-start.34
  121.7 4.5 %collective-permute-start.35 = (bf16[384,512]{1,0:T(8,128)(2,1)S(1)}, bf16[384,512]{1,0:T(8,128)(2,1)S(1)}, u32[]{:S(2)}, u32[]{:S(2)}) collective-permute-start(bf16[384,512]{1,0:T(8,128)(2,1)S(1)} %add_convert_fusion.2), channel_id=1, source_target_pairs={{0,8},{8,0},{16,24},{24,16},{1,9},{9,1},{17,25},{25,17},{2,10},{10... | collective-permute-start | bytes 1179656 | tf_op jit(solution)/shard_map/ppermute | solution.py:20
  126.3 7.0 %collective-permute-start.36 = (bf16[384,512]{1,0:T(8,128)(2,1)S(1)}, bf16[384,512]{1,0:T(8,128)(2,1)S(1)}, u32[]{:S(2)}, u32[]{:S(2)}) collective-permute-start(bf16[384,512]{1,0:T(8,128)(2,1)S(1)} %add_convert_fusion), channel_id=1, source_target_pairs={{0,8},{8,0},{16,24},{24,16},{1,9},{9,1},{17,25},{25,17},{2,10},{10... | collective-permute-start | bytes 1179656 | tf_op jit(solution)/shard_map/ppermute | solution.py:20
  133.3 1.4 join.1
  134.7 6.3 %collective-permute-done.36 = bf16[384,512]{1,0:T(8,128)(2,1)S(1)} collective-permute-done((bf16[384,512]{1,0:T(8,128)(2,1)S(1)}, bf16[384,512]{1,0:T(8,128)(2,1)S(1)}, u32[]{:S(2)}, u32[]{:S(2)}) %collective-permute-start.36) | collective-permute-done | bytes 393248 | tf_op jit(solution)/shard_map/ppermute | solution.py:20
  141.1 1.3 pad_maximum_fusion
  (60 shorter events, 4.0 us)
Async XLA Ops:
  1.7 15.0 %collective-permute-start = (bf16[128,2048]{1,0:T(8,128)(2,1)S(1)}, bf16[128,2048]{1,0:T(8,128)(2,1)S(1)}, u32[]{:S(2)}, u32[]{:S(2)}) collective-permute-start(bf16[128,2048]{1,0:T(8,128)(2,1)S(1)} %constant_dynamic-slice_fusion), channel_id=1, source_target_pairs={{0,4},{4,0},{1,5},{5,1},{2,6},{6,2},{3,7},{7,3},{8,12},{12,8},{9,1... | collective-permute-start | bytes 1572872 | tf_op jit(solution)/shard_map/ppermute | solution.py:20
  4.8 0.9 copy-start.4
  6.4 10.2 %collective-permute-start.3 = (bf16[2,96,128]{2,1,0:T(8,128)(2,1)S(1)}, bf16[2,96,128]{2,1,0:T(8,128)(2,1)S(1)}, u32[]{:S(2)}, u32[]{:S(2)}) collective-permute-start(bf16[2,96,128]{2,1,0:T(8,128)(2,1)S(1)} %get-tuple-element.72), channel_id=1, source_target_pairs={{0,1},{1,0},{2,3},{3,2},{4,5},{5,4},{6,7},{7,6},{8,9},{9,8},{10,11... | collective-permute-start | bytes 147464 | tf_op jit(solution)/shard_map/ppermute | solution.py:20
  6.5 10.1 %collective-permute-start.4 = (bf16[2,96,128]{2,1,0:T(8,128)(2,1)S(1)}, bf16[2,96,128]{2,1,0:T(8,128)(2,1)S(1)}, u32[]{:S(2)}, u32[]{:S(2)}) collective-permute-start(bf16[2,96,128]{2,1,0:T(8,128)(2,1)S(1)} %get-tuple-element.73), channel_id=1, source_target_pairs={{0,2},{1,3},{2,0},{3,1},{4,6},{5,7},{6,4},{7,5},{8,10},{9,11},{10,... | collective-permute-start | bytes 147464 | tf_op jit(solution)/shard_map/ppermute | solution.py:20
  8.0 8.6 %collective-permute-start.5 = (bf16[2,96,128]{2,1,0:T(8,128)(2,1)S(1)}, bf16[2,96,128]{2,1,0:T(8,128)(2,1)S(1)}, u32[]{:S(2)}, u32[]{:S(2)}) collective-permute-start(bf16[2,96,128]{2,1,0:T(8,128)(2,1)S(1)} %get-tuple-element.74), channel_id=1, source_target_pairs={{0,3},{1,2},{2,1},{3,0},{4,7},{5,6},{6,5},{7,4},{8,11},{9,10},{10,... | collective-permute-start | bytes 147464 | tf_op jit(solution)/shard_map/ppermute | solution.py:20
  8.3 2.8 %copy-start = (bf16[512,3,2048]{2,0,1:T(8,128)(2,1)S(1)}, bf16[512,3,2048]{2,0,1:T(8,128)(2,1)}, u32[]{:S(2)}) copy-start(bf16[512,3,2048]{2,0,1:T(8,128)(2,1)} %param.5) | copy-start | bytes 18874372
  11.1 1.4 copy-start.2
  12.5 7.6 %copy-start.1 = (bf16[512,3,2048]{2,0,1:T(8,128)(2,1)S(1)}, bf16[512,3,2048]{2,0,1:T(8,128)(2,1)}, u32[]{:S(2)}) copy-start(bf16[512,3,2048]{2,0,1:T(8,128)(2,1)} %param.5) | copy-start | bytes 18874372
  16.7 3.3 %collective-permute-start.6 = (bf16[2,3,384,128]{3,2,1,0:T(8,128)(2,1)S(1)}, bf16[2,3,384,128]{3,2,1,0:T(8,128)(2,1)S(1)}, u32[]{:S(2)}, u32[]{:S(2)}) collective-permute-start(bf16[2,3,384,128]{3,2,1,0:T(8,128)(2,1)S(1)} %get-tuple-element.75), channel_id=1, source_target_pairs={{0,1},{1,0},{2,3},{3,2},{4,5},{5,4},{6,7},{7,6},{8,9},{9,8},{10,11... | collective-permute-start | bytes 1769480 | tf_op jit(solution)/shard_map/ppermute | solution.py:20
  17.0 14.0 %collective-permute-start.2 = (bf16[128,2048]{1,0:T(8,128)(2,1)S(1)}, bf16[128,2048]{1,0:T(8,128)(2,1)S(1)}, u32[]{:S(2)}, u32[]{:S(2)}) collective-permute-start(bf16[128,2048]{1,0:T(8,128)(2,1)S(1)} %get-tuple-element.69), channel_id=1, source_target_pairs={{0,4},{4,0},{1,5},{5,1},{2,6},{6,2},{3,7},{7,3},{8,12},{12,8},{9,1... | collective-permute-start | bytes 1572872 | tf_op jit(solution)/shard_map/ppermute | solution.py:20
  18.4 14.3 %collective-permute-start.1 = (bf16[128,2048]{1,0:T(8,128)(2,1)S(1)}, bf16[128,2048]{1,0:T(8,128)(2,1)S(1)}, u32[]{:S(2)}, u32[]{:S(2)}) collective-permute-start(bf16[128,2048]{1,0:T(8,128)(2,1)S(1)} %collective-permute-done.refs_0_), channel_id=1, source_target_pairs={{0,8},{8,0},{16,24},{24,16},{1,9},{9,1},{17,25},{25,17},{2,10},{10... | collective-permute-start | bytes 1572872 | tf_op jit(solution)/shard_map/ppermute | solution.py:20
  23.3 1.6 %collective-permute-start.8 = (bf16[2,3,128,128]{3,2,1,0:T(8,128)(2,1)S(1)}, bf16[2,3,128,128]{3,2,1,0:T(8,128)(2,1)S(1)}, u32[]{:S(2)}, u32[]{:S(2)}) collective-permute-start(bf16[2,3,128,128]{3,2,1,0:T(8,128)(2,1)S(1)} %get-tuple-element.78), channel_id=1, source_target_pairs={{0,1},{1,0},{2,3},{3,2},{4,5},{5,4},{6,7},{7,6},{8,9},{9,8},{10,11... | collective-permute-start | bytes 589832 | tf_op jit(solution)/shard_map/ppermute | solution.py:20
  23.4 9.4 %collective-permute-start.7 = (bf16[1,3,384,128]{3,2,1,0:T(8,128)(2,1)S(1)}, bf16[1,3,384,128]{3,2,1,0:T(8,128)(2,1)S(1)}, u32[]{:S(2)}, u32[]{:S(2)}) collective-permute-start(bf16[1,3,384,128]{3,2,1,0:T(8,128)(2,1)S(1)} %add_convert_fusion.12), channel_id=1, source_target_pairs={{0,2},{1,3},{2,0},{3,1},{4,6},{5,7},{6,4},{7,5},{8,10},{9,11},{10,... | collective-permute-start | bytes 884744 | tf_op jit(solution)/shard_map/ppermute | solution.py:20
  24.9 23.0 %copy-start.5 = (f32[7,64]{1,0:T(8,128)S(1)}, f32[7,64]{1,0:T(8,128)}, u32[]{:S(2)}) copy-start(f32[7,64]{1,0:T(8,128)} %taps_ref.1) | copy-start | bytes 5380
  35.9 1.8 %collective-permute-start.9 = (bf16[2,3,256,128]{3,2,1,0:T(8,128)(2,1)S(1)}, bf16[2,3,256,128]{3,2,1,0:T(8,128)(2,1)S(1)}, u32[]{:S(2)}, u32[]{:S(2)}) collective-permute-start(bf16[2,3,256,128]{3,2,1,0:T(8,128)(2,1)S(1)} %get-tuple-element.81), channel_id=1, source_target_pairs={{0,1},{1,0},{2,3},{3,2},{4,5},{5,4},{6,7},{7,6},{8,9},{9,8},{10,11... | collective-permute-start | bytes 1179656 | tf_op jit(solution)/shard_map/ppermute | solution.py:20
  36.0 5.2 %collective-permute-start.11 = (bf16[1,3,128,128]{3,2,1,0:T(8,128)(2,1)S(1)}, bf16[1,3,128,128]{3,2,1,0:T(8,128)(2,1)S(1)}, u32[]{:S(2)}, u32[]{:S(2)}) collective-permute-start(bf16[1,3,128,128]{3,2,1,0:T(8,128)(2,1)S(1)} %add_convert_fusion.14), channel_id=1, source_target_pairs={{0,2},{1,3},{2,0},{3,1},{4,6},{5,7},{6,4},{7,5},{8,10},{9,11},{10,... | collective-permute-start | bytes 294920 | tf_op jit(solution)/shard_map/ppermute | solution.py:20
  41.2 6.7 %collective-permute-start.12 = (bf16[1,3,256,128]{3,2,1,0:T(8,128)(2,1)S(1)}, bf16[1,3,256,128]{3,2,1,0:T(8,128)(2,1)S(1)}, u32[]{:S(2)}, u32[]{:S(2)}) collective-permute-start(bf16[1,3,256,128]{3,2,1,0:T(8,128)(2,1)S(1)} %add_convert_fusion.13), channel_id=1, source_target_pairs={{0,2},{1,3},{2,0},{3,1},{4,6},{5,7},{6,4},{7,5},{8,10},{9,11},{10,... | collective-permute-start | bytes 589832 | tf_op jit(solution)/shard_map/ppermute | solution.py:20
  43.2 4.7 %collective-permute-start.10 = (bf16[384,128]{1,0:T(8,128)(2,1)S(1)}, bf16[384,128]{1,0:T(8,128)(2,1)S(1)}, u32[]{:S(2)}, u32[]{:S(2)}) collective-permute-start(bf16[384,128]{1,0:T(8,128)(2,1)S(1)} %get-tuple-element.84), channel_id=1, source_target_pairs={{0,4},{4,0},{1,5},{5,1},{2,6},{6,2},{3,7},{7,3},{8,12},{12,8},{9,1... | collective-permute-start | bytes 294920 | tf_op jit(solution)/shard_map/ppermute | solution.py:20
  49.5 6.5 %collective-permute-start.13 = (bf16[3,384,128]{2,1,0:T(8,128)(2,1)S(1)}, bf16[3,384,128]{2,1,0:T(8,128)(2,1)S(1)}, u32[]{:S(2)}, u32[]{:S(2)}) collective-permute-start(bf16[3,384,128]{2,1,0:T(8,128)(2,1)S(1)} %get-tuple-element.88.refs_0_), channel_id=1, source_target_pairs={{0,1},{1,0},{2,3},{3,2},{4,5},{5,4},{6,7},{7,6},{8,9},{9,8},{10,11... | collective-permute-start | bytes 884744 | tf_op jit(solution)/shard_map/ppermute | solution.py:20
  49.6 6.4 %collective-permute-start.16 = (bf16[3,384,128]{2,1,0:T(8,128)(2,1)S(1)}, bf16[3,384,128]{2,1,0:T(8,128)(2,1)S(1)}, u32[]{:S(2)}, u32[]{:S(2)}) collective-permute-start(bf16[3,384,128]{2,1,0:T(8,128)(2,1)S(1)} %get-tuple-element.87.refs_0_), channel_id=1, source_target_pairs={{0,1},{1,0},{2,3},{3,2},{4,5},{5,4},{6,7},{7,6},{8,9},{9,8},{10,11... | collective-permute-start | bytes 884744 | tf_op jit(solution)/shard_map/ppermute | solution.py:20
  50.1 9.0 %collective-permute-start.14 = (bf16[3,384,128]{2,1,0:T(8,128)(2,1)S(1)}, bf16[3,384,128]{2,1,0:T(8,128)(2,1)S(1)}, u32[]{:S(2)}, u32[]{:S(2)}) collective-permute-start(bf16[3,384,128]{2,1,0:T(8,128)(2,1)S(1)} %get-tuple-element.87.refs_0_), channel_id=1, source_target_pairs={{0,2},{1,3},{2,0},{3,1},{4,6},{5,7},{6,4},{7,5},{8,10},{9,11},{10,... | collective-permute-start | bytes 884744 | tf_op jit(solution)/shard_map/ppermute | solution.py:20
  51.3 4.7 %collective-permute-start.17 = (bf16[416,128]{1,0:T(8,128)(2,1)S(1)}, bf16[416,128]{1,0:T(8,128)(2,1)S(1)}, u32[]{:S(2)}, u32[]{:S(2)}) collective-permute-start(bf16[416,128]{1,0:T(8,128)(2,1)S(1)} %get-tuple-element.89), channel_id=1, source_target_pairs={{0,4},{4,0},{1,5},{5,1},{2,6},{6,2},{3,7},{7,3},{8,12},{12,8},{9,1... | collective-permute-start | bytes 319496 | tf_op jit(solution)/shard_map/ppermute | solution.py:20
  59.1 1.6 %collective-permute-start.18 = (bf16[3,384,128]{2,1,0:T(8,128)(2,1)S(1)}, bf16[3,384,128]{2,1,0:T(8,128)(2,1)S(1)}, u32[]{:S(2)}, u32[]{:S(2)}) collective-permute-start(bf16[3,384,128]{2,1,0:T(8,128)(2,1)S(1)} %collective-permute-done.14.refs_2_), channel_id=1, source_target_pairs={{0,1},{1,0},{2,3},{3,2},{4,5},{5,4},{6,7},{7,6},{8,9},{9,8},{10,11... | collective-permute-start | bytes 884744 | tf_op jit(solution)/shard_map/ppermute | solution.py:20
  59.1 9.4 %collective-permute-start.15 = (bf16[3,384,128]{2,1,0:T(8,128)(2,1)S(1)}, bf16[3,384,128]{2,1,0:T(8,128)(2,1)S(1)}, u32[]{:S(2)}, u32[]{:S(2)}) collective-permute-start(bf16[3,384,128]{2,1,0:T(8,128)(2,1)S(1)} %get-tuple-element.88.refs_0_), channel_id=1, source_target_pairs={{0,2},{1,3},{2,0},{3,1},{4,6},{5,7},{6,4},{7,5},{8,10},{9,11},{10,... | collective-permute-start | bytes 884744 | tf_op jit(solution)/shard_map/ppermute | solution.py:20
  62.2 12.0 %collective-permute-start.20 = (bf16[384,512]{1,0:T(8,128)(2,1)S(1)}, bf16[384,512]{1,0:T(8,128)(2,1)S(1)}, u32[]{:S(2)}, u32[]{:S(2)}) collective-permute-start(bf16[384,512]{1,0:T(8,128)(2,1)S(1)} %input_grad.4), channel_id=1, source_target_pairs={{0,4},{4,0},{1,5},{5,1},{2,6},{6,2},{3,7},{7,3},{8,12},{12,8},{9,1... | collective-permute-start | bytes 1179656 | tf_op jit(solution)/shard_map/ppermute | solution.py:20
  68.5 1.6 %collective-permute-start.19 = (bf16[3,384,128]{2,1,0:T(8,128)(2,1)S(1)}, bf16[3,384,128]{2,1,0:T(8,128)(2,1)S(1)}, u32[]{:S(2)}, u32[]{:S(2)}) collective-permute-start(bf16[3,384,128]{2,1,0:T(8,128)(2,1)S(1)} %collective-permute-done.15.refs_2_), channel_id=1, source_target_pairs={{0,1},{1,0},{2,3},{3,2},{4,5},{5,4},{6,7},{7,6},{8,9},{9,8},{10,11... | collective-permute-start | bytes 884744 | tf_op jit(solution)/shard_map/ppermute | solution.py:20
  68.5 14.1 %collective-permute-start.21 = (bf16[384,512]{1,0:T(8,128)(2,1)S(1)}, bf16[384,512]{1,0:T(8,128)(2,1)S(1)}, u32[]{:S(2)}, u32[]{:S(2)}) collective-permute-start(bf16[384,512]{1,0:T(8,128)(2,1)S(1)} %get-tuple-element.97), channel_id=1, source_target_pairs={{0,4},{4,0},{1,5},{5,1},{2,6},{6,2},{3,7},{7,3},{8,12},{12,8},{9,1... | collective-permute-start | bytes 1179656 | tf_op jit(solution)/shard_map/ppermute | solution.py:20
  74.3 9.6 %collective-permute-start.22 = (bf16[384,512]{1,0:T(8,128)(2,1)S(1)}, bf16[384,512]{1,0:T(8,128)(2,1)S(1)}, u32[]{:S(2)}, u32[]{:S(2)}) collective-permute-start(bf16[384,512]{1,0:T(8,128)(2,1)S(1)} %add_convert_fusion.11), channel_id=1, source_target_pairs={{0,8},{8,0},{16,24},{24,16},{1,9},{9,1},{17,25},{25,17},{2,10},{10... | collective-permute-start | bytes 1179656 | tf_op jit(solution)/shard_map/ppermute | solution.py:20
  75.7 15.4 %collective-permute-start.23 = (bf16[384,512]{1,0:T(8,128)(2,1)S(1)}, bf16[384,512]{1,0:T(8,128)(2,1)S(1)}, u32[]{:S(2)}, u32[]{:S(2)}) collective-permute-start(bf16[384,512]{1,0:T(8,128)(2,1)S(1)} %get-tuple-element.101), channel_id=1, source_target_pairs={{0,4},{4,0},{1,5},{5,1},{2,6},{6,2},{3,7},{7,3},{8,12},{12,8},{9,1... | collective-permute-start | bytes 1179656 | tf_op jit(solution)/shard_map/ppermute | solution.py:20
  84.0 11.4 %collective-permute-start.27 = (bf16[384,512]{1,0:T(8,128)(2,1)S(1)}, bf16[384,512]{1,0:T(8,128)(2,1)S(1)}, u32[]{:S(2)}, u32[]{:S(2)}) collective-permute-start(bf16[384,512]{1,0:T(8,128)(2,1)S(1)} %add_convert_fusion.9), channel_id=1, source_target_pairs={{0,0},{8,16},{16,8},{24,24},{1,1},{9,17},{17,9},{25,25},{2,2},{10,... | collective-permute-start | bytes 1179656 | tf_op jit(solution)/shard_map/ppermute | solution.py:602
  84.7 11.0 %collective-permute-start.28 = (bf16[384,512]{1,0:T(8,128)(2,1)S(1)}, bf16[384,512]{1,0:T(8,128)(2,1)S(1)}, u32[]{:S(2)}, u32[]{:S(2)}) collective-permute-start(bf16[384,512]{1,0:T(8,128)(2,1)S(1)} %add_convert_fusion.10), channel_id=1, source_target_pairs={{0,8},{8,0},{16,24},{24,16},{1,9},{9,1},{17,25},{25,17},{2,10},{10... | collective-permute-start | bytes 1179656 | tf_op jit(solution)/shard_map/ppermute | solution.py:20
  89.7 2.1 %collective-permute-start.24 = (bf16[2,128,128]{2,1,0:T(8,128)(2,1)S(1)}, bf16[2,128,128]{2,1,0:T(8,128)(2,1)S(1)}, u32[]{:S(2)}, u32[]{:S(2)}) collective-permute-start(bf16[2,128,128]{2,1,0:T(8,128)(2,1)S(1)} %get-tuple-element.104), channel_id=1, source_target_pairs={{0,1},{1,0},{2,3},{3,2},{4,5},{5,4},{6,7},{7,6},{8,9},{9,8},{10,11... | collective-permute-start | bytes 196616 | tf_op jit(solution)/shard_map/ppermute | solution.py:20
  89.8 4.8 %collective-permute-start.25 = (bf16[2,128,128]{2,1,0:T(8,128)(2,1)S(1)}, bf16[2,128,128]{2,1,0:T(8,128)(2,1)S(1)}, u32[]{:S(2)}, u32[]{:S(2)}) collective-permute-start(bf16[2,128,128]{2,1,0:T(8,128)(2,1)S(1)} %get-tuple-element.105), channel_id=1, source_target_pairs={{0,2},{1,3},{2,0},{3,1},{4,6},{5,7},{6,4},{7,5},{8,10},{9,11},{10,... | collective-permute-start | bytes 196616 | tf_op jit(solution)/shard_map/ppermute | solution.py:20
  91.1 4.3 %collective-permute-start.26 = (bf16[2,128,128]{2,1,0:T(8,128)(2,1)S(1)}, bf16[2,128,128]{2,1,0:T(8,128)(2,1)S(1)}, u32[]{:S(2)}, u32[]{:S(2)}) collective-permute-start(bf16[2,128,128]{2,1,0:T(8,128)(2,1)S(1)} %get-tuple-element.106), channel_id=1, source_target_pairs={{0,3},{1,2},{2,1},{3,0},{4,7},{5,6},{6,5},{7,4},{8,11},{9,10},{10,... | collective-permute-start | bytes 196616 | tf_op jit(solution)/shard_map/ppermute | solution.py:20
  91.7 8.4 %copy-start.3 = (bf16[384,2048]{1,0:T(8,128)(2,1)S(1)}, bf16[384,2048]{1,0:T(8,128)(2,1)}, u32[]{:S(2)}) copy-start(bf16[384,2048]{1,0:T(8,128)(2,1)} %refs_4_.1) | copy-start | bytes 4718596
  91.8 13.9 %collective-permute-start.29 = (bf16[384,512]{1,0:T(8,128)(2,1)S(1)}, bf16[384,512]{1,0:T(8,128)(2,1)S(1)}, u32[]{:S(2)}, u32[]{:S(2)}) collective-permute-start(bf16[384,512]{1,0:T(8,128)(2,1)S(1)} %get-tuple-element.115), channel_id=1, source_target_pairs={{0,4},{4,0},{1,5},{5,1},{2,6},{6,2},{3,7},{7,3},{8,12},{12,8},{9,1... | collective-permute-start | bytes 1179656 | tf_op jit(solution)/shard_map/ppermute | solution.py:20
  95.8 10.0 %collective-permute-start.30 = (bf16[384,512]{1,0:T(8,128)(2,1)S(1)}, bf16[384,512]{1,0:T(8,128)(2,1)S(1)}, u32[]{:S(2)}, u32[]{:S(2)}) collective-permute-start(bf16[384,512]{1,0:T(8,128)(2,1)S(1)} %add_convert_fusion.6), channel_id=1, source_target_pairs={{0,0},{8,16},{16,8},{24,24},{1,1},{9,17},{17,9},{25,25},{2,2},{10,... | collective-permute-start | bytes 1179656 | tf_op jit(solution)/shard_map/ppermute | solution.py:602
  96.7 12.2 %collective-permute-start.31 = (bf16[384,512]{1,0:T(8,128)(2,1)S(1)}, bf16[384,512]{1,0:T(8,128)(2,1)S(1)}, u32[]{:S(2)}, u32[]{:S(2)}) collective-permute-start(bf16[384,512]{1,0:T(8,128)(2,1)S(1)} %get-tuple-element.130), channel_id=1, source_target_pairs={{0,8},{8,0},{16,24},{24,16},{1,9},{9,1},{17,25},{25,17},{2,10},{10... | collective-permute-start | bytes 1179656 | tf_op jit(solution)/shard_map/ppermute | solution.py:20
  109.0 9.7 %collective-permute-start.32 = (bf16[384,512]{1,0:T(8,128)(2,1)S(1)}, bf16[384,512]{1,0:T(8,128)(2,1)S(1)}, u32[]{:S(2)}, u32[]{:S(2)}) collective-permute-start(bf16[384,512]{1,0:T(8,128)(2,1)S(1)} %add_convert_fusion.3), channel_id=1, source_target_pairs={{0,0},{8,16},{16,8},{24,24},{1,1},{9,17},{17,9},{25,25},{2,2},{10,... | collective-permute-start | bytes 1179656 | tf_op jit(solution)/shard_map/ppermute | solution.py:602
  109.7 11.1 %collective-permute-start.33 = (bf16[384,512]{1,0:T(8,128)(2,1)S(1)}, bf16[384,512]{1,0:T(8,128)(2,1)S(1)}, u32[]{:S(2)}, u32[]{:S(2)}) collective-permute-start(bf16[384,512]{1,0:T(8,128)(2,1)S(1)} %get-tuple-element.128), channel_id=1, source_target_pairs={{0,8},{8,0},{16,24},{24,16},{1,9},{9,1},{17,25},{25,17},{2,10},{10... | collective-permute-start | bytes 1179656 | tf_op jit(solution)/shard_map/ppermute | solution.py:20
  120.9 5.3 %collective-permute-start.34 = (bf16[384,512]{1,0:T(8,128)(2,1)S(1)}, bf16[384,512]{1,0:T(8,128)(2,1)S(1)}, u32[]{:S(2)}, u32[]{:S(2)}) collective-permute-start(bf16[384,512]{1,0:T(8,128)(2,1)S(1)} %add_convert_fusion.1), channel_id=1, source_target_pairs={{0,0},{8,16},{16,8},{24,24},{1,1},{9,17},{17,9},{25,25},{2,2},{10,... | collective-permute-start | bytes 1179656 | tf_op jit(solution)/shard_map/ppermute | solution.py:602
  121.7 13.0 %collective-permute-start.35 = (bf16[384,512]{1,0:T(8,128)(2,1)S(1)}, bf16[384,512]{1,0:T(8,128)(2,1)S(1)}, u32[]{:S(2)}, u32[]{:S(2)}) collective-permute-start(bf16[384,512]{1,0:T(8,128)(2,1)S(1)} %add_convert_fusion.2), channel_id=1, source_target_pairs={{0,8},{8,0},{16,24},{24,16},{1,9},{9,1},{17,25},{25,17},{2,10},{10... | collective-permute-start | bytes 1179656 | tf_op jit(solution)/shard_map/ppermute | solution.py:20
  126.3 14.7 %collective-permute-start.36 = (bf16[384,512]{1,0:T(8,128)(2,1)S(1)}, bf16[384,512]{1,0:T(8,128)(2,1)S(1)}, u32[]{:S(2)}, u32[]{:S(2)}) collective-permute-start(bf16[384,512]{1,0:T(8,128)(2,1)S(1)} %add_convert_fusion), channel_id=1, source_target_pairs={{0,8},{8,0},{16,24},{24,16},{1,9},{9,1},{17,25},{25,17},{2,10},{10... | collective-permute-start | bytes 1179656 | tf_op jit(solution)/shard_map/ppermute | solution.py:20

commit v15 on v14

--- a/solution.py
+++ b/solution.py
@@ -587,12 +587,12 @@
             if slot < chunks:
                 done[slot] = lax.psum(inward[slot], "row")
         else:
+            if 0 <= slot - 1 < chunks:
+                across[slot - 1] = added(after(inward[slot - 1], *marks), pair)
+                marks = [across[slot - 1]]
             if 0 <= slot - 2 < chunks:
                 summed[slot - 2] = added(after(across[slot - 2], *marks), cross)
                 marks = [summed[slot - 2]]
-            if 0 <= slot - 1 < chunks:
-                across[slot - 1] = added(after(inward[slot - 1], *marks), pair)
-                marks = [across[slot - 1]]
             if 0 <= slot - 3 < chunks:
                 done[slot - 3] = jnp.where(outer, pair, summed[slot - 3])
             if slot < chunks + 2:

time: 143 us -> 141 us (0.986)
  starting transfers between devices: 49.1 us -> 45.7 us
    ppermute x33, starting transfers between devices: 46.2 us -> 42.8 us  [swap(): return lax.ppermute(value, axis, [(i, i ^ flip) for i in range(count)])]
  transfers between devices with their start and end apart: 37 -> 37, of which waited for: 20 -> 18; matrix products, arithmetic and copies ran while one was open for 1% -> 1% of each run, Pallas kernels for 21% -> 22%
where the time goes in v15:
time: 141 us; the launch traced here: 140 us
  waiting for transfers between devices  49.3 us (35%)
  starting transfers between devices  45.7 us (32%)
  Pallas kernels  35.2 us (25%)
  local copies, waits for them, and re-layouts  6.22 us (4%)
  other arithmetic  3.05 us (2%)
    ppermute x33, waiting for transfers between devices, swap(): return lax.ppermute(value, axis, [(i, i ^ flip) for i in range(count)])  49.3 us
    ppermute x33, starting transfers between devices, swap(): return lax.ppermute(value, axis, [(i, i ^ flip) for i in range(count)])  42.8 us
    pallas_call x2, Pallas kernels, weight_grad(): pl.pallas_call(functools.partial(weight_grad_kernel, chained=chained, gro...  11.2 us
    pallas_call x3, Pallas kernels, project(): pl.pallas_call(functools.partial(project_kernel, pieces=len(xs), mode=mod...  10.3 us
    pallas_call x4, Pallas kernels, input_grad(): pl.pallas_call(functools.partial(input_grad_kernel if single else input_g...  7.49 us
    unnamed x12, local copies, waits for them, and re-layouts  5.14 us
    ppermute x4, starting transfers between devices, on_device(): lax.ppermute(across[slot - 1], 'row', [(0, 0), (1, 2), (2, 1), (3, 3)])  2.9 us
  transfers between devices with their start and end apart: 37, of which 18 were waited for; matrix products, arithmetic and copies ran while one was open for 1% of the time, Pallas kernels for 22%

profile of v15, /device:TPU:0, one launch (start us, length us, event | category | flops | bytes accessed | tf_op | source)
XLA Modules:
  0.0 140.5 jit_solution(4922692372327119696)
XLA Ops:
  0.6 1.1 constant_dynamic-slice_fusion
  1.7 3.0 %collective-permute-start = (bf16[128,2048]{1,0:T(8,128)(2,1)S(1)}, bf16[128,2048]{1,0:T(8,128)(2,1)S(1)}, u32[]{:S(2)}, u32[]{:S(2)}) collective-permute-start(bf16[128,2048]{1,0:T(8,128)(2,1)S(1)} %constant_dynamic-slice_fusion), channel_id=1, source_target_pairs={{0,4},{4,0},{1,5},{5,1},{2,6},{6,2},{3,7},{7,3},{8,12},{12,8},{9,1... | collective-permute-start | bytes 1572872 | tf_op jit(solution)/shard_map/ppermute | solution.py:20
  4.9 0.9 copy-done.4
  5.8 0.6 split.2
  6.5 1.6 %collective-permute-start.4 = (bf16[2,96,128]{2,1,0:T(8,128)(2,1)S(1)}, bf16[2,96,128]{2,1,0:T(8,128)(2,1)S(1)}, u32[]{:S(2)}, u32[]{:S(2)}) collective-permute-start(bf16[2,96,128]{2,1,0:T(8,128)(2,1)S(1)} %get-tuple-element.73), channel_id=1, source_target_pairs={{0,2},{1,3},{2,0},{3,1},{4,6},{5,7},{6,4},{7,5},{8,10},{9,11},{10,... | collective-permute-start | bytes 147464 | tf_op jit(solution)/shard_map/ppermute | solution.py:20
  8.3 2.8 %copy-done = bf16[512,3,2048]{2,0,1:T(8,128)(2,1)S(1)} copy-done((bf16[512,3,2048]{2,0,1:T(8,128)(2,1)S(1)}, bf16[512,3,2048]{2,0,1:T(8,128)(2,1)}, u32[]{:S(2)}) %copy-start) | copy-done | bytes 6291480
  11.1 1.4 %copy-done.2 = bf16[384,2048]{1,0:T(8,128)(2,1)S(1)} copy-done((bf16[384,2048]{1,0:T(8,128)(2,1)S(1)}, bf16[384,2048]{1,0:T(8,128)(2,1)}, u32[]{:S(2)}) %copy-start.2) | copy-done | bytes 1572888
  12.5 4.1 %project.3 = (bf16[2,3,384,128]{3,2,1,0:T(8,128)(2,1)S(1)}, bf16[2,3,384,128]{3,2,1,0:T(8,128)(2,1)S(1)}, bf16[128,2048]{1,0:T(8,128)(2,1)S(1)}) custom-call(s32[4]{0:T(128)S(1)} %pad_add_fusion.place, bf16[384,2048]{1,0:T(8,128)(2,1)S(1)} %copy-done.2, bf16[3,512,2048]{2,1,0:T(8,128)(2,1)S(1)} %bitcast.6), custom_call_target="tpu_custom_call" | custom-call | flops 1 | bytes 1 | tf_op jit(solution)/shard_map/project/pallas_call | solution.py:97
  17.0 1.4 collective-permute-start.2
  18.4 1.6 %collective-permute-start.1 = (bf16[128,2048]{1,0:T(8,128)(2,1)S(1)}, bf16[128,2048]{1,0:T(8,128)(2,1)S(1)}, u32[]{:S(2)}, u32[]{:S(2)}) collective-permute-start(bf16[128,2048]{1,0:T(8,128)(2,1)S(1)} %collective-permute-done.refs_0_), channel_id=1, source_target_pairs={{0,8},{8,0},{16,24},{24,16},{1,9},{9,1},{17,25},{25,17},{2,10},{10... | collective-permute-start | bytes 1572872 | tf_op jit(solution)/shard_map/ppermute | solution.py:20
  20.1 3.1 %project.4 = (bf16[2,3,128,128]{3,2,1,0:T(8,128)(2,1)S(1)}, bf16[2,3,128,128]{3,2,1,0:T(8,128)(2,1)S(1)}) custom-call(s32[4]{0:T(128)S(1)} %pad_add_fusion.place, bf16[128,2048]{1,0:T(8,128)(2,1)S(1)} %collective-permute-done.refs_0_, bf16[3,512,2048]{2,1,0:T(8,128)(2,1)S(1)} %bitcast.7), custom_call_target="tpu_custom_call" | custom-call | flops 1 | bytes 1 | tf_op jit(solution)/shard_map/project/pallas_call | solution.py:97
  23.4 1.6 %collective-permute-start.7 = (bf16[1,3,384,128]{3,2,1,0:T(8,128)(2,1)S(1)}, bf16[1,3,384,128]{3,2,1,0:T(8,128)(2,1)S(1)}, u32[]{:S(2)}, u32[]{:S(2)}) collective-permute-start(bf16[1,3,384,128]{3,2,1,0:T(8,128)(2,1)S(1)} %add_convert_fusion.12), channel_id=1, source_target_pairs={{0,2},{1,3},{2,0},{3,1},{4,6},{5,7},{6,4},{7,5},{8,10},{9,11},{10,... | collective-permute-start | bytes 884744 | tf_op jit(solution)/shard_map/ppermute | solution.py:20
  25.0 6.1 %collective-permute-done.2.refs_2_ = bf16[128,2048]{1,0:T(8,128)(2,1)S(1)} collective-permute-done((bf16[128,2048]{1,0:T(8,128)(2,1)S(1)}, bf16[128,2048]{1,0:T(8,128)(2,1)S(1)}, u32[]{:S(2)}, u32[]{:S(2)}) %collective-permute-start.2) | collective-permute-done | bytes 524320 | tf_op jit(solution)/shard_map/ppermute | solution.py:20
  31.0 1.7 %collective-permute-done.7.refs_4_ = bf16[1,3,384,128]{3,2,1,0:T(8,128)(2,1)S(1)} collective-permute-done((bf16[1,3,384,128]{3,2,1,0:T(8,128)(2,1)S(1)}, bf16[1,3,384,128]{3,2,1,0:T(8,128)(2,1)S(1)}, u32[]{:S(2)}, u32[]{:S(2)}) %collective-permute-start.7) | collective-permute-done | bytes 294944 | tf_op jit(solution)/shard_map/ppermute | solution.py:20
  32.8 3.1 %project.5 = (bf16[2,3,256,128]{3,2,1,0:T(8,128)(2,1)S(1)}, bf16[2,3,256,128]{3,2,1,0:T(8,128)(2,1)S(1)}, bf16[384,2048]{1,0:T(8,128)(2,1)S(1)}) custom-call(s32[4]{0:T(128)S(1)} %pad_add_fusion.place, bf16[128,2048]{1,0:T(8,128)(2,1)S(1)} %collective-permute-done.refs_0_, bf16[128,2048]{1,0:T(8,128)(2,1)S(1)} %collective-permute-done.1.refs_1_, ...), custom_call_target="tpu_custom_call" | custom-call | flops 1 | bytes 1 | tf_op jit(solution)/shard_map/project/pallas_call | solution.py:97
  36.0 1.6 %collective-permute-start.11 = (bf16[1,3,128,128]{3,2,1,0:T(8,128)(2,1)S(1)}, bf16[1,3,128,128]{3,2,1,0:T(8,128)(2,1)S(1)}, u32[]{:S(2)}, u32[]{:S(2)}) collective-permute-start(bf16[1,3,128,128]{3,2,1,0:T(8,128)(2,1)S(1)} %add_convert_fusion.14), channel_id=1, source_target_pairs={{0,2},{1,3},{2,0},{3,1},{4,6},{5,7},{6,4},{7,5},{8,10},{9,11},{10,... | collective-permute-start | bytes 294920 | tf_op jit(solution)/shard_map/ppermute | solution.py:20
  37.7 3.4 %collective-permute-done.11.refs_7_ = bf16[1,3,128,128]{3,2,1,0:T(8,128)(2,1)S(1)} collective-permute-done((bf16[1,3,128,128]{3,2,1,0:T(8,128)(2,1)S(1)}, bf16[1,3,128,128]{3,2,1,0:T(8,128)(2,1)S(1)}, u32[]{:S(2)}, u32[]{:S(2)}) %collective-permute-start.11) | collective-permute-done | bytes 98336 | tf_op jit(solution)/shard_map/ppermute | solution.py:20
  41.2 1.5 %collective-permute-start.12 = (bf16[1,3,256,128]{3,2,1,0:T(8,128)(2,1)S(1)}, bf16[1,3,256,128]{3,2,1,0:T(8,128)(2,1)S(1)}, u32[]{:S(2)}, u32[]{:S(2)}) collective-permute-start(bf16[1,3,256,128]{3,2,1,0:T(8,128)(2,1)S(1)} %add_convert_fusion.13), channel_id=1, source_target_pairs={{0,2},{1,3},{2,0},{3,1},{4,6},{5,7},{6,4},{7,5},{8,10},{9,11},{10,... | collective-permute-start | bytes 589832 | tf_op jit(solution)/shard_map/ppermute | solution.py:20
  42.7 0.6 merge.1
  43.2 0.7 collective-permute-start.10
  44.0 4.0 %collective-permute-done.10.refs_1_ = bf16[384,128]{1,0:T(8,128)(2,1)S(1)} collective-permute-done((bf16[384,128]{1,0:T(8,128)(2,1)S(1)}, bf16[384,128]{1,0:T(8,128)(2,1)S(1)}, u32[]{:S(2)}, u32[]{:S(2)}) %collective-permute-start.10) | collective-permute-done | bytes 98336 | tf_op jit(solution)/shard_map/ppermute | solution.py:20
  47.9 1.5 %middle.1 = (bf16[3,384,128]{2,1,0:T(8,128)(2,1)S(1)}, bf16[3,384,128]{2,1,0:T(8,128)(2,1)S(1)}, bf16[416,128]{1,0:T(8,128)(2,1)S(1)}, bf16[416,128]{1,0:T(8,128)(2,1)S(1)}) custom-call(s32[4]{0:T(128)S(1)} %pad_add_fusion.place, f32[7,64]{1,0:T(8,128)S(1)} %copy-done.5, bf16[384,128]{1,0:T(8,128)(2,1)S(1)} %get-tuple-element.83.refs_0_, ...), custom_call_target="tpu_custom_call" | custom-call | flops 1 | bytes 1 | tf_op jit(solution)/shard_map/middle/pallas_call | solution.py:326
  49.6 0.5 collective-permute-start.16
  50.1 1.2 collective-permute-start.14
  51.3 0.7 collective-permute-start.17
  51.9 4.1 %collective-permute-done.17.refs_1_ = bf16[416,128]{1,0:T(8,128)(2,1)S(1)} collective-permute-done((bf16[416,128]{1,0:T(8,128)(2,1)S(1)}, bf16[416,128]{1,0:T(8,128)(2,1)S(1)}, u32[]{:S(2)}, u32[]{:S(2)}) %collective-permute-start.17) | collective-permute-done | bytes 106528 | tf_op jit(solution)/shard_map/ppermute | solution.py:20
  56.0 3.1 %collective-permute-done.14.refs_2_ = bf16[3,384,128]{2,1,0:T(8,128)(2,1)S(1)} collective-permute-done((bf16[3,384,128]{2,1,0:T(8,128)(2,1)S(1)}, bf16[3,384,128]{2,1,0:T(8,128)(2,1)S(1)}, u32[]{:S(2)}, u32[]{:S(2)}) %collective-permute-start.14) | collective-permute-done | bytes 294944 | tf_op jit(solution)/shard_map/ppermute | solution.py:20
  59.1 1.2 collective-permute-start.15
  60.3 0.4 collective-permute-done.18.refs_3_
  60.6 0.7 assemble.2.grad_ref.refs_1_.refs_3_
  61.4 0.8 input_grad.4
  62.2 0.7 collective-permute-start.20
  62.9 3.0 %input_grad.5 = (bf16[384,512]{1,0:T(8,128)(2,1)S(1)}, bf16[384,512]{1,0:T(8,128)(2,1)S(1)}, bf16[384,512]{1,0:T(8,128)(2,1)S(1)}) custom-call(bf16[384,1536]{1,0:T(8,128)(2,1)S(1)} %assemble.2.grad_ref.refs_1_.refs_3_, bf16[3,512,2048]{2,1,0:T(8,128)(2,1)S(1)} %bitcast.10), custom_call_target="tpu_custom_call" | custom-call | flops 1 | bytes 1 | tf_op jit(solution)/shard_map/input_grad/pallas_call | solution.py:414
  65.9 2.6 %collective-permute-done.15.refs_2_ = bf16[3,384,128]{2,1,0:T(8,128)(2,1)S(1)} collective-permute-done((bf16[3,384,128]{2,1,0:T(8,128)(2,1)S(1)}, bf16[3,384,128]{2,1,0:T(8,128)(2,1)S(1)}, u32[]{:S(2)}, u32[]{:S(2)}) %collective-permute-start.15) | collective-permute-done | bytes 294944 | tf_op jit(solution)/shard_map/ppermute | solution.py:20
  68.5 0.7 collective-permute-start.21
  69.1 0.9 collective-permute-done.19.refs_3_
  70.1 0.7 assemble.3.grad_ref.refs_0_.refs_2_
  70.8 0.8 input_grad.6
  71.6 2.6 %collective-permute-done.20 = bf16[384,512]{1,0:T(8,128)(2,1)S(1)} collective-permute-done((bf16[384,512]{1,0:T(8,128)(2,1)S(1)}, bf16[384,512]{1,0:T(8,128)(2,1)S(1)}, u32[]{:S(2)}, u32[]{:S(2)}) %collective-permute-start.20) | collective-permute-done | bytes 393248 | tf_op jit(solution)/shard_map/ppermute | solution.py:20
  74.3 1.4 collective-permute-start.22
  75.7 0.7 collective-permute-start.23
  76.3 3.0 %input_grad.7 = (bf16[384,512]{1,0:T(8,128)(2,1)S(1)}, bf16[384,512]{1,0:T(8,128)(2,1)S(1)}, bf16[384,512]{1,0:T(8,128)(2,1)S(1)}) custom-call(bf16[384,1536]{1,0:T(8,128)(2,1)S(1)} %assemble.3.grad_ref.refs_0_.refs_2_, bf16[3,512,2048]{2,1,0:T(8,128)(2,1)S(1)} %bitcast.12), custom_call_target="tpu_custom_call" | custom-call | flops 1 | bytes 1 | tf_op jit(solution)/shard_map/input_grad/pallas_call | solution.py:414
  79.3 3.3 %collective-permute-done.21 = bf16[384,512]{1,0:T(8,128)(2,1)S(1)} collective-permute-done((bf16[384,512]{1,0:T(8,128)(2,1)S(1)}, bf16[384,512]{1,0:T(8,128)(2,1)S(1)}, u32[]{:S(2)}, u32[]{:S(2)}) %collective-permute-start.21) | collective-permute-done | bytes 393248 | tf_op jit(solution)/shard_map/ppermute | solution.py:20
  82.7 1.4 collective-permute-start.27
  84.2 0.7 collective-permute-start.28
  84.9 0.6 split.3
  85.5 1.3 collective-permute-start.25
  86.8 3.4 %collective-permute-done.23 = bf16[384,512]{1,0:T(8,128)(2,1)S(1)} collective-permute-done((bf16[384,512]{1,0:T(8,128)(2,1)S(1)}, bf16[384,512]{1,0:T(8,128)(2,1)S(1)}, u32[]{:S(2)}, u32[]{:S(2)}) %collective-permute-start.23) | collective-permute-done | bytes 393248 | tf_op jit(solution)/shard_map/ppermute | solution.py:20
  90.5 0.7 collective-permute-start.29
  91.2 3.2 %collective-permute-done.26.refs_3_ = bf16[2,128,128]{2,1,0:T(8,128)(2,1)S(1)} collective-permute-done((bf16[2,128,128]{2,1,0:T(8,128)(2,1)S(1)}, bf16[2,128,128]{2,1,0:T(8,128)(2,1)S(1)}, u32[]{:S(2)}, u32[]{:S(2)}) %collective-permute-start.26) | collective-permute-done | bytes 65568 | tf_op jit(solution)/shard_map/ppermute | solution.py:20
  94.7 2.3 %collective-permute-start.30 = (bf16[384,512]{1,0:T(8,128)(2,1)S(1)}, bf16[384,512]{1,0:T(8,128)(2,1)S(1)}, u32[]{:S(2)}, u32[]{:S(2)}) collective-permute-start(bf16[384,512]{1,0:T(8,128)(2,1)S(1)} %get-tuple-element.130), channel_id=1, source_target_pairs={{0,8},{8,0},{16,24},{24,16},{1,9},{9,1},{17,25},{25,17},{2,10},{10... | collective-permute-start | bytes 1179656 | tf_op jit(solution)/shard_map/ppermute | solution.py:20
  97.0 0.9 collective-permute-start.31
  97.8 5.6 %weight_grad.2 = (f32[3,512,2048]{2,1,0:T(8,128)}, f32[8,128]{1,0:T(8,128)S(1)}) custom-call(bf16[384,1536]{1,0:T(8,128)(2,1)S(1)} %assemble.3.grad_ref.refs_0_.refs_2_, bf16[384,1536]{1,0:T(8,128)(2,1)S(1)} %assemble.2.grad_ref.refs_1_.refs_3_, bf16[384,2048]{1,0:T(8,128)(2,1)S(1)} %copy-done.3, bf16[384,2048]{1,0:T(8,128)(2,1)S(1)} %get-tuple-element.110.refs_3_.refs_5_), custom_call_target="tpu_custom_call" | custom-call | flops 1 | bytes 1 | tf_op jit(solution)/shard_map/weight_grad/pallas_call | solution.py:471
  103.6 2.1 %collective-permute-done.30 = bf16[384,512]{1,0:T(8,128)(2,1)S(1)} collective-permute-done((bf16[384,512]{1,0:T(8,128)(2,1)S(1)}, bf16[384,512]{1,0:T(8,128)(2,1)S(1)}, u32[]{:S(2)}, u32[]{:S(2)}) %collective-permute-start.30) | collective-permute-done | bytes 393248 | tf_op jit(solution)/shard_map/ppermute | solution.py:20
  106.0 4.2 %collective-permute-start.32 = (bf16[384,512]{1,0:T(8,128)(2,1)S(1)}, bf16[384,512]{1,0:T(8,128)(2,1)S(1)}, u32[]{:S(2)}, u32[]{:S(2)}) collective-permute-start(bf16[384,512]{1,0:T(8,128)(2,1)S(1)} %get-tuple-element.128), channel_id=1, source_target_pairs={{0,8},{8,0},{16,24},{24,16},{1,9},{9,1},{17,25},{25,17},{2,10},{10... | collective-permute-start | bytes 1179656 | tf_op jit(solution)/shard_map/ppermute | solution.py:20
  110.2 0.7 collective-permute-start.33
  110.9 5.6 %weight_grad.3 = (f32[3,512,2048]{2,1,0:T(8,128)}, f32[8,128]{1,0:T(8,128)S(1)}) custom-call(f32[3,512,2048]{2,1,0:T(8,128)} %get-tuple-element.111.refs_0_, f32[8,128]{1,0:T(8,128)S(1)} %get-tuple-element.112.refs_1_, bf16[384,1536]{1,0:T(8,128)(2,1)S(1)} %assemble.3.grad_ref.refs_0_.refs_2_, ...), custom_call_target="tpu_custom_call", output_to_operand_aliasing={{0}: (0, {})} | custom-call | flops 1 | bytes 1 | tf_op jit(solution)/shard_map/weight_grad/pallas_call | solution.py:471
  116.5 2.0 %collective-permute-done.32 = bf16[384,512]{1,0:T(8,128)(2,1)S(1)} collective-permute-done((bf16[384,512]{1,0:T(8,128)(2,1)S(1)}, bf16[384,512]{1,0:T(8,128)(2,1)S(1)}, u32[]{:S(2)}, u32[]{:S(2)}) %collective-permute-start.32) | collective-permute-done | bytes 393248 | tf_op jit(solution)/shard_map/ppermute | solution.py:20
  118.6 0.7 collective-permute-start.34
  119.5 4.4 %collective-permute-start.35 = (bf16[384,512]{1,0:T(8,128)(2,1)S(1)}, bf16[384,512]{1,0:T(8,128)(2,1)S(1)}, u32[]{:S(2)}, u32[]{:S(2)}) collective-permute-start(bf16[384,512]{1,0:T(8,128)(2,1)S(1)} %add_convert_fusion.1), channel_id=1, source_target_pairs={{0,8},{8,0},{16,24},{24,16},{1,9},{9,1},{17,25},{25,17},{2,10},{10... | collective-permute-start | bytes 1179656 | tf_op jit(solution)/shard_map/ppermute | solution.py:20
  124.0 7.5 %collective-permute-start.36 = (bf16[384,512]{1,0:T(8,128)(2,1)S(1)}, bf16[384,512]{1,0:T(8,128)(2,1)S(1)}, u32[]{:S(2)}, u32[]{:S(2)}) collective-permute-start(bf16[384,512]{1,0:T(8,128)(2,1)S(1)} %add_convert_fusion), channel_id=1, source_target_pairs={{0,8},{8,0},{16,24},{24,16},{1,9},{9,1},{17,25},{25,17},{2,10},{10... | collective-permute-start | bytes 1179656 | tf_op jit(solution)/shard_map/ppermute | solution.py:20
  131.6 1.4 join.1
  133.0 6.1 %collective-permute-done.36 = bf16[384,512]{1,0:T(8,128)(2,1)S(1)} collective-permute-done((bf16[384,512]{1,0:T(8,128)(2,1)S(1)}, bf16[384,512]{1,0:T(8,128)(2,1)S(1)}, u32[]{:S(2)}, u32[]{:S(2)}) %collective-permute-start.36) | collective-permute-done | bytes 393248 | tf_op jit(solution)/shard_map/ppermute | solution.py:20
  139.2 1.3 pad_maximum_fusion
  (60 shorter events, 3.2 us)
Async XLA Ops:
  1.7 15.0 %collective-permute-start = (bf16[128,2048]{1,0:T(8,128)(2,1)S(1)}, bf16[128,2048]{1,0:T(8,128)(2,1)S(1)}, u32[]{:S(2)}, u32[]{:S(2)}) collective-permute-start(bf16[128,2048]{1,0:T(8,128)(2,1)S(1)} %constant_dynamic-slice_fusion), channel_id=1, source_target_pairs={{0,4},{4,0},{1,5},{5,1},{2,6},{6,2},{3,7},{7,3},{8,12},{12,8},{9,1... | collective-permute-start | bytes 1572872 | tf_op jit(solution)/shard_map/ppermute | solution.py:20
  4.8 0.9 copy-start.4
  6.4 10.2 %collective-permute-start.3 = (bf16[2,96,128]{2,1,0:T(8,128)(2,1)S(1)}, bf16[2,96,128]{2,1,0:T(8,128)(2,1)S(1)}, u32[]{:S(2)}, u32[]{:S(2)}) collective-permute-start(bf16[2,96,128]{2,1,0:T(8,128)(2,1)S(1)} %get-tuple-element.72), channel_id=1, source_target_pairs={{0,1},{1,0},{2,3},{3,2},{4,5},{5,4},{6,7},{7,6},{8,9},{9,8},{10,11... | collective-permute-start | bytes 147464 | tf_op jit(solution)/shard_map/ppermute | solution.py:20
  6.5 10.1 %collective-permute-start.4 = (bf16[2,96,128]{2,1,0:T(8,128)(2,1)S(1)}, bf16[2,96,128]{2,1,0:T(8,128)(2,1)S(1)}, u32[]{:S(2)}, u32[]{:S(2)}) collective-permute-start(bf16[2,96,128]{2,1,0:T(8,128)(2,1)S(1)} %get-tuple-element.73), channel_id=1, source_target_pairs={{0,2},{1,3},{2,0},{3,1},{4,6},{5,7},{6,4},{7,5},{8,10},{9,11},{10,... | collective-permute-start | bytes 147464 | tf_op jit(solution)/shard_map/ppermute | solution.py:20
  8.0 8.6 %collective-permute-start.5 = (bf16[2,96,128]{2,1,0:T(8,128)(2,1)S(1)}, bf16[2,96,128]{2,1,0:T(8,128)(2,1)S(1)}, u32[]{:S(2)}, u32[]{:S(2)}) collective-permute-start(bf16[2,96,128]{2,1,0:T(8,128)(2,1)S(1)} %get-tuple-element.74), channel_id=1, source_target_pairs={{0,3},{1,2},{2,1},{3,0},{4,7},{5,6},{6,5},{7,4},{8,11},{9,10},{10,... | collective-permute-start | bytes 147464 | tf_op jit(solution)/shard_map/ppermute | solution.py:20
  8.3 2.8 %copy-start = (bf16[512,3,2048]{2,0,1:T(8,128)(2,1)S(1)}, bf16[512,3,2048]{2,0,1:T(8,128)(2,1)}, u32[]{:S(2)}) copy-start(bf16[512,3,2048]{2,0,1:T(8,128)(2,1)} %param.5) | copy-start | bytes 18874372
  11.1 1.4 %copy-start.2 = (bf16[384,2048]{1,0:T(8,128)(2,1)S(1)}, bf16[384,2048]{1,0:T(8,128)(2,1)}, u32[]{:S(2)}) copy-start(bf16[384,2048]{1,0:T(8,128)(2,1)} %refs_4_.1) | copy-start | bytes 4718596
  12.5 7.6 %copy-start.1 = (bf16[512,3,2048]{2,0,1:T(8,128)(2,1)S(1)}, bf16[512,3,2048]{2,0,1:T(8,128)(2,1)}, u32[]{:S(2)}) copy-start(bf16[512,3,2048]{2,0,1:T(8,128)(2,1)} %param.5) | copy-start | bytes 18874372
  16.7 3.3 %collective-permute-start.6 = (bf16[2,3,384,128]{3,2,1,0:T(8,128)(2,1)S(1)}, bf16[2,3,384,128]{3,2,1,0:T(8,128)(2,1)S(1)}, u32[]{:S(2)}, u32[]{:S(2)}) collective-permute-start(bf16[2,3,384,128]{3,2,1,0:T(8,128)(2,1)S(1)} %get-tuple-element.75), channel_id=1, source_target_pairs={{0,1},{1,0},{2,3},{3,2},{4,5},{5,4},{6,7},{7,6},{8,9},{9,8},{10,11... | collective-permute-start | bytes 1769480 | tf_op jit(solution)/shard_map/ppermute | solution.py:20
  17.0 14.0 %collective-permute-start.2 = (bf16[128,2048]{1,0:T(8,128)(2,1)S(1)}, bf16[128,2048]{1,0:T(8,128)(2,1)S(1)}, u32[]{:S(2)}, u32[]{:S(2)}) collective-permute-start(bf16[128,2048]{1,0:T(8,128)(2,1)S(1)} %get-tuple-element.69), channel_id=1, source_target_pairs={{0,4},{4,0},{1,5},{5,1},{2,6},{6,2},{3,7},{7,3},{8,12},{12,8},{9,1... | collective-permute-start | bytes 1572872 | tf_op jit(solution)/shard_map/ppermute | solution.py:20
  18.4 14.3 %collective-permute-start.1 = (bf16[128,2048]{1,0:T(8,128)(2,1)S(1)}, bf16[128,2048]{1,0:T(8,128)(2,1)S(1)}, u32[]{:S(2)}, u32[]{:S(2)}) collective-permute-start(bf16[128,2048]{1,0:T(8,128)(2,1)S(1)} %collective-permute-done.refs_0_), channel_id=1, source_target_pairs={{0,8},{8,0},{16,24},{24,16},{1,9},{9,1},{17,25},{25,17},{2,10},{10... | collective-permute-start | bytes 1572872 | tf_op jit(solution)/shard_map/ppermute | solution.py:20
  23.3 1.6 %collective-permute-start.8 = (bf16[2,3,128,128]{3,2,1,0:T(8,128)(2,1)S(1)}, bf16[2,3,128,128]{3,2,1,0:T(8,128)(2,1)S(1)}, u32[]{:S(2)}, u32[]{:S(2)}) collective-permute-start(bf16[2,3,128,128]{3,2,1,0:T(8,128)(2,1)S(1)} %get-tuple-element.78), channel_id=1, source_target_pairs={{0,1},{1,0},{2,3},{3,2},{4,5},{5,4},{6,7},{7,6},{8,9},{9,8},{10,11... | collective-permute-start | bytes 589832 | tf_op jit(solution)/shard_map/ppermute | solution.py:20
  23.4 9.4 %collective-permute-start.7 = (bf16[1,3,384,128]{3,2,1,0:T(8,128)(2,1)S(1)}, bf16[1,3,384,128]{3,2,1,0:T(8,128)(2,1)S(1)}, u32[]{:S(2)}, u32[]{:S(2)}) collective-permute-start(bf16[1,3,384,128]{3,2,1,0:T(8,128)(2,1)S(1)} %add_convert_fusion.12), channel_id=1, source_target_pairs={{0,2},{1,3},{2,0},{3,1},{4,6},{5,7},{6,4},{7,5},{8,10},{9,11},{10,... | collective-permute-start | bytes 884744 | tf_op jit(solution)/shard_map/ppermute | solution.py:20
  24.9 23.0 %copy-start.5 = (f32[7,64]{1,0:T(8,128)S(1)}, f32[7,64]{1,0:T(8,128)}, u32[]{:S(2)}) copy-start(f32[7,64]{1,0:T(8,128)} %taps_ref.1) | copy-start | bytes 5380
  35.9 1.8 %collective-permute-start.9 = (bf16[2,3,256,128]{3,2,1,0:T(8,128)(2,1)S(1)}, bf16[2,3,256,128]{3,2,1,0:T(8,128)(2,1)S(1)}, u32[]{:S(2)}, u32[]{:S(2)}) collective-permute-start(bf16[2,3,256,128]{3,2,1,0:T(8,128)(2,1)S(1)} %get-tuple-element.81), channel_id=1, source_target_pairs={{0,1},{1,0},{2,3},{3,2},{4,5},{5,4},{6,7},{7,6},{8,9},{9,8},{10,11... | collective-permute-start | bytes 1179656 | tf_op jit(solution)/shard_map/ppermute | solution.py:20
  36.0 5.2 %collective-permute-start.11 = (bf16[1,3,128,128]{3,2,1,0:T(8,128)(2,1)S(1)}, bf16[1,3,128,128]{3,2,1,0:T(8,128)(2,1)S(1)}, u32[]{:S(2)}, u32[]{:S(2)}) collective-permute-start(bf16[1,3,128,128]{3,2,1,0:T(8,128)(2,1)S(1)} %add_convert_fusion.14), channel_id=1, source_target_pairs={{0,2},{1,3},{2,0},{3,1},{4,6},{5,7},{6,4},{7,5},{8,10},{9,11},{10,... | collective-permute-start | bytes 294920 | tf_op jit(solution)/shard_map/ppermute | solution.py:20
  41.2 6.7 %collective-permute-start.12 = (bf16[1,3,256,128]{3,2,1,0:T(8,128)(2,1)S(1)}, bf16[1,3,256,128]{3,2,1,0:T(8,128)(2,1)S(1)}, u32[]{:S(2)}, u32[]{:S(2)}) collective-permute-start(bf16[1,3,256,128]{3,2,1,0:T(8,128)(2,1)S(1)} %add_convert_fusion.13), channel_id=1, source_target_pairs={{0,2},{1,3},{2,0},{3,1},{4,6},{5,7},{6,4},{7,5},{8,10},{9,11},{10,... | collective-permute-start | bytes 589832 | tf_op jit(solution)/shard_map/ppermute | solution.py:20
  43.2 4.7 %collective-permute-start.10 = (bf16[384,128]{1,0:T(8,128)(2,1)S(1)}, bf16[384,128]{1,0:T(8,128)(2,1)S(1)}, u32[]{:S(2)}, u32[]{:S(2)}) collective-permute-start(bf16[384,128]{1,0:T(8,128)(2,1)S(1)} %get-tuple-element.84), channel_id=1, source_target_pairs={{0,4},{4,0},{1,5},{5,1},{2,6},{6,2},{3,7},{7,3},{8,12},{12,8},{9,1... | collective-permute-start | bytes 294920 | tf_op jit(solution)/shard_map/ppermute | solution.py:20
  49.5 6.5 %collective-permute-start.13 = (bf16[3,384,128]{2,1,0:T(8,128)(2,1)S(1)}, bf16[3,384,128]{2,1,0:T(8,128)(2,1)S(1)}, u32[]{:S(2)}, u32[]{:S(2)}) collective-permute-start(bf16[3,384,128]{2,1,0:T(8,128)(2,1)S(1)} %get-tuple-element.88.refs_0_), channel_id=1, source_target_pairs={{0,1},{1,0},{2,3},{3,2},{4,5},{5,4},{6,7},{7,6},{8,9},{9,8},{10,11... | collective-permute-start | bytes 884744 | tf_op jit(solution)/shard_map/ppermute | solution.py:20
  49.6 6.4 %collective-permute-start.16 = (bf16[3,384,128]{2,1,0:T(8,128)(2,1)S(1)}, bf16[3,384,128]{2,1,0:T(8,128)(2,1)S(1)}, u32[]{:S(2)}, u32[]{:S(2)}) collective-permute-start(bf16[3,384,128]{2,1,0:T(8,128)(2,1)S(1)} %get-tuple-element.87.refs_0_), channel_id=1, source_target_pairs={{0,1},{1,0},{2,3},{3,2},{4,5},{5,4},{6,7},{7,6},{8,9},{9,8},{10,11... | collective-permute-start | bytes 884744 | tf_op jit(solution)/shard_map/ppermute | solution.py:20
  50.1 9.0 %collective-permute-start.14 = (bf16[3,384,128]{2,1,0:T(8,128)(2,1)S(1)}, bf16[3,384,128]{2,1,0:T(8,128)(2,1)S(1)}, u32[]{:S(2)}, u32[]{:S(2)}) collective-permute-start(bf16[3,384,128]{2,1,0:T(8,128)(2,1)S(1)} %get-tuple-element.87.refs_0_), channel_id=1, source_target_pairs={{0,2},{1,3},{2,0},{3,1},{4,6},{5,7},{6,4},{7,5},{8,10},{9,11},{10,... | collective-permute-start | bytes 884744 | tf_op jit(solution)/shard_map/ppermute | solution.py:20
  51.3 4.7 %collective-permute-start.17 = (bf16[416,128]{1,0:T(8,128)(2,1)S(1)}, bf16[416,128]{1,0:T(8,128)(2,1)S(1)}, u32[]{:S(2)}, u32[]{:S(2)}) collective-permute-start(bf16[416,128]{1,0:T(8,128)(2,1)S(1)} %get-tuple-element.89), channel_id=1, source_target_pairs={{0,4},{4,0},{1,5},{5,1},{2,6},{6,2},{3,7},{7,3},{8,12},{12,8},{9,1... | collective-permute-start | bytes 319496 | tf_op jit(solution)/shard_map/ppermute | solution.py:20
  59.1 1.6 %collective-permute-start.18 = (bf16[3,384,128]{2,1,0:T(8,128)(2,1)S(1)}, bf16[3,384,128]{2,1,0:T(8,128)(2,1)S(1)}, u32[]{:S(2)}, u32[]{:S(2)}) collective-permute-start(bf16[3,384,128]{2,1,0:T(8,128)(2,1)S(1)} %collective-permute-done.14.refs_2_), channel_id=1, source_target_pairs={{0,1},{1,0},{2,3},{3,2},{4,5},{5,4},{6,7},{7,6},{8,9},{9,8},{10,11... | collective-permute-start | bytes 884744 | tf_op jit(solution)/shard_map/ppermute | solution.py:20
  59.1 9.4 %collective-permute-start.15 = (bf16[3,384,128]{2,1,0:T(8,128)(2,1)S(1)}, bf16[3,384,128]{2,1,0:T(8,128)(2,1)S(1)}, u32[]{:S(2)}, u32[]{:S(2)}) collective-permute-start(bf16[3,384,128]{2,1,0:T(8,128)(2,1)S(1)} %get-tuple-element.88.refs_0_), channel_id=1, source_target_pairs={{0,2},{1,3},{2,0},{3,1},{4,6},{5,7},{6,4},{7,5},{8,10},{9,11},{10,... | collective-permute-start | bytes 884744 | tf_op jit(solution)/shard_map/ppermute | solution.py:20
  62.2 12.0 %collective-permute-start.20 = (bf16[384,512]{1,0:T(8,128)(2,1)S(1)}, bf16[384,512]{1,0:T(8,128)(2,1)S(1)}, u32[]{:S(2)}, u32[]{:S(2)}) collective-permute-start(bf16[384,512]{1,0:T(8,128)(2,1)S(1)} %input_grad.4), channel_id=1, source_target_pairs={{0,4},{4,0},{1,5},{5,1},{2,6},{6,2},{3,7},{7,3},{8,12},{12,8},{9,1... | collective-permute-start | bytes 1179656 | tf_op jit(solution)/shard_map/ppermute | solution.py:20
  68.5 1.6 %collective-permute-start.19 = (bf16[3,384,128]{2,1,0:T(8,128)(2,1)S(1)}, bf16[3,384,128]{2,1,0:T(8,128)(2,1)S(1)}, u32[]{:S(2)}, u32[]{:S(2)}) collective-permute-start(bf16[3,384,128]{2,1,0:T(8,128)(2,1)S(1)} %collective-permute-done.15.refs_2_), channel_id=1, source_target_pairs={{0,1},{1,0},{2,3},{3,2},{4,5},{5,4},{6,7},{7,6},{8,9},{9,8},{10,11... | collective-permute-start | bytes 884744 | tf_op jit(solution)/shard_map/ppermute | solution.py:20
  68.5 14.1 %collective-permute-start.21 = (bf16[384,512]{1,0:T(8,128)(2,1)S(1)}, bf16[384,512]{1,0:T(8,128)(2,1)S(1)}, u32[]{:S(2)}, u32[]{:S(2)}) collective-permute-start(bf16[384,512]{1,0:T(8,128)(2,1)S(1)} %get-tuple-element.97), channel_id=1, source_target_pairs={{0,4},{4,0},{1,5},{5,1},{2,6},{6,2},{3,7},{7,3},{8,12},{12,8},{9,1... | collective-permute-start | bytes 1179656 | tf_op jit(solution)/shard_map/ppermute | solution.py:20
  74.3 9.8 %collective-permute-start.22 = (bf16[384,512]{1,0:T(8,128)(2,1)S(1)}, bf16[384,512]{1,0:T(8,128)(2,1)S(1)}, u32[]{:S(2)}, u32[]{:S(2)}) collective-permute-start(bf16[384,512]{1,0:T(8,128)(2,1)S(1)} %add_convert_fusion.11), channel_id=1, source_target_pairs={{0,8},{8,0},{16,24},{24,16},{1,9},{9,1},{17,25},{25,17},{2,10},{10... | collective-permute-start | bytes 1179656 | tf_op jit(solution)/shard_map/ppermute | solution.py:20
  75.7 14.6 %collective-permute-start.23 = (bf16[384,512]{1,0:T(8,128)(2,1)S(1)}, bf16[384,512]{1,0:T(8,128)(2,1)S(1)}, u32[]{:S(2)}, u32[]{:S(2)}) collective-permute-start(bf16[384,512]{1,0:T(8,128)(2,1)S(1)} %get-tuple-element.101), channel_id=1, source_target_pairs={{0,4},{4,0},{1,5},{5,1},{2,6},{6,2},{3,7},{7,3},{8,12},{12,8},{9,1... | collective-permute-start | bytes 1179656 | tf_op jit(solution)/shard_map/ppermute | solution.py:20
  82.7 11.7 %collective-permute-start.27 = (bf16[384,512]{1,0:T(8,128)(2,1)S(1)}, bf16[384,512]{1,0:T(8,128)(2,1)S(1)}, u32[]{:S(2)}, u32[]{:S(2)}) collective-permute-start(bf16[384,512]{1,0:T(8,128)(2,1)S(1)} %add_convert_fusion.10), channel_id=1, source_target_pairs={{0,8},{8,0},{16,24},{24,16},{1,9},{9,1},{17,25},{25,17},{2,10},{10... | collective-permute-start | bytes 1179656 | tf_op jit(solution)/shard_map/ppermute | solution.py:20
  84.2 10.3 %collective-permute-start.28 = (bf16[384,512]{1,0:T(8,128)(2,1)S(1)}, bf16[384,512]{1,0:T(8,128)(2,1)S(1)}, u32[]{:S(2)}, u32[]{:S(2)}) collective-permute-start(bf16[384,512]{1,0:T(8,128)(2,1)S(1)} %add_convert_fusion.9), channel_id=1, source_target_pairs={{0,0},{8,16},{16,8},{24,24},{1,1},{9,17},{17,9},{25,25},{2,2},{10,... | collective-permute-start | bytes 1179656 | tf_op jit(solution)/shard_map/ppermute | solution.py:602
  85.5 5.0 %collective-permute-start.24 = (bf16[2,128,128]{2,1,0:T(8,128)(2,1)S(1)}, bf16[2,128,128]{2,1,0:T(8,128)(2,1)S(1)}, u32[]{:S(2)}, u32[]{:S(2)}) collective-permute-start(bf16[2,128,128]{2,1,0:T(8,128)(2,1)S(1)} %get-tuple-element.104), channel_id=1, source_target_pairs={{0,1},{1,0},{2,3},{3,2},{4,5},{5,4},{6,7},{7,6},{8,9},{9,8},{10,11... | collective-permute-start | bytes 196616 | tf_op jit(solution)/shard_map/ppermute | solution.py:20
  85.5 5.7 %collective-permute-start.25 = (bf16[2,128,128]{2,1,0:T(8,128)(2,1)S(1)}, bf16[2,128,128]{2,1,0:T(8,128)(2,1)S(1)}, u32[]{:S(2)}, u32[]{:S(2)}) collective-permute-start(bf16[2,128,128]{2,1,0:T(8,128)(2,1)S(1)} %get-tuple-element.105), channel_id=1, source_target_pairs={{0,2},{1,3},{2,0},{3,1},{4,6},{5,7},{6,4},{7,5},{8,10},{9,11},{10,... | collective-permute-start | bytes 196616 | tf_op jit(solution)/shard_map/ppermute | solution.py:20
  90.2 4.2 %collective-permute-start.26 = (bf16[2,128,128]{2,1,0:T(8,128)(2,1)S(1)}, bf16[2,128,128]{2,1,0:T(8,128)(2,1)S(1)}, u32[]{:S(2)}, u32[]{:S(2)}) collective-permute-start(bf16[2,128,128]{2,1,0:T(8,128)(2,1)S(1)} %get-tuple-element.106), channel_id=1, source_target_pairs={{0,3},{1,2},{2,1},{3,0},{4,7},{5,6},{6,5},{7,4},{8,11},{9,10},{10,... | collective-permute-start | bytes 196616 | tf_op jit(solution)/shard_map/ppermute | solution.py:20
  90.5 7.4 %copy-start.3 = (bf16[384,2048]{1,0:T(8,128)(2,1)S(1)}, bf16[384,2048]{1,0:T(8,128)(2,1)}, u32[]{:S(2)}) copy-start(bf16[384,2048]{1,0:T(8,128)(2,1)} %refs_4_.1) | copy-start | bytes 4718596
  90.5 13.0 %collective-permute-start.29 = (bf16[384,512]{1,0:T(8,128)(2,1)S(1)}, bf16[384,512]{1,0:T(8,128)(2,1)S(1)}, u32[]{:S(2)}, u32[]{:S(2)}) collective-permute-start(bf16[384,512]{1,0:T(8,128)(2,1)S(1)} %get-tuple-element.115), channel_id=1, source_target_pairs={{0,4},{4,0},{1,5},{5,1},{2,6},{6,2},{3,7},{7,3},{8,12},{12,8},{9,1... | collective-permute-start | bytes 1179656 | tf_op jit(solution)/shard_map/ppermute | solution.py:20
  94.7 11.0 %collective-permute-start.30 = (bf16[384,512]{1,0:T(8,128)(2,1)S(1)}, bf16[384,512]{1,0:T(8,128)(2,1)S(1)}, u32[]{:S(2)}, u32[]{:S(2)}) collective-permute-start(bf16[384,512]{1,0:T(8,128)(2,1)S(1)} %get-tuple-element.130), channel_id=1, source_target_pairs={{0,8},{8,0},{16,24},{24,16},{1,9},{9,1},{17,25},{25,17},{2,10},{10... | collective-permute-start | bytes 1179656 | tf_op jit(solution)/shard_map/ppermute | solution.py:20
  97.0 8.8 %collective-permute-start.31 = (bf16[384,512]{1,0:T(8,128)(2,1)S(1)}, bf16[384,512]{1,0:T(8,128)(2,1)S(1)}, u32[]{:S(2)}, u32[]{:S(2)}) collective-permute-start(bf16[384,512]{1,0:T(8,128)(2,1)S(1)} %add_convert_fusion.7), channel_id=1, source_target_pairs={{0,0},{8,16},{16,8},{24,24},{1,1},{9,17},{17,9},{25,25},{2,2},{10,... | collective-permute-start | bytes 1179656 | tf_op jit(solution)/shard_map/ppermute | solution.py:602
  106.0 12.5 %collective-permute-start.32 = (bf16[384,512]{1,0:T(8,128)(2,1)S(1)}, bf16[384,512]{1,0:T(8,128)(2,1)S(1)}, u32[]{:S(2)}, u32[]{:S(2)}) collective-permute-start(bf16[384,512]{1,0:T(8,128)(2,1)S(1)} %get-tuple-element.128), channel_id=1, source_target_pairs={{0,8},{8,0},{16,24},{24,16},{1,9},{9,1},{17,25},{25,17},{2,10},{10... | collective-permute-start | bytes 1179656 | tf_op jit(solution)/shard_map/ppermute | solution.py:20
  110.2 9.1 %collective-permute-start.33 = (bf16[384,512]{1,0:T(8,128)(2,1)S(1)}, bf16[384,512]{1,0:T(8,128)(2,1)S(1)}, u32[]{:S(2)}, u32[]{:S(2)}) collective-permute-start(bf16[384,512]{1,0:T(8,128)(2,1)S(1)} %add_convert_fusion.4), channel_id=1, source_target_pairs={{0,0},{8,16},{16,8},{24,24},{1,1},{9,17},{17,9},{25,25},{2,2},{10,... | collective-permute-start | bytes 1179656 | tf_op jit(solution)/shard_map/ppermute | solution.py:602
  118.6 5.3 %collective-permute-start.34 = (bf16[384,512]{1,0:T(8,128)(2,1)S(1)}, bf16[384,512]{1,0:T(8,128)(2,1)S(1)}, u32[]{:S(2)}, u32[]{:S(2)}) collective-permute-start(bf16[384,512]{1,0:T(8,128)(2,1)S(1)} %add_convert_fusion.2), channel_id=1, source_target_pairs={{0,0},{8,16},{16,8},{24,24},{1,1},{9,17},{17,9},{25,25},{2,2},{10,... | collective-permute-start | bytes 1179656 | tf_op jit(solution)/shard_map/ppermute | solution.py:602
  119.5 13.5 %collective-permute-start.35 = (bf16[384,512]{1,0:T(8,128)(2,1)S(1)}, bf16[384,512]{1,0:T(8,128)(2,1)S(1)}, u32[]{:S(2)}, u32[]{:S(2)}) collective-permute-start(bf16[384,512]{1,0:T(8,128)(2,1)S(1)} %add_convert_fusion.1), channel_id=1, source_target_pairs={{0,8},{8,0},{16,24},{24,16},{1,9},{9,1},{17,25},{25,17},{2,10},{10... | collective-permute-start | bytes 1179656 | tf_op jit(solution)/shard_map/ppermute | solution.py:20
  124.0 15.1 %collective-permute-start.36 = (bf16[384,512]{1,0:T(8,128)(2,1)S(1)}, bf16[384,512]{1,0:T(8,128)(2,1)S(1)}, u32[]{:S(2)}, u32[]{:S(2)}) collective-permute-start(bf16[384,512]{1,0:T(8,128)(2,1)S(1)} %add_convert_fusion), channel_id=1, source_target_pairs={{0,8},{8,0},{16,24},{24,16},{1,9},{9,1},{17,25},{25,17},{2,10},{10... | collective-permute-start | bytes 1179656 | tf_op jit(solution)/shard_map/ppermute | solution.py:20

commit v16 on v13

--- a/solution.py
+++ b/solution.py
@@ -594,8 +594,10 @@
                 marks = [summed[slot - 2]]
             if 0 <= slot - 3 < chunks:
                 done[slot - 3] = jnp.where(outer, pair, summed[slot - 3])
-            if slot < chunks + 2:
-                out = summed[slot - 2] if slot >= 2 else inward[slot]
+            if slot < 2:
+                pair = lax.ppermute(inward[slot], "row", [(0, 1), (3, 2)])
+            elif slot < chunks + 2:
+                out = summed[slot - 2]
                 pair = swap(jnp.where(outer, inward[slot], out) if slot < chunks else out, "row", 1)
             if 0 <= slot - 1 < chunks:
                 cross = lax.ppermute(across[slot - 1], "row", [(0, 0), (1, 2), (2, 1), (3, 3)])

time: 136 us -> 136 us (level)
  starting transfers between devices: 43 us -> 46.6 us
  waiting for transfers between devices: 47.2 us -> 44 us
    ppermute x0 -> x2, starting transfers between devices: none -> 6.44 us  [on_device(): pair = lax.ppermute(inward[slot], 'row', [(0, 1), (3, 2)])]
    ppermute x33 -> x31, waiting for transfers between devices: 47.2 us -> 42.2 us  [swap(): return lax.ppermute(value, axis, [(i, i ^ flip) for i in range(count)])]
    ppermute x33 -> x31, starting transfers between devices: 40.1 us -> 37.2 us  [swap(): return lax.ppermute(value, axis, [(i, i ^ flip) for i in range(count)])]
    ppermute x0 -> x2, waiting for transfers between devices: none -> 1.8 us  [on_device(): pair = lax.ppermute(inward[slot], 'row', [(0, 1), (3, 2)])]
where the time goes in v16:
time: 136 us
  starting transfers between devices  46.6 us (34%)
  waiting for transfers between devices  44 us (32%)
  Pallas kernels  35.1 us (26%)
  local copies, waits for them, and re-layouts  6.22 us (5%)
  other arithmetic  3.07 us (2%)
    ppermute x31, waiting for transfers between devices, swap(): return lax.ppermute(value, axis, [(i, i ^ flip) for i in range(count)])  42.2 us
    ppermute x31, starting transfers between devices, swap(): return lax.ppermute(value, axis, [(i, i ^ flip) for i in range(count)])  37.2 us
    pallas_call x2, Pallas kernels, weight_grad(): pl.pallas_call(functools.partial(weight_grad_kernel, chained=chained, gro...  11.2 us
    pallas_call x3, Pallas kernels, project(): pl.pallas_call(functools.partial(project_kernel, pieces=len(xs), mode=mod...  10.3 us
    pallas_call x4, Pallas kernels, input_grad(): pl.pallas_call(functools.partial(input_grad_kernel if single else input_g...  7.49 us
    ppermute x2, starting transfers between devices, on_device(): pair = lax.ppermute(inward[slot], 'row', [(0, 1), (3, 2)])  6.44 us
    unnamed x12, local copies, waits for them, and re-layouts  5.14 us
    ppermute x4, starting transfers between devices, on_device(): lax.ppermute(across[slot - 1], 'row', [(0, 0), (1, 2), (2, 1), (3, 3)])  2.9 us
  transfers between devices with their start and end apart: 37, of which 17 were waited for; matrix products, arithmetic and copies ran while one was open for 1% of the time, Pallas kernels for 22%

profile of v16, /device:TPU:0, one launch (start us, length us, event | category | flops | bytes accessed | tf_op | source)
XLA Modules:
  0.0 136.0 jit_solution(12565128709005746067)
XLA Ops:
  0.6 1.1 constant_dynamic-slice_fusion
  1.7 3.0 %collective-permute-start = (bf16[128,2048]{1,0:T(8,128)(2,1)S(1)}, bf16[128,2048]{1,0:T(8,128)(2,1)S(1)}, u32[]{:S(2)}, u32[]{:S(2)}) collective-permute-start(bf16[128,2048]{1,0:T(8,128)(2,1)S(1)} %constant_dynamic-slice_fusion), channel_id=1, source_target_pairs={{0,4},{4,0},{1,5},{5,1},{2,6},{6,2},{3,7},{7,3},{8,12},{12,8},{9,1... | collective-permute-start | bytes 1572872 | tf_op jit(solution)/shard_map/ppermute | solution.py:20
  4.9 0.9 copy-done.4
  5.8 0.6 split.2
  6.5 1.6 %collective-permute-start.4 = (bf16[2,96,128]{2,1,0:T(8,128)(2,1)S(1)}, bf16[2,96,128]{2,1,0:T(8,128)(2,1)S(1)}, u32[]{:S(2)}, u32[]{:S(2)}) collective-permute-start(bf16[2,96,128]{2,1,0:T(8,128)(2,1)S(1)} %get-tuple-element.73), channel_id=1, source_target_pairs={{0,2},{1,3},{2,0},{3,1},{4,6},{5,7},{6,4},{7,5},{8,10},{9,11},{10,... | collective-permute-start | bytes 147464 | tf_op jit(solution)/shard_map/ppermute | solution.py:20
  8.3 2.8 %copy-done = bf16[512,3,2048]{2,0,1:T(8,128)(2,1)S(1)} copy-done((bf16[512,3,2048]{2,0,1:T(8,128)(2,1)S(1)}, bf16[512,3,2048]{2,0,1:T(8,128)(2,1)}, u32[]{:S(2)}) %copy-start) | copy-done | bytes 6291480
  11.1 1.4 %copy-done.2 = bf16[384,2048]{1,0:T(8,128)(2,1)S(1)} copy-done((bf16[384,2048]{1,0:T(8,128)(2,1)S(1)}, bf16[384,2048]{1,0:T(8,128)(2,1)}, u32[]{:S(2)}) %copy-start.2) | copy-done | bytes 1572888
  12.5 4.1 %project.3 = (bf16[2,3,384,128]{3,2,1,0:T(8,128)(2,1)S(1)}, bf16[2,3,384,128]{3,2,1,0:T(8,128)(2,1)S(1)}, bf16[128,2048]{1,0:T(8,128)(2,1)S(1)}) custom-call(s32[4]{0:T(128)S(1)} %pad_add_fusion.place, bf16[384,2048]{1,0:T(8,128)(2,1)S(1)} %copy-done.2, bf16[3,512,2048]{2,1,0:T(8,128)(2,1)S(1)} %bitcast.6), custom_call_target="tpu_custom_call" | custom-call | flops 1 | bytes 1 | tf_op jit(solution)/shard_map/project/pallas_call | solution.py:97
  17.0 1.4 %collective-permute-start.2 = (bf16[128,2048]{1,0:T(8,128)(2,1)S(1)}, bf16[128,2048]{1,0:T(8,128)(2,1)S(1)}, u32[]{:S(2)}, u32[]{:S(2)}) collective-permute-start(bf16[128,2048]{1,0:T(8,128)(2,1)S(1)} %get-tuple-element.69), channel_id=1, source_target_pairs={{0,4},{4,0},{1,5},{5,1},{2,6},{6,2},{3,7},{7,3},{8,12},{12,8},{9,1... | collective-permute-start | bytes 1572872 | tf_op jit(solution)/shard_map/ppermute | solution.py:20
  18.4 1.6 %collective-permute-start.1 = (bf16[128,2048]{1,0:T(8,128)(2,1)S(1)}, bf16[128,2048]{1,0:T(8,128)(2,1)S(1)}, u32[]{:S(2)}, u32[]{:S(2)}) collective-permute-start(bf16[128,2048]{1,0:T(8,128)(2,1)S(1)} %collective-permute-done.refs_0_), channel_id=1, source_target_pairs={{0,8},{8,0},{16,24},{24,16},{1,9},{9,1},{17,25},{25,17},{2,10},{10... | collective-permute-start | bytes 1572872 | tf_op jit(solution)/shard_map/ppermute | solution.py:20
  20.1 3.1 %project.4 = (bf16[2,3,128,128]{3,2,1,0:T(8,128)(2,1)S(1)}, bf16[2,3,128,128]{3,2,1,0:T(8,128)(2,1)S(1)}) custom-call(s32[4]{0:T(128)S(1)} %pad_add_fusion.place, bf16[128,2048]{1,0:T(8,128)(2,1)S(1)} %collective-permute-done.refs_0_, bf16[3,512,2048]{2,1,0:T(8,128)(2,1)S(1)} %bitcast.7), custom_call_target="tpu_custom_call" | custom-call | flops 1 | bytes 1 | tf_op jit(solution)/shard_map/project/pallas_call | solution.py:97
  23.4 1.6 %collective-permute-start.7 = (bf16[1,3,384,128]{3,2,1,0:T(8,128)(2,1)S(1)}, bf16[1,3,384,128]{3,2,1,0:T(8,128)(2,1)S(1)}, u32[]{:S(2)}, u32[]{:S(2)}) collective-permute-start(bf16[1,3,384,128]{3,2,1,0:T(8,128)(2,1)S(1)} %add_convert_fusion.12), channel_id=1, source_target_pairs={{0,2},{1,3},{2,0},{3,1},{4,6},{5,7},{6,4},{7,5},{8,10},{9,11},{10,... | collective-permute-start | bytes 884744 | tf_op jit(solution)/shard_map/ppermute | solution.py:20
  25.0 6.1 %collective-permute-done.2.refs_2_ = bf16[128,2048]{1,0:T(8,128)(2,1)S(1)} collective-permute-done((bf16[128,2048]{1,0:T(8,128)(2,1)S(1)}, bf16[128,2048]{1,0:T(8,128)(2,1)S(1)}, u32[]{:S(2)}, u32[]{:S(2)}) %collective-permute-start.2) | collective-permute-done | bytes 524320 | tf_op jit(solution)/shard_map/ppermute | solution.py:20
  31.0 1.7 %collective-permute-done.7.refs_4_ = bf16[1,3,384,128]{3,2,1,0:T(8,128)(2,1)S(1)} collective-permute-done((bf16[1,3,384,128]{3,2,1,0:T(8,128)(2,1)S(1)}, bf16[1,3,384,128]{3,2,1,0:T(8,128)(2,1)S(1)}, u32[]{:S(2)}, u32[]{:S(2)}) %collective-permute-start.7) | collective-permute-done | bytes 294944 | tf_op jit(solution)/shard_map/ppermute | solution.py:20
  32.8 3.1 %project.5 = (bf16[2,3,256,128]{3,2,1,0:T(8,128)(2,1)S(1)}, bf16[2,3,256,128]{3,2,1,0:T(8,128)(2,1)S(1)}, bf16[384,2048]{1,0:T(8,128)(2,1)S(1)}) custom-call(s32[4]{0:T(128)S(1)} %pad_add_fusion.place, bf16[128,2048]{1,0:T(8,128)(2,1)S(1)} %collective-permute-done.refs_0_, bf16[128,2048]{1,0:T(8,128)(2,1)S(1)} %collective-permute-done.1.refs_1_, ...), custom_call_target="tpu_custom_call" | custom-call | flops 1 | bytes 1 | tf_op jit(solution)/shard_map/project/pallas_call | solution.py:97
  36.0 1.6 %collective-permute-start.11 = (bf16[1,3,128,128]{3,2,1,0:T(8,128)(2,1)S(1)}, bf16[1,3,128,128]{3,2,1,0:T(8,128)(2,1)S(1)}, u32[]{:S(2)}, u32[]{:S(2)}) collective-permute-start(bf16[1,3,128,128]{3,2,1,0:T(8,128)(2,1)S(1)} %add_convert_fusion.14), channel_id=1, source_target_pairs={{0,2},{1,3},{2,0},{3,1},{4,6},{5,7},{6,4},{7,5},{8,10},{9,11},{10,... | collective-permute-start | bytes 294920 | tf_op jit(solution)/shard_map/ppermute | solution.py:20
  37.7 3.4 %collective-permute-done.11.refs_7_ = bf16[1,3,128,128]{3,2,1,0:T(8,128)(2,1)S(1)} collective-permute-done((bf16[1,3,128,128]{3,2,1,0:T(8,128)(2,1)S(1)}, bf16[1,3,128,128]{3,2,1,0:T(8,128)(2,1)S(1)}, u32[]{:S(2)}, u32[]{:S(2)}) %collective-permute-start.11) | collective-permute-done | bytes 98336 | tf_op jit(solution)/shard_map/ppermute | solution.py:20
  41.2 1.5 %collective-permute-start.12 = (bf16[1,3,256,128]{3,2,1,0:T(8,128)(2,1)S(1)}, bf16[1,3,256,128]{3,2,1,0:T(8,128)(2,1)S(1)}, u32[]{:S(2)}, u32[]{:S(2)}) collective-permute-start(bf16[1,3,256,128]{3,2,1,0:T(8,128)(2,1)S(1)} %add_convert_fusion.13), channel_id=1, source_target_pairs={{0,2},{1,3},{2,0},{3,1},{4,6},{5,7},{6,4},{7,5},{8,10},{9,11},{10,... | collective-permute-start | bytes 589832 | tf_op jit(solution)/shard_map/ppermute | solution.py:20
  42.7 0.6 merge.1
  43.2 0.7 collective-permute-start.10
  44.0 4.0 %collective-permute-done.10.refs_1_ = bf16[384,128]{1,0:T(8,128)(2,1)S(1)} collective-permute-done((bf16[384,128]{1,0:T(8,128)(2,1)S(1)}, bf16[384,128]{1,0:T(8,128)(2,1)S(1)}, u32[]{:S(2)}, u32[]{:S(2)}) %collective-permute-start.10) | collective-permute-done | bytes 98336 | tf_op jit(solution)/shard_map/ppermute | solution.py:20
  47.9 1.5 %middle.1 = (bf16[3,384,128]{2,1,0:T(8,128)(2,1)S(1)}, bf16[3,384,128]{2,1,0:T(8,128)(2,1)S(1)}, bf16[416,128]{1,0:T(8,128)(2,1)S(1)}, bf16[416,128]{1,0:T(8,128)(2,1)S(1)}) custom-call(s32[4]{0:T(128)S(1)} %pad_add_fusion.place, f32[7,64]{1,0:T(8,128)S(1)} %copy-done.5, bf16[384,128]{1,0:T(8,128)(2,1)S(1)} %get-tuple-element.83.refs_0_, ...), custom_call_target="tpu_custom_call" | custom-call | flops 1 | bytes 1 | tf_op jit(solution)/shard_map/middle/pallas_call | solution.py:326
  49.6 0.5 collective-permute-start.16
  50.1 1.2 collective-permute-start.14
  51.3 0.7 collective-permute-start.17
  51.9 4.1 %collective-permute-done.17.refs_1_ = bf16[416,128]{1,0:T(8,128)(2,1)S(1)} collective-permute-done((bf16[416,128]{1,0:T(8,128)(2,1)S(1)}, bf16[416,128]{1,0:T(8,128)(2,1)S(1)}, u32[]{:S(2)}, u32[]{:S(2)}) %collective-permute-start.17) | collective-permute-done | bytes 106528 | tf_op jit(solution)/shard_map/ppermute | solution.py:20
  56.0 3.1 %collective-permute-done.14.refs_2_ = bf16[3,384,128]{2,1,0:T(8,128)(2,1)S(1)} collective-permute-done((bf16[3,384,128]{2,1,0:T(8,128)(2,1)S(1)}, bf16[3,384,128]{2,1,0:T(8,128)(2,1)S(1)}, u32[]{:S(2)}, u32[]{:S(2)}) %collective-permute-start.14) | collective-permute-done | bytes 294944 | tf_op jit(solution)/shard_map/ppermute | solution.py:20
  59.1 1.2 collective-permute-start.15
  60.3 0.4 collective-permute-done.18.refs_3_
  60.6 0.7 assemble.2.grad_ref.refs_1_.refs_3_
  61.4 0.8 input_grad.4
  62.2 0.7 collective-permute-start.20
  62.9 3.0 %input_grad.5 = (bf16[384,512]{1,0:T(8,128)(2,1)S(1)}, bf16[384,512]{1,0:T(8,128)(2,1)S(1)}, bf16[384,512]{1,0:T(8,128)(2,1)S(1)}) custom-call(bf16[384,1536]{1,0:T(8,128)(2,1)S(1)} %assemble.2.grad_ref.refs_1_.refs_3_, bf16[3,512,2048]{2,1,0:T(8,128)(2,1)S(1)} %bitcast.10), custom_call_target="tpu_custom_call" | custom-call | flops 1 | bytes 1 | tf_op jit(solution)/shard_map/input_grad/pallas_call | solution.py:414
  65.9 2.6 %collective-permute-done.15.refs_2_ = bf16[3,384,128]{2,1,0:T(8,128)(2,1)S(1)} collective-permute-done((bf16[3,384,128]{2,1,0:T(8,128)(2,1)S(1)}, bf16[3,384,128]{2,1,0:T(8,128)(2,1)S(1)}, u32[]{:S(2)}, u32[]{:S(2)}) %collective-permute-start.15) | collective-permute-done | bytes 294944 | tf_op jit(solution)/shard_map/ppermute | solution.py:20
  68.5 0.7 collective-permute-start.21
  69.1 0.9 collective-permute-done.19.refs_3_
  70.1 0.7 assemble.3.grad_ref.refs_0_.refs_2_
  70.8 0.8 input_grad.6
  71.6 2.6 %collective-permute-done.20 = bf16[384,512]{1,0:T(8,128)(2,1)S(1)} collective-permute-done((bf16[384,512]{1,0:T(8,128)(2,1)S(1)}, bf16[384,512]{1,0:T(8,128)(2,1)S(1)}, u32[]{:S(2)}, u32[]{:S(2)}) %collective-permute-start.20) | collective-permute-done | bytes 393248 | tf_op jit(solution)/shard_map/ppermute | solution.py:20
  74.3 3.2 %collective-permute-start.22 = (bf16[384,512]{1,0:T(8,128)(2,1)S(1)}, bf16[384,512]{1,0:T(8,128)(2,1)S(1)}, u32[]{:S(2)}, u32[]{:S(2)}) collective-permute-start(bf16[384,512]{1,0:T(8,128)(2,1)S(1)} %add_convert_fusion.11), channel_id=1, source_target_pairs={{0,8},{24,16},{1,9},{25,17},{2,10},{26,18},{3,11},{27,19},{4,12},{... | collective-permute-start | bytes 1179656 | tf_op jit(solution)/shard_map/ppermute | solution.py:598
  77.5 0.8 collective-permute-start.23
  78.3 3.0 %input_grad.7 = (bf16[384,512]{1,0:T(8,128)(2,1)S(1)}, bf16[384,512]{1,0:T(8,128)(2,1)S(1)}, bf16[384,512]{1,0:T(8,128)(2,1)S(1)}) custom-call(bf16[384,1536]{1,0:T(8,128)(2,1)S(1)} %assemble.3.grad_ref.refs_0_.refs_2_, bf16[3,512,2048]{2,1,0:T(8,128)(2,1)S(1)} %bitcast.12), custom_call_target="tpu_custom_call" | custom-call | flops 1 | bytes 1 | tf_op jit(solution)/shard_map/input_grad/pallas_call | solution.py:414
  81.3 1.4 %collective-permute-done.21 = bf16[384,512]{1,0:T(8,128)(2,1)S(1)} collective-permute-done((bf16[384,512]{1,0:T(8,128)(2,1)S(1)}, bf16[384,512]{1,0:T(8,128)(2,1)S(1)}, u32[]{:S(2)}, u32[]{:S(2)}) %collective-permute-start.21) | collective-permute-done | bytes 393248 | tf_op jit(solution)/shard_map/ppermute | solution.py:20
  82.7 3.2 %collective-permute-start.24 = (bf16[384,512]{1,0:T(8,128)(2,1)S(1)}, bf16[384,512]{1,0:T(8,128)(2,1)S(1)}, u32[]{:S(2)}, u32[]{:S(2)}) collective-permute-start(bf16[384,512]{1,0:T(8,128)(2,1)S(1)} %add_convert_fusion.10), channel_id=1, source_target_pairs={{0,8},{24,16},{1,9},{25,17},{2,10},{26,18},{3,11},{27,19},{4,12},{... | collective-permute-start | bytes 1179656 | tf_op jit(solution)/shard_map/ppermute | solution.py:598
  85.9 0.8 collective-permute-start.26
  86.8 0.7 collective-permute-start.25
  87.5 3.5 %collective-permute-done.23 = bf16[384,512]{1,0:T(8,128)(2,1)S(1)} collective-permute-done((bf16[384,512]{1,0:T(8,128)(2,1)S(1)}, bf16[384,512]{1,0:T(8,128)(2,1)S(1)}, u32[]{:S(2)}, u32[]{:S(2)}) %collective-permute-start.23) | collective-permute-done | bytes 393248 | tf_op jit(solution)/shard_map/ppermute | solution.py:20
  91.2 1.8 %collective-permute-done.24 = bf16[384,512]{1,0:T(8,128)(2,1)S(1)} collective-permute-done((bf16[384,512]{1,0:T(8,128)(2,1)S(1)}, bf16[384,512]{1,0:T(8,128)(2,1)S(1)}, u32[]{:S(2)}, u32[]{:S(2)}) %collective-permute-start.24) | collective-permute-done | bytes 393248 | tf_op jit(solution)/shard_map/ppermute | solution.py:598
  93.2 4.7 %collective-permute-start.27 = (bf16[384,512]{1,0:T(8,128)(2,1)S(1)}, bf16[384,512]{1,0:T(8,128)(2,1)S(1)}, u32[]{:S(2)}, u32[]{:S(2)}) collective-permute-start(bf16[384,512]{1,0:T(8,128)(2,1)S(1)} %get-tuple-element.130), channel_id=1, source_target_pairs={{0,8},{8,0},{16,24},{24,16},{1,9},{9,1},{17,25},{25,17},{2,10},{10... | collective-permute-start | bytes 1179656 | tf_op jit(solution)/shard_map/ppermute | solution.py:20
  98.0 0.9 collective-permute-start.28
  98.8 5.6 %weight_grad.2 = (f32[3,512,2048]{2,1,0:T(8,128)}, f32[8,128]{1,0:T(8,128)S(1)}) custom-call(bf16[384,1536]{1,0:T(8,128)(2,1)S(1)} %assemble.3.grad_ref.refs_0_.refs_2_, bf16[384,1536]{1,0:T(8,128)(2,1)S(1)} %assemble.2.grad_ref.refs_1_.refs_3_, bf16[384,2048]{1,0:T(8,128)(2,1)S(1)} %copy-done.3, bf16[384,2048]{1,0:T(8,128)(2,1)S(1)} %get-tuple-element.105.refs_3_.refs_5_), custom_call_target="tpu_custom_call" | custom-call | flops 1 | bytes 1 | tf_op jit(solution)/shard_map/weight_grad/pallas_call | solution.py:471
  104.9 3.0 %collective-permute-start.29 = (bf16[384,512]{1,0:T(8,128)(2,1)S(1)}, bf16[384,512]{1,0:T(8,128)(2,1)S(1)}, u32[]{:S(2)}, u32[]{:S(2)}) collective-permute-start(bf16[384,512]{1,0:T(8,128)(2,1)S(1)} %get-tuple-element.128), channel_id=1, source_target_pairs={{0,8},{8,0},{16,24},{24,16},{1,9},{9,1},{17,25},{25,17},{2,10},{10... | collective-permute-start | bytes 1179656 | tf_op jit(solution)/shard_map/ppermute | solution.py:20
  107.9 0.7 collective-permute-start.30
  108.6 0.6 split.3
  109.3 1.3 collective-permute-start.32
  110.5 0.6 collective-permute-start.33
  111.1 2.6 %collective-permute-done.29 = bf16[384,512]{1,0:T(8,128)(2,1)S(1)} collective-permute-done((bf16[384,512]{1,0:T(8,128)(2,1)S(1)}, bf16[384,512]{1,0:T(8,128)(2,1)S(1)}, u32[]{:S(2)}, u32[]{:S(2)}) %collective-permute-start.29) | collective-permute-done | bytes 393248 | tf_op jit(solution)/shard_map/ppermute | solution.py:20
  113.8 0.7 collective-permute-start.34
  114.6 5.0 %collective-permute-start.35 = (bf16[384,512]{1,0:T(8,128)(2,1)S(1)}, bf16[384,512]{1,0:T(8,128)(2,1)S(1)}, u32[]{:S(2)}, u32[]{:S(2)}) collective-permute-start(bf16[384,512]{1,0:T(8,128)(2,1)S(1)} %add_convert_fusion.1), channel_id=1, source_target_pairs={{0,8},{8,0},{16,24},{24,16},{1,9},{9,1},{17,25},{25,17},{2,10},{10... | collective-permute-start | bytes 1179656 | tf_op jit(solution)/shard_map/ppermute | solution.py:20
  119.6 5.6 %weight_grad.3 = (f32[3,512,2048]{2,1,0:T(8,128)}, f32[8,128]{1,0:T(8,128)S(1)}) custom-call(f32[3,512,2048]{2,1,0:T(8,128)} %get-tuple-element.106.refs_0_, f32[8,128]{1,0:T(8,128)S(1)} %get-tuple-element.107.refs_1_, bf16[384,1536]{1,0:T(8,128)(2,1)S(1)} %assemble.3.grad_ref.refs_0_.refs_2_, ...), custom_call_target="tpu_custom_call", output_to_operand_aliasing={{0}: (0, {})} | custom-call | flops 1 | bytes 1 | tf_op jit(solution)/shard_map/weight_grad/pallas_call | solution.py:471
  125.4 2.2 %collective-permute-start.36 = (bf16[384,512]{1,0:T(8,128)(2,1)S(1)}, bf16[384,512]{1,0:T(8,128)(2,1)S(1)}, u32[]{:S(2)}, u32[]{:S(2)}) collective-permute-start(bf16[384,512]{1,0:T(8,128)(2,1)S(1)} %add_convert_fusion), channel_id=1, source_target_pairs={{0,8},{8,0},{16,24},{24,16},{1,9},{9,1},{17,25},{25,17},{2,10},{10... | collective-permute-start | bytes 1179656 | tf_op jit(solution)/shard_map/ppermute | solution.py:20
  127.6 1.4 join.1
  129.0 5.6 %collective-permute-done.36 = bf16[384,512]{1,0:T(8,128)(2,1)S(1)} collective-permute-done((bf16[384,512]{1,0:T(8,128)(2,1)S(1)}, bf16[384,512]{1,0:T(8,128)(2,1)S(1)}, u32[]{:S(2)}, u32[]{:S(2)}) %collective-permute-start.36) | collective-permute-done | bytes 393248 | tf_op jit(solution)/shard_map/ppermute | solution.py:20
  134.7 1.3 pad_maximum_fusion
  (60 shorter events, 3.0 us)
Async XLA Ops:
  1.7 15.0 %collective-permute-start = (bf16[128,2048]{1,0:T(8,128)(2,1)S(1)}, bf16[128,2048]{1,0:T(8,128)(2,1)S(1)}, u32[]{:S(2)}, u32[]{:S(2)}) collective-permute-start(bf16[128,2048]{1,0:T(8,128)(2,1)S(1)} %constant_dynamic-slice_fusion), channel_id=1, source_target_pairs={{0,4},{4,0},{1,5},{5,1},{2,6},{6,2},{3,7},{7,3},{8,12},{12,8},{9,1... | collective-permute-start | bytes 1572872 | tf_op jit(solution)/shard_map/ppermute | solution.py:20
  4.8 0.9 copy-start.4
  6.4 10.2 %collective-permute-start.3 = (bf16[2,96,128]{2,1,0:T(8,128)(2,1)S(1)}, bf16[2,96,128]{2,1,0:T(8,128)(2,1)S(1)}, u32[]{:S(2)}, u32[]{:S(2)}) collective-permute-start(bf16[2,96,128]{2,1,0:T(8,128)(2,1)S(1)} %get-tuple-element.72), channel_id=1, source_target_pairs={{0,1},{1,0},{2,3},{3,2},{4,5},{5,4},{6,7},{7,6},{8,9},{9,8},{10,11... | collective-permute-start | bytes 147464 | tf_op jit(solution)/shard_map/ppermute | solution.py:20
  6.5 10.1 %collective-permute-start.4 = (bf16[2,96,128]{2,1,0:T(8,128)(2,1)S(1)}, bf16[2,96,128]{2,1,0:T(8,128)(2,1)S(1)}, u32[]{:S(2)}, u32[]{:S(2)}) collective-permute-start(bf16[2,96,128]{2,1,0:T(8,128)(2,1)S(1)} %get-tuple-element.73), channel_id=1, source_target_pairs={{0,2},{1,3},{2,0},{3,1},{4,6},{5,7},{6,4},{7,5},{8,10},{9,11},{10,... | collective-permute-start | bytes 147464 | tf_op jit(solution)/shard_map/ppermute | solution.py:20
  8.0 8.6 %collective-permute-start.5 = (bf16[2,96,128]{2,1,0:T(8,128)(2,1)S(1)}, bf16[2,96,128]{2,1,0:T(8,128)(2,1)S(1)}, u32[]{:S(2)}, u32[]{:S(2)}) collective-permute-start(bf16[2,96,128]{2,1,0:T(8,128)(2,1)S(1)} %get-tuple-element.74), channel_id=1, source_target_pairs={{0,3},{1,2},{2,1},{3,0},{4,7},{5,6},{6,5},{7,4},{8,11},{9,10},{10,... | collective-permute-start | bytes 147464 | tf_op jit(solution)/shard_map/ppermute | solution.py:20
  8.3 2.8 %copy-start = (bf16[512,3,2048]{2,0,1:T(8,128)(2,1)S(1)}, bf16[512,3,2048]{2,0,1:T(8,128)(2,1)}, u32[]{:S(2)}) copy-start(bf16[512,3,2048]{2,0,1:T(8,128)(2,1)} %param.5) | copy-start | bytes 18874372
  11.1 1.4 %copy-start.2 = (bf16[384,2048]{1,0:T(8,128)(2,1)S(1)}, bf16[384,2048]{1,0:T(8,128)(2,1)}, u32[]{:S(2)}) copy-start(bf16[384,2048]{1,0:T(8,128)(2,1)} %refs_4_.1) | copy-start | bytes 4718596
  12.5 7.6 %copy-start.1 = (bf16[512,3,2048]{2,0,1:T(8,128)(2,1)S(1)}, bf16[512,3,2048]{2,0,1:T(8,128)(2,1)}, u32[]{:S(2)}) copy-start(bf16[512,3,2048]{2,0,1:T(8,128)(2,1)} %param.5) | copy-start | bytes 18874372
  16.7 3.3 %collective-permute-start.6 = (bf16[2,3,384,128]{3,2,1,0:T(8,128)(2,1)S(1)}, bf16[2,3,384,128]{3,2,1,0:T(8,128)(2,1)S(1)}, u32[]{:S(2)}, u32[]{:S(2)}) collective-permute-start(bf16[2,3,384,128]{3,2,1,0:T(8,128)(2,1)S(1)} %get-tuple-element.75), channel_id=1, source_target_pairs={{0,1},{1,0},{2,3},{3,2},{4,5},{5,4},{6,7},{7,6},{8,9},{9,8},{10,11... | collective-permute-start | bytes 1769480 | tf_op jit(solution)/shard_map/ppermute | solution.py:20
  17.0 14.0 %collective-permute-start.2 = (bf16[128,2048]{1,0:T(8,128)(2,1)S(1)}, bf16[128,2048]{1,0:T(8,128)(2,1)S(1)}, u32[]{:S(2)}, u32[]{:S(2)}) collective-permute-start(bf16[128,2048]{1,0:T(8,128)(2,1)S(1)} %get-tuple-element.69), channel_id=1, source_target_pairs={{0,4},{4,0},{1,5},{5,1},{2,6},{6,2},{3,7},{7,3},{8,12},{12,8},{9,1... | collective-permute-start | bytes 1572872 | tf_op jit(solution)/shard_map/ppermute | solution.py:20
  18.4 14.3 %collective-permute-start.1 = (bf16[128,2048]{1,0:T(8,128)(2,1)S(1)}, bf16[128,2048]{1,0:T(8,128)(2,1)S(1)}, u32[]{:S(2)}, u32[]{:S(2)}) collective-permute-start(bf16[128,2048]{1,0:T(8,128)(2,1)S(1)} %collective-permute-done.refs_0_), channel_id=1, source_target_pairs={{0,8},{8,0},{16,24},{24,16},{1,9},{9,1},{17,25},{25,17},{2,10},{10... | collective-permute-start | bytes 1572872 | tf_op jit(solution)/shard_map/ppermute | solution.py:20
  23.3 1.6 %collective-permute-start.8 = (bf16[2,3,128,128]{3,2,1,0:T(8,128)(2,1)S(1)}, bf16[2,3,128,128]{3,2,1,0:T(8,128)(2,1)S(1)}, u32[]{:S(2)}, u32[]{:S(2)}) collective-permute-start(bf16[2,3,128,128]{3,2,1,0:T(8,128)(2,1)S(1)} %get-tuple-element.78), channel_id=1, source_target_pairs={{0,1},{1,0},{2,3},{3,2},{4,5},{5,4},{6,7},{7,6},{8,9},{9,8},{10,11... | collective-permute-start | bytes 589832 | tf_op jit(solution)/shard_map/ppermute | solution.py:20
  23.4 9.4 %collective-permute-start.7 = (bf16[1,3,384,128]{3,2,1,0:T(8,128)(2,1)S(1)}, bf16[1,3,384,128]{3,2,1,0:T(8,128)(2,1)S(1)}, u32[]{:S(2)}, u32[]{:S(2)}) collective-permute-start(bf16[1,3,384,128]{3,2,1,0:T(8,128)(2,1)S(1)} %add_convert_fusion.12), channel_id=1, source_target_pairs={{0,2},{1,3},{2,0},{3,1},{4,6},{5,7},{6,4},{7,5},{8,10},{9,11},{10,... | collective-permute-start | bytes 884744 | tf_op jit(solution)/shard_map/ppermute | solution.py:20
  24.9 23.0 %copy-start.5 = (f32[7,64]{1,0:T(8,128)S(1)}, f32[7,64]{1,0:T(8,128)}, u32[]{:S(2)}) copy-start(f32[7,64]{1,0:T(8,128)} %taps_ref.1) | copy-start | bytes 5380
  35.9 1.8 %collective-permute-start.9 = (bf16[2,3,256,128]{3,2,1,0:T(8,128)(2,1)S(1)}, bf16[2,3,256,128]{3,2,1,0:T(8,128)(2,1)S(1)}, u32[]{:S(2)}, u32[]{:S(2)}) collective-permute-start(bf16[2,3,256,128]{3,2,1,0:T(8,128)(2,1)S(1)} %get-tuple-element.81), channel_id=1, source_target_pairs={{0,1},{1,0},{2,3},{3,2},{4,5},{5,4},{6,7},{7,6},{8,9},{9,8},{10,11... | collective-permute-start | bytes 1179656 | tf_op jit(solution)/shard_map/ppermute | solution.py:20
  36.0 5.2 %collective-permute-start.11 = (bf16[1,3,128,128]{3,2,1,0:T(8,128)(2,1)S(1)}, bf16[1,3,128,128]{3,2,1,0:T(8,128)(2,1)S(1)}, u32[]{:S(2)}, u32[]{:S(2)}) collective-permute-start(bf16[1,3,128,128]{3,2,1,0:T(8,128)(2,1)S(1)} %add_convert_fusion.14), channel_id=1, source_target_pairs={{0,2},{1,3},{2,0},{3,1},{4,6},{5,7},{6,4},{7,5},{8,10},{9,11},{10,... | collective-permute-start | bytes 294920 | tf_op jit(solution)/shard_map/ppermute | solution.py:20
  41.2 6.7 %collective-permute-start.12 = (bf16[1,3,256,128]{3,2,1,0:T(8,128)(2,1)S(1)}, bf16[1,3,256,128]{3,2,1,0:T(8,128)(2,1)S(1)}, u32[]{:S(2)}, u32[]{:S(2)}) collective-permute-start(bf16[1,3,256,128]{3,2,1,0:T(8,128)(2,1)S(1)} %add_convert_fusion.13), channel_id=1, source_target_pairs={{0,2},{1,3},{2,0},{3,1},{4,6},{5,7},{6,4},{7,5},{8,10},{9,11},{10,... | collective-permute-start | bytes 589832 | tf_op jit(solution)/shard_map/ppermute | solution.py:20
  43.2 4.7 %collective-permute-start.10 = (bf16[384,128]{1,0:T(8,128)(2,1)S(1)}, bf16[384,128]{1,0:T(8,128)(2,1)S(1)}, u32[]{:S(2)}, u32[]{:S(2)}) collective-permute-start(bf16[384,128]{1,0:T(8,128)(2,1)S(1)} %get-tuple-element.84), channel_id=1, source_target_pairs={{0,4},{4,0},{1,5},{5,1},{2,6},{6,2},{3,7},{7,3},{8,12},{12,8},{9,1... | collective-permute-start | bytes 294920 | tf_op jit(solution)/shard_map/ppermute | solution.py:20
  49.5 6.5 %collective-permute-start.13 = (bf16[3,384,128]{2,1,0:T(8,128)(2,1)S(1)}, bf16[3,384,128]{2,1,0:T(8,128)(2,1)S(1)}, u32[]{:S(2)}, u32[]{:S(2)}) collective-permute-start(bf16[3,384,128]{2,1,0:T(8,128)(2,1)S(1)} %get-tuple-element.88.refs_0_), channel_id=1, source_target_pairs={{0,1},{1,0},{2,3},{3,2},{4,5},{5,4},{6,7},{7,6},{8,9},{9,8},{10,11... | collective-permute-start | bytes 884744 | tf_op jit(solution)/shard_map/ppermute | solution.py:20
  49.6 6.4 %collective-permute-start.16 = (bf16[3,384,128]{2,1,0:T(8,128)(2,1)S(1)}, bf16[3,384,128]{2,1,0:T(8,128)(2,1)S(1)}, u32[]{:S(2)}, u32[]{:S(2)}) collective-permute-start(bf16[3,384,128]{2,1,0:T(8,128)(2,1)S(1)} %get-tuple-element.87.refs_0_), channel_id=1, source_target_pairs={{0,1},{1,0},{2,3},{3,2},{4,5},{5,4},{6,7},{7,6},{8,9},{9,8},{10,11... | collective-permute-start | bytes 884744 | tf_op jit(solution)/shard_map/ppermute | solution.py:20
  50.1 9.0 %collective-permute-start.14 = (bf16[3,384,128]{2,1,0:T(8,128)(2,1)S(1)}, bf16[3,384,128]{2,1,0:T(8,128)(2,1)S(1)}, u32[]{:S(2)}, u32[]{:S(2)}) collective-permute-start(bf16[3,384,128]{2,1,0:T(8,128)(2,1)S(1)} %get-tuple-element.87.refs_0_), channel_id=1, source_target_pairs={{0,2},{1,3},{2,0},{3,1},{4,6},{5,7},{6,4},{7,5},{8,10},{9,11},{10,... | collective-permute-start | bytes 884744 | tf_op jit(solution)/shard_map/ppermute | solution.py:20
  51.3 4.7 %collective-permute-start.17 = (bf16[416,128]{1,0:T(8,128)(2,1)S(1)}, bf16[416,128]{1,0:T(8,128)(2,1)S(1)}, u32[]{:S(2)}, u32[]{:S(2)}) collective-permute-start(bf16[416,128]{1,0:T(8,128)(2,1)S(1)} %get-tuple-element.89), channel_id=1, source_target_pairs={{0,4},{4,0},{1,5},{5,1},{2,6},{6,2},{3,7},{7,3},{8,12},{12,8},{9,1... | collective-permute-start | bytes 319496 | tf_op jit(solution)/shard_map/ppermute | solution.py:20
  59.1 1.6 %collective-permute-start.18 = (bf16[3,384,128]{2,1,0:T(8,128)(2,1)S(1)}, bf16[3,384,128]{2,1,0:T(8,128)(2,1)S(1)}, u32[]{:S(2)}, u32[]{:S(2)}) collective-permute-start(bf16[3,384,128]{2,1,0:T(8,128)(2,1)S(1)} %collective-permute-done.14.refs_2_), channel_id=1, source_target_pairs={{0,1},{1,0},{2,3},{3,2},{4,5},{5,4},{6,7},{7,6},{8,9},{9,8},{10,11... | collective-permute-start | bytes 884744 | tf_op jit(solution)/shard_map/ppermute | solution.py:20
  59.1 9.4 %collective-permute-start.15 = (bf16[3,384,128]{2,1,0:T(8,128)(2,1)S(1)}, bf16[3,384,128]{2,1,0:T(8,128)(2,1)S(1)}, u32[]{:S(2)}, u32[]{:S(2)}) collective-permute-start(bf16[3,384,128]{2,1,0:T(8,128)(2,1)S(1)} %get-tuple-element.88.refs_0_), channel_id=1, source_target_pairs={{0,2},{1,3},{2,0},{3,1},{4,6},{5,7},{6,4},{7,5},{8,10},{9,11},{10,... | collective-permute-start | bytes 884744 | tf_op jit(solution)/shard_map/ppermute | solution.py:20
  62.2 12.0 %collective-permute-start.20 = (bf16[384,512]{1,0:T(8,128)(2,1)S(1)}, bf16[384,512]{1,0:T(8,128)(2,1)S(1)}, u32[]{:S(2)}, u32[]{:S(2)}) collective-permute-start(bf16[384,512]{1,0:T(8,128)(2,1)S(1)} %input_grad.4), channel_id=1, source_target_pairs={{0,4},{4,0},{1,5},{5,1},{2,6},{6,2},{3,7},{7,3},{8,12},{12,8},{9,1... | collective-permute-start | bytes 1179656 | tf_op jit(solution)/shard_map/ppermute | solution.py:20
  68.5 1.6 %collective-permute-start.19 = (bf16[3,384,128]{2,1,0:T(8,128)(2,1)S(1)}, bf16[3,384,128]{2,1,0:T(8,128)(2,1)S(1)}, u32[]{:S(2)}, u32[]{:S(2)}) collective-permute-start(bf16[3,384,128]{2,1,0:T(8,128)(2,1)S(1)} %collective-permute-done.15.refs_2_), channel_id=1, source_target_pairs={{0,1},{1,0},{2,3},{3,2},{4,5},{5,4},{6,7},{7,6},{8,9},{9,8},{10,11... | collective-permute-start | bytes 884744 | tf_op jit(solution)/shard_map/ppermute | solution.py:20
  68.5 14.1 %collective-permute-start.21 = (bf16[384,512]{1,0:T(8,128)(2,1)S(1)}, bf16[384,512]{1,0:T(8,128)(2,1)S(1)}, u32[]{:S(2)}, u32[]{:S(2)}) collective-permute-start(bf16[384,512]{1,0:T(8,128)(2,1)S(1)} %get-tuple-element.97), channel_id=1, source_target_pairs={{0,4},{4,0},{1,5},{5,1},{2,6},{6,2},{3,7},{7,3},{8,12},{12,8},{9,1... | collective-permute-start | bytes 1179656 | tf_op jit(solution)/shard_map/ppermute | solution.py:20
  74.3 12.4 %collective-permute-start.22 = (bf16[384,512]{1,0:T(8,128)(2,1)S(1)}, bf16[384,512]{1,0:T(8,128)(2,1)S(1)}, u32[]{:S(2)}, u32[]{:S(2)}) collective-permute-start(bf16[384,512]{1,0:T(8,128)(2,1)S(1)} %add_convert_fusion.11), channel_id=1, source_target_pairs={{0,8},{24,16},{1,9},{25,17},{2,10},{26,18},{3,11},{27,19},{4,12},{... | collective-permute-start | bytes 1179656 | tf_op jit(solution)/shard_map/ppermute | solution.py:598
  77.5 13.5 %collective-permute-start.23 = (bf16[384,512]{1,0:T(8,128)(2,1)S(1)}, bf16[384,512]{1,0:T(8,128)(2,1)S(1)}, u32[]{:S(2)}, u32[]{:S(2)}) collective-permute-start(bf16[384,512]{1,0:T(8,128)(2,1)S(1)} %get-tuple-element.101), channel_id=1, source_target_pairs={{0,4},{4,0},{1,5},{5,1},{2,6},{6,2},{3,7},{7,3},{8,12},{12,8},{9,1... | collective-permute-start | bytes 1179656 | tf_op jit(solution)/shard_map/ppermute | solution.py:20
  82.7 10.2 %collective-permute-start.24 = (bf16[384,512]{1,0:T(8,128)(2,1)S(1)}, bf16[384,512]{1,0:T(8,128)(2,1)S(1)}, u32[]{:S(2)}, u32[]{:S(2)}) collective-permute-start(bf16[384,512]{1,0:T(8,128)(2,1)S(1)} %add_convert_fusion.10), channel_id=1, source_target_pairs={{0,8},{24,16},{1,9},{25,17},{2,10},{26,18},{3,11},{27,19},{4,12},{... | collective-permute-start | bytes 1179656 | tf_op jit(solution)/shard_map/ppermute | solution.py:598
  85.9 18.5 %collective-permute-start.26 = (bf16[384,512]{1,0:T(8,128)(2,1)S(1)}, bf16[384,512]{1,0:T(8,128)(2,1)S(1)}, u32[]{:S(2)}, u32[]{:S(2)}) collective-permute-start(bf16[384,512]{1,0:T(8,128)(2,1)S(1)} %get-tuple-element.110), channel_id=1, source_target_pairs={{0,4},{4,0},{1,5},{5,1},{2,6},{6,2},{3,7},{7,3},{8,12},{12,8},{9,1... | collective-permute-start | bytes 1179656 | tf_op jit(solution)/shard_map/ppermute | solution.py:20
  86.8 6.2 %collective-permute-start.25 = (bf16[384,512]{1,0:T(8,128)(2,1)S(1)}, bf16[384,512]{1,0:T(8,128)(2,1)S(1)}, u32[]{:S(2)}, u32[]{:S(2)}) collective-permute-start(bf16[384,512]{1,0:T(8,128)(2,1)S(1)} %add_convert_fusion.9), channel_id=1, source_target_pairs={{0,0},{8,16},{16,8},{24,24},{1,1},{9,17},{17,9},{25,25},{2,2},{10,... | collective-permute-start | bytes 1179656 | tf_op jit(solution)/shard_map/ppermute | solution.py:603
  91.1 7.7 %copy-start.3 = (bf16[384,2048]{1,0:T(8,128)(2,1)S(1)}, bf16[384,2048]{1,0:T(8,128)(2,1)}, u32[]{:S(2)}) copy-start(bf16[384,2048]{1,0:T(8,128)(2,1)} %refs_4_.1) | copy-start | bytes 4718596
  93.2 11.3 %collective-permute-start.27 = (bf16[384,512]{1,0:T(8,128)(2,1)S(1)}, bf16[384,512]{1,0:T(8,128)(2,1)S(1)}, u32[]{:S(2)}, u32[]{:S(2)}) collective-permute-start(bf16[384,512]{1,0:T(8,128)(2,1)S(1)} %get-tuple-element.130), channel_id=1, source_target_pairs={{0,8},{8,0},{16,24},{24,16},{1,9},{9,1},{17,25},{25,17},{2,10},{10... | collective-permute-start | bytes 1179656 | tf_op jit(solution)/shard_map/ppermute | solution.py:20
  98.0 6.7 %collective-permute-start.28 = (bf16[384,512]{1,0:T(8,128)(2,1)S(1)}, bf16[384,512]{1,0:T(8,128)(2,1)S(1)}, u32[]{:S(2)}, u32[]{:S(2)}) collective-permute-start(bf16[384,512]{1,0:T(8,128)(2,1)S(1)} %add_convert_fusion.7), channel_id=1, source_target_pairs={{0,0},{8,16},{16,8},{24,24},{1,1},{9,17},{17,9},{25,25},{2,2},{10,... | collective-permute-start | bytes 1179656 | tf_op jit(solution)/shard_map/ppermute | solution.py:603
  104.9 8.8 %collective-permute-start.29 = (bf16[384,512]{1,0:T(8,128)(2,1)S(1)}, bf16[384,512]{1,0:T(8,128)(2,1)S(1)}, u32[]{:S(2)}, u32[]{:S(2)}) collective-permute-start(bf16[384,512]{1,0:T(8,128)(2,1)S(1)} %get-tuple-element.128), channel_id=1, source_target_pairs={{0,8},{8,0},{16,24},{24,16},{1,9},{9,1},{17,25},{25,17},{2,10},{10... | collective-permute-start | bytes 1179656 | tf_op jit(solution)/shard_map/ppermute | solution.py:20
  107.9 6.6 %collective-permute-start.30 = (bf16[384,512]{1,0:T(8,128)(2,1)S(1)}, bf16[384,512]{1,0:T(8,128)(2,1)S(1)}, u32[]{:S(2)}, u32[]{:S(2)}) collective-permute-start(bf16[384,512]{1,0:T(8,128)(2,1)S(1)} %add_convert_fusion.4), channel_id=1, source_target_pairs={{0,0},{8,16},{16,8},{24,24},{1,1},{9,17},{17,9},{25,25},{2,2},{10,... | collective-permute-start | bytes 1179656 | tf_op jit(solution)/shard_map/ppermute | solution.py:603
  109.2 16.1 %collective-permute-start.31 = (bf16[2,128,128]{2,1,0:T(8,128)(2,1)S(1)}, bf16[2,128,128]{2,1,0:T(8,128)(2,1)S(1)}, u32[]{:S(2)}, u32[]{:S(2)}) collective-permute-start(bf16[2,128,128]{2,1,0:T(8,128)(2,1)S(1)} %get-tuple-element.120), channel_id=1, source_target_pairs={{0,1},{1,0},{2,3},{3,2},{4,5},{5,4},{6,7},{7,6},{8,9},{9,8},{10,11... | collective-permute-start | bytes 196616 | tf_op jit(solution)/shard_map/ppermute | solution.py:20
  109.3 16.0 %collective-permute-start.32 = (bf16[2,128,128]{2,1,0:T(8,128)(2,1)S(1)}, bf16[2,128,128]{2,1,0:T(8,128)(2,1)S(1)}, u32[]{:S(2)}, u32[]{:S(2)}) collective-permute-start(bf16[2,128,128]{2,1,0:T(8,128)(2,1)S(1)} %get-tuple-element.121), channel_id=1, source_target_pairs={{0,2},{1,3},{2,0},{3,1},{4,6},{5,7},{6,4},{7,5},{8,10},{9,11},{10,... | collective-permute-start | bytes 196616 | tf_op jit(solution)/shard_map/ppermute | solution.py:20
  110.5 14.7 %collective-permute-start.33 = (bf16[2,128,128]{2,1,0:T(8,128)(2,1)S(1)}, bf16[2,128,128]{2,1,0:T(8,128)(2,1)S(1)}, u32[]{:S(2)}, u32[]{:S(2)}) collective-permute-start(bf16[2,128,128]{2,1,0:T(8,128)(2,1)S(1)} %get-tuple-element.122), channel_id=1, source_target_pairs={{0,3},{1,2},{2,1},{3,0},{4,7},{5,6},{6,5},{7,4},{8,11},{9,10},{10,... | collective-permute-start | bytes 196616 | tf_op jit(solution)/shard_map/ppermute | solution.py:20
  113.8 11.5 %collective-permute-start.34 = (bf16[384,512]{1,0:T(8,128)(2,1)S(1)}, bf16[384,512]{1,0:T(8,128)(2,1)S(1)}, u32[]{:S(2)}, u32[]{:S(2)}) collective-permute-start(bf16[384,512]{1,0:T(8,128)(2,1)S(1)} %add_convert_fusion.2), channel_id=1, source_target_pairs={{0,0},{8,16},{16,8},{24,24},{1,1},{9,17},{17,9},{25,25},{2,2},{10,... | collective-permute-start | bytes 1179656 | tf_op jit(solution)/shard_map/ppermute | solution.py:603
  114.6 14.4 %collective-permute-start.35 = (bf16[384,512]{1,0:T(8,128)(2,1)S(1)}, bf16[384,512]{1,0:T(8,128)(2,1)S(1)}, u32[]{:S(2)}, u32[]{:S(2)}) collective-permute-start(bf16[384,512]{1,0:T(8,128)(2,1)S(1)} %add_convert_fusion.1), channel_id=1, source_target_pairs={{0,8},{8,0},{16,24},{24,16},{1,9},{9,1},{17,25},{25,17},{2,10},{10... | collective-permute-start | bytes 1179656 | tf_op jit(solution)/shard_map/ppermute | solution.py:20
  125.4 9.3 %collective-permute-start.36 = (bf16[384,512]{1,0:T(8,128)(2,1)S(1)}, bf16[384,512]{1,0:T(8,128)(2,1)S(1)}, u32[]{:S(2)}, u32[]{:S(2)}) collective-permute-start(bf16[384,512]{1,0:T(8,128)(2,1)S(1)} %add_convert_fusion), channel_id=1, source_target_pairs={{0,8},{8,0},{16,24},{24,16},{1,9},{9,1},{17,25},{25,17},{2,10},{10... | collective-permute-start | bytes 1179656 | tf_op jit(solution)/shard_map/ppermute | solution.py:20

commit v17 on v15

--- a/solution.py
+++ b/solution.py
@@ -534,11 +534,11 @@
         other = swap(mine, "row", 1)
         rest = swap(after(last[0], mine), "col", k)
         keep, send = project(place, [after(mine, *pairs)], w, n_depth)
-        terms, ahead, ahead_fars = sum_over_depth(keep, send)
+        terms, ahead, _ = sum_over_depth(keep, send)
         pieces.append((k, ("own",)))
         parts.append(terms)
         keep, send, x = project(place, [mine, other, after(rest, *fars, *ahead)], w, n_depth, "join")
-        terms, pairs, fars = sum_over_depth(keep, send, (), ahead_fars)
+        terms, pairs, fars = sum_over_depth(keep, send)
         pieces.append((k, ("other", "last")))
         parts.append(terms)
         xs.append(x)
@@ -605,10 +605,10 @@
             marks = [own_part[1]]
             for k, parts_of in enumerate(held):
                 sent[k] += [swap(after(part, *marks), "col", k + 1) for part in parts_of]
-        if slot in (2, 3):
-            filled = weight_grad(filled, [after(lhs[0], *marks)] + lhs[1:], xs, slot - 2, 3, width)
+        if slot in (3, 4):
+            filled = weight_grad(filled, [after(lhs[0], *marks)] + lhs[1:], xs, slot - 3, 3, width)
             marks = [filled[1]]
-        if slot == 1:
+        if slot == 2:
             blocks = split_rows(place, [after(blocks[0], *marks)] + blocks[1:], n_depth)
             blocks = [block if r == 0 else swap(block, "depth", r) for r, block in enumerate(blocks)]
             late = blocks[1:]

time: 141 us -> 140 us (level)
  starting transfers between devices: 45.7 us -> 43 us
  waiting for transfers between devices: 49.3 us -> 51.4 us
    ppermute x33, starting transfers between devices: 42.8 us -> 40.1 us  [swap(): return lax.ppermute(value, axis, [(i, i ^ flip) for i in range(count)])]
    ppermute x33, waiting for transfers between devices: 49.3 us -> 51.3 us  [swap(): return lax.ppermute(value, axis, [(i, i ^ flip) for i in range(count)])]
where the time goes in v17:
time: 140 us
  waiting for transfers between devices  51.4 us (37%)
  starting transfers between devices  43 us (31%)
  Pallas kernels  35.1 us (25%)
  local copies, waits for them, and re-layouts  6.22 us (4%)
  other arithmetic  3.06 us (2%)
    ppermute x33, waiting for transfers between devices, swap(): return lax.ppermute(value, axis, [(i, i ^ flip) for i in range(count)])  51.3 us
    ppermute x33, starting transfers between devices, swap(): return lax.ppermute(value, axis, [(i, i ^ flip) for i in range(count)])  40.1 us
    pallas_call x2, Pallas kernels, weight_grad(): pl.pallas_call(functools.partial(weight_grad_kernel, chained=chained, gro...  11.2 us
    pallas_call x3, Pallas kernels, project(): pl.pallas_call(functools.partial(project_kernel, pieces=len(xs), mode=mod...  10.3 us
    pallas_call x4, Pallas kernels, input_grad(): pl.pallas_call(functools.partial(input_grad_kernel if single else input_g...  7.49 us
    unnamed x12, local copies, waits for them, and re-layouts  5.14 us
    ppermute x4, starting transfers between devices, on_device(): lax.ppermute(across[slot - 1], 'row', [(0, 0), (1, 2), (2, 1), (3, 3)])  2.9 us
  transfers between devices with their start and end apart: 37, of which 18 were waited for; matrix products, arithmetic and copies ran while one was open for 1% of the time, Pallas kernels for 22%

profile of v17, /device:TPU:0, one launch (start us, length us, event | category | flops | bytes accessed | tf_op | source)
XLA Modules:
  0.0 139.8 jit_solution(16506648650394606717)
XLA Ops:
  0.6 1.1 constant_dynamic-slice_fusion
  1.7 3.0 %collective-permute-start = (bf16[128,2048]{1,0:T(8,128)(2,1)S(1)}, bf16[128,2048]{1,0:T(8,128)(2,1)S(1)}, u32[]{:S(2)}, u32[]{:S(2)}) collective-permute-start(bf16[128,2048]{1,0:T(8,128)(2,1)S(1)} %constant_dynamic-slice_fusion), channel_id=1, source_target_pairs={{0,4},{4,0},{1,5},{5,1},{2,6},{6,2},{3,7},{7,3},{8,12},{12,8},{9,1... | collective-permute-start | bytes 1572872 | tf_op jit(solution)/shard_map/ppermute | solution.py:20
  4.9 0.9 copy-done.4
  5.8 0.6 split.2
  6.5 1.6 %collective-permute-start.4 = (bf16[2,96,128]{2,1,0:T(8,128)(2,1)S(1)}, bf16[2,96,128]{2,1,0:T(8,128)(2,1)S(1)}, u32[]{:S(2)}, u32[]{:S(2)}) collective-permute-start(bf16[2,96,128]{2,1,0:T(8,128)(2,1)S(1)} %get-tuple-element.72), channel_id=1, source_target_pairs={{0,2},{1,3},{2,0},{3,1},{4,6},{5,7},{6,4},{7,5},{8,10},{9,11},{10,... | collective-permute-start | bytes 147464 | tf_op jit(solution)/shard_map/ppermute | solution.py:20
  8.3 2.8 %copy-done = bf16[512,3,2048]{2,0,1:T(8,128)(2,1)S(1)} copy-done((bf16[512,3,2048]{2,0,1:T(8,128)(2,1)S(1)}, bf16[512,3,2048]{2,0,1:T(8,128)(2,1)}, u32[]{:S(2)}) %copy-start) | copy-done | bytes 6291480
  11.1 1.4 %copy-done.2 = bf16[384,2048]{1,0:T(8,128)(2,1)S(1)} copy-done((bf16[384,2048]{1,0:T(8,128)(2,1)S(1)}, bf16[384,2048]{1,0:T(8,128)(2,1)}, u32[]{:S(2)}) %copy-start.2) | copy-done | bytes 1572888
  12.5 4.1 %project.3 = (bf16[2,3,384,128]{3,2,1,0:T(8,128)(2,1)S(1)}, bf16[2,3,384,128]{3,2,1,0:T(8,128)(2,1)S(1)}, bf16[128,2048]{1,0:T(8,128)(2,1)S(1)}) custom-call(s32[4]{0:T(128)S(1)} %pad_add_fusion.place, bf16[384,2048]{1,0:T(8,128)(2,1)S(1)} %copy-done.2, bf16[3,512,2048]{2,1,0:T(8,128)(2,1)S(1)} %bitcast.6), custom_call_target="tpu_custom_call" | custom-call | flops 1 | bytes 1 | tf_op jit(solution)/shard_map/project/pallas_call | solution.py:97
  17.0 1.4 collective-permute-start.2
  18.4 1.6 %collective-permute-start.1 = (bf16[128,2048]{1,0:T(8,128)(2,1)S(1)}, bf16[128,2048]{1,0:T(8,128)(2,1)S(1)}, u32[]{:S(2)}, u32[]{:S(2)}) collective-permute-start(bf16[128,2048]{1,0:T(8,128)(2,1)S(1)} %collective-permute-done.refs_0_), channel_id=1, source_target_pairs={{0,8},{8,0},{16,24},{24,16},{1,9},{9,1},{17,25},{25,17},{2,10},{10... | collective-permute-start | bytes 1572872 | tf_op jit(solution)/shard_map/ppermute | solution.py:20
  20.1 3.1 %project.4 = (bf16[2,3,128,128]{3,2,1,0:T(8,128)(2,1)S(1)}, bf16[2,3,128,128]{3,2,1,0:T(8,128)(2,1)S(1)}) custom-call(s32[4]{0:T(128)S(1)} %pad_add_fusion.place, bf16[128,2048]{1,0:T(8,128)(2,1)S(1)} %collective-permute-done.refs_0_, bf16[3,512,2048]{2,1,0:T(8,128)(2,1)S(1)} %bitcast.7), custom_call_target="tpu_custom_call" | custom-call | flops 1 | bytes 1 | tf_op jit(solution)/shard_map/project/pallas_call | solution.py:97
  23.4 1.6 %collective-permute-start.7 = (bf16[1,3,384,128]{3,2,1,0:T(8,128)(2,1)S(1)}, bf16[1,3,384,128]{3,2,1,0:T(8,128)(2,1)S(1)}, u32[]{:S(2)}, u32[]{:S(2)}) collective-permute-start(bf16[1,3,384,128]{3,2,1,0:T(8,128)(2,1)S(1)} %add_convert_fusion.12), channel_id=1, source_target_pairs={{0,2},{1,3},{2,0},{3,1},{4,6},{5,7},{6,4},{7,5},{8,10},{9,11},{10,... | collective-permute-start | bytes 884744 | tf_op jit(solution)/shard_map/ppermute | solution.py:20
  25.0 6.1 %collective-permute-done.2.refs_2_ = bf16[128,2048]{1,0:T(8,128)(2,1)S(1)} collective-permute-done((bf16[128,2048]{1,0:T(8,128)(2,1)S(1)}, bf16[128,2048]{1,0:T(8,128)(2,1)S(1)}, u32[]{:S(2)}, u32[]{:S(2)}) %collective-permute-start.2) | collective-permute-done | bytes 524320 | tf_op jit(solution)/shard_map/ppermute | solution.py:20
  31.0 1.7 %collective-permute-done.7.refs_4_ = bf16[1,3,384,128]{3,2,1,0:T(8,128)(2,1)S(1)} collective-permute-done((bf16[1,3,384,128]{3,2,1,0:T(8,128)(2,1)S(1)}, bf16[1,3,384,128]{3,2,1,0:T(8,128)(2,1)S(1)}, u32[]{:S(2)}, u32[]{:S(2)}) %collective-permute-start.7) | collective-permute-done | bytes 294944 | tf_op jit(solution)/shard_map/ppermute | solution.py:20
  32.8 3.1 %project.5 = (bf16[2,3,256,128]{3,2,1,0:T(8,128)(2,1)S(1)}, bf16[2,3,256,128]{3,2,1,0:T(8,128)(2,1)S(1)}, bf16[384,2048]{1,0:T(8,128)(2,1)S(1)}) custom-call(s32[4]{0:T(128)S(1)} %pad_add_fusion.place, bf16[128,2048]{1,0:T(8,128)(2,1)S(1)} %collective-permute-done.refs_0_, bf16[128,2048]{1,0:T(8,128)(2,1)S(1)} %collective-permute-done.1.refs_1_, ...), custom_call_target="tpu_custom_call" | custom-call | flops 1 | bytes 1 | tf_op jit(solution)/shard_map/project/pallas_call | solution.py:97
  36.0 1.7 %collective-permute-done.9.refs_9_ = bf16[2,3,256,128]{3,2,1,0:T(8,128)(2,1)S(1)} collective-permute-done((bf16[2,3,256,128]{3,2,1,0:T(8,128)(2,1)S(1)}, bf16[2,3,256,128]{3,2,1,0:T(8,128)(2,1)S(1)}, u32[]{:S(2)}, u32[]{:S(2)}) %collective-permute-start.9) | collective-permute-done | bytes 393248 | tf_op jit(solution)/shard_map/ppermute | solution.py:20
  37.7 1.6 %collective-permute-start.12 = (bf16[1,3,256,128]{3,2,1,0:T(8,128)(2,1)S(1)}, bf16[1,3,256,128]{3,2,1,0:T(8,128)(2,1)S(1)}, u32[]{:S(2)}, u32[]{:S(2)}) collective-permute-start(bf16[1,3,256,128]{3,2,1,0:T(8,128)(2,1)S(1)} %add_convert_fusion.13), channel_id=1, source_target_pairs={{0,2},{1,3},{2,0},{3,1},{4,6},{5,7},{6,4},{7,5},{8,10},{9,11},{10,... | collective-permute-start | bytes 589832 | tf_op jit(solution)/shard_map/ppermute | solution.py:20
  39.3 0.5 collective-permute-start.11
  39.8 0.6 merge.1
  40.4 0.7 collective-permute-start.10
  41.1 5.7 %collective-permute-done.11.refs_7_ = bf16[1,3,128,128]{3,2,1,0:T(8,128)(2,1)S(1)} collective-permute-done((bf16[1,3,128,128]{3,2,1,0:T(8,128)(2,1)S(1)}, bf16[1,3,128,128]{3,2,1,0:T(8,128)(2,1)S(1)}, u32[]{:S(2)}, u32[]{:S(2)}) %collective-permute-start.11) | collective-permute-done | bytes 98336 | tf_op jit(solution)/shard_map/ppermute | solution.py:20
  46.9 1.6 %middle.1 = (bf16[3,384,128]{2,1,0:T(8,128)(2,1)S(1)}, bf16[3,384,128]{2,1,0:T(8,128)(2,1)S(1)}, bf16[416,128]{1,0:T(8,128)(2,1)S(1)}, bf16[416,128]{1,0:T(8,128)(2,1)S(1)}) custom-call(s32[4]{0:T(128)S(1)} %pad_add_fusion.place, f32[7,64]{1,0:T(8,128)S(1)} %copy-done.5, bf16[384,128]{1,0:T(8,128)(2,1)S(1)} %get-tuple-element.82.refs_0_, ...), custom_call_target="tpu_custom_call" | custom-call | flops 1 | bytes 1 | tf_op jit(solution)/shard_map/middle/pallas_call | solution.py:326
  48.5 0.5 collective-permute-start.16
  49.0 1.5 %collective-permute-start.14 = (bf16[3,384,128]{2,1,0:T(8,128)(2,1)S(1)}, bf16[3,384,128]{2,1,0:T(8,128)(2,1)S(1)}, u32[]{:S(2)}, u32[]{:S(2)}) collective-permute-start(bf16[3,384,128]{2,1,0:T(8,128)(2,1)S(1)} %get-tuple-element.85.refs_0_), channel_id=1, source_target_pairs={{0,2},{1,3},{2,0},{3,1},{4,6},{5,7},{6,4},{7,5},{8,10},{9,11},{10,... | collective-permute-start | bytes 884744 | tf_op jit(solution)/shard_map/ppermute | solution.py:20
  50.5 0.7 collective-permute-start.17
  51.2 4.1 %collective-permute-done.17.refs_1_ = bf16[416,128]{1,0:T(8,128)(2,1)S(1)} collective-permute-done((bf16[416,128]{1,0:T(8,128)(2,1)S(1)}, bf16[416,128]{1,0:T(8,128)(2,1)S(1)}, u32[]{:S(2)}, u32[]{:S(2)}) %collective-permute-start.17) | collective-permute-done | bytes 106528 | tf_op jit(solution)/shard_map/ppermute | solution.py:20
  55.2 2.8 %collective-permute-done.14.refs_2_ = bf16[3,384,128]{2,1,0:T(8,128)(2,1)S(1)} collective-permute-done((bf16[3,384,128]{2,1,0:T(8,128)(2,1)S(1)}, bf16[3,384,128]{2,1,0:T(8,128)(2,1)S(1)}, u32[]{:S(2)}, u32[]{:S(2)}) %collective-permute-start.14) | collective-permute-done | bytes 294944 | tf_op jit(solution)/shard_map/ppermute | solution.py:20
  58.0 1.5 %collective-permute-start.15 = (bf16[3,384,128]{2,1,0:T(8,128)(2,1)S(1)}, bf16[3,384,128]{2,1,0:T(8,128)(2,1)S(1)}, u32[]{:S(2)}, u32[]{:S(2)}) collective-permute-start(bf16[3,384,128]{2,1,0:T(8,128)(2,1)S(1)} %get-tuple-element.86.refs_0_), channel_id=1, source_target_pairs={{0,2},{1,3},{2,0},{3,1},{4,6},{5,7},{6,4},{7,5},{8,10},{9,11},{10,... | collective-permute-start | bytes 884744 | tf_op jit(solution)/shard_map/ppermute | solution.py:20
  59.6 0.7 assemble.2.grad_ref.refs_1_.refs_3_
  60.3 0.8 input_grad.4
  61.1 0.7 collective-permute-start.20
  61.8 3.0 %input_grad.5 = (bf16[384,512]{1,0:T(8,128)(2,1)S(1)}, bf16[384,512]{1,0:T(8,128)(2,1)S(1)}, bf16[384,512]{1,0:T(8,128)(2,1)S(1)}) custom-call(bf16[384,1536]{1,0:T(8,128)(2,1)S(1)} %assemble.2.grad_ref.refs_1_.refs_3_, bf16[3,512,2048]{2,1,0:T(8,128)(2,1)S(1)} %bitcast.10), custom_call_target="tpu_custom_call" | custom-call | flops 1 | bytes 1 | tf_op jit(solution)/shard_map/input_grad/pallas_call | solution.py:414
  64.8 2.6 %collective-permute-done.15.refs_2_ = bf16[3,384,128]{2,1,0:T(8,128)(2,1)S(1)} collective-permute-done((bf16[3,384,128]{2,1,0:T(8,128)(2,1)S(1)}, bf16[3,384,128]{2,1,0:T(8,128)(2,1)S(1)}, u32[]{:S(2)}, u32[]{:S(2)}) %collective-permute-start.15) | collective-permute-done | bytes 294944 | tf_op jit(solution)/shard_map/ppermute | solution.py:20
  67.4 0.7 collective-permute-start.21
  68.1 0.9 collective-permute-done.19.refs_3_
  69.0 0.7 assemble.3.grad_ref.refs_0_.refs_2_
  69.8 0.8 input_grad.6
  70.6 2.6 %collective-permute-done.20 = bf16[384,512]{1,0:T(8,128)(2,1)S(1)} collective-permute-done((bf16[384,512]{1,0:T(8,128)(2,1)S(1)}, bf16[384,512]{1,0:T(8,128)(2,1)S(1)}, u32[]{:S(2)}, u32[]{:S(2)}) %collective-permute-start.20) | collective-permute-done | bytes 393248 | tf_op jit(solution)/shard_map/ppermute | solution.py:20
  73.2 1.4 collective-permute-start.22
  74.6 0.7 collective-permute-start.23
  75.3 3.0 %input_grad.7 = (bf16[384,512]{1,0:T(8,128)(2,1)S(1)}, bf16[384,512]{1,0:T(8,128)(2,1)S(1)}, bf16[384,512]{1,0:T(8,128)(2,1)S(1)}) custom-call(bf16[384,1536]{1,0:T(8,128)(2,1)S(1)} %assemble.3.grad_ref.refs_0_.refs_2_, bf16[3,512,2048]{2,1,0:T(8,128)(2,1)S(1)} %bitcast.12), custom_call_target="tpu_custom_call" | custom-call | flops 1 | bytes 1 | tf_op jit(solution)/shard_map/input_grad/pallas_call | solution.py:414
  78.3 3.3 %collective-permute-done.21 = bf16[384,512]{1,0:T(8,128)(2,1)S(1)} collective-permute-done((bf16[384,512]{1,0:T(8,128)(2,1)S(1)}, bf16[384,512]{1,0:T(8,128)(2,1)S(1)}, u32[]{:S(2)}, u32[]{:S(2)}) %collective-permute-start.21) | collective-permute-done | bytes 393248 | tf_op jit(solution)/shard_map/ppermute | solution.py:20
  81.7 1.4 collective-permute-start.24
  83.0 0.7 collective-permute-start.26
  83.8 0.7 collective-permute-start.25
  84.5 5.5 %collective-permute-done.23 = bf16[384,512]{1,0:T(8,128)(2,1)S(1)} collective-permute-done((bf16[384,512]{1,0:T(8,128)(2,1)S(1)}, bf16[384,512]{1,0:T(8,128)(2,1)S(1)}, u32[]{:S(2)}, u32[]{:S(2)}) %collective-permute-start.23) | collective-permute-done | bytes 393248 | tf_op jit(solution)/shard_map/ppermute | solution.py:20
  90.1 1.2 collective-permute-done.24
  91.6 4.8 %collective-permute-start.30 = (bf16[384,512]{1,0:T(8,128)(2,1)S(1)}, bf16[384,512]{1,0:T(8,128)(2,1)S(1)}, u32[]{:S(2)}, u32[]{:S(2)}) collective-permute-start(bf16[384,512]{1,0:T(8,128)(2,1)S(1)} %get-tuple-element.128), channel_id=1, source_target_pairs={{0,8},{8,0},{16,24},{24,16},{1,9},{9,1},{17,25},{25,17},{2,10},{10... | collective-permute-start | bytes 1179656 | tf_op jit(solution)/shard_map/ppermute | solution.py:20
  96.3 0.7 collective-permute-start.31
  97.0 0.6 split.3
  97.7 1.6 %collective-permute-start.28 = (bf16[2,128,128]{2,1,0:T(8,128)(2,1)S(1)}, bf16[2,128,128]{2,1,0:T(8,128)(2,1)S(1)}, u32[]{:S(2)}, u32[]{:S(2)}) collective-permute-start(bf16[2,128,128]{2,1,0:T(8,128)(2,1)S(1)} %get-tuple-element.108), channel_id=1, source_target_pairs={{0,2},{1,3},{2,0},{3,1},{4,6},{5,7},{6,4},{7,5},{8,10},{9,11},{10,... | collective-permute-start | bytes 196616 | tf_op jit(solution)/shard_map/ppermute | solution.py:20
  99.7 2.5 %collective-permute-done.28.refs_2_ = bf16[2,128,128]{2,1,0:T(8,128)(2,1)S(1)} collective-permute-done((bf16[2,128,128]{2,1,0:T(8,128)(2,1)S(1)}, bf16[2,128,128]{2,1,0:T(8,128)(2,1)S(1)}, u32[]{:S(2)}, u32[]{:S(2)}) %collective-permute-start.28) | collective-permute-done | bytes 65568 | tf_op jit(solution)/shard_map/ppermute | solution.py:20
  102.2 1.1 collective-permute-done.29.refs_3_
  103.6 3.2 %collective-permute-start.32 = (bf16[384,512]{1,0:T(8,128)(2,1)S(1)}, bf16[384,512]{1,0:T(8,128)(2,1)S(1)}, u32[]{:S(2)}, u32[]{:S(2)}) collective-permute-start(bf16[384,512]{1,0:T(8,128)(2,1)S(1)} %get-tuple-element.126), channel_id=1, source_target_pairs={{0,8},{8,0},{16,24},{24,16},{1,9},{9,1},{17,25},{25,17},{2,10},{10... | collective-permute-start | bytes 1179656 | tf_op jit(solution)/shard_map/ppermute | solution.py:20
  106.8 0.9 collective-permute-start.33
  107.7 5.6 %weight_grad.2 = (f32[3,512,2048]{2,1,0:T(8,128)}, f32[8,128]{1,0:T(8,128)S(1)}) custom-call(bf16[384,1536]{1,0:T(8,128)(2,1)S(1)} %assemble.3.grad_ref.refs_0_.refs_2_, bf16[384,1536]{1,0:T(8,128)(2,1)S(1)} %assemble.2.grad_ref.refs_1_.refs_3_, bf16[384,2048]{1,0:T(8,128)(2,1)S(1)} %copy-done.3, bf16[384,2048]{1,0:T(8,128)(2,1)S(1)} %get-tuple-element.113.refs_3_.refs_5_), custom_call_target="tpu_custom_call" | custom-call | flops 1 | bytes 1 | tf_op jit(solution)/shard_map/weight_grad/pallas_call | solution.py:471
  113.3 3.0 %collective-permute-done.32 = bf16[384,512]{1,0:T(8,128)(2,1)S(1)} collective-permute-done((bf16[384,512]{1,0:T(8,128)(2,1)S(1)}, bf16[384,512]{1,0:T(8,128)(2,1)S(1)}, u32[]{:S(2)}, u32[]{:S(2)}) %collective-permute-start.32) | collective-permute-done | bytes 393248 | tf_op jit(solution)/shard_map/ppermute | solution.py:20
  116.4 0.7 collective-permute-start.34
  117.3 3.3 %collective-permute-start.35 = (bf16[384,512]{1,0:T(8,128)(2,1)S(1)}, bf16[384,512]{1,0:T(8,128)(2,1)S(1)}, u32[]{:S(2)}, u32[]{:S(2)}) collective-permute-start(bf16[384,512]{1,0:T(8,128)(2,1)S(1)} %add_convert_fusion.1), channel_id=1, source_target_pairs={{0,8},{8,0},{16,24},{24,16},{1,9},{9,1},{17,25},{25,17},{2,10},{10... | collective-permute-start | bytes 1179656 | tf_op jit(solution)/shard_map/ppermute | solution.py:20
  120.6 5.6 %weight_grad.3 = (f32[3,512,2048]{2,1,0:T(8,128)}, f32[8,128]{1,0:T(8,128)S(1)}) custom-call(f32[3,512,2048]{2,1,0:T(8,128)} %get-tuple-element.114.refs_0_, f32[8,128]{1,0:T(8,128)S(1)} %get-tuple-element.115.refs_1_, bf16[384,1536]{1,0:T(8,128)(2,1)S(1)} %assemble.3.grad_ref.refs_0_.refs_2_, ...), custom_call_target="tpu_custom_call", output_to_operand_aliasing={{0}: (0, {})} | custom-call | flops 1 | bytes 1 | tf_op jit(solution)/shard_map/weight_grad/pallas_call | solution.py:471
  126.3 4.3 %collective-permute-start.36 = (bf16[384,512]{1,0:T(8,128)(2,1)S(1)}, bf16[384,512]{1,0:T(8,128)(2,1)S(1)}, u32[]{:S(2)}, u32[]{:S(2)}) collective-permute-start(bf16[384,512]{1,0:T(8,128)(2,1)S(1)} %add_convert_fusion), channel_id=1, source_target_pairs={{0,8},{8,0},{16,24},{24,16},{1,9},{9,1},{17,25},{25,17},{2,10},{10... | collective-permute-start | bytes 1179656 | tf_op jit(solution)/shard_map/ppermute | solution.py:20
  130.7 1.4 join.1
  132.1 6.3 %collective-permute-done.36 = bf16[384,512]{1,0:T(8,128)(2,1)S(1)} collective-permute-done((bf16[384,512]{1,0:T(8,128)(2,1)S(1)}, bf16[384,512]{1,0:T(8,128)(2,1)S(1)}, u32[]{:S(2)}, u32[]{:S(2)}) %collective-permute-start.36) | collective-permute-done | bytes 393248 | tf_op jit(solution)/shard_map/ppermute | solution.py:20
  138.5 1.3 pad_maximum_fusion
  (60 shorter events, 3.3 us)
Async XLA Ops:
  1.7 15.0 %collective-permute-start = (bf16[128,2048]{1,0:T(8,128)(2,1)S(1)}, bf16[128,2048]{1,0:T(8,128)(2,1)S(1)}, u32[]{:S(2)}, u32[]{:S(2)}) collective-permute-start(bf16[128,2048]{1,0:T(8,128)(2,1)S(1)} %constant_dynamic-slice_fusion), channel_id=1, source_target_pairs={{0,4},{4,0},{1,5},{5,1},{2,6},{6,2},{3,7},{7,3},{8,12},{12,8},{9,1... | collective-permute-start | bytes 1572872 | tf_op jit(solution)/shard_map/ppermute | solution.py:20
  4.8 0.9 copy-start.4
  6.4 10.2 %collective-permute-start.3 = (bf16[2,96,128]{2,1,0:T(8,128)(2,1)S(1)}, bf16[2,96,128]{2,1,0:T(8,128)(2,1)S(1)}, u32[]{:S(2)}, u32[]{:S(2)}) collective-permute-start(bf16[2,96,128]{2,1,0:T(8,128)(2,1)S(1)} %get-tuple-element.71), channel_id=1, source_target_pairs={{0,1},{1,0},{2,3},{3,2},{4,5},{5,4},{6,7},{7,6},{8,9},{9,8},{10,11... | collective-permute-start | bytes 147464 | tf_op jit(solution)/shard_map/ppermute | solution.py:20
  6.5 10.1 %collective-permute-start.4 = (bf16[2,96,128]{2,1,0:T(8,128)(2,1)S(1)}, bf16[2,96,128]{2,1,0:T(8,128)(2,1)S(1)}, u32[]{:S(2)}, u32[]{:S(2)}) collective-permute-start(bf16[2,96,128]{2,1,0:T(8,128)(2,1)S(1)} %get-tuple-element.72), channel_id=1, source_target_pairs={{0,2},{1,3},{2,0},{3,1},{4,6},{5,7},{6,4},{7,5},{8,10},{9,11},{10,... | collective-permute-start | bytes 147464 | tf_op jit(solution)/shard_map/ppermute | solution.py:20
  8.0 8.6 %collective-permute-start.5 = (bf16[2,96,128]{2,1,0:T(8,128)(2,1)S(1)}, bf16[2,96,128]{2,1,0:T(8,128)(2,1)S(1)}, u32[]{:S(2)}, u32[]{:S(2)}) collective-permute-start(bf16[2,96,128]{2,1,0:T(8,128)(2,1)S(1)} %get-tuple-element.73), channel_id=1, source_target_pairs={{0,3},{1,2},{2,1},{3,0},{4,7},{5,6},{6,5},{7,4},{8,11},{9,10},{10,... | collective-permute-start | bytes 147464 | tf_op jit(solution)/shard_map/ppermute | solution.py:20
  8.3 2.8 %copy-start = (bf16[512,3,2048]{2,0,1:T(8,128)(2,1)S(1)}, bf16[512,3,2048]{2,0,1:T(8,128)(2,1)}, u32[]{:S(2)}) copy-start(bf16[512,3,2048]{2,0,1:T(8,128)(2,1)} %param.5) | copy-start | bytes 18874372
  11.1 1.4 %copy-start.2 = (bf16[384,2048]{1,0:T(8,128)(2,1)S(1)}, bf16[384,2048]{1,0:T(8,128)(2,1)}, u32[]{:S(2)}) copy-start(bf16[384,2048]{1,0:T(8,128)(2,1)} %refs_4_.1) | copy-start | bytes 4718596
  12.5 7.6 %copy-start.1 = (bf16[512,3,2048]{2,0,1:T(8,128)(2,1)S(1)}, bf16[512,3,2048]{2,0,1:T(8,128)(2,1)}, u32[]{:S(2)}) copy-start(bf16[512,3,2048]{2,0,1:T(8,128)(2,1)} %param.5) | copy-start | bytes 18874372
  16.7 3.3 %collective-permute-start.6 = (bf16[2,3,384,128]{3,2,1,0:T(8,128)(2,1)S(1)}, bf16[2,3,384,128]{3,2,1,0:T(8,128)(2,1)S(1)}, u32[]{:S(2)}, u32[]{:S(2)}) collective-permute-start(bf16[2,3,384,128]{3,2,1,0:T(8,128)(2,1)S(1)} %get-tuple-element.74), channel_id=1, source_target_pairs={{0,1},{1,0},{2,3},{3,2},{4,5},{5,4},{6,7},{7,6},{8,9},{9,8},{10,11... | collective-permute-start | bytes 1769480 | tf_op jit(solution)/shard_map/ppermute | solution.py:20
  17.0 14.0 %collective-permute-start.2 = (bf16[128,2048]{1,0:T(8,128)(2,1)S(1)}, bf16[128,2048]{1,0:T(8,128)(2,1)S(1)}, u32[]{:S(2)}, u32[]{:S(2)}) collective-permute-start(bf16[128,2048]{1,0:T(8,128)(2,1)S(1)} %get-tuple-element.68), channel_id=1, source_target_pairs={{0,4},{4,0},{1,5},{5,1},{2,6},{6,2},{3,7},{7,3},{8,12},{12,8},{9,1... | collective-permute-start | bytes 1572872 | tf_op jit(solution)/shard_map/ppermute | solution.py:20
  18.4 14.3 %collective-permute-start.1 = (bf16[128,2048]{1,0:T(8,128)(2,1)S(1)}, bf16[128,2048]{1,0:T(8,128)(2,1)S(1)}, u32[]{:S(2)}, u32[]{:S(2)}) collective-permute-start(bf16[128,2048]{1,0:T(8,128)(2,1)S(1)} %collective-permute-done.refs_0_), channel_id=1, source_target_pairs={{0,8},{8,0},{16,24},{24,16},{1,9},{9,1},{17,25},{25,17},{2,10},{10... | collective-permute-start | bytes 1572872 | tf_op jit(solution)/shard_map/ppermute | solution.py:20
  23.3 1.6 %collective-permute-start.8 = (bf16[2,3,128,128]{3,2,1,0:T(8,128)(2,1)S(1)}, bf16[2,3,128,128]{3,2,1,0:T(8,128)(2,1)S(1)}, u32[]{:S(2)}, u32[]{:S(2)}) collective-permute-start(bf16[2,3,128,128]{3,2,1,0:T(8,128)(2,1)S(1)} %get-tuple-element.77), channel_id=1, source_target_pairs={{0,1},{1,0},{2,3},{3,2},{4,5},{5,4},{6,7},{7,6},{8,9},{9,8},{10,11... | collective-permute-start | bytes 589832 | tf_op jit(solution)/shard_map/ppermute | solution.py:20
  23.4 9.4 %collective-permute-start.7 = (bf16[1,3,384,128]{3,2,1,0:T(8,128)(2,1)S(1)}, bf16[1,3,384,128]{3,2,1,0:T(8,128)(2,1)S(1)}, u32[]{:S(2)}, u32[]{:S(2)}) collective-permute-start(bf16[1,3,384,128]{3,2,1,0:T(8,128)(2,1)S(1)} %add_convert_fusion.12), channel_id=1, source_target_pairs={{0,2},{1,3},{2,0},{3,1},{4,6},{5,7},{6,4},{7,5},{8,10},{9,11},{10,... | collective-permute-start | bytes 884744 | tf_op jit(solution)/shard_map/ppermute | solution.py:20
  24.9 21.9 %copy-start.5 = (f32[7,64]{1,0:T(8,128)S(1)}, f32[7,64]{1,0:T(8,128)}, u32[]{:S(2)}) copy-start(f32[7,64]{1,0:T(8,128)} %taps_ref.1) | copy-start | bytes 5380
  35.9 1.8 %collective-permute-start.9 = (bf16[2,3,256,128]{3,2,1,0:T(8,128)(2,1)S(1)}, bf16[2,3,256,128]{3,2,1,0:T(8,128)(2,1)S(1)}, u32[]{:S(2)}, u32[]{:S(2)}) collective-permute-start(bf16[2,3,256,128]{3,2,1,0:T(8,128)(2,1)S(1)} %get-tuple-element.80), channel_id=1, source_target_pairs={{0,1},{1,0},{2,3},{3,2},{4,5},{5,4},{6,7},{7,6},{8,9},{9,8},{10,11... | collective-permute-start | bytes 1179656 | tf_op jit(solution)/shard_map/ppermute | solution.py:20
  37.7 9.1 %collective-permute-start.12 = (bf16[1,3,256,128]{3,2,1,0:T(8,128)(2,1)S(1)}, bf16[1,3,256,128]{3,2,1,0:T(8,128)(2,1)S(1)}, u32[]{:S(2)}, u32[]{:S(2)}) collective-permute-start(bf16[1,3,256,128]{3,2,1,0:T(8,128)(2,1)S(1)} %add_convert_fusion.13), channel_id=1, source_target_pairs={{0,2},{1,3},{2,0},{3,1},{4,6},{5,7},{6,4},{7,5},{8,10},{9,11},{10,... | collective-permute-start | bytes 589832 | tf_op jit(solution)/shard_map/ppermute | solution.py:20
  39.3 7.5 %collective-permute-start.11 = (bf16[1,3,128,128]{3,2,1,0:T(8,128)(2,1)S(1)}, bf16[1,3,128,128]{3,2,1,0:T(8,128)(2,1)S(1)}, u32[]{:S(2)}, u32[]{:S(2)}) collective-permute-start(bf16[1,3,128,128]{3,2,1,0:T(8,128)(2,1)S(1)} %add_convert_fusion.14), channel_id=1, source_target_pairs={{0,2},{1,3},{2,0},{3,1},{4,6},{5,7},{6,4},{7,5},{8,10},{9,11},{10,... | collective-permute-start | bytes 294920 | tf_op jit(solution)/shard_map/ppermute | solution.py:20
  40.4 6.5 %collective-permute-start.10 = (bf16[384,128]{1,0:T(8,128)(2,1)S(1)}, bf16[384,128]{1,0:T(8,128)(2,1)S(1)}, u32[]{:S(2)}, u32[]{:S(2)}) collective-permute-start(bf16[384,128]{1,0:T(8,128)(2,1)S(1)} %get-tuple-element.83), channel_id=1, source_target_pairs={{0,4},{4,0},{1,5},{5,1},{2,6},{6,2},{3,7},{7,3},{8,12},{12,8},{9,1... | collective-permute-start | bytes 294920 | tf_op jit(solution)/shard_map/ppermute | solution.py:20
  48.4 6.8 %collective-permute-start.13 = (bf16[3,384,128]{2,1,0:T(8,128)(2,1)S(1)}, bf16[3,384,128]{2,1,0:T(8,128)(2,1)S(1)}, u32[]{:S(2)}, u32[]{:S(2)}) collective-permute-start(bf16[3,384,128]{2,1,0:T(8,128)(2,1)S(1)} %get-tuple-element.86.refs_0_), channel_id=1, source_target_pairs={{0,1},{1,0},{2,3},{3,2},{4,5},{5,4},{6,7},{7,6},{8,9},{9,8},{10,11... | collective-permute-start | bytes 884744 | tf_op jit(solution)/shard_map/ppermute | solution.py:20
  48.5 6.7 %collective-permute-start.16 = (bf16[3,384,128]{2,1,0:T(8,128)(2,1)S(1)}, bf16[3,384,128]{2,1,0:T(8,128)(2,1)S(1)}, u32[]{:S(2)}, u32[]{:S(2)}) collective-permute-start(bf16[3,384,128]{2,1,0:T(8,128)(2,1)S(1)} %get-tuple-element.85.refs_0_), channel_id=1, source_target_pairs={{0,1},{1,0},{2,3},{3,2},{4,5},{5,4},{6,7},{7,6},{8,9},{9,8},{10,11... | collective-permute-start | bytes 884744 | tf_op jit(solution)/shard_map/ppermute | solution.py:20
  49.0 9.0 %collective-permute-start.14 = (bf16[3,384,128]{2,1,0:T(8,128)(2,1)S(1)}, bf16[3,384,128]{2,1,0:T(8,128)(2,1)S(1)}, u32[]{:S(2)}, u32[]{:S(2)}) collective-permute-start(bf16[3,384,128]{2,1,0:T(8,128)(2,1)S(1)} %get-tuple-element.85.refs_0_), channel_id=1, source_target_pairs={{0,2},{1,3},{2,0},{3,1},{4,6},{5,7},{6,4},{7,5},{8,10},{9,11},{10,... | collective-permute-start | bytes 884744 | tf_op jit(solution)/shard_map/ppermute | solution.py:20
  50.5 4.7 %collective-permute-start.17 = (bf16[416,128]{1,0:T(8,128)(2,1)S(1)}, bf16[416,128]{1,0:T(8,128)(2,1)S(1)}, u32[]{:S(2)}, u32[]{:S(2)}) collective-permute-start(bf16[416,128]{1,0:T(8,128)(2,1)S(1)} %get-tuple-element.87), channel_id=1, source_target_pairs={{0,4},{4,0},{1,5},{5,1},{2,6},{6,2},{3,7},{7,3},{8,12},{12,8},{9,1... | collective-permute-start | bytes 319496 | tf_op jit(solution)/shard_map/ppermute | solution.py:20
  58.0 1.6 %collective-permute-start.18 = (bf16[3,384,128]{2,1,0:T(8,128)(2,1)S(1)}, bf16[3,384,128]{2,1,0:T(8,128)(2,1)S(1)}, u32[]{:S(2)}, u32[]{:S(2)}) collective-permute-start(bf16[3,384,128]{2,1,0:T(8,128)(2,1)S(1)} %collective-permute-done.14.refs_2_), channel_id=1, source_target_pairs={{0,1},{1,0},{2,3},{3,2},{4,5},{5,4},{6,7},{7,6},{8,9},{9,8},{10,11... | collective-permute-start | bytes 884744 | tf_op jit(solution)/shard_map/ppermute | solution.py:20
  58.0 9.4 %collective-permute-start.15 = (bf16[3,384,128]{2,1,0:T(8,128)(2,1)S(1)}, bf16[3,384,128]{2,1,0:T(8,128)(2,1)S(1)}, u32[]{:S(2)}, u32[]{:S(2)}) collective-permute-start(bf16[3,384,128]{2,1,0:T(8,128)(2,1)S(1)} %get-tuple-element.86.refs_0_), channel_id=1, source_target_pairs={{0,2},{1,3},{2,0},{3,1},{4,6},{5,7},{6,4},{7,5},{8,10},{9,11},{10,... | collective-permute-start | bytes 884744 | tf_op jit(solution)/shard_map/ppermute | solution.py:20
  61.1 12.0 %collective-permute-start.20 = (bf16[384,512]{1,0:T(8,128)(2,1)S(1)}, bf16[384,512]{1,0:T(8,128)(2,1)S(1)}, u32[]{:S(2)}, u32[]{:S(2)}) collective-permute-start(bf16[384,512]{1,0:T(8,128)(2,1)S(1)} %input_grad.4), channel_id=1, source_target_pairs={{0,4},{4,0},{1,5},{5,1},{2,6},{6,2},{3,7},{7,3},{8,12},{12,8},{9,1... | collective-permute-start | bytes 1179656 | tf_op jit(solution)/shard_map/ppermute | solution.py:20
  67.4 1.6 %collective-permute-start.19 = (bf16[3,384,128]{2,1,0:T(8,128)(2,1)S(1)}, bf16[3,384,128]{2,1,0:T(8,128)(2,1)S(1)}, u32[]{:S(2)}, u32[]{:S(2)}) collective-permute-start(bf16[3,384,128]{2,1,0:T(8,128)(2,1)S(1)} %collective-permute-done.15.refs_2_), channel_id=1, source_target_pairs={{0,1},{1,0},{2,3},{3,2},{4,5},{5,4},{6,7},{7,6},{8,9},{9,8},{10,11... | collective-permute-start | bytes 884744 | tf_op jit(solution)/shard_map/ppermute | solution.py:20
  67.4 14.1 %collective-permute-start.21 = (bf16[384,512]{1,0:T(8,128)(2,1)S(1)}, bf16[384,512]{1,0:T(8,128)(2,1)S(1)}, u32[]{:S(2)}, u32[]{:S(2)}) collective-permute-start(bf16[384,512]{1,0:T(8,128)(2,1)S(1)} %get-tuple-element.95), channel_id=1, source_target_pairs={{0,4},{4,0},{1,5},{5,1},{2,6},{6,2},{3,7},{7,3},{8,12},{12,8},{9,1... | collective-permute-start | bytes 1179656 | tf_op jit(solution)/shard_map/ppermute | solution.py:20
  73.2 10.5 %collective-permute-start.22 = (bf16[384,512]{1,0:T(8,128)(2,1)S(1)}, bf16[384,512]{1,0:T(8,128)(2,1)S(1)}, u32[]{:S(2)}, u32[]{:S(2)}) collective-permute-start(bf16[384,512]{1,0:T(8,128)(2,1)S(1)} %add_convert_fusion.11), channel_id=1, source_target_pairs={{0,8},{8,0},{16,24},{24,16},{1,9},{9,1},{17,25},{25,17},{2,10},{10... | collective-permute-start | bytes 1179656 | tf_op jit(solution)/shard_map/ppermute | solution.py:20
  74.6 15.4 %collective-permute-start.23 = (bf16[384,512]{1,0:T(8,128)(2,1)S(1)}, bf16[384,512]{1,0:T(8,128)(2,1)S(1)}, u32[]{:S(2)}, u32[]{:S(2)}) collective-permute-start(bf16[384,512]{1,0:T(8,128)(2,1)S(1)} %get-tuple-element.99), channel_id=1, source_target_pairs={{0,4},{4,0},{1,5},{5,1},{2,6},{6,2},{3,7},{7,3},{8,12},{12,8},{9,1... | collective-permute-start | bytes 1179656 | tf_op jit(solution)/shard_map/ppermute | solution.py:20
  81.7 9.6 %collective-permute-start.24 = (bf16[384,512]{1,0:T(8,128)(2,1)S(1)}, bf16[384,512]{1,0:T(8,128)(2,1)S(1)}, u32[]{:S(2)}, u32[]{:S(2)}) collective-permute-start(bf16[384,512]{1,0:T(8,128)(2,1)S(1)} %add_convert_fusion.10), channel_id=1, source_target_pairs={{0,8},{8,0},{16,24},{24,16},{1,9},{9,1},{17,25},{25,17},{2,10},{10... | collective-permute-start | bytes 1179656 | tf_op jit(solution)/shard_map/ppermute | solution.py:20
  83.0 16.2 %collective-permute-start.26 = (bf16[384,512]{1,0:T(8,128)(2,1)S(1)}, bf16[384,512]{1,0:T(8,128)(2,1)S(1)}, u32[]{:S(2)}, u32[]{:S(2)}) collective-permute-start(bf16[384,512]{1,0:T(8,128)(2,1)S(1)} %get-tuple-element.104), channel_id=1, source_target_pairs={{0,4},{4,0},{1,5},{5,1},{2,6},{6,2},{3,7},{7,3},{8,12},{12,8},{9,1... | collective-permute-start | bytes 1179656 | tf_op jit(solution)/shard_map/ppermute | solution.py:20
  83.8 7.6 %collective-permute-start.25 = (bf16[384,512]{1,0:T(8,128)(2,1)S(1)}, bf16[384,512]{1,0:T(8,128)(2,1)S(1)}, u32[]{:S(2)}, u32[]{:S(2)}) collective-permute-start(bf16[384,512]{1,0:T(8,128)(2,1)S(1)} %add_convert_fusion.9), channel_id=1, source_target_pairs={{0,0},{8,16},{16,8},{24,24},{1,1},{9,17},{17,9},{25,25},{2,2},{10,... | collective-permute-start | bytes 1179656 | tf_op jit(solution)/shard_map/ppermute | solution.py:602
  91.6 11.7 %collective-permute-start.30 = (bf16[384,512]{1,0:T(8,128)(2,1)S(1)}, bf16[384,512]{1,0:T(8,128)(2,1)S(1)}, u32[]{:S(2)}, u32[]{:S(2)}) collective-permute-start(bf16[384,512]{1,0:T(8,128)(2,1)S(1)} %get-tuple-element.128), channel_id=1, source_target_pairs={{0,8},{8,0},{16,24},{24,16},{1,9},{9,1},{17,25},{25,17},{2,10},{10... | collective-permute-start | bytes 1179656 | tf_op jit(solution)/shard_map/ppermute | solution.py:20
  96.3 7.0 %collective-permute-start.31 = (bf16[384,512]{1,0:T(8,128)(2,1)S(1)}, bf16[384,512]{1,0:T(8,128)(2,1)S(1)}, u32[]{:S(2)}, u32[]{:S(2)}) collective-permute-start(bf16[384,512]{1,0:T(8,128)(2,1)S(1)} %add_convert_fusion.7), channel_id=1, source_target_pairs={{0,0},{8,16},{16,8},{24,24},{1,1},{9,17},{17,9},{25,25},{2,2},{10,... | collective-permute-start | bytes 1179656 | tf_op jit(solution)/shard_map/ppermute | solution.py:602
  97.6 2.1 %collective-permute-start.27 = (bf16[2,128,128]{2,1,0:T(8,128)(2,1)S(1)}, bf16[2,128,128]{2,1,0:T(8,128)(2,1)S(1)}, u32[]{:S(2)}, u32[]{:S(2)}) collective-permute-start(bf16[2,128,128]{2,1,0:T(8,128)(2,1)S(1)} %get-tuple-element.107), channel_id=1, source_target_pairs={{0,1},{1,0},{2,3},{3,2},{4,5},{5,4},{6,7},{7,6},{8,9},{9,8},{10,11... | collective-permute-start | bytes 196616 | tf_op jit(solution)/shard_map/ppermute | solution.py:20
  97.7 4.5 %collective-permute-start.28 = (bf16[2,128,128]{2,1,0:T(8,128)(2,1)S(1)}, bf16[2,128,128]{2,1,0:T(8,128)(2,1)S(1)}, u32[]{:S(2)}, u32[]{:S(2)}) collective-permute-start(bf16[2,128,128]{2,1,0:T(8,128)(2,1)S(1)} %get-tuple-element.108), channel_id=1, source_target_pairs={{0,2},{1,3},{2,0},{3,1},{4,6},{5,7},{6,4},{7,5},{8,10},{9,11},{10,... | collective-permute-start | bytes 196616 | tf_op jit(solution)/shard_map/ppermute | solution.py:20
  99.2 4.0 %collective-permute-start.29 = (bf16[2,128,128]{2,1,0:T(8,128)(2,1)S(1)}, bf16[2,128,128]{2,1,0:T(8,128)(2,1)S(1)}, u32[]{:S(2)}, u32[]{:S(2)}) collective-permute-start(bf16[2,128,128]{2,1,0:T(8,128)(2,1)S(1)} %get-tuple-element.109), channel_id=1, source_target_pairs={{0,3},{1,2},{2,1},{3,0},{4,7},{5,6},{6,5},{7,4},{8,11},{9,10},{10,... | collective-permute-start | bytes 196616 | tf_op jit(solution)/shard_map/ppermute | solution.py:20
  99.6 8.0 %copy-start.3 = (bf16[384,2048]{1,0:T(8,128)(2,1)S(1)}, bf16[384,2048]{1,0:T(8,128)(2,1)}, u32[]{:S(2)}) copy-start(bf16[384,2048]{1,0:T(8,128)(2,1)} %refs_4_.1) | copy-start | bytes 4718596
  103.6 12.8 %collective-permute-start.32 = (bf16[384,512]{1,0:T(8,128)(2,1)S(1)}, bf16[384,512]{1,0:T(8,128)(2,1)S(1)}, u32[]{:S(2)}, u32[]{:S(2)}) collective-permute-start(bf16[384,512]{1,0:T(8,128)(2,1)S(1)} %get-tuple-element.126), channel_id=1, source_target_pairs={{0,8},{8,0},{16,24},{24,16},{1,9},{9,1},{17,25},{25,17},{2,10},{10... | collective-permute-start | bytes 1179656 | tf_op jit(solution)/shard_map/ppermute | solution.py:20
  106.8 10.4 %collective-permute-start.33 = (bf16[384,512]{1,0:T(8,128)(2,1)S(1)}, bf16[384,512]{1,0:T(8,128)(2,1)S(1)}, u32[]{:S(2)}, u32[]{:S(2)}) collective-permute-start(bf16[384,512]{1,0:T(8,128)(2,1)S(1)} %add_convert_fusion.4), channel_id=1, source_target_pairs={{0,0},{8,16},{16,8},{24,24},{1,1},{9,17},{17,9},{25,25},{2,2},{10,... | collective-permute-start | bytes 1179656 | tf_op jit(solution)/shard_map/ppermute | solution.py:602
  116.4 9.8 %collective-permute-start.34 = (bf16[384,512]{1,0:T(8,128)(2,1)S(1)}, bf16[384,512]{1,0:T(8,128)(2,1)S(1)}, u32[]{:S(2)}, u32[]{:S(2)}) collective-permute-start(bf16[384,512]{1,0:T(8,128)(2,1)S(1)} %add_convert_fusion.2), channel_id=1, source_target_pairs={{0,0},{8,16},{16,8},{24,24},{1,1},{9,17},{17,9},{25,25},{2,2},{10,... | collective-permute-start | bytes 1179656 | tf_op jit(solution)/shard_map/ppermute | solution.py:602
  117.3 14.8 %collective-permute-start.35 = (bf16[384,512]{1,0:T(8,128)(2,1)S(1)}, bf16[384,512]{1,0:T(8,128)(2,1)S(1)}, u32[]{:S(2)}, u32[]{:S(2)}) collective-permute-start(bf16[384,512]{1,0:T(8,128)(2,1)S(1)} %add_convert_fusion.1), channel_id=1, source_target_pairs={{0,8},{8,0},{16,24},{24,16},{1,9},{9,1},{17,25},{25,17},{2,10},{10... | collective-permute-start | bytes 1179656 | tf_op jit(solution)/shard_map/ppermute | solution.py:20
  126.3 12.1 %collective-permute-start.36 = (bf16[384,512]{1,0:T(8,128)(2,1)S(1)}, bf16[384,512]{1,0:T(8,128)(2,1)S(1)}, u32[]{:S(2)}, u32[]{:S(2)}) collective-permute-start(bf16[384,512]{1,0:T(8,128)(2,1)S(1)} %add_convert_fusion), channel_id=1, source_target_pairs={{0,8},{8,0},{16,24},{24,16},{1,9},{9,1},{17,25},{25,17},{2,10},{10... | collective-permute-start | bytes 1179656 | tf_op jit(solution)/shard_map/ppermute | solution.py:20

commit v18 on v13

--- a/solution.py
+++ b/solution.py
@@ -504,11 +504,10 @@
     place = jnp.stack([depth_at, col_at, row_at, col_at * n_depth + depth_at]).astype(jnp.int32)
     w = jnp.transpose(weight, (1, 0, 2))
     width = w.shape[1] // n_depth
-    def sum_over_depth(keep, send, near_after=(), far_after=()):
+    def sum_over_depth(keep, send, near_after=()):
         near = swap(after(send, *near_after) if near_after else send, "depth", 1)
         pairs = [added(keep[r // 2], near[r // 2])[None] for r in range(2, n_depth, 2)]
-        held = [after(pair, *far_after) if far_after else pair for pair in pairs]
-        fars = [swap(pair, "depth", 2 * i + 2) for i, pair in enumerate(held)]
+        fars = [swap(pair, "depth", 2 * i + 2) for i, pair in enumerate(pairs)]
         return [keep, near] + fars, pairs, fars
 
     tok = tokens.shape[0]
@@ -534,11 +533,11 @@
         other = swap(mine, "row", 1)
         rest = swap(after(last[0], mine), "col", k)
         keep, send = project(place, [after(mine, *pairs)], w, n_depth)
-        terms, ahead, ahead_fars = sum_over_depth(keep, send)
+        terms, ahead, _ = sum_over_depth(keep, send)
         pieces.append((k, ("own",)))
         parts.append(terms)
         keep, send, x = project(place, [mine, other, after(rest, *fars, *ahead)], w, n_depth, "join")
-        terms, pairs, fars = sum_over_depth(keep, send, (), ahead_fars)
+        terms, pairs, fars = sum_over_depth(keep, send)
         pieces.append((k, ("other", "last")))
         parts.append(terms)
         xs.append(x)

time: 136 us -> 135 us (level)
  transfers between devices with their start and end apart: 37 -> 37, of which waited for: 17 -> 16; matrix products, arithmetic and copies ran while one was open for 1% -> 1% of each run, Pallas kernels for 22% -> 23%
where the time goes in v18:
time: 135 us
  waiting for transfers between devices  46.6 us (35%)
  starting transfers between devices  42.6 us (32%)
  Pallas kernels  35.1 us (26%)
  local copies, waits for them, and re-layouts  6.22 us (5%)
  other arithmetic  3.07 us (2%)
    ppermute x33, waiting for transfers between devices, swap(): return lax.ppermute(value, axis, [(i, i ^ flip) for i in range(count)])  46.6 us
    ppermute x33, starting transfers between devices, swap(): return lax.ppermute(value, axis, [(i, i ^ flip) for i in range(count)])  39.7 us
    pallas_call x2, Pallas kernels, weight_grad(): pl.pallas_call(functools.partial(weight_grad_kernel, chained=chained, gro...  11.2 us
    pallas_call x3, Pallas kernels, project(): pl.pallas_call(functools.partial(project_kernel, pieces=len(xs), mode=mod...  10.3 us
    pallas_call x4, Pallas kernels, input_grad(): pl.pallas_call(functools.partial(input_grad_kernel if single else input_g...  7.49 us
    unnamed x12, local copies, waits for them, and re-layouts  5.14 us
    ppermute x4, starting transfers between devices, on_device(): lax.ppermute(across[slot - 1], 'row', [(0, 0), (1, 2), (2, 1), (3, 3)])  2.9 us
  transfers between devices with their start and end apart: 37, of which 16 were waited for; matrix products, arithmetic and copies ran while one was open for 1% of the time, Pallas kernels for 23%

profile of v18, /device:TPU:0, one launch (start us, length us, event | category | flops | bytes accessed | tf_op | source)
XLA Modules:
  0.0 134.7 jit_solution(14275926068875523591)
XLA Ops:
  0.6 1.1 constant_dynamic-slice_fusion
  1.7 3.0 %collective-permute-start = (bf16[128,2048]{1,0:T(8,128)(2,1)S(1)}, bf16[128,2048]{1,0:T(8,128)(2,1)S(1)}, u32[]{:S(2)}, u32[]{:S(2)}) collective-permute-start(bf16[128,2048]{1,0:T(8,128)(2,1)S(1)} %constant_dynamic-slice_fusion), channel_id=1, source_target_pairs={{0,4},{4,0},{1,5},{5,1},{2,6},{6,2},{3,7},{7,3},{8,12},{12,8},{9,1... | collective-permute-start | bytes 1572872 | tf_op jit(solution)/shard_map/ppermute | solution.py:20
  4.9 0.9 copy-done.4
  5.8 0.6 split.2
  6.5 1.6 %collective-permute-start.4 = (bf16[2,96,128]{2,1,0:T(8,128)(2,1)S(1)}, bf16[2,96,128]{2,1,0:T(8,128)(2,1)S(1)}, u32[]{:S(2)}, u32[]{:S(2)}) collective-permute-start(bf16[2,96,128]{2,1,0:T(8,128)(2,1)S(1)} %get-tuple-element.72), channel_id=1, source_target_pairs={{0,2},{1,3},{2,0},{3,1},{4,6},{5,7},{6,4},{7,5},{8,10},{9,11},{10,... | collective-permute-start | bytes 147464 | tf_op jit(solution)/shard_map/ppermute | solution.py:20
  8.3 2.8 %copy-done = bf16[512,3,2048]{2,0,1:T(8,128)(2,1)S(1)} copy-done((bf16[512,3,2048]{2,0,1:T(8,128)(2,1)S(1)}, bf16[512,3,2048]{2,0,1:T(8,128)(2,1)}, u32[]{:S(2)}) %copy-start) | copy-done | bytes 6291480
  11.1 1.4 %copy-done.2 = bf16[384,2048]{1,0:T(8,128)(2,1)S(1)} copy-done((bf16[384,2048]{1,0:T(8,128)(2,1)S(1)}, bf16[384,2048]{1,0:T(8,128)(2,1)}, u32[]{:S(2)}) %copy-start.2) | copy-done | bytes 1572888
  12.5 4.1 %project.3 = (bf16[2,3,384,128]{3,2,1,0:T(8,128)(2,1)S(1)}, bf16[2,3,384,128]{3,2,1,0:T(8,128)(2,1)S(1)}, bf16[128,2048]{1,0:T(8,128)(2,1)S(1)}) custom-call(s32[4]{0:T(128)S(1)} %pad_add_fusion.place, bf16[384,2048]{1,0:T(8,128)(2,1)S(1)} %copy-done.2, bf16[3,512,2048]{2,1,0:T(8,128)(2,1)S(1)} %bitcast.6), custom_call_target="tpu_custom_call" | custom-call | flops 1 | bytes 1 | tf_op jit(solution)/shard_map/project/pallas_call | solution.py:97
  16.7 0.3 collective-permute-start.6
  17.0 1.4 %collective-permute-start.2 = (bf16[128,2048]{1,0:T(8,128)(2,1)S(1)}, bf16[128,2048]{1,0:T(8,128)(2,1)S(1)}, u32[]{:S(2)}, u32[]{:S(2)}) collective-permute-start(bf16[128,2048]{1,0:T(8,128)(2,1)S(1)} %get-tuple-element.68), channel_id=1, source_target_pairs={{0,4},{4,0},{1,5},{5,1},{2,6},{6,2},{3,7},{7,3},{8,12},{12,8},{9,1... | collective-permute-start | bytes 1572872 | tf_op jit(solution)/shard_map/ppermute | solution.py:20
  18.4 1.6 %collective-permute-start.1 = (bf16[128,2048]{1,0:T(8,128)(2,1)S(1)}, bf16[128,2048]{1,0:T(8,128)(2,1)S(1)}, u32[]{:S(2)}, u32[]{:S(2)}) collective-permute-start(bf16[128,2048]{1,0:T(8,128)(2,1)S(1)} %collective-permute-done.refs_0_), channel_id=1, source_target_pairs={{0,8},{8,0},{16,24},{24,16},{1,9},{9,1},{17,25},{25,17},{2,10},{10... | collective-permute-start | bytes 1572872 | tf_op jit(solution)/shard_map/ppermute | solution.py:20
  20.1 3.1 %project.4 = (bf16[2,3,128,128]{3,2,1,0:T(8,128)(2,1)S(1)}, bf16[2,3,128,128]{3,2,1,0:T(8,128)(2,1)S(1)}) custom-call(s32[4]{0:T(128)S(1)} %pad_add_fusion.place, bf16[128,2048]{1,0:T(8,128)(2,1)S(1)} %collective-permute-done.refs_0_, bf16[3,512,2048]{2,1,0:T(8,128)(2,1)S(1)} %bitcast.7), custom_call_target="tpu_custom_call" | custom-call | flops 1 | bytes 1 | tf_op jit(solution)/shard_map/project/pallas_call | solution.py:97
  23.4 1.6 %collective-permute-start.7 = (bf16[1,3,384,128]{3,2,1,0:T(8,128)(2,1)S(1)}, bf16[1,3,384,128]{3,2,1,0:T(8,128)(2,1)S(1)}, u32[]{:S(2)}, u32[]{:S(2)}) collective-permute-start(bf16[1,3,384,128]{3,2,1,0:T(8,128)(2,1)S(1)} %add_convert_fusion.12), channel_id=1, source_target_pairs={{0,2},{1,3},{2,0},{3,1},{4,6},{5,7},{6,4},{7,5},{8,10},{9,11},{10,... | collective-permute-start | bytes 884744 | tf_op jit(solution)/shard_map/ppermute | solution.py:20
  25.0 6.1 %collective-permute-done.2.refs_2_ = bf16[128,2048]{1,0:T(8,128)(2,1)S(1)} collective-permute-done((bf16[128,2048]{1,0:T(8,128)(2,1)S(1)}, bf16[128,2048]{1,0:T(8,128)(2,1)S(1)}, u32[]{:S(2)}, u32[]{:S(2)}) %collective-permute-start.2) | collective-permute-done | bytes 524320 | tf_op jit(solution)/shard_map/ppermute | solution.py:20
  31.0 1.7 %collective-permute-done.7.refs_4_ = bf16[1,3,384,128]{3,2,1,0:T(8,128)(2,1)S(1)} collective-permute-done((bf16[1,3,384,128]{3,2,1,0:T(8,128)(2,1)S(1)}, bf16[1,3,384,128]{3,2,1,0:T(8,128)(2,1)S(1)}, u32[]{:S(2)}, u32[]{:S(2)}) %collective-permute-start.7) | collective-permute-done | bytes 294944 | tf_op jit(solution)/shard_map/ppermute | solution.py:20
  32.8 3.1 %project.5 = (bf16[2,3,256,128]{3,2,1,0:T(8,128)(2,1)S(1)}, bf16[2,3,256,128]{3,2,1,0:T(8,128)(2,1)S(1)}, bf16[384,2048]{1,0:T(8,128)(2,1)S(1)}) custom-call(s32[4]{0:T(128)S(1)} %pad_add_fusion.place, bf16[128,2048]{1,0:T(8,128)(2,1)S(1)} %collective-permute-done.refs_0_, bf16[128,2048]{1,0:T(8,128)(2,1)S(1)} %collective-permute-done.1.refs_1_, ...), custom_call_target="tpu_custom_call" | custom-call | flops 1 | bytes 1 | tf_op jit(solution)/shard_map/project/pallas_call | solution.py:97
  36.0 1.7 %collective-permute-done.9.refs_9_ = bf16[2,3,256,128]{3,2,1,0:T(8,128)(2,1)S(1)} collective-permute-done((bf16[2,3,256,128]{3,2,1,0:T(8,128)(2,1)S(1)}, bf16[2,3,256,128]{3,2,1,0:T(8,128)(2,1)S(1)}, u32[]{:S(2)}, u32[]{:S(2)}) %collective-permute-start.9) | collective-permute-done | bytes 393248 | tf_op jit(solution)/shard_map/ppermute | solution.py:20
  37.7 1.6 %collective-permute-start.12 = (bf16[1,3,256,128]{3,2,1,0:T(8,128)(2,1)S(1)}, bf16[1,3,256,128]{3,2,1,0:T(8,128)(2,1)S(1)}, u32[]{:S(2)}, u32[]{:S(2)}) collective-permute-start(bf16[1,3,256,128]{3,2,1,0:T(8,128)(2,1)S(1)} %add_convert_fusion.13), channel_id=1, source_target_pairs={{0,2},{1,3},{2,0},{3,1},{4,6},{5,7},{6,4},{7,5},{8,10},{9,11},{10,... | collective-permute-start | bytes 589832 | tf_op jit(solution)/shard_map/ppermute | solution.py:20
  39.3 0.5 collective-permute-start.11
  39.8 0.6 merge.1
  40.4 0.7 collective-permute-start.10
  41.1 5.7 %collective-permute-done.11.refs_7_ = bf16[1,3,128,128]{3,2,1,0:T(8,128)(2,1)S(1)} collective-permute-done((bf16[1,3,128,128]{3,2,1,0:T(8,128)(2,1)S(1)}, bf16[1,3,128,128]{3,2,1,0:T(8,128)(2,1)S(1)}, u32[]{:S(2)}, u32[]{:S(2)}) %collective-permute-start.11) | collective-permute-done | bytes 98336 | tf_op jit(solution)/shard_map/ppermute | solution.py:20
  46.9 1.6 %middle.1 = (bf16[3,384,128]{2,1,0:T(8,128)(2,1)S(1)}, bf16[3,384,128]{2,1,0:T(8,128)(2,1)S(1)}, bf16[416,128]{1,0:T(8,128)(2,1)S(1)}, bf16[416,128]{1,0:T(8,128)(2,1)S(1)}) custom-call(s32[4]{0:T(128)S(1)} %pad_add_fusion.place, f32[7,64]{1,0:T(8,128)S(1)} %copy-done.5, bf16[384,128]{1,0:T(8,128)(2,1)S(1)} %get-tuple-element.82.refs_0_, ...), custom_call_target="tpu_custom_call" | custom-call | flops 1 | bytes 1 | tf_op jit(solution)/shard_map/middle/pallas_call | solution.py:326
  48.5 0.5 collective-permute-start.16
  49.0 1.5 %collective-permute-start.14 = (bf16[3,384,128]{2,1,0:T(8,128)(2,1)S(1)}, bf16[3,384,128]{2,1,0:T(8,128)(2,1)S(1)}, u32[]{:S(2)}, u32[]{:S(2)}) collective-permute-start(bf16[3,384,128]{2,1,0:T(8,128)(2,1)S(1)} %get-tuple-element.85.refs_0_), channel_id=1, source_target_pairs={{0,2},{1,3},{2,0},{3,1},{4,6},{5,7},{6,4},{7,5},{8,10},{9,11},{10,... | collective-permute-start | bytes 884744 | tf_op jit(solution)/shard_map/ppermute | solution.py:20
  50.5 0.7 collective-permute-start.17
  51.2 4.1 %collective-permute-done.17.refs_1_ = bf16[416,128]{1,0:T(8,128)(2,1)S(1)} collective-permute-done((bf16[416,128]{1,0:T(8,128)(2,1)S(1)}, bf16[416,128]{1,0:T(8,128)(2,1)S(1)}, u32[]{:S(2)}, u32[]{:S(2)}) %collective-permute-start.17) | collective-permute-done | bytes 106528 | tf_op jit(solution)/shard_map/ppermute | solution.py:20
  55.2 2.8 %collective-permute-done.14.refs_2_ = bf16[3,384,128]{2,1,0:T(8,128)(2,1)S(1)} collective-permute-done((bf16[3,384,128]{2,1,0:T(8,128)(2,1)S(1)}, bf16[3,384,128]{2,1,0:T(8,128)(2,1)S(1)}, u32[]{:S(2)}, u32[]{:S(2)}) %collective-permute-start.14) | collective-permute-done | bytes 294944 | tf_op jit(solution)/shard_map/ppermute | solution.py:20
  58.0 1.5 %collective-permute-start.15 = (bf16[3,384,128]{2,1,0:T(8,128)(2,1)S(1)}, bf16[3,384,128]{2,1,0:T(8,128)(2,1)S(1)}, u32[]{:S(2)}, u32[]{:S(2)}) collective-permute-start(bf16[3,384,128]{2,1,0:T(8,128)(2,1)S(1)} %get-tuple-element.86.refs_0_), channel_id=1, source_target_pairs={{0,2},{1,3},{2,0},{3,1},{4,6},{5,7},{6,4},{7,5},{8,10},{9,11},{10,... | collective-permute-start | bytes 884744 | tf_op jit(solution)/shard_map/ppermute | solution.py:20
  59.6 0.7 assemble.2.grad_ref.refs_1_.refs_3_
  60.3 0.8 input_grad.4
  61.1 0.7 collective-permute-start.20
  61.8 3.0 %input_grad.5 = (bf16[384,512]{1,0:T(8,128)(2,1)S(1)}, bf16[384,512]{1,0:T(8,128)(2,1)S(1)}, bf16[384,512]{1,0:T(8,128)(2,1)S(1)}) custom-call(bf16[384,1536]{1,0:T(8,128)(2,1)S(1)} %assemble.2.grad_ref.refs_1_.refs_3_, bf16[3,512,2048]{2,1,0:T(8,128)(2,1)S(1)} %bitcast.10), custom_call_target="tpu_custom_call" | custom-call | flops 1 | bytes 1 | tf_op jit(solution)/shard_map/input_grad/pallas_call | solution.py:414
  64.8 2.6 %collective-permute-done.15.refs_2_ = bf16[3,384,128]{2,1,0:T(8,128)(2,1)S(1)} collective-permute-done((bf16[3,384,128]{2,1,0:T(8,128)(2,1)S(1)}, bf16[3,384,128]{2,1,0:T(8,128)(2,1)S(1)}, u32[]{:S(2)}, u32[]{:S(2)}) %collective-permute-start.15) | collective-permute-done | bytes 294944 | tf_op jit(solution)/shard_map/ppermute | solution.py:20
  67.4 0.7 collective-permute-start.21
  68.1 0.9 collective-permute-done.19.refs_3_
  69.0 0.7 assemble.3.grad_ref.refs_0_.refs_2_
  69.8 0.8 input_grad.6
  70.6 2.6 %collective-permute-done.20 = bf16[384,512]{1,0:T(8,128)(2,1)S(1)} collective-permute-done((bf16[384,512]{1,0:T(8,128)(2,1)S(1)}, bf16[384,512]{1,0:T(8,128)(2,1)S(1)}, u32[]{:S(2)}, u32[]{:S(2)}) %collective-permute-start.20) | collective-permute-done | bytes 393248 | tf_op jit(solution)/shard_map/ppermute | solution.py:20
  73.2 1.4 %collective-permute-start.22 = (bf16[384,512]{1,0:T(8,128)(2,1)S(1)}, bf16[384,512]{1,0:T(8,128)(2,1)S(1)}, u32[]{:S(2)}, u32[]{:S(2)}) collective-permute-start(bf16[384,512]{1,0:T(8,128)(2,1)S(1)} %add_convert_fusion.11), channel_id=1, source_target_pairs={{0,8},{8,0},{16,24},{24,16},{1,9},{9,1},{17,25},{25,17},{2,10},{10... | collective-permute-start | bytes 1179656 | tf_op jit(solution)/shard_map/ppermute | solution.py:20
  74.6 0.7 collective-permute-start.23
  75.3 3.0 %input_grad.7 = (bf16[384,512]{1,0:T(8,128)(2,1)S(1)}, bf16[384,512]{1,0:T(8,128)(2,1)S(1)}, bf16[384,512]{1,0:T(8,128)(2,1)S(1)}) custom-call(bf16[384,1536]{1,0:T(8,128)(2,1)S(1)} %assemble.3.grad_ref.refs_0_.refs_2_, bf16[3,512,2048]{2,1,0:T(8,128)(2,1)S(1)} %bitcast.12), custom_call_target="tpu_custom_call" | custom-call | flops 1 | bytes 1 | tf_op jit(solution)/shard_map/input_grad/pallas_call | solution.py:414
  78.3 3.3 %collective-permute-done.21 = bf16[384,512]{1,0:T(8,128)(2,1)S(1)} collective-permute-done((bf16[384,512]{1,0:T(8,128)(2,1)S(1)}, bf16[384,512]{1,0:T(8,128)(2,1)S(1)}, u32[]{:S(2)}, u32[]{:S(2)}) %collective-permute-start.21) | collective-permute-done | bytes 393248 | tf_op jit(solution)/shard_map/ppermute | solution.py:20
  81.7 1.4 %collective-permute-start.24 = (bf16[384,512]{1,0:T(8,128)(2,1)S(1)}, bf16[384,512]{1,0:T(8,128)(2,1)S(1)}, u32[]{:S(2)}, u32[]{:S(2)}) collective-permute-start(bf16[384,512]{1,0:T(8,128)(2,1)S(1)} %add_convert_fusion.10), channel_id=1, source_target_pairs={{0,8},{8,0},{16,24},{24,16},{1,9},{9,1},{17,25},{25,17},{2,10},{10... | collective-permute-start | bytes 1179656 | tf_op jit(solution)/shard_map/ppermute | solution.py:20
  83.0 0.7 collective-permute-start.26
  83.8 0.7 collective-permute-start.25
  84.5 5.5 %collective-permute-done.23 = bf16[384,512]{1,0:T(8,128)(2,1)S(1)} collective-permute-done((bf16[384,512]{1,0:T(8,128)(2,1)S(1)}, bf16[384,512]{1,0:T(8,128)(2,1)S(1)}, u32[]{:S(2)}, u32[]{:S(2)}) %collective-permute-start.23) | collective-permute-done | bytes 393248 | tf_op jit(solution)/shard_map/ppermute | solution.py:20
  90.1 1.2 collective-permute-done.24
  91.6 4.8 %collective-permute-start.27 = (bf16[384,512]{1,0:T(8,128)(2,1)S(1)}, bf16[384,512]{1,0:T(8,128)(2,1)S(1)}, u32[]{:S(2)}, u32[]{:S(2)}) collective-permute-start(bf16[384,512]{1,0:T(8,128)(2,1)S(1)} %get-tuple-element.128), channel_id=1, source_target_pairs={{0,8},{8,0},{16,24},{24,16},{1,9},{9,1},{17,25},{25,17},{2,10},{10... | collective-permute-start | bytes 1179656 | tf_op jit(solution)/shard_map/ppermute | solution.py:20
  96.3 0.9 collective-permute-start.28
  97.2 5.6 %weight_grad.2 = (f32[3,512,2048]{2,1,0:T(8,128)}, f32[8,128]{1,0:T(8,128)S(1)}) custom-call(bf16[384,1536]{1,0:T(8,128)(2,1)S(1)} %assemble.3.grad_ref.refs_0_.refs_2_, bf16[384,1536]{1,0:T(8,128)(2,1)S(1)} %assemble.2.grad_ref.refs_1_.refs_3_, bf16[384,2048]{1,0:T(8,128)(2,1)S(1)} %copy-done.3, bf16[384,2048]{1,0:T(8,128)(2,1)S(1)} %get-tuple-element.103.refs_3_.refs_5_), custom_call_target="tpu_custom_call" | custom-call | flops 1 | bytes 1 | tf_op jit(solution)/shard_map/weight_grad/pallas_call | solution.py:471
  103.2 3.6 %collective-permute-start.29 = (bf16[384,512]{1,0:T(8,128)(2,1)S(1)}, bf16[384,512]{1,0:T(8,128)(2,1)S(1)}, u32[]{:S(2)}, u32[]{:S(2)}) collective-permute-start(bf16[384,512]{1,0:T(8,128)(2,1)S(1)} %get-tuple-element.126), channel_id=1, source_target_pairs={{0,8},{8,0},{16,24},{24,16},{1,9},{9,1},{17,25},{25,17},{2,10},{10... | collective-permute-start | bytes 1179656 | tf_op jit(solution)/shard_map/ppermute | solution.py:20
  106.8 0.7 collective-permute-start.30
  107.5 0.6 split.3
  108.1 1.6 %collective-permute-start.32 = (bf16[2,128,128]{2,1,0:T(8,128)(2,1)S(1)}, bf16[2,128,128]{2,1,0:T(8,128)(2,1)S(1)}, u32[]{:S(2)}, u32[]{:S(2)}) collective-permute-start(bf16[2,128,128]{2,1,0:T(8,128)(2,1)S(1)} %get-tuple-element.119), channel_id=1, source_target_pairs={{0,2},{1,3},{2,0},{3,1},{4,6},{5,7},{6,4},{7,5},{8,10},{9,11},{10,... | collective-permute-start | bytes 196616 | tf_op jit(solution)/shard_map/ppermute | solution.py:20
  109.7 0.3 collective-permute-start.33
  110.0 2.6 %collective-permute-done.29 = bf16[384,512]{1,0:T(8,128)(2,1)S(1)} collective-permute-done((bf16[384,512]{1,0:T(8,128)(2,1)S(1)}, bf16[384,512]{1,0:T(8,128)(2,1)S(1)}, u32[]{:S(2)}, u32[]{:S(2)}) %collective-permute-start.29) | collective-permute-done | bytes 393248 | tf_op jit(solution)/shard_map/ppermute | solution.py:20
  112.7 0.7 collective-permute-start.34
  113.5 4.8 %collective-permute-start.35 = (bf16[384,512]{1,0:T(8,128)(2,1)S(1)}, bf16[384,512]{1,0:T(8,128)(2,1)S(1)}, u32[]{:S(2)}, u32[]{:S(2)}) collective-permute-start(bf16[384,512]{1,0:T(8,128)(2,1)S(1)} %add_convert_fusion.1), channel_id=1, source_target_pairs={{0,8},{8,0},{16,24},{24,16},{1,9},{9,1},{17,25},{25,17},{2,10},{10... | collective-permute-start | bytes 1179656 | tf_op jit(solution)/shard_map/ppermute | solution.py:20
  118.3 5.6 %weight_grad.3 = (f32[3,512,2048]{2,1,0:T(8,128)}, f32[8,128]{1,0:T(8,128)S(1)}) custom-call(f32[3,512,2048]{2,1,0:T(8,128)} %get-tuple-element.104.refs_0_, f32[8,128]{1,0:T(8,128)S(1)} %get-tuple-element.105.refs_1_, bf16[384,1536]{1,0:T(8,128)(2,1)S(1)} %assemble.3.grad_ref.refs_0_.refs_2_, ...), custom_call_target="tpu_custom_call", output_to_operand_aliasing={{0}: (0, {})} | custom-call | flops 1 | bytes 1 | tf_op jit(solution)/shard_map/weight_grad/pallas_call | solution.py:471
  124.0 2.2 %collective-permute-start.36 = (bf16[384,512]{1,0:T(8,128)(2,1)S(1)}, bf16[384,512]{1,0:T(8,128)(2,1)S(1)}, u32[]{:S(2)}, u32[]{:S(2)}) collective-permute-start(bf16[384,512]{1,0:T(8,128)(2,1)S(1)} %add_convert_fusion), channel_id=1, source_target_pairs={{0,8},{8,0},{16,24},{24,16},{1,9},{9,1},{17,25},{25,17},{2,10},{10... | collective-permute-start | bytes 1179656 | tf_op jit(solution)/shard_map/ppermute | solution.py:20
  126.3 1.4 %join.1 = (bf16[96,1024]{1,0:T(8,128)(2,1)}, f32[7,64]{1,0:T(8,128)}) custom-call(s32[4]{0:T(128)S(1)} %pad_add_fusion.place, f32[8,128]{1,0:T(8,128)S(1)} %get-tuple-element.114._, bf16[2,128,128]{2,1,0:T(8,128)(2,1)S(1)} %get-tuple-element.122.refs_0_, bf16[2,128,128]{2,1,0:T(8,128)(2,1)S(1)} %collective-permute-done.31.refs_1_, ...), custom_call_target="tpu_custom_call" | custom-call | flops 1 | bytes 1 | tf_op jit(solution)/shard_map/join/pallas_call | solution.py:231
  127.7 5.6 %collective-permute-done.36 = bf16[384,512]{1,0:T(8,128)(2,1)S(1)} collective-permute-done((bf16[384,512]{1,0:T(8,128)(2,1)S(1)}, bf16[384,512]{1,0:T(8,128)(2,1)S(1)}, u32[]{:S(2)}, u32[]{:S(2)}) %collective-permute-start.36) | collective-permute-done | bytes 393248 | tf_op jit(solution)/shard_map/ppermute | solution.py:20
  133.3 1.3 pad_maximum_fusion
  (60 shorter events, 2.6 us)
Async XLA Ops:
  1.7 15.0 %collective-permute-start = (bf16[128,2048]{1,0:T(8,128)(2,1)S(1)}, bf16[128,2048]{1,0:T(8,128)(2,1)S(1)}, u32[]{:S(2)}, u32[]{:S(2)}) collective-permute-start(bf16[128,2048]{1,0:T(8,128)(2,1)S(1)} %constant_dynamic-slice_fusion), channel_id=1, source_target_pairs={{0,4},{4,0},{1,5},{5,1},{2,6},{6,2},{3,7},{7,3},{8,12},{12,8},{9,1... | collective-permute-start | bytes 1572872 | tf_op jit(solution)/shard_map/ppermute | solution.py:20
  4.8 0.9 copy-start.4
  6.4 10.2 %collective-permute-start.3 = (bf16[2,96,128]{2,1,0:T(8,128)(2,1)S(1)}, bf16[2,96,128]{2,1,0:T(8,128)(2,1)S(1)}, u32[]{:S(2)}, u32[]{:S(2)}) collective-permute-start(bf16[2,96,128]{2,1,0:T(8,128)(2,1)S(1)} %get-tuple-element.71), channel_id=1, source_target_pairs={{0,1},{1,0},{2,3},{3,2},{4,5},{5,4},{6,7},{7,6},{8,9},{9,8},{10,11... | collective-permute-start | bytes 147464 | tf_op jit(solution)/shard_map/ppermute | solution.py:20
  6.5 10.1 %collective-permute-start.4 = (bf16[2,96,128]{2,1,0:T(8,128)(2,1)S(1)}, bf16[2,96,128]{2,1,0:T(8,128)(2,1)S(1)}, u32[]{:S(2)}, u32[]{:S(2)}) collective-permute-start(bf16[2,96,128]{2,1,0:T(8,128)(2,1)S(1)} %get-tuple-element.72), channel_id=1, source_target_pairs={{0,2},{1,3},{2,0},{3,1},{4,6},{5,7},{6,4},{7,5},{8,10},{9,11},{10,... | collective-permute-start | bytes 147464 | tf_op jit(solution)/shard_map/ppermute | solution.py:20
  8.0 8.6 %collective-permute-start.5 = (bf16[2,96,128]{2,1,0:T(8,128)(2,1)S(1)}, bf16[2,96,128]{2,1,0:T(8,128)(2,1)S(1)}, u32[]{:S(2)}, u32[]{:S(2)}) collective-permute-start(bf16[2,96,128]{2,1,0:T(8,128)(2,1)S(1)} %get-tuple-element.73), channel_id=1, source_target_pairs={{0,3},{1,2},{2,1},{3,0},{4,7},{5,6},{6,5},{7,4},{8,11},{9,10},{10,... | collective-permute-start | bytes 147464 | tf_op jit(solution)/shard_map/ppermute | solution.py:20
  8.3 2.8 %copy-start = (bf16[512,3,2048]{2,0,1:T(8,128)(2,1)S(1)}, bf16[512,3,2048]{2,0,1:T(8,128)(2,1)}, u32[]{:S(2)}) copy-start(bf16[512,3,2048]{2,0,1:T(8,128)(2,1)} %param.5) | copy-start | bytes 18874372
  11.1 1.4 %copy-start.2 = (bf16[384,2048]{1,0:T(8,128)(2,1)S(1)}, bf16[384,2048]{1,0:T(8,128)(2,1)}, u32[]{:S(2)}) copy-start(bf16[384,2048]{1,0:T(8,128)(2,1)} %refs_4_.1) | copy-start | bytes 4718596
  12.5 7.6 %copy-start.1 = (bf16[512,3,2048]{2,0,1:T(8,128)(2,1)S(1)}, bf16[512,3,2048]{2,0,1:T(8,128)(2,1)}, u32[]{:S(2)}) copy-start(bf16[512,3,2048]{2,0,1:T(8,128)(2,1)} %param.5) | copy-start | bytes 18874372
  16.7 3.3 %collective-permute-start.6 = (bf16[2,3,384,128]{3,2,1,0:T(8,128)(2,1)S(1)}, bf16[2,3,384,128]{3,2,1,0:T(8,128)(2,1)S(1)}, u32[]{:S(2)}, u32[]{:S(2)}) collective-permute-start(bf16[2,3,384,128]{3,2,1,0:T(8,128)(2,1)S(1)} %get-tuple-element.74), channel_id=1, source_target_pairs={{0,1},{1,0},{2,3},{3,2},{4,5},{5,4},{6,7},{7,6},{8,9},{9,8},{10,11... | collective-permute-start | bytes 1769480 | tf_op jit(solution)/shard_map/ppermute | solution.py:20
  17.0 14.0 %collective-permute-start.2 = (bf16[128,2048]{1,0:T(8,128)(2,1)S(1)}, bf16[128,2048]{1,0:T(8,128)(2,1)S(1)}, u32[]{:S(2)}, u32[]{:S(2)}) collective-permute-start(bf16[128,2048]{1,0:T(8,128)(2,1)S(1)} %get-tuple-element.68), channel_id=1, source_target_pairs={{0,4},{4,0},{1,5},{5,1},{2,6},{6,2},{3,7},{7,3},{8,12},{12,8},{9,1... | collective-permute-start | bytes 1572872 | tf_op jit(solution)/shard_map/ppermute | solution.py:20
  18.4 14.3 %collective-permute-start.1 = (bf16[128,2048]{1,0:T(8,128)(2,1)S(1)}, bf16[128,2048]{1,0:T(8,128)(2,1)S(1)}, u32[]{:S(2)}, u32[]{:S(2)}) collective-permute-start(bf16[128,2048]{1,0:T(8,128)(2,1)S(1)} %collective-permute-done.refs_0_), channel_id=1, source_target_pairs={{0,8},{8,0},{16,24},{24,16},{1,9},{9,1},{17,25},{25,17},{2,10},{10... | collective-permute-start | bytes 1572872 | tf_op jit(solution)/shard_map/ppermute | solution.py:20
  23.3 1.6 %collective-permute-start.8 = (bf16[2,3,128,128]{3,2,1,0:T(8,128)(2,1)S(1)}, bf16[2,3,128,128]{3,2,1,0:T(8,128)(2,1)S(1)}, u32[]{:S(2)}, u32[]{:S(2)}) collective-permute-start(bf16[2,3,128,128]{3,2,1,0:T(8,128)(2,1)S(1)} %get-tuple-element.77), channel_id=1, source_target_pairs={{0,1},{1,0},{2,3},{3,2},{4,5},{5,4},{6,7},{7,6},{8,9},{9,8},{10,11... | collective-permute-start | bytes 589832 | tf_op jit(solution)/shard_map/ppermute | solution.py:20
  23.4 9.4 %collective-permute-start.7 = (bf16[1,3,384,128]{3,2,1,0:T(8,128)(2,1)S(1)}, bf16[1,3,384,128]{3,2,1,0:T(8,128)(2,1)S(1)}, u32[]{:S(2)}, u32[]{:S(2)}) collective-permute-start(bf16[1,3,384,128]{3,2,1,0:T(8,128)(2,1)S(1)} %add_convert_fusion.12), channel_id=1, source_target_pairs={{0,2},{1,3},{2,0},{3,1},{4,6},{5,7},{6,4},{7,5},{8,10},{9,11},{10,... | collective-permute-start | bytes 884744 | tf_op jit(solution)/shard_map/ppermute | solution.py:20
  24.9 21.9 %copy-start.5 = (f32[7,64]{1,0:T(8,128)S(1)}, f32[7,64]{1,0:T(8,128)}, u32[]{:S(2)}) copy-start(f32[7,64]{1,0:T(8,128)} %taps_ref.1) | copy-start | bytes 5380
  35.9 1.8 %collective-permute-start.9 = (bf16[2,3,256,128]{3,2,1,0:T(8,128)(2,1)S(1)}, bf16[2,3,256,128]{3,2,1,0:T(8,128)(2,1)S(1)}, u32[]{:S(2)}, u32[]{:S(2)}) collective-permute-start(bf16[2,3,256,128]{3,2,1,0:T(8,128)(2,1)S(1)} %get-tuple-element.80), channel_id=1, source_target_pairs={{0,1},{1,0},{2,3},{3,2},{4,5},{5,4},{6,7},{7,6},{8,9},{9,8},{10,11... | collective-permute-start | bytes 1179656 | tf_op jit(solution)/shard_map/ppermute | solution.py:20
  37.7 9.1 %collective-permute-start.12 = (bf16[1,3,256,128]{3,2,1,0:T(8,128)(2,1)S(1)}, bf16[1,3,256,128]{3,2,1,0:T(8,128)(2,1)S(1)}, u32[]{:S(2)}, u32[]{:S(2)}) collective-permute-start(bf16[1,3,256,128]{3,2,1,0:T(8,128)(2,1)S(1)} %add_convert_fusion.13), channel_id=1, source_target_pairs={{0,2},{1,3},{2,0},{3,1},{4,6},{5,7},{6,4},{7,5},{8,10},{9,11},{10,... | collective-permute-start | bytes 589832 | tf_op jit(solution)/shard_map/ppermute | solution.py:20
  39.3 7.5 %collective-permute-start.11 = (bf16[1,3,128,128]{3,2,1,0:T(8,128)(2,1)S(1)}, bf16[1,3,128,128]{3,2,1,0:T(8,128)(2,1)S(1)}, u32[]{:S(2)}, u32[]{:S(2)}) collective-permute-start(bf16[1,3,128,128]{3,2,1,0:T(8,128)(2,1)S(1)} %add_convert_fusion.14), channel_id=1, source_target_pairs={{0,2},{1,3},{2,0},{3,1},{4,6},{5,7},{6,4},{7,5},{8,10},{9,11},{10,... | collective-permute-start | bytes 294920 | tf_op jit(solution)/shard_map/ppermute | solution.py:20
  40.4 6.5 %collective-permute-start.10 = (bf16[384,128]{1,0:T(8,128)(2,1)S(1)}, bf16[384,128]{1,0:T(8,128)(2,1)S(1)}, u32[]{:S(2)}, u32[]{:S(2)}) collective-permute-start(bf16[384,128]{1,0:T(8,128)(2,1)S(1)} %get-tuple-element.83), channel_id=1, source_target_pairs={{0,4},{4,0},{1,5},{5,1},{2,6},{6,2},{3,7},{7,3},{8,12},{12,8},{9,1... | collective-permute-start | bytes 294920 | tf_op jit(solution)/shard_map/ppermute | solution.py:20
  48.4 6.8 %collective-permute-start.13 = (bf16[3,384,128]{2,1,0:T(8,128)(2,1)S(1)}, bf16[3,384,128]{2,1,0:T(8,128)(2,1)S(1)}, u32[]{:S(2)}, u32[]{:S(2)}) collective-permute-start(bf16[3,384,128]{2,1,0:T(8,128)(2,1)S(1)} %get-tuple-element.86.refs_0_), channel_id=1, source_target_pairs={{0,1},{1,0},{2,3},{3,2},{4,5},{5,4},{6,7},{7,6},{8,9},{9,8},{10,11... | collective-permute-start | bytes 884744 | tf_op jit(solution)/shard_map/ppermute | solution.py:20
  48.5 6.7 %collective-permute-start.16 = (bf16[3,384,128]{2,1,0:T(8,128)(2,1)S(1)}, bf16[3,384,128]{2,1,0:T(8,128)(2,1)S(1)}, u32[]{:S(2)}, u32[]{:S(2)}) collective-permute-start(bf16[3,384,128]{2,1,0:T(8,128)(2,1)S(1)} %get-tuple-element.85.refs_0_), channel_id=1, source_target_pairs={{0,1},{1,0},{2,3},{3,2},{4,5},{5,4},{6,7},{7,6},{8,9},{9,8},{10,11... | collective-permute-start | bytes 884744 | tf_op jit(solution)/shard_map/ppermute | solution.py:20
  49.0 9.0 %collective-permute-start.14 = (bf16[3,384,128]{2,1,0:T(8,128)(2,1)S(1)}, bf16[3,384,128]{2,1,0:T(8,128)(2,1)S(1)}, u32[]{:S(2)}, u32[]{:S(2)}) collective-permute-start(bf16[3,384,128]{2,1,0:T(8,128)(2,1)S(1)} %get-tuple-element.85.refs_0_), channel_id=1, source_target_pairs={{0,2},{1,3},{2,0},{3,1},{4,6},{5,7},{6,4},{7,5},{8,10},{9,11},{10,... | collective-permute-start | bytes 884744 | tf_op jit(solution)/shard_map/ppermute | solution.py:20
  50.5 4.7 %collective-permute-start.17 = (bf16[416,128]{1,0:T(8,128)(2,1)S(1)}, bf16[416,128]{1,0:T(8,128)(2,1)S(1)}, u32[]{:S(2)}, u32[]{:S(2)}) collective-permute-start(bf16[416,128]{1,0:T(8,128)(2,1)S(1)} %get-tuple-element.87), channel_id=1, source_target_pairs={{0,4},{4,0},{1,5},{5,1},{2,6},{6,2},{3,7},{7,3},{8,12},{12,8},{9,1... | collective-permute-start | bytes 319496 | tf_op jit(solution)/shard_map/ppermute | solution.py:20
  58.0 1.6 %collective-permute-start.18 = (bf16[3,384,128]{2,1,0:T(8,128)(2,1)S(1)}, bf16[3,384,128]{2,1,0:T(8,128)(2,1)S(1)}, u32[]{:S(2)}, u32[]{:S(2)}) collective-permute-start(bf16[3,384,128]{2,1,0:T(8,128)(2,1)S(1)} %collective-permute-done.14.refs_2_), channel_id=1, source_target_pairs={{0,1},{1,0},{2,3},{3,2},{4,5},{5,4},{6,7},{7,6},{8,9},{9,8},{10,11... | collective-permute-start | bytes 884744 | tf_op jit(solution)/shard_map/ppermute | solution.py:20
  58.0 9.4 %collective-permute-start.15 = (bf16[3,384,128]{2,1,0:T(8,128)(2,1)S(1)}, bf16[3,384,128]{2,1,0:T(8,128)(2,1)S(1)}, u32[]{:S(2)}, u32[]{:S(2)}) collective-permute-start(bf16[3,384,128]{2,1,0:T(8,128)(2,1)S(1)} %get-tuple-element.86.refs_0_), channel_id=1, source_target_pairs={{0,2},{1,3},{2,0},{3,1},{4,6},{5,7},{6,4},{7,5},{8,10},{9,11},{10,... | collective-permute-start | bytes 884744 | tf_op jit(solution)/shard_map/ppermute | solution.py:20
  61.1 12.0 %collective-permute-start.20 = (bf16[384,512]{1,0:T(8,128)(2,1)S(1)}, bf16[384,512]{1,0:T(8,128)(2,1)S(1)}, u32[]{:S(2)}, u32[]{:S(2)}) collective-permute-start(bf16[384,512]{1,0:T(8,128)(2,1)S(1)} %input_grad.4), channel_id=1, source_target_pairs={{0,4},{4,0},{1,5},{5,1},{2,6},{6,2},{3,7},{7,3},{8,12},{12,8},{9,1... | collective-permute-start | bytes 1179656 | tf_op jit(solution)/shard_map/ppermute | solution.py:20
  67.4 1.6 %collective-permute-start.19 = (bf16[3,384,128]{2,1,0:T(8,128)(2,1)S(1)}, bf16[3,384,128]{2,1,0:T(8,128)(2,1)S(1)}, u32[]{:S(2)}, u32[]{:S(2)}) collective-permute-start(bf16[3,384,128]{2,1,0:T(8,128)(2,1)S(1)} %collective-permute-done.15.refs_2_), channel_id=1, source_target_pairs={{0,1},{1,0},{2,3},{3,2},{4,5},{5,4},{6,7},{7,6},{8,9},{9,8},{10,11... | collective-permute-start | bytes 884744 | tf_op jit(solution)/shard_map/ppermute | solution.py:20
  67.4 14.1 %collective-permute-start.21 = (bf16[384,512]{1,0:T(8,128)(2,1)S(1)}, bf16[384,512]{1,0:T(8,128)(2,1)S(1)}, u32[]{:S(2)}, u32[]{:S(2)}) collective-permute-start(bf16[384,512]{1,0:T(8,128)(2,1)S(1)} %get-tuple-element.95), channel_id=1, source_target_pairs={{0,4},{4,0},{1,5},{5,1},{2,6},{6,2},{3,7},{7,3},{8,12},{12,8},{9,1... | collective-permute-start | bytes 1179656 | tf_op jit(solution)/shard_map/ppermute | solution.py:20
  73.2 10.5 %collective-permute-start.22 = (bf16[384,512]{1,0:T(8,128)(2,1)S(1)}, bf16[384,512]{1,0:T(8,128)(2,1)S(1)}, u32[]{:S(2)}, u32[]{:S(2)}) collective-permute-start(bf16[384,512]{1,0:T(8,128)(2,1)S(1)} %add_convert_fusion.11), channel_id=1, source_target_pairs={{0,8},{8,0},{16,24},{24,16},{1,9},{9,1},{17,25},{25,17},{2,10},{10... | collective-permute-start | bytes 1179656 | tf_op jit(solution)/shard_map/ppermute | solution.py:20
  74.6 15.4 %collective-permute-start.23 = (bf16[384,512]{1,0:T(8,128)(2,1)S(1)}, bf16[384,512]{1,0:T(8,128)(2,1)S(1)}, u32[]{:S(2)}, u32[]{:S(2)}) collective-permute-start(bf16[384,512]{1,0:T(8,128)(2,1)S(1)} %get-tuple-element.99), channel_id=1, source_target_pairs={{0,4},{4,0},{1,5},{5,1},{2,6},{6,2},{3,7},{7,3},{8,12},{12,8},{9,1... | collective-permute-start | bytes 1179656 | tf_op jit(solution)/shard_map/ppermute | solution.py:20
  81.7 9.6 %collective-permute-start.24 = (bf16[384,512]{1,0:T(8,128)(2,1)S(1)}, bf16[384,512]{1,0:T(8,128)(2,1)S(1)}, u32[]{:S(2)}, u32[]{:S(2)}) collective-permute-start(bf16[384,512]{1,0:T(8,128)(2,1)S(1)} %add_convert_fusion.10), channel_id=1, source_target_pairs={{0,8},{8,0},{16,24},{24,16},{1,9},{9,1},{17,25},{25,17},{2,10},{10... | collective-permute-start | bytes 1179656 | tf_op jit(solution)/shard_map/ppermute | solution.py:20
  83.0 19.8 %collective-permute-start.26 = (bf16[384,512]{1,0:T(8,128)(2,1)S(1)}, bf16[384,512]{1,0:T(8,128)(2,1)S(1)}, u32[]{:S(2)}, u32[]{:S(2)}) collective-permute-start(bf16[384,512]{1,0:T(8,128)(2,1)S(1)} %get-tuple-element.108), channel_id=1, source_target_pairs={{0,4},{4,0},{1,5},{5,1},{2,6},{6,2},{3,7},{7,3},{8,12},{12,8},{9,1... | collective-permute-start | bytes 1179656 | tf_op jit(solution)/shard_map/ppermute | solution.py:20
  83.8 7.6 %collective-permute-start.25 = (bf16[384,512]{1,0:T(8,128)(2,1)S(1)}, bf16[384,512]{1,0:T(8,128)(2,1)S(1)}, u32[]{:S(2)}, u32[]{:S(2)}) collective-permute-start(bf16[384,512]{1,0:T(8,128)(2,1)S(1)} %add_convert_fusion.9), channel_id=1, source_target_pairs={{0,0},{8,16},{16,8},{24,24},{1,1},{9,17},{17,9},{25,25},{2,2},{10,... | collective-permute-start | bytes 1179656 | tf_op jit(solution)/shard_map/ppermute | solution.py:600
  90.1 7.1 %copy-start.3 = (bf16[384,2048]{1,0:T(8,128)(2,1)S(1)}, bf16[384,2048]{1,0:T(8,128)(2,1)}, u32[]{:S(2)}) copy-start(bf16[384,2048]{1,0:T(8,128)(2,1)} %refs_4_.1) | copy-start | bytes 4718596
  91.6 11.4 %collective-permute-start.27 = (bf16[384,512]{1,0:T(8,128)(2,1)S(1)}, bf16[384,512]{1,0:T(8,128)(2,1)S(1)}, u32[]{:S(2)}, u32[]{:S(2)}) collective-permute-start(bf16[384,512]{1,0:T(8,128)(2,1)S(1)} %get-tuple-element.128), channel_id=1, source_target_pairs={{0,8},{8,0},{16,24},{24,16},{1,9},{9,1},{17,25},{25,17},{2,10},{10... | collective-permute-start | bytes 1179656 | tf_op jit(solution)/shard_map/ppermute | solution.py:20
  96.3 6.7 %collective-permute-start.28 = (bf16[384,512]{1,0:T(8,128)(2,1)S(1)}, bf16[384,512]{1,0:T(8,128)(2,1)S(1)}, u32[]{:S(2)}, u32[]{:S(2)}) collective-permute-start(bf16[384,512]{1,0:T(8,128)(2,1)S(1)} %add_convert_fusion.7), channel_id=1, source_target_pairs={{0,0},{8,16},{16,8},{24,24},{1,1},{9,17},{17,9},{25,25},{2,2},{10,... | collective-permute-start | bytes 1179656 | tf_op jit(solution)/shard_map/ppermute | solution.py:600
  103.2 9.3 %collective-permute-start.29 = (bf16[384,512]{1,0:T(8,128)(2,1)S(1)}, bf16[384,512]{1,0:T(8,128)(2,1)S(1)}, u32[]{:S(2)}, u32[]{:S(2)}) collective-permute-start(bf16[384,512]{1,0:T(8,128)(2,1)S(1)} %get-tuple-element.126), channel_id=1, source_target_pairs={{0,8},{8,0},{16,24},{24,16},{1,9},{9,1},{17,25},{25,17},{2,10},{10... | collective-permute-start | bytes 1179656 | tf_op jit(solution)/shard_map/ppermute | solution.py:20
  106.8 6.6 %collective-permute-start.30 = (bf16[384,512]{1,0:T(8,128)(2,1)S(1)}, bf16[384,512]{1,0:T(8,128)(2,1)S(1)}, u32[]{:S(2)}, u32[]{:S(2)}) collective-permute-start(bf16[384,512]{1,0:T(8,128)(2,1)S(1)} %add_convert_fusion.4), channel_id=1, source_target_pairs={{0,0},{8,16},{16,8},{24,24},{1,1},{9,17},{17,9},{25,25},{2,2},{10,... | collective-permute-start | bytes 1179656 | tf_op jit(solution)/shard_map/ppermute | solution.py:600
  108.1 15.8 %collective-permute-start.31 = (bf16[2,128,128]{2,1,0:T(8,128)(2,1)S(1)}, bf16[2,128,128]{2,1,0:T(8,128)(2,1)S(1)}, u32[]{:S(2)}, u32[]{:S(2)}) collective-permute-start(bf16[2,128,128]{2,1,0:T(8,128)(2,1)S(1)} %get-tuple-element.118), channel_id=1, source_target_pairs={{0,1},{1,0},{2,3},{3,2},{4,5},{5,4},{6,7},{7,6},{8,9},{9,8},{10,11... | collective-permute-start | bytes 196616 | tf_op jit(solution)/shard_map/ppermute | solution.py:20
  108.1 15.7 %collective-permute-start.32 = (bf16[2,128,128]{2,1,0:T(8,128)(2,1)S(1)}, bf16[2,128,128]{2,1,0:T(8,128)(2,1)S(1)}, u32[]{:S(2)}, u32[]{:S(2)}) collective-permute-start(bf16[2,128,128]{2,1,0:T(8,128)(2,1)S(1)} %get-tuple-element.119), channel_id=1, source_target_pairs={{0,2},{1,3},{2,0},{3,1},{4,6},{5,7},{6,4},{7,5},{8,10},{9,11},{10,... | collective-permute-start | bytes 196616 | tf_op jit(solution)/shard_map/ppermute | solution.py:20
  109.7 14.2 %collective-permute-start.33 = (bf16[2,128,128]{2,1,0:T(8,128)(2,1)S(1)}, bf16[2,128,128]{2,1,0:T(8,128)(2,1)S(1)}, u32[]{:S(2)}, u32[]{:S(2)}) collective-permute-start(bf16[2,128,128]{2,1,0:T(8,128)(2,1)S(1)} %get-tuple-element.120), channel_id=1, source_target_pairs={{0,3},{1,2},{2,1},{3,0},{4,7},{5,6},{6,5},{7,4},{8,11},{9,10},{10,... | collective-permute-start | bytes 196616 | tf_op jit(solution)/shard_map/ppermute | solution.py:20
  112.7 11.2 %collective-permute-start.34 = (bf16[384,512]{1,0:T(8,128)(2,1)S(1)}, bf16[384,512]{1,0:T(8,128)(2,1)S(1)}, u32[]{:S(2)}, u32[]{:S(2)}) collective-permute-start(bf16[384,512]{1,0:T(8,128)(2,1)S(1)} %add_convert_fusion.2), channel_id=1, source_target_pairs={{0,0},{8,16},{16,8},{24,24},{1,1},{9,17},{17,9},{25,25},{2,2},{10,... | collective-permute-start | bytes 1179656 | tf_op jit(solution)/shard_map/ppermute | solution.py:600
  113.5 14.1 %collective-permute-start.35 = (bf16[384,512]{1,0:T(8,128)(2,1)S(1)}, bf16[384,512]{1,0:T(8,128)(2,1)S(1)}, u32[]{:S(2)}, u32[]{:S(2)}) collective-permute-start(bf16[384,512]{1,0:T(8,128)(2,1)S(1)} %add_convert_fusion.1), channel_id=1, source_target_pairs={{0,8},{8,0},{16,24},{24,16},{1,9},{9,1},{17,25},{25,17},{2,10},{10... | collective-permute-start | bytes 1179656 | tf_op jit(solution)/shard_map/ppermute | solution.py:20
  124.0 9.3 %collective-permute-start.36 = (bf16[384,512]{1,0:T(8,128)(2,1)S(1)}, bf16[384,512]{1,0:T(8,128)(2,1)S(1)}, u32[]{:S(2)}, u32[]{:S(2)}) collective-permute-start(bf16[384,512]{1,0:T(8,128)(2,1)S(1)} %add_convert_fusion), channel_id=1, source_target_pairs={{0,8},{8,0},{16,24},{24,16},{1,9},{9,1},{17,25},{25,17},{2,10},{10... | collective-permute-start | bytes 1179656 | tf_op jit(solution)/shard_map/ppermute | solution.py:20
